TPU v7x, 32 devices: a whole 2x2x4 slice. The times are simulated.
32 devices in a mesh: gx: 4 (over z), gy: 8 (over y, x, core).
Axes of the slice: x: 2, y: 2, z: 4, core: 2. Of those that a mesh axis runs over, the one named last changes fastest.
Arguments:
- cot_vort: float32 [3, 16, 1536, 1024], P(None, None, 'gy', 'gx'), may hold values from -6 to 6
- cot_vel: float32 [3, 16, 1536, 1024], P(None, None, 'gy', 'gx'), may hold values from -6 to 6
- vorticity: bfloat16 [3, 16, 1536, 1024], P(None, None, 'gy', 'gx'), may hold values from -6 to 6
- velocity: bfloat16 [3, 16, 1536, 1024], P(None, None, 'gy', 'gx'), may hold values from -6 to 6
Outputs:
- grad_vort: float32 [3, 16, 1536, 1024], P(None, None, 'gy', 'gx')
- grad_vel: float32 [3, 16, 1536, 1024], P(None, None, 'gy', 'gx')
All inputs are finite; a program needn't handle non-finite values.
Results may differ from a plain program's by a relative error of at most 0.008.
Values may be sent and summed in bfloat16 or wider, within the bound.
No kernel may reach another device: no remote copies, remote signals or barrier semaphores. Data moves between devices by JAX's collectives and lax.ppermute only.
A program may use at most 256 MiB of HBM per device.

v0:
```python
import math

import jax
import jax.numpy as jnp
from jax import lax
from jax.sharding import PartitionSpec as P

X = 1024
Y = 1536
Z = 16


step_size = 0.5


def extended(block, sides, width):
    for axis, dim in sides:
        count = lax.axis_size(axis)
        forward = [(i, i + 1) for i in range(count - 1)]
        forward.append((count - 1, 0))
        backward = [(target, source) for source, target in forward]
        low = lax.ppermute(
            lax.slice_in_dim(block, block.shape[dim] - width, None, axis=dim), axis, forward
        )
        high = lax.ppermute(lax.slice_in_dim(block, 0, width, axis=dim), axis, backward)
        block = jnp.concatenate([low, block, high], axis=dim)
    return block


def phase_tables(first_index, second, length):
    product = first_index[:, None] * second[None, :] % length
    angles = product.astype(jnp.float32) * (2.0 * math.pi / length)
    return (jnp.cos(angles), jnp.sin(angles))


def wave_numbers(indices, length):
    signed = jnp.where(indices < length // 2, indices, indices - length)
    retained = jnp.where(indices == length // 2, 0.0, 1.0).astype(jnp.float32)
    return (signed.astype(jnp.float32) * (2.0 * math.pi / length), retained)


def along_depth(stacked, cosine, sine, sign):
    cos_part = jnp.einsum("zk,czrmx->ckrmx", cosine, stacked, preferred_element_type=jnp.float32)
    sin_part = jnp.einsum("zk,czrmx->ckrmx", sine, stacked, preferred_element_type=jnp.float32)
    real_part = cos_part[:, :, 0] + sign * sin_part[:, :, 1]
    imag_part = cos_part[:, :, 1] - sign * sin_part[:, :, 0]
    return jnp.stack([real_part, imag_part], 2).astype(jnp.bfloat16)


def along_width(real_part, imag_part, cosine, sine, sign):
    f32 = jnp.float32
    out_real = jnp.dot(real_part, cosine, preferred_element_type=f32) + sign * jnp.dot(
        imag_part, sine, preferred_element_type=f32
    )
    out_imag = jnp.dot(imag_part, cosine, preferred_element_type=f32) - sign * jnp.dot(
        real_part, sine, preferred_element_type=f32
    )
    return (out_real, out_imag)


def curl_solve(real_part, imag_part, wave_x, wave_y, wave_z, retained):
    square = wave_x * wave_x + wave_y * wave_y + wave_z * wave_z
    weight = jnp.where(square > 0, retained / jnp.where(square > 0, square, 1.0), 0.0)

    def cross(vector):
        return jnp.stack(
            [
                wave_y * vector[2] - wave_z * vector[1],
                wave_z * vector[0] - wave_x * vector[2],
                wave_x * vector[1] - wave_y * vector[0],
            ]
        )

    return (-cross(imag_part) * weight, cross(real_part) * weight)


def slope(padded, direction):
    if direction == 0:
        return (padded[:, :, 1:-1, 2:] - padded[:, :, 1:-1, :-2]) * 0.5
    if direction == 1:
        return (padded[:, :, 2:, 1:-1] - padded[:, :, :-2, 1:-1]) * 0.5
    inner = padded[:, :, 1:-1, 1:-1]
    return (jnp.roll(inner, -1, 1) - jnp.roll(inner, 1, 1)) * 0.5


def stretch_terms(adjoint, velocity_pad, vorticity_pad, adjoint_pad):
    grad_vort = jnp.stack(
        [adjoint[j] + step_size * jnp.sum(adjoint * slope(velocity_pad, j), 0) for j in range(3)]
    )
    total = jnp.zeros_like(adjoint)
    for j in range(3):
        total = total + slope(vorticity_pad[j : j + 1] * adjoint_pad, j)
    return (grad_vort, -step_size * total)


def local(cot_vort, cot_vel, vorticity, velocity):
    size_x = lax.axis_size("gx")
    size_y = lax.axis_size("gy")
    half_modes = Y // 2
    local_x = cot_vel.shape[3]
    packed = cot_vel.astype(jnp.bfloat16)
    columns = lax.all_to_all(packed, "gy", split_axis=1, concat_axis=2, tiled=True)
    row_index = jnp.arange(Y, dtype=jnp.int32)
    mode_index = jnp.arange(half_modes, dtype=jnp.int32)
    cosine_y, sine_y = phase_tables(row_index, mode_index, Y)
    forward_y = jnp.concatenate([cosine_y, -sine_y], 1).astype(jnp.bfloat16)
    yspectrum = jnp.einsum(
        "czyx,ym->czmx", columns, forward_y, preferred_element_type=jnp.float32
    ).astype(jnp.bfloat16)
    yspectrum = yspectrum.reshape(yspectrum.shape[0], yspectrum.shape[1], 2, half_modes, local_x)
    share = half_modes // (size_x * size_y)
    planes = lax.all_to_all(
        lax.all_to_all(yspectrum, "gy", split_axis=3, concat_axis=1, tiled=True),
        "gx",
        split_axis=3,
        concat_axis=4,
        tiled=True,
    )
    start = lax.axis_index("gy") * (share * size_x) + lax.axis_index("gx") * share
    depth_index = jnp.arange(Z, dtype=jnp.int32)
    cosine_z, sine_z = phase_tables(depth_index, depth_index, Z)
    cosine_z = cosine_z.astype(jnp.bfloat16)
    sine_z = sine_z.astype(jnp.bfloat16)
    zspectrum = along_depth(planes, cosine_z, sine_z, 1.0)
    width_index = jnp.arange(X, dtype=jnp.int32)
    cosine_x, sine_x = phase_tables(width_index, width_index, X)
    cosine_x = cosine_x.astype(jnp.bfloat16)
    sine_x = sine_x.astype(jnp.bfloat16)
    xreal, ximag = along_width(zspectrum[:, :, 0], zspectrum[:, :, 1], cosine_x, sine_x, 1.0)
    wave_x, keep_x = wave_numbers(width_index, X)
    wave_z, keep_z = wave_numbers(depth_index, Z)
    wave_y = (start + jnp.arange(share, dtype=jnp.int32)).astype(jnp.float32) * (2.0 * math.pi / Y)
    filtered_real, filtered_imag = curl_solve(
        xreal,
        ximag,
        wave_x[None, None, :],
        wave_y[None, :, None],
        wave_z[:, None, None],
        keep_z[:, None, None] * keep_x[None, None, :],
    )
    back_real, back_imag = along_width(
        filtered_real.astype(jnp.bfloat16),
        filtered_imag.astype(jnp.bfloat16),
        cosine_x,
        sine_x,
        -1.0,
    )
    xback = jnp.stack([back_real, back_imag], 2).astype(jnp.bfloat16)
    zback = along_depth(xback, cosine_z, sine_z, -1.0)
    returned = lax.all_to_all(
        lax.all_to_all(zback, "gx", split_axis=4, concat_axis=3, tiled=True),
        "gy",
        split_axis=1,
        concat_axis=3,
        tiled=True,
    )
    cosine_b, sine_b = phase_tables(mode_index, row_index, Y)
    doubling = jnp.where(mode_index == 0, 1.0, 2.0).astype(jnp.float32)[:, None]
    inverse_y = jnp.stack([cosine_b * doubling, -sine_b * doubling], 0).astype(jnp.bfloat16)
    spatial = jnp.einsum("czrmx,rmy->czyx", returned, inverse_y, preferred_element_type=jnp.float32)
    spatial = (spatial * (1.0 / (X * Y * Z))).astype(jnp.bfloat16)
    spectral = lax.all_to_all(spatial, "gy", split_axis=2, concat_axis=1, tiled=True)
    adjoint = cot_vort + spectral.astype(jnp.float32)
    stacked = jnp.concatenate(
        [velocity.astype(jnp.float32), vorticity.astype(jnp.float32), adjoint], 0
    )
    padded = extended(stacked.astype(jnp.bfloat16), (("gx", 3), ("gy", 2)), 1).astype(stacked.dtype)
    velocity_pad = padded[:3]
    vorticity_pad = padded[3:6]
    adjoint_pad = padded[6:]
    return stretch_terms(adjoint, velocity_pad, vorticity_pad, adjoint_pad)


def solution(mesh):
    return jax.shard_map(
        local,
        mesh=mesh,
        in_specs=(
            P(None, None, "gy", "gx"),
            P(None, None, "gy", "gx"),
            P(None, None, "gy", "gx"),
            P(None, None, "gy", "gx"),
        ),
        out_specs=(P(None, None, "gy", "gx"), P(None, None, "gy", "gx")),
        check_vma=False,
    )
```

profile of v0, /device:TPU:0, one launch (start us, length us, event | category | flops | bytes accessed | tf_op | source)
XLA Modules:
  0.0 1162.3 jit_solution(2573393514309936717)
XLA Ops:
  0.6 6.5 copy.184
  7.2 5.2 all-to-all-start
  12.3 20.4 %negate_convert_fusion = (bf16[1536,768]{0,1:T(8,128)(2,1)S(1)}, bf16[1536,768]{0,1:T(8,128)(2,1)}) fusion(), kind=kLoop, calls=%fused_computation.66 | loop fusion | flops 14155776 | bytes 4718592 | tf_op jit(solution)/shard_map/convert.15
  32.8 34.4 %all-to-all-done = bf16[3,16,192,256]{3,2,0,1:T(8,128)(2,1)} async-done(((bf16[3,16,192,256]{3,2,0,1:T(8,128)(2,1)}), bf16[3,16,192,256]{3,2,0,1:T(8,128)(2,1)}, u32[]{:S(2)}, u32[]{:S(2)}) %all-to-all-start) | async-done | bytes 4718624 | tf_op jit(solution)/shard_map/all_to_all | solution.py:102
  70.3 10.1 fusion.37
  80.4 9.4 copy.128
  89.8 58.5 %all_to_all.99 = bf16[3,2,2,768,256]{4,2,1,0,3:T(2,128)(2,1)S(1)} all-to-all(bf16[3,2,2,768,256]{4,2,1,0,3:T(2,128)(2,1)} %copy.128), channel_id=1, replica_groups=mesh['gx'=4,'gy'=8] {'gy'}, dimensions={3} | all-to-all | bytes 9437184 | tf_op jit(solution)/shard_map/all_to_all | solution.py:113
  151.7 9.4 copy.131
  161.0 6.1 all-to-all-start.2
  167.8 103.4 %all-to-all-done.2 = bf16[3,16,2,96,256]{4,2,1,0,3:T(2,128)(2,1)} async-done(((bf16[3,16,2,96,256]{4,2,1,0,3:T(2,128)(2,1)}), bf16[3,16,2,96,256]{4,2,1,0,3:T(2,128)(2,1)}, u32[]{:S(2)}, u32[]{:S(2)}) %all-to-all-start.2) | async-done | bytes 4718624 | tf_op jit(solution)/shard_map/all_to_all | solution.py:112
  271.2 7.5 copy.132
  278.7 4.8 copy.133
  283.4 8.7 all_to_all.83
  299.4 18.2 %fusion.65 = f32[3,16,24,1024]{3,2,1,0:T(8,128)S(1)} fusion(bf16[3,16,24,1024]{3,1,2,0:T(8,128)(2,1)S(1)} %get-tuple-element.23), kind=kOutput, calls=%fused_computation.108 | convolution fusion | flops 2431647744 | bytes 7077888 | tf_op jit(solution)/shard_map/dot_general | solution.py:55
  317.6 18.4 %fusion.63 = f32[3,16,24,1024]{3,2,1,0:T(8,128)S(1)} fusion(bf16[3,16,24,1024]{3,1,2,0:T(8,128)(2,1)S(1)} %get-tuple-element.24), kind=kOutput, calls=%fused_computation.107 | convolution fusion | flops 2431647744 | bytes 7077888 | tf_op jit(solution)/shard_map/dot_general | solution.py:52
  336.0 18.3 %fusion.75 = f32[3,16,24,1024]{3,2,1,0:T(8,128)S(1)} fusion(f32[3,16,24,1024]{3,2,1,0:T(8,128)S(1)} %fusion.65, bf16[3,16,24,1024]{3,1,2,0:T(8,128)(2,1)S(1)} %get-tuple-element.24), kind=kOutput, calls=%fused_computation.113 | convolution fusion | flops 2432827392 | bytes 11796480 | tf_op jit(solution)/shard_map/dot_general | solution.py:55
  354.3 18.4 %fusion.78 = f32[3,16,24,1024]{3,2,1,0:T(8,128)S(1)} fusion(f32[3,16,24,1024]{3,2,1,0:T(8,128)S(1)} %fusion.63, bf16[3,16,24,1024]{3,1,2,0:T(8,128)(2,1)S(1)} %get-tuple-element.23), kind=kOutput, calls=%fused_computation.114 | convolution fusion | flops 2432827392 | bytes 11796480 | tf_op jit(solution)/shard_map/dot_general | solution.py:52
  375.9 16.9 %fusion.67 = f32[3,16,24,1024]{3,2,1,0:T(8,128)S(1)} fusion(f32[1,16,24,1024]{3,2,1,0:T(8,128)S(1)} %get-tuple-element.41, f32[1,16,24,1024]{3,2,1,0:T(8,128)S(1)} %get-tuple-element.42, f32[1,16,24,1024]{3,2,1,0:T(8,128)S(1)} %get-tuple-element.40, f32[16,24,1024]{2,1,0:T(8,128)S(1)} %fusion.85), kind=kOutput, calls=%fused_computation.109 | convolution fusion | flops 2436366336 | bytes 11010048 | tf_op jit(solution)/shard_map/dot_general | solution.py:55
  392.9 17.4 %fusion.71 = f32[3,16,24,1024]{3,2,1,0:T(8,128)S(1)} fusion(f32[1,16,24,1024]{3,2,1,0:T(8,128)S(1)} %get-tuple-element.35, f32[1,16,24,1024]{3,2,1,0:T(8,128)S(1)} %get-tuple-element.34, f32[1,16,24,1024]{3,2,1,0:T(8,128)S(1)} %copy-done.7, f32[16,24,1024]{2,1,0:T(8,128)S(1)} %fusion.85), kind=kOutput, calls=%fused_computation.111 | convolution fusion | flops 2437545984 | bytes 11010048 | tf_op jit(solution)/shard_map/dot_general | solution.py:52
  410.2 17.8 %fusion.56 = bf16[3,16,1,24,1024]{4,3,1,0,2:T(8,128)(2,1)S(1)} fusion(f32[3,16,24,1024]{3,2,1,0:T(8,128)S(1)} %fusion.67, f32[1,16,24,1024]{3,2,1,0:T(8,128)S(1)} %get-tuple-element.35, f32[1,16,24,1024]{3,2,1,0:T(8,128)S(1)} %get-tuple-element.34, f32[1,16,24,1024]{3,2,1,0:T(8,128)S(1)} %copy-done.7, f32[16,24,1024]{2,1,0:T(8,128)S(1)} %fusion.85), kind=kOutput, calls=%fused_computation.100 | convolution fusion | flops 2441084928 | bytes 13369344 | tf_op jit(solution)/shard_map/dot_general | solution.py:55
  428.0 17.5 %fusion.55 = bf16[3,16,1,24,1024]{4,3,1,0,2:T(8,128)(2,1)S(1)} fusion(f32[3,16,24,1024]{3,2,1,0:T(8,128)S(1)} %fusion.71, f32[1,16,24,1024]{3,2,1,0:T(8,128)S(1)} %get-tuple-element.41, f32[1,16,24,1024]{3,2,1,0:T(8,128)S(1)} %get-tuple-element.42, f32[1,16,24,1024]{3,2,1,0:T(8,128)S(1)} %get-tuple-element.40, f32[16,24,1024]{2,1,0:T(8,128)S(1)} %fusion.85), kind=kOutput, calls=%fused_computation.99 | convolution fusion | flops 2439905280 | bytes 13369344 | tf_op jit(solution)/shard_map/dot_general | solution.py:52
  457.9 41.3 %copy.140 = bf16[3,16,2,24,1024]{3,1,2,0,4:T(8,128)(2,1)} copy(bf16[3,16,2,24,1024]{4,1,3,2,0:T(8,128)(2,1)} %pad_maximum_fusion.3) | data formatting | bytes 9437184 | tf_op jit(solution)/shard_map/stack | solution.py:47
  499.2 48.4 %reshape.268 = bf16[4,2,294912]{2,1,0:T(2,128)(2,1)} reshape(bf16[1024,3,2,16,24]{4,3,2,1,0:T(8,128)(2,1)} %bitcast.118) | data formatting | bytes 9437184
  547.6 110.4 %all_to_all.100 = bf16[4,2,294912]{2,1,0:T(2,128)(2,1)} all-to-all(bf16[4,2,294912]{2,1,0:T(2,128)(2,1)} %reshape.268), channel_id=1, replica_groups=mesh['gx'=4,'gy'=8] {'gx'}, dimensions={0} | all-to-all | bytes 9437184 | tf_op jit(solution)/shard_map/all_to_all | solution.py:151
  658.0 51.6 %reshape.269 = bf16[1024,3,2,16,24]{4,3,2,1,0:T(8,128)(2,1)} reshape(bf16[4,2,294912]{2,1,0:T(2,128)(2,1)} %all_to_all.100) | data formatting | bytes 9437184
  709.6 27.2 %copy.164 = bf16[3,16,2,24,4,256]{5,4,3,2,1,0:T(4,128)(2,1)} copy(bf16[3,16,2,24,4,256]{3,1,2,0,5,4:T(8,128)(2,1)} %bitcast.119) | data formatting | bytes 9437184 | tf_op jit(solution)/shard_map/all_to_all | solution.py:151
  736.8 5.6 copy.165
  747.2 21.1 %multiply_convert_fusion.1 = (bf16[1,768,1536]{1,2,0:T(8,128)(2,1)S(1)}, bf16[1,768,1536]{1,2,0:T(8,128)(2,1)}) fusion(f32[768]{0:T(1024)S(1)} %fusion.101), kind=kLoop, calls=%fused_computation.72 | loop fusion | flops 16515072 | bytes 4721664 | tf_op jit(solution)/shard_map/convert.16
  768.3 33.6 %all-to-all-done.4 = bf16[3,16,2,96,256]{4,3,2,0,1:T(8,128)(2,1)} async-done(((bf16[3,16,2,96,256]{4,3,2,0,1:T(8,128)(2,1)}), bf16[3,16,2,96,256]{4,3,2,0,1:T(8,128)(2,1)}, u32[]{:S(2)}, u32[]{:S(2)}) %all-to-all-start.4) | async-done | bytes 4718624 | tf_op jit(solution)/shard_map/all_to_all | solution.py:150
  805.1 7.7 fusion.48
  812.7 30.5 %copy.146 = bf16[3,2,1536,256]{3,1,0,2:T(2,128)(2,1)S(1)} copy(bf16[3,2,1536,256]{3,2,1,0:T(8,128)(2,1)S(1)} %fusion.48) | data formatting | bytes 9437184 | tf_op jit(solution)/shard_map/convert_element_type | solution.py:161
  843.2 57.2 %all_to_all.101 = bf16[3,2,1536,256]{3,1,0,2:T(2,128)(2,1)S(1)} all-to-all(bf16[3,2,1536,256]{3,1,0,2:T(2,128)(2,1)S(1)} %copy.146), channel_id=1, replica_groups=mesh['gx'=4,'gy'=8] {'gy'}, dimensions={2} | all-to-all | bytes 9437184 | tf_op jit(solution)/shard_map/all_to_all | solution.py:162
  907.0 11.5 fusion.162
  920.6 6.5 fusion.167
  927.1 6.1 copy.150
  934.5 6.1 copy.149
  941.5 5.0 copy.152
  946.8 5.0 copy.151
  960.3 52.0 %maximum_convert_fusion = f32[9,16,194,258]{3,2,1,0:T(8,128)} fusion(bf16[9,16,1,258]{3,2,1,0:T(2,128)(2,1)S(1)} %copy.156, bf16[9,16,192,1]{3,2,1,0:T(8,128)(2,1)} %copy.152, bf16[3,16,192,256]{3,2,1,0:T(8,128)(2,1)S(1)} %bitcast.121, bf16[3,16,192,256]{3,2,1,0:T(8,128)(2,1)} %param.6, bf16[3,16,192,256]{3,2,1,0:T(8,128)(2,1)} %param.7, ...), kind=kLoop, calls=%fused_computation | loop fusion | flops 100904832 | bytes 43244928 | tf_op jit(solution)/shard_map/convert_element_type | solution.py:167
  1012.3 16.4 %fusion.163 = (f32[3,15,192,256]{3,2,1,0:T(8,128)}, f32[3,15,192,256]{3,2,1,0:T(8,128)}) fusion(f32[9,16,194,258]{3,2,1,0:T(8,128)} %maximum_convert_fusion), kind=kLoop, calls=%fused_computation.213 | loop fusion | bytes 35389440 | tf_op jit(solution)/shard_map/jit(_roll_static)/slice | solution.py:83
  1031.6 10.8 slice_bitcast_fusion
  1042.4 19.0 %slice_multiply_fusion = (f32[3,16,194,258]{3,2,1,0:T(8,128)S(1)}, f32[3,16,194,258]{3,2,1,0:T(8,128)}, f32[3,16,194,258]{3,2,1,0:T(8,128)}) fusion(f32[9,16,194,258]{3,2,1,0:T(8,128)} %maximum_convert_fusion, f32[16,194,258]{2,1,0:T(8,128)} %get-tuple-element.12, f32[16,194,258]{2,1,0:T(8,128)} %get-tuple-element.14, f32[16,194,258]{2,1,0:T(8,128)} %get-tuple-element.13), kind=kLoop, calls=%fused_computation.2 | loop fusion | flops 7207488 | bytes 48049920 | tf_op jit(solution)/shard_map/mul | solution.py:92
  1061.4 5.2 copy-done
  1068.0 16.5 %fusion.166 = (f32[3,15,192,256]{3,2,1,0:T(8,128)}, f32[3,15,192,256]{3,2,1,0:T(8,128)}) fusion(f32[3,16,194,258]{3,2,1,0:T(8,128)} %copy-done), kind=kLoop, calls=%fused_computation.216 | loop fusion | bytes 35389440 | tf_op jit(solution)/shard_map/jit(_roll_static)/slice | solution.py:83
  1084.5 31.0 %fusion.8 = (f32[16,192,256]{2,1,0:T(8,128)S(1)}, f32[16,192,256]{2,1,0:T(8,128)}, f32[16,192,256]{2,1,0:T(8,128)}) fusion(f32[3,16,192,256]{3,2,1,0:T(8,128)} %get-tuple-element.8, f32[9,16,194,258]{3,2,1,0:T(8,128)} %maximum_convert_fusion, f32[3,15,192,256]{3,2,1,0:T(8,128)} %get-tuple-element.16, f32[3,1,192,256]{3,2,1,0:T(8,128)} %get-tuple-element.18, ...), kind=kLoop, calls=%fused_computation.17 | loop fusion | flops 30670848 | bytes 75497472 | tf_op jit(solution)/shard_map/reduce_sum | solution.py:88
  1115.6 9.6 slice_add_fusion.3
  1125.2 8.6 pad_maximum_fusion.1
  1133.8 28.0 %fusion.2 = f32[3,16,192,256]{3,2,1,0:T(8,128)} fusion(f32[3,16,194,258]{3,2,1,0:T(8,128)} %get-tuple-element.11, f32[3,16,194,258]{3,2,1,0:T(8,128)} %get-tuple-element.10, f32[3,1,192,256]{3,2,1,0:T(8,128)S(1)} %copy-done.6, f32[3,15,192,256]{3,2,1,0:T(8,128)} %get-tuple-element.28, f32[3,15,192,256]{3,2,1,0:T(8,128)} %get-tuple-element.27, ...), kind=kLoop, calls=%fused_computation.8 | loop fusion | flops 18874368 | bytes 66060288 | tf_op jit(solution)/shard_map/mul | solution.py:93
  (74 shorter events, 61.6 us)
Async XLA Ops:
  7.2 60.0 %all-to-all-start = ((bf16[3,16,192,256]{3,2,0,1:T(8,128)(2,1)}), bf16[3,16,192,256]{3,2,0,1:T(8,128)(2,1)}, u32[]{:S(2)}, u32[]{:S(2)}) async-start(bf16[3,16,192,256]{3,2,0,1:T(8,128)(2,1)} %copy.184), calls=%async_computation | async-start | bytes 9437184 | tf_op jit(solution)/shard_map/all_to_all | solution.py:102
  67.2 3.1 copy-start.3
  161.0 110.2 %all-to-all-start.2 = ((bf16[3,16,2,96,256]{4,2,1,0,3:T(2,128)(2,1)}), bf16[3,16,2,96,256]{4,2,1,0,3:T(2,128)(2,1)}, u32[]{:S(2)}, u32[]{:S(2)}) async-start(bf16[3,16,2,96,256]{4,2,1,0,3:T(2,128)(2,1)} %copy.131), calls=%async_computation.2 | async-start | bytes 9437184 | tf_op jit(solution)/shard_map/all_to_all | solution.py:112
  292.1 3.9 copy-start.2
  375.9 16.9 %copy-start.7 = (f32[1,16,24,1024]{3,2,1,0:T(8,128)S(1)}, f32[1,16,24,1024]{3,2,1,0:T(8,128)}, u32[]{:S(2)}) copy-start(f32[1,16,24,1024]{3,2,1,0:T(8,128)} %get-tuple-element.39) | copy-start | bytes 4718596
  742.5 59.5 %all-to-all-start.4 = ((bf16[3,16,2,96,256]{4,3,2,0,1:T(8,128)(2,1)}), bf16[3,16,2,96,256]{4,3,2,0,1:T(8,128)(2,1)}, u32[]{:S(2)}, u32[]{:S(2)}) async-start(bf16[3,16,2,96,256]{4,3,2,0,1:T(8,128)(2,1)} %bitcast.129), calls=%async_computation.4 | async-start | bytes 9437184 | tf_op jit(solution)/shard_map/all_to_all | solution.py:150
  802.0 3.1 copy-start.4
  902.3 16.2 %slice-start.2 = ((s8[4718592]{0:T(1024)(128)(4,1)}), s8[524288]{0:T(1024)(128)(4,1)S(1)}, s32[]{:S(2)}) async-start(s8[4718592]{0:T(1024)(128)(4,1)} %bitcast.122), calls=%async_computation.8 | async-start | bytes 1048576
  902.3 16.2 %slice-start.4 = ((s8[4718592]{0:T(1024)(128)(4,1)}), s8[4194304]{0:T(1024)(128)(4,1)S(1)}, s32[]{:S(2)}) async-start(s8[4718592]{0:T(1024)(128)(4,1)} %bitcast.124), calls=%async_computation.10 | async-start | bytes 8388608
  907.0 11.5 slice-start.3
  907.0 11.5 slice-start.5
  918.4 2.2 copy-start.1
  933.2 8.3 collective-permute-start.1
  940.6 6.2 collective-permute-start
  946.8 13.4 %slice-start = ((s8[4718592]{0:T(1024)(128)(4,1)}), s8[524288]{0:T(1024)(128)(4,1)S(1)}, s32[]{:S(2)}) async-start(s8[4718592]{0:T(1024)(128)(4,1)} %bitcast.120), calls=%async_computation.6 | async-start | bytes 1048576
  951.9 8.4 slice-start.1
  954.9 3.4 collective-permute-start.3
  955.0 5.1 collective-permute-start.2
  1061.4 5.2 copy-start
  1125.2 8.6 copy-start.5
  1125.2 8.6 copy-start.6
where the time goes:
time: 1170 us; the launch traced here: 1160 us
  local copies, waits for them, and re-layouts  348 us (30%)
  blocking collectives  226 us (19%)
  other arithmetic  219 us (19%)
  waiting for transfers between devices  176 us (15%)
  matrix products  173 us (15%)
  starting transfers between devices  18.7 us (2%)
    unnamed x31, local copies, waits for them, and re-layouts  113 us
    all_to_all x1, blocking collectives, local(): lax.all_to_all(zback, 'gx', split_axis=4, concat_axis=3, tiled=True)  110 us
    all_to_all x1, waiting for transfers between devices, local(): lax.all_to_all(lax.all_to_all(yspectrum, 'gy', split_axis=3, concat_axis=...  103 us
    all_to_all x1, blocking collectives, local(): lax.all_to_all(yspectrum, 'gy', split_axis=3, concat_axis=1, tiled=True)  58.5 us
    all_to_all x1, blocking collectives, local(): lax.all_to_all(spatial, 'gy', split_axis=2, concat_axis=1, tiled=True)  57.2 us
    another operation x4, other arithmetic  55.6 us
    convert_element_type x1, other arithmetic, local(): extended(stacked.astype(jnp.bfloat16), (('gx', 3), ('gy', 2)), 1)  52 us
    another operation x1, local copies, waits for them, and re-layouts, along_depth(): return jnp.stack([real_part, imag_part], 2).astype(jnp.bfloat16)  41.3 us
  transfers between devices with their start and end apart: 7, of which 6 were waited for; matrix products, arithmetic and copies ran while one was open for 5% of the time, Pallas kernels for 0%

commit v1 on v0

v1 whole, which is shorter than its diff:
```python
import math

import jax
import jax.numpy as jnp
import ml_dtypes
import numpy as np
from jax import lax
from jax.experimental import pallas as pl
from jax.experimental.pallas import tpu as pltpu
from jax.sharding import PartitionSpec as P

X = 1024
Y = 1536
Z = 16
HALF_X = X // 2
HALF_Y = Y // 2
KZ = Z // 2

step_size = 0.5

f32 = jnp.float32
bf16 = jnp.bfloat16

FORWARD_ORDER = (0, 1, 2)
BACK_ORDER = (2, 0, 1)


def params(megabytes=40, **extra):
    return pltpu.CompilerParams(vmem_limit_bytes=megabytes * 1024 * 1024, **extra)


def cost(flops, nbytes):
    return pl.CostEstimate(flops=int(flops), bytes_accessed=int(nbytes), transcendentals=0)


def trig(first, second, length):
    angle = (np.outer(first, second) % length) * (2.0 * math.pi / length)
    return np.cos(angle), np.sin(angle)


def y_tables(blocks):
    cosine, sine = trig(np.arange(HALF_Y), np.arange(Y), Y)
    both = np.stack([cosine.reshape(blocks, -1, Y), sine.reshape(blocks, -1, Y)], 1).reshape(Y, Y)
    both = both.astype(ml_dtypes.bfloat16)
    return both, np.ascontiguousarray(both.T)


def x_tables():
    cosine, sine = trig(np.arange(X), np.arange(HALF_X), X)
    both = np.concatenate([cosine, sine], 1).astype(ml_dtypes.bfloat16)
    return both, np.ascontiguousarray(both.T)


def slope_matrix(size):
    return ((np.eye(size, k=-1) - np.eye(size, k=1)) * 0.5).astype(ml_dtypes.bfloat16)


def combine(terms):
    total = None
    for factor, value in terms:
        if abs(factor) < 1e-12:
            continue
        if abs(factor - 1.0) < 1e-12:
            part = value
        elif abs(factor + 1.0) < 1e-12:
            part = -value
        else:
            part = value * factor
        total = part if total is None else total + part
    return total


def depth_forward(values):
    even = [values[0]] + [values[n] + values[Z - n] for n in range(1, 8)] + [values[8]]
    odd = [None] + [values[n] - values[Z - n] for n in range(1, 8)]
    even_sum = [even[n] + even[8 - n] for n in range(4)] + [even[4]]
    even_dif = [even[n] - even[8 - n] for n in range(4)]
    odd_sum = [None] + [odd[n] + odd[8 - n] for n in range(1, 4)] + [odd[4]]
    odd_dif = [None] + [odd[n] - odd[8 - n] for n in range(1, 4)]
    result = []
    for k in range(KZ):
        folded = even_sum if k % 2 == 0 else even_dif
        cos_part = combine([(math.cos(math.pi * k * n / 8), folded[n]) for n in range(len(folded))])
        folded = odd_dif if k % 2 == 0 else odd_sum
        sin_part = combine(
            [(math.sin(math.pi * k * n / 8), folded[n]) for n in range(1, len(folded))]
        )
        result.append((cos_part, sin_part))
    return result


def depth_inverse(cos_parts, sin_parts):
    layers = [None] * Z
    cos_sum, sin_sum = [None] * 9, [None] * 9
    for n in range(5):
        evens = combine([(math.cos(math.pi * k * n / 8), cos_parts[k]) for k in range(0, KZ, 2)])
        odds = combine([(math.cos(math.pi * k * n / 8), cos_parts[k]) for k in range(1, KZ, 2)])
        if n == 4:
            cos_sum[4] = evens
        else:
            cos_sum[n] = evens + odds
            cos_sum[8 - n] = evens - odds
    for n in range(1, 5):
        evens = combine([(math.sin(math.pi * k * n / 8), sin_parts[k]) for k in range(0, KZ, 2)])
        odds = combine([(math.sin(math.pi * k * n / 8), sin_parts[k]) for k in range(1, KZ, 2)])
        if n == 4:
            sin_sum[4] = odds
        else:
            sin_sum[n] = odds + evens
            sin_sum[8 - n] = odds - evens
    layers[0], layers[8] = cos_sum[0], cos_sum[8]
    for n in range(1, 8):
        layers[n] = cos_sum[n] + sin_sum[n]
        layers[Z - n] = cos_sum[n] - sin_sum[n]
    return layers


ROWS = 32


def depth_forward_kernel(values_ref, planes_ref):
    height = values_ref.shape[2]
    rows = min(16, height)
    for start in range(0, height, rows):
        part = pl.ds(start, rows)
        spectrum = depth_forward([values_ref[0, n, part, :] for n in range(Z)])
        for k, (cos_part, sin_part) in enumerate(spectrum):
            planes_ref[2 * k, part, :] = cos_part.astype(bf16)
            if sin_part is None:
                sin_part = jnp.zeros_like(cos_part)
            planes_ref[2 * k + 1, part, :] = sin_part.astype(bf16)


def depth_transform(values, component):
    _, _, height, width = values.shape
    return pl.pallas_call(
        depth_forward_kernel,
        grid=(height // ROWS,),
        in_specs=[pl.BlockSpec((1, Z, ROWS, width), lambda j: (component, 0, j, 0))],
        out_specs=pl.BlockSpec((Z, ROWS, width), lambda j: (0, j, 0)),
        out_shape=jax.ShapeDtypeStruct((Z, height, width), bf16),
        compiler_params=params(),
        cost_estimate=cost(6 * Z * height * width, 6 * Z * height * width),
        name="depth_transform",
    )(values)


def y_forward_kernel(table_ref, columns_ref, modes_ref):
    planes = columns_ref.shape[1]
    width = columns_ref.shape[3]
    for plane in range(planes):
        column = columns_ref[:, plane].reshape(Y, width)
        modes = jnp.dot(table_ref[...], column, preferred_element_type=f32)
        modes_ref[0, :, plane] = modes.astype(bf16).reshape(modes_ref.shape[1:2] + modes_ref.shape[3:])


def y_transform(table, columns, blocks, halves):
    _, planes, _, width = columns.shape
    modes = HALF_Y // (blocks * halves)
    rows = Y // blocks
    return pl.pallas_call(
        y_forward_kernel,
        grid=(blocks,),
        in_specs=[
            pl.BlockSpec((rows, Y), lambda j: (j, 0)),
            pl.BlockSpec(columns.shape, lambda j: (0, 0, 0, 0)),
        ],
        out_specs=pl.BlockSpec((1, halves, planes, 2, modes, width), lambda j: (j, 0, 0, 0, 0, 0)),
        out_shape=jax.ShapeDtypeStruct((blocks, halves, planes, 2, modes, width), bf16),
        compiler_params=params(),
        cost_estimate=cost(2 * planes * Y * Y * width, 2 * Y * Y + 4 * planes * Y * width),
        name="y_transform",
    )(table, columns)


def y_inverse_kernel(table_ref, modes_ref, rows_ref):
    planes = modes_ref.shape[2]
    width = modes_ref.shape[5]
    count, _, height, _ = rows_ref.shape
    for plane in range(planes):
        modes = modes_ref[:, :, plane].reshape(Y, width)
        rows = jnp.dot(table_ref[...], modes, preferred_element_type=f32)
        rows_ref[:, plane] = rows.astype(bf16).reshape(count, height, width)


def y_inverse(table, modes, size_y):
    planes, width = modes.shape[2], modes.shape[5]
    height = Y // size_y
    count = max(1, 384 // height)
    return pl.pallas_call(
        y_inverse_kernel,
        grid=(size_y // count,),
        in_specs=[
            pl.BlockSpec((count * height, Y), lambda j: (j, 0)),
            pl.BlockSpec(modes.shape, lambda j: (0, 0, 0, 0, 0, 0)),
        ],
        out_specs=pl.BlockSpec((count, planes, height, width), lambda j: (j, 0, 0, 0)),
        out_shape=jax.ShapeDtypeStruct((size_y, planes, height, width), bf16),
        compiler_params=params(),
        cost_estimate=cost(2 * planes * Y * Y * width, 2 * Y * Y + 4 * planes * Y * width),
        name="y_inverse",
    )(table, modes)


def x_forward_kernel(table_ref, modes_ref, spectrum_ref):
    blocks, _, _, modes, width = modes_ref.shape
    rows = jnp.concatenate(
        [modes_ref[block, 0].reshape(2 * modes, width) for block in range(blocks)], axis=1
    )
    spectrum = jnp.dot(rows, table_ref[...], preferred_element_type=f32)
    spectrum_ref[0] = spectrum.reshape(2, modes, X)


def x_transform(table, modes):
    blocks, _, _, count, width = modes.shape
    return pl.pallas_call(
        x_forward_kernel,
        grid=(2,),
        in_specs=[
            pl.BlockSpec((X, X), lambda j: (0, 0)),
            pl.BlockSpec((blocks, 1, 2, count, width), lambda j: (0, j, 0, 0, 0)),
        ],
        out_specs=pl.BlockSpec((1, 2, count, X), lambda j: (j, 0, 0, 0)),
        out_shape=jax.ShapeDtypeStruct((2, 2, count, X), f32),
        compiler_params=params(),
        cost_estimate=cost(8 * count * X * X, 2 * X * X + 24 * count * X),
        name="x_transform",
    )(table, modes)


def turned(field, axis, tz, ty, tx, wave):
    index = [tz, ty, tx]
    sign = 1.0 if index[axis] == 0 else -1.0
    index[axis] = 1 - index[axis]
    value = field[index[0], index[1], :, index[2] * HALF_X : (index[2] + 1) * HALF_X]
    return value * (wave * sign)


CURL = {
    0: ((1, 2), (0, 1)),
    1: ((0, 0), (2, 2)),
    2: ((2, 1), (1, 0)),
}


def curl_kernel(axes, where_ref, table_ref, plus_ref, minus_ref, back_ref):
    blocks, _, _, count, width = back_ref.shape
    base = where_ref[0] + pl.program_id(0) * count
    depth = where_ref[1]
    mode_y = lax.broadcasted_iota(jnp.int32, (count, HALF_X), 0) + base
    mode_x = lax.broadcasted_iota(jnp.int32, (count, HALF_X), 1)
    wave_y = mode_y.astype(f32) * (2.0 * math.pi / Y)
    wave_x = mode_x.astype(f32) * (2.0 * math.pi / X)
    wave_z = jnp.full((count, HALF_X), depth, jnp.int32).astype(f32) * (2.0 * math.pi / Z)
    square = wave_x * wave_x + wave_y * wave_y + wave_z * wave_z
    doubling = (
        jnp.where(mode_x == 0, 1.0, 2.0)
        * jnp.where(mode_y == 0, 1.0, 2.0)
        * jnp.where(wave_z == 0.0, 1.0, 2.0)
    )
    weight = jnp.where(square > 0, doubling / jnp.where(square > 0, square, 1.0), 0.0)
    waves = [wave_z * weight, wave_y * weight, wave_x * weight]
    rows = []
    for tz in range(2):
        for ty in range(2):
            parts = []
            for tx in range(2):
                parts.append(
                    (
                        turned(plus_ref, axes[0], tz, ty, tx, waves[axes[0]])
                        - turned(minus_ref, axes[1], tz, ty, tx, waves[axes[1]])
                    ).astype(bf16)
                )
            rows.append(jnp.concatenate(parts, axis=1))
    rows = jnp.concatenate(rows, axis=0)
    back = jnp.dot(rows, table_ref[...], preferred_element_type=f32).astype(bf16)
    for block in range(blocks):
        back_ref[block] = back[:, block * width : (block + 1) * width].reshape(2, 2, count, width)


def curl_inverse(where, table, spectra, component, blocks):
    (plus_axis, plus), (minus_axis, minus) = CURL[component]
    total = spectra[plus].shape[2]
    width = X // blocks
    count = 96 if total % 96 == 0 else total
    spec = pl.BlockSpec((2, 2, count, X), lambda j: (0, 0, j, 0))

    def kernel(*refs):
        curl_kernel((plus_axis, minus_axis), *refs)

    return pl.pallas_call(
        kernel,
        grid=(total // count,),
        in_specs=[
            pl.BlockSpec(memory_space=pltpu.SMEM),
            pl.BlockSpec((X, X), lambda j: (0, 0)),
            spec,
            spec,
        ],
        out_specs=pl.BlockSpec((blocks, 2, 2, count, width), lambda j: (0, 0, 0, j, 0)),
        out_shape=jax.ShapeDtypeStruct((blocks, 2, 2, total, width), bf16),
        compiler_params=params(),
        cost_estimate=cost(8 * total * X * X, 2 * X * X + 40 * total * X),
        name="curl_inverse",
    )(where, table, spectra[plus], spectra[minus])


def side_columns(planes):
    width = planes[0].shape[1]
    row = lax.broadcasted_iota(jnp.int32, (2 * Z, width), 0)
    lane = lax.broadcasted_iota(jnp.int32, (2 * Z, width), 1)
    total = None
    for n in range(Z):
        pick = ((row == n) & (lane == 0)) | ((row == n + Z) & (lane == width - 1))
        part = lax.dot_general(
            pick.astype(f32).astype(bf16),
            planes[n],
            (((1,), (1,)), ((), ())),
            preferred_element_type=f32,
        )
        total = part if total is None else total + part
    return total[:Z].astype(bf16), total[Z:].astype(bf16)


def spread_columns(low, high, n, width):
    row = lax.broadcasted_iota(jnp.int32, (2 * Z, width), 0)
    lane = lax.broadcasted_iota(jnp.int32, (2 * Z, width), 1)
    place = jnp.where((row == n) & (lane == 0), -0.5, 0.0) + jnp.where(
        (row == n + Z) & (lane == width - 1), 0.5, 0.0
    )
    both = jnp.concatenate([low, high], axis=0).astype(bf16)
    return lax.dot_general(
        both, place.astype(bf16), (((0,), (0,)), ((), ())), preferred_element_type=f32
    )


def edges_kernel(field_ref, first_column_ref, last_column_ref):
    first, last = side_columns([field_ref[0, n] for n in range(Z)])
    first_column_ref[0] = first
    last_column_ref[0] = last


def edge_columns(field, components):
    _, _, height, width = field.shape
    shape = jax.ShapeDtypeStruct((components, Z, height), bf16)
    spec = pl.BlockSpec((1, Z, height), lambda i: (i, 0, 0))
    return pl.pallas_call(
        edges_kernel,
        grid=(components,),
        in_specs=[pl.BlockSpec((1, Z, height, width), lambda i: (i, 0, 0, 0))],
        out_specs=[spec, spec],
        out_shape=[shape, shape],
        compiler_params=params(),
        cost_estimate=cost(
            components * 64 * Z * height * width, 2 * components * Z * height * width
        ),
        name="edge_columns",
    )(field)


def exchange(first, last, axis):
    count = lax.axis_size(axis)
    up = [(i, (i + 1) % count) for i in range(count)]
    down = [((i + 1) % count, i) for i in range(count)]
    return lax.ppermute(last, axis, up), lax.ppermute(first, axis, down)


def adjoint_kernel(planes_ref, cotangent_ref, adjoint_ref, first_x, last_x, first_y, last_y):
    height = planes_ref.shape[1]
    scale = 1.0 / (X * Y * Z)
    rows = 16
    for start in range(0, height, rows):
        part = pl.ds(start, rows)
        layers = depth_inverse(
            [planes_ref[2 * k, part, :].astype(f32) for k in range(KZ)],
            [planes_ref[2 * k + 1, part, :].astype(f32) for k in range(KZ)],
        )
        for n in range(Z):
            adjoint_ref[n, part, :] = cotangent_ref[0, n, part, :] + layers[n] * scale
    first, last = side_columns([adjoint_ref[n].astype(bf16) for n in range(Z)])
    first_x[...] = first
    last_x[...] = last
    first_y[...] = jnp.concatenate([adjoint_ref[n, 0:1, :] for n in range(Z)], 0).astype(bf16)
    last_y[...] = jnp.concatenate(
        [adjoint_ref[n, height - 1 : height, :] for n in range(Z)], 0
    ).astype(bf16)


def make_adjoint(planes, cotangent, component):
    _, height, width = planes.shape
    column = jax.ShapeDtypeStruct((Z, height), bf16)
    row = jax.ShapeDtypeStruct((Z, width), bf16)
    column_spec = pl.BlockSpec((Z, height), lambda j: (0, 0))
    row_spec = pl.BlockSpec((Z, width), lambda j: (0, 0))
    return pl.pallas_call(
        adjoint_kernel,
        grid=(1,),
        in_specs=[
            pl.BlockSpec((Z, height, width), lambda j: (0, 0, 0)),
            pl.BlockSpec((1, Z, height, width), lambda j: (component, 0, 0, 0)),
        ],
        out_specs=[
            pl.BlockSpec((Z, height, width), lambda j: (0, 0, 0)),
            column_spec,
            column_spec,
            row_spec,
            row_spec,
        ],
        out_shape=[
            jax.ShapeDtypeStruct((Z, height, width), f32),
            column,
            column,
            row,
            row,
        ],
        compiler_params=params(),
        cost_estimate=cost(70 * Z * height * width, 10 * Z * height * width),
        name="make_adjoint",
    )(planes, cotangent)


def pick_row(rows, n):
    index = lax.broadcasted_iota(jnp.int32, rows.shape, 0)
    return jnp.sum(jnp.where(index == n, rows.astype(f32), 0.0), axis=0, keepdims=True)


def end_rows(low, high, height):
    row = lax.broadcasted_iota(jnp.int32, (height, low.shape[1]), 0)
    return jnp.where(row == 0, low * -0.5, 0.0) + jnp.where(row == height - 1, high * 0.5, 0.0)


def grad_vort_kernel(
    component, slope_x, slope_y, velocity, adjoint, low_x, high_x, low_y, high_y, *refs
):
    before, after = refs if len(refs) == 2 else (None, refs[0])
    height, width = velocity.shape[2], velocity.shape[3]
    n = pl.program_id(0)
    above = lax.rem(n + 1, Z)
    below = lax.rem(n + Z - 1, Z)
    here = velocity[0, n]
    value = adjoint[0]
    half = value * step_size
    along_x = jnp.dot(here, slope_x[...], preferred_element_type=f32)
    along_x = along_x + spread_columns(low_x[0], high_x[0], n, width)
    along_y = jnp.dot(slope_y[...], here, preferred_element_type=f32)
    along_y = along_y + end_rows(
        pick_row(low_y[0], n), pick_row(high_y[0], n), height
    )
    along_z = (velocity[0, above].astype(f32) - velocity[0, below].astype(f32)) * 0.5
    for j, slope in enumerate((along_x, along_y, along_z)):
        term = half * slope
        if j == component:
            term = term + value
        if before is not None:
            term = before[j, 0] + term
        after[j, 0] = term


def add_grad_vort(component, slopes, velocity, adjoint, halos, before):
    _, _, height, width = velocity.shape
    slope_x, slope_y = slopes
    whole = lambda shape: pl.BlockSpec(shape, lambda n: (0,) * len(shape))
    column = pl.BlockSpec((1, Z, height), lambda n: (component, 0, 0))
    row = pl.BlockSpec((1, Z, width), lambda n: (component, 0, 0))
    sums = pl.BlockSpec((3, 1, height, width), lambda n: (0, n, 0, 0))
    operands = [slope_x, slope_y, velocity, adjoint, *halos]
    in_specs = [
        whole((width, width)),
        whole((height, height)),
        pl.BlockSpec((1, Z, height, width), lambda n: (component, 0, 0, 0)),
        pl.BlockSpec((1, height, width), lambda n: (n, 0, 0)),
        column,
        column,
        row,
        row,
    ]
    aliases = {}
    if before is not None:
        aliases = {len(operands): 0}
        operands.append(before)
        in_specs.append(sums)

    def kernel(*refs):
        grad_vort_kernel(component, *refs)

    return pl.pallas_call(
        kernel,
        grid=(Z,),
        in_specs=in_specs,
        out_specs=sums,
        out_shape=jax.ShapeDtypeStruct((3, Z, height, width), f32),
        input_output_aliases=aliases,
        compiler_params=params(),
        cost_estimate=cost(
            2 * Z * height * width * (width + height), Z * height * width * (18 + 12 * len(aliases))
        ),
        name="add_grad_vort",
    )(*operands)


def grad_vel_kernel(
    slope_x,
    vorticity,
    vorticity_above,
    vorticity_below,
    adjoint,
    vort_low_x,
    vort_high_x,
    vort_low_y,
    vort_high_y,
    low_x,
    high_x,
    low_y,
    high_y,
    *refs,
):
    after, padded = refs[-2:]
    _, _, height, width = vorticity.shape
    n = pl.program_id(0)
    above = lax.rem(n + 1, Z)
    below = lax.rem(n + Z - 1, Z)
    value = adjoint[n]

    product = vorticity[0, 0].astype(f32) * value
    coarse = product.astype(bf16)
    fine = (product - coarse.astype(f32)).astype(bf16)
    total = jnp.dot(coarse, slope_x[...], preferred_element_type=f32)
    total = total + jnp.dot(fine, slope_x[...], preferred_element_type=f32)
    low = vort_low_x[...].astype(f32) * low_x[...].astype(f32)
    high = vort_high_x[...].astype(f32) * high_x[...].astype(f32)
    total = total + spread_columns(low, high, n, width)

    padded[8 : 8 + height, :] = vorticity[1, 0].astype(f32) * value
    padded[7:8, :] = pick_row(vort_low_y[...], n) * pick_row(low_y[...], n)
    padded[8 + height : 9 + height, :] = pick_row(vort_high_y[...], n) * pick_row(high_y[...], n)
    total = total + (padded[9 : 9 + height, :] - padded[7 : 7 + height, :]) * 0.5

    total = total + (
        vorticity_above[0, 0].astype(f32) * adjoint[above]
        - vorticity_below[0, 0].astype(f32) * adjoint[below]
    ) * 0.5
    after[0, 0] = total * -step_size


def write_grad_vel(component, slope_x, vorticity, adjoint, vort_halos, halos, before):
    _, _, height, width = vorticity.shape
    whole = lambda shape: pl.BlockSpec(shape, lambda n: (0,) * len(shape))
    column = whole((Z, height))
    row = whole((Z, width))
    operands = [slope_x, vorticity, vorticity, vorticity, adjoint, *vort_halos, *halos]
    in_specs = [
        whole((width, width)),
        pl.BlockSpec((2, 1, height, width), lambda n: (0, n, 0, 0)),
        pl.BlockSpec((1, 1, height, width), lambda n: (2, lax.rem(n + 1, Z), 0, 0)),
        pl.BlockSpec((1, 1, height, width), lambda n: (2, lax.rem(n + Z - 1, Z), 0, 0)),
        whole((Z, height, width)),
        column,
        column,
        row,
        row,
        column,
        column,
        row,
        row,
    ]
    aliases = {}
    if before is not None:
        aliases = {len(operands): 0}
        operands.append(before)
        in_specs.append(pl.BlockSpec(memory_space=pl.ANY))
    return pl.pallas_call(
        grad_vel_kernel,
        grid=(Z,),
        in_specs=in_specs,
        out_specs=pl.BlockSpec((1, 1, height, width), lambda n: (component, n, 0, 0)),
        out_shape=jax.ShapeDtypeStruct((3, Z, height, width), f32),
        input_output_aliases=aliases,
        scratch_shapes=[pltpu.VMEM((height + 16, width), f32)],
        compiler_params=params(),
        cost_estimate=cost(4 * Z * height * width * width, Z * height * width * 16),
        name="write_grad_vel",
    )(*operands)


def pair_exchange(parts, axis, mine):
    count = lax.axis_size(axis)
    kept = lax.dynamic_index_in_dim(parts, mine, 1, keepdims=False)
    sent = lax.dynamic_index_in_dim(parts, 1 - mine, 1, keepdims=False)
    got = lax.ppermute(sent, axis, [(i, i ^ 1) for i in range(count)])
    return jnp.where(mine == 0, jnp.stack([kept, got], 1), jnp.stack([got, kept], 1))


def local(cot_vort, cot_vel, vorticity, velocity):
    size_x = lax.axis_size("gx")
    size_y = lax.axis_size("gy")
    planes = Z // size_y
    halves = size_y // KZ
    _, _, height, width = cot_vel.shape
    modes = HALF_Y // (size_x * halves)
    place_x = lax.axis_index("gx")
    place_y = lax.axis_index("gy")
    half = lax.rem(place_y, halves)
    where = jnp.stack([(place_x * halves + half) * modes, place_y // halves]).astype(jnp.int32)

    y_table, y_back_table = y_tables(size_x * halves)
    x_table, x_back_table = x_tables()
    slope_x = slope_matrix(width)
    slope_y = np.ascontiguousarray(slope_matrix(height).T)

    velocity_first, velocity_last = edge_columns(velocity, 3)
    vorticity_first, vorticity_last = edge_columns(vorticity, 1)
    low_x, high_x = exchange(
        jnp.concatenate([velocity_first, vorticity_first]),
        jnp.concatenate([velocity_last, vorticity_last]),
        "gx",
    )
    low_y, high_y = exchange(
        jnp.concatenate([velocity[:, :, 0], vorticity[1:2, :, 0]]),
        jnp.concatenate([velocity[:, :, height - 1], vorticity[1:2, :, height - 1]]),
        "gy",
    )
    velocity_halos = (low_x, high_x, low_y, high_y)
    vorticity_halos = (low_x[3], high_x[3], low_y[3], high_y[3])

    spectra = {}
    for component in FORWARD_ORDER:
        layers = depth_transform(cot_vel, component)
        columns = lax.all_to_all(
            layers.reshape(size_y, planes, height, width), "gy", 0, 0, tiled=True
        )
        coefficients = y_transform(y_table, columns, size_x, halves)
        if halves == 1:
            coefficients = coefficients.reshape(size_x, 2, 2, modes, width)
        else:
            coefficients = pair_exchange(
                coefficients.reshape(size_x, 2, 2, modes, width), "gy", half
            )
        lines = lax.all_to_all(coefficients, "gx", 0, 0, tiled=True)
        spectra[component] = x_transform(x_table, lines)

    grad_vort = None
    grad_vel = None
    for component in BACK_ORDER:
        filtered = curl_inverse(where, x_back_table, spectra, component, size_x)
        returned = lax.all_to_all(filtered, "gx", 0, 0, tiled=True)
        if halves == 1:
            returned = returned.reshape(size_x, 1, 2, 2, modes, width)
        else:
            returned = pair_exchange(returned, "gy", half)[:, :, None]
        rows = y_inverse(y_back_table, returned, size_y)
        layers = lax.all_to_all(rows, "gy", 0, 0, tiled=True)
        adjoint, first_x, last_x, first_y, last_y = make_adjoint(
            layers.reshape(Z, height, width), cot_vort, component
        )
        halos = exchange(first_x, last_x, "gx") + exchange(first_y, last_y, "gy")
        grad_vort = add_grad_vort(
            component, (slope_x, slope_y), velocity, adjoint, velocity_halos, grad_vort
        )
        grad_vel = write_grad_vel(
            component, slope_x, vorticity, adjoint, vorticity_halos, halos, grad_vel
        )
    return grad_vort, grad_vel


def solution(mesh):
    spec = P(None, None, "gy", "gx")
    return jax.shard_map(
        local,
        mesh=mesh,
        in_specs=(spec, spec, spec, spec),
        out_specs=(spec, spec),
        check_vma=False,
    )
```

time: 1170 us -> 503 us (0.43)
  local copies, waits for them, and re-layouts: 348 us -> 70.4 us
  blocking collectives: 226 us -> 0 us
  other arithmetic: 219 us -> 0.13 us
  matrix products: 173 us -> 0 us
  Pallas kernels: 0 us -> 118 us
  waiting for transfers between devices: 176 us -> 237 us
  starting transfers between devices: 18.7 us -> 72.9 us
    all_to_all x3 -> x0, blocking collectives: 226 us -> none  [the longest x1 110 us: local(): lax.all_to_all(zback, 'gx', split_axis=4, concat_axis=3, tiled=True)]
    dot_general x14 -> x0, matrix products: 173 us -> none  [the longest x2 35.9 us: along_width(): jnp.dot(real_part, sine, preferred_element_type=f32)]
    pallas_call x0 -> x26, Pallas kernels: none -> 118 us  [the longest x3 38.9 us: add_grad_vort(): pl.pallas_call(kernel, grid=(Z,), in_specs=in_specs, out_specs=sums, out_...]
    all_to_all x11 -> x0, local copies, waits for them, and re-layouts: 72.8 us -> none  [the longest x2 32.8 us: local(): lax.all_to_all(zback, 'gx', split_axis=4, concat_axis=3, tiled=True)]
    another operation x7 -> x1, other arithmetic: 67.3 us -> 0.08 us  [local(): jnp.stack([(place_x * halves + half) * modes, place_y // halves])]
    slice x9 -> x2, local copies, waits for them, and re-layouts: 56 us -> 2.01 us  [the longest x1 1.11 us: local(): velocity[:, :, 0]]
    convert_element_type x2 -> x0, other arithmetic: 53.3 us -> none  [the longest x1 52 us: local(): extended(stacked.astype(jnp.bfloat16), (('gx', 3), ('gy', 2)), 1)]
    all_to_all x3 -> x12, waiting for transfers between devices: 171 us -> 221 us  [the longest x3 83.5 us: local(): returned = lax.all_to_all(filtered, 'gx', 0, 0, tiled=True)]
  transfers between devices with their start and end apart: 7 -> 28, of which waited for: 6 -> 12; matrix products, arithmetic and copies ran while one was open for 5% -> 0% of each run, Pallas kernels for 0% -> 21%
where the time goes in v1:
time: 503 us; the launch traced here: 500 us
  waiting for transfers between devices  237 us (47%)
  Pallas kernels  118 us (23%)
  starting transfers between devices  72.9 us (14%)
  local copies, waits for them, and re-layouts  70.4 us (14%)
    all_to_all x3, waiting for transfers between devices, local(): returned = lax.all_to_all(filtered, 'gx', 0, 0, tiled=True)  83.5 us
    all_to_all x3, waiting for transfers between devices, local(): lines = lax.all_to_all(coefficients, 'gx', 0, 0, tiled=True)  79.6 us
    unnamed x108, local copies, waits for them, and re-layouts  68.4 us
    all_to_all x3, waiting for transfers between devices, local(): lax.all_to_all(layers.reshape(size_y, planes, height, width), 'gy', 0, 0,...  41.7 us
    pallas_call x3, Pallas kernels, add_grad_vort(): pl.pallas_call(kernel, grid=(Z,), in_specs=in_specs, out_specs=sums, out_...  38.9 us
    pallas_call x3, Pallas kernels, write_grad_vel(): pl.pallas_call(grad_vel_kernel, grid=(Z,), in_specs=in_specs, out_specs=p...  23.6 us
    ppermute x16, starting transfers between devices, exchange(): return (lax.ppermute(last, axis, up), lax.ppermute(first, axis, down))  22.7 us
    all_to_all x3, waiting for transfers between devices, local(): layers = lax.all_to_all(rows, 'gy', 0, 0, tiled=True)  16.3 us
  transfers between devices with their start and end apart: 28, of which 12 were waited for; matrix products, arithmetic and copies ran while one was open for 0% of the time, Pallas kernels for 21%

profile of v1, /device:TPU:0, one launch (start us, length us, event | category | flops | bytes accessed | tf_op | source)
XLA Modules:
  0.0 500.4 jit_solution(8239473788191510758)
XLA Ops:
  0.6 3.7 copy-done.1
  7.2 5.2 %all-to-all-start = ((bf16[8,2,192,256]{3,2,1,0:T(8,128)(2,1)}), bf16[8,2,192,256]{3,2,1,0:T(8,128)(2,1)S(1)}, u32[]{:S(2)}, u32[]{:S(2)}) async-start(bf16[8,2,192,256]{3,2,1,0:T(8,128)(2,1)} %bitcast.2), calls=%async_computation | async-start | bytes 3145728 | tf_op jit(solution)/shard_map/all_to_all | solution.py:628
  12.4 3.7 copy-done.2
  18.9 14.5 %all-to-all-done.columns_ref = bf16[8,2,192,256]{3,2,1,0:T(8,128)(2,1)S(1)} async-done(((bf16[8,2,192,256]{3,2,1,0:T(8,128)(2,1)}), bf16[8,2,192,256]{3,2,1,0:T(8,128)(2,1)S(1)}, u32[]{:S(2)}, u32[]{:S(2)}) %all-to-all-start) | async-done | bytes 1572896 | tf_op jit(solution)/shard_map/all_to_all | solution.py:628
  34.5 3.6 all-to-all-start.2
  38.1 3.7 copy-done.3
  41.8 3.0 depth_transform.5
  44.8 14.3 %all-to-all-done.2.columns_ref = bf16[8,2,192,256]{3,2,1,0:T(8,128)(2,1)S(1)} async-done(((bf16[8,2,192,256]{3,2,1,0:T(8,128)(2,1)}), bf16[8,2,192,256]{3,2,1,0:T(8,128)(2,1)S(1)}, u32[]{:S(2)}, u32[]{:S(2)}) %all-to-all-start.2) | async-done | bytes 1572896 | tf_op jit(solution)/shard_map/all_to_all | solution.py:628
  59.1 3.6 all-to-all-start.6
  66.4 3.1 y_transform.3
  70.7 12.9 %all-to-all-done.6.columns_ref = bf16[8,2,192,256]{3,2,1,0:T(8,128)(2,1)S(1)} async-done(((bf16[8,2,192,256]{3,2,1,0:T(8,128)(2,1)}), bf16[8,2,192,256]{3,2,1,0:T(8,128)(2,1)S(1)}, u32[]{:S(2)}, u32[]{:S(2)}) %all-to-all-start.6) | async-done | bytes 1572896 | tf_op jit(solution)/shard_map/all_to_all | solution.py:628
  84.8 4.9 all-to-all-start.1
  92.0 3.1 y_transform.4
  96.3 27.5 %all-to-all-done.1.modes_ref = bf16[4,2,2,192,256]{4,3,2,1,0:T(8,128)(2,1)S(1)} async-done(((bf16[4,2,2,192,256]{4,3,2,1,0:T(8,128)(2,1)}), bf16[4,2,2,192,256]{4,3,2,1,0:T(8,128)(2,1)S(1)}, u32[]{:S(2)}, u32[]{:S(2)}) %all-to-all-start.1) | async-done | bytes 1572896 | tf_op jit(solution)/shard_map/all_to_all | solution.py:638
  124.9 3.6 all-to-all-start.3
  132.2 3.9 y_transform.5
  136.1 28.8 %all-to-all-done.3.modes_ref = bf16[4,2,2,192,256]{4,3,2,1,0:T(8,128)(2,1)S(1)} async-done(((bf16[4,2,2,192,256]{4,3,2,1,0:T(8,128)(2,1)}), bf16[4,2,2,192,256]{4,3,2,1,0:T(8,128)(2,1)S(1)}, u32[]{:S(2)}, u32[]{:S(2)}) %all-to-all-start.3) | async-done | bytes 1572896 | tf_op jit(solution)/shard_map/all_to_all | solution.py:638
  166.0 4.4 all-to-all-start.7
  177.7 3.0 curl_inverse.3
  183.5 23.4 %all-to-all-done.7.modes_ref = bf16[4,2,2,192,256]{4,3,2,1,0:T(8,128)(2,1)} async-done(((bf16[4,2,2,192,256]{4,3,2,1,0:T(8,128)(2,1)}), bf16[4,2,2,192,256]{4,3,2,1,0:T(8,128)(2,1)}, u32[]{:S(2)}, u32[]{:S(2)}) %all-to-all-start.7) | async-done | bytes 1572896 | tf_op jit(solution)/shard_map/all_to_all | solution.py:638
  206.9 4.3 all-to-all-start.4
  212.9 3.3 x_transform.5.refs_3_.refs_2_
  216.2 3.0 curl_inverse.4
  222.0 25.8 %all-to-all-done.4 = bf16[4,2,2,192,256]{4,3,2,1,0:T(8,128)(2,1)} async-done(((bf16[4,2,2,192,256]{4,3,2,1,0:T(8,128)(2,1)}), bf16[4,2,2,192,256]{4,3,2,1,0:T(8,128)(2,1)}, u32[]{:S(2)}, u32[]{:S(2)}) %all-to-all-start.4) | async-done | bytes 1572896 | tf_op jit(solution)/shard_map/all_to_all | solution.py:645
  247.8 4.4 all-to-all-start.8
  259.7 28.9 %all-to-all-done.8 = bf16[4,2,2,192,256]{4,3,2,1,0:T(8,128)(2,1)} async-done(((bf16[4,2,2,192,256]{4,3,2,1,0:T(8,128)(2,1)}), bf16[4,2,2,192,256]{4,3,2,1,0:T(8,128)(2,1)}, u32[]{:S(2)}, u32[]{:S(2)}) %all-to-all-start.8) | async-done | bytes 1572896 | tf_op jit(solution)/shard_map/all_to_all | solution.py:645
  288.7 3.6 all-to-all-start.10
  294.6 5.3 %y_inverse.3 = bf16[8,2,192,256]{3,2,1,0:T(8,128)(2,1)} custom-call(bf16[1536,1536]{1,0:T(8,128)(2,1)S(1)} %copy-done.42, bf16[4,1,2,2,192,256]{5,4,3,2,1,0:T(8,128)(2,1)} %bitcast.6.modes_ref), custom_call_target="tpu_custom_call" | custom-call | flops 2415919104 | bytes 7864320 | tf_op jit(solution)/shard_map/y_inverse/pallas_call | solution.py:190
  299.9 28.8 %all-to-all-done.10 = bf16[4,2,2,192,256]{4,3,2,1,0:T(8,128)(2,1)S(1)} async-done(((bf16[4,2,2,192,256]{4,3,2,1,0:T(8,128)(2,1)}), bf16[4,2,2,192,256]{4,3,2,1,0:T(8,128)(2,1)S(1)}, u32[]{:S(2)}, u32[]{:S(2)}) %all-to-all-start.10) | async-done | bytes 1572896 | tf_op jit(solution)/shard_map/all_to_all | solution.py:645
  329.8 4.9 all-to-all-start.5
  337.1 4.5 y_inverse.4
  342.7 13.0 %all-to-all-done.5 = bf16[8,2,192,256]{3,2,1,0:T(8,128)(2,1)S(1)} async-done(((bf16[8,2,192,256]{3,2,1,0:T(8,128)(2,1)}), bf16[8,2,192,256]{3,2,1,0:T(8,128)(2,1)S(1)}, u32[]{:S(2)}, u32[]{:S(2)}) %all-to-all-start.5) | async-done | bytes 1572896 | tf_op jit(solution)/shard_map/all_to_all | solution.py:651
  355.7 3.6 all-to-all-start.9
  366.5 3.9 collective-permute-start.1
  372.7 3.1 y_inverse.5
  376.9 3.3 all-to-all-done.9
  380.3 4.3 all-to-all-start.11
  389.6 16.1 %collective-permute-done.2.refs_6_ = bf16[4,16,256]{2,1,0:T(8,128)(2,1)S(1)} collective-permute-done((bf16[4,16,256]{2,1,0:T(8,128)(2,1)S(1)}, bf16[4,16,256]{2,1,0:T(8,128)(2,1)S(1)}, u32[]{:S(2)}, u32[]{:S(2)}) %collective-permute-start.2) | collective-permute-done | bytes 32800 | tf_op jit(solution)/shard_map/ppermute | solution.py:365
  405.8 3.7 copy-done.4
  415.4 3.7 copy-done.5
  422.2 3.7 collective-permute-start.13
  428.5 8.9 %add_grad_vort.3.refs_8_ = f32[3,16,192,256]{3,2,1,0:T(8,128)} custom-call(bf16[256,256]{1,0:T(8,128)(2,1)S(1)} %copy-done.30, bf16[192,192]{1,0:T(8,128)(2,1)S(1)} %copy-done.41, bf16[3,16,192,256]{3,2,1,0:T(8,128)(2,1)S(1)} %bitcast.37, f32[16,192,256]{2,1,0:T(8,128)S(1)} %get-tuple-element.27.refs_3_.adjoint, ...), custom_call_target="tpu_custom_call" | custom-call | flops 704643072 | bytes 14155776 | tf_op jit(solution)/shard_map/add_grad_vort/pallas_call | solution.py:486
  437.5 14.3 %add_grad_vort.4.refs_8_ = f32[3,16,192,256]{3,2,1,0:T(8,128)} custom-call(bf16[256,256]{1,0:T(8,128)(2,1)S(1)} %copy-done.30, bf16[192,192]{1,0:T(8,128)(2,1)S(1)} %copy-done.41, bf16[3,16,192,256]{3,2,1,0:T(8,128)(2,1)S(1)} %bitcast.37, f32[16,192,256]{2,1,0:T(8,128)S(1)} %copy-done.20, ...), custom_call_target="tpu_custom_call", output_to_operand_aliasing={{}: (8, {})} | custom-call | flops 704643072 | bytes 23592960 | tf_op jit(solution)/shard_map/add_grad_vort/pallas_call | solution.py:486
  451.8 15.6 %add_grad_vort.5 = f32[3,16,192,256]{3,2,1,0:T(8,128)} custom-call(bf16[256,256]{1,0:T(8,128)(2,1)S(1)} %copy-done.30, bf16[192,192]{1,0:T(8,128)(2,1)S(1)} %copy-done.41, bf16[3,16,192,256]{3,2,1,0:T(8,128)(2,1)S(1)} %bitcast.37, f32[16,192,256]{2,1,0:T(8,128)S(1)} %copy-done.18, ...), custom_call_target="tpu_custom_call", output_to_operand_aliasing={{}: (8, {})} | custom-call | flops 704643072 | bytes 23592960 | tf_op jit(solution)/shard_map/add_grad_vort/pallas_call | solution.py:486
  467.4 3.8 collective-permute-start.9
  473.9 7.9 %write_grad_vel.3.refs_0_ = f32[3,16,192,256]{3,2,1,0:T(8,128)} custom-call(bf16[256,256]{1,0:T(8,128)(2,1)S(1)} %copy-done.30, bf16[3,16,192,256]{3,2,1,0:T(8,128)(2,1)S(1)} %bitcast.35, bf16[3,16,192,256]{3,2,1,0:T(8,128)(2,1)S(1)} %bitcast.35, bf16[3,16,192,256]{3,2,1,0:T(8,128)(2,1)S(1)} %bitcast.35, f32[16,192,256]{2,1,0:T(8,128)S(1)} %copy-done.22, ...), custom_call_target="tpu_custom_call" | custom-call | flops 805306368 | bytes 12582912 | tf_op jit(solution)/shard_map/write_grad_vel/pallas_call | solution.py:571
  484.6 7.9 %write_grad_vel.4.refs_0_ = f32[3,16,192,256]{3,2,1,0:T(8,128)} custom-call(bf16[256,256]{1,0:T(8,128)(2,1)S(1)} %copy-done.30, bf16[3,16,192,256]{3,2,1,0:T(8,128)(2,1)S(1)} %bitcast.35, bf16[3,16,192,256]{3,2,1,0:T(8,128)(2,1)S(1)} %bitcast.35, bf16[3,16,192,256]{3,2,1,0:T(8,128)(2,1)S(1)} %bitcast.35, ...), custom_call_target="tpu_custom_call", output_to_operand_aliasing={{}: (13, {})} | custom-call | flops 805306368 | bytes 12582912 | tf_op jit(solution)/shard_map/write_grad_vel/pallas_call | solution.py:571
  492.5 7.9 %write_grad_vel.5 = f32[3,16,192,256]{3,2,1,0:T(8,128)} custom-call(bf16[256,256]{1,0:T(8,128)(2,1)S(1)} %copy-done.30, bf16[3,16,192,256]{3,2,1,0:T(8,128)(2,1)S(1)} %bitcast.35, bf16[3,16,192,256]{3,2,1,0:T(8,128)(2,1)S(1)} %bitcast.35, bf16[3,16,192,256]{3,2,1,0:T(8,128)(2,1)S(1)} %bitcast.35, ...), custom_call_target="tpu_custom_call", output_to_operand_aliasing={{}: (13, {})} | custom-call | flops 805306368 | bytes 12582912 | tf_op jit(solution)/shard_map/write_grad_vel/pallas_call | solution.py:571
  (155 shorter events, 84.2 us)
Async XLA Ops:
  0.6 3.7 copy-start.1
  7.2 26.2 %all-to-all-start = ((bf16[8,2,192,256]{3,2,1,0:T(8,128)(2,1)}), bf16[8,2,192,256]{3,2,1,0:T(8,128)(2,1)S(1)}, u32[]{:S(2)}, u32[]{:S(2)}) async-start(bf16[8,2,192,256]{3,2,1,0:T(8,128)(2,1)} %bitcast.2), calls=%async_computation | async-start | bytes 3145728 | tf_op jit(solution)/shard_map/all_to_all | solution.py:628
  12.4 3.7 copy-start.2
  34.5 24.5 %all-to-all-start.2 = ((bf16[8,2,192,256]{3,2,1,0:T(8,128)(2,1)}), bf16[8,2,192,256]{3,2,1,0:T(8,128)(2,1)S(1)}, u32[]{:S(2)}, u32[]{:S(2)}) async-start(bf16[8,2,192,256]{3,2,1,0:T(8,128)(2,1)} %bitcast.4), calls=%async_computation.2 | async-start | bytes 3145728 | tf_op jit(solution)/shard_map/all_to_all | solution.py:628
  38.1 3.7 copy-start.3
  59.1 24.5 %all-to-all-start.6 = ((bf16[8,2,192,256]{3,2,1,0:T(8,128)(2,1)}), bf16[8,2,192,256]{3,2,1,0:T(8,128)(2,1)S(1)}, u32[]{:S(2)}, u32[]{:S(2)}) async-start(bf16[8,2,192,256]{3,2,1,0:T(8,128)(2,1)} %bitcast.12), calls=%async_computation.6 | async-start | bytes 3145728 | tf_op jit(solution)/shard_map/all_to_all | solution.py:628
  84.8 39.0 %all-to-all-start.1 = ((bf16[4,2,2,192,256]{4,3,2,1,0:T(8,128)(2,1)}), bf16[4,2,2,192,256]{4,3,2,1,0:T(8,128)(2,1)S(1)}, u32[]{:S(2)}, u32[]{:S(2)}) async-start(bf16[4,2,2,192,256]{4,3,2,1,0:T(8,128)(2,1)} %bitcast.42), calls=%async_computation.1 | async-start | bytes 3145728 | tf_op jit(solution)/shard_map/all_to_all | solution.py:638
  124.9 40.0 %all-to-all-start.3 = ((bf16[4,2,2,192,256]{4,3,2,1,0:T(8,128)(2,1)}), bf16[4,2,2,192,256]{4,3,2,1,0:T(8,128)(2,1)S(1)}, u32[]{:S(2)}, u32[]{:S(2)}) async-start(bf16[4,2,2,192,256]{4,3,2,1,0:T(8,128)(2,1)} %bitcast.41), calls=%async_computation.3 | async-start | bytes 3145728 | tf_op jit(solution)/shard_map/all_to_all | solution.py:638
  166.0 40.9 %all-to-all-start.7 = ((bf16[4,2,2,192,256]{4,3,2,1,0:T(8,128)(2,1)}), bf16[4,2,2,192,256]{4,3,2,1,0:T(8,128)(2,1)}, u32[]{:S(2)}, u32[]{:S(2)}) async-start(bf16[4,2,2,192,256]{4,3,2,1,0:T(8,128)(2,1)} %bitcast.13), calls=%async_computation.7 | async-start | bytes 3145728 | tf_op jit(solution)/shard_map/all_to_all | solution.py:638
  206.9 40.9 %all-to-all-start.4 = ((bf16[4,2,2,192,256]{4,3,2,1,0:T(8,128)(2,1)}), bf16[4,2,2,192,256]{4,3,2,1,0:T(8,128)(2,1)}, u32[]{:S(2)}, u32[]{:S(2)}) async-start(bf16[4,2,2,192,256]{4,3,2,1,0:T(8,128)(2,1)} %copy-done.25), calls=%async_computation.4 | async-start | bytes 3145728 | tf_op jit(solution)/shard_map/all_to_all | solution.py:645
  212.9 3.3 copy-start.10
  212.9 3.3 copy-start.12
  247.8 40.9 %all-to-all-start.8 = ((bf16[4,2,2,192,256]{4,3,2,1,0:T(8,128)(2,1)}), bf16[4,2,2,192,256]{4,3,2,1,0:T(8,128)(2,1)}, u32[]{:S(2)}, u32[]{:S(2)}) async-start(bf16[4,2,2,192,256]{4,3,2,1,0:T(8,128)(2,1)} %copy-done.23), calls=%async_computation.8 | async-start | bytes 3145728 | tf_op jit(solution)/shard_map/all_to_all | solution.py:645
  288.7 40.0 %all-to-all-start.10 = ((bf16[4,2,2,192,256]{4,3,2,1,0:T(8,128)(2,1)}), bf16[4,2,2,192,256]{4,3,2,1,0:T(8,128)(2,1)S(1)}, u32[]{:S(2)}, u32[]{:S(2)}) async-start(bf16[4,2,2,192,256]{4,3,2,1,0:T(8,128)(2,1)} %copy-done.24), calls=%async_computation.10 | async-start | bytes 3145728 | tf_op jit(solution)/shard_map/all_to_all | solution.py:645
  292.2 2.3 copy-start.42
  329.8 25.9 %all-to-all-start.5 = ((bf16[8,2,192,256]{3,2,1,0:T(8,128)(2,1)}), bf16[8,2,192,256]{3,2,1,0:T(8,128)(2,1)S(1)}, u32[]{:S(2)}, u32[]{:S(2)}) async-start(bf16[8,2,192,256]{3,2,1,0:T(8,128)(2,1)} %y_inverse.3), calls=%async_computation.5 | async-start | bytes 3145728 | tf_op jit(solution)/shard_map/all_to_all | solution.py:651
  355.7 24.5 %all-to-all-start.9 = ((bf16[8,2,192,256]{3,2,1,0:T(8,128)(2,1)}), bf16[8,2,192,256]{3,2,1,0:T(8,128)(2,1)S(1)}, u32[]{:S(2)}, u32[]{:S(2)}) async-start(bf16[8,2,192,256]{3,2,1,0:T(8,128)(2,1)} %copy-done.34), calls=%async_computation.9 | async-start | bytes 3145728 | tf_op jit(solution)/shard_map/all_to_all | solution.py:651
  362.2 2.4 copy-start.6
  364.6 5.7 %copy-start.33 = (bf16[4,2,2,192,256]{4,3,2,1,0:T(8,128)(2,1)S(1)}, bf16[4,2,2,192,256]{4,3,2,1,0:T(8,128)(2,1)}, u32[]{:S(2)}) copy-start(bf16[4,2,2,192,256]{4,3,2,1,0:T(8,128)(2,1)} %copy-done.32) | copy-start | bytes 4718596
  366.4 23.2 %collective-permute-start = (bf16[4,16,192]{2,1,0:T(8,128)(2,1)S(1)}, bf16[4,16,192]{2,1,0:T(8,128)(2,1)S(1)}, u32[]{:S(2)}, u32[]{:S(2)}) collective-permute-start(bf16[4,16,192]{2,1,0:T(8,128)(2,1)S(1)} %pad_maximum_fusion), channel_id=1, source_target_pairs={{0,8},{8,16},{16,24},{24,0},{1,9},{9,17},{17,25},{25,1},{2,10},{10... | collective-permute-start | bytes 73736 | tf_op jit(solution)/shard_map/ppermute | solution.py:365
  366.5 23.1 %collective-permute-start.1 = (bf16[4,16,192]{2,1,0:T(8,128)(2,1)S(1)}, bf16[4,16,192]{2,1,0:T(8,128)(2,1)S(1)}, u32[]{:S(2)}, u32[]{:S(2)}) collective-permute-start(bf16[4,16,192]{2,1,0:T(8,128)(2,1)S(1)} %pad_maximum_fusion.1), channel_id=1, source_target_pairs={{8,0},{16,8},{24,16},{0,24},{9,1},{17,9},{25,17},{1,25},{10,2},{18... | collective-permute-start | bytes 73736 | tf_op jit(solution)/shard_map/ppermute | solution.py:365
  380.3 35.1 %all-to-all-start.11 = ((bf16[8,2,192,256]{3,2,1,0:T(8,128)(2,1)}), bf16[8,2,192,256]{3,2,1,0:T(8,128)(2,1)}, u32[]{:S(2)}, u32[]{:S(2)}) async-start(bf16[8,2,192,256]{3,2,1,0:T(8,128)(2,1)} %copy-done.31), calls=%async_computation.11 | async-start | bytes 3145728 | tf_op jit(solution)/shard_map/all_to_all | solution.py:651
  386.6 19.1 %collective-permute-start.2 = (bf16[4,16,256]{2,1,0:T(8,128)(2,1)S(1)}, bf16[4,16,256]{2,1,0:T(8,128)(2,1)S(1)}, u32[]{:S(2)}, u32[]{:S(2)}) collective-permute-start(bf16[4,16,256]{2,1,0:T(8,128)(2,1)S(1)} %pad_maximum_fusion.2), channel_id=1, source_target_pairs={{0,1},{1,2},{2,3},{3,4},{4,5},{5,6},{6,7},{7,0},{8,9},{9,10},{10,1... | collective-permute-start | bytes 98312 | tf_op jit(solution)/shard_map/ppermute | solution.py:365
  387.1 18.6 %collective-permute-start.3 = (bf16[4,16,256]{2,1,0:T(8,128)(2,1)S(1)}, bf16[4,16,256]{2,1,0:T(8,128)(2,1)S(1)}, u32[]{:S(2)}, u32[]{:S(2)}) collective-permute-start(bf16[4,16,256]{2,1,0:T(8,128)(2,1)S(1)} %pad_maximum_fusion.3), channel_id=1, source_target_pairs={{1,0},{2,1},{3,2},{4,3},{5,4},{6,5},{7,6},{0,7},{9,8},{10,9},{11,1... | collective-permute-start | bytes 98312 | tf_op jit(solution)/shard_map/ppermute | solution.py:365
  405.8 3.7 copy-start.4
  412.4 16.1 %slice-start.2 = ((s8[4718592]{0:T(1024)(128)(4,1)}), s8[524288]{0:T(1024)(128)(4,1)S(1)}, s32[]{:S(2)}) async-start(s8[4718592]{0:T(1024)(128)(4,1)} %bitcast.36), calls=%async_computation.14 | async-start | bytes 1048576
  415.4 3.7 copy-start.5
  419.0 9.5 %slice-start.3 = ((s8[4718592]{0:T(1024)(128)(4,1)}), s8[4194304]{0:T(1024)(128)(4,1)S(1)}, s32[]{:S(2)}) async-start(s8[4718592]{0:T(1024)(128)(4,1)} %bitcast.36), calls=%async_computation.15 | async-start | bytes 8388608
  419.0 9.5 %copy-start.30 = (bf16[256,256]{1,0:T(8,128)(2,1)S(1)}, bf16[256,256]{1,0:T(8,128)(2,1)}, u32[]{:S(2)}) copy-start(bf16[256,256]{1,0:T(8,128)(2,1)} %constant.37.clone.refs_0_.slope_x) | copy-start | bytes 393220
  419.0 9.5 %copy-start.41 = (bf16[192,192]{1,0:T(8,128)(2,1)S(1)}, bf16[192,192]{1,0:T(8,128)(2,1)}, u32[]{:S(2)}) copy-start(bf16[192,192]{1,0:T(8,128)(2,1)} %constant.38.clone.refs_1_) | copy-start | bytes 221188
  421.9 15.6 %copy-start.21 = (f32[16,192,256]{2,1,0:T(8,128)}, f32[16,192,256]{2,1,0:T(8,128)S(1)}, u32[]{:S(2)}) copy-start(f32[16,192,256]{2,1,0:T(8,128)S(1)} %get-tuple-element.27.refs_3_.adjoint) | copy-start | bytes 9437188
  421.9 70.6 %collective-permute-start.4 = (bf16[16,192]{1,0:T(8,128)(2,1)S(1)}, bf16[16,192]{1,0:T(8,128)(2,1)S(1)}, u32[]{:S(2)}, u32[]{:S(2)}) collective-permute-start(bf16[16,192]{1,0:T(8,128)(2,1)S(1)} %get-tuple-element.28), channel_id=1, source_target_pairs={{0,8},{8,16},{16,24},{24,0},{1,9},{9,17},{17,25},{25,1},{2,10},{10... | collective-permute-start | bytes 18440 | tf_op jit(solution)/shard_map/ppermute | solution.py:365
  422.0 45.4 %collective-permute-start.12 = (bf16[16,192]{1,0:T(8,128)(2,1)S(1)}, bf16[16,192]{1,0:T(8,128)(2,1)S(1)}, u32[]{:S(2)}, u32[]{:S(2)}) collective-permute-start(bf16[16,192]{1,0:T(8,128)(2,1)S(1)} %get-tuple-element.36), channel_id=1, source_target_pairs={{0,8},{8,16},{16,24},{24,0},{1,9},{9,17},{17,25},{25,1},{2,10},{10... | collective-permute-start | bytes 18440 | tf_op jit(solution)/shard_map/ppermute | solution.py:365
  422.2 45.3 %collective-permute-start.13 = (bf16[16,192]{1,0:T(8,128)(2,1)S(1)}, bf16[16,192]{1,0:T(8,128)(2,1)S(1)}, u32[]{:S(2)}, u32[]{:S(2)}) collective-permute-start(bf16[16,192]{1,0:T(8,128)(2,1)S(1)} %get-tuple-element.37), channel_id=1, source_target_pairs={{8,0},{16,8},{24,16},{0,24},{9,1},{17,9},{25,17},{1,25},{10,2},{18... | collective-permute-start | bytes 18440 | tf_op jit(solution)/shard_map/ppermute | solution.py:365
  425.8 45.4 %collective-permute-start.14 = (bf16[16,256]{1,0:T(8,128)(2,1)S(1)}, bf16[16,256]{1,0:T(8,128)(2,1)S(1)}, u32[]{:S(2)}, u32[]{:S(2)}) collective-permute-start(bf16[16,256]{1,0:T(8,128)(2,1)S(1)} %get-tuple-element.38), channel_id=1, source_target_pairs={{0,1},{1,2},{2,3},{3,4},{4,5},{5,6},{6,7},{7,0},{8,9},{9,10},{10,1... | collective-permute-start | bytes 24584 | tf_op jit(solution)/shard_map/ppermute | solution.py:365
  425.9 45.4 %collective-permute-start.15 = (bf16[16,256]{1,0:T(8,128)(2,1)S(1)}, bf16[16,256]{1,0:T(8,128)(2,1)S(1)}, u32[]{:S(2)}, u32[]{:S(2)}) collective-permute-start(bf16[16,256]{1,0:T(8,128)(2,1)S(1)} %get-tuple-element.39), channel_id=1, source_target_pairs={{1,0},{2,1},{3,2},{4,3},{5,4},{6,5},{7,6},{0,7},{9,8},{10,9},{11,1... | collective-permute-start | bytes 24584 | tf_op jit(solution)/shard_map/ppermute | solution.py:365
  428.5 9.0 %copy-start.20 = (f32[16,192,256]{2,1,0:T(8,128)S(1)}, f32[16,192,256]{2,1,0:T(8,128)}, u32[]{:S(2)}) copy-start(f32[16,192,256]{2,1,0:T(8,128)} %copy-done.19) | copy-start | bytes 9437188
  437.5 14.3 %copy-start.18 = (f32[16,192,256]{2,1,0:T(8,128)S(1)}, f32[16,192,256]{2,1,0:T(8,128)}, u32[]{:S(2)}) copy-start(f32[16,192,256]{2,1,0:T(8,128)} %copy-done.17) | copy-start | bytes 9437188
  451.8 22.1 %slice-start = ((s8[4718592]{0:T(1024)(128)(4,1)}), s8[4194304]{0:T(1024)(128)(4,1)S(1)}, s32[]{:S(2)}) async-start(s8[4718592]{0:T(1024)(128)(4,1)} %bitcast.34), calls=%async_computation.12 | async-start | bytes 8388608
  451.8 22.1 %slice-start.1 = ((s8[4718592]{0:T(1024)(128)(4,1)}), s8[524288]{0:T(1024)(128)(4,1)S(1)}, s32[]{:S(2)}) async-start(s8[4718592]{0:T(1024)(128)(4,1)} %bitcast.34), calls=%async_computation.13 | async-start | bytes 1048576
  451.8 22.1 %copy-start.22 = (f32[16,192,256]{2,1,0:T(8,128)S(1)}, f32[16,192,256]{2,1,0:T(8,128)}, u32[]{:S(2)}) copy-start(f32[16,192,256]{2,1,0:T(8,128)} %copy-done.21) | copy-start | bytes 9437188
  467.4 14.4 %collective-permute-start.8 = (bf16[16,192]{1,0:T(8,128)(2,1)S(1)}, bf16[16,192]{1,0:T(8,128)(2,1)S(1)}, u32[]{:S(2)}, u32[]{:S(2)}) collective-permute-start(bf16[16,192]{1,0:T(8,128)(2,1)S(1)} %get-tuple-element.32), channel_id=1, source_target_pairs={{0,8},{8,16},{16,24},{24,0},{1,9},{9,17},{17,25},{25,1},{2,10},{10... | collective-permute-start | bytes 18440 | tf_op jit(solution)/shard_map/ppermute | solution.py:365
  467.4 14.5 %collective-permute-start.9 = (bf16[16,192]{1,0:T(8,128)(2,1)S(1)}, bf16[16,192]{1,0:T(8,128)(2,1)S(1)}, u32[]{:S(2)}, u32[]{:S(2)}) collective-permute-start(bf16[16,192]{1,0:T(8,128)(2,1)S(1)} %get-tuple-element.33), channel_id=1, source_target_pairs={{8,0},{16,8},{24,16},{0,24},{9,1},{17,9},{25,17},{1,25},{10,2},{18... | collective-permute-start | bytes 18440 | tf_op jit(solution)/shard_map/ppermute | solution.py:365
  471.3 10.7 %collective-permute-start.10 = (bf16[16,256]{1,0:T(8,128)(2,1)S(1)}, bf16[16,256]{1,0:T(8,128)(2,1)S(1)}, u32[]{:S(2)}, u32[]{:S(2)}) collective-permute-start(bf16[16,256]{1,0:T(8,128)(2,1)S(1)} %get-tuple-element.34), channel_id=1, source_target_pairs={{0,1},{1,2},{2,3},{3,4},{4,5},{5,6},{6,7},{7,0},{8,9},{9,10},{10,1... | collective-permute-start | bytes 24584 | tf_op jit(solution)/shard_map/ppermute | solution.py:365
  471.3 13.3 %collective-permute-start.11 = (bf16[16,256]{1,0:T(8,128)(2,1)S(1)}, bf16[16,256]{1,0:T(8,128)(2,1)S(1)}, u32[]{:S(2)}, u32[]{:S(2)}) collective-permute-start(bf16[16,256]{1,0:T(8,128)(2,1)S(1)} %get-tuple-element.35), channel_id=1, source_target_pairs={{1,0},{2,1},{3,2},{4,3},{5,4},{6,5},{7,6},{0,7},{9,8},{10,9},{11,1... | collective-permute-start | bytes 24584 | tf_op jit(solution)/shard_map/ppermute | solution.py:365
  481.8 10.7 %collective-permute-start.5 = (bf16[16,192]{1,0:T(8,128)(2,1)S(1)}, bf16[16,192]{1,0:T(8,128)(2,1)S(1)}, u32[]{:S(2)}, u32[]{:S(2)}) collective-permute-start(bf16[16,192]{1,0:T(8,128)(2,1)S(1)} %get-tuple-element.29), channel_id=1, source_target_pairs={{8,0},{16,8},{24,16},{0,24},{9,1},{17,9},{25,17},{1,25},{10,2},{18... | collective-permute-start | bytes 18440 | tf_op jit(solution)/shard_map/ppermute | solution.py:365
  482.0 10.5 %collective-permute-start.6 = (bf16[16,256]{1,0:T(8,128)(2,1)S(1)}, bf16[16,256]{1,0:T(8,128)(2,1)S(1)}, u32[]{:S(2)}, u32[]{:S(2)}) collective-permute-start(bf16[16,256]{1,0:T(8,128)(2,1)S(1)} %get-tuple-element.30), channel_id=1, source_target_pairs={{0,1},{1,2},{2,3},{3,4},{4,5},{5,6},{6,7},{7,0},{8,9},{9,10},{10,1... | collective-permute-start | bytes 24584 | tf_op jit(solution)/shard_map/ppermute | solution.py:365
  482.0 10.5 %collective-permute-start.7 = (bf16[16,256]{1,0:T(8,128)(2,1)S(1)}, bf16[16,256]{1,0:T(8,128)(2,1)S(1)}, u32[]{:S(2)}, u32[]{:S(2)}) collective-permute-start(bf16[16,256]{1,0:T(8,128)(2,1)S(1)} %get-tuple-element.31), channel_id=1, source_target_pairs={{1,0},{2,1},{3,2},{4,3},{5,4},{6,5},{7,6},{0,7},{9,8},{10,9},{11,1... | collective-permute-start | bytes 24584 | tf_op jit(solution)/shard_map/ppermute | solution.py:365
  (32 other events, 51.7 us)

commit v2 on v1

--- a/solution.py
+++ b/solution.py
@@ -25,7 +25,7 @@
 BACK_ORDER = (2, 0, 1)
 
 
-def params(megabytes=40, **extra):
+def params(megabytes=56, **extra):
     return pltpu.CompilerParams(vmem_limit_bytes=megabytes * 1024 * 1024, **extra)
 
 
@@ -145,87 +145,110 @@
     )(values)
 
 
-def y_forward_kernel(table_ref, columns_ref, modes_ref):
-    planes = columns_ref.shape[1]
-    width = columns_ref.shape[3]
-    for plane in range(planes):
-        column = columns_ref[:, plane].reshape(Y, width)
-        modes = jnp.dot(table_ref[...], column, preferred_element_type=f32)
-        modes_ref[0, :, plane] = modes.astype(bf16).reshape(modes_ref.shape[1:2] + modes_ref.shape[3:])
-
-
-def y_transform(table, columns, blocks, halves):
+def y_transform(me, table, columns, blocks, halves):
     _, planes, _, width = columns.shape
     modes = HALF_Y // (blocks * halves)
     rows = Y // blocks
-    return pl.pallas_call(
-        y_forward_kernel,
-        grid=(blocks,),
-        in_specs=[
-            pl.BlockSpec((rows, Y), lambda j: (j, 0)),
-            pl.BlockSpec(columns.shape, lambda j: (0, 0, 0, 0)),
-        ],
-        out_specs=pl.BlockSpec((1, halves, planes, 2, modes, width), lambda j: (j, 0, 0, 0, 0, 0)),
-        out_shape=jax.ShapeDtypeStruct((blocks, halves, planes, 2, modes, width), bf16),
+    shape = (halves, planes, 2, modes, width)
+
+    def kernel(me_ref, table_ref, columns_ref, *outs):
+        shift = pl.program_id(0)
+        for plane in range(planes):
+            column = columns_ref[:, plane].reshape(Y, width)
+            part = jnp.dot(table_ref[...], column, preferred_element_type=f32).astype(bf16)
+            part = part.reshape(halves, 2, modes, width)
+            for s, out in enumerate(outs):
+
+                @pl.when(shift == s)
+                def _(out=out, part=part, plane=plane):
+                    out[:, plane] = part
+
+    return pl.pallas_call(
+        kernel,
+        grid_spec=pltpu.PrefetchScalarGridSpec(
+            num_scalar_prefetch=1,
+            grid=(blocks,),
+            in_specs=[
+                pl.BlockSpec((rows, Y), lambda j, me: (lax.rem(me[0] + j, blocks), 0)),
+                pl.BlockSpec(columns.shape, lambda j, me: (0, 0, 0, 0)),
+            ],
+            out_specs=[pl.BlockSpec(shape, lambda j, me: (0, 0, 0, 0, 0))] * blocks,
+        ),
+        out_shape=[jax.ShapeDtypeStruct(shape, bf16)] * blocks,
         compiler_params=params(),
         cost_estimate=cost(2 * planes * Y * Y * width, 2 * Y * Y + 4 * planes * Y * width),
         name="y_transform",
-    )(table, columns)
-
-
-def y_inverse_kernel(table_ref, modes_ref, rows_ref):
-    planes = modes_ref.shape[2]
-    width = modes_ref.shape[5]
-    count, _, height, _ = rows_ref.shape
-    for plane in range(planes):
-        modes = modes_ref[:, :, plane].reshape(Y, width)
-        rows = jnp.dot(table_ref[...], modes, preferred_element_type=f32)
-        rows_ref[:, plane] = rows.astype(bf16).reshape(count, height, width)
-
-
-def y_inverse(table, modes, size_y):
-    planes, width = modes.shape[2], modes.shape[5]
+    )(me, table, columns)
+
+
+def y_inverse(me, table, modes, size_y):
+    blocks = len(modes)
+    halves, planes, _, _, width = modes[0].shape
     height = Y // size_y
     count = max(1, 384 // height)
-    return pl.pallas_call(
-        y_inverse_kernel,
+    rows = Y // blocks
+
+    def kernel(me_ref, table_ref, *refs):
+        parts, rows_ref, held = refs[:blocks], refs[blocks], refs[blocks + 1]
+
+        @pl.when(pl.program_id(0) == 0)
+        def _():
+            for s, part in enumerate(parts):
+                source = lax.rem(me_ref[0] + blocks - s, blocks)
+                place = pl.ds(pl.multiple_of(source * rows, rows), rows)
+                for plane in range(planes):
+                    held[plane, place, :] = part[:, plane].reshape(rows, width)
+
+        for plane in range(planes):
+            out = jnp.dot(table_ref[...], held[plane], preferred_element_type=f32)
+            rows_ref[:, plane] = out.astype(bf16).reshape(count, height, width)
+
+    return pl.pallas_call(
+        kernel,
         grid=(size_y // count,),
         in_specs=[
+            pl.BlockSpec(memory_space=pltpu.SMEM),
             pl.BlockSpec((count * height, Y), lambda j: (j, 0)),
-            pl.BlockSpec(modes.shape, lambda j: (0, 0, 0, 0, 0, 0)),
-        ],
+        ]
+        + [pl.BlockSpec(modes[0].shape, lambda j: (0, 0, 0, 0, 0))] * blocks,
         out_specs=pl.BlockSpec((count, planes, height, width), lambda j: (j, 0, 0, 0)),
         out_shape=jax.ShapeDtypeStruct((size_y, planes, height, width), bf16),
+        scratch_shapes=[pltpu.VMEM((planes, Y, width), bf16)],
         compiler_params=params(),
         cost_estimate=cost(2 * planes * Y * Y * width, 2 * Y * Y + 4 * planes * Y * width),
         name="y_inverse",
-    )(table, modes)
-
-
-def x_forward_kernel(table_ref, modes_ref, spectrum_ref):
-    blocks, _, _, modes, width = modes_ref.shape
-    rows = jnp.concatenate(
-        [modes_ref[block, 0].reshape(2 * modes, width) for block in range(blocks)], axis=1
-    )
-    spectrum = jnp.dot(rows, table_ref[...], preferred_element_type=f32)
-    spectrum_ref[0] = spectrum.reshape(2, modes, X)
-
-
-def x_transform(table, modes):
-    blocks, _, _, count, width = modes.shape
-    return pl.pallas_call(
-        x_forward_kernel,
+    )(me, table, *modes)
+
+
+def x_transform(me, table, modes, after):
+    blocks = len(modes)
+    _, _, count, width = modes[0].shape
+
+    def kernel(me_ref, table_ref, *refs):
+        parts, spectrum_ref, held = refs[:blocks], refs[-2], refs[-1]
+        for s, part in enumerate(parts):
+            source = lax.rem(me_ref[0] + blocks - s, blocks)
+            place = pl.ds(pl.multiple_of(source * width, width), width)
+            held[:, place] = part[0].reshape(2 * count, width)
+        spectrum = jnp.dot(held[...], table_ref[...], preferred_element_type=f32)
+        spectrum_ref[0] = spectrum.reshape(2, count, X)
+
+    return pl.pallas_call(
+        kernel,
         grid=(2,),
         in_specs=[
+            pl.BlockSpec(memory_space=pltpu.SMEM),
             pl.BlockSpec((X, X), lambda j: (0, 0)),
-            pl.BlockSpec((blocks, 1, 2, count, width), lambda j: (0, j, 0, 0, 0)),
-        ],
+        ]
+        + [pl.BlockSpec((1, 2, count, width), lambda j: (j, 0, 0, 0))] * blocks
+        + [pl.BlockSpec(memory_space=pl.ANY)] * len(after),
         out_specs=pl.BlockSpec((1, 2, count, X), lambda j: (j, 0, 0, 0)),
         out_shape=jax.ShapeDtypeStruct((2, 2, count, X), f32),
+        scratch_shapes=[pltpu.VMEM((2 * count, X), bf16)],
         compiler_params=params(),
         cost_estimate=cost(8 * count * X * X, 2 * X * X + 24 * count * X),
         name="x_transform",
-    )(table, modes)
+    )(me, table, *modes, *after)
 
 
 def turned(field, axis, tz, ty, tx, wave):
@@ -243,8 +266,9 @@
 }
 
 
-def curl_kernel(axes, where_ref, table_ref, plus_ref, minus_ref, back_ref):
-    blocks, _, _, count, width = back_ref.shape
+def curl_kernel(axes, where_ref, table_ref, plus_ref, minus_ref, *outs):
+    blocks = len(outs)
+    _, _, count, width = outs[0].shape
     base = where_ref[0] + pl.program_id(0) * count
     depth = where_ref[1]
     mode_y = lax.broadcasted_iota(jnp.int32, (count, HALF_X), 0) + base
@@ -273,9 +297,11 @@
                 )
             rows.append(jnp.concatenate(parts, axis=1))
     rows = jnp.concatenate(rows, axis=0)
-    back = jnp.dot(rows, table_ref[...], preferred_element_type=f32).astype(bf16)
-    for block in range(blocks):
-        back_ref[block] = back[:, block * width : (block + 1) * width].reshape(2, 2, count, width)
+    for s, out in enumerate(outs):
+        target = lax.rem(where_ref[2] + s, blocks)
+        place = pl.ds(pl.multiple_of(target * width, width), width)
+        back = jnp.dot(rows, table_ref[:, place], preferred_element_type=f32)
+        out[...] = back.astype(bf16).reshape(2, 2, count, width)
 
 
 def curl_inverse(where, table, spectra, component, blocks):
@@ -297,8 +323,8 @@
             spec,
             spec,
         ],
-        out_specs=pl.BlockSpec((blocks, 2, 2, count, width), lambda j: (0, 0, 0, j, 0)),
-        out_shape=jax.ShapeDtypeStruct((blocks, 2, 2, total, width), bf16),
+        out_specs=[pl.BlockSpec((2, 2, count, width), lambda j: (0, 0, j, 0))] * blocks,
+        out_shape=[jax.ShapeDtypeStruct((2, 2, total, width), bf16)] * blocks,
         compiler_params=params(),
         cost_estimate=cost(8 * total * X * X, 2 * X * X + 40 * total * X),
         name="curl_inverse",
@@ -322,16 +348,20 @@
     return total[:Z].astype(bf16), total[Z:].astype(bf16)
 
 
-def spread_columns(low, high, n, width):
-    row = lax.broadcasted_iota(jnp.int32, (2 * Z, width), 0)
-    lane = lax.broadcasted_iota(jnp.int32, (2 * Z, width), 1)
-    place = jnp.where((row == n) & (lane == 0), -0.5, 0.0) + jnp.where(
-        (row == n + Z) & (lane == width - 1), 0.5, 0.0
-    )
+def spread_columns(low, high, first, layers, width):
+    row = lax.broadcasted_iota(jnp.int32, (2 * Z, layers * width), 0)
+    column = lax.broadcasted_iota(jnp.int32, (2 * Z, layers * width), 1)
+    place = jnp.zeros((2 * Z, layers * width), f32)
+    for n in range(layers):
+        place = place + jnp.where((row == first + n) & (column == n * width), -0.5, 0.0)
+        place = place + jnp.where(
+            (row == first + n + Z) & (column == (n + 1) * width - 1), 0.5, 0.0
+        )
     both = jnp.concatenate([low, high], axis=0).astype(bf16)
-    return lax.dot_general(
+    spread = lax.dot_general(
         both, place.astype(bf16), (((0,), (0,)), ((), ())), preferred_element_type=f32
     )
+    return [spread[:, n * width : (n + 1) * width] for n in range(layers)]
 
 
 def edges_kernel(field_ref, first_column_ref, last_column_ref):
@@ -365,7 +395,8 @@
     return lax.ppermute(last, axis, up), lax.ppermute(first, axis, down)
 
 
-def adjoint_kernel(planes_ref, cotangent_ref, adjoint_ref, first_x, last_x, first_y, last_y):
+def adjoint_kernel(planes_ref, cotangent_ref, *refs):
+    adjoint_ref, first_x, last_x, first_y, last_y = refs[-5:]
     height = planes_ref.shape[1]
     scale = 1.0 / (X * Y * Z)
     rows = 16
@@ -386,7 +417,7 @@
     ).astype(bf16)
 
 
-def make_adjoint(planes, cotangent, component):
+def make_adjoint(planes, cotangent, component, after):
     _, height, width = planes.shape
     column = jax.ShapeDtypeStruct((Z, height), bf16)
     row = jax.ShapeDtypeStruct((Z, width), bf16)
@@ -398,7 +429,8 @@
         in_specs=[
             pl.BlockSpec((Z, height, width), lambda j: (0, 0, 0)),
             pl.BlockSpec((1, Z, height, width), lambda j: (component, 0, 0, 0)),
-        ],
+        ]
+        + [pl.BlockSpec(memory_space=pl.ANY)] * len(after),
         out_specs=[
             pl.BlockSpec((Z, height, width), lambda j: (0, 0, 0)),
             column_spec,
@@ -416,7 +448,7 @@
         compiler_params=params(),
         cost_estimate=cost(70 * Z * height * width, 10 * Z * height * width),
         name="make_adjoint",
-    )(planes, cotangent)
+    )(planes, cotangent, *after)
 
 
 def pick_row(rows, n):
@@ -427,6 +459,9 @@
 def end_rows(low, high, height):
     row = lax.broadcasted_iota(jnp.int32, (height, low.shape[1]), 0)
     return jnp.where(row == 0, low * -0.5, 0.0) + jnp.where(row == height - 1, high * 0.5, 0.0)
+
+
+LAYERS = 4
 
 
 def grad_vort_kernel(
@@ -434,26 +469,28 @@
 ):
     before, after = refs if len(refs) == 2 else (None, refs[0])
     height, width = velocity.shape[2], velocity.shape[3]
-    n = pl.program_id(0)
-    above = lax.rem(n + 1, Z)
-    below = lax.rem(n + Z - 1, Z)
-    here = velocity[0, n]
-    value = adjoint[0]
-    half = value * step_size
-    along_x = jnp.dot(here, slope_x[...], preferred_element_type=f32)
-    along_x = along_x + spread_columns(low_x[0], high_x[0], n, width)
-    along_y = jnp.dot(slope_y[...], here, preferred_element_type=f32)
-    along_y = along_y + end_rows(
-        pick_row(low_y[0], n), pick_row(high_y[0], n), height
-    )
-    along_z = (velocity[0, above].astype(f32) - velocity[0, below].astype(f32)) * 0.5
-    for j, slope in enumerate((along_x, along_y, along_z)):
-        term = half * slope
-        if j == component:
-            term = term + value
-        if before is not None:
-            term = before[j, 0] + term
-        after[j, 0] = term
+    first = pl.program_id(0) * LAYERS
+    ends = spread_columns(low_x[0], high_x[0], first, LAYERS, width)
+    layers = velocity[0, pl.ds(first, LAYERS)]
+    stacked = layers.reshape(LAYERS * height, width)
+    inner = jnp.dot(stacked, slope_x[...], preferred_element_type=f32)
+    for k in range(LAYERS):
+        n = first + k
+        above = lax.rem(n + 1, Z)
+        below = lax.rem(n + Z - 1, Z)
+        value = adjoint[k]
+        half = value * step_size
+        along_x = inner[k * height : (k + 1) * height] + ends[k]
+        along_y = jnp.dot(slope_y[...], layers[k], preferred_element_type=f32)
+        along_y = along_y + end_rows(pick_row(low_y[0], n), pick_row(high_y[0], n), height)
+        along_z = (velocity[0, above].astype(f32) - velocity[0, below].astype(f32)) * 0.5
+        for j, slope in enumerate((along_x, along_y, along_z)):
+            term = half * slope
+            if j == component:
+                term = term + value
+            if before is not None:
+                term = before[j, k] + term
+            after[j, k] = term
 
 
 def add_grad_vort(component, slopes, velocity, adjoint, halos, before):
@@ -462,13 +499,13 @@
     whole = lambda shape: pl.BlockSpec(shape, lambda n: (0,) * len(shape))
     column = pl.BlockSpec((1, Z, height), lambda n: (component, 0, 0))
     row = pl.BlockSpec((1, Z, width), lambda n: (component, 0, 0))
-    sums = pl.BlockSpec((3, 1, height, width), lambda n: (0, n, 0, 0))
+    sums = pl.BlockSpec((3, LAYERS, height, width), lambda n: (0, n, 0, 0))
     operands = [slope_x, slope_y, velocity, adjoint, *halos]
     in_specs = [
         whole((width, width)),
         whole((height, height)),
         pl.BlockSpec((1, Z, height, width), lambda n: (component, 0, 0, 0)),
-        pl.BlockSpec((1, height, width), lambda n: (n, 0, 0)),
+        pl.BlockSpec((LAYERS, height, width), lambda n: (n, 0, 0)),
         column,
         column,
         row,
@@ -485,7 +522,7 @@
 
     return pl.pallas_call(
         kernel,
-        grid=(Z,),
+        grid=(Z // LAYERS,),
         in_specs=in_specs,
         out_specs=sums,
         out_shape=jax.ShapeDtypeStruct((3, Z, height, width), f32),
@@ -498,48 +535,43 @@
     )(*operands)
 
 
-def grad_vel_kernel(
-    slope_x,
-    vorticity,
-    vorticity_above,
-    vorticity_below,
-    adjoint,
-    vort_low_x,
-    vort_high_x,
-    vort_low_y,
-    vort_high_y,
-    low_x,
-    high_x,
-    low_y,
-    high_y,
-    *refs,
-):
+def grad_vel_kernel(slope_x, vorticity, vorticity_above, vorticity_below, adjoint, *refs):
+    vort_low_x, vort_high_x, vort_low_y, vort_high_y, low_x, high_x, low_y, high_y = refs[:8]
     after, padded = refs[-2:]
     _, _, height, width = vorticity.shape
-    n = pl.program_id(0)
-    above = lax.rem(n + 1, Z)
-    below = lax.rem(n + Z - 1, Z)
-    value = adjoint[n]
-
-    product = vorticity[0, 0].astype(f32) * value
+    first = pl.program_id(0) * LAYERS
+
+    def times(one, other):
+        return one.astype(f32) * other.astype(f32)
+
+    ends = spread_columns(
+        times(vort_low_x[...], low_x[...]),
+        times(vort_high_x[...], high_x[...]),
+        first,
+        LAYERS,
+        width,
+    )
+    values = adjoint[pl.ds(first, LAYERS)]
+    product = (vorticity[0].astype(f32) * values).reshape(LAYERS * height, width)
     coarse = product.astype(bf16)
     fine = (product - coarse.astype(f32)).astype(bf16)
-    total = jnp.dot(coarse, slope_x[...], preferred_element_type=f32)
-    total = total + jnp.dot(fine, slope_x[...], preferred_element_type=f32)
-    low = vort_low_x[...].astype(f32) * low_x[...].astype(f32)
-    high = vort_high_x[...].astype(f32) * high_x[...].astype(f32)
-    total = total + spread_columns(low, high, n, width)
-
-    padded[8 : 8 + height, :] = vorticity[1, 0].astype(f32) * value
-    padded[7:8, :] = pick_row(vort_low_y[...], n) * pick_row(low_y[...], n)
-    padded[8 + height : 9 + height, :] = pick_row(vort_high_y[...], n) * pick_row(high_y[...], n)
-    total = total + (padded[9 : 9 + height, :] - padded[7 : 7 + height, :]) * 0.5
-
-    total = total + (
-        vorticity_above[0, 0].astype(f32) * adjoint[above]
-        - vorticity_below[0, 0].astype(f32) * adjoint[below]
-    ) * 0.5
-    after[0, 0] = total * -step_size
+    inner = jnp.dot(coarse, slope_x[...], preferred_element_type=f32)
+    inner = inner + jnp.dot(fine, slope_x[...], preferred_element_type=f32)
+    up = adjoint[lax.rem(first + LAYERS, Z)] * vorticity_above[0, 0].astype(f32)
+    down = adjoint[lax.rem(first + Z - 1, Z)] * vorticity_below[0, 0].astype(f32)
+    deep = [down] + [vorticity[2, k].astype(f32) * values[k] for k in range(LAYERS)] + [up]
+    for k in range(LAYERS):
+        n = first + k
+        padded[k, 8 : 8 + height, :] = vorticity[1, k].astype(f32) * values[k]
+        padded[k, 7:8, :] = pick_row(vort_low_y[...], n) * pick_row(low_y[...], n)
+        padded[k, 8 + height : 9 + height, :] = pick_row(vort_high_y[...], n) * pick_row(
+            high_y[...], n
+        )
+        total = (padded[k, 9 : 9 + height, :] - padded[k, 7 : 7 + height, :]) + (
+            deep[k + 2] - deep[k]
+        )
+        total = total * 0.5 + inner[k * height : (k + 1) * height] + ends[k]
+        after[0, k] = total * -step_size
 
 
 def write_grad_vel(component, slope_x, vorticity, adjoint, vort_halos, halos, before):
@@ -550,9 +582,9 @@
     operands = [slope_x, vorticity, vorticity, vorticity, adjoint, *vort_halos, *halos]
     in_specs = [
         whole((width, width)),
-        pl.BlockSpec((2, 1, height, width), lambda n: (0, n, 0, 0)),
-        pl.BlockSpec((1, 1, height, width), lambda n: (2, lax.rem(n + 1, Z), 0, 0)),
-        pl.BlockSpec((1, 1, height, width), lambda n: (2, lax.rem(n + Z - 1, Z), 0, 0)),
+        pl.BlockSpec((3, LAYERS, height, width), lambda n: (0, n, 0, 0)),
+        pl.BlockSpec((1, 1, height, width), lambda n: (2, lax.rem((n + 1) * LAYERS, Z), 0, 0)),
+        pl.BlockSpec((1, 1, height, width), lambda n: (2, lax.rem(n * LAYERS + Z - 1, Z), 0, 0)),
         whole((Z, height, width)),
         column,
         column,
@@ -570,12 +602,12 @@
         in_specs.append(pl.BlockSpec(memory_space=pl.ANY))
     return pl.pallas_call(
         grad_vel_kernel,
-        grid=(Z,),
+        grid=(Z // LAYERS,),
         in_specs=in_specs,
-        out_specs=pl.BlockSpec((1, 1, height, width), lambda n: (component, n, 0, 0)),
+        out_specs=pl.BlockSpec((1, LAYERS, height, width), lambda n: (component, n, 0, 0)),
         out_shape=jax.ShapeDtypeStruct((3, Z, height, width), f32),
         input_output_aliases=aliases,
-        scratch_shapes=[pltpu.VMEM((height + 16, width), f32)],
+        scratch_shapes=[pltpu.VMEM((LAYERS, height + 16, width), f32)],
         compiler_params=params(),
         cost_estimate=cost(4 * Z * height * width * width, Z * height * width * 16),
         name="write_grad_vel",
@@ -584,10 +616,18 @@
 
 def pair_exchange(parts, axis, mine):
     count = lax.axis_size(axis)
-    kept = lax.dynamic_index_in_dim(parts, mine, 1, keepdims=False)
-    sent = lax.dynamic_index_in_dim(parts, 1 - mine, 1, keepdims=False)
+    kept = lax.dynamic_index_in_dim(parts, mine, 0, keepdims=False)
+    sent = lax.dynamic_index_in_dim(parts, 1 - mine, 0, keepdims=False)
     got = lax.ppermute(sent, axis, [(i, i ^ 1) for i in range(count)])
-    return jnp.where(mine == 0, jnp.stack([kept, got], 1), jnp.stack([got, kept], 1))
+    return jnp.where(mine == 0, jnp.stack([kept, got]), jnp.stack([got, kept]))
+
+
+def shifted(parts, axis):
+    count = lax.axis_size(axis)
+    return [parts[0]] + [
+        lax.ppermute(parts[s], axis, [(i, (i + s) % count) for i in range(count)])
+        for s in range(1, count)
+    ]
 
 
 def local(cot_vort, cot_vel, vorticity, velocity):
@@ -600,7 +640,10 @@
     place_x = lax.axis_index("gx")
     place_y = lax.axis_index("gy")
     half = lax.rem(place_y, halves)
-    where = jnp.stack([(place_x * halves + half) * modes, place_y // halves]).astype(jnp.int32)
+    me = place_x.astype(jnp.int32).reshape(1)
+    where = jnp.stack(
+        [(place_x * halves + half) * modes, place_y // halves, place_x]
+    ).astype(jnp.int32)
 
     y_table, y_back_table = y_tables(size_x * halves)
     x_table, x_back_table = x_tables()
@@ -628,29 +671,32 @@
         columns = lax.all_to_all(
             layers.reshape(size_y, planes, height, width), "gy", 0, 0, tiled=True
         )
-        coefficients = y_transform(y_table, columns, size_x, halves)
+        parts = y_transform(me, y_table, columns, size_x, halves)
         if halves == 1:
-            coefficients = coefficients.reshape(size_x, 2, 2, modes, width)
+            parts = [part[0] for part in parts]
         else:
-            coefficients = pair_exchange(
-                coefficients.reshape(size_x, 2, 2, modes, width), "gy", half
-            )
-        lines = lax.all_to_all(coefficients, "gx", 0, 0, tiled=True)
-        spectra[component] = x_transform(x_table, lines)
+            parts = [pair_exchange(part[:, 0], "gy", half) for part in parts]
+        first = component == FORWARD_ORDER[0]
+        spectra[component] = x_transform(
+            me, x_table, shifted(parts, "gx"), velocity_halos if first else ()
+        )
 
     grad_vort = None
     grad_vel = None
     for component in BACK_ORDER:
-        filtered = curl_inverse(where, x_back_table, spectra, component, size_x)
-        returned = lax.all_to_all(filtered, "gx", 0, 0, tiled=True)
+        parts = curl_inverse(where, x_back_table, spectra, component, size_x)
+        parts = shifted(parts, "gx")
         if halves == 1:
-            returned = returned.reshape(size_x, 1, 2, 2, modes, width)
+            parts = [part[None] for part in parts]
         else:
-            returned = pair_exchange(returned, "gy", half)[:, :, None]
-        rows = y_inverse(y_back_table, returned, size_y)
+            parts = [pair_exchange(part, "gy", half)[:, None] for part in parts]
+        rows = y_inverse(me, y_back_table, parts, size_y)
         layers = lax.all_to_all(rows, "gy", 0, 0, tiled=True)
         adjoint, first_x, last_x, first_y, last_y = make_adjoint(
-            layers.reshape(Z, height, width), cot_vort, component
+            layers.reshape(Z, height, width),
+            cot_vort,
+            component,
+            () if grad_vort is None else (grad_vort, grad_vel),
         )
         halos = exchange(first_x, last_x, "gx") + exchange(first_y, last_y, "gy")
         grad_vort = add_grad_vort(

time: 503 us -> 447 us (0.89)
  waiting for transfers between devices: 237 us -> 114 us
  starting transfers between devices: 72.9 us -> 140 us
  local copies, waits for them, and re-layouts: 70.4 us -> 19.7 us
  Pallas kernels: 118 us -> 168 us
    all_to_all x6 -> x0, waiting for transfers between devices: 163 us -> none  [the longest x3 83.5 us: local(): returned = lax.all_to_all(filtered, 'gx', 0, 0, tiled=True)]
    ppermute x0 -> x18, waiting for transfers between devices: none -> 64.9 us  [shifted(): lax.ppermute(parts[s], axis, [(i, (i + s) % count) for i in range(count)])]
    ppermute x0 -> x18, starting transfers between devices: none -> 62.1 us  [shifted(): lax.ppermute(parts[s], axis, [(i, (i + s) % count) for i in range(count)])]
    unnamed x108 -> x88, local copies, waits for them, and re-layouts: 68.4 us -> 12.5 us
    ppermute x16, starting transfers between devices: 22.7 us -> 54.4 us  [exchange(): return (lax.ppermute(last, axis, up), lax.ppermute(first, axis, down))]
    all_to_all x6 -> x0, starting transfers between devices: 25.1 us -> none  [the longest x3 12.8 us: local(): lines = lax.all_to_all(coefficients, 'gx', 0, 0, tiled=True)]
    pallas_call x15, Pallas kernels: 93 us -> 112 us  [the longest x3 27.7 us: y_transform(): pl.pallas_call(kernel, grid_spec=pltpu.PrefetchScalarGridSpec(num_scalar_...]
    all_to_all x3, waiting for transfers between devices: 16.3 us -> 0.01 us  [local(): layers = lax.all_to_all(rows, 'gy', 0, 0, tiled=True)]
  transfers between devices with their start and end apart: 28 -> 40, of which waited for: 12 -> 10; matrix products, arithmetic and copies ran while one was open for 0% -> 2% of each run, Pallas kernels for 21% -> 34%
where the time goes in v2:
time: 447 us; the launch traced here: 445 us
  Pallas kernels  168 us (38%)
  starting transfers between devices  140 us (31%)
  waiting for transfers between devices  114 us (26%)
  local copies, waits for them, and re-layouts  19.7 us (4%)
    ppermute x18, waiting for transfers between devices, shifted(): lax.ppermute(parts[s], axis, [(i, (i + s) % count) for i in range(count)])  64.9 us
    ppermute x18, starting transfers between devices, shifted(): lax.ppermute(parts[s], axis, [(i, (i + s) % count) for i in range(count)])  62.1 us
    ppermute x16, starting transfers between devices, exchange(): return (lax.ppermute(last, axis, up), lax.ppermute(first, axis, down))  54.4 us
    all_to_all x3, waiting for transfers between devices, local(): lax.all_to_all(layers.reshape(size_y, planes, height, width), 'gy', 0, 0,...  31.5 us
    pallas_call x3, Pallas kernels, y_transform(): pl.pallas_call(kernel, grid_spec=pltpu.PrefetchScalarGridSpec(num_scalar_...  27.7 us
    pallas_call x3, Pallas kernels, add_grad_vort(): pl.pallas_call(kernel, grid=(Z // LAYERS,), in_specs=in_specs, out_specs=...  26.7 us
    pallas_call x3, Pallas kernels, write_grad_vel(): pl.pallas_call(grad_vel_kernel, grid=(Z // LAYERS,), in_specs=in_specs, o...  22.9 us
    pallas_call x3, Pallas kernels, y_inverse(): pl.pallas_call(kernel, grid=(size_y // count,), in_specs=[pl.BlockSpec(me...  19.3 us
  transfers between devices with their start and end apart: 40, of which 10 were waited for; matrix products, arithmetic and copies ran while one was open for 2% of the time, Pallas kernels for 34%

profile of v2, /device:TPU:0, one launch (start us, length us, event | category | flops | bytes accessed | tf_op | source)
XLA Modules:
  0.0 445.2 jit_solution(2111415939831658458)
XLA Ops:
  0.6 5.2 %depth_transform.5 = bf16[16,192,256]{2,1,0:T(8,128)(2,1)} custom-call(f32[3,16,192,256]{3,2,1,0:T(8,128)} %values_ref.5), custom_call_target="tpu_custom_call" | custom-call | flops 4718592 | bytes 4718592 | tf_op jit(solution)/shard_map/depth_transform/pallas_call | solution.py:136
  5.9 5.2 %all-to-all-start.3 = ((bf16[8,2,192,256]{3,2,1,0:T(8,128)(2,1)}), bf16[8,2,192,256]{3,2,1,0:T(8,128)(2,1)S(1)}, u32[]{:S(2)}, u32[]{:S(2)}) async-start(bf16[8,2,192,256]{3,2,1,0:T(8,128)(2,1)} %bitcast.58), calls=%async_computation.3 | async-start | bytes 3145728 | tf_op jit(solution)/shard_map/all_to_all | solution.py:671
  11.0 5.2 %depth_transform.4 = bf16[16,192,256]{2,1,0:T(8,128)(2,1)} custom-call(f32[3,16,192,256]{3,2,1,0:T(8,128)} %values_ref.5), custom_call_target="tpu_custom_call" | custom-call | flops 4718592 | bytes 4718592 | tf_op jit(solution)/shard_map/depth_transform/pallas_call | solution.py:136
  16.3 15.8 %all-to-all-done.3.columns_ref = bf16[8,2,192,256]{3,2,1,0:T(8,128)(2,1)S(1)} async-done(((bf16[8,2,192,256]{3,2,1,0:T(8,128)(2,1)}), bf16[8,2,192,256]{3,2,1,0:T(8,128)(2,1)S(1)}, u32[]{:S(2)}, u32[]{:S(2)}) %all-to-all-start.3) | async-done | bytes 1572896 | tf_op jit(solution)/shard_map/all_to_all | solution.py:671
  32.1 3.6 all-to-all-start.1
  35.7 5.2 %depth_transform.3 = bf16[16,192,256]{2,1,0:T(8,128)(2,1)} custom-call(f32[3,16,192,256]{3,2,1,0:T(8,128)} %values_ref.5), custom_call_target="tpu_custom_call" | custom-call | flops 4718592 | bytes 4718592 | tf_op jit(solution)/shard_map/depth_transform/pallas_call | solution.py:136
  40.9 15.7 %all-to-all-done.1.columns_ref = bf16[8,2,192,256]{3,2,1,0:T(8,128)(2,1)S(1)} async-done(((bf16[8,2,192,256]{3,2,1,0:T(8,128)(2,1)}), bf16[8,2,192,256]{3,2,1,0:T(8,128)(2,1)S(1)}, u32[]{:S(2)}, u32[]{:S(2)}) %all-to-all-start.1) | async-done | bytes 1572896 | tf_op jit(solution)/shard_map/all_to_all | solution.py:671
  56.6 3.6 all-to-all-start
  60.2 9.2 %y_transform.5 = (bf16[1,2,2,192,256]{4,3,2,1,0:T(8,128)(2,1)}, bf16[1,2,2,192,256]{4,3,2,1,0:T(8,128)(2,1)}, bf16[1,2,2,192,256]{4,3,2,1,0:T(8,128)(2,1)}, bf16[1,2,2,192,256]{4,3,2,1,0:T(8,128)(2,1)}) custom-call(s32[1]{0:T(128)} %bitcast.me_ref, bf16[1536,1536]{1,0:T(8,128)(2,1)} %constant.33.clone.table_ref, bf16[8,2,192,256]{3,2,1,0:T(8,128)(2,1)} %copy-done.5), custom_call_target="tpu_custom_call" | custom-call | flops 2415919104 | bytes 7864320 | tf_op jit(solution)/shard_map/y_transform/pallas_call | solution.py:166
  75.5 9.2 %y_transform.4 = (bf16[1,2,2,192,256]{4,3,2,1,0:T(8,128)(2,1)}, bf16[1,2,2,192,256]{4,3,2,1,0:T(8,128)(2,1)}, bf16[1,2,2,192,256]{4,3,2,1,0:T(8,128)(2,1)}, bf16[1,2,2,192,256]{4,3,2,1,0:T(8,128)(2,1)}) custom-call(s32[1]{0:T(128)} %bitcast.me_ref, bf16[1536,1536]{1,0:T(8,128)(2,1)} %constant.33.clone.table_ref, bf16[8,2,192,256]{3,2,1,0:T(8,128)(2,1)} %copy-done.4), custom_call_target="tpu_custom_call" | custom-call | flops 2415919104 | bytes 7864320 | tf_op jit(solution)/shard_map/y_transform/pallas_call | solution.py:166
  91.3 4.6 %edge_columns.2 = (bf16[3,16,192]{2,1,0:T(8,128)(2,1)}, bf16[3,16,192]{2,1,0:T(8,128)(2,1)}) custom-call(bf16[3,16,192,256]{3,2,1,0:T(8,128)(2,1)} %refs_2_.5), custom_call_target="tpu_custom_call" | custom-call | flops 150994944 | bytes 4718592 | tf_op jit(solution)/shard_map/edge_columns/pallas_call | solution.py:377
  97.4 3.1 collective-permute-done.14.refs_2_
  100.4 27.2 %collective-permute-start.4 = (bf16[4,16,192]{2,1,0:T(8,128)(2,1)S(1)}, bf16[4,16,192]{2,1,0:T(8,128)(2,1)S(1)}, u32[]{:S(2)}, u32[]{:S(2)}) collective-permute-start(bf16[4,16,192]{2,1,0:T(8,128)(2,1)S(1)} %pad_maximum_fusion.1), channel_id=1, source_target_pairs={{8,0},{16,8},{24,16},{0,24},{9,1},{17,9},{25,17},{1,25},{10,2},{18... | collective-permute-start | bytes 73736 | tf_op jit(solution)/shard_map/ppermute | solution.py:395
  128.4 5.2 %x_transform.5.refs_3_.refs_2_ = f32[2,2,192,1024]{3,2,1,0:T(8,128)} custom-call(s32[1]{0:T(128)} %bitcast.me_ref, bf16[1024,1024]{1,0:T(8,128)(2,1)} %constant.34.clone.table_ref, bf16[2,2,192,256]{3,2,1,0:T(8,128)(2,1)} %bitcast.60, bf16[2,2,192,256]{3,2,1,0:T(8,128)(2,1)} %copy-done.13, bf16[2,2,192,256]{3,2,1,0:T(8,128)(2,1)} %copy-done.15, ...), custom_call_target="tpu_custom_call" | custom-call | flops 1610612736 | bytes 6815744 | tf_op jit(solution)/shard_map/x_transform/pallas_call | solution.py:236
  135.4 5.2 %x_transform.4.refs_3_.refs_2_ = f32[2,2,192,1024]{3,2,1,0:T(8,128)} custom-call(s32[1]{0:T(128)} %bitcast.me_ref, bf16[1024,1024]{1,0:T(8,128)(2,1)} %constant.34.clone.table_ref, bf16[2,2,192,256]{3,2,1,0:T(8,128)(2,1)} %bitcast.61, bf16[2,2,192,256]{3,2,1,0:T(8,128)(2,1)} %copy-done.14, bf16[2,2,192,256]{3,2,1,0:T(8,128)(2,1)} %copy-done.16, ...), custom_call_target="tpu_custom_call" | custom-call | flops 1610612736 | bytes 6815744 | tf_op jit(solution)/shard_map/x_transform/pallas_call | solution.py:236
  140.6 5.8 %curl_inverse.4 = (bf16[2,2,192,256]{3,2,1,0:T(8,128)(2,1)}, bf16[2,2,192,256]{3,2,1,0:T(8,128)(2,1)}, bf16[2,2,192,256]{3,2,1,0:T(8,128)(2,1)}, bf16[2,2,192,256]{3,2,1,0:T(8,128)(2,1)}) custom-call(s32[3]{0:T(128)} %pad_add_fusion.refs_0_, bf16[1024,1024]{1,0:T(8,128)(2,1)} %constant.35.clone.refs_1_, f32[2,2,192,1024]{3,2,1,0:T(8,128)} %x_transform.4.refs_3_.refs_2_, ...), custom_call_target="tpu_custom_call" | custom-call | flops 1610612736 | bytes 9961472 | tf_op jit(solution)/shard_map/curl_inverse/pallas_call | solution.py:317
  146.4 8.8 %collective-permute-start.16 = (bf16[2,2,192,256]{3,2,1,0:T(8,128)(2,1)}, bf16[2,2,192,256]{3,2,1,0:T(8,128)(2,1)S(1)}, u32[]{:S(2)}, u32[]{:S(2)}) collective-permute-start(bf16[2,2,192,256]{3,2,1,0:T(8,128)(2,1)} %get-tuple-element.66), channel_id=1, source_target_pairs={{0,8},{8,16},{16,24},{24,0},{1,9},{9,17},{17,25},{25,1},{2,10},{10... | collective-permute-start | bytes 1179656 | tf_op jit(solution)/shard_map/ppermute | solution.py:628
  159.7 9.2 %y_transform.3 = (bf16[1,2,2,192,256]{4,3,2,1,0:T(8,128)(2,1)}, bf16[1,2,2,192,256]{4,3,2,1,0:T(8,128)(2,1)}, bf16[1,2,2,192,256]{4,3,2,1,0:T(8,128)(2,1)}, bf16[1,2,2,192,256]{4,3,2,1,0:T(8,128)(2,1)}) custom-call(s32[1]{0:T(128)} %bitcast.me_ref, bf16[1536,1536]{1,0:T(8,128)(2,1)} %constant.33.clone.table_ref, bf16[8,2,192,256]{3,2,1,0:T(8,128)(2,1)} %copy-done.3), custom_call_target="tpu_custom_call" | custom-call | flops 2415919104 | bytes 7864320 | tf_op jit(solution)/shard_map/y_transform/pallas_call | solution.py:166
  171.2 12.6 %collective-permute-done.17 = bf16[2,2,192,256]{3,2,1,0:T(8,128)(2,1)S(1)} collective-permute-done((bf16[2,2,192,256]{3,2,1,0:T(8,128)(2,1)}, bf16[2,2,192,256]{3,2,1,0:T(8,128)(2,1)S(1)}, u32[]{:S(2)}, u32[]{:S(2)}) %collective-permute-start.17) | collective-permute-done | bytes 393248 | tf_op jit(solution)/shard_map/ppermute | solution.py:628
  185.4 9.7 %collective-permute-start.2 = (bf16[2,2,192,256]{3,2,1,0:T(8,128)(2,1)}, bf16[2,2,192,256]{3,2,1,0:T(8,128)(2,1)S(1)}, u32[]{:S(2)}, u32[]{:S(2)}) collective-permute-start(bf16[2,2,192,256]{3,2,1,0:T(8,128)(2,1)} %bitcast.66), channel_id=1, source_target_pairs={{0,24},{8,0},{16,8},{24,16},{1,25},{9,1},{17,9},{25,17},{2,26},{10... | collective-permute-start | bytes 1179656 | tf_op jit(solution)/shard_map/ppermute | solution.py:628
  195.1 6.4 %y_inverse.4 = bf16[8,2,192,256]{3,2,1,0:T(8,128)(2,1)} custom-call(s32[1]{0:T(128)} %bitcast.me_ref, bf16[1536,1536]{1,0:T(8,128)(2,1)} %constant.36.clone.table_ref, bf16[1,2,2,192,256]{4,3,2,1,0:T(8,128)(2,1)} %bitcast.73, bf16[1,2,2,192,256]{4,3,2,1,0:T(8,128)(2,1)} %bitcast.75, bf16[1,2,2,192,256]{4,3,2,1,0:T(8,128)(2,1)} %bitcast.76, ...), custom_call_target="tpu_custom_call" | custom-call | flops 2415919104 | bytes 7864320 | tf_op jit(solution)/shard_map/y_inverse/pallas_call | solution.py:206
  201.5 3.9 all-to-all-start.4
  209.4 17.3 %collective-permute-done.5.refs_6_ = bf16[4,16,256]{2,1,0:T(8,128)(2,1)S(1)} collective-permute-done((bf16[4,16,256]{2,1,0:T(8,128)(2,1)S(1)}, bf16[4,16,256]{2,1,0:T(8,128)(2,1)S(1)}, u32[]{:S(2)}, u32[]{:S(2)}) %collective-permute-start.5) | collective-permute-done | bytes 32800 | tf_op jit(solution)/shard_map/ppermute | solution.py:395
  227.7 5.2 %x_transform.3.refs_2_.refs_3_ = f32[2,2,192,1024]{3,2,1,0:T(8,128)} custom-call(s32[1]{0:T(128)} %bitcast.me_ref, bf16[1024,1024]{1,0:T(8,128)(2,1)} %constant.34.clone.table_ref, bf16[2,2,192,256]{3,2,1,0:T(8,128)(2,1)} %bitcast.59, bf16[2,2,192,256]{3,2,1,0:T(8,128)(2,1)} %copy-done.10, bf16[2,2,192,256]{3,2,1,0:T(8,128)(2,1)} %copy-done.11, ...), custom_call_target="tpu_custom_call" | custom-call | flops 1610612736 | bytes 6815744 | tf_op jit(solution)/shard_map/x_transform/pallas_call | solution.py:236
  232.9 5.8 %curl_inverse.5 = (bf16[2,2,192,256]{3,2,1,0:T(8,128)(2,1)}, bf16[2,2,192,256]{3,2,1,0:T(8,128)(2,1)}, bf16[2,2,192,256]{3,2,1,0:T(8,128)(2,1)}, bf16[2,2,192,256]{3,2,1,0:T(8,128)(2,1)}) custom-call(s32[3]{0:T(128)} %pad_add_fusion.refs_0_, bf16[1024,1024]{1,0:T(8,128)(2,1)} %constant.35.clone.refs_1_, f32[2,2,192,1024]{3,2,1,0:T(8,128)} %x_transform.5.refs_3_.refs_2_, ...), custom_call_target="tpu_custom_call" | custom-call | flops 1610612736 | bytes 9961472 | tf_op jit(solution)/shard_map/curl_inverse/pallas_call | solution.py:317
  238.7 13.5 %collective-permute-start.19 = (bf16[2,2,192,256]{3,2,1,0:T(8,128)(2,1)}, bf16[2,2,192,256]{3,2,1,0:T(8,128)(2,1)S(1)}, u32[]{:S(2)}, u32[]{:S(2)}) collective-permute-start(bf16[2,2,192,256]{3,2,1,0:T(8,128)(2,1)} %get-tuple-element.70), channel_id=1, source_target_pairs={{0,8},{8,16},{16,24},{24,0},{1,9},{9,17},{17,25},{25,1},{2,10},{10... | collective-permute-start | bytes 1179656 | tf_op jit(solution)/shard_map/ppermute | solution.py:628
  256.6 6.5 %collective-permute-done.19 = bf16[2,2,192,256]{3,2,1,0:T(8,128)(2,1)S(1)} collective-permute-done((bf16[2,2,192,256]{3,2,1,0:T(8,128)(2,1)}, bf16[2,2,192,256]{3,2,1,0:T(8,128)(2,1)S(1)}, u32[]{:S(2)}, u32[]{:S(2)}) %collective-permute-start.19) | collective-permute-done | bytes 393248 | tf_op jit(solution)/shard_map/ppermute | solution.py:628
  263.1 15.8 %collective-permute-done.20 = bf16[2,2,192,256]{3,2,1,0:T(8,128)(2,1)S(1)} collective-permute-done((bf16[2,2,192,256]{3,2,1,0:T(8,128)(2,1)}, bf16[2,2,192,256]{3,2,1,0:T(8,128)(2,1)S(1)}, u32[]{:S(2)}, u32[]{:S(2)}) %collective-permute-start.20) | collective-permute-done | bytes 393248 | tf_op jit(solution)/shard_map/ppermute | solution.py:628
  279.8 6.5 %y_inverse.5 = bf16[8,2,192,256]{3,2,1,0:T(8,128)(2,1)} custom-call(s32[1]{0:T(128)} %bitcast.me_ref, bf16[1536,1536]{1,0:T(8,128)(2,1)} %constant.36.clone.table_ref, bf16[1,2,2,192,256]{4,3,2,1,0:T(8,128)(2,1)} %bitcast.80, bf16[1,2,2,192,256]{4,3,2,1,0:T(8,128)(2,1)} %bitcast.82, bf16[1,2,2,192,256]{4,3,2,1,0:T(8,128)(2,1)} %bitcast.84, ...), custom_call_target="tpu_custom_call" | custom-call | flops 2415919104 | bytes 7864320 | tf_op jit(solution)/shard_map/y_inverse/pallas_call | solution.py:206
  286.3 3.8 all-to-all-start.5
  290.1 5.8 %curl_inverse.3 = (bf16[2,2,192,256]{3,2,1,0:T(8,128)(2,1)}, bf16[2,2,192,256]{3,2,1,0:T(8,128)(2,1)}, bf16[2,2,192,256]{3,2,1,0:T(8,128)(2,1)}, bf16[2,2,192,256]{3,2,1,0:T(8,128)(2,1)}) custom-call(s32[3]{0:T(128)} %pad_add_fusion.refs_0_, bf16[1024,1024]{1,0:T(8,128)(2,1)} %constant.35.clone.refs_1_, f32[2,2,192,1024]{3,2,1,0:T(8,128)} %x_transform.3.refs_2_.refs_3_, ...), custom_call_target="tpu_custom_call" | custom-call | flops 1610612736 | bytes 9961472 | tf_op jit(solution)/shard_map/curl_inverse/pallas_call | solution.py:317
  295.9 9.2 %collective-permute-start.10 = (bf16[2,2,192,256]{3,2,1,0:T(8,128)(2,1)}, bf16[2,2,192,256]{3,2,1,0:T(8,128)(2,1)S(1)}, u32[]{:S(2)}, u32[]{:S(2)}) collective-permute-start(bf16[2,2,192,256]{3,2,1,0:T(8,128)(2,1)} %get-tuple-element.58), channel_id=1, source_target_pairs={{0,8},{8,16},{16,24},{24,0},{1,9},{9,17},{17,25},{25,1},{2,10},{10... | collective-permute-start | bytes 1179656 | tf_op jit(solution)/shard_map/ppermute | solution.py:628
  305.0 3.3 collective-permute-start.11
  308.3 9.7 %collective-permute-done.10 = bf16[2,2,192,256]{3,2,1,0:T(8,128)(2,1)S(1)} collective-permute-done((bf16[2,2,192,256]{3,2,1,0:T(8,128)(2,1)}, bf16[2,2,192,256]{3,2,1,0:T(8,128)(2,1)S(1)}, u32[]{:S(2)}, u32[]{:S(2)}) %collective-permute-start.10) | collective-permute-done | bytes 393248 | tf_op jit(solution)/shard_map/ppermute | solution.py:628
  318.0 16.4 %collective-permute-done.11 = bf16[2,2,192,256]{3,2,1,0:T(8,128)(2,1)S(1)} collective-permute-done((bf16[2,2,192,256]{3,2,1,0:T(8,128)(2,1)}, bf16[2,2,192,256]{3,2,1,0:T(8,128)(2,1)S(1)}, u32[]{:S(2)}, u32[]{:S(2)}) %collective-permute-start.11) | collective-permute-done | bytes 393248 | tf_op jit(solution)/shard_map/ppermute | solution.py:628
  335.3 6.4 %y_inverse.3 = bf16[8,2,192,256]{3,2,1,0:T(8,128)(2,1)} custom-call(s32[1]{0:T(128)} %bitcast.me_ref, bf16[1536,1536]{1,0:T(8,128)(2,1)} %constant.36.clone.table_ref, bf16[1,2,2,192,256]{4,3,2,1,0:T(8,128)(2,1)} %bitcast.79, bf16[1,2,2,192,256]{4,3,2,1,0:T(8,128)(2,1)} %bitcast.81, bf16[1,2,2,192,256]{4,3,2,1,0:T(8,128)(2,1)} %bitcast.83, ...), custom_call_target="tpu_custom_call" | custom-call | flops 2415919104 | bytes 7864320 | tf_op jit(solution)/shard_map/y_inverse/pallas_call | solution.py:206
  341.7 3.9 all-to-all-start.2
  350.8 5.2 %make_adjoint.3 = (f32[16,192,256]{2,1,0:T(8,128)}, bf16[16,192]{1,0:T(8,128)(2,1)}, bf16[16,192]{1,0:T(8,128)(2,1)}, bf16[16,256]{1,0:T(8,128)(2,1)}, bf16[16,256]{1,0:T(8,128)(2,1)}) custom-call(bf16[16,192,256]{2,1,0:T(8,128)(2,1)} %bitcast.56, f32[3,16,192,256]{3,2,1,0:T(8,128)} %cotangent_ref.5), custom_call_target="tpu_custom_call" | custom-call | flops 55050240 | bytes 7864320 | tf_op jit(solution)/shard_map/make_adjoint/pallas_call | solution.py:426
  355.9 8.8 %collective-permute-start.22 = (bf16[16,192]{1,0:T(8,128)(2,1)}, bf16[16,192]{1,0:T(8,128)(2,1)S(1)}, u32[]{:S(2)}, u32[]{:S(2)}) collective-permute-start(bf16[16,192]{1,0:T(8,128)(2,1)} %get-tuple-element.74), channel_id=1, source_target_pairs={{0,8},{8,16},{16,24},{24,0},{1,9},{9,17},{17,25},{25,1},{2,10},{10... | collective-permute-start | bytes 18440 | tf_op jit(solution)/shard_map/ppermute | solution.py:395
  367.4 7.3 %add_grad_vort.3.refs_0_.refs_8_ = f32[3,16,192,256]{3,2,1,0:T(8,128)} custom-call(bf16[256,256]{1,0:T(8,128)(2,1)} %constant.37.clone.refs_0_.slope_x, bf16[192,192]{1,0:T(8,128)(2,1)} %constant.38.clone.refs_1_, bf16[3,16,192,256]{3,2,1,0:T(8,128)(2,1)} %refs_2_.5, f32[16,192,256]{2,1,0:T(8,128)} %get-tuple-element.73.refs_3_.adjoint, ...), custom_call_target="tpu_custom_call" | custom-call | flops 704643072 | bytes 14155776 | tf_op jit(solution)/shard_map/add_grad_vort/pallas_call | solution.py:523
  375.9 7.6 %write_grad_vel.3.refs_1_.refs_8_ = f32[3,16,192,256]{3,2,1,0:T(8,128)} custom-call(bf16[256,256]{1,0:T(8,128)(2,1)} %constant.37.clone.refs_0_.slope_x, bf16[3,16,192,256]{3,2,1,0:T(8,128)(2,1)} %vorticity_below.5, bf16[3,16,192,256]{3,2,1,0:T(8,128)(2,1)} %vorticity_below.5, bf16[3,16,192,256]{3,2,1,0:T(8,128)(2,1)} %vorticity_below.5, ...), custom_call_target="tpu_custom_call" | custom-call | flops 805306368 | bytes 12582912 | tf_op jit(solution)/shard_map/write_grad_vel/pallas_call | solution.py:603
  383.6 5.2 %make_adjoint.4 = (f32[16,192,256]{2,1,0:T(8,128)}, bf16[16,192]{1,0:T(8,128)(2,1)}, bf16[16,192]{1,0:T(8,128)(2,1)}, bf16[16,256]{1,0:T(8,128)(2,1)}, bf16[16,256]{1,0:T(8,128)(2,1)}) custom-call(bf16[16,192,256]{2,1,0:T(8,128)(2,1)} %bitcast.53, f32[3,16,192,256]{3,2,1,0:T(8,128)} %cotangent_ref.5, f32[3,16,192,256]{3,2,1,0:T(8,128)} %add_grad_vort.3.refs_0_.refs_8_, ...), custom_call_target="tpu_custom_call" | custom-call | flops 55050240 | bytes 7864320 | tf_op jit(solution)/shard_map/make_adjoint/pallas_call | solution.py:426
  395.2 9.7 %add_grad_vort.4.refs_0_.refs_8_ = f32[3,16,192,256]{3,2,1,0:T(8,128)} custom-call(bf16[256,256]{1,0:T(8,128)(2,1)} %constant.37.clone.refs_0_.slope_x, bf16[192,192]{1,0:T(8,128)(2,1)} %constant.38.clone.refs_1_, bf16[3,16,192,256]{3,2,1,0:T(8,128)(2,1)} %refs_2_.5, ...), custom_call_target="tpu_custom_call", output_to_operand_aliasing={{}: (8, {})} | custom-call | flops 704643072 | bytes 23592960 | tf_op jit(solution)/shard_map/add_grad_vort/pallas_call | solution.py:523
  406.1 7.6 %write_grad_vel.4.refs_1_.refs_8_ = f32[3,16,192,256]{3,2,1,0:T(8,128)} custom-call(bf16[256,256]{1,0:T(8,128)(2,1)} %constant.37.clone.refs_0_.slope_x, bf16[3,16,192,256]{3,2,1,0:T(8,128)(2,1)} %vorticity_below.5, bf16[3,16,192,256]{3,2,1,0:T(8,128)(2,1)} %vorticity_below.5, ...), custom_call_target="tpu_custom_call", output_to_operand_aliasing={{}: (13, {})} | custom-call | flops 805306368 | bytes 12582912 | tf_op jit(solution)/shard_map/write_grad_vel/pallas_call | solution.py:603
  414.9 5.2 %make_adjoint.5 = (f32[16,192,256]{2,1,0:T(8,128)}, bf16[16,192]{1,0:T(8,128)(2,1)}, bf16[16,192]{1,0:T(8,128)(2,1)}, bf16[16,256]{1,0:T(8,128)(2,1)}, bf16[16,256]{1,0:T(8,128)(2,1)}) custom-call(bf16[16,192,256]{2,1,0:T(8,128)(2,1)} %bitcast.54, f32[3,16,192,256]{3,2,1,0:T(8,128)} %cotangent_ref.5, f32[3,16,192,256]{3,2,1,0:T(8,128)} %add_grad_vort.4.refs_0_.refs_8_, ...), custom_call_target="tpu_custom_call" | custom-call | flops 55050240 | bytes 7864320 | tf_op jit(solution)/shard_map/make_adjoint/pallas_call | solution.py:426
  420.3 3.6 collective-permute-start.31
  426.6 9.7 %add_grad_vort.5 = f32[3,16,192,256]{3,2,1,0:T(8,128)} custom-call(bf16[256,256]{1,0:T(8,128)(2,1)} %constant.37.clone.refs_0_.slope_x, bf16[192,192]{1,0:T(8,128)(2,1)} %constant.38.clone.refs_1_, bf16[3,16,192,256]{3,2,1,0:T(8,128)(2,1)} %refs_2_.5, f32[16,192,256]{2,1,0:T(8,128)} %get-tuple-element.83.refs_3_.adjoint, ...), custom_call_target="tpu_custom_call", output_to_operand_aliasing={{}: (8, {})} | custom-call | flops 704643072 | bytes 23592960 | tf_op jit(solution)/shard_map/add_grad_vort/pallas_call | solution.py:523
  437.5 7.6 %write_grad_vel.5 = f32[3,16,192,256]{3,2,1,0:T(8,128)} custom-call(bf16[256,256]{1,0:T(8,128)(2,1)} %constant.37.clone.refs_0_.slope_x, bf16[3,16,192,256]{3,2,1,0:T(8,128)(2,1)} %vorticity_below.5, bf16[3,16,192,256]{3,2,1,0:T(8,128)(2,1)} %vorticity_below.5, bf16[3,16,192,256]{3,2,1,0:T(8,128)(2,1)} %vorticity_below.5, ...), custom_call_target="tpu_custom_call", output_to_operand_aliasing={{}: (13, {})} | custom-call | flops 805306368 | bytes 12582912 | tf_op jit(solution)/shard_map/write_grad_vel/pallas_call | solution.py:603
  (157 shorter events, 57.8 us)
Async XLA Ops:
  5.9 26.2 %all-to-all-start.3 = ((bf16[8,2,192,256]{3,2,1,0:T(8,128)(2,1)}), bf16[8,2,192,256]{3,2,1,0:T(8,128)(2,1)S(1)}, u32[]{:S(2)}, u32[]{:S(2)}) async-start(bf16[8,2,192,256]{3,2,1,0:T(8,128)(2,1)} %bitcast.58), calls=%async_computation.3 | async-start | bytes 3145728 | tf_op jit(solution)/shard_map/all_to_all | solution.py:671
  32.1 24.5 %all-to-all-start.1 = ((bf16[8,2,192,256]{3,2,1,0:T(8,128)(2,1)}), bf16[8,2,192,256]{3,2,1,0:T(8,128)(2,1)S(1)}, u32[]{:S(2)}, u32[]{:S(2)}) async-start(bf16[8,2,192,256]{3,2,1,0:T(8,128)(2,1)} %bitcast.57), calls=%async_computation.1 | async-start | bytes 3145728 | tf_op jit(solution)/shard_map/all_to_all | solution.py:671
  56.6 12.8 %copy-start.4 = (bf16[8,2,192,256]{3,2,1,0:T(8,128)(2,1)}, bf16[8,2,192,256]{3,2,1,0:T(8,128)(2,1)S(1)}, u32[]{:S(2)}) copy-start(bf16[8,2,192,256]{3,2,1,0:T(8,128)(2,1)S(1)} %all-to-all-done.1.columns_ref) | copy-start | bytes 4718596
  56.6 101.9 %all-to-all-start = ((bf16[8,2,192,256]{3,2,1,0:T(8,128)(2,1)}), bf16[8,2,192,256]{3,2,1,0:T(8,128)(2,1)S(1)}, u32[]{:S(2)}, u32[]{:S(2)}) async-start(bf16[8,2,192,256]{3,2,1,0:T(8,128)(2,1)} %bitcast.55), calls=%async_computation | async-start | bytes 3145728 | tf_op jit(solution)/shard_map/all_to_all | solution.py:671
  69.5 16.3 %collective-permute-start.13 = (bf16[2,2,192,256]{3,2,1,0:T(8,128)(2,1)}, bf16[2,2,192,256]{3,2,1,0:T(8,128)(2,1)S(1)}, u32[]{:S(2)}, u32[]{:S(2)}) collective-permute-start(bf16[2,2,192,256]{3,2,1,0:T(8,128)(2,1)} %bitcast.78), channel_id=1, source_target_pairs={{0,8},{8,16},{16,24},{24,0},{1,9},{9,17},{17,25},{25,1},{2,10},{10... | collective-permute-start | bytes 1179656 | tf_op jit(solution)/shard_map/ppermute | solution.py:628
  71.6 28.8 %collective-permute-start.14 = (bf16[2,2,192,256]{3,2,1,0:T(8,128)(2,1)}, bf16[2,2,192,256]{3,2,1,0:T(8,128)(2,1)S(1)}, u32[]{:S(2)}, u32[]{:S(2)}) collective-permute-start(bf16[2,2,192,256]{3,2,1,0:T(8,128)(2,1)} %bitcast.71), channel_id=1, source_target_pairs={{0,16},{8,24},{16,0},{24,8},{1,17},{9,25},{17,1},{25,9},{2,18},{10... | collective-permute-start | bytes 1179656 | tf_op jit(solution)/shard_map/ppermute | solution.py:628
  74.2 53.4 %collective-permute-start.15 = (bf16[2,2,192,256]{3,2,1,0:T(8,128)(2,1)}, bf16[2,2,192,256]{3,2,1,0:T(8,128)(2,1)S(1)}, u32[]{:S(2)}, u32[]{:S(2)}) collective-permute-start(bf16[2,2,192,256]{3,2,1,0:T(8,128)(2,1)} %bitcast.69), channel_id=1, source_target_pairs={{0,24},{8,0},{16,8},{24,16},{1,25},{9,1},{17,9},{25,17},{2,26},{10... | collective-permute-start | bytes 1179656 | tf_op jit(solution)/shard_map/ppermute | solution.py:628
  84.8 48.8 %collective-permute-start.7 = (bf16[2,2,192,256]{3,2,1,0:T(8,128)(2,1)}, bf16[2,2,192,256]{3,2,1,0:T(8,128)(2,1)S(1)}, u32[]{:S(2)}, u32[]{:S(2)}) collective-permute-start(bf16[2,2,192,256]{3,2,1,0:T(8,128)(2,1)} %bitcast.74), channel_id=1, source_target_pairs={{0,8},{8,16},{16,24},{24,0},{1,9},{9,17},{17,25},{25,1},{2,10},{10... | collective-permute-start | bytes 1179656 | tf_op jit(solution)/shard_map/ppermute | solution.py:628
  85.5 48.9 %collective-permute-start.8 = (bf16[2,2,192,256]{3,2,1,0:T(8,128)(2,1)}, bf16[2,2,192,256]{3,2,1,0:T(8,128)(2,1)S(1)}, u32[]{:S(2)}, u32[]{:S(2)}) collective-permute-start(bf16[2,2,192,256]{3,2,1,0:T(8,128)(2,1)} %bitcast.72), channel_id=1, source_target_pairs={{0,16},{8,24},{16,0},{24,8},{1,17},{9,25},{17,1},{25,9},{2,18},{10... | collective-permute-start | bytes 1179656 | tf_op jit(solution)/shard_map/ppermute | solution.py:628
  85.8 10.1 %copy-start.13 = (bf16[2,2,192,256]{3,2,1,0:T(8,128)(2,1)}, bf16[2,2,192,256]{3,2,1,0:T(8,128)(2,1)S(1)}, u32[]{:S(2)}) copy-start(bf16[2,2,192,256]{3,2,1,0:T(8,128)(2,1)S(1)} %collective-permute-done.13.refs_1_) | copy-start | bytes 1179652
  85.8 48.6 %collective-permute-start.9 = (bf16[2,2,192,256]{3,2,1,0:T(8,128)(2,1)}, bf16[2,2,192,256]{3,2,1,0:T(8,128)(2,1)S(1)}, u32[]{:S(2)}, u32[]{:S(2)}) collective-permute-start(bf16[2,2,192,256]{3,2,1,0:T(8,128)(2,1)} %bitcast.70), channel_id=1, source_target_pairs={{0,24},{8,0},{16,8},{24,16},{1,25},{9,1},{17,9},{25,17},{2,26},{10... | collective-permute-start | bytes 1179656 | tf_op jit(solution)/shard_map/ppermute | solution.py:628
  100.4 27.2 %copy-start.15 = (bf16[2,2,192,256]{3,2,1,0:T(8,128)(2,1)}, bf16[2,2,192,256]{3,2,1,0:T(8,128)(2,1)S(1)}, u32[]{:S(2)}) copy-start(bf16[2,2,192,256]{3,2,1,0:T(8,128)(2,1)S(1)} %collective-permute-done.14.refs_2_) | copy-start | bytes 1179652
  100.4 106.2 %collective-permute-start.4 = (bf16[4,16,192]{2,1,0:T(8,128)(2,1)S(1)}, bf16[4,16,192]{2,1,0:T(8,128)(2,1)S(1)}, u32[]{:S(2)}, u32[]{:S(2)}) collective-permute-start(bf16[4,16,192]{2,1,0:T(8,128)(2,1)S(1)} %pad_maximum_fusion.1), channel_id=1, source_target_pairs={{8,0},{16,8},{24,16},{0,24},{9,1},{17,9},{25,17},{1,25},{10,2},{18... | collective-permute-start | bytes 73736 | tf_op jit(solution)/shard_map/ppermute | solution.py:395
  127.6 79.5 %collective-permute-start.3 = (bf16[4,16,192]{2,1,0:T(8,128)(2,1)S(1)}, bf16[4,16,192]{2,1,0:T(8,128)(2,1)S(1)}, u32[]{:S(2)}, u32[]{:S(2)}) collective-permute-start(bf16[4,16,192]{2,1,0:T(8,128)(2,1)S(1)} %pad_maximum_fusion), channel_id=1, source_target_pairs={{0,8},{8,16},{16,24},{24,0},{1,9},{9,17},{17,25},{25,1},{2,10},{10... | collective-permute-start | bytes 73736 | tf_op jit(solution)/shard_map/ppermute | solution.py:395
  146.4 22.5 %collective-permute-start.16 = (bf16[2,2,192,256]{3,2,1,0:T(8,128)(2,1)}, bf16[2,2,192,256]{3,2,1,0:T(8,128)(2,1)S(1)}, u32[]{:S(2)}, u32[]{:S(2)}) collective-permute-start(bf16[2,2,192,256]{3,2,1,0:T(8,128)(2,1)} %get-tuple-element.66), channel_id=1, source_target_pairs={{0,8},{8,16},{16,24},{24,0},{1,9},{9,17},{17,25},{25,1},{2,10},{10... | collective-permute-start | bytes 1179656 | tf_op jit(solution)/shard_map/ppermute | solution.py:628
  155.2 28.6 %collective-permute-start.17 = (bf16[2,2,192,256]{3,2,1,0:T(8,128)(2,1)}, bf16[2,2,192,256]{3,2,1,0:T(8,128)(2,1)S(1)}, u32[]{:S(2)}, u32[]{:S(2)}) collective-permute-start(bf16[2,2,192,256]{3,2,1,0:T(8,128)(2,1)} %get-tuple-element.67), channel_id=1, source_target_pairs={{0,16},{8,24},{16,0},{24,8},{1,17},{9,25},{17,1},{25,9},{2,18},{10... | collective-permute-start | bytes 1179656 | tf_op jit(solution)/shard_map/ppermute | solution.py:628
  157.1 27.5 %collective-permute-start.18 = (bf16[2,2,192,256]{3,2,1,0:T(8,128)(2,1)}, bf16[2,2,192,256]{3,2,1,0:T(8,128)(2,1)S(1)}, u32[]{:S(2)}, u32[]{:S(2)}) collective-permute-start(bf16[2,2,192,256]{3,2,1,0:T(8,128)(2,1)} %get-tuple-element.68), channel_id=1, source_target_pairs={{0,24},{8,0},{16,8},{24,16},{1,25},{9,1},{17,9},{25,17},{2,26},{10... | collective-permute-start | bytes 1179656 | tf_op jit(solution)/shard_map/ppermute | solution.py:628
  169.6 57.1 %collective-permute-start = (bf16[2,2,192,256]{3,2,1,0:T(8,128)(2,1)}, bf16[2,2,192,256]{3,2,1,0:T(8,128)(2,1)S(1)}, u32[]{:S(2)}, u32[]{:S(2)}) collective-permute-start(bf16[2,2,192,256]{3,2,1,0:T(8,128)(2,1)} %bitcast.68), channel_id=1, source_target_pairs={{0,8},{8,16},{16,24},{24,0},{1,9},{9,17},{17,25},{25,1},{2,10},{10... | collective-permute-start | bytes 1179656 | tf_op jit(solution)/shard_map/ppermute | solution.py:628
  184.6 42.1 %collective-permute-start.1 = (bf16[2,2,192,256]{3,2,1,0:T(8,128)(2,1)}, bf16[2,2,192,256]{3,2,1,0:T(8,128)(2,1)S(1)}, u32[]{:S(2)}, u32[]{:S(2)}) collective-permute-start(bf16[2,2,192,256]{3,2,1,0:T(8,128)(2,1)} %bitcast.67), channel_id=1, source_target_pairs={{0,16},{8,24},{16,0},{24,8},{1,17},{9,25},{17,1},{25,9},{2,18},{10... | collective-permute-start | bytes 1179656 | tf_op jit(solution)/shard_map/ppermute | solution.py:628
  185.4 41.4 %collective-permute-start.2 = (bf16[2,2,192,256]{3,2,1,0:T(8,128)(2,1)}, bf16[2,2,192,256]{3,2,1,0:T(8,128)(2,1)S(1)}, u32[]{:S(2)}, u32[]{:S(2)}) collective-permute-start(bf16[2,2,192,256]{3,2,1,0:T(8,128)(2,1)} %bitcast.66), channel_id=1, source_target_pairs={{0,24},{8,0},{16,8},{24,16},{1,25},{9,1},{17,9},{25,17},{2,26},{10... | collective-permute-start | bytes 1179656 | tf_op jit(solution)/shard_map/ppermute | solution.py:628
  201.5 84.8 %all-to-all-start.4 = ((bf16[8,2,192,256]{3,2,1,0:T(8,128)(2,1)}), bf16[8,2,192,256]{3,2,1,0:T(8,128)(2,1)S(1)}, u32[]{:S(2)}, u32[]{:S(2)}) async-start(bf16[8,2,192,256]{3,2,1,0:T(8,128)(2,1)} %y_inverse.4), calls=%async_computation.4 | async-start | bytes 3145728 | tf_op jit(solution)/shard_map/all_to_all | solution.py:694
  206.6 20.1 %copy-start.6 = (bf16[4,16,192]{2,1,0:T(8,128)(2,1)}, bf16[4,16,192]{2,1,0:T(8,128)(2,1)S(1)}, u32[]{:S(2)}) copy-start(bf16[4,16,192]{2,1,0:T(8,128)(2,1)S(1)} %collective-permute-done.4.refs_5_) | copy-start | bytes 73732
  206.6 20.1 %collective-permute-start.5 = (bf16[4,16,256]{2,1,0:T(8,128)(2,1)S(1)}, bf16[4,16,256]{2,1,0:T(8,128)(2,1)S(1)}, u32[]{:S(2)}, u32[]{:S(2)}) collective-permute-start(bf16[4,16,256]{2,1,0:T(8,128)(2,1)S(1)} %pad_maximum_fusion.2), channel_id=1, source_target_pairs={{0,1},{1,2},{2,3},{3,4},{4,5},{5,6},{6,7},{7,0},{8,9},{9,10},{10,1... | collective-permute-start | bytes 98312 | tf_op jit(solution)/shard_map/ppermute | solution.py:395
  207.2 19.6 %copy-start.7 = (bf16[4,16,192]{2,1,0:T(8,128)(2,1)}, bf16[4,16,192]{2,1,0:T(8,128)(2,1)S(1)}, u32[]{:S(2)}) copy-start(bf16[4,16,192]{2,1,0:T(8,128)(2,1)S(1)} %collective-permute-done.3.refs_4_) | copy-start | bytes 73732
  207.2 19.5 %collective-permute-start.6 = (bf16[4,16,256]{2,1,0:T(8,128)(2,1)S(1)}, bf16[4,16,256]{2,1,0:T(8,128)(2,1)S(1)}, u32[]{:S(2)}, u32[]{:S(2)}) collective-permute-start(bf16[4,16,256]{2,1,0:T(8,128)(2,1)S(1)} %pad_maximum_fusion.3), channel_id=1, source_target_pairs={{1,0},{2,1},{3,2},{4,3},{5,4},{6,5},{7,6},{0,7},{9,8},{10,9},{11,1... | collective-permute-start | bytes 98312 | tf_op jit(solution)/shard_map/ppermute | solution.py:395
  238.7 24.3 %collective-permute-start.19 = (bf16[2,2,192,256]{3,2,1,0:T(8,128)(2,1)}, bf16[2,2,192,256]{3,2,1,0:T(8,128)(2,1)S(1)}, u32[]{:S(2)}, u32[]{:S(2)}) collective-permute-start(bf16[2,2,192,256]{3,2,1,0:T(8,128)(2,1)} %get-tuple-element.70), channel_id=1, source_target_pairs={{0,8},{8,16},{16,24},{24,0},{1,9},{9,17},{17,25},{25,1},{2,10},{10... | collective-permute-start | bytes 1179656 | tf_op jit(solution)/shard_map/ppermute | solution.py:628
  252.2 26.7 %collective-permute-start.20 = (bf16[2,2,192,256]{3,2,1,0:T(8,128)(2,1)}, bf16[2,2,192,256]{3,2,1,0:T(8,128)(2,1)S(1)}, u32[]{:S(2)}, u32[]{:S(2)}) collective-permute-start(bf16[2,2,192,256]{3,2,1,0:T(8,128)(2,1)} %get-tuple-element.71), channel_id=1, source_target_pairs={{0,16},{8,24},{16,0},{24,8},{1,17},{9,25},{17,1},{25,9},{2,18},{10... | collective-permute-start | bytes 1179656 | tf_op jit(solution)/shard_map/ppermute | solution.py:628
  253.7 25.2 %collective-permute-start.21 = (bf16[2,2,192,256]{3,2,1,0:T(8,128)(2,1)}, bf16[2,2,192,256]{3,2,1,0:T(8,128)(2,1)S(1)}, u32[]{:S(2)}, u32[]{:S(2)}) collective-permute-start(bf16[2,2,192,256]{3,2,1,0:T(8,128)(2,1)} %get-tuple-element.72), channel_id=1, source_target_pairs={{0,24},{8,0},{16,8},{24,16},{1,25},{9,1},{17,9},{25,17},{2,26},{10... | collective-permute-start | bytes 1179656 | tf_op jit(solution)/shard_map/ppermute | solution.py:628
  263.1 15.8 %copy-start.37 = (bf16[2,2,192,256]{3,2,1,0:T(8,128)(2,1)}, bf16[2,2,192,256]{3,2,1,0:T(8,128)(2,1)S(1)}, u32[]{:S(2)}) copy-start(bf16[2,2,192,256]{3,2,1,0:T(8,128)(2,1)S(1)} %collective-permute-done.19) | copy-start | bytes 1179652
  286.3 9.6 %copy-start = (bf16[8,2,192,256]{3,2,1,0:T(8,128)(2,1)}, bf16[8,2,192,256]{3,2,1,0:T(8,128)(2,1)S(1)}, u32[]{:S(2)}) copy-start(bf16[8,2,192,256]{3,2,1,0:T(8,128)(2,1)S(1)} %all-to-all-done.4) | copy-start | bytes 4718596
  286.3 55.5 %all-to-all-start.5 = ((bf16[8,2,192,256]{3,2,1,0:T(8,128)(2,1)}), bf16[8,2,192,256]{3,2,1,0:T(8,128)(2,1)S(1)}, u32[]{:S(2)}, u32[]{:S(2)}) async-start(bf16[8,2,192,256]{3,2,1,0:T(8,128)(2,1)} %y_inverse.5), calls=%async_computation.5 | async-start | bytes 3145728 | tf_op jit(solution)/shard_map/all_to_all | solution.py:694
  295.9 22.1 %collective-permute-start.10 = (bf16[2,2,192,256]{3,2,1,0:T(8,128)(2,1)}, bf16[2,2,192,256]{3,2,1,0:T(8,128)(2,1)S(1)}, u32[]{:S(2)}, u32[]{:S(2)}) collective-permute-start(bf16[2,2,192,256]{3,2,1,0:T(8,128)(2,1)} %get-tuple-element.58), channel_id=1, source_target_pairs={{0,8},{8,16},{16,24},{24,0},{1,9},{9,17},{17,25},{25,1},{2,10},{10... | collective-permute-start | bytes 1179656 | tf_op jit(solution)/shard_map/ppermute | solution.py:628
  305.0 29.4 %collective-permute-start.11 = (bf16[2,2,192,256]{3,2,1,0:T(8,128)(2,1)}, bf16[2,2,192,256]{3,2,1,0:T(8,128)(2,1)S(1)}, u32[]{:S(2)}, u32[]{:S(2)}) collective-permute-start(bf16[2,2,192,256]{3,2,1,0:T(8,128)(2,1)} %get-tuple-element.59), channel_id=1, source_target_pairs={{0,16},{8,24},{16,0},{24,8},{1,17},{9,25},{17,1},{25,9},{2,18},{10... | collective-permute-start | bytes 1179656 | tf_op jit(solution)/shard_map/ppermute | solution.py:628
  308.3 26.1 %collective-permute-start.12 = (bf16[2,2,192,256]{3,2,1,0:T(8,128)(2,1)}, bf16[2,2,192,256]{3,2,1,0:T(8,128)(2,1)S(1)}, u32[]{:S(2)}, u32[]{:S(2)}) collective-permute-start(bf16[2,2,192,256]{3,2,1,0:T(8,128)(2,1)} %get-tuple-element.60), channel_id=1, source_target_pairs={{0,24},{8,0},{16,8},{24,16},{1,25},{9,1},{17,9},{25,17},{2,26},{10... | collective-permute-start | bytes 1179656 | tf_op jit(solution)/shard_map/ppermute | solution.py:628
  318.0 16.4 %copy-start.36 = (bf16[2,2,192,256]{3,2,1,0:T(8,128)(2,1)}, bf16[2,2,192,256]{3,2,1,0:T(8,128)(2,1)S(1)}, u32[]{:S(2)}) copy-start(bf16[2,2,192,256]{3,2,1,0:T(8,128)(2,1)S(1)} %collective-permute-done.10) | copy-start | bytes 1179652
  341.7 72.0 %all-to-all-start.2 = ((bf16[8,2,192,256]{3,2,1,0:T(8,128)(2,1)}), bf16[8,2,192,256]{3,2,1,0:T(8,128)(2,1)S(1)}, u32[]{:S(2)}, u32[]{:S(2)}) async-start(bf16[8,2,192,256]{3,2,1,0:T(8,128)(2,1)} %y_inverse.3), calls=%async_computation.2 | async-start | bytes 3145728 | tf_op jit(solution)/shard_map/all_to_all | solution.py:694
  355.9 18.8 %collective-permute-start.22 = (bf16[16,192]{1,0:T(8,128)(2,1)}, bf16[16,192]{1,0:T(8,128)(2,1)S(1)}, u32[]{:S(2)}, u32[]{:S(2)}) collective-permute-start(bf16[16,192]{1,0:T(8,128)(2,1)} %get-tuple-element.74), channel_id=1, source_target_pairs={{0,8},{8,16},{16,24},{24,0},{1,9},{9,17},{17,25},{25,1},{2,10},{10... | collective-permute-start | bytes 18440 | tf_op jit(solution)/shard_map/ppermute | solution.py:395
  364.7 10.0 %collective-permute-start.23 = (bf16[16,192]{1,0:T(8,128)(2,1)}, bf16[16,192]{1,0:T(8,128)(2,1)S(1)}, u32[]{:S(2)}, u32[]{:S(2)}) collective-permute-start(bf16[16,192]{1,0:T(8,128)(2,1)} %get-tuple-element.75), channel_id=1, source_target_pairs={{8,0},{16,8},{24,16},{0,24},{9,1},{17,9},{25,17},{1,25},{10,2},{18... | collective-permute-start | bytes 18440 | tf_op jit(solution)/shard_map/ppermute | solution.py:395
  364.7 10.0 %collective-permute-start.24 = (bf16[16,256]{1,0:T(8,128)(2,1)}, bf16[16,256]{1,0:T(8,128)(2,1)S(1)}, u32[]{:S(2)}, u32[]{:S(2)}) collective-permute-start(bf16[16,256]{1,0:T(8,128)(2,1)} %get-tuple-element.76), channel_id=1, source_target_pairs={{0,1},{1,2},{2,3},{3,4},{4,5},{5,6},{6,7},{7,0},{8,9},{9,10},{10,1... | collective-permute-start | bytes 24584 | tf_op jit(solution)/shard_map/ppermute | solution.py:395
  365.0 9.8 %collective-permute-start.25 = (bf16[16,256]{1,0:T(8,128)(2,1)}, bf16[16,256]{1,0:T(8,128)(2,1)S(1)}, u32[]{:S(2)}, u32[]{:S(2)}) collective-permute-start(bf16[16,256]{1,0:T(8,128)(2,1)} %get-tuple-element.77), channel_id=1, source_target_pairs={{1,0},{2,1},{3,2},{4,3},{5,4},{6,5},{7,6},{0,7},{9,8},{10,9},{11,1... | collective-permute-start | bytes 24584 | tf_op jit(solution)/shard_map/ppermute | solution.py:395
  388.7 16.2 %collective-permute-start.26 = (bf16[16,192]{1,0:T(8,128)(2,1)}, bf16[16,192]{1,0:T(8,128)(2,1)S(1)}, u32[]{:S(2)}, u32[]{:S(2)}) collective-permute-start(bf16[16,192]{1,0:T(8,128)(2,1)} %get-tuple-element.79), channel_id=1, source_target_pairs={{0,8},{8,16},{16,24},{24,0},{1,9},{9,17},{17,25},{25,1},{2,10},{10... | collective-permute-start | bytes 18440 | tf_op jit(solution)/shard_map/ppermute | solution.py:395
  390.7 14.2 %collective-permute-start.27 = (bf16[16,192]{1,0:T(8,128)(2,1)}, bf16[16,192]{1,0:T(8,128)(2,1)S(1)}, u32[]{:S(2)}, u32[]{:S(2)}) collective-permute-start(bf16[16,192]{1,0:T(8,128)(2,1)} %get-tuple-element.80), channel_id=1, source_target_pairs={{8,0},{16,8},{24,16},{0,24},{9,1},{17,9},{25,17},{1,25},{10,2},{18... | collective-permute-start | bytes 18440 | tf_op jit(solution)/shard_map/ppermute | solution.py:395
  392.5 12.4 %collective-permute-start.28 = (bf16[16,256]{1,0:T(8,128)(2,1)}, bf16[16,256]{1,0:T(8,128)(2,1)S(1)}, u32[]{:S(2)}, u32[]{:S(2)}) collective-permute-start(bf16[16,256]{1,0:T(8,128)(2,1)} %get-tuple-element.81), channel_id=1, source_target_pairs={{0,1},{1,2},{2,3},{3,4},{4,5},{5,6},{6,7},{7,0},{8,9},{9,10},{10,1... | collective-permute-start | bytes 24584 | tf_op jit(solution)/shard_map/ppermute | solution.py:395
  392.5 12.4 %collective-permute-start.29 = (bf16[16,256]{1,0:T(8,128)(2,1)}, bf16[16,256]{1,0:T(8,128)(2,1)S(1)}, u32[]{:S(2)}, u32[]{:S(2)}) collective-permute-start(bf16[16,256]{1,0:T(8,128)(2,1)} %get-tuple-element.82), channel_id=1, source_target_pairs={{1,0},{2,1},{3,2},{4,3},{5,4},{6,5},{7,6},{0,7},{9,8},{10,9},{11,1... | collective-permute-start | bytes 24584 | tf_op jit(solution)/shard_map/ppermute | solution.py:395
  420.1 16.2 %collective-permute-start.30 = (bf16[16,192]{1,0:T(8,128)(2,1)}, bf16[16,192]{1,0:T(8,128)(2,1)S(1)}, u32[]{:S(2)}, u32[]{:S(2)}) collective-permute-start(bf16[16,192]{1,0:T(8,128)(2,1)} %get-tuple-element.84), channel_id=1, source_target_pairs={{0,8},{8,16},{16,24},{24,0},{1,9},{9,17},{17,25},{25,1},{2,10},{10... | collective-permute-start | bytes 18440 | tf_op jit(solution)/shard_map/ppermute | solution.py:395
  420.3 16.0 %collective-permute-start.31 = (bf16[16,192]{1,0:T(8,128)(2,1)}, bf16[16,192]{1,0:T(8,128)(2,1)S(1)}, u32[]{:S(2)}, u32[]{:S(2)}) collective-permute-start(bf16[16,192]{1,0:T(8,128)(2,1)} %get-tuple-element.85), channel_id=1, source_target_pairs={{8,0},{16,8},{24,16},{0,24},{9,1},{17,9},{25,17},{1,25},{10,2},{18... | collective-permute-start | bytes 18440 | tf_op jit(solution)/shard_map/ppermute | solution.py:395
  423.9 12.4 %collective-permute-start.32 = (bf16[16,256]{1,0:T(8,128)(2,1)}, bf16[16,256]{1,0:T(8,128)(2,1)S(1)}, u32[]{:S(2)}, u32[]{:S(2)}) collective-permute-start(bf16[16,256]{1,0:T(8,128)(2,1)} %get-tuple-element.86), channel_id=1, source_target_pairs={{0,1},{1,2},{2,3},{3,4},{4,5},{5,6},{6,7},{7,0},{8,9},{9,10},{10,1... | collective-permute-start | bytes 24584 | tf_op jit(solution)/shard_map/ppermute | solution.py:395
  423.9 12.4 %collective-permute-start.33 = (bf16[16,256]{1,0:T(8,128)(2,1)}, bf16[16,256]{1,0:T(8,128)(2,1)S(1)}, u32[]{:S(2)}, u32[]{:S(2)}) collective-permute-start(bf16[16,256]{1,0:T(8,128)(2,1)} %get-tuple-element.87), channel_id=1, source_target_pairs={{1,0},{2,1},{3,2},{4,3},{5,4},{6,5},{7,6},{0,7},{9,8},{10,9},{11,1... | collective-permute-start | bytes 24584 | tf_op jit(solution)/shard_map/ppermute | solution.py:395
  (34 other events, 49.9 us)

commit v3 on v2

--- a/solution.py
+++ b/solution.py
@@ -25,12 +25,16 @@
 BACK_ORDER = (2, 0, 1)
 
 
-def params(megabytes=56, **extra):
-    return pltpu.CompilerParams(vmem_limit_bytes=megabytes * 1024 * 1024, **extra)
+def params(megabytes=56):
+    return pltpu.CompilerParams(vmem_limit_bytes=megabytes * 1024 * 1024)
 
 
 def cost(flops, nbytes):
     return pl.CostEstimate(flops=int(flops), bytes_accessed=int(nbytes), transcendentals=0)
+
+
+def tied(after):
+    return [pl.BlockSpec(memory_space=pl.ANY)] * len(after)
 
 
 def trig(first, second, length):
@@ -115,20 +119,24 @@
     return layers
 
 
-ROWS = 32
+ROWS = 96
+
+
+def tiles(height, width):
+    for row in range(0, height, 16):
+        for column in range(0, width, 128):
+            yield row, pl.ds(row, 16), pl.ds(column, 128)
 
 
 def depth_forward_kernel(values_ref, planes_ref):
-    height = values_ref.shape[2]
-    rows = min(16, height)
-    for start in range(0, height, rows):
-        part = pl.ds(start, rows)
-        spectrum = depth_forward([values_ref[0, n, part, :] for n in range(Z)])
+    _, _, height, width = values_ref.shape
+    for _, rows, columns in tiles(height, width):
+        spectrum = depth_forward([values_ref[0, n, rows, columns] for n in range(Z)])
         for k, (cos_part, sin_part) in enumerate(spectrum):
-            planes_ref[2 * k, part, :] = cos_part.astype(bf16)
+            planes_ref[2 * k, rows, columns] = cos_part.astype(bf16)
             if sin_part is None:
                 sin_part = jnp.zeros_like(cos_part)
-            planes_ref[2 * k + 1, part, :] = sin_part.astype(bf16)
+            planes_ref[2 * k + 1, rows, columns] = sin_part.astype(bf16)
 
 
 def depth_transform(values, component):
@@ -145,13 +153,14 @@
     )(values)
 
 
-def y_transform(me, table, columns, blocks, halves):
+def y_transform(me, table, columns, blocks, halves, after):
     _, planes, _, width = columns.shape
     modes = HALF_Y // (blocks * halves)
     rows = Y // blocks
     shape = (halves, planes, 2, modes, width)
 
-    def kernel(me_ref, table_ref, columns_ref, *outs):
+    def kernel(me_ref, table_ref, columns_ref, *refs):
+        outs = refs[len(after) :]
         shift = pl.program_id(0)
         for plane in range(planes):
             column = columns_ref[:, plane].reshape(Y, width)
@@ -171,17 +180,18 @@
             in_specs=[
                 pl.BlockSpec((rows, Y), lambda j, me: (lax.rem(me[0] + j, blocks), 0)),
                 pl.BlockSpec(columns.shape, lambda j, me: (0, 0, 0, 0)),
-            ],
+            ]
+            + tied(after),
             out_specs=[pl.BlockSpec(shape, lambda j, me: (0, 0, 0, 0, 0))] * blocks,
         ),
         out_shape=[jax.ShapeDtypeStruct(shape, bf16)] * blocks,
-        compiler_params=params(),
+        compiler_params=params(24),
         cost_estimate=cost(2 * planes * Y * Y * width, 2 * Y * Y + 4 * planes * Y * width),
         name="y_transform",
-    )(me, table, columns)
-
-
-def y_inverse(me, table, modes, size_y):
+    )(me, table, columns, *after)
+
+
+def y_inverse(me, table, modes, size_y, after):
     blocks = len(modes)
     halves, planes, _, _, width = modes[0].shape
     height = Y // size_y
@@ -189,7 +199,7 @@
     rows = Y // blocks
 
     def kernel(me_ref, table_ref, *refs):
-        parts, rows_ref, held = refs[:blocks], refs[blocks], refs[blocks + 1]
+        parts, rows_ref, held = refs[:blocks], refs[-2], refs[-1]
 
         @pl.when(pl.program_id(0) == 0)
         def _():
@@ -210,14 +220,15 @@
             pl.BlockSpec(memory_space=pltpu.SMEM),
             pl.BlockSpec((count * height, Y), lambda j: (j, 0)),
         ]
-        + [pl.BlockSpec(modes[0].shape, lambda j: (0, 0, 0, 0, 0))] * blocks,
+        + [pl.BlockSpec(modes[0].shape, lambda j: (0, 0, 0, 0, 0))] * blocks
+        + tied(after),
         out_specs=pl.BlockSpec((count, planes, height, width), lambda j: (j, 0, 0, 0)),
         out_shape=jax.ShapeDtypeStruct((size_y, planes, height, width), bf16),
         scratch_shapes=[pltpu.VMEM((planes, Y, width), bf16)],
-        compiler_params=params(),
+        compiler_params=params(24),
         cost_estimate=cost(2 * planes * Y * Y * width, 2 * Y * Y + 4 * planes * Y * width),
         name="y_inverse",
-    )(me, table, *modes)
+    )(me, table, *modes, *after)
 
 
 def x_transform(me, table, modes, after):
@@ -241,11 +252,11 @@
             pl.BlockSpec((X, X), lambda j: (0, 0)),
         ]
         + [pl.BlockSpec((1, 2, count, width), lambda j: (j, 0, 0, 0))] * blocks
-        + [pl.BlockSpec(memory_space=pl.ANY)] * len(after),
+        + tied(after),
         out_specs=pl.BlockSpec((1, 2, count, X), lambda j: (j, 0, 0, 0)),
         out_shape=jax.ShapeDtypeStruct((2, 2, count, X), f32),
         scratch_shapes=[pltpu.VMEM((2 * count, X), bf16)],
-        compiler_params=params(),
+        compiler_params=params(24),
         cost_estimate=cost(8 * count * X * X, 2 * X * X + 24 * count * X),
         name="x_transform",
     )(me, table, *modes, *after)
@@ -304,7 +315,7 @@
         out[...] = back.astype(bf16).reshape(2, 2, count, width)
 
 
-def curl_inverse(where, table, spectra, component, blocks):
+def curl_inverse(where, table, spectra, component, blocks, after):
     (plus_axis, plus), (minus_axis, minus) = CURL[component]
     total = spectra[plus].shape[2]
     width = X // blocks
@@ -312,7 +323,7 @@
     spec = pl.BlockSpec((2, 2, count, X), lambda j: (0, 0, j, 0))
 
     def kernel(*refs):
-        curl_kernel((plus_axis, minus_axis), *refs)
+        curl_kernel((plus_axis, minus_axis), *refs[:4], *refs[4 + len(after) :])
 
     return pl.pallas_call(
         kernel,
@@ -322,13 +333,14 @@
             pl.BlockSpec((X, X), lambda j: (0, 0)),
             spec,
             spec,
-        ],
+        ]
+        + tied(after),
         out_specs=[pl.BlockSpec((2, 2, count, width), lambda j: (0, 0, j, 0))] * blocks,
         out_shape=[jax.ShapeDtypeStruct((2, 2, total, width), bf16)] * blocks,
-        compiler_params=params(),
+        compiler_params=params(24),
         cost_estimate=cost(8 * total * X * X, 2 * X * X + 40 * total * X),
         name="curl_inverse",
-    )(where, table, spectra[plus], spectra[minus])
+    )(where, table, spectra[plus], spectra[minus], *after)
 
 
 def side_columns(planes):
@@ -396,25 +408,30 @@
 
 
 def adjoint_kernel(planes_ref, cotangent_ref, *refs):
-    adjoint_ref, first_x, last_x, first_y, last_y = refs[-5:]
-    height = planes_ref.shape[1]
+    adjoint_ref, first_x, last_x, first_y, last_y, held = refs[-6:]
+    _, height, width = held.shape
     scale = 1.0 / (X * Y * Z)
-    rows = 16
-    for start in range(0, height, rows):
-        part = pl.ds(start, rows)
+    base = pl.program_id(0) * ROWS
+    for row, rows, columns in tiles(ROWS, width):
+        place = pl.ds(pl.multiple_of(base + row, 16), 16)
         layers = depth_inverse(
-            [planes_ref[2 * k, part, :].astype(f32) for k in range(KZ)],
-            [planes_ref[2 * k + 1, part, :].astype(f32) for k in range(KZ)],
+            [planes_ref[2 * k, rows, columns].astype(f32) for k in range(KZ)],
+            [planes_ref[2 * k + 1, rows, columns].astype(f32) for k in range(KZ)],
         )
         for n in range(Z):
-            adjoint_ref[n, part, :] = cotangent_ref[0, n, part, :] + layers[n] * scale
-    first, last = side_columns([adjoint_ref[n].astype(bf16) for n in range(Z)])
-    first_x[...] = first
-    last_x[...] = last
-    first_y[...] = jnp.concatenate([adjoint_ref[n, 0:1, :] for n in range(Z)], 0).astype(bf16)
-    last_y[...] = jnp.concatenate(
-        [adjoint_ref[n, height - 1 : height, :] for n in range(Z)], 0
-    ).astype(bf16)
+            value = cotangent_ref[0, n, rows, columns] + layers[n] * scale
+            adjoint_ref[n, rows, columns] = value
+            held[n, place, columns] = value.astype(bf16)
+
+    @pl.when(pl.program_id(0) == pl.num_programs(0) - 1)
+    def _():
+        first, last = side_columns([held[n] for n in range(Z)])
+        first_x[...] = first
+        last_x[...] = last
+        top = [held[n, 0:16, :].astype(f32)[0:1] for n in range(Z)]
+        bottom = [held[n, height - 16 : height, :].astype(f32)[15:16] for n in range(Z)]
+        first_y[...] = jnp.concatenate(top, 0).astype(bf16)
+        last_y[...] = jnp.concatenate(bottom, 0).astype(bf16)
 
 
 def make_adjoint(planes, cotangent, component, after):
@@ -425,14 +442,14 @@
     row_spec = pl.BlockSpec((Z, width), lambda j: (0, 0))
     return pl.pallas_call(
         adjoint_kernel,
-        grid=(1,),
+        grid=(height // ROWS,),
         in_specs=[
-            pl.BlockSpec((Z, height, width), lambda j: (0, 0, 0)),
-            pl.BlockSpec((1, Z, height, width), lambda j: (component, 0, 0, 0)),
+            pl.BlockSpec((Z, ROWS, width), lambda j: (0, j, 0)),
+            pl.BlockSpec((1, Z, ROWS, width), lambda j: (component, 0, j, 0)),
         ]
-        + [pl.BlockSpec(memory_space=pl.ANY)] * len(after),
+        + tied(after),
         out_specs=[
-            pl.BlockSpec((Z, height, width), lambda j: (0, 0, 0)),
+            pl.BlockSpec((Z, ROWS, width), lambda j: (0, j, 0)),
             column_spec,
             column_spec,
             row_spec,
@@ -445,6 +462,7 @@
             row,
             row,
         ],
+        scratch_shapes=[pltpu.VMEM((Z, height, width), bf16)],
         compiler_params=params(),
         cost_estimate=cost(70 * Z * height * width, 10 * Z * height * width),
         name="make_adjoint",
@@ -467,7 +485,7 @@
 def grad_vort_kernel(
     component, slope_x, slope_y, velocity, adjoint, low_x, high_x, low_y, high_y, *refs
 ):
-    before, after = refs if len(refs) == 2 else (None, refs[0])
+    before, after = refs
     height, width = velocity.shape[2], velocity.shape[3]
     first = pl.program_id(0) * LAYERS
     ends = spread_columns(low_x[0], high_x[0], first, LAYERS, width)
@@ -493,13 +511,14 @@
             after[j, k] = term
 
 
-def add_grad_vort(component, slopes, velocity, adjoint, halos, before):
+def add_grad_vort(component, slopes, velocity, adjoint, halos, before, after):
     _, _, height, width = velocity.shape
     slope_x, slope_y = slopes
     whole = lambda shape: pl.BlockSpec(shape, lambda n: (0,) * len(shape))
     column = pl.BlockSpec((1, Z, height), lambda n: (component, 0, 0))
     row = pl.BlockSpec((1, Z, width), lambda n: (component, 0, 0))
     sums = pl.BlockSpec((3, LAYERS, height, width), lambda n: (0, n, 0, 0))
+    sums_before = pl.BlockSpec((3, LAYERS, height, width), lambda n: (0, n, 0, 0))
     operands = [slope_x, slope_y, velocity, adjoint, *halos]
     in_specs = [
         whole((width, width)),
@@ -515,15 +534,15 @@
     if before is not None:
         aliases = {len(operands): 0}
         operands.append(before)
-        in_specs.append(sums)
+        in_specs.append(sums_before)
 
     def kernel(*refs):
-        grad_vort_kernel(component, *refs)
+        grad_vort_kernel(component, *refs[:8], None if before is None else refs[8], refs[-1])
 
     return pl.pallas_call(
         kernel,
         grid=(Z // LAYERS,),
-        in_specs=in_specs,
+        in_specs=in_specs + tied(after),
         out_specs=sums,
         out_shape=jax.ShapeDtypeStruct((3, Z, height, width), f32),
         input_output_aliases=aliases,
@@ -532,7 +551,7 @@
             2 * Z * height * width * (width + height), Z * height * width * (18 + 12 * len(aliases))
         ),
         name="add_grad_vort",
-    )(*operands)
+    )(*operands, *after)
 
 
 def grad_vel_kernel(slope_x, vorticity, vorticity_above, vorticity_below, adjoint, *refs):
@@ -545,8 +564,8 @@
         return one.astype(f32) * other.astype(f32)
 
     ends = spread_columns(
-        times(vort_low_x[...], low_x[...]),
-        times(vort_high_x[...], high_x[...]),
+        times(vort_low_x[0], low_x[...]),
+        times(vort_high_x[0], high_x[...]),
         first,
         LAYERS,
         width,
@@ -563,8 +582,8 @@
     for k in range(LAYERS):
         n = first + k
         padded[k, 8 : 8 + height, :] = vorticity[1, k].astype(f32) * values[k]
-        padded[k, 7:8, :] = pick_row(vort_low_y[...], n) * pick_row(low_y[...], n)
-        padded[k, 8 + height : 9 + height, :] = pick_row(vort_high_y[...], n) * pick_row(
+        padded[k, 7:8, :] = pick_row(vort_low_y[0], n) * pick_row(low_y[...], n)
+        padded[k, 8 + height : 9 + height, :] = pick_row(vort_high_y[0], n) * pick_row(
             high_y[...], n
         )
         total = (padded[k, 9 : 9 + height, :] - padded[k, 7 : 7 + height, :]) + (
@@ -574,22 +593,24 @@
         after[0, k] = total * -step_size
 
 
-def write_grad_vel(component, slope_x, vorticity, adjoint, vort_halos, halos, before):
+def write_grad_vel(component, slope_x, vorticity, adjoint, saved_halos, halos, before, after):
     _, _, height, width = vorticity.shape
     whole = lambda shape: pl.BlockSpec(shape, lambda n: (0,) * len(shape))
     column = whole((Z, height))
     row = whole((Z, width))
-    operands = [slope_x, vorticity, vorticity, vorticity, adjoint, *vort_halos, *halos]
+    saved_column = pl.BlockSpec((1, Z, height), lambda n: (3, 0, 0))
+    saved_row = pl.BlockSpec((1, Z, width), lambda n: (3, 0, 0))
+    operands = [slope_x, vorticity, vorticity, vorticity, adjoint, *saved_halos, *halos]
     in_specs = [
         whole((width, width)),
         pl.BlockSpec((3, LAYERS, height, width), lambda n: (0, n, 0, 0)),
         pl.BlockSpec((1, 1, height, width), lambda n: (2, lax.rem((n + 1) * LAYERS, Z), 0, 0)),
         pl.BlockSpec((1, 1, height, width), lambda n: (2, lax.rem(n * LAYERS + Z - 1, Z), 0, 0)),
         whole((Z, height, width)),
-        column,
-        column,
-        row,
-        row,
+        saved_column,
+        saved_column,
+        saved_row,
+        saved_row,
         column,
         column,
         row,
@@ -603,7 +624,7 @@
     return pl.pallas_call(
         grad_vel_kernel,
         grid=(Z // LAYERS,),
-        in_specs=in_specs,
+        in_specs=in_specs + tied(after),
         out_specs=pl.BlockSpec((1, LAYERS, height, width), lambda n: (component, n, 0, 0)),
         out_shape=jax.ShapeDtypeStruct((3, Z, height, width), f32),
         input_output_aliases=aliases,
@@ -611,7 +632,7 @@
         compiler_params=params(),
         cost_estimate=cost(4 * Z * height * width * width, Z * height * width * 16),
         name="write_grad_vel",
-    )(*operands)
+    )(*operands, *after)
 
 
 def pair_exchange(parts, axis, mine):
@@ -662,49 +683,73 @@
         jnp.concatenate([velocity[:, :, height - 1], vorticity[1:2, :, height - 1]]),
         "gy",
     )
-    velocity_halos = (low_x, high_x, low_y, high_y)
-    vorticity_halos = (low_x[3], high_x[3], low_y[3], high_y[3])
-
-    spectra = {}
-    for component in FORWARD_ORDER:
+    saved_halos = (low_x, high_x, low_y, high_y)
+    edges = (velocity_first, vorticity_first)
+
+    sent = {}
+    for place, component in enumerate(FORWARD_ORDER):
         layers = depth_transform(cot_vel, component)
         columns = lax.all_to_all(
             layers.reshape(size_y, planes, height, width), "gy", 0, 0, tiled=True
         )
-        parts = y_transform(me, y_table, columns, size_x, halves)
+        parts = y_transform(
+            me, y_table, columns, size_x, halves, edges if place == 1 else ()
+        )
         if halves == 1:
             parts = [part[0] for part in parts]
         else:
             parts = [pair_exchange(part[:, 0], "gy", half) for part in parts]
-        first = component == FORWARD_ORDER[0]
-        spectra[component] = x_transform(
-            me, x_table, shifted(parts, "gx"), velocity_halos if first else ()
-        )
-
-    grad_vort = None
-    grad_vel = None
+        sent[component] = parts
+    spectra = {}
+    for place, component in enumerate(FORWARD_ORDER):
+        after = ((sent[FORWARD_ORDER[2]][0],), saved_halos, ())[place]
+        spectra[component] = x_transform(me, x_table, shifted(sent[component], "gx"), after)
+
+    returned = {}
+    after = ()
     for component in BACK_ORDER:
-        parts = curl_inverse(where, x_back_table, spectra, component, size_x)
+        parts = curl_inverse(where, x_back_table, spectra, component, size_x, after)
+        after = (parts[0],)
         parts = shifted(parts, "gx")
         if halves == 1:
             parts = [part[None] for part in parts]
         else:
             parts = [pair_exchange(part, "gy", half)[:, None] for part in parts]
-        rows = y_inverse(me, y_back_table, parts, size_y)
+        returned[component] = parts
+
+    def rows_of(component, after):
+        return y_inverse(me, y_back_table, returned[component], size_y, after)
+
+    def adjoint_of(component, rows, after):
         layers = lax.all_to_all(rows, "gy", 0, 0, tiled=True)
         adjoint, first_x, last_x, first_y, last_y = make_adjoint(
-            layers.reshape(Z, height, width),
-            cot_vort,
-            component,
-            () if grad_vort is None else (grad_vort, grad_vel),
-        )
-        halos = exchange(first_x, last_x, "gx") + exchange(first_y, last_y, "gy")
-        grad_vort = add_grad_vort(
-            component, (slope_x, slope_y), velocity, adjoint, velocity_halos, grad_vort
-        )
-        grad_vel = write_grad_vel(
-            component, slope_x, vorticity, adjoint, vorticity_halos, halos, grad_vel
-        )
+            layers.reshape(Z, height, width), cot_vort, component, after
+        )
+        return adjoint, exchange(first_x, last_x, "gx") + exchange(first_y, last_y, "gy")
+
+    def vort_of(component, adjoint, before, after):
+        return add_grad_vort(
+            component, (slope_x, slope_y), velocity, adjoint, saved_halos, before, after
+        )
+
+    def vel_of(component, adjoint, halos, before, after):
+        return write_grad_vel(
+            component, slope_x, vorticity, adjoint, saved_halos, halos, before, after
+        )
+
+    one, two, three = BACK_ORDER
+    rows_one = rows_of(one, ())
+    rows_two = rows_of(two, (rows_one,))
+    adjoint_one, halos_one = adjoint_of(one, rows_one, (rows_two,))
+    grad_vort = vort_of(one, adjoint_one, None, ())
+    adjoint_two, halos_two = adjoint_of(two, rows_two, (grad_vort,))
+    rows_three = rows_of(three, (adjoint_two,) + halos_two)
+    grad_vel = vel_of(one, adjoint_one, halos_one, None, (rows_three,))
+    grad_vort = vort_of(two, adjoint_two, grad_vort, (rows_three,))
+    grad_vel = vel_of(two, adjoint_two, halos_two, grad_vel, ())
+    adjoint_three, halos_three = adjoint_of(three, rows_three, (grad_vort, grad_vel))
+    grad_vort = vort_of(three, adjoint_three, grad_vort, ())
+    grad_vel = vel_of(three, adjoint_three, halos_three, grad_vel, (grad_vort,))
     return grad_vort, grad_vel
 
 

time: 447 us -> 416 us (0.931)
  Pallas kernels: 168 us -> 131 us
  waiting for transfers between devices: 114 us -> 141 us
  starting transfers between devices: 140 us -> 114 us
  local copies, waits for them, and re-layouts: 19.7 us -> 27.9 us
    ppermute x18, waiting for transfers between devices: 64.9 us -> 107 us  [shifted(): lax.ppermute(parts[s], axis, [(i, (i + s) % count) for i in range(count)])]
    ppermute x16, starting transfers between devices: 54.4 us -> 32.6 us  [exchange(): return (lax.ppermute(last, axis, up), lax.ppermute(first, axis, down))]
    unnamed x88 -> x132, local copies, waits for them, and re-layouts: 12.5 us -> 25.9 us
    ppermute x16, waiting for transfers between devices: 17.3 us -> 5.72 us  [exchange(): return (lax.ppermute(last, axis, up), lax.ppermute(first, axis, down))]
    pallas_call x3, Pallas kernels: 19.3 us -> 10.6 us  [y_inverse(): pl.pallas_call(kernel, grid=(size_y // count,), in_specs=[pl.BlockSpec(me...]
    pallas_call x3, Pallas kernels: 27.7 us -> 20.4 us  [y_transform(): pl.pallas_call(kernel, grid_spec=pltpu.PrefetchScalarGridSpec(num_scalar_...]
    pallas_call x3, Pallas kernels: 17.5 us -> 10.3 us  [curl_inverse(): pl.pallas_call(kernel, grid=(total // count,), in_specs=[pl.BlockSpec(mem...]
    pallas_call x3, Pallas kernels: 15.7 us -> 8.57 us  [x_transform(): pl.pallas_call(kernel, grid=(2,), in_specs=[pl.BlockSpec(memory_space=plt...]
  transfers between devices with their start and end apart: 40 -> 40, of which waited for: 10 -> 16; matrix products, arithmetic and copies ran while one was open for 2% -> 1% of each run, Pallas kernels for 34% -> 24%
where the time goes in v3:
time: 416 us; the launch traced here: 415 us
  waiting for transfers between devices  141 us (34%)
  Pallas kernels  131 us (31%)
  starting transfers between devices  114 us (27%)
  local copies, waits for them, and re-layouts  27.9 us (7%)
    ppermute x18, waiting for transfers between devices, shifted(): lax.ppermute(parts[s], axis, [(i, (i + s) % count) for i in range(count)])  107 us
    ppermute x18, starting transfers between devices, shifted(): lax.ppermute(parts[s], axis, [(i, (i + s) % count) for i in range(count)])  56 us
    ppermute x16, starting transfers between devices, exchange(): return (lax.ppermute(last, axis, up), lax.ppermute(first, axis, down))  32.6 us
    all_to_all x3, waiting for transfers between devices, local(): lax.all_to_all(layers.reshape(size_y, planes, height, width), 'gy', 0, 0,...  28.5 us
    pallas_call x3, Pallas kernels, add_grad_vort(): pl.pallas_call(kernel, grid=(Z // LAYERS,), in_specs=in_specs + tied(afte...  26.8 us
    unnamed x132, local copies, waits for them, and re-layouts  25.9 us
    pallas_call x3, Pallas kernels, write_grad_vel(): pl.pallas_call(grad_vel_kernel, grid=(Z // LAYERS,), in_specs=in_specs +...  23 us
    pallas_call x3, Pallas kernels, y_transform(): pl.pallas_call(kernel, grid_spec=pltpu.PrefetchScalarGridSpec(num_scalar_...  20.4 us
  transfers between devices with their start and end apart: 40, of which 16 were waited for; matrix products, arithmetic and copies ran while one was open for 1% of the time, Pallas kernels for 24%

profile of v3, /device:TPU:0, one launch (start us, length us, event | category | flops | bytes accessed | tf_op | source)
XLA Modules:
  0.0 414.9 jit_solution(16313149963375862642)
XLA Ops:
  3.8 5.2 %all-to-all-start = ((bf16[8,2,192,256]{3,2,1,0:T(8,128)(2,1)}), bf16[8,2,192,256]{3,2,1,0:T(8,128)(2,1)S(1)}, u32[]{:S(2)}, u32[]{:S(2)}) async-start(bf16[8,2,192,256]{3,2,1,0:T(8,128)(2,1)} %bitcast.75), calls=%async_computation | async-start | bytes 3145728 | tf_op jit(solution)/shard_map/all_to_all | solution.py:692
  12.1 17.9 %all-to-all-done.columns_ref = bf16[8,2,192,256]{3,2,1,0:T(8,128)(2,1)S(1)} async-done(((bf16[8,2,192,256]{3,2,1,0:T(8,128)(2,1)}), bf16[8,2,192,256]{3,2,1,0:T(8,128)(2,1)S(1)}, u32[]{:S(2)}, u32[]{:S(2)}) %all-to-all-start) | async-done | bytes 1572896 | tf_op jit(solution)/shard_map/all_to_all | solution.py:692
  30.0 3.6 all-to-all-start.2
  39.4 4.6 %edge_columns.2 = (bf16[3,16,192]{2,1,0:T(8,128)(2,1)}, bf16[3,16,192]{2,1,0:T(8,128)(2,1)}) custom-call(bf16[3,16,192,256]{3,2,1,0:T(8,128)(2,1)} %refs_2_.5), custom_call_target="tpu_custom_call" | custom-call | flops 150994944 | bytes 4718592 | tf_op jit(solution)/shard_map/edge_columns/pallas_call | solution.py:389
  44.0 10.6 %all-to-all-done.2.columns_ref = bf16[8,2,192,256]{3,2,1,0:T(8,128)(2,1)S(1)} async-done(((bf16[8,2,192,256]{3,2,1,0:T(8,128)(2,1)}), bf16[8,2,192,256]{3,2,1,0:T(8,128)(2,1)S(1)}, u32[]{:S(2)}, u32[]{:S(2)}) %all-to-all-start.2) | async-done | bytes 1572896 | tf_op jit(solution)/shard_map/all_to_all | solution.py:692
  54.5 3.6 all-to-all-start.1
  58.2 3.7 collective-permute-start.10
  67.7 7.0 %y_transform.3 = (bf16[1,2,2,192,256]{4,3,2,1,0:T(8,128)(2,1)S(1)}, bf16[1,2,2,192,256]{4,3,2,1,0:T(8,128)(2,1)}, bf16[1,2,2,192,256]{4,3,2,1,0:T(8,128)(2,1)S(1)}, bf16[1,2,2,192,256]{4,3,2,1,0:T(8,128)(2,1)S(1)}) custom-call(s32[1]{0:T(128)} %bitcast.me_ref, bf16[1536,1536]{1,0:T(8,128)(2,1)S(1)} %copy-done.40, bf16[8,2,192,256]{3,2,1,0:T(8,128)(2,1)S(1)} %copy-done.20), custom_call_target="tpu_custom_call" | custom-call | flops 2415919104 | bytes 7864320 | tf_op jit(solution)/shard_map/y_transform/pallas_call | solution.py:175
  77.0 4.4 %collective-permute-start.1 = (bf16[2,2,192,256]{3,2,1,0:T(8,128)(2,1)}, bf16[2,2,192,256]{3,2,1,0:T(8,128)(2,1)}, u32[]{:S(2)}, u32[]{:S(2)}) collective-permute-start(bf16[2,2,192,256]{3,2,1,0:T(8,128)(2,1)} %bitcast.68), channel_id=1, source_target_pairs={{0,16},{8,24},{16,0},{24,8},{1,17},{9,25},{17,1},{25,9},{2,18},{10... | collective-permute-start | bytes 1179656 | tf_op jit(solution)/shard_map/ppermute | solution.py:649
  83.8 7.2 %y_transform.5 = (bf16[1,2,2,192,256]{4,3,2,1,0:T(8,128)(2,1)S(1)}, bf16[1,2,2,192,256]{4,3,2,1,0:T(8,128)(2,1)}, bf16[1,2,2,192,256]{4,3,2,1,0:T(8,128)(2,1)}, bf16[1,2,2,192,256]{4,3,2,1,0:T(8,128)(2,1)}) custom-call(s32[1]{0:T(128)} %bitcast.me_ref, bf16[1536,1536]{1,0:T(8,128)(2,1)S(1)} %copy-done.41, ...), custom_call_target="tpu_custom_call" | custom-call | flops 2415919104 | bytes 7864320 | tf_op jit(solution)/shard_map/y_transform/pallas_call | solution.py:175
  98.7 6.2 %y_transform.4 = (bf16[1,2,2,192,256]{4,3,2,1,0:T(8,128)(2,1)S(1)}, bf16[1,2,2,192,256]{4,3,2,1,0:T(8,128)(2,1)S(1)}, bf16[1,2,2,192,256]{4,3,2,1,0:T(8,128)(2,1)S(1)}, bf16[1,2,2,192,256]{4,3,2,1,0:T(8,128)(2,1)S(1)}) custom-call(s32[1]{0:T(128)} %bitcast.me_ref, bf16[1536,1536]{1,0:T(8,128)(2,1)S(1)} %copy-done.42, ...), custom_call_target="tpu_custom_call" | custom-call | flops 2415919104 | bytes 7864320 | tf_op jit(solution)/shard_map/y_transform/pallas_call | solution.py:175
  110.8 3.2 x_transform.3.refs_3_.refs_2_
  116.5 24.4 %collective-permute-done.7.refs_2_ = bf16[2,2,192,256]{3,2,1,0:T(8,128)(2,1)} collective-permute-done((bf16[2,2,192,256]{3,2,1,0:T(8,128)(2,1)}, bf16[2,2,192,256]{3,2,1,0:T(8,128)(2,1)}, u32[]{:S(2)}, u32[]{:S(2)}) %collective-permute-start.7) | collective-permute-done | bytes 393248 | tf_op jit(solution)/shard_map/ppermute | solution.py:649
  141.0 3.3 x_transform.5.refs_2_.refs_3_
  147.6 8.9 %collective-permute-start.19 = (bf16[2,2,192,256]{3,2,1,0:T(8,128)(2,1)S(1)}, bf16[2,2,192,256]{3,2,1,0:T(8,128)(2,1)S(1)}, u32[]{:S(2)}, u32[]{:S(2)}) collective-permute-start(bf16[2,2,192,256]{3,2,1,0:T(8,128)(2,1)S(1)} %get-tuple-element.70), channel_id=1, source_target_pairs={{0,8},{8,16},{16,24},{24,0},{1,9},{9,17},{17,25},{25,1},{2,10},{10... | collective-permute-start | bytes 1179656 | tf_op jit(solution)/shard_map/ppermute | solution.py:649
  158.9 7.1 %collective-permute-done.19 = bf16[2,2,192,256]{3,2,1,0:T(8,128)(2,1)S(1)} collective-permute-done((bf16[2,2,192,256]{3,2,1,0:T(8,128)(2,1)S(1)}, bf16[2,2,192,256]{3,2,1,0:T(8,128)(2,1)S(1)}, u32[]{:S(2)}, u32[]{:S(2)}) %collective-permute-start.19) | collective-permute-done | bytes 393248 | tf_op jit(solution)/shard_map/ppermute | solution.py:649
  166.0 14.9 %collective-permute-done.20 = bf16[2,2,192,256]{3,2,1,0:T(8,128)(2,1)S(1)} collective-permute-done((bf16[2,2,192,256]{3,2,1,0:T(8,128)(2,1)S(1)}, bf16[2,2,192,256]{3,2,1,0:T(8,128)(2,1)S(1)}, u32[]{:S(2)}, u32[]{:S(2)}) %collective-permute-start.20) | collective-permute-done | bytes 393248 | tf_op jit(solution)/shard_map/ppermute | solution.py:649
  181.9 3.3 y_inverse.3.refs_4_
  187.1 4.4 %all-to-all-start.4 = ((bf16[8,2,192,256]{3,2,1,0:T(8,128)(2,1)}), bf16[8,2,192,256]{3,2,1,0:T(8,128)(2,1)}, u32[]{:S(2)}, u32[]{:S(2)}) async-start(bf16[8,2,192,256]{3,2,1,0:T(8,128)(2,1)} %copy-done.11), calls=%async_computation.4 | async-start | bytes 3145728 | tf_op jit(solution)/shard_map/all_to_all | solution.py:724
  191.5 8.7 %collective-permute-start.3 = (bf16[2,2,192,256]{3,2,1,0:T(8,128)(2,1)}, bf16[2,2,192,256]{3,2,1,0:T(8,128)(2,1)S(1)}, u32[]{:S(2)}, u32[]{:S(2)}) collective-permute-start(bf16[2,2,192,256]{3,2,1,0:T(8,128)(2,1)} %bitcast.66), channel_id=1, source_target_pairs={{0,8},{8,16},{16,24},{24,0},{1,9},{9,17},{17,25},{25,1},{2,10},{10... | collective-permute-start | bytes 1179656 | tf_op jit(solution)/shard_map/ppermute | solution.py:649
  200.3 3.4 collective-permute-start.4
  203.7 9.7 %collective-permute-done.3.refs_1_ = bf16[2,2,192,256]{3,2,1,0:T(8,128)(2,1)S(1)} collective-permute-done((bf16[2,2,192,256]{3,2,1,0:T(8,128)(2,1)}, bf16[2,2,192,256]{3,2,1,0:T(8,128)(2,1)S(1)}, u32[]{:S(2)}, u32[]{:S(2)}) %collective-permute-start.3) | collective-permute-done | bytes 393248 | tf_op jit(solution)/shard_map/ppermute | solution.py:649
  213.3 16.5 %collective-permute-done.4.refs_2_ = bf16[2,2,192,256]{3,2,1,0:T(8,128)(2,1)S(1)} collective-permute-done((bf16[2,2,192,256]{3,2,1,0:T(8,128)(2,1)}, bf16[2,2,192,256]{3,2,1,0:T(8,128)(2,1)S(1)}, u32[]{:S(2)}, u32[]{:S(2)}) %collective-permute-start.4) | collective-permute-done | bytes 393248 | tf_op jit(solution)/shard_map/ppermute | solution.py:649
  233.6 3.2 curl_inverse.4
  236.8 9.1 %collective-permute-start.16 = (bf16[2,2,192,256]{3,2,1,0:T(8,128)(2,1)S(1)}, bf16[2,2,192,256]{3,2,1,0:T(8,128)(2,1)S(1)}, u32[]{:S(2)}, u32[]{:S(2)}) collective-permute-start(bf16[2,2,192,256]{3,2,1,0:T(8,128)(2,1)S(1)} %get-tuple-element.67), channel_id=1, source_target_pairs={{0,8},{8,16},{16,24},{24,0},{1,9},{9,17},{17,25},{25,1},{2,10},{10... | collective-permute-start | bytes 1179656 | tf_op jit(solution)/shard_map/ppermute | solution.py:649
  248.3 7.0 %collective-permute-done.16 = bf16[2,2,192,256]{3,2,1,0:T(8,128)(2,1)S(1)} collective-permute-done((bf16[2,2,192,256]{3,2,1,0:T(8,128)(2,1)S(1)}, bf16[2,2,192,256]{3,2,1,0:T(8,128)(2,1)S(1)}, u32[]{:S(2)}, u32[]{:S(2)}) %collective-permute-start.16) | collective-permute-done | bytes 393248 | tf_op jit(solution)/shard_map/ppermute | solution.py:649
  255.4 15.5 %collective-permute-done.17 = bf16[2,2,192,256]{3,2,1,0:T(8,128)(2,1)S(1)} collective-permute-done((bf16[2,2,192,256]{3,2,1,0:T(8,128)(2,1)S(1)}, bf16[2,2,192,256]{3,2,1,0:T(8,128)(2,1)S(1)}, u32[]{:S(2)}, u32[]{:S(2)}) %collective-permute-start.17) | collective-permute-done | bytes 393248 | tf_op jit(solution)/shard_map/ppermute | solution.py:649
  271.4 3.3 y_inverse.4.refs_0_
  275.8 4.3 %all-to-all-start.3 = ((bf16[8,2,192,256]{3,2,1,0:T(8,128)(2,1)}), bf16[8,2,192,256]{3,2,1,0:T(8,128)(2,1)}, u32[]{:S(2)}, u32[]{:S(2)}) async-start(bf16[8,2,192,256]{3,2,1,0:T(8,128)(2,1)} %copy-done.10), calls=%async_computation.3 | async-start | bytes 3145728 | tf_op jit(solution)/shard_map/all_to_all | solution.py:724
  283.6 3.9 curl_inverse.5
  288.3 8.7 %collective-permute-start.13 = (bf16[2,2,192,256]{3,2,1,0:T(8,128)(2,1)}, bf16[2,2,192,256]{3,2,1,0:T(8,128)(2,1)S(1)}, u32[]{:S(2)}, u32[]{:S(2)}) collective-permute-start(bf16[2,2,192,256]{3,2,1,0:T(8,128)(2,1)} %get-tuple-element.64), channel_id=1, source_target_pairs={{0,8},{8,16},{16,24},{24,0},{1,9},{9,17},{17,25},{25,1},{2,10},{10... | collective-permute-start | bytes 1179656 | tf_op jit(solution)/shard_map/ppermute | solution.py:649
  297.0 3.4 collective-permute-start.14
  300.3 4.8 %make_adjoint.3 = (f32[16,192,256]{2,1,0:T(8,128)}, bf16[16,192]{1,0:T(8,128)(2,1)}, bf16[16,192]{1,0:T(8,128)(2,1)}, bf16[16,256]{1,0:T(8,128)(2,1)}, bf16[16,256]{1,0:T(8,128)(2,1)}) custom-call(bf16[16,192,256]{2,1,0:T(8,128)(2,1)} %bitcast.35.planes_ref, f32[3,16,192,256]{3,2,1,0:T(8,128)} %cotangent_ref.5, bf16[8,2,192,256]{3,2,1,0:T(8,128)(2,1)} %copy-done.10), custom_call_target="tpu_custom_call" | custom-call | flops 55050240 | bytes 7864320 | tf_op jit(solution)/shard_map/make_adjoint/pallas_call | solution.py:443
  305.2 7.4 %add_grad_vort.3.refs_0_.refs_8_ = f32[3,16,192,256]{3,2,1,0:T(8,128)} custom-call(bf16[256,256]{1,0:T(8,128)(2,1)} %constant.37.clone.refs_0_.slope_x, bf16[192,192]{1,0:T(8,128)(2,1)} %constant.38.clone.refs_1_, bf16[3,16,192,256]{3,2,1,0:T(8,128)(2,1)} %refs_2_.5, f32[16,192,256]{2,1,0:T(8,128)} %get-tuple-element.73.refs_3_.adjoint, ...), custom_call_target="tpu_custom_call" | custom-call | flops 704643072 | bytes 14155776 | tf_op jit(solution)/shard_map/add_grad_vort/pallas_call | solution.py:542
  312.5 4.9 %make_adjoint.4 = (f32[16,192,256]{2,1,0:T(8,128)}, bf16[16,192]{1,0:T(8,128)(2,1)}, bf16[16,192]{1,0:T(8,128)(2,1)}, bf16[16,256]{1,0:T(8,128)(2,1)}, bf16[16,256]{1,0:T(8,128)(2,1)}) custom-call(bf16[16,192,256]{2,1,0:T(8,128)(2,1)} %bitcast.34.planes_ref, f32[3,16,192,256]{3,2,1,0:T(8,128)} %cotangent_ref.5, f32[3,16,192,256]{3,2,1,0:T(8,128)} %add_grad_vort.3.refs_0_.refs_8_), custom_call_target="tpu_custom_call" | custom-call | flops 55050240 | bytes 7864320 | tf_op jit(solution)/shard_map/make_adjoint/pallas_call | solution.py:443
  322.1 4.5 %collective-permute-done.14 = bf16[2,2,192,256]{3,2,1,0:T(8,128)(2,1)S(1)} collective-permute-done((bf16[2,2,192,256]{3,2,1,0:T(8,128)(2,1)}, bf16[2,2,192,256]{3,2,1,0:T(8,128)(2,1)S(1)}, u32[]{:S(2)}, u32[]{:S(2)}) %collective-permute-start.14) | collective-permute-done | bytes 393248 | tf_op jit(solution)/shard_map/ppermute | solution.py:649
  326.7 7.9 %collective-permute-start.23 = (bf16[16,192]{1,0:T(8,128)(2,1)}, bf16[16,192]{1,0:T(8,128)(2,1)S(1)}, u32[]{:S(2)}, u32[]{:S(2)}) collective-permute-start(bf16[16,192]{1,0:T(8,128)(2,1)} %get-tuple-element.76), channel_id=1, source_target_pairs={{8,0},{16,8},{24,16},{0,24},{9,1},{17,9},{25,17},{1,25},{10,2},{18... | collective-permute-start | bytes 18440 | tf_op jit(solution)/shard_map/ppermute | solution.py:407
  338.1 4.0 y_inverse.5.refs_9_.refs_8_
  342.2 4.0 all-to-all-start.5
  346.3 4.1 collective-permute-start.27
  353.1 9.7 %add_grad_vort.4.refs_0_.refs_8_ = f32[3,16,192,256]{3,2,1,0:T(8,128)} custom-call(bf16[256,256]{1,0:T(8,128)(2,1)} %constant.37.clone.refs_0_.slope_x, bf16[192,192]{1,0:T(8,128)(2,1)} %constant.38.clone.refs_1_, bf16[3,16,192,256]{3,2,1,0:T(8,128)(2,1)} %refs_2_.5, ...), custom_call_target="tpu_custom_call", output_to_operand_aliasing={{}: (8, {})} | custom-call | flops 704643072 | bytes 23592960 | tf_op jit(solution)/shard_map/add_grad_vort/pallas_call | solution.py:542
  362.9 4.1 collective-permute-done.28.refs_6_
  368.2 7.7 %write_grad_vel.3.refs_8_ = f32[3,16,192,256]{3,2,1,0:T(8,128)} custom-call(bf16[256,256]{1,0:T(8,128)(2,1)} %constant.37.clone.refs_0_.slope_x, bf16[3,16,192,256]{3,2,1,0:T(8,128)(2,1)} %vorticity_below.5, bf16[3,16,192,256]{3,2,1,0:T(8,128)(2,1)} %vorticity_below.5, bf16[3,16,192,256]{3,2,1,0:T(8,128)(2,1)} %vorticity_below.5, ...), custom_call_target="tpu_custom_call" | custom-call | flops 805306368 | bytes 12582912 | tf_op jit(solution)/shard_map/write_grad_vel/pallas_call | solution.py:624
  375.8 7.7 %write_grad_vel.4.refs_1_.refs_8_ = f32[3,16,192,256]{3,2,1,0:T(8,128)} custom-call(bf16[256,256]{1,0:T(8,128)(2,1)} %constant.37.clone.refs_0_.slope_x, bf16[3,16,192,256]{3,2,1,0:T(8,128)(2,1)} %vorticity_below.5, bf16[3,16,192,256]{3,2,1,0:T(8,128)(2,1)} %vorticity_below.5, ...), custom_call_target="tpu_custom_call", output_to_operand_aliasing={{}: (13, {})} | custom-call | flops 805306368 | bytes 12582912 | tf_op jit(solution)/shard_map/write_grad_vel/pallas_call | solution.py:624
  384.7 4.8 %make_adjoint.5 = (f32[16,192,256]{2,1,0:T(8,128)}, bf16[16,192]{1,0:T(8,128)(2,1)}, bf16[16,192]{1,0:T(8,128)(2,1)}, bf16[16,256]{1,0:T(8,128)(2,1)}, bf16[16,256]{1,0:T(8,128)(2,1)}) custom-call(bf16[16,192,256]{2,1,0:T(8,128)(2,1)} %bitcast.72, f32[3,16,192,256]{3,2,1,0:T(8,128)} %cotangent_ref.5, f32[3,16,192,256]{3,2,1,0:T(8,128)} %add_grad_vort.4.refs_0_.refs_8_, ...), custom_call_target="tpu_custom_call" | custom-call | flops 55050240 | bytes 7864320 | tf_op jit(solution)/shard_map/make_adjoint/pallas_call | solution.py:443
  389.6 4.1 collective-permute-start.31
  396.3 9.7 %add_grad_vort.5.refs_9_ = f32[3,16,192,256]{3,2,1,0:T(8,128)} custom-call(bf16[256,256]{1,0:T(8,128)(2,1)} %constant.37.clone.refs_0_.slope_x, bf16[192,192]{1,0:T(8,128)(2,1)} %constant.38.clone.refs_1_, bf16[3,16,192,256]{3,2,1,0:T(8,128)(2,1)} %refs_2_.5, f32[16,192,256]{2,1,0:T(8,128)} %get-tuple-element.83.refs_3_.adjoint, ...), custom_call_target="tpu_custom_call", output_to_operand_aliasing={{}: (8, {})} | custom-call | flops 704643072 | bytes 23592960 | tf_op jit(solution)/shard_map/add_grad_vort/pallas_call | solution.py:542
  407.3 7.7 %write_grad_vel.5 = f32[3,16,192,256]{3,2,1,0:T(8,128)} custom-call(bf16[256,256]{1,0:T(8,128)(2,1)} %constant.37.clone.refs_0_.slope_x, bf16[3,16,192,256]{3,2,1,0:T(8,128)(2,1)} %vorticity_below.5, bf16[3,16,192,256]{3,2,1,0:T(8,128)(2,1)} %vorticity_below.5, bf16[3,16,192,256]{3,2,1,0:T(8,128)(2,1)} %vorticity_below.5, ...), custom_call_target="tpu_custom_call", output_to_operand_aliasing={{}: (13, {})} | custom-call | flops 805306368 | bytes 12582912 | tf_op jit(solution)/shard_map/write_grad_vel/pallas_call | solution.py:624
  (200 shorter events, 76.2 us)
Async XLA Ops:
  3.8 26.2 %all-to-all-start = ((bf16[8,2,192,256]{3,2,1,0:T(8,128)(2,1)}), bf16[8,2,192,256]{3,2,1,0:T(8,128)(2,1)S(1)}, u32[]{:S(2)}, u32[]{:S(2)}) async-start(bf16[8,2,192,256]{3,2,1,0:T(8,128)(2,1)} %bitcast.75), calls=%async_computation | async-start | bytes 3145728 | tf_op jit(solution)/shard_map/all_to_all | solution.py:692
  30.0 24.5 %all-to-all-start.2 = ((bf16[8,2,192,256]{3,2,1,0:T(8,128)(2,1)}), bf16[8,2,192,256]{3,2,1,0:T(8,128)(2,1)S(1)}, u32[]{:S(2)}, u32[]{:S(2)}) async-start(bf16[8,2,192,256]{3,2,1,0:T(8,128)(2,1)} %bitcast.74), calls=%async_computation.2 | async-start | bytes 3145728 | tf_op jit(solution)/shard_map/all_to_all | solution.py:692
  54.5 41.8 %all-to-all-start.1 = ((bf16[8,2,192,256]{3,2,1,0:T(8,128)(2,1)}), bf16[8,2,192,256]{3,2,1,0:T(8,128)(2,1)S(1)}, u32[]{:S(2)}, u32[]{:S(2)}) async-start(bf16[8,2,192,256]{3,2,1,0:T(8,128)(2,1)} %bitcast.73), calls=%async_computation.1 | async-start | bytes 3145728 | tf_op jit(solution)/shard_map/all_to_all | solution.py:692
  58.2 33.6 %collective-permute-start.10 = (bf16[4,16,192]{2,1,0:T(8,128)(2,1)S(1)}, bf16[4,16,192]{2,1,0:T(8,128)(2,1)S(1)}, u32[]{:S(2)}, u32[]{:S(2)}) collective-permute-start(bf16[4,16,192]{2,1,0:T(8,128)(2,1)S(1)} %pad_maximum_fusion.1), channel_id=1, source_target_pairs={{8,0},{16,8},{24,16},{0,24},{9,1},{17,9},{25,17},{1,25},{10,2},{18... | collective-permute-start | bytes 73736 | tf_op jit(solution)/shard_map/ppermute | solution.py:407
  61.9 32.0 %collective-permute-start.9 = (bf16[4,16,192]{2,1,0:T(8,128)(2,1)S(1)}, bf16[4,16,192]{2,1,0:T(8,128)(2,1)S(1)}, u32[]{:S(2)}, u32[]{:S(2)}) collective-permute-start(bf16[4,16,192]{2,1,0:T(8,128)(2,1)S(1)} %pad_maximum_fusion), channel_id=1, source_target_pairs={{0,8},{8,16},{16,24},{24,0},{1,9},{9,17},{17,25},{25,1},{2,10},{10... | collective-permute-start | bytes 73736 | tf_op jit(solution)/shard_map/ppermute | solution.py:407
  77.0 16.9 %collective-permute-start = (bf16[2,2,192,256]{3,2,1,0:T(8,128)(2,1)}, bf16[2,2,192,256]{3,2,1,0:T(8,128)(2,1)}, u32[]{:S(2)}, u32[]{:S(2)}) collective-permute-start(bf16[2,2,192,256]{3,2,1,0:T(8,128)(2,1)} %bitcast.5), channel_id=1, source_target_pairs={{0,8},{8,16},{16,24},{24,0},{1,9},{9,17},{17,25},{25,1},{2,10},{10... | collective-permute-start | bytes 1179656 | tf_op jit(solution)/shard_map/ppermute | solution.py:649
  77.0 31.1 %collective-permute-start.1 = (bf16[2,2,192,256]{3,2,1,0:T(8,128)(2,1)}, bf16[2,2,192,256]{3,2,1,0:T(8,128)(2,1)}, u32[]{:S(2)}, u32[]{:S(2)}) collective-permute-start(bf16[2,2,192,256]{3,2,1,0:T(8,128)(2,1)} %bitcast.68), channel_id=1, source_target_pairs={{0,16},{8,24},{16,0},{24,8},{1,17},{9,25},{17,1},{25,9},{2,18},{10... | collective-permute-start | bytes 1179656 | tf_op jit(solution)/shard_map/ppermute | solution.py:649
  81.4 26.7 %collective-permute-start.2 = (bf16[2,2,192,256]{3,2,1,0:T(8,128)(2,1)}, bf16[2,2,192,256]{3,2,1,0:T(8,128)(2,1)}, u32[]{:S(2)}, u32[]{:S(2)}) collective-permute-start(bf16[2,2,192,256]{3,2,1,0:T(8,128)(2,1)} %bitcast.67), channel_id=1, source_target_pairs={{0,24},{8,0},{16,8},{24,16},{1,25},{9,1},{17,9},{25,17},{2,26},{10... | collective-permute-start | bytes 1179656 | tf_op jit(solution)/shard_map/ppermute | solution.py:649
  91.8 49.1 %copy-start.13 = (bf16[4,16,192]{2,1,0:T(8,128)(2,1)}, bf16[4,16,192]{2,1,0:T(8,128)(2,1)S(1)}, u32[]{:S(2)}) copy-start(bf16[4,16,192]{2,1,0:T(8,128)(2,1)S(1)} %collective-permute-done.10.refs_5_.refs_1_) | copy-start | bytes 73732
  91.8 24.7 %collective-permute-start.6 = (bf16[2,2,192,256]{3,2,1,0:T(8,128)(2,1)}, bf16[2,2,192,256]{3,2,1,0:T(8,128)(2,1)}, u32[]{:S(2)}, u32[]{:S(2)}) collective-permute-start(bf16[2,2,192,256]{3,2,1,0:T(8,128)(2,1)} %bitcast.15), channel_id=1, source_target_pairs={{0,8},{8,16},{16,24},{24,0},{1,9},{9,17},{17,25},{25,1},{2,10},{10... | collective-permute-start | bytes 1179656 | tf_op jit(solution)/shard_map/ppermute | solution.py:649
  93.8 47.1 %copy-start.14 = (bf16[4,16,192]{2,1,0:T(8,128)(2,1)}, bf16[4,16,192]{2,1,0:T(8,128)(2,1)S(1)}, u32[]{:S(2)}) copy-start(bf16[4,16,192]{2,1,0:T(8,128)(2,1)S(1)} %collective-permute-done.9.refs_4_.refs_0_) | copy-start | bytes 73732
  93.8 47.1 %collective-permute-start.7 = (bf16[2,2,192,256]{3,2,1,0:T(8,128)(2,1)}, bf16[2,2,192,256]{3,2,1,0:T(8,128)(2,1)}, u32[]{:S(2)}, u32[]{:S(2)}) collective-permute-start(bf16[2,2,192,256]{3,2,1,0:T(8,128)(2,1)} %bitcast.16), channel_id=1, source_target_pairs={{0,16},{8,24},{16,0},{24,8},{1,17},{9,25},{17,1},{25,9},{2,18},{10... | collective-permute-start | bytes 1179656 | tf_op jit(solution)/shard_map/ppermute | solution.py:649
  93.9 47.0 %collective-permute-start.8 = (bf16[2,2,192,256]{3,2,1,0:T(8,128)(2,1)}, bf16[2,2,192,256]{3,2,1,0:T(8,128)(2,1)}, u32[]{:S(2)}, u32[]{:S(2)}) collective-permute-start(bf16[2,2,192,256]{3,2,1,0:T(8,128)(2,1)} %bitcast.17), channel_id=1, source_target_pairs={{0,24},{8,0},{16,8},{24,16},{1,25},{9,1},{17,9},{25,17},{2,26},{10... | collective-permute-start | bytes 1179656 | tf_op jit(solution)/shard_map/ppermute | solution.py:649
  108.1 5.9 %collective-permute-start.11 = (bf16[4,16,256]{2,1,0:T(8,128)(2,1)S(1)}, bf16[4,16,256]{2,1,0:T(8,128)(2,1)S(1)}, u32[]{:S(2)}, u32[]{:S(2)}) collective-permute-start(bf16[4,16,256]{2,1,0:T(8,128)(2,1)S(1)} %pad_maximum_fusion.2), channel_id=1, source_target_pairs={{0,1},{1,2},{2,3},{3,4},{4,5},{5,6},{6,7},{7,0},{8,9},{9,10},{10,1... | collective-permute-start | bytes 98312 | tf_op jit(solution)/shard_map/ppermute | solution.py:407
  108.1 5.9 %collective-permute-start.12 = (bf16[4,16,256]{2,1,0:T(8,128)(2,1)S(1)}, bf16[4,16,256]{2,1,0:T(8,128)(2,1)S(1)}, u32[]{:S(2)}, u32[]{:S(2)}) collective-permute-start(bf16[4,16,256]{2,1,0:T(8,128)(2,1)S(1)} %pad_maximum_fusion.3), channel_id=1, source_target_pairs={{1,0},{2,1},{3,2},{4,3},{5,4},{6,5},{7,6},{0,7},{9,8},{10,9},{11,1... | collective-permute-start | bytes 98312 | tf_op jit(solution)/shard_map/ppermute | solution.py:407
  141.0 41.0 %slice-start = ((s8[4718592]{0:T(1024)(128)(4,1)}), s8[524288]{0:T(1024)(128)(4,1)S(1)}, s32[]{:S(2)}) async-start(s8[4718592]{0:T(1024)(128)(4,1)} %bitcast.45), calls=%async_computation.6 | async-start | bytes 1048576
  144.4 37.6 %slice-start.1 = ((s8[4718592]{0:T(1024)(128)(4,1)}), s8[4194304]{0:T(1024)(128)(4,1)S(1)}, s32[]{:S(2)}) async-start(s8[4718592]{0:T(1024)(128)(4,1)} %bitcast.45), calls=%async_computation.7 | async-start | bytes 8388608
  147.6 18.4 %collective-permute-start.19 = (bf16[2,2,192,256]{3,2,1,0:T(8,128)(2,1)S(1)}, bf16[2,2,192,256]{3,2,1,0:T(8,128)(2,1)S(1)}, u32[]{:S(2)}, u32[]{:S(2)}) collective-permute-start(bf16[2,2,192,256]{3,2,1,0:T(8,128)(2,1)S(1)} %get-tuple-element.70), channel_id=1, source_target_pairs={{0,8},{8,16},{16,24},{24,0},{1,9},{9,17},{17,25},{25,1},{2,10},{10... | collective-permute-start | bytes 1179656 | tf_op jit(solution)/shard_map/ppermute | solution.py:649
  156.5 24.4 %collective-permute-start.20 = (bf16[2,2,192,256]{3,2,1,0:T(8,128)(2,1)S(1)}, bf16[2,2,192,256]{3,2,1,0:T(8,128)(2,1)S(1)}, u32[]{:S(2)}, u32[]{:S(2)}) collective-permute-start(bf16[2,2,192,256]{3,2,1,0:T(8,128)(2,1)S(1)} %get-tuple-element.71), channel_id=1, source_target_pairs={{0,16},{8,24},{16,0},{24,8},{1,17},{9,25},{17,1},{25,9},{2,18},{10... | collective-permute-start | bytes 1179656 | tf_op jit(solution)/shard_map/ppermute | solution.py:649
  156.5 25.4 %collective-permute-start.21 = (bf16[2,2,192,256]{3,2,1,0:T(8,128)(2,1)S(1)}, bf16[2,2,192,256]{3,2,1,0:T(8,128)(2,1)S(1)}, u32[]{:S(2)}, u32[]{:S(2)}) collective-permute-start(bf16[2,2,192,256]{3,2,1,0:T(8,128)(2,1)S(1)} %get-tuple-element.72), channel_id=1, source_target_pairs={{0,24},{8,0},{16,8},{24,16},{1,25},{9,1},{17,9},{25,17},{2,26},{10... | collective-permute-start | bytes 1179656 | tf_op jit(solution)/shard_map/ppermute | solution.py:649
  187.1 42.8 %copy-start.18 = (bf16[1,2,2,192,256]{4,3,2,1,0:T(8,128)(2,1)S(1)}, bf16[1,2,2,192,256]{4,3,2,1,0:T(8,128)(2,1)}, u32[]{:S(2)}) copy-start(bf16[1,2,2,192,256]{4,3,2,1,0:T(8,128)(2,1)} %copy-done.17) | copy-start | bytes 1179652
  187.1 88.7 %all-to-all-start.4 = ((bf16[8,2,192,256]{3,2,1,0:T(8,128)(2,1)}), bf16[8,2,192,256]{3,2,1,0:T(8,128)(2,1)}, u32[]{:S(2)}, u32[]{:S(2)}) async-start(bf16[8,2,192,256]{3,2,1,0:T(8,128)(2,1)} %copy-done.11), calls=%async_computation.4 | async-start | bytes 3145728 | tf_op jit(solution)/shard_map/all_to_all | solution.py:724
  191.5 21.8 %collective-permute-start.3 = (bf16[2,2,192,256]{3,2,1,0:T(8,128)(2,1)}, bf16[2,2,192,256]{3,2,1,0:T(8,128)(2,1)S(1)}, u32[]{:S(2)}, u32[]{:S(2)}) collective-permute-start(bf16[2,2,192,256]{3,2,1,0:T(8,128)(2,1)} %bitcast.66), channel_id=1, source_target_pairs={{0,8},{8,16},{16,24},{24,0},{1,9},{9,17},{17,25},{25,1},{2,10},{10... | collective-permute-start | bytes 1179656 | tf_op jit(solution)/shard_map/ppermute | solution.py:649
  200.3 29.6 %collective-permute-start.4 = (bf16[2,2,192,256]{3,2,1,0:T(8,128)(2,1)}, bf16[2,2,192,256]{3,2,1,0:T(8,128)(2,1)S(1)}, u32[]{:S(2)}, u32[]{:S(2)}) collective-permute-start(bf16[2,2,192,256]{3,2,1,0:T(8,128)(2,1)} %bitcast.65), channel_id=1, source_target_pairs={{0,16},{8,24},{16,0},{24,8},{1,17},{9,25},{17,1},{25,9},{2,18},{10... | collective-permute-start | bytes 1179656 | tf_op jit(solution)/shard_map/ppermute | solution.py:649
  203.7 26.2 %collective-permute-start.5 = (bf16[2,2,192,256]{3,2,1,0:T(8,128)(2,1)}, bf16[2,2,192,256]{3,2,1,0:T(8,128)(2,1)S(1)}, u32[]{:S(2)}, u32[]{:S(2)}) collective-permute-start(bf16[2,2,192,256]{3,2,1,0:T(8,128)(2,1)} %bitcast.64), channel_id=1, source_target_pairs={{0,24},{8,0},{16,8},{24,16},{1,25},{9,1},{17,9},{25,17},{2,26},{10... | collective-permute-start | bytes 1179656 | tf_op jit(solution)/shard_map/ppermute | solution.py:649
  231.5 39.9 %slice-start.2 = ((s8[4718592]{0:T(1024)(128)(4,1)}), s8[524288]{0:T(1024)(128)(4,1)S(1)}, s32[]{:S(2)}) async-start(s8[4718592]{0:T(1024)(128)(4,1)} %bitcast.47), calls=%async_computation.8 | async-start | bytes 1048576
  233.6 37.8 %slice-start.3 = ((s8[4718592]{0:T(1024)(128)(4,1)}), s8[4194304]{0:T(1024)(128)(4,1)S(1)}, s32[]{:S(2)}) async-start(s8[4718592]{0:T(1024)(128)(4,1)} %bitcast.47), calls=%async_computation.9 | async-start | bytes 8388608
  233.6 37.8 %copy-start.12 = (bf16[8,2,192,256]{3,2,1,0:T(8,128)(2,1)S(1)}, bf16[8,2,192,256]{3,2,1,0:T(8,128)(2,1)}, u32[]{:S(2)}) copy-start(bf16[8,2,192,256]{3,2,1,0:T(8,128)(2,1)} %copy-done.11) | copy-start | bytes 4718596
  236.8 18.6 %collective-permute-start.16 = (bf16[2,2,192,256]{3,2,1,0:T(8,128)(2,1)S(1)}, bf16[2,2,192,256]{3,2,1,0:T(8,128)(2,1)S(1)}, u32[]{:S(2)}, u32[]{:S(2)}) collective-permute-start(bf16[2,2,192,256]{3,2,1,0:T(8,128)(2,1)S(1)} %get-tuple-element.67), channel_id=1, source_target_pairs={{0,8},{8,16},{16,24},{24,0},{1,9},{9,17},{17,25},{25,1},{2,10},{10... | collective-permute-start | bytes 1179656 | tf_op jit(solution)/shard_map/ppermute | solution.py:649
  245.9 25.0 %collective-permute-start.17 = (bf16[2,2,192,256]{3,2,1,0:T(8,128)(2,1)S(1)}, bf16[2,2,192,256]{3,2,1,0:T(8,128)(2,1)S(1)}, u32[]{:S(2)}, u32[]{:S(2)}) collective-permute-start(bf16[2,2,192,256]{3,2,1,0:T(8,128)(2,1)S(1)} %get-tuple-element.68), channel_id=1, source_target_pairs={{0,16},{8,24},{16,0},{24,8},{1,17},{9,25},{17,1},{25,9},{2,18},{10... | collective-permute-start | bytes 1179656 | tf_op jit(solution)/shard_map/ppermute | solution.py:649
  245.9 25.5 %collective-permute-start.18 = (bf16[2,2,192,256]{3,2,1,0:T(8,128)(2,1)S(1)}, bf16[2,2,192,256]{3,2,1,0:T(8,128)(2,1)S(1)}, u32[]{:S(2)}, u32[]{:S(2)}) collective-permute-start(bf16[2,2,192,256]{3,2,1,0:T(8,128)(2,1)S(1)} %get-tuple-element.69), channel_id=1, source_target_pairs={{0,24},{8,0},{16,8},{24,16},{1,25},{9,1},{17,9},{25,17},{2,26},{10... | collective-permute-start | bytes 1179656 | tf_op jit(solution)/shard_map/ppermute | solution.py:649
  275.8 36.7 %all-to-all-start.3 = ((bf16[8,2,192,256]{3,2,1,0:T(8,128)(2,1)}), bf16[8,2,192,256]{3,2,1,0:T(8,128)(2,1)}, u32[]{:S(2)}, u32[]{:S(2)}) async-start(bf16[8,2,192,256]{3,2,1,0:T(8,128)(2,1)} %copy-done.10), calls=%async_computation.3 | async-start | bytes 3145728 | tf_op jit(solution)/shard_map/all_to_all | solution.py:724
  288.3 31.8 %collective-permute-start.13 = (bf16[2,2,192,256]{3,2,1,0:T(8,128)(2,1)}, bf16[2,2,192,256]{3,2,1,0:T(8,128)(2,1)S(1)}, u32[]{:S(2)}, u32[]{:S(2)}) collective-permute-start(bf16[2,2,192,256]{3,2,1,0:T(8,128)(2,1)} %get-tuple-element.64), channel_id=1, source_target_pairs={{0,8},{8,16},{16,24},{24,0},{1,9},{9,17},{17,25},{25,1},{2,10},{10... | collective-permute-start | bytes 1179656 | tf_op jit(solution)/shard_map/ppermute | solution.py:649
  297.0 29.7 %collective-permute-start.14 = (bf16[2,2,192,256]{3,2,1,0:T(8,128)(2,1)}, bf16[2,2,192,256]{3,2,1,0:T(8,128)(2,1)S(1)}, u32[]{:S(2)}, u32[]{:S(2)}) collective-permute-start(bf16[2,2,192,256]{3,2,1,0:T(8,128)(2,1)} %get-tuple-element.65), channel_id=1, source_target_pairs={{0,16},{8,24},{16,0},{24,8},{1,17},{9,25},{17,1},{25,9},{2,18},{10... | collective-permute-start | bytes 1179656 | tf_op jit(solution)/shard_map/ppermute | solution.py:649
  300.3 34.3 %collective-permute-start.15 = (bf16[2,2,192,256]{3,2,1,0:T(8,128)(2,1)}, bf16[2,2,192,256]{3,2,1,0:T(8,128)(2,1)S(1)}, u32[]{:S(2)}, u32[]{:S(2)}) collective-permute-start(bf16[2,2,192,256]{3,2,1,0:T(8,128)(2,1)} %get-tuple-element.66), channel_id=1, source_target_pairs={{0,24},{8,0},{16,8},{24,16},{1,25},{9,1},{17,9},{25,17},{2,26},{10... | collective-permute-start | bytes 1179656 | tf_op jit(solution)/shard_map/ppermute | solution.py:649
  317.5 18.7 %collective-permute-start.24 = (bf16[16,256]{1,0:T(8,128)(2,1)}, bf16[16,256]{1,0:T(8,128)(2,1)S(1)}, u32[]{:S(2)}, u32[]{:S(2)}) collective-permute-start(bf16[16,256]{1,0:T(8,128)(2,1)} %get-tuple-element.77), channel_id=1, source_target_pairs={{0,1},{1,2},{2,3},{3,4},{4,5},{5,6},{6,7},{7,0},{8,9},{9,10},{10,1... | collective-permute-start | bytes 24584 | tf_op jit(solution)/shard_map/ppermute | solution.py:407
  317.5 18.7 %collective-permute-start.25 = (bf16[16,256]{1,0:T(8,128)(2,1)}, bf16[16,256]{1,0:T(8,128)(2,1)S(1)}, u32[]{:S(2)}, u32[]{:S(2)}) collective-permute-start(bf16[16,256]{1,0:T(8,128)(2,1)} %get-tuple-element.78), channel_id=1, source_target_pairs={{1,0},{2,1},{3,2},{4,3},{5,4},{6,5},{7,6},{0,7},{9,8},{10,9},{11,1... | collective-permute-start | bytes 24584 | tf_op jit(solution)/shard_map/ppermute | solution.py:407
  320.1 14.5 %collective-permute-start.22 = (bf16[16,192]{1,0:T(8,128)(2,1)}, bf16[16,192]{1,0:T(8,128)(2,1)S(1)}, u32[]{:S(2)}, u32[]{:S(2)}) collective-permute-start(bf16[16,192]{1,0:T(8,128)(2,1)} %get-tuple-element.75), channel_id=1, source_target_pairs={{0,8},{8,16},{16,24},{24,0},{1,9},{9,17},{17,25},{25,1},{2,10},{10... | collective-permute-start | bytes 18440 | tf_op jit(solution)/shard_map/ppermute | solution.py:407
  326.7 9.5 %collective-permute-start.23 = (bf16[16,192]{1,0:T(8,128)(2,1)}, bf16[16,192]{1,0:T(8,128)(2,1)S(1)}, u32[]{:S(2)}, u32[]{:S(2)}) collective-permute-start(bf16[16,192]{1,0:T(8,128)(2,1)} %get-tuple-element.76), channel_id=1, source_target_pairs={{8,0},{16,8},{24,16},{0,24},{9,1},{17,9},{25,17},{1,25},{10,2},{18... | collective-permute-start | bytes 18440 | tf_op jit(solution)/shard_map/ppermute | solution.py:407
  342.2 41.3 %all-to-all-start.5 = ((bf16[8,2,192,256]{3,2,1,0:T(8,128)(2,1)}), bf16[8,2,192,256]{3,2,1,0:T(8,128)(2,1)S(1)}, u32[]{:S(2)}, u32[]{:S(2)}) async-start(bf16[8,2,192,256]{3,2,1,0:T(8,128)(2,1)} %y_inverse.5.refs_9_.refs_8_), calls=%async_computation.5 | async-start | bytes 3145728 | tf_op jit(solution)/shard_map/all_to_all | solution.py:724
  346.3 16.6 %collective-permute-start.26 = (bf16[16,192]{1,0:T(8,128)(2,1)S(1)}, bf16[16,192]{1,0:T(8,128)(2,1)S(1)}, u32[]{:S(2)}, u32[]{:S(2)}) collective-permute-start(bf16[16,192]{1,0:T(8,128)(2,1)S(1)} %copy-done.57), channel_id=1, source_target_pairs={{0,8},{8,16},{16,24},{24,0},{1,9},{9,17},{17,25},{25,1},{2,10},{10... | collective-permute-start | bytes 18440 | tf_op jit(solution)/shard_map/ppermute | solution.py:407
  346.3 16.5 %collective-permute-start.27 = (bf16[16,192]{1,0:T(8,128)(2,1)S(1)}, bf16[16,192]{1,0:T(8,128)(2,1)S(1)}, u32[]{:S(2)}, u32[]{:S(2)}) collective-permute-start(bf16[16,192]{1,0:T(8,128)(2,1)S(1)} %copy-done.56), channel_id=1, source_target_pairs={{8,0},{16,8},{24,16},{0,24},{9,1},{17,9},{25,17},{1,25},{10,2},{18... | collective-permute-start | bytes 18440 | tf_op jit(solution)/shard_map/ppermute | solution.py:407
  350.5 16.5 %collective-permute-start.28 = (bf16[16,256]{1,0:T(8,128)(2,1)S(1)}, bf16[16,256]{1,0:T(8,128)(2,1)S(1)}, u32[]{:S(2)}, u32[]{:S(2)}) collective-permute-start(bf16[16,256]{1,0:T(8,128)(2,1)S(1)} %copy-done.55), channel_id=1, source_target_pairs={{0,1},{1,2},{2,3},{3,4},{4,5},{5,6},{6,7},{7,0},{8,9},{9,10},{10,1... | collective-permute-start | bytes 24584 | tf_op jit(solution)/shard_map/ppermute | solution.py:407
  350.6 16.3 %collective-permute-start.29 = (bf16[16,256]{1,0:T(8,128)(2,1)S(1)}, bf16[16,256]{1,0:T(8,128)(2,1)S(1)}, u32[]{:S(2)}, u32[]{:S(2)}) collective-permute-start(bf16[16,256]{1,0:T(8,128)(2,1)S(1)} %copy-done.54), channel_id=1, source_target_pairs={{1,0},{2,1},{3,2},{4,3},{5,4},{6,5},{7,6},{0,7},{9,8},{10,9},{11,1... | collective-permute-start | bytes 24584 | tf_op jit(solution)/shard_map/ppermute | solution.py:407
  389.6 16.5 %collective-permute-start.30 = (bf16[16,192]{1,0:T(8,128)(2,1)}, bf16[16,192]{1,0:T(8,128)(2,1)S(1)}, u32[]{:S(2)}, u32[]{:S(2)}) collective-permute-start(bf16[16,192]{1,0:T(8,128)(2,1)} %get-tuple-element.84), channel_id=1, source_target_pairs={{0,8},{8,16},{16,24},{24,0},{1,9},{9,17},{17,25},{25,1},{2,10},{10... | collective-permute-start | bytes 18440 | tf_op jit(solution)/shard_map/ppermute | solution.py:407
  389.6 16.5 %collective-permute-start.31 = (bf16[16,192]{1,0:T(8,128)(2,1)}, bf16[16,192]{1,0:T(8,128)(2,1)S(1)}, u32[]{:S(2)}, u32[]{:S(2)}) collective-permute-start(bf16[16,192]{1,0:T(8,128)(2,1)} %get-tuple-element.85), channel_id=1, source_target_pairs={{8,0},{16,8},{24,16},{0,24},{9,1},{17,9},{25,17},{1,25},{10,2},{18... | collective-permute-start | bytes 18440 | tf_op jit(solution)/shard_map/ppermute | solution.py:407
  393.7 12.4 %collective-permute-start.32 = (bf16[16,256]{1,0:T(8,128)(2,1)}, bf16[16,256]{1,0:T(8,128)(2,1)S(1)}, u32[]{:S(2)}, u32[]{:S(2)}) collective-permute-start(bf16[16,256]{1,0:T(8,128)(2,1)} %get-tuple-element.86), channel_id=1, source_target_pairs={{0,1},{1,2},{2,3},{3,4},{4,5},{5,6},{6,7},{7,0},{8,9},{9,10},{10,1... | collective-permute-start | bytes 24584 | tf_op jit(solution)/shard_map/ppermute | solution.py:407
  393.7 12.4 %collective-permute-start.33 = (bf16[16,256]{1,0:T(8,128)(2,1)}, bf16[16,256]{1,0:T(8,128)(2,1)S(1)}, u32[]{:S(2)}, u32[]{:S(2)}) collective-permute-start(bf16[16,256]{1,0:T(8,128)(2,1)} %get-tuple-element.87), channel_id=1, source_target_pairs={{1,0},{2,1},{3,2},{4,3},{5,4},{6,5},{7,6},{0,7},{9,8},{10,9},{11,1... | collective-permute-start | bytes 24584 | tf_op jit(solution)/shard_map/ppermute | solution.py:407
  (56 other events, 520.8 us)

commit v4 on v3

--- a/solution.py
+++ b/solution.py
@@ -29,8 +29,7 @@
     return pltpu.CompilerParams(vmem_limit_bytes=megabytes * 1024 * 1024)
 
 
-def cost(flops, nbytes):
-    return pl.CostEstimate(flops=int(flops), bytes_accessed=int(nbytes), transcendentals=0)
+SMALL = pl.CostEstimate(flops=1, bytes_accessed=1, transcendentals=0)
 
 
 def tied(after):
@@ -148,7 +147,7 @@
         out_specs=pl.BlockSpec((Z, ROWS, width), lambda j: (0, j, 0)),
         out_shape=jax.ShapeDtypeStruct((Z, height, width), bf16),
         compiler_params=params(),
-        cost_estimate=cost(6 * Z * height * width, 6 * Z * height * width),
+        cost_estimate=SMALL,
         name="depth_transform",
     )(values)
 
@@ -160,33 +159,37 @@
     shape = (halves, planes, 2, modes, width)
 
     def kernel(me_ref, table_ref, columns_ref, *refs):
-        outs = refs[len(after) :]
-        shift = pl.program_id(0)
-        for plane in range(planes):
-            column = columns_ref[:, plane].reshape(Y, width)
-            part = jnp.dot(table_ref[...], column, preferred_element_type=f32).astype(bf16)
-            part = part.reshape(halves, 2, modes, width)
-            for s, out in enumerate(outs):
-
-                @pl.when(shift == s)
-                def _(out=out, part=part, plane=plane):
-                    out[:, plane] = part
-
+        outs, held, arrived = refs[len(after) : len(after) + blocks], refs[-2], refs[-1]
+        copies = []
+        for s in range(blocks):
+            target = lax.rem(me_ref[0] + s, blocks)
+            place = pl.ds(pl.multiple_of(target * rows, rows), rows)
+            copies.append(pltpu.make_async_copy(table_ref.at[place], held.at[s], arrived.at[s]))
+            copies[s].start()
+        for s, out in enumerate(outs):
+            copies[s].wait()
+            for plane in range(planes):
+                column = columns_ref[:, plane].reshape(Y, width)
+                part = jnp.dot(held[s], column, preferred_element_type=f32)
+                out[:, plane] = part.astype(bf16).reshape(halves, 2, modes, width)
+
+    vmem = pl.BlockSpec(memory_space=pltpu.VMEM)
     return pl.pallas_call(
         kernel,
-        grid_spec=pltpu.PrefetchScalarGridSpec(
-            num_scalar_prefetch=1,
-            grid=(blocks,),
-            in_specs=[
-                pl.BlockSpec((rows, Y), lambda j, me: (lax.rem(me[0] + j, blocks), 0)),
-                pl.BlockSpec(columns.shape, lambda j, me: (0, 0, 0, 0)),
-            ]
-            + tied(after),
-            out_specs=[pl.BlockSpec(shape, lambda j, me: (0, 0, 0, 0, 0))] * blocks,
-        ),
+        in_specs=[
+            pl.BlockSpec(memory_space=pltpu.SMEM),
+            pl.BlockSpec(memory_space=pl.ANY),
+            vmem,
+        ]
+        + tied(after),
+        out_specs=[vmem] * blocks,
         out_shape=[jax.ShapeDtypeStruct(shape, bf16)] * blocks,
-        compiler_params=params(24),
-        cost_estimate=cost(2 * planes * Y * Y * width, 2 * Y * Y + 4 * planes * Y * width),
+        scratch_shapes=[
+            pltpu.VMEM((blocks, rows, Y), bf16),
+            pltpu.SemaphoreType.DMA((blocks,)),
+        ],
+        compiler_params=params(),
+        cost_estimate=SMALL,
         name="y_transform",
     )(me, table, columns, *after)
 
@@ -226,7 +229,7 @@
         out_shape=jax.ShapeDtypeStruct((size_y, planes, height, width), bf16),
         scratch_shapes=[pltpu.VMEM((planes, Y, width), bf16)],
         compiler_params=params(24),
-        cost_estimate=cost(2 * planes * Y * Y * width, 2 * Y * Y + 4 * planes * Y * width),
+        cost_estimate=SMALL,
         name="y_inverse",
     )(me, table, *modes, *after)
 
@@ -257,7 +260,7 @@
         out_shape=jax.ShapeDtypeStruct((2, 2, count, X), f32),
         scratch_shapes=[pltpu.VMEM((2 * count, X), bf16)],
         compiler_params=params(24),
-        cost_estimate=cost(8 * count * X * X, 2 * X * X + 24 * count * X),
+        cost_estimate=SMALL,
         name="x_transform",
     )(me, table, *modes, *after)
 
@@ -338,7 +341,7 @@
         out_specs=[pl.BlockSpec((2, 2, count, width), lambda j: (0, 0, j, 0))] * blocks,
         out_shape=[jax.ShapeDtypeStruct((2, 2, total, width), bf16)] * blocks,
         compiler_params=params(24),
-        cost_estimate=cost(8 * total * X * X, 2 * X * X + 40 * total * X),
+        cost_estimate=SMALL,
         name="curl_inverse",
     )(where, table, spectra[plus], spectra[minus], *after)
 
@@ -376,28 +379,27 @@
     return [spread[:, n * width : (n + 1) * width] for n in range(layers)]
 
 
-def edges_kernel(field_ref, first_column_ref, last_column_ref):
+def edges_kernel(field_ref, *refs):
+    first_column_ref, last_column_ref = refs[-2:]
     first, last = side_columns([field_ref[0, n] for n in range(Z)])
     first_column_ref[0] = first
     last_column_ref[0] = last
 
 
-def edge_columns(field, components):
+def edge_columns(field, components, after):
     _, _, height, width = field.shape
     shape = jax.ShapeDtypeStruct((components, Z, height), bf16)
     spec = pl.BlockSpec((1, Z, height), lambda i: (i, 0, 0))
     return pl.pallas_call(
         edges_kernel,
         grid=(components,),
-        in_specs=[pl.BlockSpec((1, Z, height, width), lambda i: (i, 0, 0, 0))],
+        in_specs=[pl.BlockSpec((1, Z, height, width), lambda i: (i, 0, 0, 0))] + tied(after),
         out_specs=[spec, spec],
         out_shape=[shape, shape],
         compiler_params=params(),
-        cost_estimate=cost(
-            components * 64 * Z * height * width, 2 * components * Z * height * width
-        ),
+        cost_estimate=SMALL,
         name="edge_columns",
-    )(field)
+    )(field, *after)
 
 
 def exchange(first, last, axis):
@@ -464,7 +466,7 @@
         ],
         scratch_shapes=[pltpu.VMEM((Z, height, width), bf16)],
         compiler_params=params(),
-        cost_estimate=cost(70 * Z * height * width, 10 * Z * height * width),
+        cost_estimate=SMALL,
         name="make_adjoint",
     )(planes, cotangent, *after)
 
@@ -547,9 +549,7 @@
         out_shape=jax.ShapeDtypeStruct((3, Z, height, width), f32),
         input_output_aliases=aliases,
         compiler_params=params(),
-        cost_estimate=cost(
-            2 * Z * height * width * (width + height), Z * height * width * (18 + 12 * len(aliases))
-        ),
+        cost_estimate=SMALL,
         name="add_grad_vort",
     )(*operands, *after)
 
@@ -571,11 +571,8 @@
         width,
     )
     values = adjoint[pl.ds(first, LAYERS)]
-    product = (vorticity[0].astype(f32) * values).reshape(LAYERS * height, width)
-    coarse = product.astype(bf16)
-    fine = (product - coarse.astype(f32)).astype(bf16)
-    inner = jnp.dot(coarse, slope_x[...], preferred_element_type=f32)
-    inner = inner + jnp.dot(fine, slope_x[...], preferred_element_type=f32)
+    product = (vorticity[0].astype(f32) * values).astype(bf16).reshape(LAYERS * height, width)
+    inner = jnp.dot(product, slope_x[...], preferred_element_type=f32)
     up = adjoint[lax.rem(first + LAYERS, Z)] * vorticity_above[0, 0].astype(f32)
     down = adjoint[lax.rem(first + Z - 1, Z)] * vorticity_below[0, 0].astype(f32)
     deep = [down] + [vorticity[2, k].astype(f32) * values[k] for k in range(LAYERS)] + [up]
@@ -630,7 +627,7 @@
         input_output_aliases=aliases,
         scratch_shapes=[pltpu.VMEM((LAYERS, height + 16, width), f32)],
         compiler_params=params(),
-        cost_estimate=cost(4 * Z * height * width * width, Z * height * width * 16),
+        cost_estimate=SMALL,
         name="write_grad_vel",
     )(*operands, *after)
 
@@ -671,8 +668,10 @@
     slope_x = slope_matrix(width)
     slope_y = np.ascontiguousarray(slope_matrix(height).T)
 
-    velocity_first, velocity_last = edge_columns(velocity, 3)
-    vorticity_first, vorticity_last = edge_columns(vorticity, 1)
+    layers = [depth_transform(cot_vel, component) for component in FORWARD_ORDER]
+
+    velocity_first, velocity_last = edge_columns(velocity, 3, (layers[1],))
+    vorticity_first, vorticity_last = edge_columns(vorticity, 1, (layers[1],))
     low_x, high_x = exchange(
         jnp.concatenate([velocity_first, vorticity_first]),
         jnp.concatenate([velocity_last, vorticity_last]),
@@ -686,27 +685,24 @@
     saved_halos = (low_x, high_x, low_y, high_y)
     edges = (velocity_first, vorticity_first)
 
-    sent = {}
-    for place, component in enumerate(FORWARD_ORDER):
-        layers = depth_transform(cot_vel, component)
+    sent = []
+    for place in range(3):
         columns = lax.all_to_all(
-            layers.reshape(size_y, planes, height, width), "gy", 0, 0, tiled=True
-        )
-        parts = y_transform(
-            me, y_table, columns, size_x, halves, edges if place == 1 else ()
-        )
+            layers[place].reshape(size_y, planes, height, width), "gy", 0, 0, tiled=True
+        )
+        parts = y_transform(me, y_table, columns, size_x, halves, edges if place == 0 else ())
         if halves == 1:
             parts = [part[0] for part in parts]
         else:
             parts = [pair_exchange(part[:, 0], "gy", half) for part in parts]
-        sent[component] = parts
+        sent.append(parts)
     spectra = {}
     for place, component in enumerate(FORWARD_ORDER):
-        after = ((sent[FORWARD_ORDER[2]][0],), saved_halos, ())[place]
-        spectra[component] = x_transform(me, x_table, shifted(sent[component], "gx"), after)
+        after = (sent[2][0],) + saved_halos if place == 0 else ()
+        spectra[component] = x_transform(me, x_table, shifted(sent[place], "gx"), after)
 
     returned = {}
-    after = ()
+    after = (spectra[FORWARD_ORDER[2]],)
     for component in BACK_ORDER:
         parts = curl_inverse(where, x_back_table, spectra, component, size_x, after)
         after = (parts[0],)
@@ -716,6 +712,7 @@
         else:
             parts = [pair_exchange(part, "gy", half)[:, None] for part in parts]
         returned[component] = parts
+    last_curl = after
 
     def rows_of(component, after):
         return y_inverse(me, y_back_table, returned[component], size_y, after)
@@ -738,16 +735,16 @@
         )
 
     one, two, three = BACK_ORDER
-    rows_one = rows_of(one, ())
-    rows_two = rows_of(two, (rows_one,))
-    adjoint_one, halos_one = adjoint_of(one, rows_one, (rows_two,))
-    grad_vort = vort_of(one, adjoint_one, None, ())
-    adjoint_two, halos_two = adjoint_of(two, rows_two, (grad_vort,))
-    rows_three = rows_of(three, (adjoint_two,) + halos_two)
-    grad_vel = vel_of(one, adjoint_one, halos_one, None, (rows_three,))
+    rows_one = rows_of(one, last_curl)
+    adjoint_one, halos_one = adjoint_of(one, rows_one, ())
+    rows_two = rows_of(two, (adjoint_one,))
+    grad_vort = vort_of(one, adjoint_one, None, (rows_two,))
+    grad_vel = vel_of(one, adjoint_one, halos_one, None, (grad_vort,))
+    adjoint_two, halos_two = adjoint_of(two, rows_two, (grad_vel,))
+    rows_three = rows_of(three, (adjoint_two,))
     grad_vort = vort_of(two, adjoint_two, grad_vort, (rows_three,))
-    grad_vel = vel_of(two, adjoint_two, halos_two, grad_vel, ())
-    adjoint_three, halos_three = adjoint_of(three, rows_three, (grad_vort, grad_vel))
+    grad_vel = vel_of(two, adjoint_two, halos_two, grad_vel, (grad_vort,))
+    adjoint_three, halos_three = adjoint_of(three, rows_three, (grad_vel,))
     grad_vort = vort_of(three, adjoint_three, grad_vort, ())
     grad_vel = vel_of(three, adjoint_three, halos_three, grad_vel, (grad_vort,))
     return grad_vort, grad_vel

time: 416 us -> 426 us (1.024)
  waiting for transfers between devices: 141 us -> 165 us
  local copies, waits for them, and re-layouts: 27.9 us -> 11.8 us
    ppermute x16, waiting for transfers between devices: 5.72 us -> 44.6 us  [exchange(): return (lax.ppermute(last, axis, up), lax.ppermute(first, axis, down))]
    ppermute x18, waiting for transfers between devices: 107 us -> 75 us  [shifted(): lax.ppermute(parts[s], axis, [(i, (i + s) % count) for i in range(count)])]
    unnamed x132 -> x92, local copies, waits for them, and re-layouts: 25.9 us -> 9.75 us
    ppermute x16, starting transfers between devices: 32.6 us -> 44.2 us  [exchange(): return (lax.ppermute(last, axis, up), lax.ppermute(first, axis, down))]
    ppermute x18, starting transfers between devices: 56 us -> 45.2 us  [shifted(): lax.ppermute(parts[s], axis, [(i, (i + s) % count) for i in range(count)])]
    all_to_all x3, waiting for transfers between devices: 0.01 us -> 9.68 us  [adjoint_of(): layers = lax.all_to_all(rows, 'gy', 0, 0, tiled=True)]
    all_to_all x3, waiting for transfers between devices: 28.5 us -> 35.7 us  [local(): lax.all_to_all(layers[place].reshape(size_y, planes, height, width), 'gy'...]
  transfers between devices with their start and end apart: 40 -> 40, of which waited for: 16 -> 9; matrix products, arithmetic and copies ran while one was open for 1% -> 1% of each run, Pallas kernels for 24% -> 23%
where the time goes in v4:
time: 426 us; the launch traced here: 425 us
  waiting for transfers between devices  165 us (39%)
  Pallas kernels  132 us (31%)
  starting transfers between devices  115 us (27%)
  local copies, waits for them, and re-layouts  11.8 us (3%)
    ppermute x18, waiting for transfers between devices, shifted(): lax.ppermute(parts[s], axis, [(i, (i + s) % count) for i in range(count)])  75 us
    ppermute x18, starting transfers between devices, shifted(): lax.ppermute(parts[s], axis, [(i, (i + s) % count) for i in range(count)])  45.2 us
    ppermute x16, waiting for transfers between devices, exchange(): return (lax.ppermute(last, axis, up), lax.ppermute(first, axis, down))  44.6 us
    ppermute x16, starting transfers between devices, exchange(): return (lax.ppermute(last, axis, up), lax.ppermute(first, axis, down))  44.2 us
    all_to_all x3, waiting for transfers between devices, local(): lax.all_to_all(layers[place].reshape(size_y, planes, height, width), 'gy'...  35.7 us
    pallas_call x3, Pallas kernels, add_grad_vort(): pl.pallas_call(kernel, grid=(Z // LAYERS,), in_specs=in_specs + tied(afte...  26.8 us
    pallas_call x3, Pallas kernels, write_grad_vel(): pl.pallas_call(grad_vel_kernel, grid=(Z // LAYERS,), in_specs=in_specs +...  22.3 us
    pallas_call x3, Pallas kernels, y_transform(): pl.pallas_call(kernel, in_specs=[pl.BlockSpec(memory_space=pltpu.SMEM), p...  19.9 us
  transfers between devices with their start and end apart: 40, of which 9 were waited for; matrix products, arithmetic and copies ran while one was open for 1% of the time, Pallas kernels for 23%

profile of v4, /device:TPU:0, one launch (start us, length us, event | category | flops | bytes accessed | tf_op | source)
XLA Modules:
  0.0 425.0 jit_solution(13801257014846291285)
XLA Ops:
  0.6 3.2 depth_transform.4.refs_0_
  3.8 5.2 %all-to-all-start.2 = ((bf16[8,2,192,256]{3,2,1,0:T(8,128)(2,1)}), bf16[8,2,192,256]{3,2,1,0:T(8,128)(2,1)S(1)}, u32[]{:S(2)}, u32[]{:S(2)}) async-start(bf16[8,2,192,256]{3,2,1,0:T(8,128)(2,1)} %bitcast.67), calls=%async_computation.2 | async-start | bytes 3145728 | tf_op jit(solution)/shard_map/all_to_all | solution.py:690
  9.0 3.2 depth_transform.5
  12.1 17.9 %all-to-all-done.2.columns_ref = bf16[8,2,192,256]{3,2,1,0:T(8,128)(2,1)S(1)} async-done(((bf16[8,2,192,256]{3,2,1,0:T(8,128)(2,1)}), bf16[8,2,192,256]{3,2,1,0:T(8,128)(2,1)S(1)}, u32[]{:S(2)}, u32[]{:S(2)}) %all-to-all-start.2) | async-done | bytes 1572896 | tf_op jit(solution)/shard_map/all_to_all | solution.py:690
  31.2 3.6 all-to-all-start.1
  34.7 3.2 depth_transform.3
  37.9 17.8 %all-to-all-done.1.columns_ref = bf16[8,2,192,256]{3,2,1,0:T(8,128)(2,1)S(1)} async-done(((bf16[8,2,192,256]{3,2,1,0:T(8,128)(2,1)}), bf16[8,2,192,256]{3,2,1,0:T(8,128)(2,1)S(1)}, u32[]{:S(2)}, u32[]{:S(2)}) %all-to-all-start.1) | async-done | bytes 1572896 | tf_op jit(solution)/shard_map/all_to_all | solution.py:690
  55.7 4.3 %all-to-all-start = ((bf16[8,2,192,256]{3,2,1,0:T(8,128)(2,1)}), bf16[8,2,192,256]{3,2,1,0:T(8,128)(2,1)}, u32[]{:S(2)}, u32[]{:S(2)}) async-start(bf16[8,2,192,256]{3,2,1,0:T(8,128)(2,1)} %bitcast.69), calls=%async_computation | async-start | bytes 3145728 | tf_op jit(solution)/shard_map/all_to_all | solution.py:690
  62.6 4.6 %edge_columns.2 = (bf16[3,16,192]{2,1,0:T(8,128)(2,1)}, bf16[3,16,192]{2,1,0:T(8,128)(2,1)}) custom-call(bf16[3,16,192,256]{3,2,1,0:T(8,128)(2,1)} %refs_2_.5, bf16[16,192,256]{2,1,0:T(8,128)(2,1)} %depth_transform.4.refs_0_), custom_call_target="tpu_custom_call" | custom-call | flops 1 | bytes 1 | tf_op jit(solution)/shard_map/edge_columns/pallas_call | solution.py:393
  67.2 6.6 %y_transform.5 = (bf16[1,2,2,192,256]{4,3,2,1,0:T(8,128)(2,1)}, bf16[1,2,2,192,256]{4,3,2,1,0:T(8,128)(2,1)}, bf16[1,2,2,192,256]{4,3,2,1,0:T(8,128)(2,1)}, bf16[1,2,2,192,256]{4,3,2,1,0:T(8,128)(2,1)}) custom-call(s32[1]{0:T(128)} %bitcast.me_ref, bf16[1536,1536]{1,0:T(8,128)(2,1)} %constant.33.clone.table_ref, bf16[8,2,192,256]{3,2,1,0:T(8,128)(2,1)} %copy-done.13), custom_call_target="tpu_custom_call" | custom-call | flops 1 | bytes 1 | tf_op jit(solution)/shard_map/y_transform/pallas_call | solution.py:177
  79.4 6.6 %y_transform.4 = (bf16[1,2,2,192,256]{4,3,2,1,0:T(8,128)(2,1)}, bf16[1,2,2,192,256]{4,3,2,1,0:T(8,128)(2,1)}, bf16[1,2,2,192,256]{4,3,2,1,0:T(8,128)(2,1)}, bf16[1,2,2,192,256]{4,3,2,1,0:T(8,128)(2,1)}) custom-call(s32[1]{0:T(128)} %bitcast.me_ref, bf16[1536,1536]{1,0:T(8,128)(2,1)} %constant.33.clone.table_ref, bf16[8,2,192,256]{3,2,1,0:T(8,128)(2,1)} %copy-done.12), custom_call_target="tpu_custom_call" | custom-call | flops 1 | bytes 1 | tf_op jit(solution)/shard_map/y_transform/pallas_call | solution.py:177
  86.8 3.2 collective-permute-start.4
  90.0 23.3 %collective-permute-done.4.refs_6_.refs_5_.refs_1_ = bf16[4,16,192]{2,1,0:T(8,128)(2,1)S(1)} collective-permute-done((bf16[4,16,192]{2,1,0:T(8,128)(2,1)S(1)}, bf16[4,16,192]{2,1,0:T(8,128)(2,1)S(1)}, u32[]{:S(2)}, u32[]{:S(2)}) %collective-permute-start.4) | collective-permute-done | bytes 24608 | tf_op jit(solution)/shard_map/ppermute | solution.py:409
  113.3 9.8 %collective-permute-start.3 = (bf16[4,16,192]{2,1,0:T(8,128)(2,1)S(1)}, bf16[4,16,192]{2,1,0:T(8,128)(2,1)S(1)}, u32[]{:S(2)}, u32[]{:S(2)}) collective-permute-start(bf16[4,16,192]{2,1,0:T(8,128)(2,1)S(1)} %pad_maximum_fusion), channel_id=1, source_target_pairs={{0,8},{8,16},{16,24},{24,0},{1,9},{9,17},{17,25},{25,1},{2,10},{10... | collective-permute-start | bytes 73736 | tf_op jit(solution)/shard_map/ppermute | solution.py:409
  124.2 6.7 %y_transform.3 = (bf16[1,2,2,192,256]{4,3,2,1,0:T(8,128)(2,1)}, bf16[1,2,2,192,256]{4,3,2,1,0:T(8,128)(2,1)}, bf16[1,2,2,192,256]{4,3,2,1,0:T(8,128)(2,1)}, bf16[1,2,2,192,256]{4,3,2,1,0:T(8,128)(2,1)}) custom-call(s32[1]{0:T(128)} %bitcast.me_ref, bf16[1536,1536]{1,0:T(8,128)(2,1)} %constant.33.clone.table_ref, ...), custom_call_target="tpu_custom_call" | custom-call | flops 1 | bytes 1 | tf_op jit(solution)/shard_map/y_transform/pallas_call | solution.py:177
  131.1 3.8 collective-permute-start.2
  138.8 47.4 %collective-permute-done.8.refs_2_ = bf16[2,2,192,256]{3,2,1,0:T(8,128)(2,1)} collective-permute-done((bf16[2,2,192,256]{3,2,1,0:T(8,128)(2,1)}, bf16[2,2,192,256]{3,2,1,0:T(8,128)(2,1)}, u32[]{:S(2)}, u32[]{:S(2)}) %collective-permute-start.8) | collective-permute-done | bytes 393248 | tf_op jit(solution)/shard_map/ppermute | solution.py:646
  189.0 3.0 x_transform.5.refs_2_.refs_3_
  192.0 3.2 x_transform.4.refs_4_.refs_2_.refs_3_
  195.4 3.3 x_transform.3.refs_3_.refs_2_
  198.7 3.1 curl_inverse.3
  201.9 6.8 %collective-permute-start.19 = (bf16[2,2,192,256]{3,2,1,0:T(8,128)(2,1)S(1)}, bf16[2,2,192,256]{3,2,1,0:T(8,128)(2,1)S(1)}, u32[]{:S(2)}, u32[]{:S(2)}) collective-permute-start(bf16[2,2,192,256]{3,2,1,0:T(8,128)(2,1)S(1)} %get-tuple-element.70), channel_id=1, source_target_pairs={{0,8},{8,16},{16,24},{24,0},{1,9},{9,17},{17,25},{25,1},{2,10},{10... | collective-permute-start | bytes 1179656 | tf_op jit(solution)/shard_map/ppermute | solution.py:646
  211.1 3.8 curl_inverse.4
  214.9 3.1 curl_inverse.5
  219.5 15.2 %collective-permute-done.20 = bf16[2,2,192,256]{3,2,1,0:T(8,128)(2,1)S(1)} collective-permute-done((bf16[2,2,192,256]{3,2,1,0:T(8,128)(2,1)S(1)}, bf16[2,2,192,256]{3,2,1,0:T(8,128)(2,1)S(1)}, u32[]{:S(2)}, u32[]{:S(2)}) %collective-permute-start.20) | collective-permute-done | bytes 393248 | tf_op jit(solution)/shard_map/ppermute | solution.py:646
  234.7 4.0 y_inverse.3
  238.8 4.3 %all-to-all-start.3 = ((bf16[8,2,192,256]{3,2,1,0:T(8,128)(2,1)}), bf16[8,2,192,256]{3,2,1,0:T(8,128)(2,1)}, u32[]{:S(2)}, u32[]{:S(2)}) async-start(bf16[8,2,192,256]{3,2,1,0:T(8,128)(2,1)} %y_inverse.3), calls=%async_computation.3 | async-start | bytes 3145728 | tf_op jit(solution)/shard_map/all_to_all | solution.py:721
  243.1 8.9 %collective-permute-start.16 = (bf16[2,2,192,256]{3,2,1,0:T(8,128)(2,1)}, bf16[2,2,192,256]{3,2,1,0:T(8,128)(2,1)S(1)}, u32[]{:S(2)}, u32[]{:S(2)}) collective-permute-start(bf16[2,2,192,256]{3,2,1,0:T(8,128)(2,1)} %get-tuple-element.67), channel_id=1, source_target_pairs={{0,8},{8,16},{16,24},{24,0},{1,9},{9,17},{17,25},{25,1},{2,10},{10... | collective-permute-start | bytes 1179656 | tf_op jit(solution)/shard_map/ppermute | solution.py:646
  254.4 9.7 %all-to-all-done.3 = bf16[8,2,192,256]{3,2,1,0:T(8,128)(2,1)} async-done(((bf16[8,2,192,256]{3,2,1,0:T(8,128)(2,1)}), bf16[8,2,192,256]{3,2,1,0:T(8,128)(2,1)}, u32[]{:S(2)}, u32[]{:S(2)}) %all-to-all-start.3) | async-done | bytes 1572896 | tf_op jit(solution)/shard_map/all_to_all | solution.py:721
  264.1 4.9 %make_adjoint.3 = (f32[16,192,256]{2,1,0:T(8,128)}, bf16[16,192]{1,0:T(8,128)(2,1)}, bf16[16,192]{1,0:T(8,128)(2,1)}, bf16[16,256]{1,0:T(8,128)(2,1)}, bf16[16,256]{1,0:T(8,128)(2,1)}) custom-call(bf16[16,192,256]{2,1,0:T(8,128)(2,1)} %bitcast.34.planes_ref, f32[3,16,192,256]{3,2,1,0:T(8,128)} %cotangent_ref.5), custom_call_target="tpu_custom_call" | custom-call | flops 1 | bytes 1 | tf_op jit(solution)/shard_map/make_adjoint/pallas_call | solution.py:445
  269.0 10.9 %collective-permute-done.17 = bf16[2,2,192,256]{3,2,1,0:T(8,128)(2,1)S(1)} collective-permute-done((bf16[2,2,192,256]{3,2,1,0:T(8,128)(2,1)}, bf16[2,2,192,256]{3,2,1,0:T(8,128)(2,1)S(1)}, u32[]{:S(2)}, u32[]{:S(2)}) %collective-permute-start.17) | collective-permute-done | bytes 393248 | tf_op jit(solution)/shard_map/ppermute | solution.py:646
  281.9 4.0 y_inverse.4.refs_8_
  285.9 4.4 %all-to-all-start.4 = ((bf16[8,2,192,256]{3,2,1,0:T(8,128)(2,1)}), bf16[8,2,192,256]{3,2,1,0:T(8,128)(2,1)}, u32[]{:S(2)}, u32[]{:S(2)}) async-start(bf16[8,2,192,256]{3,2,1,0:T(8,128)(2,1)} %y_inverse.4.refs_8_), calls=%async_computation.4 | async-start | bytes 3145728 | tf_op jit(solution)/shard_map/all_to_all | solution.py:721
  290.3 9.0 %collective-permute-start.13 = (bf16[2,2,192,256]{3,2,1,0:T(8,128)(2,1)S(1)}, bf16[2,2,192,256]{3,2,1,0:T(8,128)(2,1)S(1)}, u32[]{:S(2)}, u32[]{:S(2)}) collective-permute-start(bf16[2,2,192,256]{3,2,1,0:T(8,128)(2,1)S(1)} %get-tuple-element.64), channel_id=1, source_target_pairs={{0,8},{8,16},{16,24},{24,0},{1,9},{9,17},{17,25},{25,1},{2,10},{10... | collective-permute-start | bytes 1179656 | tf_op jit(solution)/shard_map/ppermute | solution.py:646
  302.5 3.1 collective-permute-start.23
  305.6 21.2 %collective-permute-done.22.refs_4_ = bf16[16,192]{1,0:T(8,128)(2,1)S(1)} collective-permute-done((bf16[16,192]{1,0:T(8,128)(2,1)S(1)}, bf16[16,192]{1,0:T(8,128)(2,1)S(1)}, u32[]{:S(2)}, u32[]{:S(2)}) %collective-permute-start.22) | collective-permute-done | bytes 6176 | tf_op jit(solution)/shard_map/ppermute | solution.py:409
  329.7 7.3 %add_grad_vort.3.refs_8_ = f32[3,16,192,256]{3,2,1,0:T(8,128)} custom-call(bf16[256,256]{1,0:T(8,128)(2,1)} %constant.37.clone.refs_0_.slope_x, bf16[192,192]{1,0:T(8,128)(2,1)} %constant.38.clone.refs_1_, bf16[3,16,192,256]{3,2,1,0:T(8,128)(2,1)} %refs_2_.5, f32[16,192,256]{2,1,0:T(8,128)} %get-tuple-element.73.refs_4_.refs_3_.adjoint, ...), custom_call_target="tpu_custom_call" | custom-call | flops 1 | bytes 1 | tf_op jit(solution)/shard_map/add_grad_vort/pallas_call | solution.py:544
  338.3 7.4 %write_grad_vel.3.refs_0_.refs_8_ = f32[3,16,192,256]{3,2,1,0:T(8,128)} custom-call(bf16[256,256]{1,0:T(8,128)(2,1)} %constant.37.clone.refs_0_.slope_x, bf16[3,16,192,256]{3,2,1,0:T(8,128)(2,1)} %vorticity_below.5, bf16[3,16,192,256]{3,2,1,0:T(8,128)(2,1)} %vorticity_below.5, bf16[3,16,192,256]{3,2,1,0:T(8,128)(2,1)} %vorticity_below.5, ...), custom_call_target="tpu_custom_call" | custom-call | flops 1 | bytes 1 | tf_op jit(solution)/shard_map/write_grad_vel/pallas_call | solution.py:621
  345.7 4.9 %make_adjoint.4 = (f32[16,192,256]{2,1,0:T(8,128)}, bf16[16,192]{1,0:T(8,128)(2,1)}, bf16[16,192]{1,0:T(8,128)(2,1)}, bf16[16,256]{1,0:T(8,128)(2,1)}, bf16[16,256]{1,0:T(8,128)(2,1)}) custom-call(bf16[16,192,256]{2,1,0:T(8,128)(2,1)} %bitcast.35.planes_ref, f32[3,16,192,256]{3,2,1,0:T(8,128)} %cotangent_ref.5, f32[3,16,192,256]{3,2,1,0:T(8,128)} %write_grad_vel.3.refs_0_.refs_8_), custom_call_target="tpu_custom_call" | custom-call | flops 1 | bytes 1 | tf_op jit(solution)/shard_map/make_adjoint/pallas_call | solution.py:445
  352.6 4.0 y_inverse.5.refs_9_
  356.6 3.7 all-to-all-start.5
  363.1 8.3 %collective-permute-start.26 = (bf16[16,192]{1,0:T(8,128)(2,1)S(1)}, bf16[16,192]{1,0:T(8,128)(2,1)S(1)}, u32[]{:S(2)}, u32[]{:S(2)}) collective-permute-start(bf16[16,192]{1,0:T(8,128)(2,1)S(1)} %copy-done.37), channel_id=1, source_target_pairs={{0,8},{8,16},{16,24},{24,0},{1,9},{9,17},{17,25},{25,1},{2,10},{10... | collective-permute-start | bytes 18440 | tf_op jit(solution)/shard_map/ppermute | solution.py:409
  371.3 9.7 %add_grad_vort.4.refs_9_.refs_8_ = f32[3,16,192,256]{3,2,1,0:T(8,128)} custom-call(bf16[256,256]{1,0:T(8,128)(2,1)} %constant.37.clone.refs_0_.slope_x, bf16[192,192]{1,0:T(8,128)(2,1)} %constant.38.clone.refs_1_, bf16[3,16,192,256]{3,2,1,0:T(8,128)(2,1)} %refs_2_.5, ...), custom_call_target="tpu_custom_call", output_to_operand_aliasing={{}: (8, {})} | custom-call | flops 1 | bytes 1 | tf_op jit(solution)/shard_map/add_grad_vort/pallas_call | solution.py:544
  382.3 7.4 %write_grad_vel.4.refs_0_.refs_8_ = f32[3,16,192,256]{3,2,1,0:T(8,128)} custom-call(bf16[256,256]{1,0:T(8,128)(2,1)} %constant.37.clone.refs_0_.slope_x, bf16[3,16,192,256]{3,2,1,0:T(8,128)(2,1)} %vorticity_below.5, bf16[3,16,192,256]{3,2,1,0:T(8,128)(2,1)} %vorticity_below.5, ...), custom_call_target="tpu_custom_call", output_to_operand_aliasing={{}: (13, {})} | custom-call | flops 1 | bytes 1 | tf_op jit(solution)/shard_map/write_grad_vel/pallas_call | solution.py:621
  390.9 4.8 %make_adjoint.5 = (f32[16,192,256]{2,1,0:T(8,128)}, bf16[16,192]{1,0:T(8,128)(2,1)}, bf16[16,192]{1,0:T(8,128)(2,1)}, bf16[16,256]{1,0:T(8,128)(2,1)}, bf16[16,256]{1,0:T(8,128)(2,1)}) custom-call(bf16[16,192,256]{2,1,0:T(8,128)(2,1)} %bitcast.68, f32[3,16,192,256]{3,2,1,0:T(8,128)} %cotangent_ref.5, f32[3,16,192,256]{3,2,1,0:T(8,128)} %write_grad_vel.4.refs_0_.refs_8_), custom_call_target="tpu_custom_call" | custom-call | flops 1 | bytes 1 | tf_op jit(solution)/shard_map/make_adjoint/pallas_call | solution.py:445
  398.4 8.2 %collective-permute-start.30 = (bf16[16,192]{1,0:T(8,128)(2,1)}, bf16[16,192]{1,0:T(8,128)(2,1)S(1)}, u32[]{:S(2)}, u32[]{:S(2)}) collective-permute-start(bf16[16,192]{1,0:T(8,128)(2,1)} %get-tuple-element.84), channel_id=1, source_target_pairs={{0,8},{8,16},{16,24},{24,0},{1,9},{9,17},{17,25},{25,1},{2,10},{10... | collective-permute-start | bytes 18440 | tf_op jit(solution)/shard_map/ppermute | solution.py:409
  406.5 9.7 %add_grad_vort.5.refs_9_ = f32[3,16,192,256]{3,2,1,0:T(8,128)} custom-call(bf16[256,256]{1,0:T(8,128)(2,1)} %constant.37.clone.refs_0_.slope_x, bf16[192,192]{1,0:T(8,128)(2,1)} %constant.38.clone.refs_1_, bf16[3,16,192,256]{3,2,1,0:T(8,128)(2,1)} %refs_2_.5, f32[16,192,256]{2,1,0:T(8,128)} %get-tuple-element.83.refs_3_.adjoint, ...), custom_call_target="tpu_custom_call", output_to_operand_aliasing={{}: (8, {})} | custom-call | flops 1 | bytes 1 | tf_op jit(solution)/shard_map/add_grad_vort/pallas_call | solution.py:544
  417.5 7.4 %write_grad_vel.5 = f32[3,16,192,256]{3,2,1,0:T(8,128)} custom-call(bf16[256,256]{1,0:T(8,128)(2,1)} %constant.37.clone.refs_0_.slope_x, bf16[3,16,192,256]{3,2,1,0:T(8,128)(2,1)} %vorticity_below.5, bf16[3,16,192,256]{3,2,1,0:T(8,128)(2,1)} %vorticity_below.5, bf16[3,16,192,256]{3,2,1,0:T(8,128)(2,1)} %vorticity_below.5, ...), custom_call_target="tpu_custom_call", output_to_operand_aliasing={{}: (13, {})} | custom-call | flops 1 | bytes 1 | tf_op jit(solution)/shard_map/write_grad_vel/pallas_call | solution.py:621
  (160 shorter events, 44.4 us)
Async XLA Ops:
  3.8 26.2 %all-to-all-start.2 = ((bf16[8,2,192,256]{3,2,1,0:T(8,128)(2,1)}), bf16[8,2,192,256]{3,2,1,0:T(8,128)(2,1)S(1)}, u32[]{:S(2)}, u32[]{:S(2)}) async-start(bf16[8,2,192,256]{3,2,1,0:T(8,128)(2,1)} %bitcast.67), calls=%async_computation.2 | async-start | bytes 3145728 | tf_op jit(solution)/shard_map/all_to_all | solution.py:690
  31.2 24.5 %all-to-all-start.1 = ((bf16[8,2,192,256]{3,2,1,0:T(8,128)(2,1)}), bf16[8,2,192,256]{3,2,1,0:T(8,128)(2,1)S(1)}, u32[]{:S(2)}, u32[]{:S(2)}) async-start(bf16[8,2,192,256]{3,2,1,0:T(8,128)(2,1)} %bitcast.70), calls=%async_computation.1 | async-start | bytes 3145728 | tf_op jit(solution)/shard_map/all_to_all | solution.py:690
  55.7 68.5 %all-to-all-start = ((bf16[8,2,192,256]{3,2,1,0:T(8,128)(2,1)}), bf16[8,2,192,256]{3,2,1,0:T(8,128)(2,1)}, u32[]{:S(2)}, u32[]{:S(2)}) async-start(bf16[8,2,192,256]{3,2,1,0:T(8,128)(2,1)} %bitcast.69), calls=%async_computation | async-start | bytes 3145728 | tf_op jit(solution)/shard_map/all_to_all | solution.py:690
  73.8 57.3 %collective-permute-start.10 = (bf16[2,2,192,256]{3,2,1,0:T(8,128)(2,1)}, bf16[2,2,192,256]{3,2,1,0:T(8,128)(2,1)S(1)}, u32[]{:S(2)}, u32[]{:S(2)}) collective-permute-start(bf16[2,2,192,256]{3,2,1,0:T(8,128)(2,1)} %bitcast.81), channel_id=1, source_target_pairs={{0,8},{8,16},{16,24},{24,0},{1,9},{9,17},{17,25},{25,1},{2,10},{10... | collective-permute-start | bytes 1179656 | tf_op jit(solution)/shard_map/ppermute | solution.py:646
  75.4 55.7 %collective-permute-start.11 = (bf16[2,2,192,256]{3,2,1,0:T(8,128)(2,1)}, bf16[2,2,192,256]{3,2,1,0:T(8,128)(2,1)S(1)}, u32[]{:S(2)}, u32[]{:S(2)}) collective-permute-start(bf16[2,2,192,256]{3,2,1,0:T(8,128)(2,1)} %bitcast.79), channel_id=1, source_target_pairs={{0,16},{8,24},{16,0},{24,8},{1,17},{9,25},{17,1},{25,9},{2,18},{10... | collective-permute-start | bytes 1179656 | tf_op jit(solution)/shard_map/ppermute | solution.py:646
  78.0 56.9 %collective-permute-start.12 = (bf16[2,2,192,256]{3,2,1,0:T(8,128)(2,1)}, bf16[2,2,192,256]{3,2,1,0:T(8,128)(2,1)}, u32[]{:S(2)}, u32[]{:S(2)}) collective-permute-start(bf16[2,2,192,256]{3,2,1,0:T(8,128)(2,1)} %bitcast.78), channel_id=1, source_target_pairs={{0,24},{8,0},{16,8},{24,16},{1,25},{9,1},{17,9},{25,17},{2,26},{10... | collective-permute-start | bytes 1179656 | tf_op jit(solution)/shard_map/ppermute | solution.py:646
  86.0 50.9 %collective-permute-start.7 = (bf16[2,2,192,256]{3,2,1,0:T(8,128)(2,1)}, bf16[2,2,192,256]{3,2,1,0:T(8,128)(2,1)}, u32[]{:S(2)}, u32[]{:S(2)}) collective-permute-start(bf16[2,2,192,256]{3,2,1,0:T(8,128)(2,1)} %bitcast.80), channel_id=1, source_target_pairs={{0,8},{8,16},{16,24},{24,0},{1,9},{9,17},{17,25},{25,1},{2,10},{10... | collective-permute-start | bytes 1179656 | tf_op jit(solution)/shard_map/ppermute | solution.py:646
  86.8 26.5 %collective-permute-start.4 = (bf16[4,16,192]{2,1,0:T(8,128)(2,1)S(1)}, bf16[4,16,192]{2,1,0:T(8,128)(2,1)S(1)}, u32[]{:S(2)}, u32[]{:S(2)}) collective-permute-start(bf16[4,16,192]{2,1,0:T(8,128)(2,1)S(1)} %pad_maximum_fusion.1), channel_id=1, source_target_pairs={{8,0},{16,8},{24,16},{0,24},{9,1},{17,9},{25,17},{1,25},{10,2},{18... | collective-permute-start | bytes 73736 | tf_op jit(solution)/shard_map/ppermute | solution.py:409
  113.3 82.1 %copy-start.4 = (bf16[4,16,192]{2,1,0:T(8,128)(2,1)}, bf16[4,16,192]{2,1,0:T(8,128)(2,1)S(1)}, u32[]{:S(2)}) copy-start(bf16[4,16,192]{2,1,0:T(8,128)(2,1)S(1)} %collective-permute-done.4.refs_6_.refs_5_.refs_1_) | copy-start | bytes 73732
  113.3 17.7 %collective-permute-start.3 = (bf16[4,16,192]{2,1,0:T(8,128)(2,1)S(1)}, bf16[4,16,192]{2,1,0:T(8,128)(2,1)S(1)}, u32[]{:S(2)}, u32[]{:S(2)}) collective-permute-start(bf16[4,16,192]{2,1,0:T(8,128)(2,1)S(1)} %pad_maximum_fusion), channel_id=1, source_target_pairs={{0,8},{8,16},{16,24},{24,0},{1,9},{9,17},{17,25},{25,1},{2,10},{10... | collective-permute-start | bytes 73736 | tf_op jit(solution)/shard_map/ppermute | solution.py:409
  124.2 64.8 %copy-start.3 = (bf16[1024,1024]{1,0:T(8,128)(2,1)S(1)}, bf16[1024,1024]{1,0:T(8,128)(2,1)}, u32[]{:S(2)}) copy-start(bf16[1024,1024]{1,0:T(8,128)(2,1)} %constant.34.clone.table_ref) | copy-start | bytes 6291460
  124.2 64.8 %copy-start.9 = (bf16[1,2,2,192,256]{4,3,2,1,0:T(8,128)(2,1)S(1)}, bf16[1,2,2,192,256]{4,3,2,1,0:T(8,128)(2,1)}, u32[]{:S(2)}) copy-start(bf16[1,2,2,192,256]{4,3,2,1,0:T(8,128)(2,1)} %get-tuple-element.57) | copy-start | bytes 1179652
  130.9 64.4 %copy-start.5 = (bf16[4,16,192]{2,1,0:T(8,128)(2,1)}, bf16[4,16,192]{2,1,0:T(8,128)(2,1)S(1)}, u32[]{:S(2)}) copy-start(bf16[4,16,192]{2,1,0:T(8,128)(2,1)S(1)} %collective-permute-done.3.refs_5_.refs_4_.refs_0_) | copy-start | bytes 73732
  130.9 64.3 %collective-permute-start = (bf16[2,2,192,256]{3,2,1,0:T(8,128)(2,1)}, bf16[2,2,192,256]{3,2,1,0:T(8,128)(2,1)}, u32[]{:S(2)}, u32[]{:S(2)}) collective-permute-start(bf16[2,2,192,256]{3,2,1,0:T(8,128)(2,1)} %bitcast.77), channel_id=1, source_target_pairs={{0,8},{8,16},{16,24},{24,0},{1,9},{9,17},{17,25},{25,1},{2,10},{10... | collective-permute-start | bytes 1179656 | tf_op jit(solution)/shard_map/ppermute | solution.py:646
  131.0 64.3 %collective-permute-start.1 = (bf16[2,2,192,256]{3,2,1,0:T(8,128)(2,1)}, bf16[2,2,192,256]{3,2,1,0:T(8,128)(2,1)}, u32[]{:S(2)}, u32[]{:S(2)}) collective-permute-start(bf16[2,2,192,256]{3,2,1,0:T(8,128)(2,1)} %bitcast.76), channel_id=1, source_target_pairs={{0,16},{8,24},{16,0},{24,8},{1,17},{9,25},{17,1},{25,9},{2,18},{10... | collective-permute-start | bytes 1179656 | tf_op jit(solution)/shard_map/ppermute | solution.py:646
  131.1 64.2 %collective-permute-start.2 = (bf16[2,2,192,256]{3,2,1,0:T(8,128)(2,1)}, bf16[2,2,192,256]{3,2,1,0:T(8,128)(2,1)}, u32[]{:S(2)}, u32[]{:S(2)}) collective-permute-start(bf16[2,2,192,256]{3,2,1,0:T(8,128)(2,1)} %bitcast.75), channel_id=1, source_target_pairs={{0,24},{8,0},{16,8},{24,16},{1,25},{9,1},{17,9},{25,17},{2,26},{10... | collective-permute-start | bytes 1179656 | tf_op jit(solution)/shard_map/ppermute | solution.py:646
  134.9 51.3 %collective-permute-start.8 = (bf16[2,2,192,256]{3,2,1,0:T(8,128)(2,1)}, bf16[2,2,192,256]{3,2,1,0:T(8,128)(2,1)}, u32[]{:S(2)}, u32[]{:S(2)}) collective-permute-start(bf16[2,2,192,256]{3,2,1,0:T(8,128)(2,1)} %bitcast.15), channel_id=1, source_target_pairs={{0,16},{8,24},{16,0},{24,8},{1,17},{9,25},{17,1},{25,9},{2,18},{10... | collective-permute-start | bytes 1179656 | tf_op jit(solution)/shard_map/ppermute | solution.py:646
  136.9 49.4 %collective-permute-start.9 = (bf16[2,2,192,256]{3,2,1,0:T(8,128)(2,1)}, bf16[2,2,192,256]{3,2,1,0:T(8,128)(2,1)}, u32[]{:S(2)}, u32[]{:S(2)}) collective-permute-start(bf16[2,2,192,256]{3,2,1,0:T(8,128)(2,1)} %bitcast.16), channel_id=1, source_target_pairs={{0,24},{8,0},{16,8},{24,16},{1,25},{9,1},{17,9},{25,17},{2,26},{10... | collective-permute-start | bytes 1179656 | tf_op jit(solution)/shard_map/ppermute | solution.py:646
  186.2 9.0 %collective-permute-start.5 = (bf16[4,16,256]{2,1,0:T(8,128)(2,1)S(1)}, bf16[4,16,256]{2,1,0:T(8,128)(2,1)S(1)}, u32[]{:S(2)}, u32[]{:S(2)}) collective-permute-start(bf16[4,16,256]{2,1,0:T(8,128)(2,1)S(1)} %pad_maximum_fusion.2), channel_id=1, source_target_pairs={{0,1},{1,2},{2,3},{3,4},{4,5},{5,6},{6,7},{7,0},{8,9},{9,10},{10,1... | collective-permute-start | bytes 98312 | tf_op jit(solution)/shard_map/ppermute | solution.py:409
  186.2 9.0 %collective-permute-start.6 = (bf16[4,16,256]{2,1,0:T(8,128)(2,1)S(1)}, bf16[4,16,256]{2,1,0:T(8,128)(2,1)S(1)}, u32[]{:S(2)}, u32[]{:S(2)}) collective-permute-start(bf16[4,16,256]{2,1,0:T(8,128)(2,1)S(1)} %pad_maximum_fusion.3), channel_id=1, source_target_pairs={{1,0},{2,1},{3,2},{4,3},{5,4},{6,5},{7,6},{0,7},{9,8},{10,9},{11,1... | collective-permute-start | bytes 98312 | tf_op jit(solution)/shard_map/ppermute | solution.py:409
  201.9 17.6 %collective-permute-start.19 = (bf16[2,2,192,256]{3,2,1,0:T(8,128)(2,1)S(1)}, bf16[2,2,192,256]{3,2,1,0:T(8,128)(2,1)S(1)}, u32[]{:S(2)}, u32[]{:S(2)}) collective-permute-start(bf16[2,2,192,256]{3,2,1,0:T(8,128)(2,1)S(1)} %get-tuple-element.70), channel_id=1, source_target_pairs={{0,8},{8,16},{16,24},{24,0},{1,9},{9,17},{17,25},{25,1},{2,10},{10... | collective-permute-start | bytes 1179656 | tf_op jit(solution)/shard_map/ppermute | solution.py:646
  208.7 26.0 %collective-permute-start.20 = (bf16[2,2,192,256]{3,2,1,0:T(8,128)(2,1)S(1)}, bf16[2,2,192,256]{3,2,1,0:T(8,128)(2,1)S(1)}, u32[]{:S(2)}, u32[]{:S(2)}) collective-permute-start(bf16[2,2,192,256]{3,2,1,0:T(8,128)(2,1)S(1)} %get-tuple-element.71), channel_id=1, source_target_pairs={{0,16},{8,24},{16,0},{24,8},{1,17},{9,25},{17,1},{25,9},{2,18},{10... | collective-permute-start | bytes 1179656 | tf_op jit(solution)/shard_map/ppermute | solution.py:646
  209.9 24.8 %collective-permute-start.21 = (bf16[2,2,192,256]{3,2,1,0:T(8,128)(2,1)S(1)}, bf16[2,2,192,256]{3,2,1,0:T(8,128)(2,1)S(1)}, u32[]{:S(2)}, u32[]{:S(2)}) collective-permute-start(bf16[2,2,192,256]{3,2,1,0:T(8,128)(2,1)S(1)} %get-tuple-element.72), channel_id=1, source_target_pairs={{0,24},{8,0},{16,8},{24,16},{1,25},{9,1},{17,9},{25,17},{2,26},{10... | collective-permute-start | bytes 1179656 | tf_op jit(solution)/shard_map/ppermute | solution.py:646
  214.9 19.8 %slice-start = ((s8[4718592]{0:T(1024)(128)(4,1)}), s8[4194304]{0:T(1024)(128)(4,1)S(1)}, s32[]{:S(2)}) async-start(s8[4718592]{0:T(1024)(128)(4,1)} %bitcast.45), calls=%async_computation.6 | async-start | bytes 8388608
  214.9 19.8 %slice-start.1 = ((s8[4718592]{0:T(1024)(128)(4,1)}), s8[524288]{0:T(1024)(128)(4,1)S(1)}, s32[]{:S(2)}) async-start(s8[4718592]{0:T(1024)(128)(4,1)} %bitcast.45), calls=%async_computation.7 | async-start | bytes 1048576
  238.8 25.3 %all-to-all-start.3 = ((bf16[8,2,192,256]{3,2,1,0:T(8,128)(2,1)}), bf16[8,2,192,256]{3,2,1,0:T(8,128)(2,1)}, u32[]{:S(2)}, u32[]{:S(2)}) async-start(bf16[8,2,192,256]{3,2,1,0:T(8,128)(2,1)} %y_inverse.3), calls=%async_computation.3 | async-start | bytes 3145728 | tf_op jit(solution)/shard_map/all_to_all | solution.py:721
  243.1 25.9 %collective-permute-start.16 = (bf16[2,2,192,256]{3,2,1,0:T(8,128)(2,1)}, bf16[2,2,192,256]{3,2,1,0:T(8,128)(2,1)S(1)}, u32[]{:S(2)}, u32[]{:S(2)}) collective-permute-start(bf16[2,2,192,256]{3,2,1,0:T(8,128)(2,1)} %get-tuple-element.67), channel_id=1, source_target_pairs={{0,8},{8,16},{16,24},{24,0},{1,9},{9,17},{17,25},{25,1},{2,10},{10... | collective-permute-start | bytes 1179656 | tf_op jit(solution)/shard_map/ppermute | solution.py:646
  252.0 28.0 %collective-permute-start.17 = (bf16[2,2,192,256]{3,2,1,0:T(8,128)(2,1)}, bf16[2,2,192,256]{3,2,1,0:T(8,128)(2,1)S(1)}, u32[]{:S(2)}, u32[]{:S(2)}) collective-permute-start(bf16[2,2,192,256]{3,2,1,0:T(8,128)(2,1)} %get-tuple-element.68), channel_id=1, source_target_pairs={{0,16},{8,24},{16,0},{24,8},{1,17},{9,25},{17,1},{25,9},{2,18},{10... | collective-permute-start | bytes 1179656 | tf_op jit(solution)/shard_map/ppermute | solution.py:646
  253.7 26.2 %collective-permute-start.18 = (bf16[2,2,192,256]{3,2,1,0:T(8,128)(2,1)S(1)}, bf16[2,2,192,256]{3,2,1,0:T(8,128)(2,1)S(1)}, u32[]{:S(2)}, u32[]{:S(2)}) collective-permute-start(bf16[2,2,192,256]{3,2,1,0:T(8,128)(2,1)S(1)} %get-tuple-element.69), channel_id=1, source_target_pairs={{0,24},{8,0},{16,8},{24,16},{1,25},{9,1},{17,9},{25,17},{2,26},{10... | collective-permute-start | bytes 1179656 | tf_op jit(solution)/shard_map/ppermute | solution.py:646
  285.9 40.9 %copy-start.31 = (bf16[16,256]{1,0:T(8,128)(2,1)S(1)}, bf16[16,256]{1,0:T(8,128)(2,1)}, u32[]{:S(2)}) copy-start(bf16[16,256]{1,0:T(8,128)(2,1)} %get-tuple-element.76) | copy-start | bytes 24580
  285.9 41.0 %copy-start.30 = (bf16[16,256]{1,0:T(8,128)(2,1)S(1)}, bf16[16,256]{1,0:T(8,128)(2,1)}, u32[]{:S(2)}) copy-start(bf16[16,256]{1,0:T(8,128)(2,1)} %get-tuple-element.77) | copy-start | bytes 24580
  285.9 59.8 %all-to-all-start.4 = ((bf16[8,2,192,256]{3,2,1,0:T(8,128)(2,1)}), bf16[8,2,192,256]{3,2,1,0:T(8,128)(2,1)}, u32[]{:S(2)}, u32[]{:S(2)}) async-start(bf16[8,2,192,256]{3,2,1,0:T(8,128)(2,1)} %y_inverse.4.refs_8_), calls=%async_computation.4 | async-start | bytes 3145728 | tf_op jit(solution)/shard_map/all_to_all | solution.py:721
  290.3 60.3 %collective-permute-start.13 = (bf16[2,2,192,256]{3,2,1,0:T(8,128)(2,1)S(1)}, bf16[2,2,192,256]{3,2,1,0:T(8,128)(2,1)S(1)}, u32[]{:S(2)}, u32[]{:S(2)}) collective-permute-start(bf16[2,2,192,256]{3,2,1,0:T(8,128)(2,1)S(1)} %get-tuple-element.64), channel_id=1, source_target_pairs={{0,8},{8,16},{16,24},{24,0},{1,9},{9,17},{17,25},{25,1},{2,10},{10... | collective-permute-start | bytes 1179656 | tf_op jit(solution)/shard_map/ppermute | solution.py:646
  299.3 51.4 %collective-permute-start.14 = (bf16[2,2,192,256]{3,2,1,0:T(8,128)(2,1)S(1)}, bf16[2,2,192,256]{3,2,1,0:T(8,128)(2,1)S(1)}, u32[]{:S(2)}, u32[]{:S(2)}) collective-permute-start(bf16[2,2,192,256]{3,2,1,0:T(8,128)(2,1)S(1)} %get-tuple-element.65), channel_id=1, source_target_pairs={{0,16},{8,24},{16,0},{24,8},{1,17},{9,25},{17,1},{25,9},{2,18},{10... | collective-permute-start | bytes 1179656 | tf_op jit(solution)/shard_map/ppermute | solution.py:646
  300.5 50.2 %collective-permute-start.15 = (bf16[2,2,192,256]{3,2,1,0:T(8,128)(2,1)S(1)}, bf16[2,2,192,256]{3,2,1,0:T(8,128)(2,1)S(1)}, u32[]{:S(2)}, u32[]{:S(2)}) collective-permute-start(bf16[2,2,192,256]{3,2,1,0:T(8,128)(2,1)S(1)} %get-tuple-element.66), channel_id=1, source_target_pairs={{0,24},{8,0},{16,8},{24,16},{1,25},{9,1},{17,9},{25,17},{2,26},{10... | collective-permute-start | bytes 1179656 | tf_op jit(solution)/shard_map/ppermute | solution.py:646
  301.7 25.1 %collective-permute-start.22 = (bf16[16,192]{1,0:T(8,128)(2,1)S(1)}, bf16[16,192]{1,0:T(8,128)(2,1)S(1)}, u32[]{:S(2)}, u32[]{:S(2)}) collective-permute-start(bf16[16,192]{1,0:T(8,128)(2,1)S(1)} %copy-done.36), channel_id=1, source_target_pairs={{0,8},{8,16},{16,24},{24,0},{1,9},{9,17},{17,25},{25,1},{2,10},{10... | collective-permute-start | bytes 18440 | tf_op jit(solution)/shard_map/ppermute | solution.py:409
  302.5 24.3 %collective-permute-start.23 = (bf16[16,192]{1,0:T(8,128)(2,1)S(1)}, bf16[16,192]{1,0:T(8,128)(2,1)S(1)}, u32[]{:S(2)}, u32[]{:S(2)}) collective-permute-start(bf16[16,192]{1,0:T(8,128)(2,1)S(1)} %copy-done.33), channel_id=1, source_target_pairs={{8,0},{16,8},{24,16},{0,24},{9,1},{17,9},{25,17},{1,25},{10,2},{18... | collective-permute-start | bytes 18440 | tf_op jit(solution)/shard_map/ppermute | solution.py:409
  326.8 10.2 %collective-permute-start.24 = (bf16[16,256]{1,0:T(8,128)(2,1)S(1)}, bf16[16,256]{1,0:T(8,128)(2,1)S(1)}, u32[]{:S(2)}, u32[]{:S(2)}) collective-permute-start(bf16[16,256]{1,0:T(8,128)(2,1)S(1)} %copy-done.31), channel_id=1, source_target_pairs={{0,1},{1,2},{2,3},{3,4},{4,5},{5,6},{6,7},{7,0},{8,9},{9,10},{10,1... | collective-permute-start | bytes 24584 | tf_op jit(solution)/shard_map/ppermute | solution.py:409
  326.8 10.2 %collective-permute-start.25 = (bf16[16,256]{1,0:T(8,128)(2,1)S(1)}, bf16[16,256]{1,0:T(8,128)(2,1)S(1)}, u32[]{:S(2)}, u32[]{:S(2)}) collective-permute-start(bf16[16,256]{1,0:T(8,128)(2,1)S(1)} %copy-done.30), channel_id=1, source_target_pairs={{1,0},{2,1},{3,2},{4,3},{5,4},{6,5},{7,6},{0,7},{9,8},{10,9},{11,1... | collective-permute-start | bytes 24584 | tf_op jit(solution)/shard_map/ppermute | solution.py:409
  356.6 33.1 %all-to-all-start.5 = ((bf16[8,2,192,256]{3,2,1,0:T(8,128)(2,1)}), bf16[8,2,192,256]{3,2,1,0:T(8,128)(2,1)S(1)}, u32[]{:S(2)}, u32[]{:S(2)}) async-start(bf16[8,2,192,256]{3,2,1,0:T(8,128)(2,1)} %y_inverse.5.refs_9_), calls=%async_computation.5 | async-start | bytes 3145728 | tf_op jit(solution)/shard_map/all_to_all | solution.py:721
  360.4 20.8 %collective-permute-start.28 = (bf16[16,256]{1,0:T(8,128)(2,1)S(1)}, bf16[16,256]{1,0:T(8,128)(2,1)S(1)}, u32[]{:S(2)}, u32[]{:S(2)}) collective-permute-start(bf16[16,256]{1,0:T(8,128)(2,1)S(1)} %copy-done.34), channel_id=1, source_target_pairs={{0,1},{1,2},{2,3},{3,4},{4,5},{5,6},{6,7},{7,0},{8,9},{9,10},{10,1... | collective-permute-start | bytes 24584 | tf_op jit(solution)/shard_map/ppermute | solution.py:409
  360.8 20.4 %collective-permute-start.29 = (bf16[16,256]{1,0:T(8,128)(2,1)S(1)}, bf16[16,256]{1,0:T(8,128)(2,1)S(1)}, u32[]{:S(2)}, u32[]{:S(2)}) collective-permute-start(bf16[16,256]{1,0:T(8,128)(2,1)S(1)} %copy-done.32), channel_id=1, source_target_pairs={{1,0},{2,1},{3,2},{4,3},{5,4},{6,5},{7,6},{0,7},{9,8},{10,9},{11,1... | collective-permute-start | bytes 24584 | tf_op jit(solution)/shard_map/ppermute | solution.py:409
  363.1 18.0 %collective-permute-start.26 = (bf16[16,192]{1,0:T(8,128)(2,1)S(1)}, bf16[16,192]{1,0:T(8,128)(2,1)S(1)}, u32[]{:S(2)}, u32[]{:S(2)}) collective-permute-start(bf16[16,192]{1,0:T(8,128)(2,1)S(1)} %copy-done.37), channel_id=1, source_target_pairs={{0,8},{8,16},{16,24},{24,0},{1,9},{9,17},{17,25},{25,1},{2,10},{10... | collective-permute-start | bytes 18440 | tf_op jit(solution)/shard_map/ppermute | solution.py:409
  371.3 9.8 %collective-permute-start.27 = (bf16[16,192]{1,0:T(8,128)(2,1)S(1)}, bf16[16,192]{1,0:T(8,128)(2,1)S(1)}, u32[]{:S(2)}, u32[]{:S(2)}) collective-permute-start(bf16[16,192]{1,0:T(8,128)(2,1)S(1)} %copy-done.35), channel_id=1, source_target_pairs={{8,0},{16,8},{24,16},{0,24},{9,1},{17,9},{25,17},{1,25},{10,2},{18... | collective-permute-start | bytes 18440 | tf_op jit(solution)/shard_map/ppermute | solution.py:409
  395.7 20.6 %collective-permute-start.32 = (bf16[16,256]{1,0:T(8,128)(2,1)}, bf16[16,256]{1,0:T(8,128)(2,1)S(1)}, u32[]{:S(2)}, u32[]{:S(2)}) collective-permute-start(bf16[16,256]{1,0:T(8,128)(2,1)} %get-tuple-element.86), channel_id=1, source_target_pairs={{0,1},{1,2},{2,3},{3,4},{4,5},{5,6},{6,7},{7,0},{8,9},{9,10},{10,1... | collective-permute-start | bytes 24584 | tf_op jit(solution)/shard_map/ppermute | solution.py:409
  395.8 20.6 %collective-permute-start.33 = (bf16[16,256]{1,0:T(8,128)(2,1)}, bf16[16,256]{1,0:T(8,128)(2,1)S(1)}, u32[]{:S(2)}, u32[]{:S(2)}) collective-permute-start(bf16[16,256]{1,0:T(8,128)(2,1)} %get-tuple-element.87), channel_id=1, source_target_pairs={{1,0},{2,1},{3,2},{4,3},{5,4},{6,5},{7,6},{0,7},{9,8},{10,9},{11,1... | collective-permute-start | bytes 24584 | tf_op jit(solution)/shard_map/ppermute | solution.py:409
  398.4 17.9 %collective-permute-start.30 = (bf16[16,192]{1,0:T(8,128)(2,1)}, bf16[16,192]{1,0:T(8,128)(2,1)S(1)}, u32[]{:S(2)}, u32[]{:S(2)}) collective-permute-start(bf16[16,192]{1,0:T(8,128)(2,1)} %get-tuple-element.84), channel_id=1, source_target_pairs={{0,8},{8,16},{16,24},{24,0},{1,9},{9,17},{17,25},{25,1},{2,10},{10... | collective-permute-start | bytes 18440 | tf_op jit(solution)/shard_map/ppermute | solution.py:409
  406.5 9.8 %collective-permute-start.31 = (bf16[16,192]{1,0:T(8,128)(2,1)}, bf16[16,192]{1,0:T(8,128)(2,1)S(1)}, u32[]{:S(2)}, u32[]{:S(2)}) collective-permute-start(bf16[16,192]{1,0:T(8,128)(2,1)} %get-tuple-element.85), channel_id=1, source_target_pairs={{8,0},{16,8},{24,16},{0,24},{9,1},{17,9},{25,17},{1,25},{10,2},{18... | collective-permute-start | bytes 18440 | tf_op jit(solution)/shard_map/ppermute | solution.py:409
  (36 other events, 200.6 us)

commit v5 on v4

--- a/solution.py
+++ b/solution.py
@@ -29,7 +29,8 @@
     return pltpu.CompilerParams(vmem_limit_bytes=megabytes * 1024 * 1024)
 
 
-SMALL = pl.CostEstimate(flops=1, bytes_accessed=1, transcendentals=0)
+def takes(microseconds):
+    return pl.CostEstimate(flops=1, bytes_accessed=int(microseconds * 3.0e6), transcendentals=0)
 
 
 def tied(after):
@@ -138,42 +139,119 @@
             planes_ref[2 * k + 1, rows, columns] = sin_part.astype(bf16)
 
 
-def depth_transform(values, component):
+def depth_transform(values, component, me=None, size_y=1, after=()):
     _, _, height, width = values.shape
+    planes = Z // size_y
+    shifted_out = me is not None
+
+    def kernel(*refs):
+        if not shifted_out:
+            depth_forward_kernel(*refs)
+            return
+        me_ref, values_ref, outs, held = refs[0], refs[1], refs[2 + len(after) : -1], refs[-1]
+        depth_forward_kernel(values_ref, held)
+        for s, out in enumerate(outs):
+            target = lax.rem(me_ref[0] + s, size_y)
+            out[...] = held[pl.ds(target * planes, planes)]
+
+    block = (Z // size_y, ROWS, width)
+    out_spec = pl.BlockSpec(block, lambda j: (0, j, 0))
+    out_shape = jax.ShapeDtypeStruct((planes, height, width), bf16)
+    smem = pl.BlockSpec(memory_space=pltpu.SMEM)
     return pl.pallas_call(
-        depth_forward_kernel,
+        kernel,
         grid=(height // ROWS,),
-        in_specs=[pl.BlockSpec((1, Z, ROWS, width), lambda j: (component, 0, j, 0))],
-        out_specs=pl.BlockSpec((Z, ROWS, width), lambda j: (0, j, 0)),
-        out_shape=jax.ShapeDtypeStruct((Z, height, width), bf16),
+        in_specs=([smem] if shifted_out else [])
+        + [pl.BlockSpec((1, Z, ROWS, width), lambda j: (component, 0, j, 0))]
+        + tied(after),
+        out_specs=[out_spec] * size_y if shifted_out else out_spec,
+        out_shape=[out_shape] * size_y if shifted_out else out_shape,
+        scratch_shapes=[pltpu.VMEM((Z, ROWS, width), bf16)] if shifted_out else [],
         compiler_params=params(),
-        cost_estimate=SMALL,
+        cost_estimate=takes(3),
         name="depth_transform",
-    )(values)
+    )(*(([me] if shifted_out else []) + [values, *after]))
+
+
+def fetch_blocks(table_ref, held, arrived, order):
+    count, rows, _ = held.shape
+    copies = []
+    for s in range(count):
+        place = pl.ds(pl.multiple_of(order(s) * rows, rows), rows)
+        copies.append(pltpu.make_async_copy(table_ref.at[place], held.at[s], arrived.at[s]))
+        copies[s].start()
+    return copies
 
 
 def y_transform(me, table, columns, blocks, halves, after):
-    _, planes, _, width = columns.shape
+    whole = len(columns) == 1
+    size_y = columns[0].shape[0] if whole else len(columns)
+    planes, height, width = columns[0].shape[-3:]
     modes = HALF_Y // (blocks * halves)
     rows = Y // blocks
-    shape = (halves, planes, 2, modes, width)
-
-    def kernel(me_ref, table_ref, columns_ref, *refs):
-        outs, held, arrived = refs[len(after) : len(after) + blocks], refs[-2], refs[-1]
-        copies = []
+
+    def kernel(me_ref, table_ref, *refs):
+        parts = refs[: len(columns)]
+        out, held, arrived, lines = refs[-4:]
+        copies = fetch_blocks(table_ref, held, arrived, lambda s: s)
+        for s in range(size_y):
+            source = lax.rem(me_ref[0] + size_y - s, size_y)
+            for plane in range(planes):
+                if whole:
+                    lines[plane, s * height : (s + 1) * height, :] = parts[0][s, plane]
+                else:
+                    place = pl.ds(pl.multiple_of(source * height, height), height)
+                    lines[plane, place, :] = parts[s][plane]
         for s in range(blocks):
-            target = lax.rem(me_ref[0] + s, blocks)
-            place = pl.ds(pl.multiple_of(target * rows, rows), rows)
-            copies.append(pltpu.make_async_copy(table_ref.at[place], held.at[s], arrived.at[s]))
-            copies[s].start()
-        for s, out in enumerate(outs):
             copies[s].wait()
             for plane in range(planes):
-                column = columns_ref[:, plane].reshape(Y, width)
-                part = jnp.dot(held[s], column, preferred_element_type=f32)
-                out[:, plane] = part.astype(bf16).reshape(halves, 2, modes, width)
+                part = jnp.dot(held[s], lines[plane], preferred_element_type=f32)
+                out[s, :, plane] = part.astype(bf16).reshape(halves, 2, modes, width)
 
     vmem = pl.BlockSpec(memory_space=pltpu.VMEM)
+    return pl.pallas_call(
+        kernel,
+        in_specs=[pl.BlockSpec(memory_space=pltpu.SMEM), pl.BlockSpec(memory_space=pl.ANY)]
+        + [vmem] * len(columns)
+        + tied(after),
+        out_specs=vmem,
+        out_shape=jax.ShapeDtypeStruct((blocks, halves, planes, 2, modes, width), bf16),
+        scratch_shapes=[
+            pltpu.VMEM((blocks, rows, Y), bf16),
+            pltpu.SemaphoreType.DMA((blocks,)),
+            pltpu.VMEM((planes, Y, width), bf16),
+        ],
+        compiler_params=params(),
+        cost_estimate=takes(5),
+        name="y_transform",
+    )(me, table, *columns, *after)
+
+
+def y_inverse(me, table, modes, size_y, split, after):
+    planes, width = modes.shape[2], modes.shape[5]
+    height = Y // size_y
+    shape = (planes, height, width)
+
+    def kernel(me_ref, table_ref, modes_ref, *refs):
+        outs, held, arrived = refs[len(after) : -2], refs[-2], refs[-1]
+        copies = fetch_blocks(
+            table_ref, held, arrived, lambda s: lax.rem(me_ref[0] + s, size_y) if split else s
+        )
+        lines = [modes_ref[:, :, plane].reshape(Y, width) for plane in range(planes)]
+        for s in range(size_y):
+            copies[s].wait()
+            for plane in range(planes):
+                rows = jnp.dot(held[s], lines[plane], preferred_element_type=f32).astype(bf16)
+                if split:
+                    outs[s][plane] = rows
+                else:
+                    outs[0][s, plane] = rows
+
+    vmem = pl.BlockSpec(memory_space=pltpu.VMEM)
+    if split:
+        out_shape = [jax.ShapeDtypeStruct(shape, bf16)] * size_y
+    else:
+        out_shape = [jax.ShapeDtypeStruct((size_y,) + shape, bf16)]
     return pl.pallas_call(
         kernel,
         in_specs=[
@@ -182,87 +260,43 @@
             vmem,
         ]
         + tied(after),
-        out_specs=[vmem] * blocks,
-        out_shape=[jax.ShapeDtypeStruct(shape, bf16)] * blocks,
+        out_specs=[vmem] * len(out_shape),
+        out_shape=out_shape,
         scratch_shapes=[
-            pltpu.VMEM((blocks, rows, Y), bf16),
-            pltpu.SemaphoreType.DMA((blocks,)),
+            pltpu.VMEM((size_y, height, Y), bf16),
+            pltpu.SemaphoreType.DMA((size_y,)),
         ],
         compiler_params=params(),
-        cost_estimate=SMALL,
-        name="y_transform",
-    )(me, table, columns, *after)
-
-
-def y_inverse(me, table, modes, size_y, after):
-    blocks = len(modes)
-    halves, planes, _, _, width = modes[0].shape
-    height = Y // size_y
-    count = max(1, 384 // height)
-    rows = Y // blocks
-
-    def kernel(me_ref, table_ref, *refs):
-        parts, rows_ref, held = refs[:blocks], refs[-2], refs[-1]
-
-        @pl.when(pl.program_id(0) == 0)
-        def _():
-            for s, part in enumerate(parts):
-                source = lax.rem(me_ref[0] + blocks - s, blocks)
-                place = pl.ds(pl.multiple_of(source * rows, rows), rows)
-                for plane in range(planes):
-                    held[plane, place, :] = part[:, plane].reshape(rows, width)
-
-        for plane in range(planes):
-            out = jnp.dot(table_ref[...], held[plane], preferred_element_type=f32)
-            rows_ref[:, plane] = out.astype(bf16).reshape(count, height, width)
-
-    return pl.pallas_call(
-        kernel,
-        grid=(size_y // count,),
-        in_specs=[
-            pl.BlockSpec(memory_space=pltpu.SMEM),
-            pl.BlockSpec((count * height, Y), lambda j: (j, 0)),
-        ]
-        + [pl.BlockSpec(modes[0].shape, lambda j: (0, 0, 0, 0, 0))] * blocks
-        + tied(after),
-        out_specs=pl.BlockSpec((count, planes, height, width), lambda j: (j, 0, 0, 0)),
-        out_shape=jax.ShapeDtypeStruct((size_y, planes, height, width), bf16),
-        scratch_shapes=[pltpu.VMEM((planes, Y, width), bf16)],
-        compiler_params=params(24),
-        cost_estimate=SMALL,
+        cost_estimate=takes(4),
         name="y_inverse",
-    )(me, table, *modes, *after)
-
-
-def x_transform(me, table, modes, after):
-    blocks = len(modes)
-    _, _, count, width = modes[0].shape
-
-    def kernel(me_ref, table_ref, *refs):
-        parts, spectrum_ref, held = refs[:blocks], refs[-2], refs[-1]
-        for s, part in enumerate(parts):
-            source = lax.rem(me_ref[0] + blocks - s, blocks)
-            place = pl.ds(pl.multiple_of(source * width, width), width)
-            held[:, place] = part[0].reshape(2 * count, width)
-        spectrum = jnp.dot(held[...], table_ref[...], preferred_element_type=f32)
+    )(me, table, modes, *after)
+
+
+def x_transform(table, modes, after):
+    blocks, _, _, count, width = modes.shape
+
+    def kernel(table_ref, modes_ref, *refs):
+        spectrum_ref = refs[-1]
+        rows = jnp.concatenate(
+            [modes_ref[block, 0].reshape(2 * count, width) for block in range(blocks)], axis=1
+        )
+        spectrum = jnp.dot(rows, table_ref[...], preferred_element_type=f32)
         spectrum_ref[0] = spectrum.reshape(2, count, X)
 
     return pl.pallas_call(
         kernel,
         grid=(2,),
         in_specs=[
-            pl.BlockSpec(memory_space=pltpu.SMEM),
             pl.BlockSpec((X, X), lambda j: (0, 0)),
+            pl.BlockSpec((blocks, 1, 2, count, width), lambda j: (0, j, 0, 0, 0)),
         ]
-        + [pl.BlockSpec((1, 2, count, width), lambda j: (j, 0, 0, 0))] * blocks
         + tied(after),
         out_specs=pl.BlockSpec((1, 2, count, X), lambda j: (j, 0, 0, 0)),
         out_shape=jax.ShapeDtypeStruct((2, 2, count, X), f32),
-        scratch_shapes=[pltpu.VMEM((2 * count, X), bf16)],
         compiler_params=params(24),
-        cost_estimate=SMALL,
+        cost_estimate=takes(3),
         name="x_transform",
-    )(me, table, *modes, *after)
+    )(table, modes, *after)
 
 
 def turned(field, axis, tz, ty, tx, wave):
@@ -280,9 +314,8 @@
 }
 
 
-def curl_kernel(axes, where_ref, table_ref, plus_ref, minus_ref, *outs):
-    blocks = len(outs)
-    _, _, count, width = outs[0].shape
+def curl_kernel(axes, where_ref, table_ref, plus_ref, minus_ref, back_ref):
+    blocks, _, _, count, width = back_ref.shape
     base = where_ref[0] + pl.program_id(0) * count
     depth = where_ref[1]
     mode_y = lax.broadcasted_iota(jnp.int32, (count, HALF_X), 0) + base
@@ -311,11 +344,9 @@
                 )
             rows.append(jnp.concatenate(parts, axis=1))
     rows = jnp.concatenate(rows, axis=0)
-    for s, out in enumerate(outs):
-        target = lax.rem(where_ref[2] + s, blocks)
-        place = pl.ds(pl.multiple_of(target * width, width), width)
-        back = jnp.dot(rows, table_ref[:, place], preferred_element_type=f32)
-        out[...] = back.astype(bf16).reshape(2, 2, count, width)
+    back = jnp.dot(rows, table_ref[...], preferred_element_type=f32).astype(bf16)
+    for block in range(blocks):
+        back_ref[block] = back[:, block * width : (block + 1) * width].reshape(2, 2, count, width)
 
 
 def curl_inverse(where, table, spectra, component, blocks, after):
@@ -326,7 +357,7 @@
     spec = pl.BlockSpec((2, 2, count, X), lambda j: (0, 0, j, 0))
 
     def kernel(*refs):
-        curl_kernel((plus_axis, minus_axis), *refs[:4], *refs[4 + len(after) :])
+        curl_kernel((plus_axis, minus_axis), *refs[:4], refs[-1])
 
     return pl.pallas_call(
         kernel,
@@ -338,10 +369,10 @@
             spec,
         ]
         + tied(after),
-        out_specs=[pl.BlockSpec((2, 2, count, width), lambda j: (0, 0, j, 0))] * blocks,
-        out_shape=[jax.ShapeDtypeStruct((2, 2, total, width), bf16)] * blocks,
+        out_specs=pl.BlockSpec((blocks, 2, 2, count, width), lambda j: (0, 0, 0, j, 0)),
+        out_shape=jax.ShapeDtypeStruct((blocks, 2, 2, total, width), bf16),
         compiler_params=params(24),
-        cost_estimate=SMALL,
+        cost_estimate=takes(4),
         name="curl_inverse",
     )(where, table, spectra[plus], spectra[minus], *after)
 
@@ -397,7 +428,7 @@
         out_specs=[spec, spec],
         out_shape=[shape, shape],
         compiler_params=params(),
-        cost_estimate=SMALL,
+        cost_estimate=takes(4),
         name="edge_columns",
     )(field, *after)
 
@@ -410,7 +441,7 @@
 
 
 def adjoint_kernel(planes_ref, cotangent_ref, *refs):
-    adjoint_ref, first_x, last_x, first_y, last_y, held = refs[-6:]
+    adjoint_ref, first_x, last_x, first_y, last_y, held = refs
     _, height, width = held.shape
     scale = 1.0 / (X * Y * Z)
     base = pl.program_id(0) * ROWS
@@ -436,19 +467,31 @@
         last_y[...] = jnp.concatenate(bottom, 0).astype(bf16)
 
 
-def make_adjoint(planes, cotangent, component, after):
-    _, height, width = planes.shape
+def make_adjoint(me, parts, cotangent, component, after):
+    whole = len(parts) == 1
+    planes, height, width = parts[0].shape
     column = jax.ShapeDtypeStruct((Z, height), bf16)
     row = jax.ShapeDtypeStruct((Z, width), bf16)
     column_spec = pl.BlockSpec((Z, height), lambda j: (0, 0))
     row_spec = pl.BlockSpec((Z, width), lambda j: (0, 0))
+
+    def kernel(me_ref, *refs):
+        part_refs, cotangent_ref = refs[: len(parts)], refs[len(parts)]
+        outs, held, spectrum = refs[-7:-2], refs[-2], refs[-1]
+        if whole:
+            spectrum = part_refs[0]
+        else:
+            for s, part in enumerate(part_refs):
+                source = lax.rem(me_ref[0] + len(parts) - s, len(parts))
+                spectrum[pl.ds(source * planes, planes)] = part[...]
+        adjoint_kernel(spectrum, cotangent_ref, *outs, held)
+
     return pl.pallas_call(
-        adjoint_kernel,
+        kernel,
         grid=(height // ROWS,),
-        in_specs=[
-            pl.BlockSpec((Z, ROWS, width), lambda j: (0, j, 0)),
-            pl.BlockSpec((1, Z, ROWS, width), lambda j: (component, 0, j, 0)),
-        ]
+        in_specs=[pl.BlockSpec(memory_space=pltpu.SMEM)]
+        + [pl.BlockSpec((planes, ROWS, width), lambda j: (0, j, 0))] * len(parts)
+        + [pl.BlockSpec((1, Z, ROWS, width), lambda j: (component, 0, j, 0))]
         + tied(after),
         out_specs=[
             pl.BlockSpec((Z, ROWS, width), lambda j: (0, j, 0)),
@@ -464,11 +507,14 @@
             row,
             row,
         ],
-        scratch_shapes=[pltpu.VMEM((Z, height, width), bf16)],
+        scratch_shapes=[
+            pltpu.VMEM((Z, height, width), bf16),
+            pltpu.VMEM((Z, ROWS, width), bf16),
+        ],
         compiler_params=params(),
-        cost_estimate=SMALL,
+        cost_estimate=takes(5),
         name="make_adjoint",
-    )(planes, cotangent, *after)
+    )(me, *parts, cotangent, *after)
 
 
 def pick_row(rows, n):
@@ -549,7 +595,7 @@
         out_shape=jax.ShapeDtypeStruct((3, Z, height, width), f32),
         input_output_aliases=aliases,
         compiler_params=params(),
-        cost_estimate=SMALL,
+        cost_estimate=takes(9),
         name="add_grad_vort",
     )(*operands, *after)
 
@@ -627,17 +673,17 @@
         input_output_aliases=aliases,
         scratch_shapes=[pltpu.VMEM((LAYERS, height + 16, width), f32)],
         compiler_params=params(),
-        cost_estimate=SMALL,
+        cost_estimate=takes(7),
         name="write_grad_vel",
     )(*operands, *after)
 
 
 def pair_exchange(parts, axis, mine):
     count = lax.axis_size(axis)
-    kept = lax.dynamic_index_in_dim(parts, mine, 0, keepdims=False)
-    sent = lax.dynamic_index_in_dim(parts, 1 - mine, 0, keepdims=False)
+    kept = lax.dynamic_index_in_dim(parts, mine, 1, keepdims=False)
+    sent = lax.dynamic_index_in_dim(parts, 1 - mine, 1, keepdims=False)
     got = lax.ppermute(sent, axis, [(i, i ^ 1) for i in range(count)])
-    return jnp.where(mine == 0, jnp.stack([kept, got]), jnp.stack([got, kept]))
+    return jnp.where(mine == 0, jnp.stack([kept, got], 1), jnp.stack([got, kept], 1))
 
 
 def shifted(parts, axis):
@@ -658,20 +704,20 @@
     place_x = lax.axis_index("gx")
     place_y = lax.axis_index("gy")
     half = lax.rem(place_y, halves)
-    me = place_x.astype(jnp.int32).reshape(1)
-    where = jnp.stack(
-        [(place_x * halves + half) * modes, place_y // halves, place_x]
-    ).astype(jnp.int32)
+    me = place_y.astype(jnp.int32).reshape(1)
+    where = jnp.stack([(place_x * halves + half) * modes, place_y // halves]).astype(jnp.int32)
 
     y_table, y_back_table = y_tables(size_x * halves)
     x_table, x_back_table = x_tables()
     slope_x = slope_matrix(width)
     slope_y = np.ascontiguousarray(slope_matrix(height).T)
 
-    layers = [depth_transform(cot_vel, component) for component in FORWARD_ORDER]
-
-    velocity_first, velocity_last = edge_columns(velocity, 3, (layers[1],))
-    vorticity_first, vorticity_last = edge_columns(vorticity, 1, (layers[1],))
+    layers = [depth_transform(cot_vel, FORWARD_ORDER[0])]
+    layers.append(depth_transform(cot_vel, FORWARD_ORDER[1], me, size_y, (layers[0],)))
+    layers.append(depth_transform(cot_vel, FORWARD_ORDER[2], me, size_y, (layers[1][0],)))
+
+    velocity_first, velocity_last = edge_columns(velocity, 3, (layers[0],))
+    vorticity_first, vorticity_last = edge_columns(vorticity, 1, (layers[0],))
     low_x, high_x = exchange(
         jnp.concatenate([velocity_first, vorticity_first]),
         jnp.concatenate([velocity_last, vorticity_last]),
@@ -687,40 +733,40 @@
 
     sent = []
     for place in range(3):
-        columns = lax.all_to_all(
-            layers[place].reshape(size_y, planes, height, width), "gy", 0, 0, tiled=True
-        )
+        if place == 0:
+            columns = layers[0].reshape(size_y, planes, height, width)
+            columns = [lax.all_to_all(columns, "gy", 0, 0, tiled=True)]
+        else:
+            columns = shifted(layers[place], "gy")
         parts = y_transform(me, y_table, columns, size_x, halves, edges if place == 0 else ())
-        if halves == 1:
-            parts = [part[0] for part in parts]
-        else:
-            parts = [pair_exchange(part[:, 0], "gy", half) for part in parts]
-        sent.append(parts)
+        parts = parts.reshape(size_x, 2, 2, modes, width)
+        sent.append(parts if halves == 1 else pair_exchange(parts, "gy", half))
     spectra = {}
     for place, component in enumerate(FORWARD_ORDER):
-        after = (sent[2][0],) + saved_halos if place == 0 else ()
-        spectra[component] = x_transform(me, x_table, shifted(sent[place], "gx"), after)
+        lines = lax.all_to_all(sent[place], "gx", 0, 0, tiled=True)
+        spectra[component] = x_transform(x_table, lines, saved_halos if place == 1 else ())
 
     returned = {}
-    after = (spectra[FORWARD_ORDER[2]],)
+    after = (sent[2],)
     for component in BACK_ORDER:
         parts = curl_inverse(where, x_back_table, spectra, component, size_x, after)
-        after = (parts[0],)
-        parts = shifted(parts, "gx")
-        if halves == 1:
-            parts = [part[None] for part in parts]
+        after = (parts,)
+        parts = lax.all_to_all(parts, "gx", 0, 0, tiled=True)
+        if halves == 2:
+            parts = pair_exchange(parts, "gy", half)
+        returned[component] = parts.reshape(size_x, halves, planes, 2, modes, width)
+
+    def rows_of(component, after):
+        split = component != BACK_ORDER[2]
+        return y_inverse(me, y_back_table, returned[component], size_y, split, after)
+
+    def adjoint_of(component, rows, after):
+        if len(rows) == 1:
+            parts = [lax.all_to_all(rows[0], "gy", 0, 0, tiled=True).reshape(Z, height, width)]
         else:
-            parts = [pair_exchange(part, "gy", half)[:, None] for part in parts]
-        returned[component] = parts
-    last_curl = after
-
-    def rows_of(component, after):
-        return y_inverse(me, y_back_table, returned[component], size_y, after)
-
-    def adjoint_of(component, rows, after):
-        layers = lax.all_to_all(rows, "gy", 0, 0, tiled=True)
+            parts = shifted(rows, "gy")
         adjoint, first_x, last_x, first_y, last_y = make_adjoint(
-            layers.reshape(Z, height, width), cot_vort, component, after
+            me, parts, cot_vort, component, after
         )
         return adjoint, exchange(first_x, last_x, "gx") + exchange(first_y, last_y, "gy")
 
@@ -735,14 +781,14 @@
         )
 
     one, two, three = BACK_ORDER
-    rows_one = rows_of(one, last_curl)
+    rows_one = rows_of(one, ())
     adjoint_one, halos_one = adjoint_of(one, rows_one, ())
-    rows_two = rows_of(two, (adjoint_one,))
-    grad_vort = vort_of(one, adjoint_one, None, (rows_two,))
-    grad_vel = vel_of(one, adjoint_one, halos_one, None, (grad_vort,))
-    adjoint_two, halos_two = adjoint_of(two, rows_two, (grad_vel,))
+    rows_two = rows_of(two, ())
+    grad_vort = vort_of(one, adjoint_one, None, (rows_two[0],))
+    adjoint_two, halos_two = adjoint_of(two, rows_two, (grad_vort,))
     rows_three = rows_of(three, (adjoint_two,))
-    grad_vort = vort_of(two, adjoint_two, grad_vort, (rows_three,))
+    grad_vel = vel_of(one, adjoint_one, halos_one, None, (rows_three[0],))
+    grad_vort = vort_of(two, adjoint_two, grad_vort, (grad_vel,))
     grad_vel = vel_of(two, adjoint_two, halos_two, grad_vel, (grad_vort,))
     adjoint_three, halos_three = adjoint_of(three, rows_three, (grad_vel,))
     grad_vort = vort_of(three, adjoint_three, grad_vort, ())

time: 426 us -> 429 us (level)
  blocking collectives: 0 us -> 41.8 us
  waiting for transfers between devices: 165 us -> 128 us
  starting transfers between devices: 115 us -> 90.4 us
  local copies, waits for them, and re-layouts: 11.8 us -> 25.1 us
  Pallas kernels: 132 us -> 140 us
    all_to_all x0 -> x1, blocking collectives: none -> 41.8 us  [local(): parts = lax.all_to_all(parts, 'gx', 0, 0, tiled=True)]
    ppermute x18 -> x28, waiting for transfers between devices: 75 us -> 39.2 us  [shifted(): lax.ppermute(parts[s], axis, [(i, (i + s) % count) for i in range(count)])]
    ppermute x16, starting transfers between devices: 44.2 us -> 25.6 us  [exchange(): return (lax.ppermute(last, axis, up), lax.ppermute(first, axis, down))]
    ppermute x16, waiting for transfers between devices: 44.6 us -> 28.6 us  [exchange(): return (lax.ppermute(last, axis, up), lax.ppermute(first, axis, down))]
    all_to_all x6 -> x7, waiting for transfers between devices: 45.3 us -> 60.3 us  [the longest x3 33.2 us: local(): lines = lax.all_to_all(sent[place], 'gx', 0, 0, tiled=True)]
    unnamed x92 -> x160, local copies, waits for them, and re-layouts: 9.75 us -> 23.1 us
    ppermute x18 -> x28, starting transfers between devices: 45.2 us -> 34.8 us  [shifted(): lax.ppermute(parts[s], axis, [(i, (i + s) % count) for i in range(count)])]
    pallas_call x12, Pallas kernels: 45.7 us -> 53.8 us  [the longest x3 21.8 us: y_inverse(): pl.pallas_call(kernel, in_specs=[pl.BlockSpec(memory_space=pltpu.SMEM), p...]
  transfers between devices with their start and end apart: 40 -> 51, of which waited for: 9 -> 22; matrix products, arithmetic and copies ran while one was open for 1% -> 1% of each run, Pallas kernels for 23% -> 25%
where the time goes in v5:
time: 429 us; the launch traced here: 427 us
  Pallas kernels  140 us (33%)
  waiting for transfers between devices  128 us (30%)
  starting transfers between devices  90.4 us (21%)
  blocking collectives  41.8 us (10%)
  local copies, waits for them, and re-layouts  25.1 us (6%)
    all_to_all x1, blocking collectives, local(): parts = lax.all_to_all(parts, 'gx', 0, 0, tiled=True)  41.8 us
    ppermute x28, waiting for transfers between devices, shifted(): lax.ppermute(parts[s], axis, [(i, (i + s) % count) for i in range(count)])  39.2 us
    ppermute x28, starting transfers between devices, shifted(): lax.ppermute(parts[s], axis, [(i, (i + s) % count) for i in range(count)])  34.8 us
    all_to_all x3, waiting for transfers between devices, local(): lines = lax.all_to_all(sent[place], 'gx', 0, 0, tiled=True)  33.2 us
    ppermute x16, waiting for transfers between devices, exchange(): return (lax.ppermute(last, axis, up), lax.ppermute(first, axis, down))  28.6 us
    all_to_all x2, waiting for transfers between devices, local(): parts = lax.all_to_all(parts, 'gx', 0, 0, tiled=True)  27.1 us
    pallas_call x3, Pallas kernels, add_grad_vort(): pl.pallas_call(kernel, grid=(Z // LAYERS,), in_specs=in_specs + tied(afte...  26.8 us
    ppermute x16, starting transfers between devices, exchange(): return (lax.ppermute(last, axis, up), lax.ppermute(first, axis, down))  25.6 us
  transfers between devices with their start and end apart: 51, of which 22 were waited for; matrix products, arithmetic and copies ran while one was open for 1% of the time, Pallas kernels for 25%

profile of v5, /device:TPU:0, one launch (start us, length us, event | category | flops | bytes accessed | tf_op | source)
XLA Modules:
  0.0 427.1 jit_solution(6558533202099527811)
XLA Ops:
  0.6 3.2 depth_transform.3.refs_0_.refs_2_
  3.8 5.2 %all-to-all-start = ((bf16[8,2,192,256]{3,2,1,0:T(8,128)(2,1)}), bf16[8,2,192,256]{3,2,1,0:T(8,128)(2,1)S(1)}, u32[]{:S(2)}, u32[]{:S(2)}) async-start(bf16[8,2,192,256]{3,2,1,0:T(8,128)(2,1)} %bitcast.24), calls=%async_computation | async-start | bytes 3145728 | tf_op jit(solution)/shard_map/all_to_all | solution.py:738
  9.0 3.3 depth_transform.4
  17.4 16.5 %collective-permute-done.7.refs_1_ = bf16[2,192,256]{2,1,0:T(8,128)(2,1)S(1)} collective-permute-done((bf16[2,192,256]{2,1,0:T(8,128)(2,1)}, bf16[2,192,256]{2,1,0:T(8,128)(2,1)S(1)}, u32[]{:S(2)}, u32[]{:S(2)}) %collective-permute-start.7) | collective-permute-done | bytes 196640 | tf_op jit(solution)/shard_map/ppermute | solution.py:692
  34.8 3.2 collective-permute-start.13
  38.0 3.2 collective-permute-done.9.refs_3_
  44.7 7.0 %y_transform.5 = bf16[4,1,2,2,192,256]{5,4,3,2,1,0:T(8,128)(2,1)} custom-call(s32[1]{0:T(128)} %bitcast.me_ref.refs_0_, bf16[1536,1536]{1,0:T(8,128)(2,1)} %constant.33.clone.table_ref, bf16[2,192,256]{2,1,0:T(8,128)(2,1)} %get-tuple-element.55.refs_2_.refs_0_, bf16[2,192,256]{2,1,0:T(8,128)(2,1)} %copy-done.39, bf16[2,192,256]{2,1,0:T(8,128)(2,1)} %copy-done.41, ...), custom_call_target="tpu_custom_call" | custom-call | flops 1 | bytes 15000000 | tf_op jit(solution)/shard_map/y_transform/pallas_call | solution.py:212
  52.9 4.9 %all-to-all-start.3 = ((bf16[4,2,2,192,256]{4,3,2,1,0:T(8,128)(2,1)}), bf16[4,2,2,192,256]{4,3,2,1,0:T(8,128)(2,1)S(1)}, u32[]{:S(2)}, u32[]{:S(2)}) async-start(bf16[4,2,2,192,256]{4,3,2,1,0:T(8,128)(2,1)} %bitcast.28), calls=%async_computation.3 | async-start | bytes 3145728 | tf_op jit(solution)/shard_map/all_to_all | solution.py:746
  57.8 3.3 depth_transform.5
  67.3 2.9 collective-permute-start.5
  74.2 3.6 collective-permute-done.2.refs_3_
  77.9 3.4 collective-permute-done.4.refs_5_
  82.2 7.0 %y_transform.4 = bf16[4,1,2,2,192,256]{5,4,3,2,1,0:T(8,128)(2,1)} custom-call(s32[1]{0:T(128)} %bitcast.me_ref.refs_0_, bf16[1536,1536]{1,0:T(8,128)(2,1)} %constant.33.clone.table_ref, bf16[2,192,256]{2,1,0:T(8,128)(2,1)} %get-tuple-element.56.refs_0_, bf16[2,192,256]{2,1,0:T(8,128)(2,1)} %copy-done.38, bf16[2,192,256]{2,1,0:T(8,128)(2,1)} %copy-done.40, ...), custom_call_target="tpu_custom_call" | custom-call | flops 1 | bytes 15000000 | tf_op jit(solution)/shard_map/y_transform/pallas_call | solution.py:212
  89.2 6.4 %all-to-all-done.3.modes_ref = bf16[4,2,2,192,256]{4,3,2,1,0:T(8,128)(2,1)S(1)} async-done(((bf16[4,2,2,192,256]{4,3,2,1,0:T(8,128)(2,1)}), bf16[4,2,2,192,256]{4,3,2,1,0:T(8,128)(2,1)S(1)}, u32[]{:S(2)}, u32[]{:S(2)}) %all-to-all-start.3) | async-done | bytes 1572896 | tf_op jit(solution)/shard_map/all_to_all | solution.py:746
  95.6 3.6 all-to-all-start.2
  101.8 4.6 %edge_columns.2 = (bf16[3,16,192]{2,1,0:T(8,128)(2,1)}, bf16[3,16,192]{2,1,0:T(8,128)(2,1)}) custom-call(bf16[3,16,192,256]{3,2,1,0:T(8,128)(2,1)} %refs_2_.5, bf16[16,192,256]{2,1,0:T(8,128)(2,1)} %depth_transform.3.refs_0_.refs_2_), custom_call_target="tpu_custom_call" | custom-call | flops 1 | bytes 12000000 | tf_op jit(solution)/shard_map/edge_columns/pallas_call | solution.py:424
  106.3 7.0 %y_transform.3 = bf16[4,1,2,2,192,256]{5,4,3,2,1,0:T(8,128)(2,1)} custom-call(s32[1]{0:T(128)} %bitcast.me_ref.refs_0_, bf16[1536,1536]{1,0:T(8,128)(2,1)} %constant.33.clone.table_ref, bf16[8,2,192,256]{3,2,1,0:T(8,128)(2,1)} %copy-done.22, bf16[3,16,192]{2,1,0:T(8,128)(2,1)} %get-tuple-element.53.refs_1_, bf16[1,16,192]{2,1,0:T(8,128)(2,1)} %get-tuple-element.54.refs_2_), custom_call_target="tpu_custom_call" | custom-call | flops 1 | bytes 15000000 | tf_op jit(solution)/shard_map/y_transform/pallas_call | solution.py:212
  113.4 23.5 %all-to-all-done.2.modes_ref = bf16[4,2,2,192,256]{4,3,2,1,0:T(8,128)(2,1)S(1)} async-done(((bf16[4,2,2,192,256]{4,3,2,1,0:T(8,128)(2,1)}), bf16[4,2,2,192,256]{4,3,2,1,0:T(8,128)(2,1)S(1)}, u32[]{:S(2)}, u32[]{:S(2)}) %all-to-all-start.2) | async-done | bytes 1572896 | tf_op jit(solution)/shard_map/all_to_all | solution.py:746
  136.9 4.4 %all-to-all-start.1 = ((bf16[4,2,2,192,256]{4,3,2,1,0:T(8,128)(2,1)}), bf16[4,2,2,192,256]{4,3,2,1,0:T(8,128)(2,1)}, u32[]{:S(2)}, u32[]{:S(2)}) async-start(bf16[4,2,2,192,256]{4,3,2,1,0:T(8,128)(2,1)} %bitcast.29), calls=%async_computation.1 | async-start | bytes 3145728 | tf_op jit(solution)/shard_map/all_to_all | solution.py:746
  146.2 3.8 collective-permute-start.15
  155.5 12.4 %collective-permute-done.15.refs_1_.refs_5_ = bf16[4,16,192]{2,1,0:T(8,128)(2,1)S(1)} collective-permute-done((bf16[4,16,192]{2,1,0:T(8,128)(2,1)S(1)}, bf16[4,16,192]{2,1,0:T(8,128)(2,1)S(1)}, u32[]{:S(2)}, u32[]{:S(2)}) %collective-permute-start.15) | collective-permute-done | bytes 24608 | tf_op jit(solution)/shard_map/ppermute | solution.py:440
  167.8 4.4 %collective-permute-done.14.refs_0_.refs_4_ = bf16[4,16,192]{2,1,0:T(8,128)(2,1)S(1)} collective-permute-done((bf16[4,16,192]{2,1,0:T(8,128)(2,1)S(1)}, bf16[4,16,192]{2,1,0:T(8,128)(2,1)S(1)}, u32[]{:S(2)}, u32[]{:S(2)}) %collective-permute-start.14) | collective-permute-done | bytes 24608 | tf_op jit(solution)/shard_map/ppermute | solution.py:440
  176.0 3.3 all-to-all-done.1.modes_ref
  181.0 3.3 x_transform.3.refs_3_.refs_2_
  187.4 3.0 curl_inverse.4.refs_4_
  190.4 41.8 %all_to_all.40 = bf16[4,2,2,192,256]{4,3,2,1,0:T(8,128)(2,1)} all-to-all(bf16[4,2,2,192,256]{4,3,2,1,0:T(8,128)(2,1)S(1)} %curl_inverse.4.refs_4_), channel_id=1, replica_groups=mesh['gx'=4,'gy'=8] {'gx'}, dimensions={0} | all-to-all | bytes 3145728 | tf_op jit(solution)/shard_map/all_to_all | solution.py:754
  233.3 4.3 %all-to-all-start.6 = ((bf16[4,2,2,192,256]{4,3,2,1,0:T(8,128)(2,1)}), bf16[4,2,2,192,256]{4,3,2,1,0:T(8,128)(2,1)}, u32[]{:S(2)}, u32[]{:S(2)}) async-start(bf16[4,2,2,192,256]{4,3,2,1,0:T(8,128)(2,1)} %copy-done.9), calls=%async_computation.6 | async-start | bytes 3145728 | tf_op jit(solution)/shard_map/all_to_all | solution.py:754
  242.6 3.0 curl_inverse.5
  246.7 27.1 %all-to-all-done.6 = bf16[4,2,2,192,256]{4,3,2,1,0:T(8,128)(2,1)} async-done(((bf16[4,2,2,192,256]{4,3,2,1,0:T(8,128)(2,1)}), bf16[4,2,2,192,256]{4,3,2,1,0:T(8,128)(2,1)}, u32[]{:S(2)}, u32[]{:S(2)}) %all-to-all-start.6) | async-done | bytes 1572896 | tf_op jit(solution)/shard_map/all_to_all | solution.py:754
  273.8 3.6 all-to-all-start.4
  277.4 7.1 %y_inverse.4 = (bf16[2,192,256]{2,1,0:T(8,128)(2,1)}, bf16[2,192,256]{2,1,0:T(8,128)(2,1)}, bf16[2,192,256]{2,1,0:T(8,128)(2,1)}, bf16[2,192,256]{2,1,0:T(8,128)...) custom-call(s32[1]{0:T(128)} %bitcast.me_ref.refs_0_, ...), custom_call_target="tpu_custom_call" | custom-call | flops 1 | bytes 12000000 | tf_op jit(solution)/shard_map/y_inverse/pallas_call | solution.py:255
  288.7 7.1 %y_inverse.3 = (bf16[2,192,256]{2,1,0:T(8,128)(2,1)}, bf16[2,192,256]{2,1,0:T(8,128)(2,1)}, bf16[2,192,256]{2,1,0:T(8,128)(2,1)}, bf16[2,192,256]{2,1,0:T(8,128)...) custom-call(s32[1]{0:T(128)} %bitcast.me_ref.refs_0_, ...), custom_call_target="tpu_custom_call" | custom-call | flops 1 | bytes 12000000 | tf_op jit(solution)/shard_map/y_inverse/pallas_call | solution.py:255
  301.3 3.2 collective-permute-done.29.refs_5_
  304.5 3.2 collective-permute-start.20
  313.7 5.0 %make_adjoint.3 = (f32[16,192,256]{2,1,0:T(8,128)}, bf16[16,192]{1,0:T(8,128)(2,1)}, bf16[16,192]{1,0:T(8,128)(2,1)}, bf16[16,256]{1,0:T(8,128)(2,1)}, bf16[16,256]{1,0:T(8,128)(2,1)}) custom-call(s32[1]{0:T(128)} %bitcast.me_ref.refs_0_, bf16[2,192,256]{2,1,0:T(8,128)(2,1)} %get-tuple-element.81.refs_0_, bf16[2,192,256]{2,1,0:T(8,128)(2,1)} %copy-done.31, ...), custom_call_target="tpu_custom_call" | custom-call | flops 1 | bytes 15000000 | tf_op jit(solution)/shard_map/make_adjoint/pallas_call | solution.py:489
  318.7 7.4 %add_grad_vort.3.refs_9_.refs_8_ = f32[3,16,192,256]{3,2,1,0:T(8,128)} custom-call(bf16[256,256]{1,0:T(8,128)(2,1)} %constant.37.clone.refs_0_.slope_x, bf16[192,192]{1,0:T(8,128)(2,1)} %constant.38.clone.refs_1_, bf16[3,16,192,256]{3,2,1,0:T(8,128)(2,1)} %refs_2_.5, f32[16,192,256]{2,1,0:T(8,128)} %get-tuple-element.89.refs_3_.adjoint, ...), custom_call_target="tpu_custom_call" | custom-call | flops 1 | bytes 27000000 | tf_op jit(solution)/shard_map/add_grad_vort/pallas_call | solution.py:590
  327.6 5.0 %make_adjoint.4 = (f32[16,192,256]{2,1,0:T(8,128)}, bf16[16,192]{1,0:T(8,128)(2,1)}, bf16[16,192]{1,0:T(8,128)(2,1)}, bf16[16,256]{1,0:T(8,128)(2,1)}, bf16[16,256]{1,0:T(8,128)(2,1)}) custom-call(s32[1]{0:T(128)} %bitcast.me_ref.refs_0_, bf16[2,192,256]{2,1,0:T(8,128)(2,1)} %get-tuple-element.73.refs_8_.refs_0_, bf16[2,192,256]{2,1,0:T(8,128)(2,1)} %copy-done.24, ...), custom_call_target="tpu_custom_call" | custom-call | flops 1 | bytes 15000000 | tf_op jit(solution)/shard_map/make_adjoint/pallas_call | solution.py:489
  333.8 7.6 %y_inverse.5.refs_8_ = bf16[8,2,192,256]{3,2,1,0:T(8,128)(2,1)} custom-call(s32[1]{0:T(128)} %bitcast.me_ref.refs_0_, bf16[1536,1536]{1,0:T(8,128)(2,1)} %constant.36.clone.table_ref, bf16[4,1,2,2,192,256]{5,4,3,2,1,0:T(8,128)(2,1)} %bitcast.27, f32[16,192,256]{2,1,0:T(8,128)} %get-tuple-element.90.refs_0_.refs_3_.adjoint), custom_call_target="tpu_custom_call" | custom-call | flops 1 | bytes 12000000 | tf_op jit(solution)/shard_map/y_inverse/pallas_call | solution.py:255
  341.4 4.1 all-to-all-start.7
  354.4 11.9 %collective-permute-done.38.refs_6_ = bf16[16,256]{1,0:T(8,128)(2,1)S(1)} collective-permute-done((bf16[16,256]{1,0:T(8,128)(2,1)S(1)}, bf16[16,256]{1,0:T(8,128)(2,1)S(1)}, u32[]{:S(2)}, u32[]{:S(2)}) %collective-permute-start.38) | collective-permute-done | bytes 8224 | tf_op jit(solution)/shard_map/ppermute | solution.py:440
  366.3 3.5 collective-permute-start.33
  370.4 7.4 %write_grad_vel.3.refs_9_.refs_8_ = f32[3,16,192,256]{3,2,1,0:T(8,128)} custom-call(bf16[256,256]{1,0:T(8,128)(2,1)} %constant.37.clone.refs_0_.slope_x, bf16[3,16,192,256]{3,2,1,0:T(8,128)(2,1)} %vorticity_below.5, bf16[3,16,192,256]{3,2,1,0:T(8,128)(2,1)} %vorticity_below.5, bf16[3,16,192,256]{3,2,1,0:T(8,128)(2,1)} %vorticity_below.5, ...), custom_call_target="tpu_custom_call" | custom-call | flops 1 | bytes 21000000 | tf_op jit(solution)/shard_map/write_grad_vel/pallas_call | solution.py:667
  377.9 9.7 %add_grad_vort.4.refs_9_.refs_8_ = f32[3,16,192,256]{3,2,1,0:T(8,128)} custom-call(bf16[256,256]{1,0:T(8,128)(2,1)} %constant.37.clone.refs_0_.slope_x, bf16[192,192]{1,0:T(8,128)(2,1)} %constant.38.clone.refs_1_, bf16[3,16,192,256]{3,2,1,0:T(8,128)(2,1)} %refs_2_.5, ...), custom_call_target="tpu_custom_call", output_to_operand_aliasing={{}: (8, {})} | custom-call | flops 1 | bytes 27000000 | tf_op jit(solution)/shard_map/add_grad_vort/pallas_call | solution.py:590
  388.8 7.4 %write_grad_vel.4.refs_2_.refs_8_ = f32[3,16,192,256]{3,2,1,0:T(8,128)} custom-call(bf16[256,256]{1,0:T(8,128)(2,1)} %constant.37.clone.refs_0_.slope_x, bf16[3,16,192,256]{3,2,1,0:T(8,128)(2,1)} %vorticity_below.5, bf16[3,16,192,256]{3,2,1,0:T(8,128)(2,1)} %vorticity_below.5, ...), custom_call_target="tpu_custom_call", output_to_operand_aliasing={{}: (13, {})} | custom-call | flops 1 | bytes 21000000 | tf_op jit(solution)/shard_map/write_grad_vel/pallas_call | solution.py:667
  397.4 4.8 %make_adjoint.5 = (f32[16,192,256]{2,1,0:T(8,128)}, bf16[16,192]{1,0:T(8,128)(2,1)}, bf16[16,192]{1,0:T(8,128)(2,1)}, bf16[16,256]{1,0:T(8,128)(2,1)}, bf16[16,256]{1,0:T(8,128)(2,1)}) custom-call(s32[1]{0:T(128)} %bitcast.me_ref.refs_0_, bf16[16,192,256]{2,1,0:T(8,128)(2,1)} %bitcast.25, f32[3,16,192,256]{3,2,1,0:T(8,128)} %refs_1_.11, ...), custom_call_target="tpu_custom_call" | custom-call | flops 1 | bytes 15000000 | tf_op jit(solution)/shard_map/make_adjoint/pallas_call | solution.py:489
  404.9 3.8 collective-permute-start.41
  408.7 9.7 %add_grad_vort.5.refs_9_ = f32[3,16,192,256]{3,2,1,0:T(8,128)} custom-call(bf16[256,256]{1,0:T(8,128)(2,1)} %constant.37.clone.refs_0_.slope_x, bf16[192,192]{1,0:T(8,128)(2,1)} %constant.38.clone.refs_1_, bf16[3,16,192,256]{3,2,1,0:T(8,128)(2,1)} %refs_2_.5, f32[16,192,256]{2,1,0:T(8,128)} %get-tuple-element.99.refs_3_.adjoint, ...), custom_call_target="tpu_custom_call", output_to_operand_aliasing={{}: (8, {})} | custom-call | flops 1 | bytes 27000000 | tf_op jit(solution)/shard_map/add_grad_vort/pallas_call | solution.py:590
  419.7 7.4 %write_grad_vel.5 = f32[3,16,192,256]{3,2,1,0:T(8,128)} custom-call(bf16[256,256]{1,0:T(8,128)(2,1)} %constant.37.clone.refs_0_.slope_x, bf16[3,16,192,256]{3,2,1,0:T(8,128)(2,1)} %vorticity_below.5, bf16[3,16,192,256]{3,2,1,0:T(8,128)(2,1)} %vorticity_below.5, bf16[3,16,192,256]{3,2,1,0:T(8,128)(2,1)} %vorticity_below.5, ...), custom_call_target="tpu_custom_call", output_to_operand_aliasing={{}: (13, {})} | custom-call | flops 1 | bytes 21000000 | tf_op jit(solution)/shard_map/write_grad_vel/pallas_call | solution.py:667
  (248 shorter events, 84.2 us)
Async XLA Ops:
  3.8 47.9 %all-to-all-start = ((bf16[8,2,192,256]{3,2,1,0:T(8,128)(2,1)}), bf16[8,2,192,256]{3,2,1,0:T(8,128)(2,1)S(1)}, u32[]{:S(2)}, u32[]{:S(2)}) async-start(bf16[8,2,192,256]{3,2,1,0:T(8,128)(2,1)} %bitcast.24), calls=%async_computation | async-start | bytes 3145728 | tf_op jit(solution)/shard_map/all_to_all | solution.py:738
  12.3 21.6 %collective-permute-start.7 = (bf16[2,192,256]{2,1,0:T(8,128)(2,1)}, bf16[2,192,256]{2,1,0:T(8,128)(2,1)S(1)}, u32[]{:S(2)}, u32[]{:S(2)}) collective-permute-start(bf16[2,192,256]{2,1,0:T(8,128)(2,1)} %get-tuple-element.64), channel_id=1, source_target_pairs={{0,1},{1,2},{2,3},{3,4},{4,5},{5,6},{6,7},{7,0},{8,9},{9,10},{10,1... | collective-permute-start | bytes 589832 | tf_op jit(solution)/shard_map/ppermute | solution.py:692
  12.8 22.0 %collective-permute-start.8 = (bf16[2,192,256]{2,1,0:T(8,128)(2,1)}, bf16[2,192,256]{2,1,0:T(8,128)(2,1)S(1)}, u32[]{:S(2)}, u32[]{:S(2)}) collective-permute-start(bf16[2,192,256]{2,1,0:T(8,128)(2,1)} %get-tuple-element.65), channel_id=1, source_target_pairs={{0,2},{1,3},{2,4},{3,5},{4,6},{5,7},{6,0},{7,1},{8,10},{9,11},{10,... | collective-permute-start | bytes 589832 | tf_op jit(solution)/shard_map/ppermute | solution.py:692
  14.4 26.8 %collective-permute-start.9 = (bf16[2,192,256]{2,1,0:T(8,128)(2,1)}, bf16[2,192,256]{2,1,0:T(8,128)(2,1)S(1)}, u32[]{:S(2)}, u32[]{:S(2)}) collective-permute-start(bf16[2,192,256]{2,1,0:T(8,128)(2,1)} %get-tuple-element.66), channel_id=1, source_target_pairs={{0,3},{1,4},{2,5},{3,6},{4,7},{5,0},{6,1},{7,2},{8,11},{9,12},{10,... | collective-permute-start | bytes 589832 | tf_op jit(solution)/shard_map/ppermute | solution.py:692
  16.6 25.5 %collective-permute-start.10 = (bf16[2,192,256]{2,1,0:T(8,128)(2,1)}, bf16[2,192,256]{2,1,0:T(8,128)(2,1)S(1)}, u32[]{:S(2)}, u32[]{:S(2)}) collective-permute-start(bf16[2,192,256]{2,1,0:T(8,128)(2,1)} %get-tuple-element.67), channel_id=1, source_target_pairs={{0,4},{1,5},{2,6},{3,7},{4,0},{5,1},{6,2},{7,3},{8,12},{9,13},{10,... | collective-permute-start | bytes 589832 | tf_op jit(solution)/shard_map/ppermute | solution.py:692
  17.2 26.7 %collective-permute-start.11 = (bf16[2,192,256]{2,1,0:T(8,128)(2,1)}, bf16[2,192,256]{2,1,0:T(8,128)(2,1)S(1)}, u32[]{:S(2)}, u32[]{:S(2)}) collective-permute-start(bf16[2,192,256]{2,1,0:T(8,128)(2,1)} %get-tuple-element.68), channel_id=1, source_target_pairs={{0,5},{1,6},{2,7},{3,0},{4,1},{5,2},{6,3},{7,4},{8,13},{9,14},{10,... | collective-permute-start | bytes 589832 | tf_op jit(solution)/shard_map/ppermute | solution.py:692
  33.8 10.1 %collective-permute-start.12 = (bf16[2,192,256]{2,1,0:T(8,128)(2,1)}, bf16[2,192,256]{2,1,0:T(8,128)(2,1)S(1)}, u32[]{:S(2)}, u32[]{:S(2)}) collective-permute-start(bf16[2,192,256]{2,1,0:T(8,128)(2,1)} %get-tuple-element.69), channel_id=1, source_target_pairs={{0,6},{1,7},{2,0},{3,1},{4,2},{5,3},{6,4},{7,5},{8,14},{9,15},{10,... | collective-permute-start | bytes 589832 | tf_op jit(solution)/shard_map/ppermute | solution.py:692
  34.8 9.2 %collective-permute-start.13 = (bf16[2,192,256]{2,1,0:T(8,128)(2,1)}, bf16[2,192,256]{2,1,0:T(8,128)(2,1)S(1)}, u32[]{:S(2)}, u32[]{:S(2)}) collective-permute-start(bf16[2,192,256]{2,1,0:T(8,128)(2,1)} %get-tuple-element.70), channel_id=1, source_target_pairs={{0,7},{1,0},{2,1},{3,2},{4,3},{5,4},{6,5},{7,6},{8,15},{9,8},{10,9... | collective-permute-start | bytes 589832 | tf_op jit(solution)/shard_map/ppermute | solution.py:692
  52.9 42.7 %all-to-all-start.3 = ((bf16[4,2,2,192,256]{4,3,2,1,0:T(8,128)(2,1)}), bf16[4,2,2,192,256]{4,3,2,1,0:T(8,128)(2,1)S(1)}, u32[]{:S(2)}, u32[]{:S(2)}) async-start(bf16[4,2,2,192,256]{4,3,2,1,0:T(8,128)(2,1)} %bitcast.28), calls=%async_computation.3 | async-start | bytes 3145728 | tf_op jit(solution)/shard_map/all_to_all | solution.py:746
  62.7 9.0 %collective-permute-start.1 = (bf16[2,192,256]{2,1,0:T(8,128)(2,1)}, bf16[2,192,256]{2,1,0:T(8,128)(2,1)S(1)}, u32[]{:S(2)}, u32[]{:S(2)}) collective-permute-start(bf16[2,192,256]{2,1,0:T(8,128)(2,1)} %get-tuple-element.58), channel_id=1, source_target_pairs={{0,2},{1,3},{2,4},{3,5},{4,6},{5,7},{6,0},{7,1},{8,10},{9,11},{10,... | collective-permute-start | bytes 589832 | tf_op jit(solution)/shard_map/ppermute | solution.py:692
  64.1 13.7 %collective-permute-start.2 = (bf16[2,192,256]{2,1,0:T(8,128)(2,1)}, bf16[2,192,256]{2,1,0:T(8,128)(2,1)S(1)}, u32[]{:S(2)}, u32[]{:S(2)}) collective-permute-start(bf16[2,192,256]{2,1,0:T(8,128)(2,1)} %get-tuple-element.59), channel_id=1, source_target_pairs={{0,3},{1,4},{2,5},{3,6},{4,7},{5,0},{6,1},{7,2},{8,11},{9,12},{10,... | collective-permute-start | bytes 589832 | tf_op jit(solution)/shard_map/ppermute | solution.py:692
  65.1 12.8 %collective-permute-start.3 = (bf16[2,192,256]{2,1,0:T(8,128)(2,1)}, bf16[2,192,256]{2,1,0:T(8,128)(2,1)S(1)}, u32[]{:S(2)}, u32[]{:S(2)}) collective-permute-start(bf16[2,192,256]{2,1,0:T(8,128)(2,1)} %get-tuple-element.60), channel_id=1, source_target_pairs={{0,4},{1,5},{2,6},{3,7},{4,0},{5,1},{6,2},{7,3},{8,12},{9,13},{10,... | collective-permute-start | bytes 589832 | tf_op jit(solution)/shard_map/ppermute | solution.py:692
  65.7 15.7 %collective-permute-start.4 = (bf16[2,192,256]{2,1,0:T(8,128)(2,1)}, bf16[2,192,256]{2,1,0:T(8,128)(2,1)S(1)}, u32[]{:S(2)}, u32[]{:S(2)}) collective-permute-start(bf16[2,192,256]{2,1,0:T(8,128)(2,1)} %get-tuple-element.61), channel_id=1, source_target_pairs={{0,5},{1,6},{2,7},{3,0},{4,1},{5,2},{6,3},{7,4},{8,13},{9,14},{10,... | collective-permute-start | bytes 589832 | tf_op jit(solution)/shard_map/ppermute | solution.py:692
  67.3 14.0 %collective-permute-start.5 = (bf16[2,192,256]{2,1,0:T(8,128)(2,1)}, bf16[2,192,256]{2,1,0:T(8,128)(2,1)S(1)}, u32[]{:S(2)}, u32[]{:S(2)}) collective-permute-start(bf16[2,192,256]{2,1,0:T(8,128)(2,1)} %get-tuple-element.62), channel_id=1, source_target_pairs={{0,6},{1,7},{2,0},{3,1},{4,2},{5,3},{6,4},{7,5},{8,14},{9,15},{10,... | collective-permute-start | bytes 589832 | tf_op jit(solution)/shard_map/ppermute | solution.py:692
  71.7 9.7 %collective-permute-start.6 = (bf16[2,192,256]{2,1,0:T(8,128)(2,1)}, bf16[2,192,256]{2,1,0:T(8,128)(2,1)S(1)}, u32[]{:S(2)}, u32[]{:S(2)}) collective-permute-start(bf16[2,192,256]{2,1,0:T(8,128)(2,1)} %get-tuple-element.63), channel_id=1, source_target_pairs={{0,7},{1,0},{2,1},{3,2},{4,3},{5,4},{6,5},{7,6},{8,15},{9,8},{10,9... | collective-permute-start | bytes 589832 | tf_op jit(solution)/shard_map/ppermute | solution.py:692
  95.6 41.3 %all-to-all-start.2 = ((bf16[4,2,2,192,256]{4,3,2,1,0:T(8,128)(2,1)}), bf16[4,2,2,192,256]{4,3,2,1,0:T(8,128)(2,1)S(1)}, u32[]{:S(2)}, u32[]{:S(2)}) async-start(bf16[4,2,2,192,256]{4,3,2,1,0:T(8,128)(2,1)} %bitcast.22), calls=%async_computation.2 | async-start | bytes 3145728 | tf_op jit(solution)/shard_map/all_to_all | solution.py:746
  136.9 42.5 %all-to-all-start.1 = ((bf16[4,2,2,192,256]{4,3,2,1,0:T(8,128)(2,1)}), bf16[4,2,2,192,256]{4,3,2,1,0:T(8,128)(2,1)}, u32[]{:S(2)}, u32[]{:S(2)}) async-start(bf16[4,2,2,192,256]{4,3,2,1,0:T(8,128)(2,1)} %bitcast.29), calls=%async_computation.1 | async-start | bytes 3145728 | tf_op jit(solution)/shard_map/all_to_all | solution.py:746
  143.4 28.8 %collective-permute-start.16 = (bf16[4,16,256]{2,1,0:T(8,128)(2,1)S(1)}, bf16[4,16,256]{2,1,0:T(8,128)(2,1)S(1)}, u32[]{:S(2)}, u32[]{:S(2)}) collective-permute-start(bf16[4,16,256]{2,1,0:T(8,128)(2,1)S(1)} %pad_maximum_fusion.2), channel_id=1, source_target_pairs={{0,1},{1,2},{2,3},{3,4},{4,5},{5,6},{6,7},{7,0},{8,9},{9,10},{10,1... | collective-permute-start | bytes 98312 | tf_op jit(solution)/shard_map/ppermute | solution.py:440
  143.5 28.7 %collective-permute-start.17 = (bf16[4,16,256]{2,1,0:T(8,128)(2,1)S(1)}, bf16[4,16,256]{2,1,0:T(8,128)(2,1)S(1)}, u32[]{:S(2)}, u32[]{:S(2)}) collective-permute-start(bf16[4,16,256]{2,1,0:T(8,128)(2,1)S(1)} %pad_maximum_fusion.3), channel_id=1, source_target_pairs={{1,0},{2,1},{3,2},{4,3},{5,4},{6,5},{7,6},{0,7},{9,8},{10,9},{11,1... | collective-permute-start | bytes 98312 | tf_op jit(solution)/shard_map/ppermute | solution.py:440
  146.2 21.6 %collective-permute-start.15 = (bf16[4,16,192]{2,1,0:T(8,128)(2,1)S(1)}, bf16[4,16,192]{2,1,0:T(8,128)(2,1)S(1)}, u32[]{:S(2)}, u32[]{:S(2)}) collective-permute-start(bf16[4,16,192]{2,1,0:T(8,128)(2,1)S(1)} %pad_maximum_fusion.1), channel_id=1, source_target_pairs={{8,0},{16,8},{24,16},{0,24},{9,1},{17,9},{25,17},{1,25},{10,2},{18... | collective-permute-start | bytes 73736 | tf_op jit(solution)/shard_map/ppermute | solution.py:440
  150.0 22.2 %collective-permute-start.14 = (bf16[4,16,192]{2,1,0:T(8,128)(2,1)S(1)}, bf16[4,16,192]{2,1,0:T(8,128)(2,1)S(1)}, u32[]{:S(2)}, u32[]{:S(2)}) collective-permute-start(bf16[4,16,192]{2,1,0:T(8,128)(2,1)S(1)} %pad_maximum_fusion), channel_id=1, source_target_pairs={{0,8},{8,16},{16,24},{24,0},{1,9},{9,17},{17,25},{25,1},{2,10},{10... | collective-permute-start | bytes 73736 | tf_op jit(solution)/shard_map/ppermute | solution.py:440
  233.3 40.4 %all-to-all-start.6 = ((bf16[4,2,2,192,256]{4,3,2,1,0:T(8,128)(2,1)}), bf16[4,2,2,192,256]{4,3,2,1,0:T(8,128)(2,1)}, u32[]{:S(2)}, u32[]{:S(2)}) async-start(bf16[4,2,2,192,256]{4,3,2,1,0:T(8,128)(2,1)} %copy-done.9), calls=%async_computation.6 | async-start | bytes 3145728 | tf_op jit(solution)/shard_map/all_to_all | solution.py:754
  273.8 58.8 %all-to-all-start.4 = ((bf16[4,2,2,192,256]{4,3,2,1,0:T(8,128)(2,1)}), bf16[4,2,2,192,256]{4,3,2,1,0:T(8,128)(2,1)S(1)}, u32[]{:S(2)}, u32[]{:S(2)}) async-start(bf16[4,2,2,192,256]{4,3,2,1,0:T(8,128)(2,1)} %copy-done.14), calls=%async_computation.4 | async-start | bytes 3145728 | tf_op jit(solution)/shard_map/all_to_all | solution.py:754
  284.4 11.4 %collective-permute-start.25 = (bf16[2,192,256]{2,1,0:T(8,128)(2,1)}, bf16[2,192,256]{2,1,0:T(8,128)(2,1)S(1)}, u32[]{:S(2)}, u32[]{:S(2)}) collective-permute-start(bf16[2,192,256]{2,1,0:T(8,128)(2,1)} %get-tuple-element.82), channel_id=1, source_target_pairs={{0,1},{1,2},{2,3},{3,4},{4,5},{5,6},{6,7},{7,0},{8,9},{9,10},{10,1... | collective-permute-start | bytes 589832 | tf_op jit(solution)/shard_map/ppermute | solution.py:692
  284.5 13.1 %collective-permute-start.26 = (bf16[2,192,256]{2,1,0:T(8,128)(2,1)}, bf16[2,192,256]{2,1,0:T(8,128)(2,1)S(1)}, u32[]{:S(2)}, u32[]{:S(2)}) collective-permute-start(bf16[2,192,256]{2,1,0:T(8,128)(2,1)} %get-tuple-element.83), channel_id=1, source_target_pairs={{0,2},{1,3},{2,4},{3,5},{4,6},{5,7},{6,0},{7,1},{8,10},{9,11},{10,... | collective-permute-start | bytes 589832 | tf_op jit(solution)/shard_map/ppermute | solution.py:692
  285.9 15.3 %collective-permute-start.27 = (bf16[2,192,256]{2,1,0:T(8,128)(2,1)}, bf16[2,192,256]{2,1,0:T(8,128)(2,1)S(1)}, u32[]{:S(2)}, u32[]{:S(2)}) collective-permute-start(bf16[2,192,256]{2,1,0:T(8,128)(2,1)} %get-tuple-element.84), channel_id=1, source_target_pairs={{0,3},{1,4},{2,5},{3,6},{4,7},{5,0},{6,1},{7,2},{8,11},{9,12},{10,... | collective-permute-start | bytes 589832 | tf_op jit(solution)/shard_map/ppermute | solution.py:692
  287.1 14.2 %collective-permute-start.28 = (bf16[2,192,256]{2,1,0:T(8,128)(2,1)}, bf16[2,192,256]{2,1,0:T(8,128)(2,1)S(1)}, u32[]{:S(2)}, u32[]{:S(2)}) collective-permute-start(bf16[2,192,256]{2,1,0:T(8,128)(2,1)} %get-tuple-element.85), channel_id=1, source_target_pairs={{0,4},{1,5},{2,6},{3,7},{4,0},{5,1},{6,2},{7,3},{8,12},{9,13},{10,... | collective-permute-start | bytes 589832 | tf_op jit(solution)/shard_map/ppermute | solution.py:692
  288.7 15.8 %collective-permute-start.29 = (bf16[2,192,256]{2,1,0:T(8,128)(2,1)}, bf16[2,192,256]{2,1,0:T(8,128)(2,1)S(1)}, u32[]{:S(2)}, u32[]{:S(2)}) collective-permute-start(bf16[2,192,256]{2,1,0:T(8,128)(2,1)} %get-tuple-element.86), channel_id=1, source_target_pairs={{0,5},{1,6},{2,7},{3,0},{4,1},{5,2},{6,3},{7,4},{8,13},{9,14},{10,... | collective-permute-start | bytes 589832 | tf_op jit(solution)/shard_map/ppermute | solution.py:692
  295.9 11.8 %collective-permute-start.30 = (bf16[2,192,256]{2,1,0:T(8,128)(2,1)S(1)}, bf16[2,192,256]{2,1,0:T(8,128)(2,1)S(1)}, u32[]{:S(2)}, u32[]{:S(2)}) collective-permute-start(bf16[2,192,256]{2,1,0:T(8,128)(2,1)S(1)} %copy-done.69), channel_id=1, source_target_pairs={{0,6},{1,7},{2,0},{3,1},{4,2},{5,3},{6,4},{7,5},{8,14},{9,15},{10,... | collective-permute-start | bytes 589832 | tf_op jit(solution)/shard_map/ppermute | solution.py:692
  297.6 10.4 %collective-permute-start.31 = (bf16[2,192,256]{2,1,0:T(8,128)(2,1)S(1)}, bf16[2,192,256]{2,1,0:T(8,128)(2,1)S(1)}, u32[]{:S(2)}, u32[]{:S(2)}) collective-permute-start(bf16[2,192,256]{2,1,0:T(8,128)(2,1)S(1)} %copy-done.68), channel_id=1, source_target_pairs={{0,7},{1,0},{2,1},{3,2},{4,3},{5,4},{6,5},{7,6},{8,15},{9,8},{10,9... | collective-permute-start | bytes 589832 | tf_op jit(solution)/shard_map/ppermute | solution.py:692
  301.1 8.6 %collective-permute-start.18 = (bf16[2,192,256]{2,1,0:T(8,128)(2,1)}, bf16[2,192,256]{2,1,0:T(8,128)(2,1)S(1)}, u32[]{:S(2)}, u32[]{:S(2)}) collective-permute-start(bf16[2,192,256]{2,1,0:T(8,128)(2,1)} %get-tuple-element.74), channel_id=1, source_target_pairs={{0,1},{1,2},{2,3},{3,4},{4,5},{5,6},{6,7},{7,0},{8,9},{9,10},{10,1... | collective-permute-start | bytes 589832 | tf_op jit(solution)/shard_map/ppermute | solution.py:692
  301.3 10.2 %collective-permute-start.19 = (bf16[2,192,256]{2,1,0:T(8,128)(2,1)}, bf16[2,192,256]{2,1,0:T(8,128)(2,1)S(1)}, u32[]{:S(2)}, u32[]{:S(2)}) collective-permute-start(bf16[2,192,256]{2,1,0:T(8,128)(2,1)} %get-tuple-element.75), channel_id=1, source_target_pairs={{0,2},{1,3},{2,4},{3,5},{4,6},{5,7},{6,0},{7,1},{8,10},{9,11},{10,... | collective-permute-start | bytes 589832 | tf_op jit(solution)/shard_map/ppermute | solution.py:692
  304.5 21.6 %collective-permute-start.20 = (bf16[2,192,256]{2,1,0:T(8,128)(2,1)}, bf16[2,192,256]{2,1,0:T(8,128)(2,1)S(1)}, u32[]{:S(2)}, u32[]{:S(2)}) collective-permute-start(bf16[2,192,256]{2,1,0:T(8,128)(2,1)} %get-tuple-element.76), channel_id=1, source_target_pairs={{0,3},{1,4},{2,5},{3,6},{4,7},{5,0},{6,1},{7,2},{8,11},{9,12},{10,... | collective-permute-start | bytes 589832 | tf_op jit(solution)/shard_map/ppermute | solution.py:692
  307.7 18.4 %collective-permute-start.21 = (bf16[2,192,256]{2,1,0:T(8,128)(2,1)}, bf16[2,192,256]{2,1,0:T(8,128)(2,1)S(1)}, u32[]{:S(2)}, u32[]{:S(2)}) collective-permute-start(bf16[2,192,256]{2,1,0:T(8,128)(2,1)} %get-tuple-element.77), channel_id=1, source_target_pairs={{0,4},{1,5},{2,6},{3,7},{4,0},{5,1},{6,2},{7,3},{8,12},{9,13},{10,... | collective-permute-start | bytes 589832 | tf_op jit(solution)/shard_map/ppermute | solution.py:692
  308.0 18.1 %collective-permute-start.22 = (bf16[2,192,256]{2,1,0:T(8,128)(2,1)}, bf16[2,192,256]{2,1,0:T(8,128)(2,1)S(1)}, u32[]{:S(2)}, u32[]{:S(2)}) collective-permute-start(bf16[2,192,256]{2,1,0:T(8,128)(2,1)} %get-tuple-element.78), channel_id=1, source_target_pairs={{0,5},{1,6},{2,7},{3,0},{4,1},{5,2},{6,3},{7,4},{8,13},{9,14},{10,... | collective-permute-start | bytes 589832 | tf_op jit(solution)/shard_map/ppermute | solution.py:692
  309.7 16.4 %collective-permute-start.23 = (bf16[2,192,256]{2,1,0:T(8,128)(2,1)}, bf16[2,192,256]{2,1,0:T(8,128)(2,1)S(1)}, u32[]{:S(2)}, u32[]{:S(2)}) collective-permute-start(bf16[2,192,256]{2,1,0:T(8,128)(2,1)} %get-tuple-element.79), channel_id=1, source_target_pairs={{0,6},{1,7},{2,0},{3,1},{4,2},{5,3},{6,4},{7,5},{8,14},{9,15},{10,... | collective-permute-start | bytes 589832 | tf_op jit(solution)/shard_map/ppermute | solution.py:692
  311.5 14.7 %collective-permute-start.24 = (bf16[2,192,256]{2,1,0:T(8,128)(2,1)}, bf16[2,192,256]{2,1,0:T(8,128)(2,1)S(1)}, u32[]{:S(2)}, u32[]{:S(2)}) collective-permute-start(bf16[2,192,256]{2,1,0:T(8,128)(2,1)} %get-tuple-element.80), channel_id=1, source_target_pairs={{0,7},{1,0},{2,1},{3,2},{4,3},{5,4},{6,5},{7,6},{8,15},{9,8},{10,9... | collective-permute-start | bytes 589832 | tf_op jit(solution)/shard_map/ppermute | solution.py:692
  341.4 54.9 %all-to-all-start.7 = ((bf16[8,2,192,256]{3,2,1,0:T(8,128)(2,1)}), bf16[8,2,192,256]{3,2,1,0:T(8,128)(2,1)S(1)}, u32[]{:S(2)}, u32[]{:S(2)}) async-start(bf16[8,2,192,256]{3,2,1,0:T(8,128)(2,1)} %y_inverse.5.refs_8_), calls=%async_computation.7 | async-start | bytes 3145728 | tf_op jit(solution)/shard_map/all_to_all | solution.py:765
  345.5 20.7 %collective-permute-start.38 = (bf16[16,256]{1,0:T(8,128)(2,1)S(1)}, bf16[16,256]{1,0:T(8,128)(2,1)S(1)}, u32[]{:S(2)}, u32[]{:S(2)}) collective-permute-start(bf16[16,256]{1,0:T(8,128)(2,1)S(1)} %copy-done.71), channel_id=1, source_target_pairs={{0,1},{1,2},{2,3},{3,4},{4,5},{5,6},{6,7},{7,0},{8,9},{9,10},{10,1... | collective-permute-start | bytes 24584 | tf_op jit(solution)/shard_map/ppermute | solution.py:440
  349.9 19.9 %collective-permute-start.39 = (bf16[16,256]{1,0:T(8,128)(2,1)S(1)}, bf16[16,256]{1,0:T(8,128)(2,1)S(1)}, u32[]{:S(2)}, u32[]{:S(2)}) collective-permute-start(bf16[16,256]{1,0:T(8,128)(2,1)S(1)} %copy-done.70), channel_id=1, source_target_pairs={{1,0},{2,1},{3,2},{4,3},{5,4},{6,5},{7,6},{0,7},{9,8},{10,9},{11,1... | collective-permute-start | bytes 24584 | tf_op jit(solution)/shard_map/ppermute | solution.py:440
  351.6 36.0 %collective-permute-start.34 = (bf16[16,256]{1,0:T(8,128)(2,1)S(1)}, bf16[16,256]{1,0:T(8,128)(2,1)S(1)}, u32[]{:S(2)}, u32[]{:S(2)}) collective-permute-start(bf16[16,256]{1,0:T(8,128)(2,1)S(1)} %copy-done.74), channel_id=1, source_target_pairs={{0,1},{1,2},{2,3},{3,4},{4,5},{5,6},{6,7},{7,0},{8,9},{9,10},{10,1... | collective-permute-start | bytes 24584 | tf_op jit(solution)/shard_map/ppermute | solution.py:440
  351.6 36.0 %collective-permute-start.35 = (bf16[16,256]{1,0:T(8,128)(2,1)S(1)}, bf16[16,256]{1,0:T(8,128)(2,1)S(1)}, u32[]{:S(2)}, u32[]{:S(2)}) collective-permute-start(bf16[16,256]{1,0:T(8,128)(2,1)S(1)} %copy-done.72), channel_id=1, source_target_pairs={{1,0},{2,1},{3,2},{4,3},{5,4},{6,5},{7,6},{0,7},{9,8},{10,9},{11,1... | collective-permute-start | bytes 24584 | tf_op jit(solution)/shard_map/ppermute | solution.py:440
  354.3 33.3 %collective-permute-start.32 = (bf16[16,192]{1,0:T(8,128)(2,1)S(1)}, bf16[16,192]{1,0:T(8,128)(2,1)S(1)}, u32[]{:S(2)}, u32[]{:S(2)}) collective-permute-start(bf16[16,192]{1,0:T(8,128)(2,1)S(1)} %copy-done.76), channel_id=1, source_target_pairs={{0,8},{8,16},{16,24},{24,0},{1,9},{9,17},{17,25},{25,1},{2,10},{10... | collective-permute-start | bytes 18440 | tf_op jit(solution)/shard_map/ppermute | solution.py:440
  366.3 21.4 %collective-permute-start.33 = (bf16[16,192]{1,0:T(8,128)(2,1)S(1)}, bf16[16,192]{1,0:T(8,128)(2,1)S(1)}, u32[]{:S(2)}, u32[]{:S(2)}) collective-permute-start(bf16[16,192]{1,0:T(8,128)(2,1)S(1)} %copy-done.75), channel_id=1, source_target_pairs={{8,0},{16,8},{24,16},{0,24},{9,1},{17,9},{25,17},{1,25},{10,2},{18... | collective-permute-start | bytes 18440 | tf_op jit(solution)/shard_map/ppermute | solution.py:440
  402.2 16.3 %collective-permute-start.42 = (bf16[16,256]{1,0:T(8,128)(2,1)}, bf16[16,256]{1,0:T(8,128)(2,1)S(1)}, u32[]{:S(2)}, u32[]{:S(2)}) collective-permute-start(bf16[16,256]{1,0:T(8,128)(2,1)} %get-tuple-element.102), channel_id=1, source_target_pairs={{0,1},{1,2},{2,3},{3,4},{4,5},{5,6},{6,7},{7,0},{8,9},{9,10},{10,1... | collective-permute-start | bytes 24584 | tf_op jit(solution)/shard_map/ppermute | solution.py:440
  402.3 16.2 %collective-permute-start.43 = (bf16[16,256]{1,0:T(8,128)(2,1)}, bf16[16,256]{1,0:T(8,128)(2,1)S(1)}, u32[]{:S(2)}, u32[]{:S(2)}) collective-permute-start(bf16[16,256]{1,0:T(8,128)(2,1)} %get-tuple-element.103), channel_id=1, source_target_pairs={{1,0},{2,1},{3,2},{4,3},{5,4},{6,5},{7,6},{0,7},{9,8},{10,9},{11,1... | collective-permute-start | bytes 24584 | tf_op jit(solution)/shard_map/ppermute | solution.py:440
  404.9 13.5 %collective-permute-start.40 = (bf16[16,192]{1,0:T(8,128)(2,1)}, bf16[16,192]{1,0:T(8,128)(2,1)S(1)}, u32[]{:S(2)}, u32[]{:S(2)}) collective-permute-start(bf16[16,192]{1,0:T(8,128)(2,1)} %get-tuple-element.100), channel_id=1, source_target_pairs={{0,8},{8,16},{16,24},{24,0},{1,9},{9,17},{17,25},{25,1},{2,10},{10... | collective-permute-start | bytes 18440 | tf_op jit(solution)/shard_map/ppermute | solution.py:440
  404.9 13.5 %collective-permute-start.41 = (bf16[16,192]{1,0:T(8,128)(2,1)}, bf16[16,192]{1,0:T(8,128)(2,1)S(1)}, u32[]{:S(2)}, u32[]{:S(2)}) collective-permute-start(bf16[16,192]{1,0:T(8,128)(2,1)} %get-tuple-element.101), channel_id=1, source_target_pairs={{8,0},{16,8},{24,16},{0,24},{9,1},{17,9},{25,17},{1,25},{10,2},{18... | collective-permute-start | bytes 18440 | tf_op jit(solution)/shard_map/ppermute | solution.py:440
  (81 other events, 540.8 us)

commit v6 on v5

--- a/solution.py
+++ b/solution.py
@@ -600,8 +600,9 @@
     )(*operands, *after)
 
 
-def grad_vel_kernel(slope_x, vorticity, vorticity_above, vorticity_below, adjoint, *refs):
-    vort_low_x, vort_high_x, vort_low_y, vort_high_y, low_x, high_x, low_y, high_y = refs[:8]
+def grad_vel_kernel(count, slope_x, vorticity, vorticity_above, vorticity_below, *refs):
+    adjoints, saved, halos = refs[: 3 * count], refs[3 * count :], refs[3 * count + 4 :]
+    vort_low_x, vort_high_x, vort_low_y, vort_high_y = saved[:4]
     after, padded = refs[-2:]
     _, _, height, width = vorticity.shape
     first = pl.program_id(0) * LAYERS
@@ -609,71 +610,84 @@
     def times(one, other):
         return one.astype(f32) * other.astype(f32)
 
-    ends = spread_columns(
-        times(vort_low_x[0], low_x[...]),
-        times(vort_high_x[0], high_x[...]),
-        first,
-        LAYERS,
-        width,
-    )
-    values = adjoint[pl.ds(first, LAYERS)]
-    product = (vorticity[0].astype(f32) * values).astype(bf16).reshape(LAYERS * height, width)
-    inner = jnp.dot(product, slope_x[...], preferred_element_type=f32)
-    up = adjoint[lax.rem(first + LAYERS, Z)] * vorticity_above[0, 0].astype(f32)
-    down = adjoint[lax.rem(first + Z - 1, Z)] * vorticity_below[0, 0].astype(f32)
-    deep = [down] + [vorticity[2, k].astype(f32) * values[k] for k in range(LAYERS)] + [up]
-    for k in range(LAYERS):
-        n = first + k
-        padded[k, 8 : 8 + height, :] = vorticity[1, k].astype(f32) * values[k]
-        padded[k, 7:8, :] = pick_row(vort_low_y[0], n) * pick_row(low_y[...], n)
-        padded[k, 8 + height : 9 + height, :] = pick_row(vort_high_y[0], n) * pick_row(
-            high_y[...], n
-        )
-        total = (padded[k, 9 : 9 + height, :] - padded[k, 7 : 7 + height, :]) + (
-            deep[k + 2] - deep[k]
-        )
-        total = total * 0.5 + inner[k * height : (k + 1) * height] + ends[k]
-        after[0, k] = total * -step_size
-
-
-def write_grad_vel(component, slope_x, vorticity, adjoint, saved_halos, halos, before, after):
+    for c in range(count):
+        here, above, below = adjoints[3 * c : 3 * c + 3]
+        low_x, high_x, low_y, high_y = halos[4 * c : 4 * c + 4]
+        ends = spread_columns(
+            times(vort_low_x[0], low_x[...]),
+            times(vort_high_x[0], high_x[...]),
+            first,
+            LAYERS,
+            width,
+        )
+        product = [times(vorticity[0, k], here[k]).astype(bf16) for k in range(LAYERS)]
+        inner = jnp.dot(
+            jnp.concatenate(product, axis=0), slope_x[...], preferred_element_type=f32
+        )
+        deep = [times(vorticity_below[0, 0], below[0])]
+        deep = deep + [times(vorticity[2, k], here[k]) for k in range(LAYERS)]
+        deep = deep + [times(vorticity_above[0, 0], above[0])]
+        for k in range(LAYERS):
+            n = first + k
+            padded[k, 8 : 8 + height, :] = times(vorticity[1, k], here[k])
+            padded[k, 7:8, :] = pick_row(vort_low_y[0], n) * pick_row(low_y[...], n)
+            padded[k, 8 + height : 9 + height, :] = pick_row(vort_high_y[0], n) * pick_row(
+                high_y[...], n
+            )
+            total = (padded[k, 9 : 9 + height, :] - padded[k, 7 : 7 + height, :]) + (
+                deep[k + 2] - deep[k]
+            )
+            total = total * 0.5 + inner[k * height : (k + 1) * height] + ends[k]
+            after[c, k] = total * -step_size
+
+
+def write_grad_vel(components, slope_x, vorticity, adjoints, saved_halos, halos, before, after):
     _, _, height, width = vorticity.shape
+    count = len(components)
+    start = components[0] // count
     whole = lambda shape: pl.BlockSpec(shape, lambda n: (0,) * len(shape))
-    column = whole((Z, height))
-    row = whole((Z, width))
     saved_column = pl.BlockSpec((1, Z, height), lambda n: (3, 0, 0))
     saved_row = pl.BlockSpec((1, Z, width), lambda n: (3, 0, 0))
-    operands = [slope_x, vorticity, vorticity, vorticity, adjoint, *saved_halos, *halos]
+    layer_above = lambda n: lax.rem((n + 1) * LAYERS, Z)
+    layer_below = lambda n: lax.rem(n * LAYERS + Z - 1, Z)
+    operands = [slope_x, vorticity, vorticity, vorticity]
     in_specs = [
         whole((width, width)),
         pl.BlockSpec((3, LAYERS, height, width), lambda n: (0, n, 0, 0)),
-        pl.BlockSpec((1, 1, height, width), lambda n: (2, lax.rem((n + 1) * LAYERS, Z), 0, 0)),
-        pl.BlockSpec((1, 1, height, width), lambda n: (2, lax.rem(n * LAYERS + Z - 1, Z), 0, 0)),
-        whole((Z, height, width)),
-        saved_column,
-        saved_column,
-        saved_row,
-        saved_row,
-        column,
-        column,
-        row,
-        row,
+        pl.BlockSpec((1, 1, height, width), lambda n: (2, layer_above(n), 0, 0)),
+        pl.BlockSpec((1, 1, height, width), lambda n: (2, layer_below(n), 0, 0)),
     ]
+    for adjoint in adjoints:
+        operands = operands + [adjoint] * 3
+        in_specs = in_specs + [
+            pl.BlockSpec((LAYERS, height, width), lambda n: (n, 0, 0)),
+            pl.BlockSpec((1, height, width), lambda n: (layer_above(n), 0, 0)),
+            pl.BlockSpec((1, height, width), lambda n: (layer_below(n), 0, 0)),
+        ]
+    operands = operands + list(saved_halos)
+    in_specs = in_specs + [saved_column, saved_column, saved_row, saved_row]
+    for edge in halos:
+        operands = operands + list(edge)
+        in_specs = in_specs + [whole((Z, height))] * 2 + [whole((Z, width))] * 2
     aliases = {}
     if before is not None:
         aliases = {len(operands): 0}
         operands.append(before)
         in_specs.append(pl.BlockSpec(memory_space=pl.ANY))
+
+    def kernel(*refs):
+        grad_vel_kernel(count, *refs)
+
     return pl.pallas_call(
-        grad_vel_kernel,
+        kernel,
         grid=(Z // LAYERS,),
         in_specs=in_specs + tied(after),
-        out_specs=pl.BlockSpec((1, LAYERS, height, width), lambda n: (component, n, 0, 0)),
+        out_specs=pl.BlockSpec((count, LAYERS, height, width), lambda n: (start, n, 0, 0)),
         out_shape=jax.ShapeDtypeStruct((3, Z, height, width), f32),
         input_output_aliases=aliases,
         scratch_shapes=[pltpu.VMEM((LAYERS, height + 16, width), f32)],
         compiler_params=params(),
-        cost_estimate=takes(7),
+        cost_estimate=takes(6 * count),
         name="write_grad_vel",
     )(*operands, *after)
 
@@ -712,12 +726,10 @@
     slope_x = slope_matrix(width)
     slope_y = np.ascontiguousarray(slope_matrix(height).T)
 
-    layers = [depth_transform(cot_vel, FORWARD_ORDER[0])]
-    layers.append(depth_transform(cot_vel, FORWARD_ORDER[1], me, size_y, (layers[0],)))
-    layers.append(depth_transform(cot_vel, FORWARD_ORDER[2], me, size_y, (layers[1][0],)))
-
-    velocity_first, velocity_last = edge_columns(velocity, 3, (layers[0],))
-    vorticity_first, vorticity_last = edge_columns(vorticity, 1, (layers[0],))
+    layers = depth_transform(cot_vel, FORWARD_ORDER[0])
+
+    velocity_first, velocity_last = edge_columns(velocity, 3, (layers,))
+    vorticity_first, vorticity_last = edge_columns(vorticity, 1, (layers,))
     low_x, high_x = exchange(
         jnp.concatenate([velocity_first, vorticity_first]),
         jnp.concatenate([velocity_last, vorticity_last]),
@@ -731,30 +743,38 @@
     saved_halos = (low_x, high_x, low_y, high_y)
     edges = (velocity_first, vorticity_first)
 
+    columns = layers.reshape(size_y, planes, height, width)
+    columns = [lax.all_to_all(columns, "gy", 0, 0, tiled=True)]
     sent = []
     for place in range(3):
-        if place == 0:
-            columns = layers[0].reshape(size_y, planes, height, width)
-            columns = [lax.all_to_all(columns, "gy", 0, 0, tiled=True)]
-        else:
-            columns = shifted(layers[place], "gy")
+        if place > 0:
+            layers = depth_transform(cot_vel, FORWARD_ORDER[place], me, size_y, (sent[-1],))
+            columns = shifted(layers, "gy")
         parts = y_transform(me, y_table, columns, size_x, halves, edges if place == 0 else ())
         parts = parts.reshape(size_x, 2, 2, modes, width)
         sent.append(parts if halves == 1 else pair_exchange(parts, "gy", half))
-    spectra = {}
-    for place, component in enumerate(FORWARD_ORDER):
+
+    def spectrum(place, after):
         lines = lax.all_to_all(sent[place], "gx", 0, 0, tiled=True)
-        spectra[component] = x_transform(x_table, lines, saved_halos if place == 1 else ())
-
-    returned = {}
-    after = (sent[2],)
-    for component in BACK_ORDER:
-        parts = curl_inverse(where, x_back_table, spectra, component, size_x, after)
-        after = (parts,)
-        parts = lax.all_to_all(parts, "gx", 0, 0, tiled=True)
+        return x_transform(x_table, lines, after)
+
+    def curl(component, after):
+        return curl_inverse(where, x_back_table, spectra, component, size_x, after)
+
+    def back(filtered):
+        parts = lax.all_to_all(filtered, "gx", 0, 0, tiled=True)
         if halves == 2:
             parts = pair_exchange(parts, "gy", half)
-        returned[component] = parts.reshape(size_x, halves, planes, 2, modes, width)
+        return parts.reshape(size_x, halves, planes, 2, modes, width)
+
+    one, two, three = BACK_ORDER
+    spectra = {FORWARD_ORDER[0]: spectrum(0, (sent[1],))}
+    spectra[FORWARD_ORDER[1]] = spectrum(1, (sent[2],) + saved_halos)
+    curl_one = curl(one, ())
+    spectra[FORWARD_ORDER[2]] = spectrum(2, (curl_one,))
+    curl_two = curl(two, ())
+    curl_three = curl(three, (curl_two,))
+    returned = {one: back(curl_one), two: back(curl_two), three: back(curl_three)}
 
     def rows_of(component, after):
         split = component != BACK_ORDER[2]
@@ -775,24 +795,24 @@
             component, (slope_x, slope_y), velocity, adjoint, saved_halos, before, after
         )
 
-    def vel_of(component, adjoint, halos, before, after):
+    def vel_of(components, adjoints, halos, before, after):
         return write_grad_vel(
-            component, slope_x, vorticity, adjoint, saved_halos, halos, before, after
-        )
-
-    one, two, three = BACK_ORDER
-    rows_one = rows_of(one, ())
+            components, slope_x, vorticity, adjoints, saved_halos, halos, before, after
+        )
+
+    rows_one = rows_of(one, (curl_three,))
     adjoint_one, halos_one = adjoint_of(one, rows_one, ())
-    rows_two = rows_of(two, ())
+    rows_two = rows_of(two, (adjoint_one,))
     grad_vort = vort_of(one, adjoint_one, None, (rows_two[0],))
     adjoint_two, halos_two = adjoint_of(two, rows_two, (grad_vort,))
-    rows_three = rows_of(three, (adjoint_two,))
-    grad_vel = vel_of(one, adjoint_one, halos_one, None, (rows_three[0],))
+    rows_three = rows_of(three, (adjoint_two,) + halos_one)
+    grad_vel = vel_of((one,), [adjoint_one], [halos_one], None, (rows_three[0],))
     grad_vort = vort_of(two, adjoint_two, grad_vort, (grad_vel,))
-    grad_vel = vel_of(two, adjoint_two, halos_two, grad_vel, (grad_vort,))
-    adjoint_three, halos_three = adjoint_of(three, rows_three, (grad_vel,))
+    adjoint_three, halos_three = adjoint_of(three, rows_three, (grad_vort,))
     grad_vort = vort_of(three, adjoint_three, grad_vort, ())
-    grad_vel = vel_of(three, adjoint_three, halos_three, grad_vel, (grad_vort,))
+    grad_vel = vel_of(
+        (two, three), [adjoint_two, adjoint_three], [halos_two, halos_three], grad_vel, (grad_vort,)
+    )
     return grad_vort, grad_vel
 
 

time: 429 us -> 402 us (0.937)
  blocking collectives: 41.8 us -> 0 us
  starting transfers between devices: 90.4 us -> 110 us
    all_to_all x1 -> x0, blocking collectives: 41.8 us -> none  [local(): parts = lax.all_to_all(parts, 'gx', 0, 0, tiled=True)]
    all_to_all x1, waiting for transfers between devices: 0.01 us -> 13.9 us  [local(): columns = [lax.all_to_all(columns, 'gy', 0, 0, tiled=True)]]
    ppermute x16, waiting for transfers between devices: 28.6 us -> 17.7 us  [exchange(): return (lax.ppermute(last, axis, up), lax.ppermute(first, axis, down))]
    all_to_all x5 -> x6, starting transfers between devices: 20.7 us -> 30.8 us  [the longest x3 17.2 us: back(): parts = lax.all_to_all(filtered, 'gx', 0, 0, tiled=True)]
    ppermute x28, starting transfers between devices: 34.8 us -> 43.2 us  [shifted(): lax.ppermute(parts[s], axis, [(i, (i + s) % count) for i in range(count)])]
    pallas_call x3 -> x2, Pallas kernels: 22.3 us -> 18.4 us  [write_grad_vel(): pl.pallas_call(kernel, grid=(Z // LAYERS,), in_specs=in_specs + tied(afte...]
    unnamed x160 -> x154, local copies, waits for them, and re-layouts: 23.1 us -> 22.2 us
    all_to_all x5 -> x6, waiting for transfers between devices: 60.3 us -> 59.5 us  [the longest x3 51.3 us: back(): parts = lax.all_to_all(filtered, 'gx', 0, 0, tiled=True)]
  transfers between devices with their start and end apart: 51 -> 52, of which waited for: 22 -> 26; matrix products, arithmetic and copies ran while one was open for 1% -> 1% of each run, Pallas kernels for 25% -> 27%
where the time goes in v6:
time: 402 us; the launch traced here: 401 us
  Pallas kernels  137 us (34%)
  waiting for transfers between devices  128 us (32%)
  starting transfers between devices  110 us (27%)
  local copies, waits for them, and re-layouts  24.2 us (6%)
    all_to_all x3, waiting for transfers between devices, back(): parts = lax.all_to_all(filtered, 'gx', 0, 0, tiled=True)  51.3 us
    ppermute x28, starting transfers between devices, shifted(): lax.ppermute(parts[s], axis, [(i, (i + s) % count) for i in range(count)])  43.2 us
    ppermute x28, waiting for transfers between devices, shifted(): lax.ppermute(parts[s], axis, [(i, (i + s) % count) for i in range(count)])  36.6 us
    pallas_call x3, Pallas kernels, add_grad_vort(): pl.pallas_call(kernel, grid=(Z // LAYERS,), in_specs=in_specs + tied(afte...  26.7 us
    ppermute x16, starting transfers between devices, exchange(): return (lax.ppermute(last, axis, up), lax.ppermute(first, axis, down))  26 us
    unnamed x154, local copies, waits for them, and re-layouts  22.2 us
    pallas_call x3, Pallas kernels, y_inverse(): pl.pallas_call(kernel, in_specs=[pl.BlockSpec(memory_space=pltpu.SMEM), p...  21.8 us
    pallas_call x3, Pallas kernels, y_transform(): pl.pallas_call(kernel, in_specs=[pl.BlockSpec(memory_space=pltpu.SMEM), p...  21 us
  transfers between devices with their start and end apart: 52, of which 26 were waited for; matrix products, arithmetic and copies ran while one was open for 1% of the time, Pallas kernels for 27%

profile of v6, /device:TPU:0, one launch (start us, length us, event | category | flops | bytes accessed | tf_op | source)
XLA Modules:
  0.0 400.5 jit_solution(5857006629645621454)
XLA Ops:
  0.6 3.2 depth_transform.3.refs_0_
  3.8 5.2 %all-to-all-start = ((bf16[8,2,192,256]{3,2,1,0:T(8,128)(2,1)}), bf16[8,2,192,256]{3,2,1,0:T(8,128)(2,1)S(1)}, u32[]{:S(2)}, u32[]{:S(2)}) async-start(bf16[8,2,192,256]{3,2,1,0:T(8,128)(2,1)} %bitcast.27), calls=%async_computation | async-start | bytes 3145728 | tf_op jit(solution)/shard_map/all_to_all | solution.py:747
  11.5 4.6 %edge_columns.2 = (bf16[3,16,192]{2,1,0:T(8,128)(2,1)}, bf16[3,16,192]{2,1,0:T(8,128)(2,1)}) custom-call(bf16[3,16,192,256]{3,2,1,0:T(8,128)(2,1)} %refs_2_.8, bf16[16,192,256]{2,1,0:T(8,128)(2,1)} %depth_transform.3.refs_0_), custom_call_target="tpu_custom_call" | custom-call | flops 1 | bytes 12000000 | tf_op jit(solution)/shard_map/edge_columns/pallas_call | solution.py:424
  16.1 13.9 %all-to-all-done.refs_0_ = bf16[8,2,192,256]{3,2,1,0:T(8,128)(2,1)S(1)} async-done(((bf16[8,2,192,256]{3,2,1,0:T(8,128)(2,1)}), bf16[8,2,192,256]{3,2,1,0:T(8,128)(2,1)S(1)}, u32[]{:S(2)}, u32[]{:S(2)}) %all-to-all-start) | async-done | bytes 1572896 | tf_op jit(solution)/shard_map/all_to_all | solution.py:747
  31.1 7.0 %y_transform.3 = bf16[4,1,2,2,192,256]{5,4,3,2,1,0:T(8,128)(2,1)} custom-call(s32[1]{0:T(128)} %bitcast.me_ref.refs_0_, bf16[1536,1536]{1,0:T(8,128)(2,1)} %constant.33.clone.table_ref, bf16[8,2,192,256]{3,2,1,0:T(8,128)(2,1)} %copy-done.22, bf16[3,16,192]{2,1,0:T(8,128)(2,1)} %get-tuple-element.53.refs_1_, bf16[1,16,192]{2,1,0:T(8,128)(2,1)} %get-tuple-element.54.refs_2_), custom_call_target="tpu_custom_call" | custom-call | flops 1 | bytes 15000000 | tf_op jit(solution)/shard_map/y_transform/pallas_call | solution.py:212
  38.1 4.9 %all-to-all-start.1 = ((bf16[4,2,2,192,256]{4,3,2,1,0:T(8,128)(2,1)}), bf16[4,2,2,192,256]{4,3,2,1,0:T(8,128)(2,1)S(1)}, u32[]{:S(2)}, u32[]{:S(2)}) async-start(bf16[4,2,2,192,256]{4,3,2,1,0:T(8,128)(2,1)} %bitcast.28), calls=%async_computation.1 | async-start | bytes 3145728 | tf_op jit(solution)/shard_map/all_to_all | solution.py:758
  43.0 3.3 depth_transform.4
  49.7 4.4 %collective-permute-done.refs_1_ = bf16[2,192,256]{2,1,0:T(8,128)(2,1)S(1)} collective-permute-done((bf16[2,192,256]{2,1,0:T(8,128)(2,1)}, bf16[2,192,256]{2,1,0:T(8,128)(2,1)S(1)}, u32[]{:S(2)}, u32[]{:S(2)}) %collective-permute-start) | collective-permute-done | bytes 196640 | tf_op jit(solution)/shard_map/ppermute | solution.py:706
  57.6 5.3 %collective-permute-done.2.refs_3_ = bf16[2,192,256]{2,1,0:T(8,128)(2,1)S(1)} collective-permute-done((bf16[2,192,256]{2,1,0:T(8,128)(2,1)}, bf16[2,192,256]{2,1,0:T(8,128)(2,1)S(1)}, u32[]{:S(2)}, u32[]{:S(2)}) %collective-permute-start.2) | collective-permute-done | bytes 196640 | tf_op jit(solution)/shard_map/ppermute | solution.py:706
  66.2 7.0 %y_transform.4 = bf16[4,1,2,2,192,256]{5,4,3,2,1,0:T(8,128)(2,1)} custom-call(s32[1]{0:T(128)} %bitcast.me_ref.refs_0_, bf16[1536,1536]{1,0:T(8,128)(2,1)} %constant.33.clone.table_ref, bf16[2,192,256]{2,1,0:T(8,128)(2,1)} %get-tuple-element.55.refs_0_, bf16[2,192,256]{2,1,0:T(8,128)(2,1)} %copy-done.33, bf16[2,192,256]{2,1,0:T(8,128)(2,1)} %copy-done.36, ...), custom_call_target="tpu_custom_call" | custom-call | flops 1 | bytes 15000000 | tf_op jit(solution)/shard_map/y_transform/pallas_call | solution.py:212
  73.3 3.9 all-to-all-done.1.modes_ref
  77.2 4.3 %all-to-all-start.3 = ((bf16[4,2,2,192,256]{4,3,2,1,0:T(8,128)(2,1)}), bf16[4,2,2,192,256]{4,3,2,1,0:T(8,128)(2,1)}, u32[]{:S(2)}, u32[]{:S(2)}) async-start(bf16[4,2,2,192,256]{4,3,2,1,0:T(8,128)(2,1)} %bitcast.22), calls=%async_computation.3 | async-start | bytes 3145728 | tf_op jit(solution)/shard_map/all_to_all | solution.py:758
  81.5 3.3 depth_transform.5
  84.8 3.6 collective-permute-start.8
  95.0 4.0 %collective-permute-start.13 = (bf16[2,192,256]{2,1,0:T(8,128)(2,1)}, bf16[2,192,256]{2,1,0:T(8,128)(2,1)S(1)}, u32[]{:S(2)}, u32[]{:S(2)}) collective-permute-start(bf16[2,192,256]{2,1,0:T(8,128)(2,1)} %get-tuple-element.70), channel_id=1, source_target_pairs={{0,7},{1,0},{2,1},{3,2},{4,3},{5,4},{6,5},{7,6},{8,15},{9,8},{10,9... | collective-permute-start | bytes 589832 | tf_op jit(solution)/shard_map/ppermute | solution.py:706
  101.7 3.1 collective-permute-done.11.refs_5_
  106.7 7.0 %y_transform.5 = bf16[4,1,2,2,192,256]{5,4,3,2,1,0:T(8,128)(2,1)} custom-call(s32[1]{0:T(128)} %bitcast.me_ref.refs_0_, bf16[1536,1536]{1,0:T(8,128)(2,1)} %constant.33.clone.table_ref, bf16[2,192,256]{2,1,0:T(8,128)(2,1)} %get-tuple-element.63.refs_0_, bf16[2,192,256]{2,1,0:T(8,128)(2,1)} %copy-done.32, bf16[2,192,256]{2,1,0:T(8,128)(2,1)} %copy-done.35, ...), custom_call_target="tpu_custom_call" | custom-call | flops 1 | bytes 15000000 | tf_op jit(solution)/shard_map/y_transform/pallas_call | solution.py:212
  113.8 4.2 %all-to-all-done.3.modes_ref = bf16[4,2,2,192,256]{4,3,2,1,0:T(8,128)(2,1)} async-done(((bf16[4,2,2,192,256]{4,3,2,1,0:T(8,128)(2,1)}), bf16[4,2,2,192,256]{4,3,2,1,0:T(8,128)(2,1)}, u32[]{:S(2)}, u32[]{:S(2)}) %all-to-all-start.3) | async-done | bytes 1572896 | tf_op jit(solution)/shard_map/all_to_all | solution.py:758
  118.0 4.3 %all-to-all-start.2 = ((bf16[4,2,2,192,256]{4,3,2,1,0:T(8,128)(2,1)}), bf16[4,2,2,192,256]{4,3,2,1,0:T(8,128)(2,1)}, u32[]{:S(2)}, u32[]{:S(2)}) async-start(bf16[4,2,2,192,256]{4,3,2,1,0:T(8,128)(2,1)} %bitcast.25), calls=%async_computation.2 | async-start | bytes 3145728 | tf_op jit(solution)/shard_map/all_to_all | solution.py:758
  127.2 3.8 collective-permute-start.15
  135.1 13.2 %collective-permute-done.15.refs_2_.refs_5_.refs_8_.refs_11_ = bf16[4,16,192]{2,1,0:T(8,128)(2,1)S(1)} collective-permute-done((bf16[4,16,192]{2,1,0:T(8,128)(2,1)S(1)}, bf16[4,16,192]{2,1,0:T(8,128)(2,1)S(1)}, u32[]{:S(2)}, u32[]{:S(2)}) %collective-permute-start.15) | collective-permute-done | bytes 24608 | tf_op jit(solution)/shard_map/ppermute | solution.py:440
  148.4 4.4 %collective-permute-done.14.refs_1_.refs_4_.refs_7_.refs_10_ = bf16[4,16,192]{2,1,0:T(8,128)(2,1)S(1)} collective-permute-done((bf16[4,16,192]{2,1,0:T(8,128)(2,1)S(1)}, bf16[4,16,192]{2,1,0:T(8,128)(2,1)S(1)}, u32[]{:S(2)}, u32[]{:S(2)}) %collective-permute-start.14) | collective-permute-done | bytes 24608 | tf_op jit(solution)/shard_map/ppermute | solution.py:440
  152.8 3.1 x_transform.4.refs_2_.refs_3_
  160.1 9.3 %all-to-all-start.6 = ((bf16[4,2,2,192,256]{4,3,2,1,0:T(8,128)(2,1)}), bf16[4,2,2,192,256]{4,3,2,1,0:T(8,128)(2,1)}, u32[]{:S(2)}, u32[]{:S(2)}) async-start(bf16[4,2,2,192,256]{4,3,2,1,0:T(8,128)(2,1)} %copy-done.10), calls=%async_computation.6 | async-start | bytes 3145728 | tf_op jit(solution)/shard_map/all_to_all | solution.py:765
  172.4 3.3 x_transform.5.refs_2_.refs_3_
  181.6 23.8 %all-to-all-done.6 = bf16[4,2,2,192,256]{4,3,2,1,0:T(8,128)(2,1)} async-done(((bf16[4,2,2,192,256]{4,3,2,1,0:T(8,128)(2,1)}), bf16[4,2,2,192,256]{4,3,2,1,0:T(8,128)(2,1)}, u32[]{:S(2)}, u32[]{:S(2)}) %all-to-all-start.6) | async-done | bytes 1572896 | tf_op jit(solution)/shard_map/all_to_all | solution.py:765
  205.4 4.4 %all-to-all-start.5 = ((bf16[4,2,2,192,256]{4,3,2,1,0:T(8,128)(2,1)}), bf16[4,2,2,192,256]{4,3,2,1,0:T(8,128)(2,1)}, u32[]{:S(2)}, u32[]{:S(2)}) async-start(bf16[4,2,2,192,256]{4,3,2,1,0:T(8,128)(2,1)} %copy-done.13), calls=%async_computation.5 | async-start | bytes 3145728 | tf_op jit(solution)/shard_map/all_to_all | solution.py:765
  218.8 27.5 %all-to-all-done.5 = bf16[4,2,2,192,256]{4,3,2,1,0:T(8,128)(2,1)} async-done(((bf16[4,2,2,192,256]{4,3,2,1,0:T(8,128)(2,1)}), bf16[4,2,2,192,256]{4,3,2,1,0:T(8,128)(2,1)}, u32[]{:S(2)}, u32[]{:S(2)}) %all-to-all-start.5) | async-done | bytes 1572896 | tf_op jit(solution)/shard_map/all_to_all | solution.py:765
  246.3 3.6 all-to-all-start.4
  249.9 7.1 %y_inverse.3 = (bf16[2,192,256]{2,1,0:T(8,128)(2,1)}, bf16[2,192,256]{2,1,0:T(8,128)(2,1)}, bf16[2,192,256]{2,1,0:T(8,128)(2,1)}, bf16[2,192,256]{2,1,0:T(8,128)...) custom-call(s32[1]{0:T(128)} %bitcast.me_ref.refs_0_, ...), custom_call_target="tpu_custom_call" | custom-call | flops 1 | bytes 12000000 | tf_op jit(solution)/shard_map/y_inverse/pallas_call | solution.py:255
  257.0 3.6 collective-permute-start.19
  267.2 3.9 collective-permute-start.24
  279.0 5.0 %make_adjoint.3 = (f32[16,192,256]{2,1,0:T(8,128)}, bf16[16,192]{1,0:T(8,128)(2,1)}, bf16[16,192]{1,0:T(8,128)(2,1)}, bf16[16,256]{1,0:T(8,128)(2,1)}, bf16[16,256]{1,0:T(8,128)(2,1)}) custom-call(s32[1]{0:T(128)} %bitcast.me_ref.refs_0_, bf16[2,192,256]{2,1,0:T(8,128)(2,1)} %get-tuple-element.73.refs_0_, bf16[2,192,256]{2,1,0:T(8,128)(2,1)} %copy-done.30, ...), custom_call_target="tpu_custom_call" | custom-call | flops 1 | bytes 15000000 | tf_op jit(solution)/shard_map/make_adjoint/pallas_call | solution.py:489
  284.0 7.1 %y_inverse.4 = (bf16[2,192,256]{2,1,0:T(8,128)(2,1)}, bf16[2,192,256]{2,1,0:T(8,128)(2,1)}, bf16[2,192,256]{2,1,0:T(8,128)(2,1)}, bf16[2,192,256]{2,1,0:T(8,128)...) custom-call(s32[1]{0:T(128)} %bitcast.me_ref.refs_0_, ...), custom_call_target="tpu_custom_call" | custom-call | flops 1 | bytes 12000000 | tf_op jit(solution)/shard_map/y_inverse/pallas_call | solution.py:255
  291.2 3.5 collective-permute-start.26
  300.4 3.9 collective-permute-start.31
  304.4 3.5 collective-permute-done.27.refs_3_
  316.0 7.3 %add_grad_vort.3.refs_9_.refs_8_ = f32[3,16,192,256]{3,2,1,0:T(8,128)} custom-call(bf16[256,256]{1,0:T(8,128)(2,1)} %constant.37.clone.refs_0_, bf16[192,192]{1,0:T(8,128)(2,1)} %constant.38.clone.refs_1_, bf16[3,16,192,256]{3,2,1,0:T(8,128)(2,1)} %refs_2_.8, f32[16,192,256]{2,1,0:T(8,128)} %get-tuple-element.81.refs_0_.refs_3_.refs_4_.refs_5_.refs_6_, ...), custom_call_target="tpu_custom_call" | custom-call | flops 1 | bytes 27000000 | tf_op jit(solution)/shard_map/add_grad_vort/pallas_call | solution.py:590
  324.1 5.0 %make_adjoint.4 = (f32[16,192,256]{2,1,0:T(8,128)}, bf16[16,192]{1,0:T(8,128)(2,1)}, bf16[16,192]{1,0:T(8,128)(2,1)}, bf16[16,256]{1,0:T(8,128)(2,1)}, bf16[16,256]{1,0:T(8,128)(2,1)}) custom-call(s32[1]{0:T(128)} %bitcast.me_ref.refs_0_, bf16[2,192,256]{2,1,0:T(8,128)(2,1)} %get-tuple-element.82.refs_8_.refs_0_, bf16[2,192,256]{2,1,0:T(8,128)(2,1)} %copy-done.23, ...), custom_call_target="tpu_custom_call" | custom-call | flops 1 | bytes 15000000 | tf_op jit(solution)/shard_map/make_adjoint/pallas_call | solution.py:489
  330.2 7.6 %y_inverse.5.refs_15_ = bf16[8,2,192,256]{3,2,1,0:T(8,128)(2,1)} custom-call(s32[1]{0:T(128)} %bitcast.me_ref.refs_0_, bf16[1536,1536]{1,0:T(8,128)(2,1)} %constant.36.clone.table_ref, bf16[4,1,2,2,192,256]{5,4,3,2,1,0:T(8,128)(2,1)} %bitcast.31, f32[16,192,256]{2,1,0:T(8,128)} %get-tuple-element.90.refs_0_.refs_3_.refs_4_.refs_5_.refs_6_, ...), custom_call_target="tpu_custom_call" | custom-call | flops 1 | bytes 12000000 | tf_op jit(solution)/shard_map/y_inverse/pallas_call | solution.py:255
  337.9 4.7 %all-to-all-start.7 = ((bf16[8,2,192,256]{3,2,1,0:T(8,128)(2,1)}), bf16[8,2,192,256]{3,2,1,0:T(8,128)(2,1)S(1)}, u32[]{:S(2)}, u32[]{:S(2)}) async-start(bf16[8,2,192,256]{3,2,1,0:T(8,128)(2,1)} %y_inverse.5.refs_15_), calls=%async_computation.7 | async-start | bytes 3145728 | tf_op jit(solution)/shard_map/all_to_all | solution.py:785
  343.1 3.8 collective-permute-start.37
  346.9 7.5 %write_grad_vel.2.refs_9_.refs_22_ = f32[3,16,192,256]{3,2,1,0:T(8,128)} custom-call(bf16[256,256]{1,0:T(8,128)(2,1)} %constant.37.clone.refs_0_, bf16[3,16,192,256]{3,2,1,0:T(8,128)(2,1)} %refs_3_.3, bf16[3,16,192,256]{3,2,1,0:T(8,128)(2,1)} %refs_3_.3, bf16[3,16,192,256]{3,2,1,0:T(8,128)(2,1)} %refs_3_.3, ...), custom_call_target="tpu_custom_call" | custom-call | flops 1 | bytes 18000000 | tf_op jit(solution)/shard_map/write_grad_vel/pallas_call | solution.py:681
  356.1 9.7 %add_grad_vort.4.refs_2_.refs_8_ = f32[3,16,192,256]{3,2,1,0:T(8,128)} custom-call(bf16[256,256]{1,0:T(8,128)(2,1)} %constant.37.clone.refs_0_, bf16[192,192]{1,0:T(8,128)(2,1)} %constant.38.clone.refs_1_, bf16[3,16,192,256]{3,2,1,0:T(8,128)(2,1)} %refs_2_.8, ...), custom_call_target="tpu_custom_call", output_to_operand_aliasing={{}: (8, {})} | custom-call | flops 1 | bytes 27000000 | tf_op jit(solution)/shard_map/add_grad_vort/pallas_call | solution.py:590
  367.1 4.8 %make_adjoint.5 = (f32[16,192,256]{2,1,0:T(8,128)}, bf16[16,192]{1,0:T(8,128)(2,1)}, bf16[16,192]{1,0:T(8,128)(2,1)}, bf16[16,256]{1,0:T(8,128)(2,1)}, bf16[16,256]{1,0:T(8,128)(2,1)}) custom-call(s32[1]{0:T(128)} %bitcast.me_ref.refs_0_, bf16[16,192,256]{2,1,0:T(8,128)(2,1)} %bitcast.30, f32[3,16,192,256]{3,2,1,0:T(8,128)} %refs_1_.14, ...), custom_call_target="tpu_custom_call" | custom-call | flops 1 | bytes 15000000 | tf_op jit(solution)/shard_map/make_adjoint/pallas_call | solution.py:489
  374.6 3.8 collective-permute-start.41
  378.4 9.7 %add_grad_vort.5.refs_23_ = f32[3,16,192,256]{3,2,1,0:T(8,128)} custom-call(bf16[256,256]{1,0:T(8,128)(2,1)} %constant.37.clone.refs_0_, bf16[192,192]{1,0:T(8,128)(2,1)} %constant.38.clone.refs_1_, bf16[3,16,192,256]{3,2,1,0:T(8,128)(2,1)} %refs_2_.8, ...), custom_call_target="tpu_custom_call", output_to_operand_aliasing={{}: (8, {})} | custom-call | flops 1 | bytes 27000000 | tf_op jit(solution)/shard_map/add_grad_vort/pallas_call | solution.py:590
  389.4 11.0 %write_grad_vel.3 = f32[3,16,192,256]{3,2,1,0:T(8,128)} custom-call(bf16[256,256]{1,0:T(8,128)(2,1)} %constant.37.clone.refs_0_, bf16[3,16,192,256]{3,2,1,0:T(8,128)(2,1)} %refs_3_.3, bf16[3,16,192,256]{3,2,1,0:T(8,128)(2,1)} %refs_3_.3, bf16[3,16,192,256]{3,2,1,0:T(8,128)(2,1)} %refs_3_.3, ...), custom_call_target="tpu_custom_call", output_to_operand_aliasing={{}: (22, {})} | custom-call | flops 1 | bytes 36000000 | tf_op jit(solution)/shard_map/write_grad_vel/pallas_call | solution.py:681
  (242 shorter events, 93.4 us)
Async XLA Ops:
  3.8 26.2 %all-to-all-start = ((bf16[8,2,192,256]{3,2,1,0:T(8,128)(2,1)}), bf16[8,2,192,256]{3,2,1,0:T(8,128)(2,1)S(1)}, u32[]{:S(2)}, u32[]{:S(2)}) async-start(bf16[8,2,192,256]{3,2,1,0:T(8,128)(2,1)} %bitcast.27), calls=%async_computation | async-start | bytes 3145728 | tf_op jit(solution)/shard_map/all_to_all | solution.py:747
  38.1 39.1 %all-to-all-start.1 = ((bf16[4,2,2,192,256]{4,3,2,1,0:T(8,128)(2,1)}), bf16[4,2,2,192,256]{4,3,2,1,0:T(8,128)(2,1)S(1)}, u32[]{:S(2)}, u32[]{:S(2)}) async-start(bf16[4,2,2,192,256]{4,3,2,1,0:T(8,128)(2,1)} %bitcast.28), calls=%async_computation.1 | async-start | bytes 3145728 | tf_op jit(solution)/shard_map/all_to_all | solution.py:758
  46.3 9.0 %collective-permute-start.1 = (bf16[2,192,256]{2,1,0:T(8,128)(2,1)}, bf16[2,192,256]{2,1,0:T(8,128)(2,1)S(1)}, u32[]{:S(2)}, u32[]{:S(2)}) collective-permute-start(bf16[2,192,256]{2,1,0:T(8,128)(2,1)} %get-tuple-element.57), channel_id=1, source_target_pairs={{0,2},{1,3},{2,4},{3,5},{4,6},{5,7},{6,0},{7,1},{8,10},{9,11},{10,... | collective-permute-start | bytes 589832 | tf_op jit(solution)/shard_map/ppermute | solution.py:706
  46.8 16.1 %collective-permute-start.2 = (bf16[2,192,256]{2,1,0:T(8,128)(2,1)}, bf16[2,192,256]{2,1,0:T(8,128)(2,1)S(1)}, u32[]{:S(2)}, u32[]{:S(2)}) collective-permute-start(bf16[2,192,256]{2,1,0:T(8,128)(2,1)} %get-tuple-element.58), channel_id=1, source_target_pairs={{0,3},{1,4},{2,5},{3,6},{4,7},{5,0},{6,1},{7,2},{8,11},{9,12},{10,... | collective-permute-start | bytes 589832 | tf_op jit(solution)/shard_map/ppermute | solution.py:706
  48.3 14.8 %collective-permute-start.3 = (bf16[2,192,256]{2,1,0:T(8,128)(2,1)}, bf16[2,192,256]{2,1,0:T(8,128)(2,1)S(1)}, u32[]{:S(2)}, u32[]{:S(2)}) collective-permute-start(bf16[2,192,256]{2,1,0:T(8,128)(2,1)} %get-tuple-element.59), channel_id=1, source_target_pairs={{0,4},{1,5},{2,6},{3,7},{4,0},{5,1},{6,2},{7,3},{8,12},{9,13},{10,... | collective-permute-start | bytes 589832 | tf_op jit(solution)/shard_map/ppermute | solution.py:706
  49.7 15.7 %collective-permute-start.4 = (bf16[2,192,256]{2,1,0:T(8,128)(2,1)}, bf16[2,192,256]{2,1,0:T(8,128)(2,1)S(1)}, u32[]{:S(2)}, u32[]{:S(2)}) collective-permute-start(bf16[2,192,256]{2,1,0:T(8,128)(2,1)} %get-tuple-element.60), channel_id=1, source_target_pairs={{0,5},{1,6},{2,7},{3,0},{4,1},{5,2},{6,3},{7,4},{8,13},{9,14},{10,... | collective-permute-start | bytes 589832 | tf_op jit(solution)/shard_map/ppermute | solution.py:706
  54.1 11.3 %collective-permute-start.5 = (bf16[2,192,256]{2,1,0:T(8,128)(2,1)}, bf16[2,192,256]{2,1,0:T(8,128)(2,1)S(1)}, u32[]{:S(2)}, u32[]{:S(2)}) collective-permute-start(bf16[2,192,256]{2,1,0:T(8,128)(2,1)} %get-tuple-element.61), channel_id=1, source_target_pairs={{0,6},{1,7},{2,0},{3,1},{4,2},{5,3},{6,4},{7,5},{8,14},{9,15},{10,... | collective-permute-start | bytes 589832 | tf_op jit(solution)/shard_map/ppermute | solution.py:706
  55.3 10.2 %collective-permute-start.6 = (bf16[2,192,256]{2,1,0:T(8,128)(2,1)}, bf16[2,192,256]{2,1,0:T(8,128)(2,1)S(1)}, u32[]{:S(2)}, u32[]{:S(2)}) collective-permute-start(bf16[2,192,256]{2,1,0:T(8,128)(2,1)} %get-tuple-element.62), channel_id=1, source_target_pairs={{0,7},{1,0},{2,1},{3,2},{4,3},{5,4},{6,5},{7,6},{8,15},{9,8},{10,9... | collective-permute-start | bytes 589832 | tf_op jit(solution)/shard_map/ppermute | solution.py:706
  77.2 40.9 %all-to-all-start.3 = ((bf16[4,2,2,192,256]{4,3,2,1,0:T(8,128)(2,1)}), bf16[4,2,2,192,256]{4,3,2,1,0:T(8,128)(2,1)}, u32[]{:S(2)}, u32[]{:S(2)}) async-start(bf16[4,2,2,192,256]{4,3,2,1,0:T(8,128)(2,1)} %bitcast.22), calls=%async_computation.3 | async-start | bytes 3145728 | tf_op jit(solution)/shard_map/all_to_all | solution.py:758
  84.8 10.2 %collective-permute-start.8 = (bf16[2,192,256]{2,1,0:T(8,128)(2,1)}, bf16[2,192,256]{2,1,0:T(8,128)(2,1)S(1)}, u32[]{:S(2)}, u32[]{:S(2)}) collective-permute-start(bf16[2,192,256]{2,1,0:T(8,128)(2,1)} %get-tuple-element.65), channel_id=1, source_target_pairs={{0,2},{1,3},{2,4},{3,5},{4,6},{5,7},{6,0},{7,1},{8,10},{9,11},{10,... | collective-permute-start | bytes 589832 | tf_op jit(solution)/shard_map/ppermute | solution.py:706
  88.4 13.1 %collective-permute-start.9 = (bf16[2,192,256]{2,1,0:T(8,128)(2,1)}, bf16[2,192,256]{2,1,0:T(8,128)(2,1)S(1)}, u32[]{:S(2)}, u32[]{:S(2)}) collective-permute-start(bf16[2,192,256]{2,1,0:T(8,128)(2,1)} %get-tuple-element.66), channel_id=1, source_target_pairs={{0,3},{1,4},{2,5},{3,6},{4,7},{5,0},{6,1},{7,2},{8,11},{9,12},{10,... | collective-permute-start | bytes 589832 | tf_op jit(solution)/shard_map/ppermute | solution.py:706
  89.6 12.0 %collective-permute-start.10 = (bf16[2,192,256]{2,1,0:T(8,128)(2,1)}, bf16[2,192,256]{2,1,0:T(8,128)(2,1)S(1)}, u32[]{:S(2)}, u32[]{:S(2)}) collective-permute-start(bf16[2,192,256]{2,1,0:T(8,128)(2,1)} %get-tuple-element.67), channel_id=1, source_target_pairs={{0,4},{1,5},{2,6},{3,7},{4,0},{5,1},{6,2},{7,3},{8,12},{9,13},{10,... | collective-permute-start | bytes 589832 | tf_op jit(solution)/shard_map/ppermute | solution.py:706
  91.3 13.5 %collective-permute-start.11 = (bf16[2,192,256]{2,1,0:T(8,128)(2,1)}, bf16[2,192,256]{2,1,0:T(8,128)(2,1)S(1)}, u32[]{:S(2)}, u32[]{:S(2)}) collective-permute-start(bf16[2,192,256]{2,1,0:T(8,128)(2,1)} %get-tuple-element.68), channel_id=1, source_target_pairs={{0,5},{1,6},{2,7},{3,0},{4,1},{5,2},{6,3},{7,4},{8,13},{9,14},{10,... | collective-permute-start | bytes 589832 | tf_op jit(solution)/shard_map/ppermute | solution.py:706
  92.1 12.6 %collective-permute-start.12 = (bf16[2,192,256]{2,1,0:T(8,128)(2,1)}, bf16[2,192,256]{2,1,0:T(8,128)(2,1)S(1)}, u32[]{:S(2)}, u32[]{:S(2)}) collective-permute-start(bf16[2,192,256]{2,1,0:T(8,128)(2,1)} %get-tuple-element.69), channel_id=1, source_target_pairs={{0,6},{1,7},{2,0},{3,1},{4,2},{5,3},{6,4},{7,5},{8,14},{9,15},{10,... | collective-permute-start | bytes 589832 | tf_op jit(solution)/shard_map/ppermute | solution.py:706
  95.0 11.1 %collective-permute-start.13 = (bf16[2,192,256]{2,1,0:T(8,128)(2,1)}, bf16[2,192,256]{2,1,0:T(8,128)(2,1)S(1)}, u32[]{:S(2)}, u32[]{:S(2)}) collective-permute-start(bf16[2,192,256]{2,1,0:T(8,128)(2,1)} %get-tuple-element.70), channel_id=1, source_target_pairs={{0,7},{1,0},{2,1},{3,2},{4,3},{5,4},{6,5},{7,6},{8,15},{9,8},{10,9... | collective-permute-start | bytes 589832 | tf_op jit(solution)/shard_map/ppermute | solution.py:706
  118.0 42.1 %all-to-all-start.2 = ((bf16[4,2,2,192,256]{4,3,2,1,0:T(8,128)(2,1)}), bf16[4,2,2,192,256]{4,3,2,1,0:T(8,128)(2,1)}, u32[]{:S(2)}, u32[]{:S(2)}) async-start(bf16[4,2,2,192,256]{4,3,2,1,0:T(8,128)(2,1)} %bitcast.25), calls=%async_computation.2 | async-start | bytes 3145728 | tf_op jit(solution)/shard_map/all_to_all | solution.py:758
  124.4 28.3 %collective-permute-start.16 = (bf16[4,16,256]{2,1,0:T(8,128)(2,1)S(1)}, bf16[4,16,256]{2,1,0:T(8,128)(2,1)S(1)}, u32[]{:S(2)}, u32[]{:S(2)}) collective-permute-start(bf16[4,16,256]{2,1,0:T(8,128)(2,1)S(1)} %pad_maximum_fusion.2), channel_id=1, source_target_pairs={{0,1},{1,2},{2,3},{3,4},{4,5},{5,6},{6,7},{7,0},{8,9},{9,10},{10,1... | collective-permute-start | bytes 98312 | tf_op jit(solution)/shard_map/ppermute | solution.py:440
  124.6 28.2 %collective-permute-start.17 = (bf16[4,16,256]{2,1,0:T(8,128)(2,1)S(1)}, bf16[4,16,256]{2,1,0:T(8,128)(2,1)S(1)}, u32[]{:S(2)}, u32[]{:S(2)}) collective-permute-start(bf16[4,16,256]{2,1,0:T(8,128)(2,1)S(1)} %pad_maximum_fusion.3), channel_id=1, source_target_pairs={{1,0},{2,1},{3,2},{4,3},{5,4},{6,5},{7,6},{0,7},{9,8},{10,9},{11,1... | collective-permute-start | bytes 98312 | tf_op jit(solution)/shard_map/ppermute | solution.py:440
  127.2 21.1 %collective-permute-start.15 = (bf16[4,16,192]{2,1,0:T(8,128)(2,1)S(1)}, bf16[4,16,192]{2,1,0:T(8,128)(2,1)S(1)}, u32[]{:S(2)}, u32[]{:S(2)}) collective-permute-start(bf16[4,16,192]{2,1,0:T(8,128)(2,1)S(1)} %pad_maximum_fusion.1), channel_id=1, source_target_pairs={{8,0},{16,8},{24,16},{0,24},{9,1},{17,9},{25,17},{1,25},{10,2},{18... | collective-permute-start | bytes 73736 | tf_op jit(solution)/shard_map/ppermute | solution.py:440
  131.1 21.7 %collective-permute-start.14 = (bf16[4,16,192]{2,1,0:T(8,128)(2,1)S(1)}, bf16[4,16,192]{2,1,0:T(8,128)(2,1)S(1)}, u32[]{:S(2)}, u32[]{:S(2)}) collective-permute-start(bf16[4,16,192]{2,1,0:T(8,128)(2,1)S(1)} %pad_maximum_fusion), channel_id=1, source_target_pairs={{0,8},{8,16},{16,24},{24,0},{1,9},{9,17},{17,25},{25,1},{2,10},{10... | collective-permute-start | bytes 73736 | tf_op jit(solution)/shard_map/ppermute | solution.py:440
  160.1 45.3 %all-to-all-start.6 = ((bf16[4,2,2,192,256]{4,3,2,1,0:T(8,128)(2,1)}), bf16[4,2,2,192,256]{4,3,2,1,0:T(8,128)(2,1)}, u32[]{:S(2)}, u32[]{:S(2)}) async-start(bf16[4,2,2,192,256]{4,3,2,1,0:T(8,128)(2,1)} %copy-done.10), calls=%async_computation.6 | async-start | bytes 3145728 | tf_op jit(solution)/shard_map/all_to_all | solution.py:765
  205.4 40.9 %all-to-all-start.5 = ((bf16[4,2,2,192,256]{4,3,2,1,0:T(8,128)(2,1)}), bf16[4,2,2,192,256]{4,3,2,1,0:T(8,128)(2,1)}, u32[]{:S(2)}, u32[]{:S(2)}) async-start(bf16[4,2,2,192,256]{4,3,2,1,0:T(8,128)(2,1)} %copy-done.13), calls=%async_computation.5 | async-start | bytes 3145728 | tf_op jit(solution)/shard_map/all_to_all | solution.py:765
  246.3 82.7 %all-to-all-start.4 = ((bf16[4,2,2,192,256]{4,3,2,1,0:T(8,128)(2,1)}), bf16[4,2,2,192,256]{4,3,2,1,0:T(8,128)(2,1)S(1)}, u32[]{:S(2)}, u32[]{:S(2)}) async-start(bf16[4,2,2,192,256]{4,3,2,1,0:T(8,128)(2,1)} %copy-done.15), calls=%async_computation.4 | async-start | bytes 3145728 | tf_op jit(solution)/shard_map/all_to_all | solution.py:765
  257.0 10.1 %collective-permute-start.19 = (bf16[2,192,256]{2,1,0:T(8,128)(2,1)}, bf16[2,192,256]{2,1,0:T(8,128)(2,1)S(1)}, u32[]{:S(2)}, u32[]{:S(2)}) collective-permute-start(bf16[2,192,256]{2,1,0:T(8,128)(2,1)} %get-tuple-element.75), channel_id=1, source_target_pairs={{0,2},{1,3},{2,4},{3,5},{4,6},{5,7},{6,0},{7,1},{8,10},{9,11},{10,... | collective-permute-start | bytes 589832 | tf_op jit(solution)/shard_map/ppermute | solution.py:706
  260.6 13.0 %collective-permute-start.20 = (bf16[2,192,256]{2,1,0:T(8,128)(2,1)}, bf16[2,192,256]{2,1,0:T(8,128)(2,1)S(1)}, u32[]{:S(2)}, u32[]{:S(2)}) collective-permute-start(bf16[2,192,256]{2,1,0:T(8,128)(2,1)} %get-tuple-element.76), channel_id=1, source_target_pairs={{0,3},{1,4},{2,5},{3,6},{4,7},{5,0},{6,1},{7,2},{8,11},{9,12},{10,... | collective-permute-start | bytes 589832 | tf_op jit(solution)/shard_map/ppermute | solution.py:706
  261.8 12.0 %collective-permute-start.21 = (bf16[2,192,256]{2,1,0:T(8,128)(2,1)}, bf16[2,192,256]{2,1,0:T(8,128)(2,1)S(1)}, u32[]{:S(2)}, u32[]{:S(2)}) collective-permute-start(bf16[2,192,256]{2,1,0:T(8,128)(2,1)} %get-tuple-element.77), channel_id=1, source_target_pairs={{0,4},{1,5},{2,6},{3,7},{4,0},{5,1},{6,2},{7,3},{8,12},{9,13},{10,... | collective-permute-start | bytes 589832 | tf_op jit(solution)/shard_map/ppermute | solution.py:706
  263.5 13.4 %collective-permute-start.22 = (bf16[2,192,256]{2,1,0:T(8,128)(2,1)}, bf16[2,192,256]{2,1,0:T(8,128)(2,1)S(1)}, u32[]{:S(2)}, u32[]{:S(2)}) collective-permute-start(bf16[2,192,256]{2,1,0:T(8,128)(2,1)} %get-tuple-element.78), channel_id=1, source_target_pairs={{0,5},{1,6},{2,7},{3,0},{4,1},{5,2},{6,3},{7,4},{8,13},{9,14},{10,... | collective-permute-start | bytes 589832 | tf_op jit(solution)/shard_map/ppermute | solution.py:706
  264.3 12.7 %collective-permute-start.23 = (bf16[2,192,256]{2,1,0:T(8,128)(2,1)}, bf16[2,192,256]{2,1,0:T(8,128)(2,1)S(1)}, u32[]{:S(2)}, u32[]{:S(2)}) collective-permute-start(bf16[2,192,256]{2,1,0:T(8,128)(2,1)} %get-tuple-element.79), channel_id=1, source_target_pairs={{0,6},{1,7},{2,0},{3,1},{4,2},{5,3},{6,4},{7,5},{8,14},{9,15},{10,... | collective-permute-start | bytes 589832 | tf_op jit(solution)/shard_map/ppermute | solution.py:706
  267.2 11.1 %collective-permute-start.24 = (bf16[2,192,256]{2,1,0:T(8,128)(2,1)}, bf16[2,192,256]{2,1,0:T(8,128)(2,1)S(1)}, u32[]{:S(2)}, u32[]{:S(2)}) collective-permute-start(bf16[2,192,256]{2,1,0:T(8,128)(2,1)} %get-tuple-element.80), channel_id=1, source_target_pairs={{0,7},{1,0},{2,1},{3,2},{4,3},{5,4},{6,5},{7,6},{8,15},{9,8},{10,9... | collective-permute-start | bytes 589832 | tf_op jit(solution)/shard_map/ppermute | solution.py:706
  291.2 9.3 %collective-permute-start.26 = (bf16[2,192,256]{2,1,0:T(8,128)(2,1)}, bf16[2,192,256]{2,1,0:T(8,128)(2,1)S(1)}, u32[]{:S(2)}, u32[]{:S(2)}) collective-permute-start(bf16[2,192,256]{2,1,0:T(8,128)(2,1)} %get-tuple-element.84), channel_id=1, source_target_pairs={{0,2},{1,3},{2,4},{3,5},{4,6},{5,7},{6,0},{7,1},{8,10},{9,11},{10,... | collective-permute-start | bytes 589832 | tf_op jit(solution)/shard_map/ppermute | solution.py:706
  294.7 13.2 %collective-permute-start.27 = (bf16[2,192,256]{2,1,0:T(8,128)(2,1)}, bf16[2,192,256]{2,1,0:T(8,128)(2,1)S(1)}, u32[]{:S(2)}, u32[]{:S(2)}) collective-permute-start(bf16[2,192,256]{2,1,0:T(8,128)(2,1)} %get-tuple-element.85), channel_id=1, source_target_pairs={{0,3},{1,4},{2,5},{3,6},{4,7},{5,0},{6,1},{7,2},{8,11},{9,12},{10,... | collective-permute-start | bytes 589832 | tf_op jit(solution)/shard_map/ppermute | solution.py:706
  295.4 12.7 %collective-permute-start.28 = (bf16[2,192,256]{2,1,0:T(8,128)(2,1)}, bf16[2,192,256]{2,1,0:T(8,128)(2,1)S(1)}, u32[]{:S(2)}, u32[]{:S(2)}) collective-permute-start(bf16[2,192,256]{2,1,0:T(8,128)(2,1)} %get-tuple-element.86), channel_id=1, source_target_pairs={{0,4},{1,5},{2,6},{3,7},{4,0},{5,1},{6,2},{7,3},{8,12},{9,13},{10,... | collective-permute-start | bytes 589832 | tf_op jit(solution)/shard_map/ppermute | solution.py:706
  295.4 16.4 %collective-permute-start.29 = (bf16[2,192,256]{2,1,0:T(8,128)(2,1)}, bf16[2,192,256]{2,1,0:T(8,128)(2,1)S(1)}, u32[]{:S(2)}, u32[]{:S(2)}) collective-permute-start(bf16[2,192,256]{2,1,0:T(8,128)(2,1)} %get-tuple-element.87), channel_id=1, source_target_pairs={{0,5},{1,6},{2,7},{3,0},{4,1},{5,2},{6,3},{7,4},{8,13},{9,14},{10,... | collective-permute-start | bytes 589832 | tf_op jit(solution)/shard_map/ppermute | solution.py:706
  299.0 14.8 %collective-permute-start.30 = (bf16[2,192,256]{2,1,0:T(8,128)(2,1)}, bf16[2,192,256]{2,1,0:T(8,128)(2,1)S(1)}, u32[]{:S(2)}, u32[]{:S(2)}) collective-permute-start(bf16[2,192,256]{2,1,0:T(8,128)(2,1)} %get-tuple-element.88), channel_id=1, source_target_pairs={{0,6},{1,7},{2,0},{3,1},{4,2},{5,3},{6,4},{7,5},{8,14},{9,15},{10,... | collective-permute-start | bytes 589832 | tf_op jit(solution)/shard_map/ppermute | solution.py:706
  300.4 22.9 %collective-permute-start.31 = (bf16[2,192,256]{2,1,0:T(8,128)(2,1)}, bf16[2,192,256]{2,1,0:T(8,128)(2,1)S(1)}, u32[]{:S(2)}, u32[]{:S(2)}) collective-permute-start(bf16[2,192,256]{2,1,0:T(8,128)(2,1)} %get-tuple-element.89), channel_id=1, source_target_pairs={{0,7},{1,0},{2,1},{3,2},{4,3},{5,4},{6,5},{7,6},{8,15},{9,8},{10,9... | collective-permute-start | bytes 589832 | tf_op jit(solution)/shard_map/ppermute | solution.py:706
  307.9 21.2 %collective-permute-start.34 = (bf16[16,256]{1,0:T(8,128)(2,1)S(1)}, bf16[16,256]{1,0:T(8,128)(2,1)S(1)}, u32[]{:S(2)}, u32[]{:S(2)}) collective-permute-start(bf16[16,256]{1,0:T(8,128)(2,1)S(1)} %copy-done.68), channel_id=1, source_target_pairs={{0,1},{1,2},{2,3},{3,4},{4,5},{5,6},{6,7},{7,0},{8,9},{9,10},{10,1... | collective-permute-start | bytes 24584 | tf_op jit(solution)/shard_map/ppermute | solution.py:440
  308.1 21.0 %collective-permute-start.35 = (bf16[16,256]{1,0:T(8,128)(2,1)S(1)}, bf16[16,256]{1,0:T(8,128)(2,1)S(1)}, u32[]{:S(2)}, u32[]{:S(2)}) collective-permute-start(bf16[16,256]{1,0:T(8,128)(2,1)S(1)} %copy-done.67), channel_id=1, source_target_pairs={{1,0},{2,1},{3,2},{4,3},{5,4},{6,5},{7,6},{0,7},{9,8},{10,9},{11,1... | collective-permute-start | bytes 24584 | tf_op jit(solution)/shard_map/ppermute | solution.py:440
  311.8 17.2 %collective-permute-start.32 = (bf16[16,192]{1,0:T(8,128)(2,1)S(1)}, bf16[16,192]{1,0:T(8,128)(2,1)S(1)}, u32[]{:S(2)}, u32[]{:S(2)}) collective-permute-start(bf16[16,192]{1,0:T(8,128)(2,1)S(1)} %copy-done.70), channel_id=1, source_target_pairs={{0,8},{8,16},{16,24},{24,0},{1,9},{9,17},{17,25},{25,1},{2,10},{10... | collective-permute-start | bytes 18440 | tf_op jit(solution)/shard_map/ppermute | solution.py:440
  313.8 15.3 %collective-permute-start.33 = (bf16[16,192]{1,0:T(8,128)(2,1)S(1)}, bf16[16,192]{1,0:T(8,128)(2,1)S(1)}, u32[]{:S(2)}, u32[]{:S(2)}) collective-permute-start(bf16[16,192]{1,0:T(8,128)(2,1)S(1)} %copy-done.69), channel_id=1, source_target_pairs={{8,0},{16,8},{24,16},{0,24},{9,1},{17,9},{25,17},{1,25},{10,2},{18... | collective-permute-start | bytes 18440 | tf_op jit(solution)/shard_map/ppermute | solution.py:440
  337.9 28.0 %all-to-all-start.7 = ((bf16[8,2,192,256]{3,2,1,0:T(8,128)(2,1)}), bf16[8,2,192,256]{3,2,1,0:T(8,128)(2,1)S(1)}, u32[]{:S(2)}, u32[]{:S(2)}) async-start(bf16[8,2,192,256]{3,2,1,0:T(8,128)(2,1)} %y_inverse.5.refs_15_), calls=%async_computation.7 | async-start | bytes 3145728 | tf_op jit(solution)/shard_map/all_to_all | solution.py:785
  342.6 31.9 %collective-permute-start.38 = (bf16[16,256]{1,0:T(8,128)(2,1)S(1)}, bf16[16,256]{1,0:T(8,128)(2,1)S(1)}, u32[]{:S(2)}, u32[]{:S(2)}) collective-permute-start(bf16[16,256]{1,0:T(8,128)(2,1)S(1)} %copy-done.72), channel_id=1, source_target_pairs={{0,1},{1,2},{2,3},{3,4},{4,5},{5,6},{6,7},{7,0},{8,9},{9,10},{10,1... | collective-permute-start | bytes 24584 | tf_op jit(solution)/shard_map/ppermute | solution.py:440
  343.1 28.8 %collective-permute-start.36 = (bf16[16,192]{1,0:T(8,128)(2,1)S(1)}, bf16[16,192]{1,0:T(8,128)(2,1)S(1)}, u32[]{:S(2)}, u32[]{:S(2)}) collective-permute-start(bf16[16,192]{1,0:T(8,128)(2,1)S(1)} %copy-done.74), channel_id=1, source_target_pairs={{0,8},{8,16},{16,24},{24,0},{1,9},{9,17},{17,25},{25,1},{2,10},{10... | collective-permute-start | bytes 18440 | tf_op jit(solution)/shard_map/ppermute | solution.py:440
  343.1 31.4 %collective-permute-start.37 = (bf16[16,192]{1,0:T(8,128)(2,1)S(1)}, bf16[16,192]{1,0:T(8,128)(2,1)S(1)}, u32[]{:S(2)}, u32[]{:S(2)}) collective-permute-start(bf16[16,192]{1,0:T(8,128)(2,1)S(1)} %copy-done.73), channel_id=1, source_target_pairs={{8,0},{16,8},{24,16},{0,24},{9,1},{17,9},{25,17},{1,25},{10,2},{18... | collective-permute-start | bytes 18440 | tf_op jit(solution)/shard_map/ppermute | solution.py:440
  354.4 33.7 %collective-permute-start.39 = (bf16[16,256]{1,0:T(8,128)(2,1)S(1)}, bf16[16,256]{1,0:T(8,128)(2,1)S(1)}, u32[]{:S(2)}, u32[]{:S(2)}) collective-permute-start(bf16[16,256]{1,0:T(8,128)(2,1)S(1)} %copy-done.71), channel_id=1, source_target_pairs={{1,0},{2,1},{3,2},{4,3},{5,4},{6,5},{7,6},{0,7},{9,8},{10,9},{11,1... | collective-permute-start | bytes 24584 | tf_op jit(solution)/shard_map/ppermute | solution.py:440
  371.8 16.3 %collective-permute-start.42 = (bf16[16,256]{1,0:T(8,128)(2,1)}, bf16[16,256]{1,0:T(8,128)(2,1)S(1)}, u32[]{:S(2)}, u32[]{:S(2)}) collective-permute-start(bf16[16,256]{1,0:T(8,128)(2,1)} %get-tuple-element.102), channel_id=1, source_target_pairs={{0,1},{1,2},{2,3},{3,4},{4,5},{5,6},{6,7},{7,0},{8,9},{9,10},{10,1... | collective-permute-start | bytes 24584 | tf_op jit(solution)/shard_map/ppermute | solution.py:440
  371.9 16.3 %collective-permute-start.43 = (bf16[16,256]{1,0:T(8,128)(2,1)}, bf16[16,256]{1,0:T(8,128)(2,1)S(1)}, u32[]{:S(2)}, u32[]{:S(2)}) collective-permute-start(bf16[16,256]{1,0:T(8,128)(2,1)} %get-tuple-element.103), channel_id=1, source_target_pairs={{1,0},{2,1},{3,2},{4,3},{5,4},{6,5},{7,6},{0,7},{9,8},{10,9},{11,1... | collective-permute-start | bytes 24584 | tf_op jit(solution)/shard_map/ppermute | solution.py:440
  374.5 13.6 %collective-permute-start.40 = (bf16[16,192]{1,0:T(8,128)(2,1)}, bf16[16,192]{1,0:T(8,128)(2,1)S(1)}, u32[]{:S(2)}, u32[]{:S(2)}) collective-permute-start(bf16[16,192]{1,0:T(8,128)(2,1)} %get-tuple-element.100), channel_id=1, source_target_pairs={{0,8},{8,16},{16,24},{24,0},{1,9},{9,17},{17,25},{25,1},{2,10},{10... | collective-permute-start | bytes 18440 | tf_op jit(solution)/shard_map/ppermute | solution.py:440
  374.6 13.6 %collective-permute-start.41 = (bf16[16,192]{1,0:T(8,128)(2,1)}, bf16[16,192]{1,0:T(8,128)(2,1)S(1)}, u32[]{:S(2)}, u32[]{:S(2)}) collective-permute-start(bf16[16,192]{1,0:T(8,128)(2,1)} %get-tuple-element.101), channel_id=1, source_target_pairs={{8,0},{16,8},{24,16},{0,24},{9,1},{17,9},{25,17},{1,25},{10,2},{18... | collective-permute-start | bytes 18440 | tf_op jit(solution)/shard_map/ppermute | solution.py:440
  (79 other events, 623.8 us)

commit v7 on v6

--- a/solution.py
+++ b/solution.py
@@ -566,7 +566,6 @@
     column = pl.BlockSpec((1, Z, height), lambda n: (component, 0, 0))
     row = pl.BlockSpec((1, Z, width), lambda n: (component, 0, 0))
     sums = pl.BlockSpec((3, LAYERS, height, width), lambda n: (0, n, 0, 0))
-    sums_before = pl.BlockSpec((3, LAYERS, height, width), lambda n: (0, n, 0, 0))
     operands = [slope_x, slope_y, velocity, adjoint, *halos]
     in_specs = [
         whole((width, width)),
@@ -578,11 +577,9 @@
         row,
         row,
     ]
-    aliases = {}
     if before is not None:
-        aliases = {len(operands): 0}
         operands.append(before)
-        in_specs.append(sums_before)
+        in_specs.append(sums)
 
     def kernel(*refs):
         grad_vort_kernel(component, *refs[:8], None if before is None else refs[8], refs[-1])
@@ -593,7 +590,6 @@
         in_specs=in_specs + tied(after),
         out_specs=sums,
         out_shape=jax.ShapeDtypeStruct((3, Z, height, width), f32),
-        input_output_aliases=aliases,
         compiler_params=params(),
         cost_estimate=takes(9),
         name="add_grad_vort",
@@ -767,24 +763,26 @@
             parts = pair_exchange(parts, "gy", half)
         return parts.reshape(size_x, halves, planes, 2, modes, width)
 
+    def rows_of(component, modes_back, after):
+        split = component != BACK_ORDER[2]
+        return y_inverse(me, y_back_table, modes_back, size_y, split, after)
+
+    def layers_of(rows):
+        if len(rows) == 1:
+            return [lax.all_to_all(rows[0], "gy", 0, 0, tiled=True).reshape(Z, height, width)]
+        return shifted(rows, "gy")
+
     one, two, three = BACK_ORDER
     spectra = {FORWARD_ORDER[0]: spectrum(0, (sent[1],))}
     spectra[FORWARD_ORDER[1]] = spectrum(1, (sent[2],) + saved_halos)
     curl_one = curl(one, ())
     spectra[FORWARD_ORDER[2]] = spectrum(2, (curl_one,))
     curl_two = curl(two, ())
-    curl_three = curl(three, (curl_two,))
-    returned = {one: back(curl_one), two: back(curl_two), three: back(curl_three)}
-
-    def rows_of(component, after):
-        split = component != BACK_ORDER[2]
-        return y_inverse(me, y_back_table, returned[component], size_y, split, after)
-
-    def adjoint_of(component, rows, after):
-        if len(rows) == 1:
-            parts = [lax.all_to_all(rows[0], "gy", 0, 0, tiled=True).reshape(Z, height, width)]
-        else:
-            parts = shifted(rows, "gy")
+    rows_one = rows_of(one, back(curl_one), (curl_two,))
+    layers_one = layers_of(rows_one)
+    curl_three = curl(three, tuple(layers_one))
+
+    def adjoint_of(component, parts, after):
         adjoint, first_x, last_x, first_y, last_y = make_adjoint(
             me, parts, cot_vort, component, after
         )
@@ -800,15 +798,14 @@
             components, slope_x, vorticity, adjoints, saved_halos, halos, before, after
         )
 
-    rows_one = rows_of(one, (curl_three,))
-    adjoint_one, halos_one = adjoint_of(one, rows_one, ())
-    rows_two = rows_of(two, (adjoint_one,))
+    adjoint_one, halos_one = adjoint_of(one, layers_one, ())
+    rows_two = rows_of(two, back(curl_two), (adjoint_one,))
     grad_vort = vort_of(one, adjoint_one, None, (rows_two[0],))
-    adjoint_two, halos_two = adjoint_of(two, rows_two, (grad_vort,))
-    rows_three = rows_of(three, (adjoint_two,) + halos_one)
+    adjoint_two, halos_two = adjoint_of(two, layers_of(rows_two), (grad_vort,))
+    rows_three = rows_of(three, back(curl_three), (adjoint_two,) + halos_one)
     grad_vel = vel_of((one,), [adjoint_one], [halos_one], None, (rows_three[0],))
     grad_vort = vort_of(two, adjoint_two, grad_vort, (grad_vel,))
-    adjoint_three, halos_three = adjoint_of(three, rows_three, (grad_vort,))
+    adjoint_three, halos_three = adjoint_of(three, layers_of(rows_three), (grad_vort,))
     grad_vort = vort_of(three, adjoint_three, grad_vort, ())
     grad_vel = vel_of(
         (two, three), [adjoint_two, adjoint_three], [halos_two, halos_three], grad_vel, (grad_vort,)

time: 402 us -> 373 us (0.928)
  waiting for transfers between devices: 128 us -> 101 us
  local copies, waits for them, and re-layouts: 24.2 us -> 20.1 us
    all_to_all x3, waiting for transfers between devices: 51.3 us -> 24.7 us  [back(): parts = lax.all_to_all(filtered, 'gx', 0, 0, tiled=True)]
    unnamed x154 -> x152, local copies, waits for them, and re-layouts: 22.2 us -> 18 us
  transfers between devices with their start and end apart: 52 -> 52, of which waited for: 26 -> 27; matrix products, arithmetic and copies ran while one was open for 1% -> 1% of each run, Pallas kernels for 27% -> 30%
where the time goes in v7:
time: 373 us; the launch traced here: 372 us
  Pallas kernels  139 us (37%)
  starting transfers between devices  110 us (29%)
  waiting for transfers between devices  101 us (27%)
  local copies, waits for them, and re-layouts  20.1 us (5%)
    ppermute x28, starting transfers between devices, shifted(): lax.ppermute(parts[s], axis, [(i, (i + s) % count) for i in range(count)])  43.2 us
    ppermute x28, waiting for transfers between devices, shifted(): lax.ppermute(parts[s], axis, [(i, (i + s) % count) for i in range(count)])  36.7 us
    pallas_call x3, Pallas kernels, add_grad_vort(): pl.pallas_call(kernel, grid=(Z // LAYERS,), in_specs=in_specs + tied(afte...  26.8 us
    ppermute x16, starting transfers between devices, exchange(): return (lax.ppermute(last, axis, up), lax.ppermute(first, axis, down))  25.7 us
    all_to_all x3, waiting for transfers between devices, back(): parts = lax.all_to_all(filtered, 'gx', 0, 0, tiled=True)  24.7 us
    pallas_call x3, Pallas kernels, y_inverse(): pl.pallas_call(kernel, in_specs=[pl.BlockSpec(memory_space=pltpu.SMEM), p...  22.6 us
    pallas_call x3, Pallas kernels, y_transform(): pl.pallas_call(kernel, in_specs=[pl.BlockSpec(memory_space=pltpu.SMEM), p...  21 us
    pallas_call x2, Pallas kernels, write_grad_vel(): pl.pallas_call(kernel, grid=(Z // LAYERS,), in_specs=in_specs + tied(afte...  18.4 us
  transfers between devices with their start and end apart: 52, of which 27 were waited for; matrix products, arithmetic and copies ran while one was open for 1% of the time, Pallas kernels for 30%

profile of v7, /device:TPU:0, one launch (start us, length us, event | category | flops | bytes accessed | tf_op | source)
XLA Modules:
  0.0 372.0 jit_solution(6294308663549097538)
XLA Ops:
  0.6 3.2 depth_transform.3.refs_0_
  3.8 5.2 %all-to-all-start = ((bf16[8,2,192,256]{3,2,1,0:T(8,128)(2,1)}), bf16[8,2,192,256]{3,2,1,0:T(8,128)(2,1)S(1)}, u32[]{:S(2)}, u32[]{:S(2)}) async-start(bf16[8,2,192,256]{3,2,1,0:T(8,128)(2,1)} %bitcast.27), calls=%async_computation | async-start | bytes 3145728 | tf_op jit(solution)/shard_map/all_to_all | solution.py:743
  11.6 4.6 %edge_columns.2 = (bf16[3,16,192]{2,1,0:T(8,128)(2,1)}, bf16[3,16,192]{2,1,0:T(8,128)(2,1)}) custom-call(bf16[3,16,192,256]{3,2,1,0:T(8,128)(2,1)} %refs_2_.8, bf16[16,192,256]{2,1,0:T(8,128)(2,1)} %depth_transform.3.refs_0_), custom_call_target="tpu_custom_call" | custom-call | flops 1 | bytes 12000000 | tf_op jit(solution)/shard_map/edge_columns/pallas_call | solution.py:424
  16.1 13.9 %all-to-all-done.refs_0_ = bf16[8,2,192,256]{3,2,1,0:T(8,128)(2,1)S(1)} async-done(((bf16[8,2,192,256]{3,2,1,0:T(8,128)(2,1)}), bf16[8,2,192,256]{3,2,1,0:T(8,128)(2,1)S(1)}, u32[]{:S(2)}, u32[]{:S(2)}) %all-to-all-start) | async-done | bytes 1572896 | tf_op jit(solution)/shard_map/all_to_all | solution.py:743
  31.1 7.0 %y_transform.3 = bf16[4,1,2,2,192,256]{5,4,3,2,1,0:T(8,128)(2,1)} custom-call(s32[1]{0:T(128)} %bitcast.me_ref.refs_0_, bf16[1536,1536]{1,0:T(8,128)(2,1)} %constant.33.clone.table_ref, bf16[8,2,192,256]{3,2,1,0:T(8,128)(2,1)} %copy-done.28, bf16[3,16,192]{2,1,0:T(8,128)(2,1)} %get-tuple-element.53.refs_1_, bf16[1,16,192]{2,1,0:T(8,128)(2,1)} %get-tuple-element.54.refs_2_), custom_call_target="tpu_custom_call" | custom-call | flops 1 | bytes 15000000 | tf_op jit(solution)/shard_map/y_transform/pallas_call | solution.py:212
  38.1 4.9 %all-to-all-start.1 = ((bf16[4,2,2,192,256]{4,3,2,1,0:T(8,128)(2,1)}), bf16[4,2,2,192,256]{4,3,2,1,0:T(8,128)(2,1)S(1)}, u32[]{:S(2)}, u32[]{:S(2)}) async-start(bf16[4,2,2,192,256]{4,3,2,1,0:T(8,128)(2,1)} %bitcast.28), calls=%async_computation.1 | async-start | bytes 3145728 | tf_op jit(solution)/shard_map/all_to_all | solution.py:754
  43.0 3.3 depth_transform.4
  49.7 4.4 %collective-permute-done.refs_1_ = bf16[2,192,256]{2,1,0:T(8,128)(2,1)S(1)} collective-permute-done((bf16[2,192,256]{2,1,0:T(8,128)(2,1)}, bf16[2,192,256]{2,1,0:T(8,128)(2,1)S(1)}, u32[]{:S(2)}, u32[]{:S(2)}) %collective-permute-start) | collective-permute-done | bytes 196640 | tf_op jit(solution)/shard_map/ppermute | solution.py:702
  57.6 5.3 %collective-permute-done.2.refs_3_ = bf16[2,192,256]{2,1,0:T(8,128)(2,1)S(1)} collective-permute-done((bf16[2,192,256]{2,1,0:T(8,128)(2,1)}, bf16[2,192,256]{2,1,0:T(8,128)(2,1)S(1)}, u32[]{:S(2)}, u32[]{:S(2)}) %collective-permute-start.2) | collective-permute-done | bytes 196640 | tf_op jit(solution)/shard_map/ppermute | solution.py:702
  66.2 7.0 %y_transform.4 = bf16[4,1,2,2,192,256]{5,4,3,2,1,0:T(8,128)(2,1)} custom-call(s32[1]{0:T(128)} %bitcast.me_ref.refs_0_, bf16[1536,1536]{1,0:T(8,128)(2,1)} %constant.33.clone.table_ref, bf16[2,192,256]{2,1,0:T(8,128)(2,1)} %get-tuple-element.55.refs_0_, bf16[2,192,256]{2,1,0:T(8,128)(2,1)} %copy-done.37, bf16[2,192,256]{2,1,0:T(8,128)(2,1)} %copy-done.39, ...), custom_call_target="tpu_custom_call" | custom-call | flops 1 | bytes 15000000 | tf_op jit(solution)/shard_map/y_transform/pallas_call | solution.py:212
  73.2 3.9 %all-to-all-done.1.modes_ref = bf16[4,2,2,192,256]{4,3,2,1,0:T(8,128)(2,1)S(1)} async-done(((bf16[4,2,2,192,256]{4,3,2,1,0:T(8,128)(2,1)}), bf16[4,2,2,192,256]{4,3,2,1,0:T(8,128)(2,1)S(1)}, u32[]{:S(2)}, u32[]{:S(2)}) %all-to-all-start.1) | async-done | bytes 1572896 | tf_op jit(solution)/shard_map/all_to_all | solution.py:754
  77.2 4.3 %all-to-all-start.3 = ((bf16[4,2,2,192,256]{4,3,2,1,0:T(8,128)(2,1)}), bf16[4,2,2,192,256]{4,3,2,1,0:T(8,128)(2,1)}, u32[]{:S(2)}, u32[]{:S(2)}) async-start(bf16[4,2,2,192,256]{4,3,2,1,0:T(8,128)(2,1)} %bitcast.22), calls=%async_computation.3 | async-start | bytes 3145728 | tf_op jit(solution)/shard_map/all_to_all | solution.py:754
  81.5 3.3 depth_transform.5
  84.8 3.6 collective-permute-start.8
  95.0 4.0 %collective-permute-start.13 = (bf16[2,192,256]{2,1,0:T(8,128)(2,1)}, bf16[2,192,256]{2,1,0:T(8,128)(2,1)S(1)}, u32[]{:S(2)}, u32[]{:S(2)}) collective-permute-start(bf16[2,192,256]{2,1,0:T(8,128)(2,1)} %get-tuple-element.70), channel_id=1, source_target_pairs={{0,7},{1,0},{2,1},{3,2},{4,3},{5,4},{6,5},{7,6},{8,15},{9,8},{10,9... | collective-permute-start | bytes 589832 | tf_op jit(solution)/shard_map/ppermute | solution.py:702
  101.7 3.1 collective-permute-done.11.refs_5_
  106.7 7.0 %y_transform.5 = bf16[4,1,2,2,192,256]{5,4,3,2,1,0:T(8,128)(2,1)} custom-call(s32[1]{0:T(128)} %bitcast.me_ref.refs_0_, bf16[1536,1536]{1,0:T(8,128)(2,1)} %constant.33.clone.table_ref, bf16[2,192,256]{2,1,0:T(8,128)(2,1)} %get-tuple-element.63.refs_0_, bf16[2,192,256]{2,1,0:T(8,128)(2,1)} %copy-done.36, bf16[2,192,256]{2,1,0:T(8,128)(2,1)} %copy-done.38, ...), custom_call_target="tpu_custom_call" | custom-call | flops 1 | bytes 15000000 | tf_op jit(solution)/shard_map/y_transform/pallas_call | solution.py:212
  113.8 4.2 %all-to-all-done.3.modes_ref = bf16[4,2,2,192,256]{4,3,2,1,0:T(8,128)(2,1)} async-done(((bf16[4,2,2,192,256]{4,3,2,1,0:T(8,128)(2,1)}), bf16[4,2,2,192,256]{4,3,2,1,0:T(8,128)(2,1)}, u32[]{:S(2)}, u32[]{:S(2)}) %all-to-all-start.3) | async-done | bytes 1572896 | tf_op jit(solution)/shard_map/all_to_all | solution.py:754
  118.0 4.3 %all-to-all-start.2 = ((bf16[4,2,2,192,256]{4,3,2,1,0:T(8,128)(2,1)}), bf16[4,2,2,192,256]{4,3,2,1,0:T(8,128)(2,1)}, u32[]{:S(2)}, u32[]{:S(2)}) async-start(bf16[4,2,2,192,256]{4,3,2,1,0:T(8,128)(2,1)} %bitcast.25), calls=%async_computation.2 | async-start | bytes 3145728 | tf_op jit(solution)/shard_map/all_to_all | solution.py:754
  127.2 3.8 %collective-permute-start.15 = (bf16[4,16,192]{2,1,0:T(8,128)(2,1)S(1)}, bf16[4,16,192]{2,1,0:T(8,128)(2,1)S(1)}, u32[]{:S(2)}, u32[]{:S(2)}) collective-permute-start(bf16[4,16,192]{2,1,0:T(8,128)(2,1)S(1)} %pad_maximum_fusion.1), channel_id=1, source_target_pairs={{8,0},{16,8},{24,16},{0,24},{9,1},{17,9},{25,17},{1,25},{10,2},{18... | collective-permute-start | bytes 73736 | tf_op jit(solution)/shard_map/ppermute | solution.py:440
  135.1 13.2 %collective-permute-done.15.refs_2_.refs_5_.refs_8_.refs_11_ = bf16[4,16,192]{2,1,0:T(8,128)(2,1)S(1)} collective-permute-done((bf16[4,16,192]{2,1,0:T(8,128)(2,1)S(1)}, bf16[4,16,192]{2,1,0:T(8,128)(2,1)S(1)}, u32[]{:S(2)}, u32[]{:S(2)}) %collective-permute-start.15) | collective-permute-done | bytes 24608 | tf_op jit(solution)/shard_map/ppermute | solution.py:440
  148.4 4.4 %collective-permute-done.14.refs_1_.refs_4_.refs_7_.refs_10_ = bf16[4,16,192]{2,1,0:T(8,128)(2,1)S(1)} collective-permute-done((bf16[4,16,192]{2,1,0:T(8,128)(2,1)S(1)}, bf16[4,16,192]{2,1,0:T(8,128)(2,1)S(1)}, u32[]{:S(2)}, u32[]{:S(2)}) %collective-permute-start.14) | collective-permute-done | bytes 24608 | tf_op jit(solution)/shard_map/ppermute | solution.py:440
  152.8 3.1 x_transform.4.refs_2_.refs_3_
  160.1 9.3 %all-to-all-start.4 = ((bf16[4,2,2,192,256]{4,3,2,1,0:T(8,128)(2,1)}), bf16[4,2,2,192,256]{4,3,2,1,0:T(8,128)(2,1)}, u32[]{:S(2)}, u32[]{:S(2)}) async-start(bf16[4,2,2,192,256]{4,3,2,1,0:T(8,128)(2,1)} %copy-done.10), calls=%async_computation.4 | async-start | bytes 3145728 | tf_op jit(solution)/shard_map/all_to_all | solution.py:761
  172.4 3.3 x_transform.5.refs_2_.refs_3_
  181.6 23.9 %all-to-all-done.4 = bf16[4,2,2,192,256]{4,3,2,1,0:T(8,128)(2,1)} async-done(((bf16[4,2,2,192,256]{4,3,2,1,0:T(8,128)(2,1)}), bf16[4,2,2,192,256]{4,3,2,1,0:T(8,128)(2,1)}, u32[]{:S(2)}, u32[]{:S(2)}) %all-to-all-start.4) | async-done | bytes 1572896 | tf_op jit(solution)/shard_map/all_to_all | solution.py:761
  205.4 4.4 %all-to-all-start.6 = ((bf16[4,2,2,192,256]{4,3,2,1,0:T(8,128)(2,1)}), bf16[4,2,2,192,256]{4,3,2,1,0:T(8,128)(2,1)}, u32[]{:S(2)}, u32[]{:S(2)}) async-start(bf16[4,2,2,192,256]{4,3,2,1,0:T(8,128)(2,1)} %copy-done.13), calls=%async_computation.6 | async-start | bytes 3145728 | tf_op jit(solution)/shard_map/all_to_all | solution.py:761
  209.8 8.0 %y_inverse.3 = (bf16[2,192,256]{2,1,0:T(8,128)(2,1)}, bf16[2,192,256]{2,1,0:T(8,128)(2,1)}, bf16[2,192,256]{2,1,0:T(8,128)(2,1)}, bf16[2,192,256]{2,1,0:T(8,128)...) custom-call(s32[1]{0:T(128)} %bitcast.me_ref.refs_0_, ...), custom_call_target="tpu_custom_call" | custom-call | flops 1 | bytes 12000000 | tf_op jit(solution)/shard_map/y_inverse/pallas_call | solution.py:255
  217.9 3.6 collective-permute-start.19
  228.0 3.7 collective-permute-start.24
  241.7 3.8 %curl_inverse.5 = bf16[4,2,2,192,256]{4,3,2,1,0:T(8,128)(2,1)} custom-call(s32[2]{0:T(128)S(1)} %pad_add_fusion.refs_0_, bf16[1024,1024]{1,0:T(8,128)(2,1)S(1)} %copy-done.7, f32[2,2,192,1024]{3,2,1,0:T(8,128)S(1)} %copy-done.1, f32[2,2,192,1024]{3,2,1,0:T(8,128)S(1)} %copy-done.3, bf16[2,192,256]{2,1,0:T(8,128)(2,1)S(1)} %copy-done.18, ...), custom_call_target="tpu_custom_call" | custom-call | flops 1 | bytes 12000000 | tf_op jit(solution)/shard_map/curl_inverse/pallas_call | solution.py:362
  246.3 4.3 %all-to-all-start.5 = ((bf16[4,2,2,192,256]{4,3,2,1,0:T(8,128)(2,1)}), bf16[4,2,2,192,256]{4,3,2,1,0:T(8,128)(2,1)S(1)}, u32[]{:S(2)}, u32[]{:S(2)}) async-start(bf16[4,2,2,192,256]{4,3,2,1,0:T(8,128)(2,1)} %curl_inverse.5), calls=%async_computation.5 | async-start | bytes 3145728 | tf_op jit(solution)/shard_map/all_to_all | solution.py:761
  250.6 4.9 %make_adjoint.3 = (f32[16,192,256]{2,1,0:T(8,128)}, bf16[16,192]{1,0:T(8,128)(2,1)}, bf16[16,192]{1,0:T(8,128)(2,1)}, bf16[16,256]{1,0:T(8,128)(2,1)}, bf16[16,256]{1,0:T(8,128)(2,1)}) custom-call(s32[1]{0:T(128)} %bitcast.me_ref.refs_0_, bf16[2,192,256]{2,1,0:T(8,128)(2,1)} %get-tuple-element.73.refs_4_.refs_0_, bf16[2,192,256]{2,1,0:T(8,128)(2,1)} %copy-done.19, ...), custom_call_target="tpu_custom_call" | custom-call | flops 1 | bytes 15000000 | tf_op jit(solution)/shard_map/make_adjoint/pallas_call | solution.py:489
  255.6 7.1 %y_inverse.4 = (bf16[2,192,256]{2,1,0:T(8,128)(2,1)}, bf16[2,192,256]{2,1,0:T(8,128)(2,1)}, bf16[2,192,256]{2,1,0:T(8,128)(2,1)}, bf16[2,192,256]{2,1,0:T(8,128)...) custom-call(s32[1]{0:T(128)} %bitcast.me_ref.refs_0_, ...), custom_call_target="tpu_custom_call" | custom-call | flops 1 | bytes 12000000 | tf_op jit(solution)/shard_map/y_inverse/pallas_call | solution.py:255
  262.7 3.7 collective-permute-start.26
  272.1 3.9 %collective-permute-start.31 = (bf16[2,192,256]{2,1,0:T(8,128)(2,1)}, bf16[2,192,256]{2,1,0:T(8,128)(2,1)S(1)}, u32[]{:S(2)}, u32[]{:S(2)}) collective-permute-start(bf16[2,192,256]{2,1,0:T(8,128)(2,1)} %get-tuple-element.89), channel_id=1, source_target_pairs={{0,7},{1,0},{2,1},{3,2},{4,3},{5,4},{6,5},{7,6},{8,15},{9,8},{10,9... | collective-permute-start | bytes 589832 | tf_op jit(solution)/shard_map/ppermute | solution.py:702
  275.9 3.7 collective-permute-done.27.refs_3_
  287.4 7.3 %add_grad_vort.3.refs_9_.refs_8_ = f32[3,16,192,256]{3,2,1,0:T(8,128)} custom-call(bf16[256,256]{1,0:T(8,128)(2,1)} %constant.37.clone.refs_0_, bf16[192,192]{1,0:T(8,128)(2,1)} %constant.38.clone.refs_1_, bf16[3,16,192,256]{3,2,1,0:T(8,128)(2,1)} %refs_2_.8, f32[16,192,256]{2,1,0:T(8,128)} %get-tuple-element.81.refs_0_.refs_3_.refs_4_.refs_5_.refs_6_, ...), custom_call_target="tpu_custom_call" | custom-call | flops 1 | bytes 27000000 | tf_op jit(solution)/shard_map/add_grad_vort/pallas_call | solution.py:587
  295.5 5.0 %make_adjoint.4 = (f32[16,192,256]{2,1,0:T(8,128)}, bf16[16,192]{1,0:T(8,128)(2,1)}, bf16[16,192]{1,0:T(8,128)(2,1)}, bf16[16,256]{1,0:T(8,128)(2,1)}, bf16[16,256]{1,0:T(8,128)(2,1)}) custom-call(s32[1]{0:T(128)} %bitcast.me_ref.refs_0_, bf16[2,192,256]{2,1,0:T(8,128)(2,1)} %get-tuple-element.82.refs_8_.refs_0_, bf16[2,192,256]{2,1,0:T(8,128)(2,1)} %copy-done.29, ...), custom_call_target="tpu_custom_call" | custom-call | flops 1 | bytes 15000000 | tf_op jit(solution)/shard_map/make_adjoint/pallas_call | solution.py:489
  301.7 7.5 %y_inverse.5.refs_15_ = bf16[8,2,192,256]{3,2,1,0:T(8,128)(2,1)} custom-call(s32[1]{0:T(128)} %bitcast.me_ref.refs_0_, bf16[1536,1536]{1,0:T(8,128)(2,1)} %constant.36.clone.table_ref, bf16[4,1,2,2,192,256]{5,4,3,2,1,0:T(8,128)(2,1)} %bitcast.31, f32[16,192,256]{2,1,0:T(8,128)} %get-tuple-element.90.refs_0_.refs_3_.refs_4_.refs_5_.refs_6_, ...), custom_call_target="tpu_custom_call" | custom-call | flops 1 | bytes 12000000 | tf_op jit(solution)/shard_map/y_inverse/pallas_call | solution.py:255
  309.3 4.9 %all-to-all-start.7 = ((bf16[8,2,192,256]{3,2,1,0:T(8,128)(2,1)}), bf16[8,2,192,256]{3,2,1,0:T(8,128)(2,1)S(1)}, u32[]{:S(2)}, u32[]{:S(2)}) async-start(bf16[8,2,192,256]{3,2,1,0:T(8,128)(2,1)} %y_inverse.5.refs_15_), calls=%async_computation.7 | async-start | bytes 3145728 | tf_op jit(solution)/shard_map/all_to_all | solution.py:772
  314.7 3.8 %collective-permute-start.37 = (bf16[16,192]{1,0:T(8,128)(2,1)S(1)}, bf16[16,192]{1,0:T(8,128)(2,1)S(1)}, u32[]{:S(2)}, u32[]{:S(2)}) collective-permute-start(bf16[16,192]{1,0:T(8,128)(2,1)S(1)} %copy-done.72), channel_id=1, source_target_pairs={{8,0},{16,8},{24,16},{0,24},{9,1},{17,9},{25,17},{1,25},{10,2},{18... | collective-permute-start | bytes 18440 | tf_op jit(solution)/shard_map/ppermute | solution.py:440
  318.5 7.5 %write_grad_vel.2.refs_9_.refs_22_ = f32[3,16,192,256]{3,2,1,0:T(8,128)} custom-call(bf16[256,256]{1,0:T(8,128)(2,1)} %constant.37.clone.refs_0_, bf16[3,16,192,256]{3,2,1,0:T(8,128)(2,1)} %refs_3_.3, bf16[3,16,192,256]{3,2,1,0:T(8,128)(2,1)} %refs_3_.3, bf16[3,16,192,256]{3,2,1,0:T(8,128)(2,1)} %refs_3_.3, ...), custom_call_target="tpu_custom_call" | custom-call | flops 1 | bytes 18000000 | tf_op jit(solution)/shard_map/write_grad_vel/pallas_call | solution.py:677
  327.7 9.7 %add_grad_vort.4.refs_2_.refs_8_ = f32[3,16,192,256]{3,2,1,0:T(8,128)} custom-call(bf16[256,256]{1,0:T(8,128)(2,1)} %constant.37.clone.refs_0_, bf16[192,192]{1,0:T(8,128)(2,1)} %constant.38.clone.refs_1_, bf16[3,16,192,256]{3,2,1,0:T(8,128)(2,1)} %refs_2_.8, f32[16,192,256]{2,1,0:T(8,128)} %get-tuple-element.90.refs_0_.refs_3_.refs_4_.refs_5_.refs_6_, ...), custom_call_target="tpu_custom_call" | custom-call | flops 1 | bytes 27000000 | tf_op jit(solution)/shard_map/add_grad_vort/pallas_call | solution.py:587
  338.6 4.8 %make_adjoint.5 = (f32[16,192,256]{2,1,0:T(8,128)}, bf16[16,192]{1,0:T(8,128)(2,1)}, bf16[16,192]{1,0:T(8,128)(2,1)}, bf16[16,256]{1,0:T(8,128)(2,1)}, bf16[16,256]{1,0:T(8,128)(2,1)}) custom-call(s32[1]{0:T(128)} %bitcast.me_ref.refs_0_, bf16[16,192,256]{2,1,0:T(8,128)(2,1)} %bitcast.30, f32[3,16,192,256]{3,2,1,0:T(8,128)} %refs_1_.14, ...), custom_call_target="tpu_custom_call" | custom-call | flops 1 | bytes 15000000 | tf_op jit(solution)/shard_map/make_adjoint/pallas_call | solution.py:489
  346.0 3.8 %collective-permute-start.41 = (bf16[16,192]{1,0:T(8,128)(2,1)}, bf16[16,192]{1,0:T(8,128)(2,1)S(1)}, u32[]{:S(2)}, u32[]{:S(2)}) collective-permute-start(bf16[16,192]{1,0:T(8,128)(2,1)} %get-tuple-element.101), channel_id=1, source_target_pairs={{8,0},{16,8},{24,16},{0,24},{9,1},{17,9},{25,17},{1,25},{10,2},{18... | collective-permute-start | bytes 18440 | tf_op jit(solution)/shard_map/ppermute | solution.py:440
  349.8 9.7 %add_grad_vort.5.refs_23_ = f32[3,16,192,256]{3,2,1,0:T(8,128)} custom-call(bf16[256,256]{1,0:T(8,128)(2,1)} %constant.37.clone.refs_0_, bf16[192,192]{1,0:T(8,128)(2,1)} %constant.38.clone.refs_1_, bf16[3,16,192,256]{3,2,1,0:T(8,128)(2,1)} %refs_2_.8, f32[16,192,256]{2,1,0:T(8,128)} %get-tuple-element.95.refs_3_.refs_7_.refs_8_.refs_9_, ...), custom_call_target="tpu_custom_call" | custom-call | flops 1 | bytes 27000000 | tf_op jit(solution)/shard_map/add_grad_vort/pallas_call | solution.py:587
  360.8 10.9 %write_grad_vel.3 = f32[3,16,192,256]{3,2,1,0:T(8,128)} custom-call(bf16[256,256]{1,0:T(8,128)(2,1)} %constant.37.clone.refs_0_, bf16[3,16,192,256]{3,2,1,0:T(8,128)(2,1)} %refs_3_.3, bf16[3,16,192,256]{3,2,1,0:T(8,128)(2,1)} %refs_3_.3, bf16[3,16,192,256]{3,2,1,0:T(8,128)(2,1)} %refs_3_.3, ...), custom_call_target="tpu_custom_call", output_to_operand_aliasing={{}: (22, {})} | custom-call | flops 1 | bytes 36000000 | tf_op jit(solution)/shard_map/write_grad_vel/pallas_call | solution.py:677
  (240 shorter events, 86.9 us)
Async XLA Ops:
  3.8 26.2 %all-to-all-start = ((bf16[8,2,192,256]{3,2,1,0:T(8,128)(2,1)}), bf16[8,2,192,256]{3,2,1,0:T(8,128)(2,1)S(1)}, u32[]{:S(2)}, u32[]{:S(2)}) async-start(bf16[8,2,192,256]{3,2,1,0:T(8,128)(2,1)} %bitcast.27), calls=%async_computation | async-start | bytes 3145728 | tf_op jit(solution)/shard_map/all_to_all | solution.py:743
  38.1 39.1 %all-to-all-start.1 = ((bf16[4,2,2,192,256]{4,3,2,1,0:T(8,128)(2,1)}), bf16[4,2,2,192,256]{4,3,2,1,0:T(8,128)(2,1)S(1)}, u32[]{:S(2)}, u32[]{:S(2)}) async-start(bf16[4,2,2,192,256]{4,3,2,1,0:T(8,128)(2,1)} %bitcast.28), calls=%async_computation.1 | async-start | bytes 3145728 | tf_op jit(solution)/shard_map/all_to_all | solution.py:754
  46.3 9.0 %collective-permute-start.1 = (bf16[2,192,256]{2,1,0:T(8,128)(2,1)}, bf16[2,192,256]{2,1,0:T(8,128)(2,1)S(1)}, u32[]{:S(2)}, u32[]{:S(2)}) collective-permute-start(bf16[2,192,256]{2,1,0:T(8,128)(2,1)} %get-tuple-element.57), channel_id=1, source_target_pairs={{0,2},{1,3},{2,4},{3,5},{4,6},{5,7},{6,0},{7,1},{8,10},{9,11},{10,... | collective-permute-start | bytes 589832 | tf_op jit(solution)/shard_map/ppermute | solution.py:702
  46.8 16.1 %collective-permute-start.2 = (bf16[2,192,256]{2,1,0:T(8,128)(2,1)}, bf16[2,192,256]{2,1,0:T(8,128)(2,1)S(1)}, u32[]{:S(2)}, u32[]{:S(2)}) collective-permute-start(bf16[2,192,256]{2,1,0:T(8,128)(2,1)} %get-tuple-element.58), channel_id=1, source_target_pairs={{0,3},{1,4},{2,5},{3,6},{4,7},{5,0},{6,1},{7,2},{8,11},{9,12},{10,... | collective-permute-start | bytes 589832 | tf_op jit(solution)/shard_map/ppermute | solution.py:702
  48.3 14.8 %collective-permute-start.3 = (bf16[2,192,256]{2,1,0:T(8,128)(2,1)}, bf16[2,192,256]{2,1,0:T(8,128)(2,1)S(1)}, u32[]{:S(2)}, u32[]{:S(2)}) collective-permute-start(bf16[2,192,256]{2,1,0:T(8,128)(2,1)} %get-tuple-element.59), channel_id=1, source_target_pairs={{0,4},{1,5},{2,6},{3,7},{4,0},{5,1},{6,2},{7,3},{8,12},{9,13},{10,... | collective-permute-start | bytes 589832 | tf_op jit(solution)/shard_map/ppermute | solution.py:702
  49.7 15.7 %collective-permute-start.4 = (bf16[2,192,256]{2,1,0:T(8,128)(2,1)}, bf16[2,192,256]{2,1,0:T(8,128)(2,1)S(1)}, u32[]{:S(2)}, u32[]{:S(2)}) collective-permute-start(bf16[2,192,256]{2,1,0:T(8,128)(2,1)} %get-tuple-element.60), channel_id=1, source_target_pairs={{0,5},{1,6},{2,7},{3,0},{4,1},{5,2},{6,3},{7,4},{8,13},{9,14},{10,... | collective-permute-start | bytes 589832 | tf_op jit(solution)/shard_map/ppermute | solution.py:702
  54.1 11.3 %collective-permute-start.5 = (bf16[2,192,256]{2,1,0:T(8,128)(2,1)}, bf16[2,192,256]{2,1,0:T(8,128)(2,1)S(1)}, u32[]{:S(2)}, u32[]{:S(2)}) collective-permute-start(bf16[2,192,256]{2,1,0:T(8,128)(2,1)} %get-tuple-element.61), channel_id=1, source_target_pairs={{0,6},{1,7},{2,0},{3,1},{4,2},{5,3},{6,4},{7,5},{8,14},{9,15},{10,... | collective-permute-start | bytes 589832 | tf_op jit(solution)/shard_map/ppermute | solution.py:702
  55.3 10.1 %collective-permute-start.6 = (bf16[2,192,256]{2,1,0:T(8,128)(2,1)}, bf16[2,192,256]{2,1,0:T(8,128)(2,1)S(1)}, u32[]{:S(2)}, u32[]{:S(2)}) collective-permute-start(bf16[2,192,256]{2,1,0:T(8,128)(2,1)} %get-tuple-element.62), channel_id=1, source_target_pairs={{0,7},{1,0},{2,1},{3,2},{4,3},{5,4},{6,5},{7,6},{8,15},{9,8},{10,9... | collective-permute-start | bytes 589832 | tf_op jit(solution)/shard_map/ppermute | solution.py:702
  77.2 40.9 %all-to-all-start.3 = ((bf16[4,2,2,192,256]{4,3,2,1,0:T(8,128)(2,1)}), bf16[4,2,2,192,256]{4,3,2,1,0:T(8,128)(2,1)}, u32[]{:S(2)}, u32[]{:S(2)}) async-start(bf16[4,2,2,192,256]{4,3,2,1,0:T(8,128)(2,1)} %bitcast.22), calls=%async_computation.3 | async-start | bytes 3145728 | tf_op jit(solution)/shard_map/all_to_all | solution.py:754
  84.8 10.2 %collective-permute-start.8 = (bf16[2,192,256]{2,1,0:T(8,128)(2,1)}, bf16[2,192,256]{2,1,0:T(8,128)(2,1)S(1)}, u32[]{:S(2)}, u32[]{:S(2)}) collective-permute-start(bf16[2,192,256]{2,1,0:T(8,128)(2,1)} %get-tuple-element.65), channel_id=1, source_target_pairs={{0,2},{1,3},{2,4},{3,5},{4,6},{5,7},{6,0},{7,1},{8,10},{9,11},{10,... | collective-permute-start | bytes 589832 | tf_op jit(solution)/shard_map/ppermute | solution.py:702
  88.4 13.1 %collective-permute-start.9 = (bf16[2,192,256]{2,1,0:T(8,128)(2,1)}, bf16[2,192,256]{2,1,0:T(8,128)(2,1)S(1)}, u32[]{:S(2)}, u32[]{:S(2)}) collective-permute-start(bf16[2,192,256]{2,1,0:T(8,128)(2,1)} %get-tuple-element.66), channel_id=1, source_target_pairs={{0,3},{1,4},{2,5},{3,6},{4,7},{5,0},{6,1},{7,2},{8,11},{9,12},{10,... | collective-permute-start | bytes 589832 | tf_op jit(solution)/shard_map/ppermute | solution.py:702
  89.6 12.0 %collective-permute-start.10 = (bf16[2,192,256]{2,1,0:T(8,128)(2,1)}, bf16[2,192,256]{2,1,0:T(8,128)(2,1)S(1)}, u32[]{:S(2)}, u32[]{:S(2)}) collective-permute-start(bf16[2,192,256]{2,1,0:T(8,128)(2,1)} %get-tuple-element.67), channel_id=1, source_target_pairs={{0,4},{1,5},{2,6},{3,7},{4,0},{5,1},{6,2},{7,3},{8,12},{9,13},{10,... | collective-permute-start | bytes 589832 | tf_op jit(solution)/shard_map/ppermute | solution.py:702
  91.3 13.5 %collective-permute-start.11 = (bf16[2,192,256]{2,1,0:T(8,128)(2,1)}, bf16[2,192,256]{2,1,0:T(8,128)(2,1)S(1)}, u32[]{:S(2)}, u32[]{:S(2)}) collective-permute-start(bf16[2,192,256]{2,1,0:T(8,128)(2,1)} %get-tuple-element.68), channel_id=1, source_target_pairs={{0,5},{1,6},{2,7},{3,0},{4,1},{5,2},{6,3},{7,4},{8,13},{9,14},{10,... | collective-permute-start | bytes 589832 | tf_op jit(solution)/shard_map/ppermute | solution.py:702
  92.1 12.6 %collective-permute-start.12 = (bf16[2,192,256]{2,1,0:T(8,128)(2,1)}, bf16[2,192,256]{2,1,0:T(8,128)(2,1)S(1)}, u32[]{:S(2)}, u32[]{:S(2)}) collective-permute-start(bf16[2,192,256]{2,1,0:T(8,128)(2,1)} %get-tuple-element.69), channel_id=1, source_target_pairs={{0,6},{1,7},{2,0},{3,1},{4,2},{5,3},{6,4},{7,5},{8,14},{9,15},{10,... | collective-permute-start | bytes 589832 | tf_op jit(solution)/shard_map/ppermute | solution.py:702
  95.0 11.1 %collective-permute-start.13 = (bf16[2,192,256]{2,1,0:T(8,128)(2,1)}, bf16[2,192,256]{2,1,0:T(8,128)(2,1)S(1)}, u32[]{:S(2)}, u32[]{:S(2)}) collective-permute-start(bf16[2,192,256]{2,1,0:T(8,128)(2,1)} %get-tuple-element.70), channel_id=1, source_target_pairs={{0,7},{1,0},{2,1},{3,2},{4,3},{5,4},{6,5},{7,6},{8,15},{9,8},{10,9... | collective-permute-start | bytes 589832 | tf_op jit(solution)/shard_map/ppermute | solution.py:702
  118.0 42.1 %all-to-all-start.2 = ((bf16[4,2,2,192,256]{4,3,2,1,0:T(8,128)(2,1)}), bf16[4,2,2,192,256]{4,3,2,1,0:T(8,128)(2,1)}, u32[]{:S(2)}, u32[]{:S(2)}) async-start(bf16[4,2,2,192,256]{4,3,2,1,0:T(8,128)(2,1)} %bitcast.25), calls=%async_computation.2 | async-start | bytes 3145728 | tf_op jit(solution)/shard_map/all_to_all | solution.py:754
  124.4 28.3 %collective-permute-start.16 = (bf16[4,16,256]{2,1,0:T(8,128)(2,1)S(1)}, bf16[4,16,256]{2,1,0:T(8,128)(2,1)S(1)}, u32[]{:S(2)}, u32[]{:S(2)}) collective-permute-start(bf16[4,16,256]{2,1,0:T(8,128)(2,1)S(1)} %pad_maximum_fusion.2), channel_id=1, source_target_pairs={{0,1},{1,2},{2,3},{3,4},{4,5},{5,6},{6,7},{7,0},{8,9},{9,10},{10,1... | collective-permute-start | bytes 98312 | tf_op jit(solution)/shard_map/ppermute | solution.py:440
  124.5 28.2 %collective-permute-start.17 = (bf16[4,16,256]{2,1,0:T(8,128)(2,1)S(1)}, bf16[4,16,256]{2,1,0:T(8,128)(2,1)S(1)}, u32[]{:S(2)}, u32[]{:S(2)}) collective-permute-start(bf16[4,16,256]{2,1,0:T(8,128)(2,1)S(1)} %pad_maximum_fusion.3), channel_id=1, source_target_pairs={{1,0},{2,1},{3,2},{4,3},{5,4},{6,5},{7,6},{0,7},{9,8},{10,9},{11,1... | collective-permute-start | bytes 98312 | tf_op jit(solution)/shard_map/ppermute | solution.py:440
  127.2 21.1 %collective-permute-start.15 = (bf16[4,16,192]{2,1,0:T(8,128)(2,1)S(1)}, bf16[4,16,192]{2,1,0:T(8,128)(2,1)S(1)}, u32[]{:S(2)}, u32[]{:S(2)}) collective-permute-start(bf16[4,16,192]{2,1,0:T(8,128)(2,1)S(1)} %pad_maximum_fusion.1), channel_id=1, source_target_pairs={{8,0},{16,8},{24,16},{0,24},{9,1},{17,9},{25,17},{1,25},{10,2},{18... | collective-permute-start | bytes 73736 | tf_op jit(solution)/shard_map/ppermute | solution.py:440
  131.1 21.7 %collective-permute-start.14 = (bf16[4,16,192]{2,1,0:T(8,128)(2,1)S(1)}, bf16[4,16,192]{2,1,0:T(8,128)(2,1)S(1)}, u32[]{:S(2)}, u32[]{:S(2)}) collective-permute-start(bf16[4,16,192]{2,1,0:T(8,128)(2,1)S(1)} %pad_maximum_fusion), channel_id=1, source_target_pairs={{0,8},{8,16},{16,24},{24,0},{1,9},{9,17},{17,25},{25,1},{2,10},{10... | collective-permute-start | bytes 73736 | tf_op jit(solution)/shard_map/ppermute | solution.py:440
  160.1 45.3 %all-to-all-start.4 = ((bf16[4,2,2,192,256]{4,3,2,1,0:T(8,128)(2,1)}), bf16[4,2,2,192,256]{4,3,2,1,0:T(8,128)(2,1)}, u32[]{:S(2)}, u32[]{:S(2)}) async-start(bf16[4,2,2,192,256]{4,3,2,1,0:T(8,128)(2,1)} %copy-done.10), calls=%async_computation.4 | async-start | bytes 3145728 | tf_op jit(solution)/shard_map/all_to_all | solution.py:761
  205.4 40.9 %all-to-all-start.6 = ((bf16[4,2,2,192,256]{4,3,2,1,0:T(8,128)(2,1)}), bf16[4,2,2,192,256]{4,3,2,1,0:T(8,128)(2,1)}, u32[]{:S(2)}, u32[]{:S(2)}) async-start(bf16[4,2,2,192,256]{4,3,2,1,0:T(8,128)(2,1)} %copy-done.13), calls=%async_computation.6 | async-start | bytes 3145728 | tf_op jit(solution)/shard_map/all_to_all | solution.py:761
  217.9 10.1 %collective-permute-start.19 = (bf16[2,192,256]{2,1,0:T(8,128)(2,1)}, bf16[2,192,256]{2,1,0:T(8,128)(2,1)S(1)}, u32[]{:S(2)}, u32[]{:S(2)}) collective-permute-start(bf16[2,192,256]{2,1,0:T(8,128)(2,1)} %get-tuple-element.75), channel_id=1, source_target_pairs={{0,2},{1,3},{2,4},{3,5},{4,6},{5,7},{6,0},{7,1},{8,10},{9,11},{10,... | collective-permute-start | bytes 589832 | tf_op jit(solution)/shard_map/ppermute | solution.py:702
  221.5 13.0 %collective-permute-start.20 = (bf16[2,192,256]{2,1,0:T(8,128)(2,1)}, bf16[2,192,256]{2,1,0:T(8,128)(2,1)S(1)}, u32[]{:S(2)}, u32[]{:S(2)}) collective-permute-start(bf16[2,192,256]{2,1,0:T(8,128)(2,1)} %get-tuple-element.76), channel_id=1, source_target_pairs={{0,3},{1,4},{2,5},{3,6},{4,7},{5,0},{6,1},{7,2},{8,11},{9,12},{10,... | collective-permute-start | bytes 589832 | tf_op jit(solution)/shard_map/ppermute | solution.py:702
  222.6 12.0 %collective-permute-start.21 = (bf16[2,192,256]{2,1,0:T(8,128)(2,1)}, bf16[2,192,256]{2,1,0:T(8,128)(2,1)S(1)}, u32[]{:S(2)}, u32[]{:S(2)}) collective-permute-start(bf16[2,192,256]{2,1,0:T(8,128)(2,1)} %get-tuple-element.77), channel_id=1, source_target_pairs={{0,4},{1,5},{2,6},{3,7},{4,0},{5,1},{6,2},{7,3},{8,12},{9,13},{10,... | collective-permute-start | bytes 589832 | tf_op jit(solution)/shard_map/ppermute | solution.py:702
  224.4 13.4 %collective-permute-start.22 = (bf16[2,192,256]{2,1,0:T(8,128)(2,1)}, bf16[2,192,256]{2,1,0:T(8,128)(2,1)S(1)}, u32[]{:S(2)}, u32[]{:S(2)}) collective-permute-start(bf16[2,192,256]{2,1,0:T(8,128)(2,1)} %get-tuple-element.78), channel_id=1, source_target_pairs={{0,5},{1,6},{2,7},{3,0},{4,1},{5,2},{6,3},{7,4},{8,13},{9,14},{10,... | collective-permute-start | bytes 589832 | tf_op jit(solution)/shard_map/ppermute | solution.py:702
  225.2 12.6 %collective-permute-start.23 = (bf16[2,192,256]{2,1,0:T(8,128)(2,1)}, bf16[2,192,256]{2,1,0:T(8,128)(2,1)S(1)}, u32[]{:S(2)}, u32[]{:S(2)}) collective-permute-start(bf16[2,192,256]{2,1,0:T(8,128)(2,1)} %get-tuple-element.79), channel_id=1, source_target_pairs={{0,6},{1,7},{2,0},{3,1},{4,2},{5,3},{6,4},{7,5},{8,14},{9,15},{10,... | collective-permute-start | bytes 589832 | tf_op jit(solution)/shard_map/ppermute | solution.py:702
  228.0 11.1 %collective-permute-start.24 = (bf16[2,192,256]{2,1,0:T(8,128)(2,1)}, bf16[2,192,256]{2,1,0:T(8,128)(2,1)S(1)}, u32[]{:S(2)}, u32[]{:S(2)}) collective-permute-start(bf16[2,192,256]{2,1,0:T(8,128)(2,1)} %get-tuple-element.80), channel_id=1, source_target_pairs={{0,7},{1,0},{2,1},{3,2},{4,3},{5,4},{6,5},{7,6},{8,15},{9,8},{10,9... | collective-permute-start | bytes 589832 | tf_op jit(solution)/shard_map/ppermute | solution.py:702
  246.3 54.2 %all-to-all-start.5 = ((bf16[4,2,2,192,256]{4,3,2,1,0:T(8,128)(2,1)}), bf16[4,2,2,192,256]{4,3,2,1,0:T(8,128)(2,1)S(1)}, u32[]{:S(2)}, u32[]{:S(2)}) async-start(bf16[4,2,2,192,256]{4,3,2,1,0:T(8,128)(2,1)} %curl_inverse.5), calls=%async_computation.5 | async-start | bytes 3145728 | tf_op jit(solution)/shard_map/all_to_all | solution.py:761
  262.7 9.3 %collective-permute-start.26 = (bf16[2,192,256]{2,1,0:T(8,128)(2,1)}, bf16[2,192,256]{2,1,0:T(8,128)(2,1)S(1)}, u32[]{:S(2)}, u32[]{:S(2)}) collective-permute-start(bf16[2,192,256]{2,1,0:T(8,128)(2,1)} %get-tuple-element.84), channel_id=1, source_target_pairs={{0,2},{1,3},{2,4},{3,5},{4,6},{5,7},{6,0},{7,1},{8,10},{9,11},{10,... | collective-permute-start | bytes 589832 | tf_op jit(solution)/shard_map/ppermute | solution.py:702
  266.4 13.2 %collective-permute-start.27 = (bf16[2,192,256]{2,1,0:T(8,128)(2,1)}, bf16[2,192,256]{2,1,0:T(8,128)(2,1)S(1)}, u32[]{:S(2)}, u32[]{:S(2)}) collective-permute-start(bf16[2,192,256]{2,1,0:T(8,128)(2,1)} %get-tuple-element.85), channel_id=1, source_target_pairs={{0,3},{1,4},{2,5},{3,6},{4,7},{5,0},{6,1},{7,2},{8,11},{9,12},{10,... | collective-permute-start | bytes 589832 | tf_op jit(solution)/shard_map/ppermute | solution.py:702
  267.0 12.7 %collective-permute-start.28 = (bf16[2,192,256]{2,1,0:T(8,128)(2,1)}, bf16[2,192,256]{2,1,0:T(8,128)(2,1)S(1)}, u32[]{:S(2)}, u32[]{:S(2)}) collective-permute-start(bf16[2,192,256]{2,1,0:T(8,128)(2,1)} %get-tuple-element.86), channel_id=1, source_target_pairs={{0,4},{1,5},{2,6},{3,7},{4,0},{5,1},{6,2},{7,3},{8,12},{9,13},{10,... | collective-permute-start | bytes 589832 | tf_op jit(solution)/shard_map/ppermute | solution.py:702
  268.5 15.0 %collective-permute-start.29 = (bf16[2,192,256]{2,1,0:T(8,128)(2,1)}, bf16[2,192,256]{2,1,0:T(8,128)(2,1)S(1)}, u32[]{:S(2)}, u32[]{:S(2)}) collective-permute-start(bf16[2,192,256]{2,1,0:T(8,128)(2,1)} %get-tuple-element.87), channel_id=1, source_target_pairs={{0,5},{1,6},{2,7},{3,0},{4,1},{5,2},{6,3},{7,4},{8,13},{9,14},{10,... | collective-permute-start | bytes 589832 | tf_op jit(solution)/shard_map/ppermute | solution.py:702
  270.7 14.6 %collective-permute-start.30 = (bf16[2,192,256]{2,1,0:T(8,128)(2,1)}, bf16[2,192,256]{2,1,0:T(8,128)(2,1)S(1)}, u32[]{:S(2)}, u32[]{:S(2)}) collective-permute-start(bf16[2,192,256]{2,1,0:T(8,128)(2,1)} %get-tuple-element.88), channel_id=1, source_target_pairs={{0,6},{1,7},{2,0},{3,1},{4,2},{5,3},{6,4},{7,5},{8,14},{9,15},{10,... | collective-permute-start | bytes 589832 | tf_op jit(solution)/shard_map/ppermute | solution.py:702
  272.1 22.7 %collective-permute-start.31 = (bf16[2,192,256]{2,1,0:T(8,128)(2,1)}, bf16[2,192,256]{2,1,0:T(8,128)(2,1)S(1)}, u32[]{:S(2)}, u32[]{:S(2)}) collective-permute-start(bf16[2,192,256]{2,1,0:T(8,128)(2,1)} %get-tuple-element.89), channel_id=1, source_target_pairs={{0,7},{1,0},{2,1},{3,2},{4,3},{5,4},{6,5},{7,6},{8,15},{9,8},{10,9... | collective-permute-start | bytes 589832 | tf_op jit(solution)/shard_map/ppermute | solution.py:702
  279.6 20.9 %collective-permute-start.34 = (bf16[16,256]{1,0:T(8,128)(2,1)S(1)}, bf16[16,256]{1,0:T(8,128)(2,1)S(1)}, u32[]{:S(2)}, u32[]{:S(2)}) collective-permute-start(bf16[16,256]{1,0:T(8,128)(2,1)S(1)} %copy-done.67), channel_id=1, source_target_pairs={{0,1},{1,2},{2,3},{3,4},{4,5},{5,6},{6,7},{7,0},{8,9},{9,10},{10,1... | collective-permute-start | bytes 24584 | tf_op jit(solution)/shard_map/ppermute | solution.py:440
  279.8 20.7 %collective-permute-start.35 = (bf16[16,256]{1,0:T(8,128)(2,1)S(1)}, bf16[16,256]{1,0:T(8,128)(2,1)S(1)}, u32[]{:S(2)}, u32[]{:S(2)}) collective-permute-start(bf16[16,256]{1,0:T(8,128)(2,1)S(1)} %copy-done.66), channel_id=1, source_target_pairs={{1,0},{2,1},{3,2},{4,3},{5,4},{6,5},{7,6},{0,7},{9,8},{10,9},{11,1... | collective-permute-start | bytes 24584 | tf_op jit(solution)/shard_map/ppermute | solution.py:440
  283.5 16.9 %collective-permute-start.32 = (bf16[16,192]{1,0:T(8,128)(2,1)S(1)}, bf16[16,192]{1,0:T(8,128)(2,1)S(1)}, u32[]{:S(2)}, u32[]{:S(2)}) collective-permute-start(bf16[16,192]{1,0:T(8,128)(2,1)S(1)} %copy-done.69), channel_id=1, source_target_pairs={{0,8},{8,16},{16,24},{24,0},{1,9},{9,17},{17,25},{25,1},{2,10},{10... | collective-permute-start | bytes 18440 | tf_op jit(solution)/shard_map/ppermute | solution.py:440
  285.3 15.2 %collective-permute-start.33 = (bf16[16,192]{1,0:T(8,128)(2,1)S(1)}, bf16[16,192]{1,0:T(8,128)(2,1)S(1)}, u32[]{:S(2)}, u32[]{:S(2)}) collective-permute-start(bf16[16,192]{1,0:T(8,128)(2,1)S(1)} %copy-done.68), channel_id=1, source_target_pairs={{8,0},{16,8},{24,16},{0,24},{9,1},{17,9},{25,17},{1,25},{10,2},{18... | collective-permute-start | bytes 18440 | tf_op jit(solution)/shard_map/ppermute | solution.py:440
  309.3 28.2 %all-to-all-start.7 = ((bf16[8,2,192,256]{3,2,1,0:T(8,128)(2,1)}), bf16[8,2,192,256]{3,2,1,0:T(8,128)(2,1)S(1)}, u32[]{:S(2)}, u32[]{:S(2)}) async-start(bf16[8,2,192,256]{3,2,1,0:T(8,128)(2,1)} %y_inverse.5.refs_15_), calls=%async_computation.7 | async-start | bytes 3145728 | tf_op jit(solution)/shard_map/all_to_all | solution.py:772
  314.1 31.9 %collective-permute-start.38 = (bf16[16,256]{1,0:T(8,128)(2,1)S(1)}, bf16[16,256]{1,0:T(8,128)(2,1)S(1)}, u32[]{:S(2)}, u32[]{:S(2)}) collective-permute-start(bf16[16,256]{1,0:T(8,128)(2,1)S(1)} %copy-done.71), channel_id=1, source_target_pairs={{0,1},{1,2},{2,3},{3,4},{4,5},{5,6},{6,7},{7,0},{8,9},{9,10},{10,1... | collective-permute-start | bytes 24584 | tf_op jit(solution)/shard_map/ppermute | solution.py:440
  314.6 28.7 %collective-permute-start.36 = (bf16[16,192]{1,0:T(8,128)(2,1)S(1)}, bf16[16,192]{1,0:T(8,128)(2,1)S(1)}, u32[]{:S(2)}, u32[]{:S(2)}) collective-permute-start(bf16[16,192]{1,0:T(8,128)(2,1)S(1)} %copy-done.73), channel_id=1, source_target_pairs={{0,8},{8,16},{16,24},{24,0},{1,9},{9,17},{17,25},{25,1},{2,10},{10... | collective-permute-start | bytes 18440 | tf_op jit(solution)/shard_map/ppermute | solution.py:440
  314.7 31.3 %collective-permute-start.37 = (bf16[16,192]{1,0:T(8,128)(2,1)S(1)}, bf16[16,192]{1,0:T(8,128)(2,1)S(1)}, u32[]{:S(2)}, u32[]{:S(2)}) collective-permute-start(bf16[16,192]{1,0:T(8,128)(2,1)S(1)} %copy-done.72), channel_id=1, source_target_pairs={{8,0},{16,8},{24,16},{0,24},{9,1},{17,9},{25,17},{1,25},{10,2},{18... | collective-permute-start | bytes 18440 | tf_op jit(solution)/shard_map/ppermute | solution.py:440
  326.0 33.6 %collective-permute-start.39 = (bf16[16,256]{1,0:T(8,128)(2,1)S(1)}, bf16[16,256]{1,0:T(8,128)(2,1)S(1)}, u32[]{:S(2)}, u32[]{:S(2)}) collective-permute-start(bf16[16,256]{1,0:T(8,128)(2,1)S(1)} %copy-done.70), channel_id=1, source_target_pairs={{1,0},{2,1},{3,2},{4,3},{5,4},{6,5},{7,6},{0,7},{9,8},{10,9},{11,1... | collective-permute-start | bytes 24584 | tf_op jit(solution)/shard_map/ppermute | solution.py:440
  343.3 16.3 %collective-permute-start.42 = (bf16[16,256]{1,0:T(8,128)(2,1)}, bf16[16,256]{1,0:T(8,128)(2,1)S(1)}, u32[]{:S(2)}, u32[]{:S(2)}) collective-permute-start(bf16[16,256]{1,0:T(8,128)(2,1)} %get-tuple-element.102), channel_id=1, source_target_pairs={{0,1},{1,2},{2,3},{3,4},{4,5},{5,6},{6,7},{7,0},{8,9},{9,10},{10,1... | collective-permute-start | bytes 24584 | tf_op jit(solution)/shard_map/ppermute | solution.py:440
  343.4 16.3 %collective-permute-start.43 = (bf16[16,256]{1,0:T(8,128)(2,1)}, bf16[16,256]{1,0:T(8,128)(2,1)S(1)}, u32[]{:S(2)}, u32[]{:S(2)}) collective-permute-start(bf16[16,256]{1,0:T(8,128)(2,1)} %get-tuple-element.103), channel_id=1, source_target_pairs={{1,0},{2,1},{3,2},{4,3},{5,4},{6,5},{7,6},{0,7},{9,8},{10,9},{11,1... | collective-permute-start | bytes 24584 | tf_op jit(solution)/shard_map/ppermute | solution.py:440
  346.0 13.6 %collective-permute-start.40 = (bf16[16,192]{1,0:T(8,128)(2,1)}, bf16[16,192]{1,0:T(8,128)(2,1)S(1)}, u32[]{:S(2)}, u32[]{:S(2)}) collective-permute-start(bf16[16,192]{1,0:T(8,128)(2,1)} %get-tuple-element.100), channel_id=1, source_target_pairs={{0,8},{8,16},{16,24},{24,0},{1,9},{9,17},{17,25},{25,1},{2,10},{10... | collective-permute-start | bytes 18440 | tf_op jit(solution)/shard_map/ppermute | solution.py:440
  346.0 13.6 %collective-permute-start.41 = (bf16[16,192]{1,0:T(8,128)(2,1)}, bf16[16,192]{1,0:T(8,128)(2,1)S(1)}, u32[]{:S(2)}, u32[]{:S(2)}) collective-permute-start(bf16[16,192]{1,0:T(8,128)(2,1)} %get-tuple-element.101), channel_id=1, source_target_pairs={{8,0},{16,8},{24,16},{0,24},{9,1},{17,9},{25,17},{1,25},{10,2},{18... | collective-permute-start | bytes 18440 | tf_op jit(solution)/shard_map/ppermute | solution.py:440
  (78 other events, 692.0 us)

commit v8 on v7

--- a/solution.py
+++ b/solution.py
@@ -189,37 +189,52 @@
     planes, height, width = columns[0].shape[-3:]
     modes = HALF_Y // (blocks * halves)
     rows = Y // blocks
+    shape = (blocks, halves, planes, 2, modes, width)
 
     def kernel(me_ref, table_ref, *refs):
         parts = refs[: len(columns)]
-        out, held, arrived, lines = refs[-4:]
-        copies = fetch_blocks(table_ref, held, arrived, lambda s: s)
+        out, held, lines, ready, table_in, lines_in, ready_out = refs[-7:]
+        copies = []
         for s in range(size_y):
-            source = lax.rem(me_ref[0] + size_y - s, size_y)
+            source = s if whole else lax.rem(me_ref[0] + size_y - s, size_y)
+            place = pl.ds(pl.multiple_of(source * height, height), height)
             for plane in range(planes):
-                if whole:
-                    lines[plane, s * height : (s + 1) * height, :] = parts[0][s, plane]
-                else:
-                    place = pl.ds(pl.multiple_of(source * height, height), height)
-                    lines[plane, place, :] = parts[s][plane]
+                part = parts[0].at[s, plane] if whole else parts[s].at[plane]
+                copies.append(
+                    pltpu.make_async_copy(
+                        part, lines.at[plane, place], lines_in.at[s * planes + plane]
+                    )
+                )
+                copies[-1].start()
+        tables = fetch_blocks(table_ref, held, table_in, lambda s: s)
+        for copy in copies:
+            copy.wait()
+        results = []
         for s in range(blocks):
-            copies[s].wait()
+            tables[s].wait()
             for plane in range(planes):
                 part = jnp.dot(held[s], lines[plane], preferred_element_type=f32)
-                out[s, :, plane] = part.astype(bf16).reshape(halves, 2, modes, width)
-
-    vmem = pl.BlockSpec(memory_space=pltpu.VMEM)
+                ready[s, :, plane] = part.astype(bf16).reshape(halves, 2, modes, width)
+            results.append(pltpu.make_async_copy(ready.at[s], out.at[s], ready_out.at[s]))
+            results[s].start()
+        for result in results:
+            result.wait()
+
+    anywhere = pl.BlockSpec(memory_space=pl.ANY)
     return pl.pallas_call(
         kernel,
-        in_specs=[pl.BlockSpec(memory_space=pltpu.SMEM), pl.BlockSpec(memory_space=pl.ANY)]
-        + [vmem] * len(columns)
+        in_specs=[pl.BlockSpec(memory_space=pltpu.SMEM), anywhere]
+        + [anywhere] * len(columns)
         + tied(after),
-        out_specs=vmem,
-        out_shape=jax.ShapeDtypeStruct((blocks, halves, planes, 2, modes, width), bf16),
+        out_specs=anywhere,
+        out_shape=jax.ShapeDtypeStruct(shape, bf16),
         scratch_shapes=[
             pltpu.VMEM((blocks, rows, Y), bf16),
+            pltpu.VMEM((planes, Y, width), bf16),
+            pltpu.VMEM(shape, bf16),
             pltpu.SemaphoreType.DMA((blocks,)),
-            pltpu.VMEM((planes, Y, width), bf16),
+            pltpu.SemaphoreType.DMA((size_y * planes,)),
+            pltpu.SemaphoreType.DMA((blocks,)),
         ],
         compiler_params=params(),
         cost_estimate=takes(5),
@@ -228,42 +243,59 @@
 
 
 def y_inverse(me, table, modes, size_y, split, after):
-    planes, width = modes.shape[2], modes.shape[5]
+    blocks, halves, planes, _, count, width = modes.shape
     height = Y // size_y
     shape = (planes, height, width)
 
     def kernel(me_ref, table_ref, modes_ref, *refs):
-        outs, held, arrived = refs[len(after) : -2], refs[-2], refs[-1]
-        copies = fetch_blocks(
-            table_ref, held, arrived, lambda s: lax.rem(me_ref[0] + s, size_y) if split else s
-        )
-        lines = [modes_ref[:, :, plane].reshape(Y, width) for plane in range(planes)]
+        outs = refs[len(after) : -6]
+        held, lines, ready, table_in, lines_in, ready_out = refs[-6:]
+        copies = []
+        for block in range(blocks):
+            for h in range(halves):
+                for plane in range(planes):
+                    copies.append(
+                        pltpu.make_async_copy(
+                            modes_ref.at[block, h, plane],
+                            lines.at[plane, block, h],
+                            lines_in.at[(block * halves + h) * planes + plane],
+                        )
+                    )
+                    copies[-1].start()
+        tables = fetch_blocks(
+            table_ref, held, table_in, lambda s: lax.rem(me_ref[0] + s, size_y) if split else s
+        )
+        for copy in copies:
+            copy.wait()
+        results = []
         for s in range(size_y):
-            copies[s].wait()
+            tables[s].wait()
             for plane in range(planes):
-                rows = jnp.dot(held[s], lines[plane], preferred_element_type=f32).astype(bf16)
-                if split:
-                    outs[s][plane] = rows
-                else:
-                    outs[0][s, plane] = rows
-
-    vmem = pl.BlockSpec(memory_space=pltpu.VMEM)
+                columns = lines[plane].reshape(Y, width)
+                rows = jnp.dot(held[s], columns, preferred_element_type=f32)
+                ready[s, plane] = rows.astype(bf16)
+            out = outs[s] if split else outs[0].at[s]
+            results.append(pltpu.make_async_copy(ready.at[s], out, ready_out.at[s]))
+            results[s].start()
+        for result in results:
+            result.wait()
+
+    anywhere = pl.BlockSpec(memory_space=pl.ANY)
     if split:
         out_shape = [jax.ShapeDtypeStruct(shape, bf16)] * size_y
     else:
         out_shape = [jax.ShapeDtypeStruct((size_y,) + shape, bf16)]
     return pl.pallas_call(
         kernel,
-        in_specs=[
-            pl.BlockSpec(memory_space=pltpu.SMEM),
-            pl.BlockSpec(memory_space=pl.ANY),
-            vmem,
-        ]
-        + tied(after),
-        out_specs=[vmem] * len(out_shape),
+        in_specs=[pl.BlockSpec(memory_space=pltpu.SMEM), anywhere, anywhere] + tied(after),
+        out_specs=[anywhere] * len(out_shape),
         out_shape=out_shape,
         scratch_shapes=[
             pltpu.VMEM((size_y, height, Y), bf16),
+            pltpu.VMEM((planes, blocks, halves, 2, count, width), bf16),
+            pltpu.VMEM((size_y,) + shape, bf16),
+            pltpu.SemaphoreType.DMA((size_y,)),
+            pltpu.SemaphoreType.DMA((blocks * halves * planes,)),
             pltpu.SemaphoreType.DMA((size_y,)),
         ],
         compiler_params=params(),
@@ -441,7 +473,7 @@
 
 
 def adjoint_kernel(planes_ref, cotangent_ref, *refs):
-    adjoint_ref, first_x, last_x, first_y, last_y, held = refs
+    adjoint_ref, short_ref, first_x, last_x, first_y, last_y, held = refs
     _, height, width = held.shape
     scale = 1.0 / (X * Y * Z)
     base = pl.program_id(0) * ROWS
@@ -454,6 +486,7 @@
         for n in range(Z):
             value = cotangent_ref[0, n, rows, columns] + layers[n] * scale
             adjoint_ref[n, rows, columns] = value
+            short_ref[n, rows, columns] = value.astype(bf16)
             held[n, place, columns] = value.astype(bf16)
 
     @pl.when(pl.program_id(0) == pl.num_programs(0) - 1)
@@ -477,7 +510,7 @@
 
     def kernel(me_ref, *refs):
         part_refs, cotangent_ref = refs[: len(parts)], refs[len(parts)]
-        outs, held, spectrum = refs[-7:-2], refs[-2], refs[-1]
+        outs, held, spectrum = refs[-8:-2], refs[-2], refs[-1]
         if whole:
             spectrum = part_refs[0]
         else:
@@ -495,6 +528,7 @@
         + tied(after),
         out_specs=[
             pl.BlockSpec((Z, ROWS, width), lambda j: (0, j, 0)),
+            pl.BlockSpec((Z, ROWS, width), lambda j: (0, j, 0)),
             column_spec,
             column_spec,
             row_spec,
@@ -502,6 +536,7 @@
         ],
         out_shape=[
             jax.ShapeDtypeStruct((Z, height, width), f32),
+            jax.ShapeDtypeStruct((Z, height, width), bf16),
             column,
             column,
             row,
@@ -555,11 +590,11 @@
             if j == component:
                 term = term + value
             if before is not None:
-                term = before[j, k] + term
-            after[j, k] = term
-
-
-def add_grad_vort(component, slopes, velocity, adjoint, halos, before, after):
+                term = before[j, k].astype(f32) + term
+            after[j, k] = term.astype(after.dtype)
+
+
+def add_grad_vort(component, slopes, velocity, adjoint, halos, before, after, kind):
     _, _, height, width = velocity.shape
     slope_x, slope_y = slopes
     whole = lambda shape: pl.BlockSpec(shape, lambda n: (0,) * len(shape))
@@ -589,7 +624,7 @@
         grid=(Z // LAYERS,),
         in_specs=in_specs + tied(after),
         out_specs=sums,
-        out_shape=jax.ShapeDtypeStruct((3, Z, height, width), f32),
+        out_shape=jax.ShapeDtypeStruct((3, Z, height, width), kind),
         compiler_params=params(),
         cost_estimate=takes(9),
         name="add_grad_vort",
@@ -737,7 +772,7 @@
         "gy",
     )
     saved_halos = (low_x, high_x, low_y, high_y)
-    edges = (velocity_first, vorticity_first)
+    early = ((low_x, high_x), (low_y, high_y), ())
 
     columns = layers.reshape(size_y, planes, height, width)
     columns = [lax.all_to_all(columns, "gy", 0, 0, tiled=True)]
@@ -746,7 +781,7 @@
         if place > 0:
             layers = depth_transform(cot_vel, FORWARD_ORDER[place], me, size_y, (sent[-1],))
             columns = shifted(layers, "gy")
-        parts = y_transform(me, y_table, columns, size_x, halves, edges if place == 0 else ())
+        parts = y_transform(me, y_table, columns, size_x, halves, early[place])
         parts = parts.reshape(size_x, 2, 2, modes, width)
         sent.append(parts if halves == 1 else pair_exchange(parts, "gy", half))
 
@@ -774,7 +809,7 @@
 
     one, two, three = BACK_ORDER
     spectra = {FORWARD_ORDER[0]: spectrum(0, (sent[1],))}
-    spectra[FORWARD_ORDER[1]] = spectrum(1, (sent[2],) + saved_halos)
+    spectra[FORWARD_ORDER[1]] = spectrum(1, (sent[2],))
     curl_one = curl(one, ())
     spectra[FORWARD_ORDER[2]] = spectrum(2, (curl_one,))
     curl_two = curl(two, ())
@@ -783,14 +818,15 @@
     curl_three = curl(three, tuple(layers_one))
 
     def adjoint_of(component, parts, after):
-        adjoint, first_x, last_x, first_y, last_y = make_adjoint(
+        adjoint, short, first_x, last_x, first_y, last_y = make_adjoint(
             me, parts, cot_vort, component, after
         )
-        return adjoint, exchange(first_x, last_x, "gx") + exchange(first_y, last_y, "gy")
+        return adjoint, short, exchange(first_x, last_x, "gx") + exchange(first_y, last_y, "gy")
 
     def vort_of(component, adjoint, before, after):
+        kind = f32 if component == three else bf16
         return add_grad_vort(
-            component, (slope_x, slope_y), velocity, adjoint, saved_halos, before, after
+            component, (slope_x, slope_y), velocity, adjoint, saved_halos, before, after, kind
         )
 
     def vel_of(components, adjoints, halos, before, after):
@@ -798,17 +834,20 @@
             components, slope_x, vorticity, adjoints, saved_halos, halos, before, after
         )
 
-    adjoint_one, halos_one = adjoint_of(one, layers_one, ())
+    adjoint_one, short_one, halos_one = adjoint_of(one, layers_one, ())
     rows_two = rows_of(two, back(curl_two), (adjoint_one,))
-    grad_vort = vort_of(one, adjoint_one, None, (rows_two[0],))
-    adjoint_two, halos_two = adjoint_of(two, layers_of(rows_two), (grad_vort,))
-    rows_three = rows_of(three, back(curl_three), (adjoint_two,) + halos_one)
-    grad_vel = vel_of((one,), [adjoint_one], [halos_one], None, (rows_three[0],))
+    layers_two = layers_of(rows_two)
+    rows_three = rows_of(three, back(curl_three), tuple(layers_two) + halos_one)
+    grad_vort = vort_of(one, adjoint_one, None, (rows_three[0],))
+    adjoint_two, short_two, halos_two = adjoint_of(two, layers_two, (grad_vort,))
+    grad_vel = vel_of((one,), [short_one], [halos_one], None, (grad_vort,))
     grad_vort = vort_of(two, adjoint_two, grad_vort, (grad_vel,))
-    adjoint_three, halos_three = adjoint_of(three, layers_of(rows_three), (grad_vort,))
+    adjoint_three, short_three, halos_three = adjoint_of(
+        three, layers_of(rows_three), (grad_vort,)
+    )
     grad_vort = vort_of(three, adjoint_three, grad_vort, ())
     grad_vel = vel_of(
-        (two, three), [adjoint_two, adjoint_three], [halos_two, halos_three], grad_vel, (grad_vort,)
+        (two, three), [short_two, short_three], [halos_two, halos_three], grad_vel, (grad_vort,)
     )
     return grad_vort, grad_vel
 

time: 373 us -> 389 us (1.043)
  waiting for transfers between devices: 101 us -> 124 us
  Pallas kernels: 139 us -> 134 us
    all_to_all x3, waiting for transfers between devices: 8.14 us -> 30.1 us  [spectrum(): lines = lax.all_to_all(sent[place], 'gx', 0, 0, tiled=True)]
    ppermute x16, waiting for transfers between devices: 17.7 us -> 32.1 us  [exchange(): return (lax.ppermute(last, axis, up), lax.ppermute(first, axis, down))]
    all_to_all x1, waiting for transfers between devices: 13.9 us -> 2.92 us  [local(): columns = [lax.all_to_all(columns, 'gy', 0, 0, tiled=True)]]
    all_to_all x1, starting transfers between devices: 4.88 us -> 10.3 us  [layers_of(): lax.all_to_all(rows[0], 'gy', 0, 0, tiled=True).reshape(Z, height, width)]
    all_to_all x3, starting transfers between devices: 18 us -> 13.2 us  [back(): parts = lax.all_to_all(filtered, 'gx', 0, 0, tiled=True)]
    pallas_call x3, Pallas kernels: 26.8 us -> 22.8 us  [add_grad_vort(): pl.pallas_call(kernel, grid=(Z // LAYERS,), in_specs=in_specs + tied(afte...]
    unnamed x152 -> x140, local copies, waits for them, and re-layouts: 18 us -> 16.8 us
  transfers between devices with their start and end apart: 52 -> 52, of which waited for: 27 -> 28; matrix products, arithmetic and copies ran while one was open for 1% -> 1% of each run, Pallas kernels for 30% -> 27%
where the time goes in v8:
time: 389 us; the launch traced here: 388 us
  Pallas kernels  134 us (34%)
  waiting for transfers between devices  124 us (32%)
  starting transfers between devices  108 us (28%)
  local copies, waits for them, and re-layouts  18.8 us (5%)
    ppermute x28, starting transfers between devices, shifted(): lax.ppermute(parts[s], axis, [(i, (i + s) % count) for i in range(count)])  41.9 us
    ppermute x28, waiting for transfers between devices, shifted(): lax.ppermute(parts[s], axis, [(i, (i + s) % count) for i in range(count)])  32.9 us
    ppermute x16, waiting for transfers between devices, exchange(): return (lax.ppermute(last, axis, up), lax.ppermute(first, axis, down))  32.1 us
    all_to_all x3, waiting for transfers between devices, spectrum(): lines = lax.all_to_all(sent[place], 'gx', 0, 0, tiled=True)  30.1 us
    all_to_all x3, waiting for transfers between devices, back(): parts = lax.all_to_all(filtered, 'gx', 0, 0, tiled=True)  25.6 us
    ppermute x16, starting transfers between devices, exchange(): return (lax.ppermute(last, axis, up), lax.ppermute(first, axis, down))  23.4 us
    pallas_call x3, Pallas kernels, add_grad_vort(): pl.pallas_call(kernel, grid=(Z // LAYERS,), in_specs=in_specs + tied(afte...  22.8 us
    pallas_call x3, Pallas kernels, y_inverse(): pl.pallas_call(kernel, in_specs=[pl.BlockSpec(memory_space=pltpu.SMEM), a...  22 us
  transfers between devices with their start and end apart: 52, of which 28 were waited for; matrix products, arithmetic and copies ran while one was open for 1% of the time, Pallas kernels for 27%

profile of v8, /device:TPU:0, one launch (start us, length us, event | category | flops | bytes accessed | tf_op | source)
XLA Modules:
  0.0 387.7 jit_solution(10788332907647496182)
XLA Ops:
  0.6 3.2 depth_transform.3.refs_0_
  3.8 5.2 %all-to-all-start = ((bf16[8,2,192,256]{3,2,1,0:T(8,128)(2,1)}), bf16[8,2,192,256]{3,2,1,0:T(8,128)(2,1)S(1)}, u32[]{:S(2)}, u32[]{:S(2)}) async-start(bf16[8,2,192,256]{3,2,1,0:T(8,128)(2,1)} %bitcast.27), calls=%async_computation | async-start | bytes 3145728 | tf_op jit(solution)/shard_map/all_to_all | solution.py:778
  11.6 4.6 %edge_columns.2 = (bf16[3,16,192]{2,1,0:T(8,128)(2,1)}, bf16[3,16,192]{2,1,0:T(8,128)(2,1)}) custom-call(bf16[3,16,192,256]{3,2,1,0:T(8,128)(2,1)} %refs_2_.8, bf16[16,192,256]{2,1,0:T(8,128)(2,1)} %depth_transform.3.refs_0_), custom_call_target="tpu_custom_call" | custom-call | flops 1 | bytes 12000000 | tf_op jit(solution)/shard_map/edge_columns/pallas_call | solution.py:456
  16.9 3.7 collective-permute-start.1
  22.2 4.9 %collective-permute-done.refs_1_.refs_4_.refs_7_.refs_10_ = bf16[4,16,192]{2,1,0:T(8,128)(2,1)S(1)} collective-permute-done((bf16[4,16,192]{2,1,0:T(8,128)(2,1)S(1)}, bf16[4,16,192]{2,1,0:T(8,128)(2,1)S(1)}, u32[]{:S(2)}, u32[]{:S(2)}) %collective-permute-start) | collective-permute-done | bytes 24608 | tf_op jit(solution)/shard_map/ppermute | solution.py:472
  31.1 6.6 %y_transform.3 = bf16[4,1,2,2,192,256]{5,4,3,2,1,0:T(8,128)(2,1)} custom-call(s32[1]{0:T(128)} %bitcast.me_ref.refs_0_, bf16[1536,1536]{1,0:T(8,128)(2,1)} %constant.33.clone.table_ref, bf16[8,2,192,256]{3,2,1,0:T(8,128)(2,1)} %copy-done.24, bf16[4,16,192]{2,1,0:T(8,128)(2,1)} %copy-done.26, bf16[4,16,192]{2,1,0:T(8,128)(2,1)} %copy-done.25), custom_call_target="tpu_custom_call" | custom-call | flops 1 | bytes 15000000 | tf_op jit(solution)/shard_map/y_transform/pallas_call | solution.py:224
  37.7 4.9 %all-to-all-start.1 = ((bf16[4,2,2,192,256]{4,3,2,1,0:T(8,128)(2,1)}), bf16[4,2,2,192,256]{4,3,2,1,0:T(8,128)(2,1)S(1)}, u32[]{:S(2)}, u32[]{:S(2)}) async-start(bf16[4,2,2,192,256]{4,3,2,1,0:T(8,128)(2,1)} %bitcast.28), calls=%async_computation.1 | async-start | bytes 3145728 | tf_op jit(solution)/shard_map/all_to_all | solution.py:789
  44.6 3.3 depth_transform.4
  51.3 9.4 %collective-permute-done.9.refs_8_.refs_6_.refs_9_.refs_12_ = bf16[4,16,256]{2,1,0:T(8,128)(2,1)S(1)} collective-permute-done((bf16[4,16,256]{2,1,0:T(8,128)(2,1)S(1)}, bf16[4,16,256]{2,1,0:T(8,128)(2,1)S(1)}, u32[]{:S(2)}, u32[]{:S(2)}) %collective-permute-start.9) | collective-permute-done | bytes 32800 | tf_op jit(solution)/shard_map/ppermute | solution.py:472
  64.0 3.2 collective-permute-done.5.refs_4_
  71.7 6.6 %y_transform.4 = bf16[4,1,2,2,192,256]{5,4,3,2,1,0:T(8,128)(2,1)} custom-call(s32[1]{0:T(128)} %bitcast.me_ref.refs_0_, bf16[1536,1536]{1,0:T(8,128)(2,1)} %constant.33.clone.table_ref, bf16[2,192,256]{2,1,0:T(8,128)(2,1)} %get-tuple-element.60.refs_0_, bf16[2,192,256]{2,1,0:T(8,128)(2,1)} %copy-done.36, bf16[2,192,256]{2,1,0:T(8,128)(2,1)} %copy-done.37, ...), custom_call_target="tpu_custom_call" | custom-call | flops 1 | bytes 15000000 | tf_op jit(solution)/shard_map/y_transform/pallas_call | solution.py:224
  78.3 5.1 %all-to-all-start.3 = ((bf16[4,2,2,192,256]{4,3,2,1,0:T(8,128)(2,1)}), bf16[4,2,2,192,256]{4,3,2,1,0:T(8,128)(2,1)}, u32[]{:S(2)}, u32[]{:S(2)}) async-start(bf16[4,2,2,192,256]{4,3,2,1,0:T(8,128)(2,1)} %bitcast.22), calls=%async_computation.3 | async-start | bytes 3145728 | tf_op jit(solution)/shard_map/all_to_all | solution.py:789
  83.4 3.3 depth_transform.5
  88.4 4.2 %collective-permute-start.12 = (bf16[2,192,256]{2,1,0:T(8,128)(2,1)}, bf16[2,192,256]{2,1,0:T(8,128)(2,1)S(1)}, u32[]{:S(2)}, u32[]{:S(2)}) collective-permute-start(bf16[2,192,256]{2,1,0:T(8,128)(2,1)} %get-tuple-element.70), channel_id=1, source_target_pairs={{0,2},{1,3},{2,4},{3,5},{4,6},{5,7},{6,0},{7,1},{8,10},{9,11},{10,... | collective-permute-start | bytes 589832 | tf_op jit(solution)/shard_map/ppermute | solution.py:737
  101.7 5.3 %collective-permute-done.13.refs_3_ = bf16[2,192,256]{2,1,0:T(8,128)(2,1)S(1)} collective-permute-done((bf16[2,192,256]{2,1,0:T(8,128)(2,1)}, bf16[2,192,256]{2,1,0:T(8,128)(2,1)S(1)}, u32[]{:S(2)}, u32[]{:S(2)}) %collective-permute-start.13) | collective-permute-done | bytes 196640 | tf_op jit(solution)/shard_map/ppermute | solution.py:737
  110.4 6.6 %y_transform.5 = bf16[4,1,2,2,192,256]{5,4,3,2,1,0:T(8,128)(2,1)} custom-call(s32[1]{0:T(128)} %bitcast.me_ref.refs_0_, bf16[1536,1536]{1,0:T(8,128)(2,1)} %constant.33.clone.table_ref, bf16[2,192,256]{2,1,0:T(8,128)(2,1)} %get-tuple-element.68.refs_0_, bf16[2,192,256]{2,1,0:T(8,128)(2,1)} %copy-done.39, bf16[2,192,256]{2,1,0:T(8,128)(2,1)} %copy-done.40, ...), custom_call_target="tpu_custom_call" | custom-call | flops 1 | bytes 15000000 | tf_op jit(solution)/shard_map/y_transform/pallas_call | solution.py:224
  117.0 4.1 %all-to-all-done.3.modes_ref = bf16[4,2,2,192,256]{4,3,2,1,0:T(8,128)(2,1)} async-done(((bf16[4,2,2,192,256]{4,3,2,1,0:T(8,128)(2,1)}), bf16[4,2,2,192,256]{4,3,2,1,0:T(8,128)(2,1)}, u32[]{:S(2)}, u32[]{:S(2)}) %all-to-all-start.3) | async-done | bytes 1572896 | tf_op jit(solution)/shard_map/all_to_all | solution.py:789
  121.1 4.5 %all-to-all-start.2 = ((bf16[4,2,2,192,256]{4,3,2,1,0:T(8,128)(2,1)}), bf16[4,2,2,192,256]{4,3,2,1,0:T(8,128)(2,1)}, u32[]{:S(2)}, u32[]{:S(2)}) async-start(bf16[4,2,2,192,256]{4,3,2,1,0:T(8,128)(2,1)} %bitcast.25), calls=%async_computation.2 | async-start | bytes 3145728 | tf_op jit(solution)/shard_map/all_to_all | solution.py:789
  129.5 3.9 x_transform.4.refs_2_.refs_3_
  133.4 3.0 curl_inverse.3.refs_0_
  137.5 26.0 %all-to-all-done.2.modes_ref = bf16[4,2,2,192,256]{4,3,2,1,0:T(8,128)(2,1)} async-done(((bf16[4,2,2,192,256]{4,3,2,1,0:T(8,128)(2,1)}), bf16[4,2,2,192,256]{4,3,2,1,0:T(8,128)(2,1)}, u32[]{:S(2)}, u32[]{:S(2)}) %all-to-all-start.2) | async-done | bytes 1572896 | tf_op jit(solution)/shard_map/all_to_all | solution.py:789
  163.5 4.4 %all-to-all-start.4 = ((bf16[4,2,2,192,256]{4,3,2,1,0:T(8,128)(2,1)}), bf16[4,2,2,192,256]{4,3,2,1,0:T(8,128)(2,1)}, u32[]{:S(2)}, u32[]{:S(2)}) async-start(bf16[4,2,2,192,256]{4,3,2,1,0:T(8,128)(2,1)} %copy-done.10), calls=%async_computation.4 | async-start | bytes 3145728 | tf_op jit(solution)/shard_map/all_to_all | solution.py:796
  170.9 3.3 x_transform.5.refs_2_.refs_3_
  174.2 3.0 curl_inverse.4.refs_0_
  180.0 25.1 %all-to-all-done.4 = bf16[4,2,2,192,256]{4,3,2,1,0:T(8,128)(2,1)} async-done(((bf16[4,2,2,192,256]{4,3,2,1,0:T(8,128)(2,1)}), bf16[4,2,2,192,256]{4,3,2,1,0:T(8,128)(2,1)}, u32[]{:S(2)}, u32[]{:S(2)}) %all-to-all-start.4) | async-done | bytes 1572896 | tf_op jit(solution)/shard_map/all_to_all | solution.py:796
  205.1 4.3 %all-to-all-start.6 = ((bf16[4,2,2,192,256]{4,3,2,1,0:T(8,128)(2,1)}), bf16[4,2,2,192,256]{4,3,2,1,0:T(8,128)(2,1)}, u32[]{:S(2)}, u32[]{:S(2)}) async-start(bf16[4,2,2,192,256]{4,3,2,1,0:T(8,128)(2,1)} %copy-done.12), calls=%async_computation.6 | async-start | bytes 3145728 | tf_op jit(solution)/shard_map/all_to_all | solution.py:796
  209.5 7.4 %y_inverse.3 = (bf16[2,192,256]{2,1,0:T(8,128)(2,1)}, bf16[2,192,256]{2,1,0:T(8,128)(2,1)}, bf16[2,192,256]{2,1,0:T(8,128)(2,1)}, bf16[2,192,256]{2,1,0:T(8,128)...) custom-call(s32[1]{0:T(128)} %bitcast.me_ref.refs_0_, ...), custom_call_target="tpu_custom_call" | custom-call | flops 1 | bytes 12000000 | tf_op jit(solution)/shard_map/y_inverse/pallas_call | solution.py:288
  216.9 4.4 %collective-permute-start.19 = (bf16[2,192,256]{2,1,0:T(8,128)(2,1)}, bf16[2,192,256]{2,1,0:T(8,128)(2,1)S(1)}, u32[]{:S(2)}, u32[]{:S(2)}) collective-permute-start(bf16[2,192,256]{2,1,0:T(8,128)(2,1)} %get-tuple-element.78), channel_id=1, source_target_pairs={{0,2},{1,3},{2,4},{3,5},{4,6},{5,7},{6,0},{7,1},{8,10},{9,11},{10,... | collective-permute-start | bytes 589832 | tf_op jit(solution)/shard_map/ppermute | solution.py:737
  224.4 4.3 %collective-permute-start.23 = (bf16[2,192,256]{2,1,0:T(8,128)(2,1)}, bf16[2,192,256]{2,1,0:T(8,128)(2,1)S(1)}, u32[]{:S(2)}, u32[]{:S(2)}) collective-permute-start(bf16[2,192,256]{2,1,0:T(8,128)(2,1)} %get-tuple-element.82), channel_id=1, source_target_pairs={{0,6},{1,7},{2,0},{3,1},{4,2},{5,3},{6,4},{7,5},{8,14},{9,15},{10,... | collective-permute-start | bytes 589832 | tf_op jit(solution)/shard_map/ppermute | solution.py:737
  228.7 4.0 %collective-permute-start.24 = (bf16[2,192,256]{2,1,0:T(8,128)(2,1)}, bf16[2,192,256]{2,1,0:T(8,128)(2,1)S(1)}, u32[]{:S(2)}, u32[]{:S(2)}) collective-permute-start(bf16[2,192,256]{2,1,0:T(8,128)(2,1)} %get-tuple-element.83), channel_id=1, source_target_pairs={{0,7},{1,0},{2,1},{3,2},{4,3},{5,4},{6,5},{7,6},{8,15},{9,8},{10,9... | collective-permute-start | bytes 589832 | tf_op jit(solution)/shard_map/ppermute | solution.py:737
  241.6 3.8 curl_inverse.5
  246.0 4.5 %all-to-all-start.5 = ((bf16[4,2,2,192,256]{4,3,2,1,0:T(8,128)(2,1)}), bf16[4,2,2,192,256]{4,3,2,1,0:T(8,128)(2,1)S(1)}, u32[]{:S(2)}, u32[]{:S(2)}) async-start(bf16[4,2,2,192,256]{4,3,2,1,0:T(8,128)(2,1)} %curl_inverse.5), calls=%async_computation.5 | async-start | bytes 3145728 | tf_op jit(solution)/shard_map/all_to_all | solution.py:796
  250.5 5.3 %make_adjoint.3 = (f32[16,192,256]{2,1,0:T(8,128)}, bf16[16,192,256]{2,1,0:T(8,128)(2,1)}, bf16[16,192]{1,0:T(8,128)(2,1)}, bf16[16,192]{1,0:T(8,128)(2,1)}, bf1...) custom-call(s32[1]{0:T(128)} %bitcast.me_ref.refs_0_, bf16[2,192,256]{2,1,0:T(8,128)(2,1)} %get-tuple-element.76.refs_4_.refs_0_, ...), custom_call_target="tpu_custom_call" | custom-call | flops 1 | bytes 15000000 | tf_op jit(solution)/shard_map/make_adjoint/pallas_call | solution.py:522
  255.8 7.3 %y_inverse.4 = (bf16[2,192,256]{2,1,0:T(8,128)(2,1)}, bf16[2,192,256]{2,1,0:T(8,128)(2,1)}, bf16[2,192,256]{2,1,0:T(8,128)(2,1)}, bf16[2,192,256]{2,1,0:T(8,128)...) custom-call(s32[1]{0:T(128)} %bitcast.me_ref.refs_0_, ...), custom_call_target="tpu_custom_call" | custom-call | flops 1 | bytes 12000000 | tf_op jit(solution)/shard_map/y_inverse/pallas_call | solution.py:288
  263.1 3.7 collective-permute-start.26
  271.2 9.1 %collective-permute-done.32.refs_8_.refs_11_ = bf16[16,192]{1,0:T(8,128)(2,1)S(1)} collective-permute-done((bf16[16,192]{1,0:T(8,128)(2,1)S(1)}, bf16[16,192]{1,0:T(8,128)(2,1)S(1)}, u32[]{:S(2)}, u32[]{:S(2)}) %collective-permute-start.32) | collective-permute-done | bytes 6176 | tf_op jit(solution)/shard_map/ppermute | solution.py:472
  280.3 7.8 %collective-permute-done.33.refs_9_.refs_12_ = bf16[16,192]{1,0:T(8,128)(2,1)S(1)} collective-permute-done((bf16[16,192]{1,0:T(8,128)(2,1)S(1)}, bf16[16,192]{1,0:T(8,128)(2,1)S(1)}, u32[]{:S(2)}, u32[]{:S(2)}) %collective-permute-start.33) | collective-permute-done | bytes 6176 | tf_op jit(solution)/shard_map/ppermute | solution.py:472
  288.2 3.1 collective-permute-start.27
  295.8 4.0 %collective-permute-done.28.refs_4_ = bf16[2,192,256]{2,1,0:T(8,128)(2,1)S(1)} collective-permute-done((bf16[2,192,256]{2,1,0:T(8,128)(2,1)}, bf16[2,192,256]{2,1,0:T(8,128)(2,1)S(1)}, u32[]{:S(2)}, u32[]{:S(2)}) %collective-permute-start.28) | collective-permute-done | bytes 196640 | tf_op jit(solution)/shard_map/ppermute | solution.py:737
  304.5 7.4 %y_inverse.5.refs_8_ = bf16[8,2,192,256]{3,2,1,0:T(8,128)(2,1)} custom-call(s32[1]{0:T(128)} %bitcast.me_ref.refs_0_, bf16[1536,1536]{1,0:T(8,128)(2,1)} %constant.36.clone.table_ref, bf16[4,1,2,2,192,256]{5,4,3,2,1,0:T(8,128)(2,1)} %bitcast.30, bf16[2,192,256]{2,1,0:T(8,128)(2,1)} %get-tuple-element.85.refs_0_, bf16[2,192,256]{2,1,0:T(8,128)(2,1)} %copy-done.29, ...), custom_call_target="tpu_custom_call" | custom-call | flops 1 | bytes 12000000 | tf_op jit(solution)/shard_map/y_inverse/pallas_call | solution.py:288
  311.9 10.3 %all-to-all-start.7 = ((bf16[8,2,192,256]{3,2,1,0:T(8,128)(2,1)}), bf16[8,2,192,256]{3,2,1,0:T(8,128)(2,1)S(1)}, u32[]{:S(2)}, u32[]{:S(2)}) async-start(bf16[8,2,192,256]{3,2,1,0:T(8,128)(2,1)} %y_inverse.5.refs_8_), calls=%async_computation.7 | async-start | bytes 3145728 | tf_op jit(solution)/shard_map/all_to_all | solution.py:807
  322.2 6.2 %add_grad_vort.3.refs_9_.refs_15_.refs_8_ = bf16[3,16,192,256]{3,2,1,0:T(8,128)(2,1)} custom-call(bf16[256,256]{1,0:T(8,128)(2,1)} %constant.37.clone.refs_0_, bf16[192,192]{1,0:T(8,128)(2,1)} %constant.38.clone.refs_1_, bf16[3,16,192,256]{3,2,1,0:T(8,128)(2,1)} %refs_2_.8, f32[16,192,256]{2,1,0:T(8,128)} %get-tuple-element.84.refs_0_.refs_3_, ...), custom_call_target="tpu_custom_call" | custom-call | flops 1 | bytes 27000000 | tf_op jit(solution)/shard_map/add_grad_vort/pallas_call | solution.py:622
  328.4 5.3 %make_adjoint.4 = (f32[16,192,256]{2,1,0:T(8,128)}, bf16[16,192,256]{2,1,0:T(8,128)(2,1)}, bf16[16,192]{1,0:T(8,128)(2,1)}, bf16[16,192]{1,0:T(8,128)(2,1)}, bf1...) custom-call(s32[1]{0:T(128)} %bitcast.me_ref.refs_0_, bf16[2,192,256]{2,1,0:T(8,128)(2,1)} %get-tuple-element.85.refs_0_, ...), custom_call_target="tpu_custom_call" | custom-call | flops 1 | bytes 15000000 | tf_op jit(solution)/shard_map/make_adjoint/pallas_call | solution.py:522
  339.8 7.1 %write_grad_vel.2.refs_9_.refs_22_ = f32[3,16,192,256]{3,2,1,0:T(8,128)} custom-call(bf16[256,256]{1,0:T(8,128)(2,1)} %constant.37.clone.refs_0_, bf16[3,16,192,256]{3,2,1,0:T(8,128)(2,1)} %refs_3_.3, bf16[3,16,192,256]{3,2,1,0:T(8,128)(2,1)} %refs_3_.3, bf16[3,16,192,256]{3,2,1,0:T(8,128)(2,1)} %refs_3_.3, ...), custom_call_target="tpu_custom_call" | custom-call | flops 1 | bytes 18000000 | tf_op jit(solution)/shard_map/write_grad_vel/pallas_call | solution.py:712
  346.9 7.8 %add_grad_vort.4.refs_2_.refs_8_ = bf16[3,16,192,256]{3,2,1,0:T(8,128)(2,1)} custom-call(bf16[256,256]{1,0:T(8,128)(2,1)} %constant.37.clone.refs_0_, bf16[192,192]{1,0:T(8,128)(2,1)} %constant.38.clone.refs_1_, bf16[3,16,192,256]{3,2,1,0:T(8,128)(2,1)} %refs_2_.8, f32[16,192,256]{2,1,0:T(8,128)} %get-tuple-element.97.refs_3_, ...), custom_call_target="tpu_custom_call" | custom-call | flops 1 | bytes 27000000 | tf_op jit(solution)/shard_map/add_grad_vort/pallas_call | solution.py:622
  355.8 5.2 %make_adjoint.5 = (f32[16,192,256]{2,1,0:T(8,128)}, bf16[16,192,256]{2,1,0:T(8,128)(2,1)}, bf16[16,192]{1,0:T(8,128)(2,1)}, bf16[16,192]{1,0:T(8,128)(2,1)}, bf1...) custom-call(s32[1]{0:T(128)} %bitcast.me_ref.refs_0_, bf16[16,192,256]{2,1,0:T(8,128)(2,1)} %bitcast.31, ...), custom_call_target="tpu_custom_call" | custom-call | flops 1 | bytes 15000000 | tf_op jit(solution)/shard_map/make_adjoint/pallas_call | solution.py:522
  367.6 8.8 %add_grad_vort.5.refs_23_ = f32[3,16,192,256]{3,2,1,0:T(8,128)} custom-call(bf16[256,256]{1,0:T(8,128)(2,1)} %constant.37.clone.refs_0_, bf16[192,192]{1,0:T(8,128)(2,1)} %constant.38.clone.refs_1_, bf16[3,16,192,256]{3,2,1,0:T(8,128)(2,1)} %refs_2_.8, f32[16,192,256]{2,1,0:T(8,128)} %get-tuple-element.99.refs_3_, bf16[4,16,192]{2,1,0:T(8,128)(2,1)} %copy-done.26, ...), custom_call_target="tpu_custom_call" | custom-call | flops 1 | bytes 27000000 | tf_op jit(solution)/shard_map/add_grad_vort/pallas_call | solution.py:622
  377.1 10.5 %write_grad_vel.3 = f32[3,16,192,256]{3,2,1,0:T(8,128)} custom-call(bf16[256,256]{1,0:T(8,128)(2,1)} %constant.37.clone.refs_0_, bf16[3,16,192,256]{3,2,1,0:T(8,128)(2,1)} %refs_3_.3, bf16[3,16,192,256]{3,2,1,0:T(8,128)(2,1)} %refs_3_.3, bf16[3,16,192,256]{3,2,1,0:T(8,128)(2,1)} %refs_3_.3, ...), custom_call_target="tpu_custom_call", output_to_operand_aliasing={{}: (22, {})} | custom-call | flops 1 | bytes 36000000 | tf_op jit(solution)/shard_map/write_grad_vel/pallas_call | solution.py:712
  (228 shorter events, 87.4 us)
Async XLA Ops:
  3.8 26.2 %all-to-all-start = ((bf16[8,2,192,256]{3,2,1,0:T(8,128)(2,1)}), bf16[8,2,192,256]{3,2,1,0:T(8,128)(2,1)S(1)}, u32[]{:S(2)}, u32[]{:S(2)}) async-start(bf16[8,2,192,256]{3,2,1,0:T(8,128)(2,1)} %bitcast.27), calls=%async_computation | async-start | bytes 3145728 | tf_op jit(solution)/shard_map/all_to_all | solution.py:778
  37.7 40.5 %all-to-all-start.1 = ((bf16[4,2,2,192,256]{4,3,2,1,0:T(8,128)(2,1)}), bf16[4,2,2,192,256]{4,3,2,1,0:T(8,128)(2,1)S(1)}, u32[]{:S(2)}, u32[]{:S(2)}) async-start(bf16[4,2,2,192,256]{4,3,2,1,0:T(8,128)(2,1)} %bitcast.28), calls=%async_computation.1 | async-start | bytes 3145728 | tf_op jit(solution)/shard_map/all_to_all | solution.py:789
  47.9 13.3 %collective-permute-start.2 = (bf16[2,192,256]{2,1,0:T(8,128)(2,1)}, bf16[2,192,256]{2,1,0:T(8,128)(2,1)S(1)}, u32[]{:S(2)}, u32[]{:S(2)}) collective-permute-start(bf16[2,192,256]{2,1,0:T(8,128)(2,1)} %get-tuple-element.61), channel_id=1, source_target_pairs={{0,1},{1,2},{2,3},{3,4},{4,5},{5,6},{6,7},{7,0},{8,9},{9,10},{10,1... | collective-permute-start | bytes 589832 | tf_op jit(solution)/shard_map/ppermute | solution.py:737
  48.0 13.8 %collective-permute-start.3 = (bf16[2,192,256]{2,1,0:T(8,128)(2,1)}, bf16[2,192,256]{2,1,0:T(8,128)(2,1)S(1)}, u32[]{:S(2)}, u32[]{:S(2)}) collective-permute-start(bf16[2,192,256]{2,1,0:T(8,128)(2,1)} %get-tuple-element.62), channel_id=1, source_target_pairs={{0,2},{1,3},{2,4},{3,5},{4,6},{5,7},{6,0},{7,1},{8,10},{9,11},{10,... | collective-permute-start | bytes 589832 | tf_op jit(solution)/shard_map/ppermute | solution.py:737
  48.5 12.1 %collective-permute-start.9 = (bf16[4,16,256]{2,1,0:T(8,128)(2,1)S(1)}, bf16[4,16,256]{2,1,0:T(8,128)(2,1)S(1)}, u32[]{:S(2)}, u32[]{:S(2)}) collective-permute-start(bf16[4,16,256]{2,1,0:T(8,128)(2,1)S(1)} %pad_maximum_fusion.2), channel_id=1, source_target_pairs={{0,1},{1,2},{2,3},{3,4},{4,5},{5,6},{6,7},{7,0},{8,9},{9,10},{10,1... | collective-permute-start | bytes 98312 | tf_op jit(solution)/shard_map/ppermute | solution.py:472
  49.8 11.4 %collective-permute-start.10 = (bf16[4,16,256]{2,1,0:T(8,128)(2,1)S(1)}, bf16[4,16,256]{2,1,0:T(8,128)(2,1)S(1)}, u32[]{:S(2)}, u32[]{:S(2)}) collective-permute-start(bf16[4,16,256]{2,1,0:T(8,128)(2,1)S(1)} %pad_maximum_fusion.3), channel_id=1, source_target_pairs={{1,0},{2,1},{3,2},{4,3},{5,4},{6,5},{7,6},{0,7},{9,8},{10,9},{11,1... | collective-permute-start | bytes 98312 | tf_op jit(solution)/shard_map/ppermute | solution.py:472
  51.3 12.7 %collective-permute-start.4 = (bf16[2,192,256]{2,1,0:T(8,128)(2,1)}, bf16[2,192,256]{2,1,0:T(8,128)(2,1)S(1)}, u32[]{:S(2)}, u32[]{:S(2)}) collective-permute-start(bf16[2,192,256]{2,1,0:T(8,128)(2,1)} %get-tuple-element.63), channel_id=1, source_target_pairs={{0,3},{1,4},{2,5},{3,6},{4,7},{5,0},{6,1},{7,2},{8,11},{9,12},{10,... | collective-permute-start | bytes 589832 | tf_op jit(solution)/shard_map/ppermute | solution.py:737
  61.3 8.0 %collective-permute-start.7 = (bf16[2,192,256]{2,1,0:T(8,128)(2,1)}, bf16[2,192,256]{2,1,0:T(8,128)(2,1)S(1)}, u32[]{:S(2)}, u32[]{:S(2)}) collective-permute-start(bf16[2,192,256]{2,1,0:T(8,128)(2,1)} %get-tuple-element.66), channel_id=1, source_target_pairs={{0,6},{1,7},{2,0},{3,1},{4,2},{5,3},{6,4},{7,5},{8,14},{9,15},{10,... | collective-permute-start | bytes 589832 | tf_op jit(solution)/shard_map/ppermute | solution.py:737
  61.8 9.2 %collective-permute-start.8 = (bf16[2,192,256]{2,1,0:T(8,128)(2,1)}, bf16[2,192,256]{2,1,0:T(8,128)(2,1)S(1)}, u32[]{:S(2)}, u32[]{:S(2)}) collective-permute-start(bf16[2,192,256]{2,1,0:T(8,128)(2,1)} %get-tuple-element.67), channel_id=1, source_target_pairs={{0,7},{1,0},{2,1},{3,2},{4,3},{5,4},{6,5},{7,6},{8,15},{9,8},{10,9... | collective-permute-start | bytes 589832 | tf_op jit(solution)/shard_map/ppermute | solution.py:737
  78.3 42.9 %all-to-all-start.3 = ((bf16[4,2,2,192,256]{4,3,2,1,0:T(8,128)(2,1)}), bf16[4,2,2,192,256]{4,3,2,1,0:T(8,128)(2,1)}, u32[]{:S(2)}, u32[]{:S(2)}) async-start(bf16[4,2,2,192,256]{4,3,2,1,0:T(8,128)(2,1)} %bitcast.22), calls=%async_computation.3 | async-start | bytes 3145728 | tf_op jit(solution)/shard_map/all_to_all | solution.py:789
  86.6 11.5 %collective-permute-start.11 = (bf16[2,192,256]{2,1,0:T(8,128)(2,1)}, bf16[2,192,256]{2,1,0:T(8,128)(2,1)S(1)}, u32[]{:S(2)}, u32[]{:S(2)}) collective-permute-start(bf16[2,192,256]{2,1,0:T(8,128)(2,1)} %get-tuple-element.69), channel_id=1, source_target_pairs={{0,1},{1,2},{2,3},{3,4},{4,5},{5,6},{6,7},{7,0},{8,9},{9,10},{10,1... | collective-permute-start | bytes 589832 | tf_op jit(solution)/shard_map/ppermute | solution.py:737
  88.4 11.0 %collective-permute-start.12 = (bf16[2,192,256]{2,1,0:T(8,128)(2,1)}, bf16[2,192,256]{2,1,0:T(8,128)(2,1)S(1)}, u32[]{:S(2)}, u32[]{:S(2)}) collective-permute-start(bf16[2,192,256]{2,1,0:T(8,128)(2,1)} %get-tuple-element.70), channel_id=1, source_target_pairs={{0,2},{1,3},{2,4},{3,5},{4,6},{5,7},{6,0},{7,1},{8,10},{9,11},{10,... | collective-permute-start | bytes 589832 | tf_op jit(solution)/shard_map/ppermute | solution.py:737
  92.6 14.4 %collective-permute-start.13 = (bf16[2,192,256]{2,1,0:T(8,128)(2,1)}, bf16[2,192,256]{2,1,0:T(8,128)(2,1)S(1)}, u32[]{:S(2)}, u32[]{:S(2)}) collective-permute-start(bf16[2,192,256]{2,1,0:T(8,128)(2,1)} %get-tuple-element.71), channel_id=1, source_target_pairs={{0,3},{1,4},{2,5},{3,6},{4,7},{5,0},{6,1},{7,2},{8,11},{9,12},{10,... | collective-permute-start | bytes 589832 | tf_op jit(solution)/shard_map/ppermute | solution.py:737
  93.3 13.9 %collective-permute-start.14 = (bf16[2,192,256]{2,1,0:T(8,128)(2,1)}, bf16[2,192,256]{2,1,0:T(8,128)(2,1)S(1)}, u32[]{:S(2)}, u32[]{:S(2)}) collective-permute-start(bf16[2,192,256]{2,1,0:T(8,128)(2,1)} %get-tuple-element.72), channel_id=1, source_target_pairs={{0,4},{1,5},{2,6},{3,7},{4,0},{5,1},{6,2},{7,3},{8,12},{9,13},{10,... | collective-permute-start | bytes 589832 | tf_op jit(solution)/shard_map/ppermute | solution.py:737
  94.8 14.8 %collective-permute-start.15 = (bf16[2,192,256]{2,1,0:T(8,128)(2,1)}, bf16[2,192,256]{2,1,0:T(8,128)(2,1)S(1)}, u32[]{:S(2)}, u32[]{:S(2)}) collective-permute-start(bf16[2,192,256]{2,1,0:T(8,128)(2,1)} %get-tuple-element.73), channel_id=1, source_target_pairs={{0,5},{1,6},{2,7},{3,0},{4,1},{5,2},{6,3},{7,4},{8,13},{9,14},{10,... | collective-permute-start | bytes 589832 | tf_op jit(solution)/shard_map/ppermute | solution.py:737
  98.1 11.5 %collective-permute-start.16 = (bf16[2,192,256]{2,1,0:T(8,128)(2,1)}, bf16[2,192,256]{2,1,0:T(8,128)(2,1)S(1)}, u32[]{:S(2)}, u32[]{:S(2)}) collective-permute-start(bf16[2,192,256]{2,1,0:T(8,128)(2,1)} %get-tuple-element.74), channel_id=1, source_target_pairs={{0,6},{1,7},{2,0},{3,1},{4,2},{5,3},{6,4},{7,5},{8,14},{9,15},{10,... | collective-permute-start | bytes 589832 | tf_op jit(solution)/shard_map/ppermute | solution.py:737
  99.4 10.2 %collective-permute-start.17 = (bf16[2,192,256]{2,1,0:T(8,128)(2,1)}, bf16[2,192,256]{2,1,0:T(8,128)(2,1)S(1)}, u32[]{:S(2)}, u32[]{:S(2)}) collective-permute-start(bf16[2,192,256]{2,1,0:T(8,128)(2,1)} %get-tuple-element.75), channel_id=1, source_target_pairs={{0,7},{1,0},{2,1},{3,2},{4,3},{5,4},{6,5},{7,6},{8,15},{9,8},{10,9... | collective-permute-start | bytes 589832 | tf_op jit(solution)/shard_map/ppermute | solution.py:737
  121.1 42.4 %all-to-all-start.2 = ((bf16[4,2,2,192,256]{4,3,2,1,0:T(8,128)(2,1)}), bf16[4,2,2,192,256]{4,3,2,1,0:T(8,128)(2,1)}, u32[]{:S(2)}, u32[]{:S(2)}) async-start(bf16[4,2,2,192,256]{4,3,2,1,0:T(8,128)(2,1)} %bitcast.25), calls=%async_computation.2 | async-start | bytes 3145728 | tf_op jit(solution)/shard_map/all_to_all | solution.py:789
  163.5 41.6 %all-to-all-start.4 = ((bf16[4,2,2,192,256]{4,3,2,1,0:T(8,128)(2,1)}), bf16[4,2,2,192,256]{4,3,2,1,0:T(8,128)(2,1)}, u32[]{:S(2)}, u32[]{:S(2)}) async-start(bf16[4,2,2,192,256]{4,3,2,1,0:T(8,128)(2,1)} %copy-done.10), calls=%async_computation.4 | async-start | bytes 3145728 | tf_op jit(solution)/shard_map/all_to_all | solution.py:796
  205.1 40.9 %all-to-all-start.6 = ((bf16[4,2,2,192,256]{4,3,2,1,0:T(8,128)(2,1)}), bf16[4,2,2,192,256]{4,3,2,1,0:T(8,128)(2,1)}, u32[]{:S(2)}, u32[]{:S(2)}) async-start(bf16[4,2,2,192,256]{4,3,2,1,0:T(8,128)(2,1)} %copy-done.12), calls=%async_computation.6 | async-start | bytes 3145728 | tf_op jit(solution)/shard_map/all_to_all | solution.py:796
  216.9 7.6 %collective-permute-start.18 = (bf16[2,192,256]{2,1,0:T(8,128)(2,1)}, bf16[2,192,256]{2,1,0:T(8,128)(2,1)S(1)}, u32[]{:S(2)}, u32[]{:S(2)}) collective-permute-start(bf16[2,192,256]{2,1,0:T(8,128)(2,1)} %get-tuple-element.77), channel_id=1, source_target_pairs={{0,1},{1,2},{2,3},{3,4},{4,5},{5,6},{6,7},{7,0},{8,9},{9,10},{10,1... | collective-permute-start | bytes 589832 | tf_op jit(solution)/shard_map/ppermute | solution.py:737
  216.9 11.8 %collective-permute-start.19 = (bf16[2,192,256]{2,1,0:T(8,128)(2,1)}, bf16[2,192,256]{2,1,0:T(8,128)(2,1)S(1)}, u32[]{:S(2)}, u32[]{:S(2)}) collective-permute-start(bf16[2,192,256]{2,1,0:T(8,128)(2,1)} %get-tuple-element.78), channel_id=1, source_target_pairs={{0,2},{1,3},{2,4},{3,5},{4,6},{5,7},{6,0},{7,1},{8,10},{9,11},{10,... | collective-permute-start | bytes 589832 | tf_op jit(solution)/shard_map/ppermute | solution.py:737
  221.4 13.2 %collective-permute-start.20 = (bf16[2,192,256]{2,1,0:T(8,128)(2,1)}, bf16[2,192,256]{2,1,0:T(8,128)(2,1)S(1)}, u32[]{:S(2)}, u32[]{:S(2)}) collective-permute-start(bf16[2,192,256]{2,1,0:T(8,128)(2,1)} %get-tuple-element.79), channel_id=1, source_target_pairs={{0,3},{1,4},{2,5},{3,6},{4,7},{5,0},{6,1},{7,2},{8,11},{9,12},{10,... | collective-permute-start | bytes 589832 | tf_op jit(solution)/shard_map/ppermute | solution.py:737
  223.4 11.4 %collective-permute-start.21 = (bf16[2,192,256]{2,1,0:T(8,128)(2,1)}, bf16[2,192,256]{2,1,0:T(8,128)(2,1)S(1)}, u32[]{:S(2)}, u32[]{:S(2)}) collective-permute-start(bf16[2,192,256]{2,1,0:T(8,128)(2,1)} %get-tuple-element.80), channel_id=1, source_target_pairs={{0,4},{1,5},{2,6},{3,7},{4,0},{5,1},{6,2},{7,3},{8,12},{9,13},{10,... | collective-permute-start | bytes 589832 | tf_op jit(solution)/shard_map/ppermute | solution.py:737
  224.2 13.1 %collective-permute-start.22 = (bf16[2,192,256]{2,1,0:T(8,128)(2,1)}, bf16[2,192,256]{2,1,0:T(8,128)(2,1)S(1)}, u32[]{:S(2)}, u32[]{:S(2)}) collective-permute-start(bf16[2,192,256]{2,1,0:T(8,128)(2,1)} %get-tuple-element.81), channel_id=1, source_target_pairs={{0,5},{1,6},{2,7},{3,0},{4,1},{5,2},{6,3},{7,4},{8,13},{9,14},{10,... | collective-permute-start | bytes 589832 | tf_op jit(solution)/shard_map/ppermute | solution.py:737
  224.4 12.9 %collective-permute-start.23 = (bf16[2,192,256]{2,1,0:T(8,128)(2,1)}, bf16[2,192,256]{2,1,0:T(8,128)(2,1)S(1)}, u32[]{:S(2)}, u32[]{:S(2)}) collective-permute-start(bf16[2,192,256]{2,1,0:T(8,128)(2,1)} %get-tuple-element.82), channel_id=1, source_target_pairs={{0,6},{1,7},{2,0},{3,1},{4,2},{5,3},{6,4},{7,5},{8,14},{9,15},{10,... | collective-permute-start | bytes 589832 | tf_op jit(solution)/shard_map/ppermute | solution.py:737
  228.7 10.3 %collective-permute-start.24 = (bf16[2,192,256]{2,1,0:T(8,128)(2,1)}, bf16[2,192,256]{2,1,0:T(8,128)(2,1)S(1)}, u32[]{:S(2)}, u32[]{:S(2)}) collective-permute-start(bf16[2,192,256]{2,1,0:T(8,128)(2,1)} %get-tuple-element.83), channel_id=1, source_target_pairs={{0,7},{1,0},{2,1},{3,2},{4,3},{5,4},{6,5},{7,6},{8,15},{9,8},{10,9... | collective-permute-start | bytes 589832 | tf_op jit(solution)/shard_map/ppermute | solution.py:737
  246.0 57.3 %all-to-all-start.5 = ((bf16[4,2,2,192,256]{4,3,2,1,0:T(8,128)(2,1)}), bf16[4,2,2,192,256]{4,3,2,1,0:T(8,128)(2,1)S(1)}, u32[]{:S(2)}, u32[]{:S(2)}) async-start(bf16[4,2,2,192,256]{4,3,2,1,0:T(8,128)(2,1)} %curl_inverse.5), calls=%async_computation.5 | async-start | bytes 3145728 | tf_op jit(solution)/shard_map/all_to_all | solution.py:796
  263.0 29.5 %collective-permute-start.25 = (bf16[2,192,256]{2,1,0:T(8,128)(2,1)}, bf16[2,192,256]{2,1,0:T(8,128)(2,1)S(1)}, u32[]{:S(2)}, u32[]{:S(2)}) collective-permute-start(bf16[2,192,256]{2,1,0:T(8,128)(2,1)} %get-tuple-element.86), channel_id=1, source_target_pairs={{0,1},{1,2},{2,3},{3,4},{4,5},{5,6},{6,7},{7,0},{8,9},{9,10},{10,1... | collective-permute-start | bytes 589832 | tf_op jit(solution)/shard_map/ppermute | solution.py:737
  263.1 32.0 %collective-permute-start.26 = (bf16[2,192,256]{2,1,0:T(8,128)(2,1)}, bf16[2,192,256]{2,1,0:T(8,128)(2,1)S(1)}, u32[]{:S(2)}, u32[]{:S(2)}) collective-permute-start(bf16[2,192,256]{2,1,0:T(8,128)(2,1)} %get-tuple-element.87), channel_id=1, source_target_pairs={{0,2},{1,3},{2,4},{3,5},{4,6},{5,7},{6,0},{7,1},{8,10},{9,11},{10,... | collective-permute-start | bytes 589832 | tf_op jit(solution)/shard_map/ppermute | solution.py:737
  266.8 13.5 %collective-permute-start.32 = (bf16[16,192]{1,0:T(8,128)(2,1)S(1)}, bf16[16,192]{1,0:T(8,128)(2,1)S(1)}, u32[]{:S(2)}, u32[]{:S(2)}) collective-permute-start(bf16[16,192]{1,0:T(8,128)(2,1)S(1)} %copy-done.67), channel_id=1, source_target_pairs={{0,8},{8,16},{16,24},{24,0},{1,9},{9,17},{17,25},{25,1},{2,10},{10... | collective-permute-start | bytes 18440 | tf_op jit(solution)/shard_map/ppermute | solution.py:472
  268.6 22.7 %collective-permute-start.34 = (bf16[16,256]{1,0:T(8,128)(2,1)S(1)}, bf16[16,256]{1,0:T(8,128)(2,1)S(1)}, u32[]{:S(2)}, u32[]{:S(2)}) collective-permute-start(bf16[16,256]{1,0:T(8,128)(2,1)S(1)} %copy-done.65), channel_id=1, source_target_pairs={{0,1},{1,2},{2,3},{3,4},{4,5},{5,6},{6,7},{7,0},{8,9},{9,10},{10,1... | collective-permute-start | bytes 24584 | tf_op jit(solution)/shard_map/ppermute | solution.py:472
  268.6 23.9 %collective-permute-start.35 = (bf16[16,256]{1,0:T(8,128)(2,1)S(1)}, bf16[16,256]{1,0:T(8,128)(2,1)S(1)}, u32[]{:S(2)}, u32[]{:S(2)}) collective-permute-start(bf16[16,256]{1,0:T(8,128)(2,1)S(1)} %copy-done.64), channel_id=1, source_target_pairs={{1,0},{2,1},{3,2},{4,3},{5,4},{6,5},{7,6},{0,7},{9,8},{10,9},{11,1... | collective-permute-start | bytes 24584 | tf_op jit(solution)/shard_map/ppermute | solution.py:472
  280.3 7.9 %collective-permute-start.33 = (bf16[16,192]{1,0:T(8,128)(2,1)S(1)}, bf16[16,192]{1,0:T(8,128)(2,1)S(1)}, u32[]{:S(2)}, u32[]{:S(2)}) collective-permute-start(bf16[16,192]{1,0:T(8,128)(2,1)S(1)} %copy-done.66), channel_id=1, source_target_pairs={{8,0},{16,8},{24,16},{0,24},{9,1},{17,9},{25,17},{1,25},{10,2},{18... | collective-permute-start | bytes 18440 | tf_op jit(solution)/shard_map/ppermute | solution.py:472
  288.2 7.6 %collective-permute-start.27 = (bf16[2,192,256]{2,1,0:T(8,128)(2,1)}, bf16[2,192,256]{2,1,0:T(8,128)(2,1)S(1)}, u32[]{:S(2)}, u32[]{:S(2)}) collective-permute-start(bf16[2,192,256]{2,1,0:T(8,128)(2,1)} %get-tuple-element.88), channel_id=1, source_target_pairs={{0,3},{1,4},{2,5},{3,6},{4,7},{5,0},{6,1},{7,2},{8,11},{9,12},{10,... | collective-permute-start | bytes 589832 | tf_op jit(solution)/shard_map/ppermute | solution.py:737
  291.3 8.5 %collective-permute-start.28 = (bf16[2,192,256]{2,1,0:T(8,128)(2,1)}, bf16[2,192,256]{2,1,0:T(8,128)(2,1)S(1)}, u32[]{:S(2)}, u32[]{:S(2)}) collective-permute-start(bf16[2,192,256]{2,1,0:T(8,128)(2,1)} %get-tuple-element.89), channel_id=1, source_target_pairs={{0,4},{1,5},{2,6},{3,7},{4,0},{5,1},{6,2},{7,3},{8,12},{9,13},{10,... | collective-permute-start | bytes 589832 | tf_op jit(solution)/shard_map/ppermute | solution.py:737
  292.5 7.9 %collective-permute-start.29 = (bf16[2,192,256]{2,1,0:T(8,128)(2,1)}, bf16[2,192,256]{2,1,0:T(8,128)(2,1)S(1)}, u32[]{:S(2)}, u32[]{:S(2)}) collective-permute-start(bf16[2,192,256]{2,1,0:T(8,128)(2,1)} %get-tuple-element.90), channel_id=1, source_target_pairs={{0,5},{1,6},{2,7},{3,0},{4,1},{5,2},{6,3},{7,4},{8,13},{9,14},{10,... | collective-permute-start | bytes 589832 | tf_op jit(solution)/shard_map/ppermute | solution.py:737
  292.5 8.2 %collective-permute-start.30 = (bf16[2,192,256]{2,1,0:T(8,128)(2,1)}, bf16[2,192,256]{2,1,0:T(8,128)(2,1)S(1)}, u32[]{:S(2)}, u32[]{:S(2)}) collective-permute-start(bf16[2,192,256]{2,1,0:T(8,128)(2,1)} %get-tuple-element.91), channel_id=1, source_target_pairs={{0,6},{1,7},{2,0},{3,1},{4,2},{5,3},{6,4},{7,5},{8,14},{9,15},{10,... | collective-permute-start | bytes 589832 | tf_op jit(solution)/shard_map/ppermute | solution.py:737
  295.1 8.2 %collective-permute-start.31 = (bf16[2,192,256]{2,1,0:T(8,128)(2,1)}, bf16[2,192,256]{2,1,0:T(8,128)(2,1)S(1)}, u32[]{:S(2)}, u32[]{:S(2)}) collective-permute-start(bf16[2,192,256]{2,1,0:T(8,128)(2,1)} %get-tuple-element.92), channel_id=1, source_target_pairs={{0,7},{1,0},{2,1},{3,2},{4,3},{5,4},{6,5},{7,6},{8,15},{9,8},{10,9... | collective-permute-start | bytes 589832 | tf_op jit(solution)/shard_map/ppermute | solution.py:737
  311.9 42.8 %all-to-all-start.7 = ((bf16[8,2,192,256]{3,2,1,0:T(8,128)(2,1)}), bf16[8,2,192,256]{3,2,1,0:T(8,128)(2,1)S(1)}, u32[]{:S(2)}, u32[]{:S(2)}) async-start(bf16[8,2,192,256]{3,2,1,0:T(8,128)(2,1)} %y_inverse.5.refs_8_), calls=%async_computation.7 | async-start | bytes 3145728 | tf_op jit(solution)/shard_map/all_to_all | solution.py:807
  333.7 31.0 %collective-permute-start.38 = (bf16[16,256]{1,0:T(8,128)(2,1)}, bf16[16,256]{1,0:T(8,128)(2,1)S(1)}, u32[]{:S(2)}, u32[]{:S(2)}) collective-permute-start(bf16[16,256]{1,0:T(8,128)(2,1)} %get-tuple-element.104), channel_id=1, source_target_pairs={{0,1},{1,2},{2,3},{3,4},{4,5},{5,6},{6,7},{7,0},{8,9},{9,10},{10,1... | collective-permute-start | bytes 24584 | tf_op jit(solution)/shard_map/ppermute | solution.py:472
  334.2 26.9 %collective-permute-start.36 = (bf16[16,192]{1,0:T(8,128)(2,1)}, bf16[16,192]{1,0:T(8,128)(2,1)S(1)}, u32[]{:S(2)}, u32[]{:S(2)}) collective-permute-start(bf16[16,192]{1,0:T(8,128)(2,1)} %get-tuple-element.102), channel_id=1, source_target_pairs={{0,8},{8,16},{16,24},{24,0},{1,9},{9,17},{17,25},{25,1},{2,10},{10... | collective-permute-start | bytes 18440 | tf_op jit(solution)/shard_map/ppermute | solution.py:472
  336.7 27.1 %collective-permute-start.37 = (bf16[16,192]{1,0:T(8,128)(2,1)}, bf16[16,192]{1,0:T(8,128)(2,1)S(1)}, u32[]{:S(2)}, u32[]{:S(2)}) collective-permute-start(bf16[16,192]{1,0:T(8,128)(2,1)} %get-tuple-element.103), channel_id=1, source_target_pairs={{8,0},{16,8},{24,16},{0,24},{9,1},{17,9},{25,17},{1,25},{10,2},{18... | collective-permute-start | bytes 18440 | tf_op jit(solution)/shard_map/ppermute | solution.py:472
  338.1 38.3 %collective-permute-start.39 = (bf16[16,256]{1,0:T(8,128)(2,1)}, bf16[16,256]{1,0:T(8,128)(2,1)S(1)}, u32[]{:S(2)}, u32[]{:S(2)}) collective-permute-start(bf16[16,256]{1,0:T(8,128)(2,1)} %get-tuple-element.105), channel_id=1, source_target_pairs={{1,0},{2,1},{3,2},{4,3},{5,4},{6,5},{7,6},{0,7},{9,8},{10,9},{11,1... | collective-permute-start | bytes 24584 | tf_op jit(solution)/shard_map/ppermute | solution.py:472
  361.1 15.4 %collective-permute-start.42 = (bf16[16,256]{1,0:T(8,128)(2,1)}, bf16[16,256]{1,0:T(8,128)(2,1)S(1)}, u32[]{:S(2)}, u32[]{:S(2)}) collective-permute-start(bf16[16,256]{1,0:T(8,128)(2,1)} %get-tuple-element.108), channel_id=1, source_target_pairs={{0,1},{1,2},{2,3},{3,4},{4,5},{5,6},{6,7},{7,0},{8,9},{9,10},{10,1... | collective-permute-start | bytes 24584 | tf_op jit(solution)/shard_map/ppermute | solution.py:472
  361.2 15.3 %collective-permute-start.43 = (bf16[16,256]{1,0:T(8,128)(2,1)}, bf16[16,256]{1,0:T(8,128)(2,1)S(1)}, u32[]{:S(2)}, u32[]{:S(2)}) collective-permute-start(bf16[16,256]{1,0:T(8,128)(2,1)} %get-tuple-element.109), channel_id=1, source_target_pairs={{1,0},{2,1},{3,2},{4,3},{5,4},{6,5},{7,6},{0,7},{9,8},{10,9},{11,1... | collective-permute-start | bytes 24584 | tf_op jit(solution)/shard_map/ppermute | solution.py:472
  363.8 12.6 %collective-permute-start.40 = (bf16[16,192]{1,0:T(8,128)(2,1)}, bf16[16,192]{1,0:T(8,128)(2,1)S(1)}, u32[]{:S(2)}, u32[]{:S(2)}) collective-permute-start(bf16[16,192]{1,0:T(8,128)(2,1)} %get-tuple-element.106), channel_id=1, source_target_pairs={{0,8},{8,16},{16,24},{24,0},{1,9},{9,17},{17,25},{25,1},{2,10},{10... | collective-permute-start | bytes 18440 | tf_op jit(solution)/shard_map/ppermute | solution.py:472
  364.7 11.7 %collective-permute-start.41 = (bf16[16,192]{1,0:T(8,128)(2,1)}, bf16[16,192]{1,0:T(8,128)(2,1)S(1)}, u32[]{:S(2)}, u32[]{:S(2)}) collective-permute-start(bf16[16,192]{1,0:T(8,128)(2,1)} %get-tuple-element.107), channel_id=1, source_target_pairs={{8,0},{16,8},{24,16},{0,24},{9,1},{17,9},{25,17},{1,25},{10,2},{18... | collective-permute-start | bytes 18440 | tf_op jit(solution)/shard_map/ppermute | solution.py:472
  (72 other events, 512.0 us)

commit v9 on v8

--- a/solution.py
+++ b/solution.py
@@ -492,21 +492,22 @@
     @pl.when(pl.program_id(0) == pl.num_programs(0) - 1)
     def _():
         first, last = side_columns([held[n] for n in range(Z)])
-        first_x[...] = first
-        last_x[...] = last
+        first_x[0] = first
+        last_x[0] = last
         top = [held[n, 0:16, :].astype(f32)[0:1] for n in range(Z)]
         bottom = [held[n, height - 16 : height, :].astype(f32)[15:16] for n in range(Z)]
-        first_y[...] = jnp.concatenate(top, 0).astype(bf16)
-        last_y[...] = jnp.concatenate(bottom, 0).astype(bf16)
-
-
-def make_adjoint(me, parts, cotangent, component, after):
+        first_y[0] = jnp.concatenate(top, 0).astype(bf16)
+        last_y[0] = jnp.concatenate(bottom, 0).astype(bf16)
+
+
+def make_adjoint(me, parts, cotangent, component, edges, after):
     whole = len(parts) == 1
     planes, height, width = parts[0].shape
-    column = jax.ShapeDtypeStruct((Z, height), bf16)
-    row = jax.ShapeDtypeStruct((Z, width), bf16)
-    column_spec = pl.BlockSpec((Z, height), lambda j: (0, 0))
-    row_spec = pl.BlockSpec((Z, width), lambda j: (0, 0))
+    column = jax.ShapeDtypeStruct((3, Z, height), bf16)
+    row = jax.ShapeDtypeStruct((3, Z, width), bf16)
+    column_spec = pl.BlockSpec((1, Z, height), lambda j: (component, 0, 0))
+    row_spec = pl.BlockSpec((1, Z, width), lambda j: (component, 0, 0))
+    first_edge = 2 + len(parts)
 
     def kernel(me_ref, *refs):
         part_refs, cotangent_ref = refs[: len(parts)], refs[len(parts)]
@@ -525,6 +526,7 @@
         in_specs=[pl.BlockSpec(memory_space=pltpu.SMEM)]
         + [pl.BlockSpec((planes, ROWS, width), lambda j: (0, j, 0))] * len(parts)
         + [pl.BlockSpec((1, Z, ROWS, width), lambda j: (component, 0, j, 0))]
+        + tied(edges)
         + tied(after),
         out_specs=[
             pl.BlockSpec((Z, ROWS, width), lambda j: (0, j, 0)),
@@ -542,6 +544,7 @@
             row,
             row,
         ],
+        input_output_aliases={first_edge + n: 2 + n for n in range(len(edges))},
         scratch_shapes=[
             pltpu.VMEM((Z, height, width), bf16),
             pltpu.VMEM((Z, ROWS, width), bf16),
@@ -549,7 +552,7 @@
         compiler_params=params(),
         cost_estimate=takes(5),
         name="make_adjoint",
-    )(me, *parts, cotangent, *after)
+    )(me, *parts, cotangent, *edges, *after)
 
 
 def pick_row(rows, n):
@@ -562,7 +565,7 @@
     return jnp.where(row == 0, low * -0.5, 0.0) + jnp.where(row == height - 1, high * 0.5, 0.0)
 
 
-LAYERS = 4
+LAYERS = 2
 
 
 def grad_vort_kernel(
@@ -632,8 +635,8 @@
 
 
 def grad_vel_kernel(count, slope_x, vorticity, vorticity_above, vorticity_below, *refs):
-    adjoints, saved, halos = refs[: 3 * count], refs[3 * count :], refs[3 * count + 4 :]
-    vort_low_x, vort_high_x, vort_low_y, vort_high_y = saved[:4]
+    adjoints, edges = refs[: 3 * count], refs[3 * count :]
+    vort_low_x, vort_high_x, vort_low_y, vort_high_y, low_x, high_x, low_y, high_y = edges[:8]
     after, padded = refs[-2:]
     _, _, height, width = vorticity.shape
     first = pl.program_id(0) * LAYERS
@@ -643,10 +646,9 @@
 
     for c in range(count):
         here, above, below = adjoints[3 * c : 3 * c + 3]
-        low_x, high_x, low_y, high_y = halos[4 * c : 4 * c + 4]
         ends = spread_columns(
-            times(vort_low_x[0], low_x[...]),
-            times(vort_high_x[0], high_x[...]),
+            times(vort_low_x[0], low_x[c]),
+            times(vort_high_x[0], high_x[c]),
             first,
             LAYERS,
             width,
@@ -661,9 +663,9 @@
         for k in range(LAYERS):
             n = first + k
             padded[k, 8 : 8 + height, :] = times(vorticity[1, k], here[k])
-            padded[k, 7:8, :] = pick_row(vort_low_y[0], n) * pick_row(low_y[...], n)
+            padded[k, 7:8, :] = pick_row(vort_low_y[0], n) * pick_row(low_y[c], n)
             padded[k, 8 + height : 9 + height, :] = pick_row(vort_high_y[0], n) * pick_row(
-                high_y[...], n
+                high_y[c], n
             )
             total = (padded[k, 9 : 9 + height, :] - padded[k, 7 : 7 + height, :]) + (
                 deep[k + 2] - deep[k]
@@ -672,10 +674,9 @@
             after[c, k] = total * -step_size
 
 
-def write_grad_vel(components, slope_x, vorticity, adjoints, saved_halos, halos, before, after):
+def write_grad_vel(slope_x, vorticity, adjoints, saved_halos, halos, after):
     _, _, height, width = vorticity.shape
-    count = len(components)
-    start = components[0] // count
+    count = len(adjoints)
     whole = lambda shape: pl.BlockSpec(shape, lambda n: (0,) * len(shape))
     saved_column = pl.BlockSpec((1, Z, height), lambda n: (3, 0, 0))
     saved_row = pl.BlockSpec((1, Z, width), lambda n: (3, 0, 0))
@@ -695,16 +696,9 @@
             pl.BlockSpec((1, height, width), lambda n: (layer_above(n), 0, 0)),
             pl.BlockSpec((1, height, width), lambda n: (layer_below(n), 0, 0)),
         ]
-    operands = operands + list(saved_halos)
+    operands = operands + list(saved_halos) + list(halos)
     in_specs = in_specs + [saved_column, saved_column, saved_row, saved_row]
-    for edge in halos:
-        operands = operands + list(edge)
-        in_specs = in_specs + [whole((Z, height))] * 2 + [whole((Z, width))] * 2
-    aliases = {}
-    if before is not None:
-        aliases = {len(operands): 0}
-        operands.append(before)
-        in_specs.append(pl.BlockSpec(memory_space=pl.ANY))
+    in_specs = in_specs + [whole((count, Z, height))] * 2 + [whole((count, Z, width))] * 2
 
     def kernel(*refs):
         grad_vel_kernel(count, *refs)
@@ -713,12 +707,11 @@
         kernel,
         grid=(Z // LAYERS,),
         in_specs=in_specs + tied(after),
-        out_specs=pl.BlockSpec((count, LAYERS, height, width), lambda n: (start, n, 0, 0)),
-        out_shape=jax.ShapeDtypeStruct((3, Z, height, width), f32),
-        input_output_aliases=aliases,
+        out_specs=pl.BlockSpec((count, LAYERS, height, width), lambda n: (0, n, 0, 0)),
+        out_shape=jax.ShapeDtypeStruct((count, Z, height, width), f32),
         scratch_shapes=[pltpu.VMEM((LAYERS, height + 16, width), f32)],
         compiler_params=params(),
-        cost_estimate=takes(6 * count),
+        cost_estimate=takes(12),
         name="write_grad_vel",
     )(*operands, *after)
 
@@ -817,37 +810,29 @@
     layers_one = layers_of(rows_one)
     curl_three = curl(three, tuple(layers_one))
 
-    def adjoint_of(component, parts, after):
-        adjoint, short, first_x, last_x, first_y, last_y = make_adjoint(
-            me, parts, cot_vort, component, after
-        )
-        return adjoint, short, exchange(first_x, last_x, "gx") + exchange(first_y, last_y, "gy")
-
     def vort_of(component, adjoint, before, after):
         kind = f32 if component == three else bf16
         return add_grad_vort(
             component, (slope_x, slope_y), velocity, adjoint, saved_halos, before, after, kind
         )
 
-    def vel_of(components, adjoints, halos, before, after):
-        return write_grad_vel(
-            components, slope_x, vorticity, adjoints, saved_halos, halos, before, after
-        )
-
-    adjoint_one, short_one, halos_one = adjoint_of(one, layers_one, ())
+    adjoint_one, short_one, *edges = make_adjoint(me, layers_one, cot_vort, one, [], ())
     rows_two = rows_of(two, back(curl_two), (adjoint_one,))
     layers_two = layers_of(rows_two)
-    rows_three = rows_of(three, back(curl_three), tuple(layers_two) + halos_one)
-    grad_vort = vort_of(one, adjoint_one, None, (rows_three[0],))
-    adjoint_two, short_two, halos_two = adjoint_of(two, layers_two, (grad_vort,))
-    grad_vel = vel_of((one,), [short_one], [halos_one], None, (grad_vort,))
-    grad_vort = vort_of(two, adjoint_two, grad_vort, (grad_vel,))
-    adjoint_three, short_three, halos_three = adjoint_of(
-        three, layers_of(rows_three), (grad_vort,)
+    grad_vort = vort_of(one, adjoint_one, None, (rows_two[0],))
+    rows_three = rows_of(three, back(curl_three), tuple(layers_two) + (grad_vort,))
+    adjoint_two, short_two, *edges = make_adjoint(
+        me, layers_two, cot_vort, two, edges, (rows_three[0],)
     )
+    grad_vort = vort_of(two, adjoint_two, grad_vort, ())
+    adjoint_three, short_three, *edges = make_adjoint(
+        me, layers_of(rows_three), cot_vort, three, edges, (grad_vort,)
+    )
+    halos = exchange(edges[0], edges[1], "gx") + exchange(edges[2], edges[3], "gy")
     grad_vort = vort_of(three, adjoint_three, grad_vort, ())
-    grad_vel = vel_of(
-        (two, three), [short_two, short_three], [halos_two, halos_three], grad_vel, (grad_vort,)
+    shorts = {one: short_one, two: short_two, three: short_three}
+    grad_vel = write_grad_vel(
+        slope_x, vorticity, [shorts[i] for i in range(3)], saved_halos, halos, (grad_vort,)
     )
     return grad_vort, grad_vel
 

time: 389 us -> 365 us (0.938)
  waiting for transfers between devices: 124 us -> 109 us
  starting transfers between devices: 108 us -> 94.9 us
    ppermute x16 -> x8, waiting for transfers between devices: 32.1 us -> 15.1 us  [exchange(): return (lax.ppermute(last, axis, up), lax.ppermute(first, axis, down))]
    ppermute x16 -> x8, starting transfers between devices: 23.4 us -> 12.9 us  [exchange(): return (lax.ppermute(last, axis, up), lax.ppermute(first, axis, down))]
    all_to_all x1, waiting for transfers between devices: 0.01 us -> 6.15 us  [layers_of(): lax.all_to_all(rows[0], 'gy', 0, 0, tiled=True).reshape(Z, height, width)]
    pallas_call x3, Pallas kernels: 22.8 us -> 28.7 us  [add_grad_vort(): pl.pallas_call(kernel, grid=(Z // LAYERS,), in_specs=in_specs + tied(afte...]
    ppermute x28, waiting for transfers between devices: 32.9 us -> 27.6 us  [shifted(): lax.ppermute(parts[s], axis, [(i, (i + s) % count) for i in range(count)])]
    all_to_all x1, starting transfers between devices: 10.3 us -> 5.83 us  [layers_of(): lax.all_to_all(rows[0], 'gy', 0, 0, tiled=True).reshape(Z, height, width)]
    pallas_call x2 -> x1, Pallas kernels: 17.6 us -> 15.1 us  [write_grad_vel(): pl.pallas_call(kernel, grid=(Z // LAYERS,), in_specs=in_specs + tied(afte...]
    unnamed x140 -> x116, local copies, waits for them, and re-layouts: 16.8 us -> 16.7 us
  transfers between devices with their start and end apart: 52 -> 44, of which waited for: 28 -> 25; matrix products, arithmetic and copies ran while one was open for 1% -> 1% of each run, Pallas kernels for 27% -> 28%
where the time goes in v9:
time: 365 us; the launch traced here: 363 us
  Pallas kernels  137 us (38%)
  waiting for transfers between devices  109 us (30%)
  starting transfers between devices  94.9 us (26%)
  local copies, waits for them, and re-layouts  18.7 us (5%)
    ppermute x28, starting transfers between devices, shifted(): lax.ppermute(parts[s], axis, [(i, (i + s) % count) for i in range(count)])  43.3 us
    all_to_all x3, waiting for transfers between devices, spectrum(): lines = lax.all_to_all(sent[place], 'gx', 0, 0, tiled=True)  30.1 us
    pallas_call x3, Pallas kernels, add_grad_vort(): pl.pallas_call(kernel, grid=(Z // LAYERS,), in_specs=in_specs + tied(afte...  28.7 us
    ppermute x28, waiting for transfers between devices, shifted(): lax.ppermute(parts[s], axis, [(i, (i + s) % count) for i in range(count)])  27.6 us
    all_to_all x3, waiting for transfers between devices, back(): parts = lax.all_to_all(filtered, 'gx', 0, 0, tiled=True)  26.7 us
    pallas_call x3, Pallas kernels, y_inverse(): pl.pallas_call(kernel, in_specs=[pl.BlockSpec(memory_space=pltpu.SMEM), a...  21.9 us
    pallas_call x3, Pallas kernels, y_transform(): pl.pallas_call(kernel, in_specs=[pl.BlockSpec(memory_space=pltpu.SMEM), a...  19.7 us
    unnamed x116, local copies, waits for them, and re-layouts  16.7 us
  transfers between devices with their start and end apart: 44, of which 25 were waited for; matrix products, arithmetic and copies ran while one was open for 1% of the time, Pallas kernels for 28%

profile of v9, /device:TPU:0, one launch (start us, length us, event | category | flops | bytes accessed | tf_op | source)
XLA Modules:
  0.0 362.6 jit_solution(257786224244667317)
XLA Ops:
  0.6 3.2 depth_transform.3.refs_0_
  3.8 5.2 %all-to-all-start = ((bf16[8,2,192,256]{3,2,1,0:T(8,128)(2,1)}), bf16[8,2,192,256]{3,2,1,0:T(8,128)(2,1)S(1)}, u32[]{:S(2)}, u32[]{:S(2)}) async-start(bf16[8,2,192,256]{3,2,1,0:T(8,128)(2,1)} %bitcast.27), calls=%async_computation | async-start | bytes 3145728 | tf_op jit(solution)/shard_map/all_to_all | solution.py:771
  11.6 4.6 %edge_columns.2 = (bf16[3,16,192]{2,1,0:T(8,128)(2,1)}, bf16[3,16,192]{2,1,0:T(8,128)(2,1)}) custom-call(bf16[3,16,192,256]{3,2,1,0:T(8,128)(2,1)} %refs_2_.6, bf16[16,192,256]{2,1,0:T(8,128)(2,1)} %depth_transform.3.refs_0_), custom_call_target="tpu_custom_call" | custom-call | flops 1 | bytes 12000000 | tf_op jit(solution)/shard_map/edge_columns/pallas_call | solution.py:456
  16.9 3.7 %collective-permute-start.1 = (bf16[4,16,192]{2,1,0:T(8,128)(2,1)S(1)}, bf16[4,16,192]{2,1,0:T(8,128)(2,1)S(1)}, u32[]{:S(2)}, u32[]{:S(2)}) collective-permute-start(bf16[4,16,192]{2,1,0:T(8,128)(2,1)S(1)} %pad_maximum_fusion.1), channel_id=1, source_target_pairs={{8,0},{16,8},{24,16},{0,24},{9,1},{17,9},{25,17},{1,25},{10,2},{18... | collective-permute-start | bytes 73736 | tf_op jit(solution)/shard_map/ppermute | solution.py:472
  22.2 4.9 %collective-permute-done.refs_1_.refs_4_.refs_13_ = bf16[4,16,192]{2,1,0:T(8,128)(2,1)S(1)} collective-permute-done((bf16[4,16,192]{2,1,0:T(8,128)(2,1)S(1)}, bf16[4,16,192]{2,1,0:T(8,128)(2,1)S(1)}, u32[]{:S(2)}, u32[]{:S(2)}) %collective-permute-start) | collective-permute-done | bytes 24608 | tf_op jit(solution)/shard_map/ppermute | solution.py:472
  27.1 2.9 all-to-all-done.refs_0_
  31.1 6.6 %y_transform.3 = bf16[4,1,2,2,192,256]{5,4,3,2,1,0:T(8,128)(2,1)} custom-call(s32[1]{0:T(128)} %bitcast.me_ref.refs_0_, bf16[1536,1536]{1,0:T(8,128)(2,1)} %constant.33.clone.table_ref, bf16[8,2,192,256]{3,2,1,0:T(8,128)(2,1)} %copy-done.24, bf16[4,16,192]{2,1,0:T(8,128)(2,1)} %copy-done.26, bf16[4,16,192]{2,1,0:T(8,128)(2,1)} %copy-done.25), custom_call_target="tpu_custom_call" | custom-call | flops 1 | bytes 15000000 | tf_op jit(solution)/shard_map/y_transform/pallas_call | solution.py:224
  37.7 4.9 %all-to-all-start.1 = ((bf16[4,2,2,192,256]{4,3,2,1,0:T(8,128)(2,1)}), bf16[4,2,2,192,256]{4,3,2,1,0:T(8,128)(2,1)S(1)}, u32[]{:S(2)}, u32[]{:S(2)}) async-start(bf16[4,2,2,192,256]{4,3,2,1,0:T(8,128)(2,1)} %bitcast.28), calls=%async_computation.1 | async-start | bytes 3145728 | tf_op jit(solution)/shard_map/all_to_all | solution.py:782
  44.6 3.3 depth_transform.4
  51.3 9.4 %collective-permute-done.9.refs_8_.refs_6_.refs_15_ = bf16[4,16,256]{2,1,0:T(8,128)(2,1)S(1)} collective-permute-done((bf16[4,16,256]{2,1,0:T(8,128)(2,1)S(1)}, bf16[4,16,256]{2,1,0:T(8,128)(2,1)S(1)}, u32[]{:S(2)}, u32[]{:S(2)}) %collective-permute-start.9) | collective-permute-done | bytes 32800 | tf_op jit(solution)/shard_map/ppermute | solution.py:472
  64.0 3.2 collective-permute-done.5.refs_4_
  71.7 6.6 %y_transform.4 = bf16[4,1,2,2,192,256]{5,4,3,2,1,0:T(8,128)(2,1)} custom-call(s32[1]{0:T(128)} %bitcast.me_ref.refs_0_, bf16[1536,1536]{1,0:T(8,128)(2,1)} %constant.33.clone.table_ref, bf16[2,192,256]{2,1,0:T(8,128)(2,1)} %get-tuple-element.60.refs_0_, bf16[2,192,256]{2,1,0:T(8,128)(2,1)} %copy-done.36, bf16[2,192,256]{2,1,0:T(8,128)(2,1)} %copy-done.37, ...), custom_call_target="tpu_custom_call" | custom-call | flops 1 | bytes 15000000 | tf_op jit(solution)/shard_map/y_transform/pallas_call | solution.py:224
  78.3 5.1 %all-to-all-start.3 = ((bf16[4,2,2,192,256]{4,3,2,1,0:T(8,128)(2,1)}), bf16[4,2,2,192,256]{4,3,2,1,0:T(8,128)(2,1)}, u32[]{:S(2)}, u32[]{:S(2)}) async-start(bf16[4,2,2,192,256]{4,3,2,1,0:T(8,128)(2,1)} %bitcast.22), calls=%async_computation.3 | async-start | bytes 3145728 | tf_op jit(solution)/shard_map/all_to_all | solution.py:782
  83.4 3.3 depth_transform.5
  88.4 4.2 %collective-permute-start.12 = (bf16[2,192,256]{2,1,0:T(8,128)(2,1)}, bf16[2,192,256]{2,1,0:T(8,128)(2,1)S(1)}, u32[]{:S(2)}, u32[]{:S(2)}) collective-permute-start(bf16[2,192,256]{2,1,0:T(8,128)(2,1)} %get-tuple-element.70), channel_id=1, source_target_pairs={{0,2},{1,3},{2,4},{3,5},{4,6},{5,7},{6,0},{7,1},{8,10},{9,11},{10,... | collective-permute-start | bytes 589832 | tf_op jit(solution)/shard_map/ppermute | solution.py:730
  95.4 2.7 collective-permute-done.11.refs_1_
  101.7 5.3 %collective-permute-done.13.refs_3_ = bf16[2,192,256]{2,1,0:T(8,128)(2,1)S(1)} collective-permute-done((bf16[2,192,256]{2,1,0:T(8,128)(2,1)}, bf16[2,192,256]{2,1,0:T(8,128)(2,1)S(1)}, u32[]{:S(2)}, u32[]{:S(2)}) %collective-permute-start.13) | collective-permute-done | bytes 196640 | tf_op jit(solution)/shard_map/ppermute | solution.py:730
  110.4 6.6 %y_transform.5 = bf16[4,1,2,2,192,256]{5,4,3,2,1,0:T(8,128)(2,1)} custom-call(s32[1]{0:T(128)} %bitcast.me_ref.refs_0_, bf16[1536,1536]{1,0:T(8,128)(2,1)} %constant.33.clone.table_ref, bf16[2,192,256]{2,1,0:T(8,128)(2,1)} %get-tuple-element.68.refs_0_, bf16[2,192,256]{2,1,0:T(8,128)(2,1)} %copy-done.39, bf16[2,192,256]{2,1,0:T(8,128)(2,1)} %copy-done.40, ...), custom_call_target="tpu_custom_call" | custom-call | flops 1 | bytes 15000000 | tf_op jit(solution)/shard_map/y_transform/pallas_call | solution.py:224
  117.0 4.1 %all-to-all-done.3.modes_ref = bf16[4,2,2,192,256]{4,3,2,1,0:T(8,128)(2,1)} async-done(((bf16[4,2,2,192,256]{4,3,2,1,0:T(8,128)(2,1)}), bf16[4,2,2,192,256]{4,3,2,1,0:T(8,128)(2,1)}, u32[]{:S(2)}, u32[]{:S(2)}) %all-to-all-start.3) | async-done | bytes 1572896 | tf_op jit(solution)/shard_map/all_to_all | solution.py:782
  121.1 4.5 %all-to-all-start.2 = ((bf16[4,2,2,192,256]{4,3,2,1,0:T(8,128)(2,1)}), bf16[4,2,2,192,256]{4,3,2,1,0:T(8,128)(2,1)}, u32[]{:S(2)}, u32[]{:S(2)}) async-start(bf16[4,2,2,192,256]{4,3,2,1,0:T(8,128)(2,1)} %bitcast.25), calls=%async_computation.2 | async-start | bytes 3145728 | tf_op jit(solution)/shard_map/all_to_all | solution.py:782
  129.5 3.9 %x_transform.4.refs_2_.refs_3_ = f32[2,2,192,1024]{3,2,1,0:T(8,128)S(1)} custom-call(bf16[1024,1024]{1,0:T(8,128)(2,1)S(1)} %copy-done.8, bf16[4,2,2,192,256]{4,3,2,1,0:T(8,128)(2,1)} %all-to-all-done.3.modes_ref, bf16[4,2,2,192,256]{4,3,2,1,0:T(8,128)(2,1)S(1)} %bitcast.26), custom_call_target="tpu_custom_call" | custom-call | flops 1 | bytes 9000000 | tf_op jit(solution)/shard_map/x_transform/pallas_call | solution.py:318
  133.4 3.0 curl_inverse.3.refs_0_
  137.5 26.0 %all-to-all-done.2.modes_ref = bf16[4,2,2,192,256]{4,3,2,1,0:T(8,128)(2,1)} async-done(((bf16[4,2,2,192,256]{4,3,2,1,0:T(8,128)(2,1)}), bf16[4,2,2,192,256]{4,3,2,1,0:T(8,128)(2,1)}, u32[]{:S(2)}, u32[]{:S(2)}) %all-to-all-start.2) | async-done | bytes 1572896 | tf_op jit(solution)/shard_map/all_to_all | solution.py:782
  163.5 4.4 %all-to-all-start.4 = ((bf16[4,2,2,192,256]{4,3,2,1,0:T(8,128)(2,1)}), bf16[4,2,2,192,256]{4,3,2,1,0:T(8,128)(2,1)}, u32[]{:S(2)}, u32[]{:S(2)}) async-start(bf16[4,2,2,192,256]{4,3,2,1,0:T(8,128)(2,1)} %copy-done.10), calls=%async_computation.4 | async-start | bytes 3145728 | tf_op jit(solution)/shard_map/all_to_all | solution.py:789
  170.9 3.3 x_transform.5.refs_2_.refs_3_
  174.1 3.0 curl_inverse.4.refs_0_
  180.0 25.1 %all-to-all-done.4 = bf16[4,2,2,192,256]{4,3,2,1,0:T(8,128)(2,1)} async-done(((bf16[4,2,2,192,256]{4,3,2,1,0:T(8,128)(2,1)}), bf16[4,2,2,192,256]{4,3,2,1,0:T(8,128)(2,1)}, u32[]{:S(2)}, u32[]{:S(2)}) %all-to-all-start.4) | async-done | bytes 1572896 | tf_op jit(solution)/shard_map/all_to_all | solution.py:789
  205.1 4.4 %all-to-all-start.6 = ((bf16[4,2,2,192,256]{4,3,2,1,0:T(8,128)(2,1)}), bf16[4,2,2,192,256]{4,3,2,1,0:T(8,128)(2,1)}, u32[]{:S(2)}, u32[]{:S(2)}) async-start(bf16[4,2,2,192,256]{4,3,2,1,0:T(8,128)(2,1)} %copy-done.12), calls=%async_computation.6 | async-start | bytes 3145728 | tf_op jit(solution)/shard_map/all_to_all | solution.py:789
  209.5 7.4 %y_inverse.3 = (bf16[2,192,256]{2,1,0:T(8,128)(2,1)}, bf16[2,192,256]{2,1,0:T(8,128)(2,1)}, bf16[2,192,256]{2,1,0:T(8,128)(2,1)}, bf16[2,192,256]{2,1,0:T(8,128)...) custom-call(s32[1]{0:T(128)} %bitcast.me_ref.refs_0_, ...), custom_call_target="tpu_custom_call" | custom-call | flops 1 | bytes 12000000 | tf_op jit(solution)/shard_map/y_inverse/pallas_call | solution.py:288
  216.9 4.4 %collective-permute-start.19 = (bf16[2,192,256]{2,1,0:T(8,128)(2,1)}, bf16[2,192,256]{2,1,0:T(8,128)(2,1)S(1)}, u32[]{:S(2)}, u32[]{:S(2)}) collective-permute-start(bf16[2,192,256]{2,1,0:T(8,128)(2,1)} %get-tuple-element.78), channel_id=1, source_target_pairs={{0,2},{1,3},{2,4},{3,5},{4,6},{5,7},{6,0},{7,1},{8,10},{9,11},{10,... | collective-permute-start | bytes 589832 | tf_op jit(solution)/shard_map/ppermute | solution.py:730
  224.5 4.2 %collective-permute-start.23 = (bf16[2,192,256]{2,1,0:T(8,128)(2,1)}, bf16[2,192,256]{2,1,0:T(8,128)(2,1)S(1)}, u32[]{:S(2)}, u32[]{:S(2)}) collective-permute-start(bf16[2,192,256]{2,1,0:T(8,128)(2,1)} %get-tuple-element.82), channel_id=1, source_target_pairs={{0,6},{1,7},{2,0},{3,1},{4,2},{5,3},{6,4},{7,5},{8,14},{9,15},{10,... | collective-permute-start | bytes 589832 | tf_op jit(solution)/shard_map/ppermute | solution.py:730
  228.7 4.0 %collective-permute-start.24 = (bf16[2,192,256]{2,1,0:T(8,128)(2,1)}, bf16[2,192,256]{2,1,0:T(8,128)(2,1)S(1)}, u32[]{:S(2)}, u32[]{:S(2)}) collective-permute-start(bf16[2,192,256]{2,1,0:T(8,128)(2,1)} %get-tuple-element.83), channel_id=1, source_target_pairs={{0,7},{1,0},{2,1},{3,2},{4,3},{5,4},{6,5},{7,6},{8,15},{9,8},{10,9... | collective-permute-start | bytes 589832 | tf_op jit(solution)/shard_map/ppermute | solution.py:730
  241.6 3.8 %curl_inverse.5 = bf16[4,2,2,192,256]{4,3,2,1,0:T(8,128)(2,1)} custom-call(s32[2]{0:T(128)S(1)} %pad_add_fusion.refs_0_, bf16[1024,1024]{1,0:T(8,128)(2,1)S(1)} %copy-done.7, f32[2,2,192,1024]{3,2,1,0:T(8,128)S(1)} %copy-done.1, f32[2,2,192,1024]{3,2,1,0:T(8,128)S(1)} %copy-done.3, bf16[2,192,256]{2,1,0:T(8,128)(2,1)S(1)} %copy-done.14, ...), custom_call_target="tpu_custom_call" | custom-call | flops 1 | bytes 12000000 | tf_op jit(solution)/shard_map/curl_inverse/pallas_call | solution.py:394
  246.0 4.5 %all-to-all-start.5 = ((bf16[4,2,2,192,256]{4,3,2,1,0:T(8,128)(2,1)}), bf16[4,2,2,192,256]{4,3,2,1,0:T(8,128)(2,1)S(1)}, u32[]{:S(2)}, u32[]{:S(2)}) async-start(bf16[4,2,2,192,256]{4,3,2,1,0:T(8,128)(2,1)} %curl_inverse.5), calls=%async_computation.5 | async-start | bytes 3145728 | tf_op jit(solution)/shard_map/all_to_all | solution.py:789
  250.5 5.3 %make_adjoint.3 = (f32[16,192,256]{2,1,0:T(8,128)}, bf16[16,192,256]{2,1,0:T(8,128)(2,1)}, bf16[3,16,192]{2,1,0:T(8,128)(2,1)}, bf16[3,16,192]{2,1,0:T(8,128)(2,...) custom-call(s32[1]{0:T(128)} %bitcast.me_ref.refs_0_, ...), custom_call_target="tpu_custom_call" | custom-call | flops 1 | bytes 15000000 | tf_op jit(solution)/shard_map/make_adjoint/pallas_call | solution.py:523
  255.8 7.2 %y_inverse.4 = (bf16[2,192,256]{2,1,0:T(8,128)(2,1)}, bf16[2,192,256]{2,1,0:T(8,128)(2,1)}, bf16[2,192,256]{2,1,0:T(8,128)(2,1)}, bf16[2,192,256]{2,1,0:T(8,128)...) custom-call(s32[1]{0:T(128)} %bitcast.me_ref.refs_0_, ...), custom_call_target="tpu_custom_call" | custom-call | flops 1 | bytes 12000000 | tf_op jit(solution)/shard_map/y_inverse/pallas_call | solution.py:288
  263.1 3.7 %collective-permute-start.26 = (bf16[2,192,256]{2,1,0:T(8,128)(2,1)}, bf16[2,192,256]{2,1,0:T(8,128)(2,1)S(1)}, u32[]{:S(2)}, u32[]{:S(2)}) collective-permute-start(bf16[2,192,256]{2,1,0:T(8,128)(2,1)} %get-tuple-element.87), channel_id=1, source_target_pairs={{0,2},{1,3},{2,4},{3,5},{4,6},{5,7},{6,0},{7,1},{8,10},{9,11},{10,... | collective-permute-start | bytes 589832 | tf_op jit(solution)/shard_map/ppermute | solution.py:730
  274.1 3.9 %collective-permute-start.31 = (bf16[2,192,256]{2,1,0:T(8,128)(2,1)}, bf16[2,192,256]{2,1,0:T(8,128)(2,1)S(1)}, u32[]{:S(2)}, u32[]{:S(2)}) collective-permute-start(bf16[2,192,256]{2,1,0:T(8,128)(2,1)} %get-tuple-element.92), channel_id=1, source_target_pairs={{0,7},{1,0},{2,1},{3,2},{4,3},{5,4},{6,5},{7,6},{8,15},{9,8},{10,9... | collective-permute-start | bytes 589832 | tf_op jit(solution)/shard_map/ppermute | solution.py:730
  278.1 8.3 %add_grad_vort.3.refs_8_ = bf16[3,16,192,256]{3,2,1,0:T(8,128)(2,1)} custom-call(bf16[256,256]{1,0:T(8,128)(2,1)} %constant.37.clone.refs_0_, bf16[192,192]{1,0:T(8,128)(2,1)} %constant.38.clone.refs_1_, bf16[3,16,192,256]{3,2,1,0:T(8,128)(2,1)} %refs_2_.6, f32[16,192,256]{2,1,0:T(8,128)} %get-tuple-element.84.refs_0_.refs_3_, ...), custom_call_target="tpu_custom_call" | custom-call | flops 1 | bytes 27000000 | tf_op jit(solution)/shard_map/add_grad_vort/pallas_call | solution.py:625
  288.7 7.4 %y_inverse.5.refs_13_ = bf16[8,2,192,256]{3,2,1,0:T(8,128)(2,1)} custom-call(s32[1]{0:T(128)} %bitcast.me_ref.refs_0_, bf16[1536,1536]{1,0:T(8,128)(2,1)} %constant.36.clone.table_ref, bf16[4,1,2,2,192,256]{5,4,3,2,1,0:T(8,128)(2,1)} %bitcast.31, bf16[2,192,256]{2,1,0:T(8,128)(2,1)} %get-tuple-element.85.refs_8_.refs_0_, bf16[2,192,256]{2,1,0:T(8,128)(2,1)} %copy-done.29, ...), custom_call_target="tpu_custom_call" | custom-call | flops 1 | bytes 12000000 | tf_op jit(solution)/shard_map/y_inverse/pallas_call | solution.py:288
  296.1 5.8 %all-to-all-start.7 = ((bf16[8,2,192,256]{3,2,1,0:T(8,128)(2,1)}), bf16[8,2,192,256]{3,2,1,0:T(8,128)(2,1)S(1)}, u32[]{:S(2)}, u32[]{:S(2)}) async-start(bf16[8,2,192,256]{3,2,1,0:T(8,128)(2,1)} %y_inverse.5.refs_13_), calls=%async_computation.7 | async-start | bytes 3145728 | tf_op jit(solution)/shard_map/all_to_all | solution.py:800
  301.9 5.3 %make_adjoint.4 = (f32[16,192,256]{2,1,0:T(8,128)}, bf16[16,192,256]{2,1,0:T(8,128)(2,1)}, bf16[3,16,192]{2,1,0:T(8,128)(2,1)}, bf16[3,16,192]{2,1,0:T(8,128)(2,...) custom-call(s32[1]{0:T(128)} %bitcast.me_ref.refs_0_, ...), custom_call_target="tpu_custom_call", output_to_operand_aliasing={{2}: (10, {}), {3}: (11, {}), {4}: (12, {}), {5}: (13, {})} | custom-call | flops 1 | bytes 15000000 | tf_op jit(solution)/shard_map/make_adjoint/pallas_call | solution.py:523
  307.2 9.6 %add_grad_vort.4.refs_6_.refs_8_ = bf16[3,16,192,256]{3,2,1,0:T(8,128)(2,1)} custom-call(bf16[256,256]{1,0:T(8,128)(2,1)} %constant.37.clone.refs_0_, bf16[192,192]{1,0:T(8,128)(2,1)} %constant.38.clone.refs_1_, bf16[3,16,192,256]{3,2,1,0:T(8,128)(2,1)} %refs_2_.6, f32[16,192,256]{2,1,0:T(8,128)} %get-tuple-element.101.refs_3_, ...), custom_call_target="tpu_custom_call" | custom-call | flops 1 | bytes 27000000 | tf_op jit(solution)/shard_map/add_grad_vort/pallas_call | solution.py:625
  316.8 6.2 %all-to-all-done.7 = bf16[8,2,192,256]{3,2,1,0:T(8,128)(2,1)S(1)} async-done(((bf16[8,2,192,256]{3,2,1,0:T(8,128)(2,1)}), bf16[8,2,192,256]{3,2,1,0:T(8,128)(2,1)S(1)}, u32[]{:S(2)}, u32[]{:S(2)}) %all-to-all-start.7) | async-done | bytes 1572896 | tf_op jit(solution)/shard_map/all_to_all | solution.py:800
  324.1 5.2 %make_adjoint.5 = (f32[16,192,256]{2,1,0:T(8,128)}, bf16[16,192,256]{2,1,0:T(8,128)(2,1)}, bf16[3,16,192]{2,1,0:T(8,128)(2,1)}, bf16[3,16,192]{2,1,0:T(8,128)(2,...) custom-call(s32[1]{0:T(128)} %bitcast.me_ref.refs_0_, ...), custom_call_target="tpu_custom_call", output_to_operand_aliasing={{2}: (3, {}), {3}: (4, {}), {4}: (5, {}), {5}: (6, {})} | custom-call | flops 1 | bytes 15000000 | tf_op jit(solution)/shard_map/make_adjoint/pallas_call | solution.py:523
  332.0 3.8 %collective-permute-start.33 = (bf16[3,16,192]{2,1,0:T(8,128)(2,1)}, bf16[3,16,192]{2,1,0:T(8,128)(2,1)S(1)}, u32[]{:S(2)}, u32[]{:S(2)}) collective-permute-start(bf16[3,16,192]{2,1,0:T(8,128)(2,1)} %get-tuple-element.107), channel_id=1, source_target_pairs={{8,0},{16,8},{24,16},{0,24},{9,1},{17,9},{25,17},{1,25},{10,2},{18... | collective-permute-start | bytes 55304 | tf_op jit(solution)/shard_map/ppermute | solution.py:472
  335.8 10.9 %add_grad_vort.5.refs_21_ = f32[3,16,192,256]{3,2,1,0:T(8,128)} custom-call(bf16[256,256]{1,0:T(8,128)(2,1)} %constant.37.clone.refs_0_, bf16[192,192]{1,0:T(8,128)(2,1)} %constant.38.clone.refs_1_, bf16[3,16,192,256]{3,2,1,0:T(8,128)(2,1)} %refs_2_.6, f32[16,192,256]{2,1,0:T(8,128)} %get-tuple-element.102.refs_3_, bf16[4,16,192]{2,1,0:T(8,128)(2,1)} %copy-done.26, ...), custom_call_target="tpu_custom_call" | custom-call | flops 1 | bytes 27000000 | tf_op jit(solution)/shard_map/add_grad_vort/pallas_call | solution.py:625
  347.3 15.1 %write_grad_vel.1 = f32[3,16,192,256]{3,2,1,0:T(8,128)} custom-call(bf16[256,256]{1,0:T(8,128)(2,1)} %constant.37.clone.refs_0_, bf16[3,16,192,256]{3,2,1,0:T(8,128)(2,1)} %refs_3_.1, bf16[3,16,192,256]{3,2,1,0:T(8,128)(2,1)} %refs_3_.1, bf16[3,16,192,256]{3,2,1,0:T(8,128)(2,1)} %refs_3_.1, bf16[16,192,256]{2,1,0:T(8,128)(2,1)} %get-tuple-element.103.refs_4_.refs_5_.refs_6_, ...), custom_call_target="tpu_custom_call" | custom-call | flops 1 | bytes 36000000 | tf_op jit(solution)/shard_map/write_grad_vel/pallas_call | solution.py:706
  (187 shorter events, 68.1 us)
Async XLA Ops:
  3.8 26.2 %all-to-all-start = ((bf16[8,2,192,256]{3,2,1,0:T(8,128)(2,1)}), bf16[8,2,192,256]{3,2,1,0:T(8,128)(2,1)S(1)}, u32[]{:S(2)}, u32[]{:S(2)}) async-start(bf16[8,2,192,256]{3,2,1,0:T(8,128)(2,1)} %bitcast.27), calls=%async_computation | async-start | bytes 3145728 | tf_op jit(solution)/shard_map/all_to_all | solution.py:771
  16.9 5.3 %collective-permute-start.1 = (bf16[4,16,192]{2,1,0:T(8,128)(2,1)S(1)}, bf16[4,16,192]{2,1,0:T(8,128)(2,1)S(1)}, u32[]{:S(2)}, u32[]{:S(2)}) collective-permute-start(bf16[4,16,192]{2,1,0:T(8,128)(2,1)S(1)} %pad_maximum_fusion.1), channel_id=1, source_target_pairs={{8,0},{16,8},{24,16},{0,24},{9,1},{17,9},{25,17},{1,25},{10,2},{18... | collective-permute-start | bytes 73736 | tf_op jit(solution)/shard_map/ppermute | solution.py:472
  21.3 5.8 %collective-permute-start = (bf16[4,16,192]{2,1,0:T(8,128)(2,1)S(1)}, bf16[4,16,192]{2,1,0:T(8,128)(2,1)S(1)}, u32[]{:S(2)}, u32[]{:S(2)}) collective-permute-start(bf16[4,16,192]{2,1,0:T(8,128)(2,1)S(1)} %pad_maximum_fusion), channel_id=1, source_target_pairs={{0,8},{8,16},{16,24},{24,0},{1,9},{9,17},{17,25},{25,1},{2,10},{10... | collective-permute-start | bytes 73736 | tf_op jit(solution)/shard_map/ppermute | solution.py:472
  37.7 40.5 %all-to-all-start.1 = ((bf16[4,2,2,192,256]{4,3,2,1,0:T(8,128)(2,1)}), bf16[4,2,2,192,256]{4,3,2,1,0:T(8,128)(2,1)S(1)}, u32[]{:S(2)}, u32[]{:S(2)}) async-start(bf16[4,2,2,192,256]{4,3,2,1,0:T(8,128)(2,1)} %bitcast.28), calls=%async_computation.1 | async-start | bytes 3145728 | tf_op jit(solution)/shard_map/all_to_all | solution.py:782
  47.9 13.3 %collective-permute-start.2 = (bf16[2,192,256]{2,1,0:T(8,128)(2,1)}, bf16[2,192,256]{2,1,0:T(8,128)(2,1)S(1)}, u32[]{:S(2)}, u32[]{:S(2)}) collective-permute-start(bf16[2,192,256]{2,1,0:T(8,128)(2,1)} %get-tuple-element.61), channel_id=1, source_target_pairs={{0,1},{1,2},{2,3},{3,4},{4,5},{5,6},{6,7},{7,0},{8,9},{9,10},{10,1... | collective-permute-start | bytes 589832 | tf_op jit(solution)/shard_map/ppermute | solution.py:730
  48.0 13.8 %collective-permute-start.3 = (bf16[2,192,256]{2,1,0:T(8,128)(2,1)}, bf16[2,192,256]{2,1,0:T(8,128)(2,1)S(1)}, u32[]{:S(2)}, u32[]{:S(2)}) collective-permute-start(bf16[2,192,256]{2,1,0:T(8,128)(2,1)} %get-tuple-element.62), channel_id=1, source_target_pairs={{0,2},{1,3},{2,4},{3,5},{4,6},{5,7},{6,0},{7,1},{8,10},{9,11},{10,... | collective-permute-start | bytes 589832 | tf_op jit(solution)/shard_map/ppermute | solution.py:730
  48.5 12.1 %collective-permute-start.9 = (bf16[4,16,256]{2,1,0:T(8,128)(2,1)S(1)}, bf16[4,16,256]{2,1,0:T(8,128)(2,1)S(1)}, u32[]{:S(2)}, u32[]{:S(2)}) collective-permute-start(bf16[4,16,256]{2,1,0:T(8,128)(2,1)S(1)} %pad_maximum_fusion.2), channel_id=1, source_target_pairs={{0,1},{1,2},{2,3},{3,4},{4,5},{5,6},{6,7},{7,0},{8,9},{9,10},{10,1... | collective-permute-start | bytes 98312 | tf_op jit(solution)/shard_map/ppermute | solution.py:472
  49.8 11.4 %collective-permute-start.10 = (bf16[4,16,256]{2,1,0:T(8,128)(2,1)S(1)}, bf16[4,16,256]{2,1,0:T(8,128)(2,1)S(1)}, u32[]{:S(2)}, u32[]{:S(2)}) collective-permute-start(bf16[4,16,256]{2,1,0:T(8,128)(2,1)S(1)} %pad_maximum_fusion.3), channel_id=1, source_target_pairs={{1,0},{2,1},{3,2},{4,3},{5,4},{6,5},{7,6},{0,7},{9,8},{10,9},{11,1... | collective-permute-start | bytes 98312 | tf_op jit(solution)/shard_map/ppermute | solution.py:472
  51.3 12.7 %collective-permute-start.4 = (bf16[2,192,256]{2,1,0:T(8,128)(2,1)}, bf16[2,192,256]{2,1,0:T(8,128)(2,1)S(1)}, u32[]{:S(2)}, u32[]{:S(2)}) collective-permute-start(bf16[2,192,256]{2,1,0:T(8,128)(2,1)} %get-tuple-element.63), channel_id=1, source_target_pairs={{0,3},{1,4},{2,5},{3,6},{4,7},{5,0},{6,1},{7,2},{8,11},{9,12},{10,... | collective-permute-start | bytes 589832 | tf_op jit(solution)/shard_map/ppermute | solution.py:730
  60.7 6.5 %collective-permute-start.5 = (bf16[2,192,256]{2,1,0:T(8,128)(2,1)}, bf16[2,192,256]{2,1,0:T(8,128)(2,1)S(1)}, u32[]{:S(2)}, u32[]{:S(2)}) collective-permute-start(bf16[2,192,256]{2,1,0:T(8,128)(2,1)} %get-tuple-element.64), channel_id=1, source_target_pairs={{0,4},{1,5},{2,6},{3,7},{4,0},{5,1},{6,2},{7,3},{8,12},{9,13},{10,... | collective-permute-start | bytes 589832 | tf_op jit(solution)/shard_map/ppermute | solution.py:730
  61.2 6.8 %collective-permute-start.6 = (bf16[2,192,256]{2,1,0:T(8,128)(2,1)}, bf16[2,192,256]{2,1,0:T(8,128)(2,1)S(1)}, u32[]{:S(2)}, u32[]{:S(2)}) collective-permute-start(bf16[2,192,256]{2,1,0:T(8,128)(2,1)} %get-tuple-element.65), channel_id=1, source_target_pairs={{0,5},{1,6},{2,7},{3,0},{4,1},{5,2},{6,3},{7,4},{8,13},{9,14},{10,... | collective-permute-start | bytes 589832 | tf_op jit(solution)/shard_map/ppermute | solution.py:730
  61.3 8.0 %collective-permute-start.7 = (bf16[2,192,256]{2,1,0:T(8,128)(2,1)}, bf16[2,192,256]{2,1,0:T(8,128)(2,1)S(1)}, u32[]{:S(2)}, u32[]{:S(2)}) collective-permute-start(bf16[2,192,256]{2,1,0:T(8,128)(2,1)} %get-tuple-element.66), channel_id=1, source_target_pairs={{0,6},{1,7},{2,0},{3,1},{4,2},{5,3},{6,4},{7,5},{8,14},{9,15},{10,... | collective-permute-start | bytes 589832 | tf_op jit(solution)/shard_map/ppermute | solution.py:730
  61.8 9.2 %collective-permute-start.8 = (bf16[2,192,256]{2,1,0:T(8,128)(2,1)}, bf16[2,192,256]{2,1,0:T(8,128)(2,1)S(1)}, u32[]{:S(2)}, u32[]{:S(2)}) collective-permute-start(bf16[2,192,256]{2,1,0:T(8,128)(2,1)} %get-tuple-element.67), channel_id=1, source_target_pairs={{0,7},{1,0},{2,1},{3,2},{4,3},{5,4},{6,5},{7,6},{8,15},{9,8},{10,9... | collective-permute-start | bytes 589832 | tf_op jit(solution)/shard_map/ppermute | solution.py:730
  78.3 42.9 %all-to-all-start.3 = ((bf16[4,2,2,192,256]{4,3,2,1,0:T(8,128)(2,1)}), bf16[4,2,2,192,256]{4,3,2,1,0:T(8,128)(2,1)}, u32[]{:S(2)}, u32[]{:S(2)}) async-start(bf16[4,2,2,192,256]{4,3,2,1,0:T(8,128)(2,1)} %bitcast.22), calls=%async_computation.3 | async-start | bytes 3145728 | tf_op jit(solution)/shard_map/all_to_all | solution.py:782
  86.6 11.5 %collective-permute-start.11 = (bf16[2,192,256]{2,1,0:T(8,128)(2,1)}, bf16[2,192,256]{2,1,0:T(8,128)(2,1)S(1)}, u32[]{:S(2)}, u32[]{:S(2)}) collective-permute-start(bf16[2,192,256]{2,1,0:T(8,128)(2,1)} %get-tuple-element.69), channel_id=1, source_target_pairs={{0,1},{1,2},{2,3},{3,4},{4,5},{5,6},{6,7},{7,0},{8,9},{9,10},{10,1... | collective-permute-start | bytes 589832 | tf_op jit(solution)/shard_map/ppermute | solution.py:730
  88.4 11.0 %collective-permute-start.12 = (bf16[2,192,256]{2,1,0:T(8,128)(2,1)}, bf16[2,192,256]{2,1,0:T(8,128)(2,1)S(1)}, u32[]{:S(2)}, u32[]{:S(2)}) collective-permute-start(bf16[2,192,256]{2,1,0:T(8,128)(2,1)} %get-tuple-element.70), channel_id=1, source_target_pairs={{0,2},{1,3},{2,4},{3,5},{4,6},{5,7},{6,0},{7,1},{8,10},{9,11},{10,... | collective-permute-start | bytes 589832 | tf_op jit(solution)/shard_map/ppermute | solution.py:730
  92.6 14.4 %collective-permute-start.13 = (bf16[2,192,256]{2,1,0:T(8,128)(2,1)}, bf16[2,192,256]{2,1,0:T(8,128)(2,1)S(1)}, u32[]{:S(2)}, u32[]{:S(2)}) collective-permute-start(bf16[2,192,256]{2,1,0:T(8,128)(2,1)} %get-tuple-element.71), channel_id=1, source_target_pairs={{0,3},{1,4},{2,5},{3,6},{4,7},{5,0},{6,1},{7,2},{8,11},{9,12},{10,... | collective-permute-start | bytes 589832 | tf_op jit(solution)/shard_map/ppermute | solution.py:730
  93.3 13.9 %collective-permute-start.14 = (bf16[2,192,256]{2,1,0:T(8,128)(2,1)}, bf16[2,192,256]{2,1,0:T(8,128)(2,1)S(1)}, u32[]{:S(2)}, u32[]{:S(2)}) collective-permute-start(bf16[2,192,256]{2,1,0:T(8,128)(2,1)} %get-tuple-element.72), channel_id=1, source_target_pairs={{0,4},{1,5},{2,6},{3,7},{4,0},{5,1},{6,2},{7,3},{8,12},{9,13},{10,... | collective-permute-start | bytes 589832 | tf_op jit(solution)/shard_map/ppermute | solution.py:730
  94.8 14.8 %collective-permute-start.15 = (bf16[2,192,256]{2,1,0:T(8,128)(2,1)}, bf16[2,192,256]{2,1,0:T(8,128)(2,1)S(1)}, u32[]{:S(2)}, u32[]{:S(2)}) collective-permute-start(bf16[2,192,256]{2,1,0:T(8,128)(2,1)} %get-tuple-element.73), channel_id=1, source_target_pairs={{0,5},{1,6},{2,7},{3,0},{4,1},{5,2},{6,3},{7,4},{8,13},{9,14},{10,... | collective-permute-start | bytes 589832 | tf_op jit(solution)/shard_map/ppermute | solution.py:730
  98.1 11.5 %collective-permute-start.16 = (bf16[2,192,256]{2,1,0:T(8,128)(2,1)}, bf16[2,192,256]{2,1,0:T(8,128)(2,1)S(1)}, u32[]{:S(2)}, u32[]{:S(2)}) collective-permute-start(bf16[2,192,256]{2,1,0:T(8,128)(2,1)} %get-tuple-element.74), channel_id=1, source_target_pairs={{0,6},{1,7},{2,0},{3,1},{4,2},{5,3},{6,4},{7,5},{8,14},{9,15},{10,... | collective-permute-start | bytes 589832 | tf_op jit(solution)/shard_map/ppermute | solution.py:730
  99.4 10.2 %collective-permute-start.17 = (bf16[2,192,256]{2,1,0:T(8,128)(2,1)}, bf16[2,192,256]{2,1,0:T(8,128)(2,1)S(1)}, u32[]{:S(2)}, u32[]{:S(2)}) collective-permute-start(bf16[2,192,256]{2,1,0:T(8,128)(2,1)} %get-tuple-element.75), channel_id=1, source_target_pairs={{0,7},{1,0},{2,1},{3,2},{4,3},{5,4},{6,5},{7,6},{8,15},{9,8},{10,9... | collective-permute-start | bytes 589832 | tf_op jit(solution)/shard_map/ppermute | solution.py:730
  121.1 42.4 %all-to-all-start.2 = ((bf16[4,2,2,192,256]{4,3,2,1,0:T(8,128)(2,1)}), bf16[4,2,2,192,256]{4,3,2,1,0:T(8,128)(2,1)}, u32[]{:S(2)}, u32[]{:S(2)}) async-start(bf16[4,2,2,192,256]{4,3,2,1,0:T(8,128)(2,1)} %bitcast.25), calls=%async_computation.2 | async-start | bytes 3145728 | tf_op jit(solution)/shard_map/all_to_all | solution.py:782
  163.5 41.6 %all-to-all-start.4 = ((bf16[4,2,2,192,256]{4,3,2,1,0:T(8,128)(2,1)}), bf16[4,2,2,192,256]{4,3,2,1,0:T(8,128)(2,1)}, u32[]{:S(2)}, u32[]{:S(2)}) async-start(bf16[4,2,2,192,256]{4,3,2,1,0:T(8,128)(2,1)} %copy-done.10), calls=%async_computation.4 | async-start | bytes 3145728 | tf_op jit(solution)/shard_map/all_to_all | solution.py:789
  205.1 40.9 %all-to-all-start.6 = ((bf16[4,2,2,192,256]{4,3,2,1,0:T(8,128)(2,1)}), bf16[4,2,2,192,256]{4,3,2,1,0:T(8,128)(2,1)}, u32[]{:S(2)}, u32[]{:S(2)}) async-start(bf16[4,2,2,192,256]{4,3,2,1,0:T(8,128)(2,1)} %copy-done.12), calls=%async_computation.6 | async-start | bytes 3145728 | tf_op jit(solution)/shard_map/all_to_all | solution.py:789
  209.4 29.6 %copy-start.1 = (f32[2,2,192,1024]{3,2,1,0:T(8,128)S(1)}, f32[2,2,192,1024]{3,2,1,0:T(8,128)}, u32[]{:S(2)}) copy-start(f32[2,2,192,1024]{3,2,1,0:T(8,128)} %copy-done) | copy-start | bytes 9437188
  209.5 29.5 %copy-start.3 = (f32[2,2,192,1024]{3,2,1,0:T(8,128)S(1)}, f32[2,2,192,1024]{3,2,1,0:T(8,128)}, u32[]{:S(2)}) copy-start(f32[2,2,192,1024]{3,2,1,0:T(8,128)} %copy-done.2) | copy-start | bytes 9437188
  216.8 7.6 %collective-permute-start.18 = (bf16[2,192,256]{2,1,0:T(8,128)(2,1)}, bf16[2,192,256]{2,1,0:T(8,128)(2,1)S(1)}, u32[]{:S(2)}, u32[]{:S(2)}) collective-permute-start(bf16[2,192,256]{2,1,0:T(8,128)(2,1)} %get-tuple-element.77), channel_id=1, source_target_pairs={{0,1},{1,2},{2,3},{3,4},{4,5},{5,6},{6,7},{7,0},{8,9},{9,10},{10,1... | collective-permute-start | bytes 589832 | tf_op jit(solution)/shard_map/ppermute | solution.py:730
  216.9 11.8 %collective-permute-start.19 = (bf16[2,192,256]{2,1,0:T(8,128)(2,1)}, bf16[2,192,256]{2,1,0:T(8,128)(2,1)S(1)}, u32[]{:S(2)}, u32[]{:S(2)}) collective-permute-start(bf16[2,192,256]{2,1,0:T(8,128)(2,1)} %get-tuple-element.78), channel_id=1, source_target_pairs={{0,2},{1,3},{2,4},{3,5},{4,6},{5,7},{6,0},{7,1},{8,10},{9,11},{10,... | collective-permute-start | bytes 589832 | tf_op jit(solution)/shard_map/ppermute | solution.py:730
  221.3 13.2 %collective-permute-start.20 = (bf16[2,192,256]{2,1,0:T(8,128)(2,1)}, bf16[2,192,256]{2,1,0:T(8,128)(2,1)S(1)}, u32[]{:S(2)}, u32[]{:S(2)}) collective-permute-start(bf16[2,192,256]{2,1,0:T(8,128)(2,1)} %get-tuple-element.79), channel_id=1, source_target_pairs={{0,3},{1,4},{2,5},{3,6},{4,7},{5,0},{6,1},{7,2},{8,11},{9,12},{10,... | collective-permute-start | bytes 589832 | tf_op jit(solution)/shard_map/ppermute | solution.py:730
  223.3 11.4 %collective-permute-start.21 = (bf16[2,192,256]{2,1,0:T(8,128)(2,1)}, bf16[2,192,256]{2,1,0:T(8,128)(2,1)S(1)}, u32[]{:S(2)}, u32[]{:S(2)}) collective-permute-start(bf16[2,192,256]{2,1,0:T(8,128)(2,1)} %get-tuple-element.80), channel_id=1, source_target_pairs={{0,4},{1,5},{2,6},{3,7},{4,0},{5,1},{6,2},{7,3},{8,12},{9,13},{10,... | collective-permute-start | bytes 589832 | tf_op jit(solution)/shard_map/ppermute | solution.py:730
  224.2 13.1 %collective-permute-start.22 = (bf16[2,192,256]{2,1,0:T(8,128)(2,1)}, bf16[2,192,256]{2,1,0:T(8,128)(2,1)S(1)}, u32[]{:S(2)}, u32[]{:S(2)}) collective-permute-start(bf16[2,192,256]{2,1,0:T(8,128)(2,1)} %get-tuple-element.81), channel_id=1, source_target_pairs={{0,5},{1,6},{2,7},{3,0},{4,1},{5,2},{6,3},{7,4},{8,13},{9,14},{10,... | collective-permute-start | bytes 589832 | tf_op jit(solution)/shard_map/ppermute | solution.py:730
  224.4 20.9 %copy-start.15 = (bf16[2,192,256]{2,1,0:T(8,128)(2,1)}, bf16[2,192,256]{2,1,0:T(8,128)(2,1)S(1)}, u32[]{:S(2)}) copy-start(bf16[2,192,256]{2,1,0:T(8,128)(2,1)S(1)} %collective-permute-done.18.refs_5_.refs_1_) | copy-start | bytes 589828
  224.5 12.9 %collective-permute-start.23 = (bf16[2,192,256]{2,1,0:T(8,128)(2,1)}, bf16[2,192,256]{2,1,0:T(8,128)(2,1)S(1)}, u32[]{:S(2)}, u32[]{:S(2)}) collective-permute-start(bf16[2,192,256]{2,1,0:T(8,128)(2,1)} %get-tuple-element.82), channel_id=1, source_target_pairs={{0,6},{1,7},{2,0},{3,1},{4,2},{5,3},{6,4},{7,5},{8,14},{9,15},{10,... | collective-permute-start | bytes 589832 | tf_op jit(solution)/shard_map/ppermute | solution.py:730
  228.7 16.7 %copy-start.16 = (bf16[2,192,256]{2,1,0:T(8,128)(2,1)}, bf16[2,192,256]{2,1,0:T(8,128)(2,1)S(1)}, u32[]{:S(2)}) copy-start(bf16[2,192,256]{2,1,0:T(8,128)(2,1)S(1)} %collective-permute-done.19.refs_6_.refs_2_) | copy-start | bytes 589828
  228.7 10.3 %collective-permute-start.24 = (bf16[2,192,256]{2,1,0:T(8,128)(2,1)}, bf16[2,192,256]{2,1,0:T(8,128)(2,1)S(1)}, u32[]{:S(2)}, u32[]{:S(2)}) collective-permute-start(bf16[2,192,256]{2,1,0:T(8,128)(2,1)} %get-tuple-element.83), channel_id=1, source_target_pairs={{0,7},{1,0},{2,1},{3,2},{4,3},{5,4},{6,5},{7,6},{8,15},{9,8},{10,9... | collective-permute-start | bytes 589832 | tf_op jit(solution)/shard_map/ppermute | solution.py:730
  246.0 41.6 %all-to-all-start.5 = ((bf16[4,2,2,192,256]{4,3,2,1,0:T(8,128)(2,1)}), bf16[4,2,2,192,256]{4,3,2,1,0:T(8,128)(2,1)S(1)}, u32[]{:S(2)}, u32[]{:S(2)}) async-start(bf16[4,2,2,192,256]{4,3,2,1,0:T(8,128)(2,1)} %curl_inverse.5), calls=%async_computation.5 | async-start | bytes 3145728 | tf_op jit(solution)/shard_map/all_to_all | solution.py:789
  263.0 8.9 %collective-permute-start.25 = (bf16[2,192,256]{2,1,0:T(8,128)(2,1)}, bf16[2,192,256]{2,1,0:T(8,128)(2,1)S(1)}, u32[]{:S(2)}, u32[]{:S(2)}) collective-permute-start(bf16[2,192,256]{2,1,0:T(8,128)(2,1)} %get-tuple-element.86), channel_id=1, source_target_pairs={{0,1},{1,2},{2,3},{3,4},{4,5},{5,6},{6,7},{7,0},{8,9},{9,10},{10,1... | collective-permute-start | bytes 589832 | tf_op jit(solution)/shard_map/ppermute | solution.py:730
  263.1 11.1 %collective-permute-start.26 = (bf16[2,192,256]{2,1,0:T(8,128)(2,1)}, bf16[2,192,256]{2,1,0:T(8,128)(2,1)S(1)}, u32[]{:S(2)}, u32[]{:S(2)}) collective-permute-start(bf16[2,192,256]{2,1,0:T(8,128)(2,1)} %get-tuple-element.87), channel_id=1, source_target_pairs={{0,2},{1,3},{2,4},{3,5},{4,6},{5,7},{6,0},{7,1},{8,10},{9,11},{10,... | collective-permute-start | bytes 589832 | tf_op jit(solution)/shard_map/ppermute | solution.py:730
  266.8 19.6 %collective-permute-start.27 = (bf16[2,192,256]{2,1,0:T(8,128)(2,1)}, bf16[2,192,256]{2,1,0:T(8,128)(2,1)S(1)}, u32[]{:S(2)}, u32[]{:S(2)}) collective-permute-start(bf16[2,192,256]{2,1,0:T(8,128)(2,1)} %get-tuple-element.88), channel_id=1, source_target_pairs={{0,3},{1,4},{2,5},{3,6},{4,7},{5,0},{6,1},{7,2},{8,11},{9,12},{10,... | collective-permute-start | bytes 589832 | tf_op jit(solution)/shard_map/ppermute | solution.py:730
  268.8 17.6 %collective-permute-start.28 = (bf16[2,192,256]{2,1,0:T(8,128)(2,1)}, bf16[2,192,256]{2,1,0:T(8,128)(2,1)S(1)}, u32[]{:S(2)}, u32[]{:S(2)}) collective-permute-start(bf16[2,192,256]{2,1,0:T(8,128)(2,1)} %get-tuple-element.89), channel_id=1, source_target_pairs={{0,4},{1,5},{2,6},{3,7},{4,0},{5,1},{6,2},{7,3},{8,12},{9,13},{10,... | collective-permute-start | bytes 589832 | tf_op jit(solution)/shard_map/ppermute | solution.py:730
  269.6 16.8 %collective-permute-start.29 = (bf16[2,192,256]{2,1,0:T(8,128)(2,1)}, bf16[2,192,256]{2,1,0:T(8,128)(2,1)S(1)}, u32[]{:S(2)}, u32[]{:S(2)}) collective-permute-start(bf16[2,192,256]{2,1,0:T(8,128)(2,1)} %get-tuple-element.90), channel_id=1, source_target_pairs={{0,5},{1,6},{2,7},{3,0},{4,1},{5,2},{6,3},{7,4},{8,13},{9,14},{10,... | collective-permute-start | bytes 589832 | tf_op jit(solution)/shard_map/ppermute | solution.py:730
  271.9 14.5 %collective-permute-start.30 = (bf16[2,192,256]{2,1,0:T(8,128)(2,1)}, bf16[2,192,256]{2,1,0:T(8,128)(2,1)S(1)}, u32[]{:S(2)}, u32[]{:S(2)}) collective-permute-start(bf16[2,192,256]{2,1,0:T(8,128)(2,1)} %get-tuple-element.91), channel_id=1, source_target_pairs={{0,6},{1,7},{2,0},{3,1},{4,2},{5,3},{6,4},{7,5},{8,14},{9,15},{10,... | collective-permute-start | bytes 589832 | tf_op jit(solution)/shard_map/ppermute | solution.py:730
  274.1 12.3 %collective-permute-start.31 = (bf16[2,192,256]{2,1,0:T(8,128)(2,1)}, bf16[2,192,256]{2,1,0:T(8,128)(2,1)S(1)}, u32[]{:S(2)}, u32[]{:S(2)}) collective-permute-start(bf16[2,192,256]{2,1,0:T(8,128)(2,1)} %get-tuple-element.92), channel_id=1, source_target_pairs={{0,7},{1,0},{2,1},{3,2},{4,3},{5,4},{6,5},{7,6},{8,15},{9,8},{10,9... | collective-permute-start | bytes 589832 | tf_op jit(solution)/shard_map/ppermute | solution.py:730
  296.1 26.9 %all-to-all-start.7 = ((bf16[8,2,192,256]{3,2,1,0:T(8,128)(2,1)}), bf16[8,2,192,256]{3,2,1,0:T(8,128)(2,1)S(1)}, u32[]{:S(2)}, u32[]{:S(2)}) async-start(bf16[8,2,192,256]{3,2,1,0:T(8,128)(2,1)} %y_inverse.5.refs_13_), calls=%async_computation.7 | async-start | bytes 3145728 | tf_op jit(solution)/shard_map/all_to_all | solution.py:800
  329.3 17.4 %collective-permute-start.34 = (bf16[3,16,256]{2,1,0:T(8,128)(2,1)}, bf16[3,16,256]{2,1,0:T(8,128)(2,1)S(1)}, u32[]{:S(2)}, u32[]{:S(2)}) collective-permute-start(bf16[3,16,256]{2,1,0:T(8,128)(2,1)} %get-tuple-element.108), channel_id=1, source_target_pairs={{0,1},{1,2},{2,3},{3,4},{4,5},{5,6},{6,7},{7,0},{8,9},{9,10},{10,1... | collective-permute-start | bytes 73736 | tf_op jit(solution)/shard_map/ppermute | solution.py:472
  329.3 17.4 %collective-permute-start.35 = (bf16[3,16,256]{2,1,0:T(8,128)(2,1)}, bf16[3,16,256]{2,1,0:T(8,128)(2,1)S(1)}, u32[]{:S(2)}, u32[]{:S(2)}) collective-permute-start(bf16[3,16,256]{2,1,0:T(8,128)(2,1)} %get-tuple-element.109), channel_id=1, source_target_pairs={{1,0},{2,1},{3,2},{4,3},{5,4},{6,5},{7,6},{0,7},{9,8},{10,9},{11,1... | collective-permute-start | bytes 73736 | tf_op jit(solution)/shard_map/ppermute | solution.py:472
  332.0 14.7 %collective-permute-start.32 = (bf16[3,16,192]{2,1,0:T(8,128)(2,1)}, bf16[3,16,192]{2,1,0:T(8,128)(2,1)S(1)}, u32[]{:S(2)}, u32[]{:S(2)}) collective-permute-start(bf16[3,16,192]{2,1,0:T(8,128)(2,1)} %get-tuple-element.106), channel_id=1, source_target_pairs={{0,8},{8,16},{16,24},{24,0},{1,9},{9,17},{17,25},{25,1},{2,10},{10... | collective-permute-start | bytes 55304 | tf_op jit(solution)/shard_map/ppermute | solution.py:472
  332.0 14.7 %collective-permute-start.33 = (bf16[3,16,192]{2,1,0:T(8,128)(2,1)}, bf16[3,16,192]{2,1,0:T(8,128)(2,1)S(1)}, u32[]{:S(2)}, u32[]{:S(2)}) collective-permute-start(bf16[3,16,192]{2,1,0:T(8,128)(2,1)} %get-tuple-element.107), channel_id=1, source_target_pairs={{8,0},{16,8},{24,16},{0,24},{9,1},{17,9},{25,17},{1,25},{10,2},{18... | collective-permute-start | bytes 55304 | tf_op jit(solution)/shard_map/ppermute | solution.py:472
  (52 other events, 224.6 us)

commit v10 on v9

--- a/solution.py
+++ b/solution.py
@@ -236,7 +236,7 @@
             pltpu.SemaphoreType.DMA((size_y * planes,)),
             pltpu.SemaphoreType.DMA((blocks,)),
         ],
-        compiler_params=params(),
+        compiler_params=params(24),
         cost_estimate=takes(5),
         name="y_transform",
     )(me, table, *columns, *after)
@@ -298,7 +298,7 @@
             pltpu.SemaphoreType.DMA((blocks * halves * planes,)),
             pltpu.SemaphoreType.DMA((size_y,)),
         ],
-        compiler_params=params(),
+        compiler_params=params(24),
         cost_estimate=takes(4),
         name="y_inverse",
     )(me, table, modes, *after)
@@ -565,29 +565,39 @@
     return jnp.where(row == 0, low * -0.5, 0.0) + jnp.where(row == height - 1, high * 0.5, 0.0)
 
 
-LAYERS = 2
+LAYERS = 4
 
 
 def grad_vort_kernel(
-    component, slope_x, slope_y, velocity, adjoint, low_x, high_x, low_y, high_y, *refs
+    component,
+    slope_x,
+    slope_y,
+    velocity,
+    velocity_above,
+    velocity_below,
+    adjoint,
+    low_x,
+    high_x,
+    low_y,
+    high_y,
+    *refs,
 ):
     before, after = refs
     height, width = velocity.shape[2], velocity.shape[3]
     first = pl.program_id(0) * LAYERS
     ends = spread_columns(low_x[0], high_x[0], first, LAYERS, width)
-    layers = velocity[0, pl.ds(first, LAYERS)]
+    layers = velocity[0]
     stacked = layers.reshape(LAYERS * height, width)
+    deep = [velocity_below[0, 0]] + [layers[k] for k in range(LAYERS)] + [velocity_above[0, 0]]
     inner = jnp.dot(stacked, slope_x[...], preferred_element_type=f32)
     for k in range(LAYERS):
         n = first + k
-        above = lax.rem(n + 1, Z)
-        below = lax.rem(n + Z - 1, Z)
         value = adjoint[k]
         half = value * step_size
         along_x = inner[k * height : (k + 1) * height] + ends[k]
         along_y = jnp.dot(slope_y[...], layers[k], preferred_element_type=f32)
         along_y = along_y + end_rows(pick_row(low_y[0], n), pick_row(high_y[0], n), height)
-        along_z = (velocity[0, above].astype(f32) - velocity[0, below].astype(f32)) * 0.5
+        along_z = (deep[k + 2].astype(f32) - deep[k].astype(f32)) * 0.5
         for j, slope in enumerate((along_x, along_y, along_z)):
             term = half * slope
             if j == component:
@@ -604,11 +614,15 @@
     column = pl.BlockSpec((1, Z, height), lambda n: (component, 0, 0))
     row = pl.BlockSpec((1, Z, width), lambda n: (component, 0, 0))
     sums = pl.BlockSpec((3, LAYERS, height, width), lambda n: (0, n, 0, 0))
-    operands = [slope_x, slope_y, velocity, adjoint, *halos]
+    layer_above = lambda n: lax.rem((n + 1) * LAYERS, Z)
+    layer_below = lambda n: lax.rem(n * LAYERS + Z - 1, Z)
+    operands = [slope_x, slope_y, velocity, velocity, velocity, adjoint, *halos]
     in_specs = [
         whole((width, width)),
         whole((height, height)),
-        pl.BlockSpec((1, Z, height, width), lambda n: (component, 0, 0, 0)),
+        pl.BlockSpec((1, LAYERS, height, width), lambda n: (component, n, 0, 0)),
+        pl.BlockSpec((1, 1, height, width), lambda n: (component, layer_above(n), 0, 0)),
+        pl.BlockSpec((1, 1, height, width), lambda n: (component, layer_below(n), 0, 0)),
         pl.BlockSpec((LAYERS, height, width), lambda n: (n, 0, 0)),
         column,
         column,
@@ -620,7 +634,7 @@
         in_specs.append(sums)
 
     def kernel(*refs):
-        grad_vort_kernel(component, *refs[:8], None if before is None else refs[8], refs[-1])
+        grad_vort_kernel(component, *refs[:10], None if before is None else refs[10], refs[-1])
 
     return pl.pallas_call(
         kernel,
@@ -819,8 +833,8 @@
     adjoint_one, short_one, *edges = make_adjoint(me, layers_one, cot_vort, one, [], ())
     rows_two = rows_of(two, back(curl_two), (adjoint_one,))
     layers_two = layers_of(rows_two)
+    rows_three = rows_of(three, back(curl_three), tuple(layers_two))
     grad_vort = vort_of(one, adjoint_one, None, (rows_two[0],))
-    rows_three = rows_of(three, back(curl_three), tuple(layers_two) + (grad_vort,))
     adjoint_two, short_two, *edges = make_adjoint(
         me, layers_two, cot_vort, two, edges, (rows_three[0],)
     )

time: 365 us -> 368 us (level)
  local copies, waits for them, and re-layouts: 18.7 us -> 28.6 us
  starting transfers between devices: 94.9 us -> 89.6 us
  Pallas kernels: 137 us -> 132 us
  waiting for transfers between devices: 109 us -> 113 us
    ppermute x28, waiting for transfers between devices: 27.6 us -> 38 us  [shifted(): lax.ppermute(parts[s], axis, [(i, (i + s) % count) for i in range(count)])]
    unnamed x116 -> x120, local copies, waits for them, and re-layouts: 16.7 us -> 26.6 us
    ppermute x28, starting transfers between devices: 43.3 us -> 37.7 us  [shifted(): lax.ppermute(parts[s], axis, [(i, (i + s) % count) for i in range(count)])]
    pallas_call x3, Pallas kernels: 28.7 us -> 23.1 us  [add_grad_vort(): pl.pallas_call(kernel, grid=(Z // LAYERS,), in_specs=in_specs + tied(afte...]
    all_to_all x1, waiting for transfers between devices: 6.15 us -> 1.51 us  [layers_of(): lax.all_to_all(rows[0], 'gy', 0, 0, tiled=True).reshape(Z, height, width)]
  transfers between devices with their start and end apart: 44 -> 44, of which waited for: 25 -> 27; matrix products, arithmetic and copies ran while one was open for 1% -> 1% of each run, Pallas kernels for 28% -> 26%
where the time goes in v10:
time: 368 us; the launch traced here: 366 us
  Pallas kernels  132 us (36%)
  waiting for transfers between devices  113 us (31%)
  starting transfers between devices  89.6 us (24%)
  local copies, waits for them, and re-layouts  28.6 us (8%)
    ppermute x28, waiting for transfers between devices, shifted(): lax.ppermute(parts[s], axis, [(i, (i + s) % count) for i in range(count)])  38 us
    ppermute x28, starting transfers between devices, shifted(): lax.ppermute(parts[s], axis, [(i, (i + s) % count) for i in range(count)])  37.7 us
    all_to_all x3, waiting for transfers between devices, spectrum(): lines = lax.all_to_all(sent[place], 'gx', 0, 0, tiled=True)  28.4 us
    all_to_all x3, waiting for transfers between devices, back(): parts = lax.all_to_all(filtered, 'gx', 0, 0, tiled=True)  26.7 us
    unnamed x120, local copies, waits for them, and re-layouts  26.6 us
    pallas_call x3, Pallas kernels, add_grad_vort(): pl.pallas_call(kernel, grid=(Z // LAYERS,), in_specs=in_specs + tied(afte...  23.1 us
    pallas_call x3, Pallas kernels, y_inverse(): pl.pallas_call(kernel, in_specs=[pl.BlockSpec(memory_space=pltpu.SMEM), a...  22.8 us
    pallas_call x3, Pallas kernels, y_transform(): pl.pallas_call(kernel, in_specs=[pl.BlockSpec(memory_space=pltpu.SMEM), a...  21.2 us
  transfers between devices with their start and end apart: 44, of which 27 were waited for; matrix products, arithmetic and copies ran while one was open for 1% of the time, Pallas kernels for 26%

profile of v10, /device:TPU:0, one launch (start us, length us, event | category | flops | bytes accessed | tf_op | source)
XLA Modules:
  0.0 366.2 jit_solution(6729319652728910871)
XLA Ops:
  0.6 3.2 depth_transform.3.refs_0_
  3.8 5.2 %all-to-all-start = ((bf16[8,2,192,256]{3,2,1,0:T(8,128)(2,1)}), bf16[8,2,192,256]{3,2,1,0:T(8,128)(2,1)S(1)}, u32[]{:S(2)}, u32[]{:S(2)}) async-start(bf16[8,2,192,256]{3,2,1,0:T(8,128)(2,1)} %bitcast.31), calls=%async_computation | async-start | bytes 3145728 | tf_op jit(solution)/shard_map/all_to_all | solution.py:785
  11.5 4.6 %edge_columns.2 = (bf16[3,16,192]{2,1,0:T(8,128)(2,1)}, bf16[3,16,192]{2,1,0:T(8,128)(2,1)}) custom-call(bf16[3,16,192,256]{3,2,1,0:T(8,128)(2,1)} %refs_4_.5, bf16[16,192,256]{2,1,0:T(8,128)(2,1)} %depth_transform.3.refs_0_), custom_call_target="tpu_custom_call" | custom-call | flops 1 | bytes 12000000 | tf_op jit(solution)/shard_map/edge_columns/pallas_call | solution.py:456
  16.9 3.7 collective-permute-start.1
  22.1 4.9 %collective-permute-done.refs_1_.refs_6_.refs_13_ = bf16[4,16,192]{2,1,0:T(8,128)(2,1)S(1)} collective-permute-done((bf16[4,16,192]{2,1,0:T(8,128)(2,1)S(1)}, bf16[4,16,192]{2,1,0:T(8,128)(2,1)S(1)}, u32[]{:S(2)}, u32[]{:S(2)}) %collective-permute-start) | collective-permute-done | bytes 24608 | tf_op jit(solution)/shard_map/ppermute | solution.py:472
  27.1 2.9 all-to-all-done.refs_0_
  32.3 7.0 %y_transform.3 = bf16[4,1,2,2,192,256]{5,4,3,2,1,0:T(8,128)(2,1)} custom-call(s32[1]{0:T(128)} %bitcast.me_ref.refs_0_, bf16[1536,1536]{1,0:T(8,128)(2,1)S(1)} %copy-done.2, bf16[8,2,192,256]{3,2,1,0:T(8,128)(2,1)S(1)} %all-to-all-done.refs_0_, bf16[4,16,192]{2,1,0:T(8,128)(2,1)S(1)} %collective-permute-done.refs_1_.refs_6_.refs_13_, ...), custom_call_target="tpu_custom_call" | custom-call | flops 1 | bytes 15000000 | tf_op jit(solution)/shard_map/y_transform/pallas_call | solution.py:224
  39.4 4.9 %all-to-all-start.1 = ((bf16[4,2,2,192,256]{4,3,2,1,0:T(8,128)(2,1)}), bf16[4,2,2,192,256]{4,3,2,1,0:T(8,128)(2,1)S(1)}, u32[]{:S(2)}, u32[]{:S(2)}) async-start(bf16[4,2,2,192,256]{4,3,2,1,0:T(8,128)(2,1)} %bitcast.3.refs_2_), calls=%async_computation.1 | async-start | bytes 3145728 | tf_op jit(solution)/shard_map/all_to_all | solution.py:796
  46.4 3.4 depth_transform.4
  53.1 9.4 %collective-permute-done.9.refs_8_.refs_15_ = bf16[4,16,256]{2,1,0:T(8,128)(2,1)S(1)} collective-permute-done((bf16[4,16,256]{2,1,0:T(8,128)(2,1)S(1)}, bf16[4,16,256]{2,1,0:T(8,128)(2,1)S(1)}, u32[]{:S(2)}, u32[]{:S(2)}) %collective-permute-start.9) | collective-permute-done | bytes 32800 | tf_op jit(solution)/shard_map/ppermute | solution.py:472
  65.8 3.2 collective-permute-done.5.refs_4_
  73.8 7.1 %y_transform.4 = bf16[4,1,2,2,192,256]{5,4,3,2,1,0:T(8,128)(2,1)} custom-call(s32[1]{0:T(128)} %bitcast.me_ref.refs_0_, bf16[1536,1536]{1,0:T(8,128)(2,1)S(1)} %bitcast.25, bf16[2,192,256]{2,1,0:T(8,128)(2,1)S(1)} %copy-done.43, bf16[2,192,256]{2,1,0:T(8,128)(2,1)S(1)} %collective-permute-done.2.refs_1_, ...), custom_call_target="tpu_custom_call" | custom-call | flops 1 | bytes 15000000 | tf_op jit(solution)/shard_map/y_transform/pallas_call | solution.py:224
  82.1 5.2 %all-to-all-start.3 = ((bf16[4,2,2,192,256]{4,3,2,1,0:T(8,128)(2,1)}), bf16[4,2,2,192,256]{4,3,2,1,0:T(8,128)(2,1)}, u32[]{:S(2)}, u32[]{:S(2)}) async-start(bf16[4,2,2,192,256]{4,3,2,1,0:T(8,128)(2,1)} %bitcast.8.refs_0_.refs_2_), calls=%async_computation.3 | async-start | bytes 3145728 | tf_op jit(solution)/shard_map/all_to_all | solution.py:796
  87.3 3.5 depth_transform.5
  92.5 4.1 %collective-permute-start.12 = (bf16[2,192,256]{2,1,0:T(8,128)(2,1)}, bf16[2,192,256]{2,1,0:T(8,128)(2,1)S(1)}, u32[]{:S(2)}, u32[]{:S(2)}) collective-permute-start(bf16[2,192,256]{2,1,0:T(8,128)(2,1)} %get-tuple-element.70), channel_id=1, source_target_pairs={{0,2},{1,3},{2,4},{3,5},{4,6},{5,7},{6,0},{7,1},{8,10},{9,11},{10,... | collective-permute-start | bytes 589832 | tf_op jit(solution)/shard_map/ppermute | solution.py:744
  99.3 2.7 collective-permute-done.11.refs_1_
  105.5 5.3 %collective-permute-done.13.refs_3_ = bf16[2,192,256]{2,1,0:T(8,128)(2,1)S(1)} collective-permute-done((bf16[2,192,256]{2,1,0:T(8,128)(2,1)}, bf16[2,192,256]{2,1,0:T(8,128)(2,1)S(1)}, u32[]{:S(2)}, u32[]{:S(2)}) %collective-permute-start.13) | collective-permute-done | bytes 196640 | tf_op jit(solution)/shard_map/ppermute | solution.py:744
  114.6 7.1 %y_transform.5 = bf16[4,1,2,2,192,256]{5,4,3,2,1,0:T(8,128)(2,1)S(1)} custom-call(s32[1]{0:T(128)} %bitcast.me_ref.refs_0_, bf16[1536,1536]{1,0:T(8,128)(2,1)S(1)} %bitcast.27, bf16[2,192,256]{2,1,0:T(8,128)(2,1)S(1)} %copy-done.44, bf16[2,192,256]{2,1,0:T(8,128)(2,1)S(1)} %collective-permute-done.11.refs_1_, ...), custom_call_target="tpu_custom_call" | custom-call | flops 1 | bytes 15000000 | tf_op jit(solution)/shard_map/y_transform/pallas_call | solution.py:224
  125.1 4.5 %all-to-all-start.2 = ((bf16[4,2,2,192,256]{4,3,2,1,0:T(8,128)(2,1)}), bf16[4,2,2,192,256]{4,3,2,1,0:T(8,128)(2,1)}, u32[]{:S(2)}, u32[]{:S(2)}) async-start(bf16[4,2,2,192,256]{4,3,2,1,0:T(8,128)(2,1)} %bitcast.28), calls=%async_computation.2 | async-start | bytes 3145728 | tf_op jit(solution)/shard_map/all_to_all | solution.py:796
  133.2 3.9 %x_transform.4.refs_2_.refs_3_ = f32[2,2,192,1024]{3,2,1,0:T(8,128)S(1)} custom-call(bf16[1024,1024]{1,0:T(8,128)(2,1)S(1)} %copy-done.11, bf16[4,2,2,192,256]{4,3,2,1,0:T(8,128)(2,1)} %all-to-all-done.3.modes_ref, bf16[4,2,2,192,256]{4,3,2,1,0:T(8,128)(2,1)S(1)} %bitcast.29), custom_call_target="tpu_custom_call" | custom-call | flops 1 | bytes 9000000 | tf_op jit(solution)/shard_map/x_transform/pallas_call | solution.py:318
  137.1 2.9 curl_inverse.3.refs_0_
  141.2 26.2 %all-to-all-done.2.modes_ref = bf16[4,2,2,192,256]{4,3,2,1,0:T(8,128)(2,1)} async-done(((bf16[4,2,2,192,256]{4,3,2,1,0:T(8,128)(2,1)}), bf16[4,2,2,192,256]{4,3,2,1,0:T(8,128)(2,1)}, u32[]{:S(2)}, u32[]{:S(2)}) %all-to-all-start.2) | async-done | bytes 1572896 | tf_op jit(solution)/shard_map/all_to_all | solution.py:796
  167.4 4.3 %all-to-all-start.4 = ((bf16[4,2,2,192,256]{4,3,2,1,0:T(8,128)(2,1)}), bf16[4,2,2,192,256]{4,3,2,1,0:T(8,128)(2,1)}, u32[]{:S(2)}, u32[]{:S(2)}) async-start(bf16[4,2,2,192,256]{4,3,2,1,0:T(8,128)(2,1)} %copy-done.13), calls=%async_computation.4 | async-start | bytes 3145728 | tf_op jit(solution)/shard_map/all_to_all | solution.py:803
  174.8 3.3 x_transform.5.refs_2_.refs_3_
  178.1 3.0 curl_inverse.4.refs_0_
  183.9 25.1 %all-to-all-done.4 = bf16[4,2,2,192,256]{4,3,2,1,0:T(8,128)(2,1)} async-done(((bf16[4,2,2,192,256]{4,3,2,1,0:T(8,128)(2,1)}), bf16[4,2,2,192,256]{4,3,2,1,0:T(8,128)(2,1)}, u32[]{:S(2)}, u32[]{:S(2)}) %all-to-all-start.4) | async-done | bytes 1572896 | tf_op jit(solution)/shard_map/all_to_all | solution.py:803
  209.0 4.5 %all-to-all-start.6 = ((bf16[4,2,2,192,256]{4,3,2,1,0:T(8,128)(2,1)}), bf16[4,2,2,192,256]{4,3,2,1,0:T(8,128)(2,1)}, u32[]{:S(2)}, u32[]{:S(2)}) async-start(bf16[4,2,2,192,256]{4,3,2,1,0:T(8,128)(2,1)} %copy-done.15), calls=%async_computation.6 | async-start | bytes 3145728 | tf_op jit(solution)/shard_map/all_to_all | solution.py:803
  217.3 7.6 %y_inverse.3 = (bf16[2,192,256]{2,1,0:T(8,128)(2,1)S(1)}, bf16[2,192,256]{2,1,0:T(8,128)(2,1)S(1)}, bf16[2,192,256]{2,1,0:T(8,128)(2,1)S(1)}, bf16[2,192,256]{2,...) custom-call(s32[1]{0:T(128)} %bitcast.me_ref.refs_0_, ...), custom_call_target="tpu_custom_call" | custom-call | flops 1 | bytes 12000000 | tf_op jit(solution)/shard_map/y_inverse/pallas_call | solution.py:288
  225.0 4.3 %collective-permute-start.19 = (bf16[2,192,256]{2,1,0:T(8,128)(2,1)S(1)}, bf16[2,192,256]{2,1,0:T(8,128)(2,1)S(1)}, u32[]{:S(2)}, u32[]{:S(2)}) collective-permute-start(bf16[2,192,256]{2,1,0:T(8,128)(2,1)S(1)} %get-tuple-element.78), channel_id=1, source_target_pairs={{0,2},{1,3},{2,4},{3,5},{4,6},{5,7},{6,0},{7,1},{8,10},{9,11},{10,... | collective-permute-start | bytes 589832 | tf_op jit(solution)/shard_map/ppermute | solution.py:744
  232.2 4.1 %collective-permute-start.23 = (bf16[2,192,256]{2,1,0:T(8,128)(2,1)S(1)}, bf16[2,192,256]{2,1,0:T(8,128)(2,1)S(1)}, u32[]{:S(2)}, u32[]{:S(2)}) collective-permute-start(bf16[2,192,256]{2,1,0:T(8,128)(2,1)S(1)} %get-tuple-element.82), channel_id=1, source_target_pairs={{0,6},{1,7},{2,0},{3,1},{4,2},{5,3},{6,4},{7,5},{8,14},{9,15},{10,... | collective-permute-start | bytes 589832 | tf_op jit(solution)/shard_map/ppermute | solution.py:744
  236.2 3.6 collective-permute-start.24
  242.2 2.7 collective-permute-done.22.refs_9_.refs_5_
  246.6 3.0 curl_inverse.5
  251.5 5.2 %all-to-all-start.5 = ((bf16[4,2,2,192,256]{4,3,2,1,0:T(8,128)(2,1)}), bf16[4,2,2,192,256]{4,3,2,1,0:T(8,128)(2,1)S(1)}, u32[]{:S(2)}, u32[]{:S(2)}) async-start(bf16[4,2,2,192,256]{4,3,2,1,0:T(8,128)(2,1)} %copy-done.22), calls=%async_computation.5 | async-start | bytes 3145728 | tf_op jit(solution)/shard_map/all_to_all | solution.py:803
  256.7 5.4 %make_adjoint.3 = (f32[16,192,256]{2,1,0:T(8,128)}, bf16[16,192,256]{2,1,0:T(8,128)(2,1)}, bf16[3,16,192]{2,1,0:T(8,128)(2,1)}, bf16[3,16,192]{2,1,0:T(8,128)(2,...) custom-call(s32[1]{0:T(128)} %bitcast.me_ref.refs_0_, bf16[2,192,256]{2,1,0:T(8,128)(2,1)} %copy-done.28, ...), custom_call_target="tpu_custom_call" | custom-call | flops 1 | bytes 15000000 | tf_op jit(solution)/shard_map/make_adjoint/pallas_call | solution.py:523
  264.0 7.5 %y_inverse.4 = (bf16[2,192,256]{2,1,0:T(8,128)(2,1)S(1)}, bf16[2,192,256]{2,1,0:T(8,128)(2,1)S(1)}, bf16[2,192,256]{2,1,0:T(8,128)(2,1)S(1)}, bf16[2,192,256]{2,...) custom-call(s32[1]{0:T(128)} %bitcast.me_ref.refs_0_, ...), custom_call_target="tpu_custom_call" | custom-call | flops 1 | bytes 12000000 | tf_op jit(solution)/shard_map/y_inverse/pallas_call | solution.py:288
  271.6 3.6 collective-permute-start.26
  283.5 5.5 %collective-permute-done.27.refs_3_ = bf16[2,192,256]{2,1,0:T(8,128)(2,1)S(1)} collective-permute-done((bf16[2,192,256]{2,1,0:T(8,128)(2,1)S(1)}, bf16[2,192,256]{2,1,0:T(8,128)(2,1)S(1)}, u32[]{:S(2)}, u32[]{:S(2)}) %collective-permute-start.27) | collective-permute-done | bytes 196640 | tf_op jit(solution)/shard_map/ppermute | solution.py:744
  289.2 2.7 collective-permute-done.29.refs_5_
  295.9 7.7 %y_inverse.5.refs_13_ = bf16[8,2,192,256]{3,2,1,0:T(8,128)(2,1)} custom-call(s32[1]{0:T(128)} %bitcast.me_ref.refs_0_, bf16[1536,1536]{1,0:T(8,128)(2,1)S(1)} %copy-done.1, bf16[4,1,2,2,192,256]{5,4,3,2,1,0:T(8,128)(2,1)S(1)} %bitcast.30, bf16[2,192,256]{2,1,0:T(8,128)(2,1)S(1)} %get-tuple-element.85.refs_0_.refs_10_, ...), custom_call_target="tpu_custom_call" | custom-call | flops 1 | bytes 12000000 | tf_op jit(solution)/shard_map/y_inverse/pallas_call | solution.py:288
  303.7 5.2 %all-to-all-start.7 = ((bf16[8,2,192,256]{3,2,1,0:T(8,128)(2,1)}), bf16[8,2,192,256]{3,2,1,0:T(8,128)(2,1)S(1)}, u32[]{:S(2)}, u32[]{:S(2)}) async-start(bf16[8,2,192,256]{3,2,1,0:T(8,128)(2,1)} %y_inverse.5.refs_13_), calls=%async_computation.7 | async-start | bytes 3145728 | tf_op jit(solution)/shard_map/all_to_all | solution.py:814
  308.8 6.5 %add_grad_vort.3.refs_10_ = bf16[3,16,192,256]{3,2,1,0:T(8,128)(2,1)} custom-call(bf16[256,256]{1,0:T(8,128)(2,1)} %constant.37.clone.refs_0_, bf16[192,192]{1,0:T(8,128)(2,1)} %constant.38.clone.refs_1_, bf16[3,16,192,256]{3,2,1,0:T(8,128)(2,1)} %refs_4_.5, bf16[3,16,192,256]{3,2,1,0:T(8,128)(2,1)} %refs_4_.5, bf16[3,16,192,256]{3,2,1,0:T(8,128)(2,1)} %refs_4_.5, ...), custom_call_target="tpu_custom_call" | custom-call | flops 1 | bytes 27000000 | tf_op jit(solution)/shard_map/add_grad_vort/pallas_call | solution.py:639
  315.4 5.3 %make_adjoint.4 = (f32[16,192,256]{2,1,0:T(8,128)}, bf16[16,192,256]{2,1,0:T(8,128)(2,1)}, bf16[3,16,192]{2,1,0:T(8,128)(2,1)}, bf16[3,16,192]{2,1,0:T(8,128)(2,...) custom-call(s32[1]{0:T(128)} %bitcast.me_ref.refs_0_, ...), custom_call_target="tpu_custom_call", output_to_operand_aliasing={{2}: (10, {}), {3}: (11, {}), {4}: (12, {}), {5}: (13, {})} | custom-call | flops 1 | bytes 15000000 | tf_op jit(solution)/shard_map/make_adjoint/pallas_call | solution.py:523
  320.6 7.7 %add_grad_vort.4.refs_6_.refs_10_ = bf16[3,16,192,256]{3,2,1,0:T(8,128)(2,1)} custom-call(bf16[256,256]{1,0:T(8,128)(2,1)} %constant.37.clone.refs_0_, bf16[192,192]{1,0:T(8,128)(2,1)} %constant.38.clone.refs_1_, bf16[3,16,192,256]{3,2,1,0:T(8,128)(2,1)} %refs_4_.5, bf16[3,16,192,256]{3,2,1,0:T(8,128)(2,1)} %refs_4_.5, bf16[3,16,192,256]{3,2,1,0:T(8,128)(2,1)} %refs_4_.5, ...), custom_call_target="tpu_custom_call" | custom-call | flops 1 | bytes 27000000 | tf_op jit(solution)/shard_map/add_grad_vort/pallas_call | solution.py:639
  331.0 5.2 %make_adjoint.5 = (f32[16,192,256]{2,1,0:T(8,128)}, bf16[16,192,256]{2,1,0:T(8,128)(2,1)}, bf16[3,16,192]{2,1,0:T(8,128)(2,1)}, bf16[3,16,192]{2,1,0:T(8,128)(2,...) custom-call(s32[1]{0:T(128)} %bitcast.me_ref.refs_0_, ...), custom_call_target="tpu_custom_call", output_to_operand_aliasing={{2}: (3, {}), {3}: (4, {}), {4}: (5, {}), {5}: (6, {})} | custom-call | flops 1 | bytes 15000000 | tf_op jit(solution)/shard_map/make_adjoint/pallas_call | solution.py:523
  338.9 3.8 %collective-permute-start.33 = (bf16[3,16,192]{2,1,0:T(8,128)(2,1)}, bf16[3,16,192]{2,1,0:T(8,128)(2,1)S(1)}, u32[]{:S(2)}, u32[]{:S(2)}) collective-permute-start(bf16[3,16,192]{2,1,0:T(8,128)(2,1)} %get-tuple-element.107), channel_id=1, source_target_pairs={{8,0},{16,8},{24,16},{0,24},{9,1},{17,9},{25,17},{1,25},{10,2},{18... | collective-permute-start | bytes 55304 | tf_op jit(solution)/shard_map/ppermute | solution.py:472
  342.7 8.8 %add_grad_vort.5.refs_21_ = f32[3,16,192,256]{3,2,1,0:T(8,128)} custom-call(bf16[256,256]{1,0:T(8,128)(2,1)} %constant.37.clone.refs_0_, bf16[192,192]{1,0:T(8,128)(2,1)} %constant.38.clone.refs_1_, bf16[3,16,192,256]{3,2,1,0:T(8,128)(2,1)} %refs_4_.5, bf16[3,16,192,256]{3,2,1,0:T(8,128)(2,1)} %refs_4_.5, bf16[3,16,192,256]{3,2,1,0:T(8,128)(2,1)} %refs_4_.5, ...), custom_call_target="tpu_custom_call" | custom-call | flops 1 | bytes 27000000 | tf_op jit(solution)/shard_map/add_grad_vort/pallas_call | solution.py:639
  352.2 13.8 %write_grad_vel.1 = f32[3,16,192,256]{3,2,1,0:T(8,128)} custom-call(bf16[256,256]{1,0:T(8,128)(2,1)} %constant.37.clone.refs_0_, bf16[3,16,192,256]{3,2,1,0:T(8,128)(2,1)} %refs_3_.7, bf16[3,16,192,256]{3,2,1,0:T(8,128)(2,1)} %refs_3_.7, bf16[3,16,192,256]{3,2,1,0:T(8,128)(2,1)} %refs_3_.7, bf16[16,192,256]{2,1,0:T(8,128)(2,1)} %get-tuple-element.103.refs_4_.refs_5_.refs_6_, ...), custom_call_target="tpu_custom_call" | custom-call | flops 1 | bytes 36000000 | tf_op jit(solution)/shard_map/write_grad_vel/pallas_call | solution.py:720
  (194 shorter events, 80.3 us)
Async XLA Ops:
  3.8 26.2 %all-to-all-start = ((bf16[8,2,192,256]{3,2,1,0:T(8,128)(2,1)}), bf16[8,2,192,256]{3,2,1,0:T(8,128)(2,1)S(1)}, u32[]{:S(2)}, u32[]{:S(2)}) async-start(bf16[8,2,192,256]{3,2,1,0:T(8,128)(2,1)} %bitcast.31), calls=%async_computation | async-start | bytes 3145728 | tf_op jit(solution)/shard_map/all_to_all | solution.py:785
  16.9 5.3 %collective-permute-start.1 = (bf16[4,16,192]{2,1,0:T(8,128)(2,1)S(1)}, bf16[4,16,192]{2,1,0:T(8,128)(2,1)S(1)}, u32[]{:S(2)}, u32[]{:S(2)}) collective-permute-start(bf16[4,16,192]{2,1,0:T(8,128)(2,1)S(1)} %pad_maximum_fusion.1), channel_id=1, source_target_pairs={{8,0},{16,8},{24,16},{0,24},{9,1},{17,9},{25,17},{1,25},{10,2},{18... | collective-permute-start | bytes 73736 | tf_op jit(solution)/shard_map/ppermute | solution.py:472
  21.3 5.8 %collective-permute-start = (bf16[4,16,192]{2,1,0:T(8,128)(2,1)S(1)}, bf16[4,16,192]{2,1,0:T(8,128)(2,1)S(1)}, u32[]{:S(2)}, u32[]{:S(2)}) collective-permute-start(bf16[4,16,192]{2,1,0:T(8,128)(2,1)S(1)} %pad_maximum_fusion), channel_id=1, source_target_pairs={{0,8},{8,16},{16,24},{24,0},{1,9},{9,17},{17,25},{25,1},{2,10},{10... | collective-permute-start | bytes 73736 | tf_op jit(solution)/shard_map/ppermute | solution.py:472
  39.4 41.5 %all-to-all-start.1 = ((bf16[4,2,2,192,256]{4,3,2,1,0:T(8,128)(2,1)}), bf16[4,2,2,192,256]{4,3,2,1,0:T(8,128)(2,1)S(1)}, u32[]{:S(2)}, u32[]{:S(2)}) async-start(bf16[4,2,2,192,256]{4,3,2,1,0:T(8,128)(2,1)} %bitcast.3.refs_2_), calls=%async_computation.1 | async-start | bytes 3145728 | tf_op jit(solution)/shard_map/all_to_all | solution.py:796
  49.8 13.3 %collective-permute-start.2 = (bf16[2,192,256]{2,1,0:T(8,128)(2,1)}, bf16[2,192,256]{2,1,0:T(8,128)(2,1)S(1)}, u32[]{:S(2)}, u32[]{:S(2)}) collective-permute-start(bf16[2,192,256]{2,1,0:T(8,128)(2,1)} %get-tuple-element.61), channel_id=1, source_target_pairs={{0,1},{1,2},{2,3},{3,4},{4,5},{5,6},{6,7},{7,0},{8,9},{9,10},{10,1... | collective-permute-start | bytes 589832 | tf_op jit(solution)/shard_map/ppermute | solution.py:744
  49.8 13.8 %collective-permute-start.3 = (bf16[2,192,256]{2,1,0:T(8,128)(2,1)}, bf16[2,192,256]{2,1,0:T(8,128)(2,1)S(1)}, u32[]{:S(2)}, u32[]{:S(2)}) collective-permute-start(bf16[2,192,256]{2,1,0:T(8,128)(2,1)} %get-tuple-element.62), channel_id=1, source_target_pairs={{0,2},{1,3},{2,4},{3,5},{4,6},{5,7},{6,0},{7,1},{8,10},{9,11},{10,... | collective-permute-start | bytes 589832 | tf_op jit(solution)/shard_map/ppermute | solution.py:744
  50.4 12.1 %collective-permute-start.9 = (bf16[4,16,256]{2,1,0:T(8,128)(2,1)S(1)}, bf16[4,16,256]{2,1,0:T(8,128)(2,1)S(1)}, u32[]{:S(2)}, u32[]{:S(2)}) collective-permute-start(bf16[4,16,256]{2,1,0:T(8,128)(2,1)S(1)} %pad_maximum_fusion.2), channel_id=1, source_target_pairs={{0,1},{1,2},{2,3},{3,4},{4,5},{5,6},{6,7},{7,0},{8,9},{9,10},{10,1... | collective-permute-start | bytes 98312 | tf_op jit(solution)/shard_map/ppermute | solution.py:472
  51.7 11.4 %collective-permute-start.10 = (bf16[4,16,256]{2,1,0:T(8,128)(2,1)S(1)}, bf16[4,16,256]{2,1,0:T(8,128)(2,1)S(1)}, u32[]{:S(2)}, u32[]{:S(2)}) collective-permute-start(bf16[4,16,256]{2,1,0:T(8,128)(2,1)S(1)} %pad_maximum_fusion.3), channel_id=1, source_target_pairs={{1,0},{2,1},{3,2},{4,3},{5,4},{6,5},{7,6},{0,7},{9,8},{10,9},{11,1... | collective-permute-start | bytes 98312 | tf_op jit(solution)/shard_map/ppermute | solution.py:472
  53.1 12.7 %collective-permute-start.4 = (bf16[2,192,256]{2,1,0:T(8,128)(2,1)}, bf16[2,192,256]{2,1,0:T(8,128)(2,1)S(1)}, u32[]{:S(2)}, u32[]{:S(2)}) collective-permute-start(bf16[2,192,256]{2,1,0:T(8,128)(2,1)} %get-tuple-element.63), channel_id=1, source_target_pairs={{0,3},{1,4},{2,5},{3,6},{4,7},{5,0},{6,1},{7,2},{8,11},{9,12},{10,... | collective-permute-start | bytes 589832 | tf_op jit(solution)/shard_map/ppermute | solution.py:744
  62.5 6.5 %collective-permute-start.5 = (bf16[2,192,256]{2,1,0:T(8,128)(2,1)}, bf16[2,192,256]{2,1,0:T(8,128)(2,1)S(1)}, u32[]{:S(2)}, u32[]{:S(2)}) collective-permute-start(bf16[2,192,256]{2,1,0:T(8,128)(2,1)} %get-tuple-element.64), channel_id=1, source_target_pairs={{0,4},{1,5},{2,6},{3,7},{4,0},{5,1},{6,2},{7,3},{8,12},{9,13},{10,... | collective-permute-start | bytes 589832 | tf_op jit(solution)/shard_map/ppermute | solution.py:744
  63.1 6.8 %collective-permute-start.6 = (bf16[2,192,256]{2,1,0:T(8,128)(2,1)}, bf16[2,192,256]{2,1,0:T(8,128)(2,1)S(1)}, u32[]{:S(2)}, u32[]{:S(2)}) collective-permute-start(bf16[2,192,256]{2,1,0:T(8,128)(2,1)} %get-tuple-element.65), channel_id=1, source_target_pairs={{0,5},{1,6},{2,7},{3,0},{4,1},{5,2},{6,3},{7,4},{8,13},{9,14},{10,... | collective-permute-start | bytes 589832 | tf_op jit(solution)/shard_map/ppermute | solution.py:744
  63.1 8.0 %collective-permute-start.7 = (bf16[2,192,256]{2,1,0:T(8,128)(2,1)}, bf16[2,192,256]{2,1,0:T(8,128)(2,1)S(1)}, u32[]{:S(2)}, u32[]{:S(2)}) collective-permute-start(bf16[2,192,256]{2,1,0:T(8,128)(2,1)} %get-tuple-element.66), channel_id=1, source_target_pairs={{0,6},{1,7},{2,0},{3,1},{4,2},{5,3},{6,4},{7,5},{8,14},{9,15},{10,... | collective-permute-start | bytes 589832 | tf_op jit(solution)/shard_map/ppermute | solution.py:744
  63.6 9.2 %collective-permute-start.8 = (bf16[2,192,256]{2,1,0:T(8,128)(2,1)}, bf16[2,192,256]{2,1,0:T(8,128)(2,1)S(1)}, u32[]{:S(2)}, u32[]{:S(2)}) collective-permute-start(bf16[2,192,256]{2,1,0:T(8,128)(2,1)} %get-tuple-element.67), channel_id=1, source_target_pairs={{0,7},{1,0},{2,1},{3,2},{4,3},{5,4},{6,5},{7,6},{8,15},{9,8},{10,9... | collective-permute-start | bytes 589832 | tf_op jit(solution)/shard_map/ppermute | solution.py:744
  82.1 31.5 %slice-start.4 = ((s8[4718592]{0:T(1024)(128)(4,1)}), s8[524288]{0:T(1024)(128)(4,1)S(1)}, s32[]{:S(2)}) async-start(s8[4718592]{0:T(1024)(128)(4,1)} %bitcast.26), calls=%async_computation.12 | async-start | bytes 1048576
  82.1 43.0 %all-to-all-start.3 = ((bf16[4,2,2,192,256]{4,3,2,1,0:T(8,128)(2,1)}), bf16[4,2,2,192,256]{4,3,2,1,0:T(8,128)(2,1)}, u32[]{:S(2)}, u32[]{:S(2)}) async-start(bf16[4,2,2,192,256]{4,3,2,1,0:T(8,128)(2,1)} %bitcast.8.refs_0_.refs_2_), calls=%async_computation.3 | async-start | bytes 3145728 | tf_op jit(solution)/shard_map/all_to_all | solution.py:796
  90.8 11.2 %collective-permute-start.11 = (bf16[2,192,256]{2,1,0:T(8,128)(2,1)}, bf16[2,192,256]{2,1,0:T(8,128)(2,1)S(1)}, u32[]{:S(2)}, u32[]{:S(2)}) collective-permute-start(bf16[2,192,256]{2,1,0:T(8,128)(2,1)} %get-tuple-element.69), channel_id=1, source_target_pairs={{0,1},{1,2},{2,3},{3,4},{4,5},{5,6},{6,7},{7,0},{8,9},{9,10},{10,1... | collective-permute-start | bytes 589832 | tf_op jit(solution)/shard_map/ppermute | solution.py:744
  92.5 10.7 %collective-permute-start.12 = (bf16[2,192,256]{2,1,0:T(8,128)(2,1)}, bf16[2,192,256]{2,1,0:T(8,128)(2,1)S(1)}, u32[]{:S(2)}, u32[]{:S(2)}) collective-permute-start(bf16[2,192,256]{2,1,0:T(8,128)(2,1)} %get-tuple-element.70), channel_id=1, source_target_pairs={{0,2},{1,3},{2,4},{3,5},{4,6},{5,7},{6,0},{7,1},{8,10},{9,11},{10,... | collective-permute-start | bytes 589832 | tf_op jit(solution)/shard_map/ppermute | solution.py:744
  96.6 14.2 %collective-permute-start.13 = (bf16[2,192,256]{2,1,0:T(8,128)(2,1)}, bf16[2,192,256]{2,1,0:T(8,128)(2,1)S(1)}, u32[]{:S(2)}, u32[]{:S(2)}) collective-permute-start(bf16[2,192,256]{2,1,0:T(8,128)(2,1)} %get-tuple-element.71), channel_id=1, source_target_pairs={{0,3},{1,4},{2,5},{3,6},{4,7},{5,0},{6,1},{7,2},{8,11},{9,12},{10,... | collective-permute-start | bytes 589832 | tf_op jit(solution)/shard_map/ppermute | solution.py:744
  97.3 13.7 %collective-permute-start.14 = (bf16[2,192,256]{2,1,0:T(8,128)(2,1)}, bf16[2,192,256]{2,1,0:T(8,128)(2,1)S(1)}, u32[]{:S(2)}, u32[]{:S(2)}) collective-permute-start(bf16[2,192,256]{2,1,0:T(8,128)(2,1)} %get-tuple-element.72), channel_id=1, source_target_pairs={{0,4},{1,5},{2,6},{3,7},{4,0},{5,1},{6,2},{7,3},{8,12},{9,13},{10,... | collective-permute-start | bytes 589832 | tf_op jit(solution)/shard_map/ppermute | solution.py:744
  98.8 14.8 %collective-permute-start.15 = (bf16[2,192,256]{2,1,0:T(8,128)(2,1)}, bf16[2,192,256]{2,1,0:T(8,128)(2,1)S(1)}, u32[]{:S(2)}, u32[]{:S(2)}) collective-permute-start(bf16[2,192,256]{2,1,0:T(8,128)(2,1)} %get-tuple-element.73), channel_id=1, source_target_pairs={{0,5},{1,6},{2,7},{3,0},{4,1},{5,2},{6,3},{7,4},{8,13},{9,14},{10,... | collective-permute-start | bytes 589832 | tf_op jit(solution)/shard_map/ppermute | solution.py:744
  102.0 11.6 %collective-permute-start.16 = (bf16[2,192,256]{2,1,0:T(8,128)(2,1)}, bf16[2,192,256]{2,1,0:T(8,128)(2,1)S(1)}, u32[]{:S(2)}, u32[]{:S(2)}) collective-permute-start(bf16[2,192,256]{2,1,0:T(8,128)(2,1)} %get-tuple-element.74), channel_id=1, source_target_pairs={{0,6},{1,7},{2,0},{3,1},{4,2},{5,3},{6,4},{7,5},{8,14},{9,15},{10,... | collective-permute-start | bytes 589832 | tf_op jit(solution)/shard_map/ppermute | solution.py:744
  103.3 10.4 %collective-permute-start.17 = (bf16[2,192,256]{2,1,0:T(8,128)(2,1)}, bf16[2,192,256]{2,1,0:T(8,128)(2,1)S(1)}, u32[]{:S(2)}, u32[]{:S(2)}) collective-permute-start(bf16[2,192,256]{2,1,0:T(8,128)(2,1)} %get-tuple-element.75), channel_id=1, source_target_pairs={{0,7},{1,0},{2,1},{3,2},{4,3},{5,4},{6,5},{7,6},{8,15},{9,8},{10,9... | collective-permute-start | bytes 589832 | tf_op jit(solution)/shard_map/ppermute | solution.py:744
  125.1 42.4 %all-to-all-start.2 = ((bf16[4,2,2,192,256]{4,3,2,1,0:T(8,128)(2,1)}), bf16[4,2,2,192,256]{4,3,2,1,0:T(8,128)(2,1)}, u32[]{:S(2)}, u32[]{:S(2)}) async-start(bf16[4,2,2,192,256]{4,3,2,1,0:T(8,128)(2,1)} %bitcast.28), calls=%async_computation.2 | async-start | bytes 3145728 | tf_op jit(solution)/shard_map/all_to_all | solution.py:796
  167.4 41.6 %all-to-all-start.4 = ((bf16[4,2,2,192,256]{4,3,2,1,0:T(8,128)(2,1)}), bf16[4,2,2,192,256]{4,3,2,1,0:T(8,128)(2,1)}, u32[]{:S(2)}, u32[]{:S(2)}) async-start(bf16[4,2,2,192,256]{4,3,2,1,0:T(8,128)(2,1)} %copy-done.13), calls=%async_computation.4 | async-start | bytes 3145728 | tf_op jit(solution)/shard_map/all_to_all | solution.py:803
  209.0 37.6 %copy-start.9 = (bf16[1024,1024]{1,0:T(8,128)(2,1)S(1)}, bf16[1024,1024]{1,0:T(8,128)(2,1)}, u32[]{:S(2)}) copy-start(bf16[1024,1024]{1,0:T(8,128)(2,1)} %constant.35.clone.refs_1_) | copy-start | bytes 6291460
  209.0 42.5 %all-to-all-start.6 = ((bf16[4,2,2,192,256]{4,3,2,1,0:T(8,128)(2,1)}), bf16[4,2,2,192,256]{4,3,2,1,0:T(8,128)(2,1)}, u32[]{:S(2)}, u32[]{:S(2)}) async-start(bf16[4,2,2,192,256]{4,3,2,1,0:T(8,128)(2,1)} %copy-done.15), calls=%async_computation.6 | async-start | bytes 3145728 | tf_op jit(solution)/shard_map/all_to_all | solution.py:803
  217.3 29.4 %copy-start.6 = (f32[2,2,192,1024]{3,2,1,0:T(8,128)S(1)}, f32[2,2,192,1024]{3,2,1,0:T(8,128)}, u32[]{:S(2)}) copy-start(f32[2,2,192,1024]{3,2,1,0:T(8,128)} %copy-done.5) | copy-start | bytes 9437188
  224.9 7.2 %collective-permute-start.18 = (bf16[2,192,256]{2,1,0:T(8,128)(2,1)S(1)}, bf16[2,192,256]{2,1,0:T(8,128)(2,1)S(1)}, u32[]{:S(2)}, u32[]{:S(2)}) collective-permute-start(bf16[2,192,256]{2,1,0:T(8,128)(2,1)S(1)} %get-tuple-element.77), channel_id=1, source_target_pairs={{0,1},{1,2},{2,3},{3,4},{4,5},{5,6},{6,7},{7,0},{8,9},{9,10},{10,1... | collective-permute-start | bytes 589832 | tf_op jit(solution)/shard_map/ppermute | solution.py:744
  225.0 11.2 %collective-permute-start.19 = (bf16[2,192,256]{2,1,0:T(8,128)(2,1)S(1)}, bf16[2,192,256]{2,1,0:T(8,128)(2,1)S(1)}, u32[]{:S(2)}, u32[]{:S(2)}) collective-permute-start(bf16[2,192,256]{2,1,0:T(8,128)(2,1)S(1)} %get-tuple-element.78), channel_id=1, source_target_pairs={{0,2},{1,3},{2,4},{3,5},{4,6},{5,7},{6,0},{7,1},{8,10},{9,11},{10,... | collective-permute-start | bytes 589832 | tf_op jit(solution)/shard_map/ppermute | solution.py:744
  229.3 12.8 %collective-permute-start.20 = (bf16[2,192,256]{2,1,0:T(8,128)(2,1)S(1)}, bf16[2,192,256]{2,1,0:T(8,128)(2,1)S(1)}, u32[]{:S(2)}, u32[]{:S(2)}) collective-permute-start(bf16[2,192,256]{2,1,0:T(8,128)(2,1)S(1)} %get-tuple-element.79), channel_id=1, source_target_pairs={{0,3},{1,4},{2,5},{3,6},{4,7},{5,0},{6,1},{7,2},{8,11},{9,12},{10,... | collective-permute-start | bytes 589832 | tf_op jit(solution)/shard_map/ppermute | solution.py:744
  231.1 11.2 %collective-permute-start.21 = (bf16[2,192,256]{2,1,0:T(8,128)(2,1)S(1)}, bf16[2,192,256]{2,1,0:T(8,128)(2,1)S(1)}, u32[]{:S(2)}, u32[]{:S(2)}) collective-permute-start(bf16[2,192,256]{2,1,0:T(8,128)(2,1)S(1)} %get-tuple-element.80), channel_id=1, source_target_pairs={{0,4},{1,5},{2,6},{3,7},{4,0},{5,1},{6,2},{7,3},{8,12},{9,13},{10,... | collective-permute-start | bytes 589832 | tf_op jit(solution)/shard_map/ppermute | solution.py:744
  232.2 12.8 %collective-permute-start.22 = (bf16[2,192,256]{2,1,0:T(8,128)(2,1)S(1)}, bf16[2,192,256]{2,1,0:T(8,128)(2,1)S(1)}, u32[]{:S(2)}, u32[]{:S(2)}) collective-permute-start(bf16[2,192,256]{2,1,0:T(8,128)(2,1)S(1)} %get-tuple-element.81), channel_id=1, source_target_pairs={{0,5},{1,6},{2,7},{3,0},{4,1},{5,2},{6,3},{7,4},{8,13},{9,14},{10,... | collective-permute-start | bytes 589832 | tf_op jit(solution)/shard_map/ppermute | solution.py:744
  232.2 12.8 %collective-permute-start.23 = (bf16[2,192,256]{2,1,0:T(8,128)(2,1)S(1)}, bf16[2,192,256]{2,1,0:T(8,128)(2,1)S(1)}, u32[]{:S(2)}, u32[]{:S(2)}) collective-permute-start(bf16[2,192,256]{2,1,0:T(8,128)(2,1)S(1)} %get-tuple-element.82), channel_id=1, source_target_pairs={{0,6},{1,7},{2,0},{3,1},{4,2},{5,3},{6,4},{7,5},{8,14},{9,15},{10,... | collective-permute-start | bytes 589832 | tf_op jit(solution)/shard_map/ppermute | solution.py:744
  236.2 10.4 %collective-permute-start.24 = (bf16[2,192,256]{2,1,0:T(8,128)(2,1)S(1)}, bf16[2,192,256]{2,1,0:T(8,128)(2,1)S(1)}, u32[]{:S(2)}, u32[]{:S(2)}) collective-permute-start(bf16[2,192,256]{2,1,0:T(8,128)(2,1)S(1)} %get-tuple-element.83), channel_id=1, source_target_pairs={{0,7},{1,0},{2,1},{3,2},{4,3},{5,4},{6,5},{7,6},{8,15},{9,8},{10,9... | collective-permute-start | bytes 589832 | tf_op jit(solution)/shard_map/ppermute | solution.py:744
  251.5 42.0 %all-to-all-start.5 = ((bf16[4,2,2,192,256]{4,3,2,1,0:T(8,128)(2,1)}), bf16[4,2,2,192,256]{4,3,2,1,0:T(8,128)(2,1)S(1)}, u32[]{:S(2)}, u32[]{:S(2)}) async-start(bf16[4,2,2,192,256]{4,3,2,1,0:T(8,128)(2,1)} %copy-done.22), calls=%async_computation.5 | async-start | bytes 3145728 | tf_op jit(solution)/shard_map/all_to_all | solution.py:803
  271.5 32.0 %copy-start.23 = (bf16[2,192,256]{2,1,0:T(8,128)(2,1)}, bf16[2,192,256]{2,1,0:T(8,128)(2,1)S(1)}, u32[]{:S(2)}) copy-start(bf16[2,192,256]{2,1,0:T(8,128)(2,1)S(1)} %get-tuple-element.85.refs_0_.refs_10_) | copy-start | bytes 589828
  271.5 8.6 %collective-permute-start.25 = (bf16[2,192,256]{2,1,0:T(8,128)(2,1)S(1)}, bf16[2,192,256]{2,1,0:T(8,128)(2,1)S(1)}, u32[]{:S(2)}, u32[]{:S(2)}) collective-permute-start(bf16[2,192,256]{2,1,0:T(8,128)(2,1)S(1)} %get-tuple-element.86), channel_id=1, source_target_pairs={{0,1},{1,2},{2,3},{3,4},{4,5},{5,6},{6,7},{7,0},{8,9},{9,10},{10,1... | collective-permute-start | bytes 589832 | tf_op jit(solution)/shard_map/ppermute | solution.py:744
  271.6 9.8 %collective-permute-start.26 = (bf16[2,192,256]{2,1,0:T(8,128)(2,1)S(1)}, bf16[2,192,256]{2,1,0:T(8,128)(2,1)S(1)}, u32[]{:S(2)}, u32[]{:S(2)}) collective-permute-start(bf16[2,192,256]{2,1,0:T(8,128)(2,1)S(1)} %get-tuple-element.87), channel_id=1, source_target_pairs={{0,2},{1,3},{2,4},{3,5},{4,6},{5,7},{6,0},{7,1},{8,10},{9,11},{10,... | collective-permute-start | bytes 589832 | tf_op jit(solution)/shard_map/ppermute | solution.py:744
  275.2 13.8 %collective-permute-start.27 = (bf16[2,192,256]{2,1,0:T(8,128)(2,1)S(1)}, bf16[2,192,256]{2,1,0:T(8,128)(2,1)S(1)}, u32[]{:S(2)}, u32[]{:S(2)}) collective-permute-start(bf16[2,192,256]{2,1,0:T(8,128)(2,1)S(1)} %get-tuple-element.88), channel_id=1, source_target_pairs={{0,3},{1,4},{2,5},{3,6},{4,7},{5,0},{6,1},{7,2},{8,11},{9,12},{10,... | collective-permute-start | bytes 589832 | tf_op jit(solution)/shard_map/ppermute | solution.py:744
  275.7 13.5 %collective-permute-start.28 = (bf16[2,192,256]{2,1,0:T(8,128)(2,1)S(1)}, bf16[2,192,256]{2,1,0:T(8,128)(2,1)S(1)}, u32[]{:S(2)}, u32[]{:S(2)}) collective-permute-start(bf16[2,192,256]{2,1,0:T(8,128)(2,1)S(1)} %get-tuple-element.89), channel_id=1, source_target_pairs={{0,4},{1,5},{2,6},{3,7},{4,0},{5,1},{6,2},{7,3},{8,12},{9,13},{10,... | collective-permute-start | bytes 589832 | tf_op jit(solution)/shard_map/ppermute | solution.py:744
  276.7 15.2 %collective-permute-start.29 = (bf16[2,192,256]{2,1,0:T(8,128)(2,1)S(1)}, bf16[2,192,256]{2,1,0:T(8,128)(2,1)S(1)}, u32[]{:S(2)}, u32[]{:S(2)}) collective-permute-start(bf16[2,192,256]{2,1,0:T(8,128)(2,1)S(1)} %get-tuple-element.90), channel_id=1, source_target_pairs={{0,5},{1,6},{2,7},{3,0},{4,1},{5,2},{6,3},{7,4},{8,13},{9,14},{10,... | collective-permute-start | bytes 589832 | tf_op jit(solution)/shard_map/ppermute | solution.py:744
  280.1 11.8 %collective-permute-start.30 = (bf16[2,192,256]{2,1,0:T(8,128)(2,1)S(1)}, bf16[2,192,256]{2,1,0:T(8,128)(2,1)S(1)}, u32[]{:S(2)}, u32[]{:S(2)}) collective-permute-start(bf16[2,192,256]{2,1,0:T(8,128)(2,1)S(1)} %get-tuple-element.91), channel_id=1, source_target_pairs={{0,6},{1,7},{2,0},{3,1},{4,2},{5,3},{6,4},{7,5},{8,14},{9,15},{10,... | collective-permute-start | bytes 589832 | tf_op jit(solution)/shard_map/ppermute | solution.py:744
  281.4 10.5 %collective-permute-start.31 = (bf16[2,192,256]{2,1,0:T(8,128)(2,1)S(1)}, bf16[2,192,256]{2,1,0:T(8,128)(2,1)S(1)}, u32[]{:S(2)}, u32[]{:S(2)}) collective-permute-start(bf16[2,192,256]{2,1,0:T(8,128)(2,1)S(1)} %get-tuple-element.92), channel_id=1, source_target_pairs={{0,7},{1,0},{2,1},{3,2},{4,3},{5,4},{6,5},{7,6},{8,15},{9,8},{10,9... | collective-permute-start | bytes 589832 | tf_op jit(solution)/shard_map/ppermute | solution.py:744
  303.7 26.2 %all-to-all-start.7 = ((bf16[8,2,192,256]{3,2,1,0:T(8,128)(2,1)}), bf16[8,2,192,256]{3,2,1,0:T(8,128)(2,1)S(1)}, u32[]{:S(2)}, u32[]{:S(2)}) async-start(bf16[8,2,192,256]{3,2,1,0:T(8,128)(2,1)} %y_inverse.5.refs_13_), calls=%async_computation.7 | async-start | bytes 3145728 | tf_op jit(solution)/shard_map/all_to_all | solution.py:814
  336.2 15.4 %collective-permute-start.34 = (bf16[3,16,256]{2,1,0:T(8,128)(2,1)}, bf16[3,16,256]{2,1,0:T(8,128)(2,1)S(1)}, u32[]{:S(2)}, u32[]{:S(2)}) collective-permute-start(bf16[3,16,256]{2,1,0:T(8,128)(2,1)} %get-tuple-element.108), channel_id=1, source_target_pairs={{0,1},{1,2},{2,3},{3,4},{4,5},{5,6},{6,7},{7,0},{8,9},{9,10},{10,1... | collective-permute-start | bytes 73736 | tf_op jit(solution)/shard_map/ppermute | solution.py:472
  336.2 15.3 %collective-permute-start.35 = (bf16[3,16,256]{2,1,0:T(8,128)(2,1)}, bf16[3,16,256]{2,1,0:T(8,128)(2,1)S(1)}, u32[]{:S(2)}, u32[]{:S(2)}) collective-permute-start(bf16[3,16,256]{2,1,0:T(8,128)(2,1)} %get-tuple-element.109), channel_id=1, source_target_pairs={{1,0},{2,1},{3,2},{4,3},{5,4},{6,5},{7,6},{0,7},{9,8},{10,9},{11,1... | collective-permute-start | bytes 73736 | tf_op jit(solution)/shard_map/ppermute | solution.py:472
  338.9 12.7 %collective-permute-start.32 = (bf16[3,16,192]{2,1,0:T(8,128)(2,1)}, bf16[3,16,192]{2,1,0:T(8,128)(2,1)S(1)}, u32[]{:S(2)}, u32[]{:S(2)}) collective-permute-start(bf16[3,16,192]{2,1,0:T(8,128)(2,1)} %get-tuple-element.106), channel_id=1, source_target_pairs={{0,8},{8,16},{16,24},{24,0},{1,9},{9,17},{17,25},{25,1},{2,10},{10... | collective-permute-start | bytes 55304 | tf_op jit(solution)/shard_map/ppermute | solution.py:472
  338.9 12.7 %collective-permute-start.33 = (bf16[3,16,192]{2,1,0:T(8,128)(2,1)}, bf16[3,16,192]{2,1,0:T(8,128)(2,1)S(1)}, u32[]{:S(2)}, u32[]{:S(2)}) collective-permute-start(bf16[3,16,192]{2,1,0:T(8,128)(2,1)} %get-tuple-element.107), channel_id=1, source_target_pairs={{8,0},{16,8},{24,16},{0,24},{9,1},{17,9},{25,17},{1,25},{10,2},{18... | collective-permute-start | bytes 55304 | tf_op jit(solution)/shard_map/ppermute | solution.py:472
  (54 other events, 444.6 us)

commit v11 on v10

--- a/solution.py
+++ b/solution.py
@@ -183,9 +183,36 @@
     return copies
 
 
-def y_transform(me, table, columns, blocks, halves, after):
-    whole = len(columns) == 1
-    size_y = columns[0].shape[0] if whole else len(columns)
+def y_transform(table, columns, blocks, halves, after):
+    _, planes, _, width = columns.shape
+    modes = HALF_Y // (blocks * halves)
+    rows = Y // blocks
+
+    def kernel(table_ref, columns_ref, *refs):
+        out = refs[-1]
+        for plane in range(planes):
+            column = columns_ref[:, plane].reshape(Y, width)
+            part = jnp.dot(table_ref[...], column, preferred_element_type=f32)
+            out[0, :, plane] = part.astype(bf16).reshape(halves, 2, modes, width)
+
+    return pl.pallas_call(
+        kernel,
+        grid=(blocks,),
+        in_specs=[
+            pl.BlockSpec((rows, Y), lambda j: (j, 0)),
+            pl.BlockSpec(columns.shape, lambda j: (0, 0, 0, 0)),
+        ]
+        + tied(after),
+        out_specs=pl.BlockSpec((1, halves, planes, 2, modes, width), lambda j: (j, 0, 0, 0, 0, 0)),
+        out_shape=jax.ShapeDtypeStruct((blocks, halves, planes, 2, modes, width), bf16),
+        compiler_params=params(24),
+        cost_estimate=takes(4),
+        name="y_transform",
+    )(table, columns, *after)
+
+
+def y_transform_parts(me, table, columns, blocks, halves, after):
+    size_y = len(columns)
     planes, height, width = columns[0].shape[-3:]
     modes = HALF_Y // (blocks * halves)
     rows = Y // blocks
@@ -196,13 +223,14 @@
         out, held, lines, ready, table_in, lines_in, ready_out = refs[-7:]
         copies = []
         for s in range(size_y):
-            source = s if whole else lax.rem(me_ref[0] + size_y - s, size_y)
+            source = lax.rem(me_ref[0] + size_y - s, size_y)
             place = pl.ds(pl.multiple_of(source * height, height), height)
             for plane in range(planes):
-                part = parts[0].at[s, plane] if whole else parts[s].at[plane]
                 copies.append(
                     pltpu.make_async_copy(
-                        part, lines.at[plane, place], lines_in.at[s * planes + plane]
+                        parts[s].at[plane],
+                        lines.at[plane, place],
+                        lines_in.at[s * planes + plane],
                     )
                 )
                 copies[-1].start()
@@ -236,13 +264,41 @@
             pltpu.SemaphoreType.DMA((size_y * planes,)),
             pltpu.SemaphoreType.DMA((blocks,)),
         ],
+        compiler_params=params(),
+        cost_estimate=takes(5),
+        name="y_transform_parts",
+    )(me, table, *columns, *after)
+
+
+def y_inverse(table, modes, size_y, after):
+    planes, width = modes.shape[2], modes.shape[5]
+    height = Y // size_y
+    count = 384 // height
+
+    def kernel(table_ref, modes_ref, *refs):
+        out = refs[-1]
+        for plane in range(planes):
+            columns = modes_ref[:, :, plane].reshape(Y, width)
+            rows = jnp.dot(table_ref[...], columns, preferred_element_type=f32)
+            out[:, plane] = rows.astype(bf16).reshape(count, height, width)
+
+    return pl.pallas_call(
+        kernel,
+        grid=(size_y // count,),
+        in_specs=[
+            pl.BlockSpec((count * height, Y), lambda j: (j, 0)),
+            pl.BlockSpec(modes.shape, lambda j: (0, 0, 0, 0, 0, 0)),
+        ]
+        + tied(after),
+        out_specs=pl.BlockSpec((count, planes, height, width), lambda j: (j, 0, 0, 0)),
+        out_shape=jax.ShapeDtypeStruct((size_y, planes, height, width), bf16),
         compiler_params=params(24),
-        cost_estimate=takes(5),
-        name="y_transform",
-    )(me, table, *columns, *after)
-
-
-def y_inverse(me, table, modes, size_y, split, after):
+        cost_estimate=takes(4),
+        name="y_inverse",
+    )(table, modes, *after)
+
+
+def y_inverse_parts(me, table, modes, size_y, after):
     blocks, halves, planes, _, count, width = modes.shape
     height = Y // size_y
     shape = (planes, height, width)
@@ -263,7 +319,7 @@
                     )
                     copies[-1].start()
         tables = fetch_blocks(
-            table_ref, held, table_in, lambda s: lax.rem(me_ref[0] + s, size_y) if split else s
+            table_ref, held, table_in, lambda s: lax.rem(me_ref[0] + s, size_y)
         )
         for copy in copies:
             copy.wait()
@@ -274,17 +330,13 @@
                 columns = lines[plane].reshape(Y, width)
                 rows = jnp.dot(held[s], columns, preferred_element_type=f32)
                 ready[s, plane] = rows.astype(bf16)
-            out = outs[s] if split else outs[0].at[s]
-            results.append(pltpu.make_async_copy(ready.at[s], out, ready_out.at[s]))
+            results.append(pltpu.make_async_copy(ready.at[s], outs[s], ready_out.at[s]))
             results[s].start()
         for result in results:
             result.wait()
 
     anywhere = pl.BlockSpec(memory_space=pl.ANY)
-    if split:
-        out_shape = [jax.ShapeDtypeStruct(shape, bf16)] * size_y
-    else:
-        out_shape = [jax.ShapeDtypeStruct((size_y,) + shape, bf16)]
+    out_shape = [jax.ShapeDtypeStruct(shape, bf16)] * size_y
     return pl.pallas_call(
         kernel,
         in_specs=[pl.BlockSpec(memory_space=pltpu.SMEM), anywhere, anywhere] + tied(after),
@@ -298,9 +350,9 @@
             pltpu.SemaphoreType.DMA((blocks * halves * planes,)),
             pltpu.SemaphoreType.DMA((size_y,)),
         ],
-        compiler_params=params(24),
+        compiler_params=params(),
         cost_estimate=takes(4),
-        name="y_inverse",
+        name="y_inverse_parts",
     )(me, table, modes, *after)
 
 
@@ -648,12 +700,15 @@
     )(*operands, *after)
 
 
-def grad_vel_kernel(count, slope_x, vorticity, vorticity_above, vorticity_below, *refs):
+def grad_vel_kernel(
+    count, slope_x, slope_y, vorticity, vorticity_above, vorticity_below, *refs
+):
     adjoints, edges = refs[: 3 * count], refs[3 * count :]
     vort_low_x, vort_high_x, vort_low_y, vort_high_y, low_x, high_x, low_y, high_y = edges[:8]
-    after, padded = refs[-2:]
+    after = refs[-1]
     _, _, height, width = vorticity.shape
     first = pl.program_id(0) * LAYERS
+    factor = -0.5 * step_size
 
     def times(one, other):
         return one.astype(f32) * other.astype(f32)
@@ -661,34 +716,38 @@
     for c in range(count):
         here, above, below = adjoints[3 * c : 3 * c + 3]
         ends = spread_columns(
-            times(vort_low_x[0], low_x[c]),
-            times(vort_high_x[0], high_x[c]),
+            times(vort_low_x[0], low_x[c]) * -step_size,
+            times(vort_high_x[0], high_x[c]) * -step_size,
             first,
             LAYERS,
             width,
         )
-        product = [times(vorticity[0, k], here[k]).astype(bf16) for k in range(LAYERS)]
-        inner = jnp.dot(
-            jnp.concatenate(product, axis=0), slope_x[...], preferred_element_type=f32
+        deep = [times(vorticity_below[0, 0], below[0])]
+        along_x = []
+        along_y = []
+        for k in range(LAYERS):
+            value = here[k].astype(f32)
+            along_x.append((vorticity[0, k].astype(f32) * value).astype(bf16))
+            along_y.append((vorticity[1, k].astype(f32) * value).astype(bf16))
+            deep.append(vorticity[2, k].astype(f32) * value)
+        deep.append(times(vorticity_above[0, 0], above[0]))
+        along_x = jnp.dot(
+            jnp.concatenate(along_x, axis=0), slope_x[...], preferred_element_type=f32
         )
-        deep = [times(vorticity_below[0, 0], below[0])]
-        deep = deep + [times(vorticity[2, k], here[k]) for k in range(LAYERS)]
-        deep = deep + [times(vorticity_above[0, 0], above[0])]
         for k in range(LAYERS):
             n = first + k
-            padded[k, 8 : 8 + height, :] = times(vorticity[1, k], here[k])
-            padded[k, 7:8, :] = pick_row(vort_low_y[0], n) * pick_row(low_y[c], n)
-            padded[k, 8 + height : 9 + height, :] = pick_row(vort_high_y[0], n) * pick_row(
-                high_y[c], n
+            total = jnp.dot(slope_y[...], along_y[k], preferred_element_type=f32)
+            total = total + along_x[k * height : (k + 1) * height] + ends[k]
+            after[c, k] = total + (deep[k + 2] - deep[k]) * factor
+            low = pick_row(vort_low_y[0], n) * pick_row(low_y[c], n)
+            high = pick_row(vort_high_y[0], n) * pick_row(high_y[c], n)
+            after[c, k, 0:1, :] = after[c, k, 0:1, :] - low * factor
+            after[c, k, height - 1 : height, :] = (
+                after[c, k, height - 1 : height, :] + high * factor
             )
-            total = (padded[k, 9 : 9 + height, :] - padded[k, 7 : 7 + height, :]) + (
-                deep[k + 2] - deep[k]
-            )
-            total = total * 0.5 + inner[k * height : (k + 1) * height] + ends[k]
-            after[c, k] = total * -step_size
-
-
-def write_grad_vel(slope_x, vorticity, adjoints, saved_halos, halos, after):
+
+
+def write_grad_vel(slopes, vorticity, adjoints, saved_halos, halos, after):
     _, _, height, width = vorticity.shape
     count = len(adjoints)
     whole = lambda shape: pl.BlockSpec(shape, lambda n: (0,) * len(shape))
@@ -696,9 +755,10 @@
     saved_row = pl.BlockSpec((1, Z, width), lambda n: (3, 0, 0))
     layer_above = lambda n: lax.rem((n + 1) * LAYERS, Z)
     layer_below = lambda n: lax.rem(n * LAYERS + Z - 1, Z)
-    operands = [slope_x, vorticity, vorticity, vorticity]
+    operands = [*slopes, vorticity, vorticity, vorticity]
     in_specs = [
         whole((width, width)),
+        whole((height, height)),
         pl.BlockSpec((3, LAYERS, height, width), lambda n: (0, n, 0, 0)),
         pl.BlockSpec((1, 1, height, width), lambda n: (2, layer_above(n), 0, 0)),
         pl.BlockSpec((1, 1, height, width), lambda n: (2, layer_below(n), 0, 0)),
@@ -723,7 +783,6 @@
         in_specs=in_specs + tied(after),
         out_specs=pl.BlockSpec((count, LAYERS, height, width), lambda n: (0, n, 0, 0)),
         out_shape=jax.ShapeDtypeStruct((count, Z, height, width), f32),
-        scratch_shapes=[pltpu.VMEM((LAYERS, height + 16, width), f32)],
         compiler_params=params(),
         cost_estimate=takes(12),
         name="write_grad_vel",
@@ -782,13 +841,16 @@
     early = ((low_x, high_x), (low_y, high_y), ())
 
     columns = layers.reshape(size_y, planes, height, width)
-    columns = [lax.all_to_all(columns, "gy", 0, 0, tiled=True)]
+    columns = lax.all_to_all(columns, "gy", 0, 0, tiled=True)
     sent = []
     for place in range(3):
         if place > 0:
             layers = depth_transform(cot_vel, FORWARD_ORDER[place], me, size_y, (sent[-1],))
             columns = shifted(layers, "gy")
-        parts = y_transform(me, y_table, columns, size_x, halves, early[place])
+        if place == 0:
+            parts = y_transform(y_table, columns, size_x, halves, early[place])
+        else:
+            parts = y_transform_parts(me, y_table, columns, size_x, halves, early[place])
         parts = parts.reshape(size_x, 2, 2, modes, width)
         sent.append(parts if halves == 1 else pair_exchange(parts, "gy", half))
 
@@ -806,8 +868,9 @@
         return parts.reshape(size_x, halves, planes, 2, modes, width)
 
     def rows_of(component, modes_back, after):
-        split = component != BACK_ORDER[2]
-        return y_inverse(me, y_back_table, modes_back, size_y, split, after)
+        if component == BACK_ORDER[2]:
+            return [y_inverse(y_back_table, modes_back, size_y, after)]
+        return y_inverse_parts(me, y_back_table, modes_back, size_y, after)
 
     def layers_of(rows):
         if len(rows) == 1:
@@ -845,8 +908,9 @@
     halos = exchange(edges[0], edges[1], "gx") + exchange(edges[2], edges[3], "gy")
     grad_vort = vort_of(three, adjoint_three, grad_vort, ())
     shorts = {one: short_one, two: short_two, three: short_three}
+    scaled = [(slope * np.float32(-step_size)).astype(slope.dtype) for slope in (slope_x, slope_y)]
     grad_vel = write_grad_vel(
-        slope_x, vorticity, [shorts[i] for i in range(3)], saved_halos, halos, (grad_vort,)
+        scaled, vorticity, [shorts[i] for i in range(3)], saved_halos, halos, (grad_vort,)
     )
     return grad_vort, grad_vel
 

time: 368 us -> 355 us (0.965)
  Pallas kernels: 132 us -> 121 us
  local copies, waits for them, and re-layouts: 28.6 us -> 22 us
  starting transfers between devices: 89.6 us -> 94.3 us
    pallas_call x6, Pallas kernels: 44.1 us -> 35.5 us  [the longest x2 14.6 us: y_inverse_parts(): pl.pallas_call(kernel, in_specs=[pl.BlockSpec(memory_space=pltpu.SMEM), a...]
    unnamed x120 -> x118, local copies, waits for them, and re-layouts: 26.6 us -> 20 us
    ppermute x28, starting transfers between devices: 37.7 us -> 42.8 us  [shifted(): lax.ppermute(parts[s], axis, [(i, (i + s) % count) for i in range(count)])]
    ppermute x28, waiting for transfers between devices: 38 us -> 34.3 us  [shifted(): lax.ppermute(parts[s], axis, [(i, (i + s) % count) for i in range(count)])]
  transfers between devices with their start and end apart: 44 -> 44, of which waited for: 27 -> 29; matrix products, arithmetic and copies ran while one was open for 1% -> 1% of each run, Pallas kernels for 26% -> 27%
where the time goes in v11:
time: 355 us; the launch traced here: 354 us
  Pallas kernels  121 us (34%)
  waiting for transfers between devices  113 us (32%)
  starting transfers between devices  94.3 us (27%)
  local copies, waits for them, and re-layouts  22 us (6%)
    ppermute x28, starting transfers between devices, shifted(): lax.ppermute(parts[s], axis, [(i, (i + s) % count) for i in range(count)])  42.8 us
    ppermute x28, waiting for transfers between devices, shifted(): lax.ppermute(parts[s], axis, [(i, (i + s) % count) for i in range(count)])  34.3 us
    all_to_all x3, waiting for transfers between devices, spectrum(): lines = lax.all_to_all(sent[place], 'gx', 0, 0, tiled=True)  30.3 us
    all_to_all x3, waiting for transfers between devices, back(): parts = lax.all_to_all(filtered, 'gx', 0, 0, tiled=True)  28.8 us
    pallas_call x3, Pallas kernels, add_grad_vort(): pl.pallas_call(kernel, grid=(Z // LAYERS,), in_specs=in_specs + tied(afte...  23.1 us
    unnamed x118, local copies, waits for them, and re-layouts  20 us
    pallas_call x3, Pallas kernels, make_adjoint(): pl.pallas_call(kernel, grid=(height // ROWS,), in_specs=[pl.BlockSpec(mem...  15.8 us
    ppermute x8, waiting for transfers between devices, exchange(): return (lax.ppermute(last, axis, up), lax.ppermute(first, axis, down))  15.1 us
  transfers between devices with their start and end apart: 44, of which 29 were waited for; matrix products, arithmetic and copies ran while one was open for 1% of the time, Pallas kernels for 27%

profile of v11, /device:TPU:0, one launch (start us, length us, event | category | flops | bytes accessed | tf_op | source)
XLA Modules:
  0.0 353.6 jit_solution(1672106688281274702)
XLA Ops:
  0.6 3.2 depth_transform.3.refs_0_
  3.8 5.2 %all-to-all-start = ((bf16[8,2,192,256]{3,2,1,0:T(8,128)(2,1)}), bf16[8,2,192,256]{3,2,1,0:T(8,128)(2,1)S(1)}, u32[]{:S(2)}, u32[]{:S(2)}) async-start(bf16[8,2,192,256]{3,2,1,0:T(8,128)(2,1)} %bitcast.28), calls=%async_computation | async-start | bytes 3145728 | tf_op jit(solution)/shard_map/all_to_all | solution.py:844
  11.6 4.6 %edge_columns.2 = (bf16[3,16,192]{2,1,0:T(8,128)(2,1)}, bf16[3,16,192]{2,1,0:T(8,128)(2,1)}) custom-call(bf16[3,16,192,256]{3,2,1,0:T(8,128)(2,1)} %refs_4_.6, bf16[16,192,256]{2,1,0:T(8,128)(2,1)} %depth_transform.3.refs_0_), custom_call_target="tpu_custom_call" | custom-call | flops 1 | bytes 12000000 | tf_op jit(solution)/shard_map/edge_columns/pallas_call | solution.py:508
  16.9 3.7 %collective-permute-start.1 = (bf16[4,16,192]{2,1,0:T(8,128)(2,1)S(1)}, bf16[4,16,192]{2,1,0:T(8,128)(2,1)S(1)}, u32[]{:S(2)}, u32[]{:S(2)}) collective-permute-start(bf16[4,16,192]{2,1,0:T(8,128)(2,1)S(1)} %pad_maximum_fusion.1), channel_id=1, source_target_pairs={{8,0},{16,8},{24,16},{0,24},{9,1},{17,9},{25,17},{1,25},{10,2},{18... | collective-permute-start | bytes 73736 | tf_op jit(solution)/shard_map/ppermute | solution.py:524
  22.2 4.9 %collective-permute-done.refs_0_.refs_6_.refs_14_ = bf16[4,16,192]{2,1,0:T(8,128)(2,1)S(1)} collective-permute-done((bf16[4,16,192]{2,1,0:T(8,128)(2,1)S(1)}, bf16[4,16,192]{2,1,0:T(8,128)(2,1)S(1)}, u32[]{:S(2)}, u32[]{:S(2)}) %collective-permute-start) | collective-permute-done | bytes 24608 | tf_op jit(solution)/shard_map/ppermute | solution.py:524
  27.1 2.9 all-to-all-done.columns_ref
  32.3 3.9 %y_transform.1 = bf16[4,1,2,2,192,256]{5,4,3,2,1,0:T(8,128)(2,1)} custom-call(bf16[1536,1536]{1,0:T(8,128)(2,1)S(1)} %copy-done.1, bf16[8,2,192,256]{3,2,1,0:T(8,128)(2,1)S(1)} %all-to-all-done.columns_ref, bf16[4,16,192]{2,1,0:T(8,128)(2,1)S(1)} %collective-permute-done.refs_0_.refs_6_.refs_14_, ...), custom_call_target="tpu_custom_call" | custom-call | flops 1 | bytes 12000000 | tf_op jit(solution)/shard_map/y_transform/pallas_call | solution.py:198
  36.2 4.9 %all-to-all-start.1 = ((bf16[4,2,2,192,256]{4,3,2,1,0:T(8,128)(2,1)}), bf16[4,2,2,192,256]{4,3,2,1,0:T(8,128)(2,1)S(1)}, u32[]{:S(2)}, u32[]{:S(2)}) async-start(bf16[4,2,2,192,256]{4,3,2,1,0:T(8,128)(2,1)} %bitcast.3.refs_2_), calls=%async_computation.1 | async-start | bytes 3145728 | tf_op jit(solution)/shard_map/all_to_all | solution.py:858
  43.1 3.3 depth_transform.4
  49.7 9.4 %collective-permute-done.9.refs_8_.refs_16_ = bf16[4,16,256]{2,1,0:T(8,128)(2,1)S(1)} collective-permute-done((bf16[4,16,256]{2,1,0:T(8,128)(2,1)S(1)}, bf16[4,16,256]{2,1,0:T(8,128)(2,1)S(1)}, u32[]{:S(2)}, u32[]{:S(2)}) %collective-permute-start.9) | collective-permute-done | bytes 32800 | tf_op jit(solution)/shard_map/ppermute | solution.py:524
  62.5 3.2 collective-permute-done.5.refs_4_
  70.1 6.6 %y_transform_parts.2 = bf16[4,1,2,2,192,256]{5,4,3,2,1,0:T(8,128)(2,1)} custom-call(s32[1]{0:T(128)} %bitcast.refs_0_.me_ref, bf16[1536,1536]{1,0:T(8,128)(2,1)} %constant.37.clone.table_ref, bf16[2,192,256]{2,1,0:T(8,128)(2,1)} %get-tuple-element.60.refs_0_, bf16[2,192,256]{2,1,0:T(8,128)(2,1)} %copy-done.37, bf16[2,192,256]{2,1,0:T(8,128)(2,1)} %copy-done.38, ...), custom_call_target="tpu_custom_call" | custom-call | flops 1 | bytes 15000000 | tf_op jit(solution)/shard_map/y_transform_parts/pallas_call | solution.py:252
  76.7 5.1 %all-to-all-start.3 = ((bf16[4,2,2,192,256]{4,3,2,1,0:T(8,128)(2,1)}), bf16[4,2,2,192,256]{4,3,2,1,0:T(8,128)(2,1)}, u32[]{:S(2)}, u32[]{:S(2)}) async-start(bf16[4,2,2,192,256]{4,3,2,1,0:T(8,128)(2,1)} %bitcast.22), calls=%async_computation.3 | async-start | bytes 3145728 | tf_op jit(solution)/shard_map/all_to_all | solution.py:858
  81.8 3.3 depth_transform.5
  86.9 4.2 %collective-permute-start.12 = (bf16[2,192,256]{2,1,0:T(8,128)(2,1)}, bf16[2,192,256]{2,1,0:T(8,128)(2,1)S(1)}, u32[]{:S(2)}, u32[]{:S(2)}) collective-permute-start(bf16[2,192,256]{2,1,0:T(8,128)(2,1)} %get-tuple-element.70), channel_id=1, source_target_pairs={{0,2},{1,3},{2,4},{3,5},{4,6},{5,7},{6,0},{7,1},{8,10},{9,11},{10,... | collective-permute-start | bytes 589832 | tf_op jit(solution)/shard_map/ppermute | solution.py:803
  100.1 5.3 %collective-permute-done.13.refs_3_ = bf16[2,192,256]{2,1,0:T(8,128)(2,1)S(1)} collective-permute-done((bf16[2,192,256]{2,1,0:T(8,128)(2,1)}, bf16[2,192,256]{2,1,0:T(8,128)(2,1)S(1)}, u32[]{:S(2)}, u32[]{:S(2)}) %collective-permute-start.13) | collective-permute-done | bytes 196640 | tf_op jit(solution)/shard_map/ppermute | solution.py:803
  108.9 6.6 %y_transform_parts.3 = bf16[4,1,2,2,192,256]{5,4,3,2,1,0:T(8,128)(2,1)} custom-call(s32[1]{0:T(128)} %bitcast.refs_0_.me_ref, bf16[1536,1536]{1,0:T(8,128)(2,1)} %constant.37.clone.table_ref, bf16[2,192,256]{2,1,0:T(8,128)(2,1)} %get-tuple-element.68.refs_0_, bf16[2,192,256]{2,1,0:T(8,128)(2,1)} %copy-done.40, bf16[2,192,256]{2,1,0:T(8,128)(2,1)} %copy-done.41, ...), custom_call_target="tpu_custom_call" | custom-call | flops 1 | bytes 15000000 | tf_op jit(solution)/shard_map/y_transform_parts/pallas_call | solution.py:252
  115.5 4.1 %all-to-all-done.3.modes_ref = bf16[4,2,2,192,256]{4,3,2,1,0:T(8,128)(2,1)} async-done(((bf16[4,2,2,192,256]{4,3,2,1,0:T(8,128)(2,1)}), bf16[4,2,2,192,256]{4,3,2,1,0:T(8,128)(2,1)}, u32[]{:S(2)}, u32[]{:S(2)}) %all-to-all-start.3) | async-done | bytes 1572896 | tf_op jit(solution)/shard_map/all_to_all | solution.py:858
  119.6 4.4 %all-to-all-start.2 = ((bf16[4,2,2,192,256]{4,3,2,1,0:T(8,128)(2,1)}), bf16[4,2,2,192,256]{4,3,2,1,0:T(8,128)(2,1)}, u32[]{:S(2)}, u32[]{:S(2)}) async-start(bf16[4,2,2,192,256]{4,3,2,1,0:T(8,128)(2,1)} %bitcast.25), calls=%async_computation.2 | async-start | bytes 3145728 | tf_op jit(solution)/shard_map/all_to_all | solution.py:858
  127.8 3.9 %x_transform.4.refs_2_.refs_3_ = f32[2,2,192,1024]{3,2,1,0:T(8,128)S(1)} custom-call(bf16[1024,1024]{1,0:T(8,128)(2,1)S(1)} %copy-done.10, bf16[4,2,2,192,256]{4,3,2,1,0:T(8,128)(2,1)} %all-to-all-done.3.modes_ref, bf16[4,2,2,192,256]{4,3,2,1,0:T(8,128)(2,1)S(1)} %bitcast.26), custom_call_target="tpu_custom_call" | custom-call | flops 1 | bytes 9000000 | tf_op jit(solution)/shard_map/x_transform/pallas_call | solution.py:370
  131.7 3.0 curl_inverse.3.refs_0_
  135.8 26.2 %all-to-all-done.2.modes_ref = bf16[4,2,2,192,256]{4,3,2,1,0:T(8,128)(2,1)} async-done(((bf16[4,2,2,192,256]{4,3,2,1,0:T(8,128)(2,1)}), bf16[4,2,2,192,256]{4,3,2,1,0:T(8,128)(2,1)}, u32[]{:S(2)}, u32[]{:S(2)}) %all-to-all-start.2) | async-done | bytes 1572896 | tf_op jit(solution)/shard_map/all_to_all | solution.py:858
  162.0 4.5 %all-to-all-start.4 = ((bf16[4,2,2,192,256]{4,3,2,1,0:T(8,128)(2,1)}), bf16[4,2,2,192,256]{4,3,2,1,0:T(8,128)(2,1)}, u32[]{:S(2)}, u32[]{:S(2)}) async-start(bf16[4,2,2,192,256]{4,3,2,1,0:T(8,128)(2,1)} %copy-done.12), calls=%async_computation.4 | async-start | bytes 3145728 | tf_op jit(solution)/shard_map/all_to_all | solution.py:865
  169.5 3.3 x_transform.5.refs_2_.refs_3_
  172.8 3.0 curl_inverse.4.refs_0_
  178.7 24.9 %all-to-all-done.4 = bf16[4,2,2,192,256]{4,3,2,1,0:T(8,128)(2,1)} async-done(((bf16[4,2,2,192,256]{4,3,2,1,0:T(8,128)(2,1)}), bf16[4,2,2,192,256]{4,3,2,1,0:T(8,128)(2,1)}, u32[]{:S(2)}, u32[]{:S(2)}) %all-to-all-start.4) | async-done | bytes 1572896 | tf_op jit(solution)/shard_map/all_to_all | solution.py:865
  203.6 4.4 %all-to-all-start.6 = ((bf16[4,2,2,192,256]{4,3,2,1,0:T(8,128)(2,1)}), bf16[4,2,2,192,256]{4,3,2,1,0:T(8,128)(2,1)}, u32[]{:S(2)}, u32[]{:S(2)}) async-start(bf16[4,2,2,192,256]{4,3,2,1,0:T(8,128)(2,1)} %copy-done.14), calls=%async_computation.6 | async-start | bytes 3145728 | tf_op jit(solution)/shard_map/all_to_all | solution.py:865
  208.0 7.4 %y_inverse_parts.2 = (bf16[2,192,256]{2,1,0:T(8,128)(2,1)}, bf16[2,192,256]{2,1,0:T(8,128)(2,1)}, bf16[2,192,256]{2,1,0:T(8,128)(2,1)}, bf16[2,192,256]{2,1,0:T(...) custom-call(s32[1]{0:T(128)} %bitcast.refs_0_.me_ref, ...), custom_call_target="tpu_custom_call" | custom-call | flops 1 | bytes 12000000 | tf_op jit(solution)/shard_map/y_inverse_parts/pallas_call | solution.py:340
  215.4 4.4 %collective-permute-start.19 = (bf16[2,192,256]{2,1,0:T(8,128)(2,1)}, bf16[2,192,256]{2,1,0:T(8,128)(2,1)S(1)}, u32[]{:S(2)}, u32[]{:S(2)}) collective-permute-start(bf16[2,192,256]{2,1,0:T(8,128)(2,1)} %get-tuple-element.78), channel_id=1, source_target_pairs={{0,2},{1,3},{2,4},{3,5},{4,6},{5,7},{6,0},{7,1},{8,10},{9,11},{10,... | collective-permute-start | bytes 589832 | tf_op jit(solution)/shard_map/ppermute | solution.py:803
  222.9 4.3 %collective-permute-start.23 = (bf16[2,192,256]{2,1,0:T(8,128)(2,1)}, bf16[2,192,256]{2,1,0:T(8,128)(2,1)S(1)}, u32[]{:S(2)}, u32[]{:S(2)}) collective-permute-start(bf16[2,192,256]{2,1,0:T(8,128)(2,1)} %get-tuple-element.82), channel_id=1, source_target_pairs={{0,6},{1,7},{2,0},{3,1},{4,2},{5,3},{6,4},{7,5},{8,14},{9,15},{10,... | collective-permute-start | bytes 589832 | tf_op jit(solution)/shard_map/ppermute | solution.py:803
  227.2 4.0 %collective-permute-start.24 = (bf16[2,192,256]{2,1,0:T(8,128)(2,1)}, bf16[2,192,256]{2,1,0:T(8,128)(2,1)S(1)}, u32[]{:S(2)}, u32[]{:S(2)}) collective-permute-start(bf16[2,192,256]{2,1,0:T(8,128)(2,1)} %get-tuple-element.83), channel_id=1, source_target_pairs={{0,7},{1,0},{2,1},{3,2},{4,3},{5,4},{6,5},{7,6},{8,15},{9,8},{10,9... | collective-permute-start | bytes 589832 | tf_op jit(solution)/shard_map/ppermute | solution.py:803
  240.0 3.8 %curl_inverse.5 = bf16[4,2,2,192,256]{4,3,2,1,0:T(8,128)(2,1)} custom-call(s32[2]{0:T(128)S(1)} %pad_add_fusion.refs_0_, bf16[1024,1024]{1,0:T(8,128)(2,1)S(1)} %copy-done.9, f32[2,2,192,1024]{3,2,1,0:T(8,128)S(1)} %copy-done.3, f32[2,2,192,1024]{3,2,1,0:T(8,128)S(1)} %copy-done.5, bf16[2,192,256]{2,1,0:T(8,128)(2,1)S(1)} %copy-done.19, ...), custom_call_target="tpu_custom_call" | custom-call | flops 1 | bytes 12000000 | tf_op jit(solution)/shard_map/curl_inverse/pallas_call | solution.py:446
  244.5 4.4 %all-to-all-start.5 = ((bf16[4,2,2,192,256]{4,3,2,1,0:T(8,128)(2,1)}), bf16[4,2,2,192,256]{4,3,2,1,0:T(8,128)(2,1)S(1)}, u32[]{:S(2)}, u32[]{:S(2)}) async-start(bf16[4,2,2,192,256]{4,3,2,1,0:T(8,128)(2,1)} %curl_inverse.5), calls=%async_computation.5 | async-start | bytes 3145728 | tf_op jit(solution)/shard_map/all_to_all | solution.py:865
  248.9 5.3 %make_adjoint.3 = (f32[16,192,256]{2,1,0:T(8,128)}, bf16[16,192,256]{2,1,0:T(8,128)(2,1)}, bf16[3,16,192]{2,1,0:T(8,128)(2,1)}, bf16[3,16,192]{2,1,0:T(8,128)(2,...) custom-call(s32[1]{0:T(128)} %bitcast.refs_0_.me_ref, ...), custom_call_target="tpu_custom_call" | custom-call | flops 1 | bytes 15000000 | tf_op jit(solution)/shard_map/make_adjoint/pallas_call | solution.py:575
  254.2 7.2 %y_inverse_parts.3 = (bf16[2,192,256]{2,1,0:T(8,128)(2,1)}, bf16[2,192,256]{2,1,0:T(8,128)(2,1)}, bf16[2,192,256]{2,1,0:T(8,128)(2,1)}, bf16[2,192,256]{2,1,0:T(...) custom-call(s32[1]{0:T(128)} %bitcast.refs_0_.me_ref, ...), custom_call_target="tpu_custom_call" | custom-call | flops 1 | bytes 12000000 | tf_op jit(solution)/shard_map/y_inverse_parts/pallas_call | solution.py:340
  261.5 3.6 %collective-permute-start.26 = (bf16[2,192,256]{2,1,0:T(8,128)(2,1)}, bf16[2,192,256]{2,1,0:T(8,128)(2,1)S(1)}, u32[]{:S(2)}, u32[]{:S(2)}) collective-permute-start(bf16[2,192,256]{2,1,0:T(8,128)(2,1)} %get-tuple-element.87), channel_id=1, source_target_pairs={{0,2},{1,3},{2,4},{3,5},{4,6},{5,7},{6,0},{7,1},{8,10},{9,11},{10,... | collective-permute-start | bytes 589832 | tf_op jit(solution)/shard_map/ppermute | solution.py:803
  272.4 3.9 %collective-permute-start.31 = (bf16[2,192,256]{2,1,0:T(8,128)(2,1)}, bf16[2,192,256]{2,1,0:T(8,128)(2,1)S(1)}, u32[]{:S(2)}, u32[]{:S(2)}) collective-permute-start(bf16[2,192,256]{2,1,0:T(8,128)(2,1)} %get-tuple-element.92), channel_id=1, source_target_pairs={{0,7},{1,0},{2,1},{3,2},{4,3},{5,4},{6,5},{7,6},{8,15},{9,8},{10,9... | collective-permute-start | bytes 589832 | tf_op jit(solution)/shard_map/ppermute | solution.py:803
  276.3 3.0 collective-permute-done.27.refs_3_
  282.7 3.3 all-to-all-done.5
  289.2 3.9 %y_inverse.1.refs_13_ = bf16[8,2,192,256]{3,2,1,0:T(8,128)(2,1)} custom-call(bf16[1536,1536]{1,0:T(8,128)(2,1)S(1)} %copy-done, bf16[4,1,2,2,192,256]{5,4,3,2,1,0:T(8,128)(2,1)S(1)} %bitcast.27, bf16[2,192,256]{2,1,0:T(8,128)(2,1)S(1)} %copy-done.16, bf16[2,192,256]{2,1,0:T(8,128)(2,1)S(1)} %collective-permute-done.25.refs_1_, ...), custom_call_target="tpu_custom_call" | custom-call | flops 1 | bytes 12000000 | tf_op jit(solution)/shard_map/y_inverse/pallas_call | solution.py:285
  293.2 5.8 %all-to-all-start.7 = ((bf16[8,2,192,256]{3,2,1,0:T(8,128)(2,1)}), bf16[8,2,192,256]{3,2,1,0:T(8,128)(2,1)S(1)}, u32[]{:S(2)}, u32[]{:S(2)}) async-start(bf16[8,2,192,256]{3,2,1,0:T(8,128)(2,1)} %y_inverse.1.refs_13_), calls=%async_computation.7 | async-start | bytes 3145728 | tf_op jit(solution)/shard_map/all_to_all | solution.py:877
  299.0 6.5 %add_grad_vort.3.refs_10_ = bf16[3,16,192,256]{3,2,1,0:T(8,128)(2,1)} custom-call(bf16[256,256]{1,0:T(8,128)(2,1)} %constant.41.clone.refs_0_, bf16[192,192]{1,0:T(8,128)(2,1)} %constant.42.clone.refs_1_, bf16[3,16,192,256]{3,2,1,0:T(8,128)(2,1)} %refs_4_.6, bf16[3,16,192,256]{3,2,1,0:T(8,128)(2,1)} %refs_4_.6, bf16[3,16,192,256]{3,2,1,0:T(8,128)(2,1)} %refs_4_.6, ...), custom_call_target="tpu_custom_call" | custom-call | flops 1 | bytes 27000000 | tf_op jit(solution)/shard_map/add_grad_vort/pallas_call | solution.py:691
  305.6 5.3 %make_adjoint.4 = (f32[16,192,256]{2,1,0:T(8,128)}, bf16[16,192,256]{2,1,0:T(8,128)(2,1)}, bf16[3,16,192]{2,1,0:T(8,128)(2,1)}, bf16[3,16,192]{2,1,0:T(8,128)(2,...) custom-call(s32[1]{0:T(128)} %bitcast.refs_0_.me_ref, ...), custom_call_target="tpu_custom_call", output_to_operand_aliasing={{2}: (10, {}), {3}: (11, {}), {4}: (12, {}), {5}: (13, {})} | custom-call | flops 1 | bytes 15000000 | tf_op jit(solution)/shard_map/make_adjoint/pallas_call | solution.py:575
  310.8 7.8 %add_grad_vort.4.refs_6_.refs_10_ = bf16[3,16,192,256]{3,2,1,0:T(8,128)(2,1)} custom-call(bf16[256,256]{1,0:T(8,128)(2,1)} %constant.41.clone.refs_0_, bf16[192,192]{1,0:T(8,128)(2,1)} %constant.42.clone.refs_1_, bf16[3,16,192,256]{3,2,1,0:T(8,128)(2,1)} %refs_4_.6, bf16[3,16,192,256]{3,2,1,0:T(8,128)(2,1)} %refs_4_.6, bf16[3,16,192,256]{3,2,1,0:T(8,128)(2,1)} %refs_4_.6, ...), custom_call_target="tpu_custom_call" | custom-call | flops 1 | bytes 27000000 | tf_op jit(solution)/shard_map/add_grad_vort/pallas_call | solution.py:691
  321.2 5.2 %make_adjoint.5 = (f32[16,192,256]{2,1,0:T(8,128)}, bf16[16,192,256]{2,1,0:T(8,128)(2,1)}, bf16[3,16,192]{2,1,0:T(8,128)(2,1)}, bf16[3,16,192]{2,1,0:T(8,128)(2,...) custom-call(s32[1]{0:T(128)} %bitcast.refs_0_.me_ref, ...), custom_call_target="tpu_custom_call", output_to_operand_aliasing={{2}: (3, {}), {3}: (4, {}), {4}: (5, {}), {5}: (6, {})} | custom-call | flops 1 | bytes 15000000 | tf_op jit(solution)/shard_map/make_adjoint/pallas_call | solution.py:575
  329.1 3.8 %collective-permute-start.33 = (bf16[3,16,192]{2,1,0:T(8,128)(2,1)}, bf16[3,16,192]{2,1,0:T(8,128)(2,1)S(1)}, u32[]{:S(2)}, u32[]{:S(2)}) collective-permute-start(bf16[3,16,192]{2,1,0:T(8,128)(2,1)} %get-tuple-element.107), channel_id=1, source_target_pairs={{8,0},{16,8},{24,16},{0,24},{9,1},{17,9},{25,17},{1,25},{10,2},{18... | collective-permute-start | bytes 55304 | tf_op jit(solution)/shard_map/ppermute | solution.py:524
  332.9 8.8 %add_grad_vort.5.refs_22_ = f32[3,16,192,256]{3,2,1,0:T(8,128)} custom-call(bf16[256,256]{1,0:T(8,128)(2,1)} %constant.41.clone.refs_0_, bf16[192,192]{1,0:T(8,128)(2,1)} %constant.42.clone.refs_1_, bf16[3,16,192,256]{3,2,1,0:T(8,128)(2,1)} %refs_4_.6, bf16[3,16,192,256]{3,2,1,0:T(8,128)(2,1)} %refs_4_.6, bf16[3,16,192,256]{3,2,1,0:T(8,128)(2,1)} %refs_4_.6, ...), custom_call_target="tpu_custom_call" | custom-call | flops 1 | bytes 27000000 | tf_op jit(solution)/shard_map/add_grad_vort/pallas_call | solution.py:691
  342.4 11.0 %write_grad_vel.1 = f32[3,16,192,256]{3,2,1,0:T(8,128)} custom-call(bf16[256,256]{1,0:T(8,128)(2,1)} %constant.43.clone.refs_0_, bf16[192,192]{1,0:T(8,128)(2,1)} %constant.44.clone.refs_1_, bf16[3,16,192,256]{3,2,1,0:T(8,128)(2,1)} %refs_4_.7, bf16[3,16,192,256]{3,2,1,0:T(8,128)(2,1)} %refs_4_.7, bf16[3,16,192,256]{3,2,1,0:T(8,128)(2,1)} %refs_4_.7, ...), custom_call_target="tpu_custom_call" | custom-call | flops 1 | bytes 36000000 | tf_op jit(solution)/shard_map/write_grad_vel/pallas_call | solution.py:780
  (189 shorter events, 77.7 us)
Async XLA Ops:
  3.8 26.2 %all-to-all-start = ((bf16[8,2,192,256]{3,2,1,0:T(8,128)(2,1)}), bf16[8,2,192,256]{3,2,1,0:T(8,128)(2,1)S(1)}, u32[]{:S(2)}, u32[]{:S(2)}) async-start(bf16[8,2,192,256]{3,2,1,0:T(8,128)(2,1)} %bitcast.28), calls=%async_computation | async-start | bytes 3145728 | tf_op jit(solution)/shard_map/all_to_all | solution.py:844
  16.9 5.3 %collective-permute-start.1 = (bf16[4,16,192]{2,1,0:T(8,128)(2,1)S(1)}, bf16[4,16,192]{2,1,0:T(8,128)(2,1)S(1)}, u32[]{:S(2)}, u32[]{:S(2)}) collective-permute-start(bf16[4,16,192]{2,1,0:T(8,128)(2,1)S(1)} %pad_maximum_fusion.1), channel_id=1, source_target_pairs={{8,0},{16,8},{24,16},{0,24},{9,1},{17,9},{25,17},{1,25},{10,2},{18... | collective-permute-start | bytes 73736 | tf_op jit(solution)/shard_map/ppermute | solution.py:524
  21.3 5.8 %collective-permute-start = (bf16[4,16,192]{2,1,0:T(8,128)(2,1)S(1)}, bf16[4,16,192]{2,1,0:T(8,128)(2,1)S(1)}, u32[]{:S(2)}, u32[]{:S(2)}) collective-permute-start(bf16[4,16,192]{2,1,0:T(8,128)(2,1)S(1)} %pad_maximum_fusion), channel_id=1, source_target_pairs={{0,8},{8,16},{16,24},{24,0},{1,9},{9,17},{17,25},{25,1},{2,10},{10... | collective-permute-start | bytes 73736 | tf_op jit(solution)/shard_map/ppermute | solution.py:524
  36.2 40.5 %all-to-all-start.1 = ((bf16[4,2,2,192,256]{4,3,2,1,0:T(8,128)(2,1)}), bf16[4,2,2,192,256]{4,3,2,1,0:T(8,128)(2,1)S(1)}, u32[]{:S(2)}, u32[]{:S(2)}) async-start(bf16[4,2,2,192,256]{4,3,2,1,0:T(8,128)(2,1)} %bitcast.3.refs_2_), calls=%async_computation.1 | async-start | bytes 3145728 | tf_op jit(solution)/shard_map/all_to_all | solution.py:858
  46.4 13.3 %collective-permute-start.2 = (bf16[2,192,256]{2,1,0:T(8,128)(2,1)}, bf16[2,192,256]{2,1,0:T(8,128)(2,1)S(1)}, u32[]{:S(2)}, u32[]{:S(2)}) collective-permute-start(bf16[2,192,256]{2,1,0:T(8,128)(2,1)} %get-tuple-element.61), channel_id=1, source_target_pairs={{0,1},{1,2},{2,3},{3,4},{4,5},{5,6},{6,7},{7,0},{8,9},{9,10},{10,1... | collective-permute-start | bytes 589832 | tf_op jit(solution)/shard_map/ppermute | solution.py:803
  46.4 13.8 %collective-permute-start.3 = (bf16[2,192,256]{2,1,0:T(8,128)(2,1)}, bf16[2,192,256]{2,1,0:T(8,128)(2,1)S(1)}, u32[]{:S(2)}, u32[]{:S(2)}) collective-permute-start(bf16[2,192,256]{2,1,0:T(8,128)(2,1)} %get-tuple-element.62), channel_id=1, source_target_pairs={{0,2},{1,3},{2,4},{3,5},{4,6},{5,7},{6,0},{7,1},{8,10},{9,11},{10,... | collective-permute-start | bytes 589832 | tf_op jit(solution)/shard_map/ppermute | solution.py:803
  47.0 12.1 %collective-permute-start.9 = (bf16[4,16,256]{2,1,0:T(8,128)(2,1)S(1)}, bf16[4,16,256]{2,1,0:T(8,128)(2,1)S(1)}, u32[]{:S(2)}, u32[]{:S(2)}) collective-permute-start(bf16[4,16,256]{2,1,0:T(8,128)(2,1)S(1)} %pad_maximum_fusion.2), channel_id=1, source_target_pairs={{0,1},{1,2},{2,3},{3,4},{4,5},{5,6},{6,7},{7,0},{8,9},{9,10},{10,1... | collective-permute-start | bytes 98312 | tf_op jit(solution)/shard_map/ppermute | solution.py:524
  48.3 11.4 %collective-permute-start.10 = (bf16[4,16,256]{2,1,0:T(8,128)(2,1)S(1)}, bf16[4,16,256]{2,1,0:T(8,128)(2,1)S(1)}, u32[]{:S(2)}, u32[]{:S(2)}) collective-permute-start(bf16[4,16,256]{2,1,0:T(8,128)(2,1)S(1)} %pad_maximum_fusion.3), channel_id=1, source_target_pairs={{1,0},{2,1},{3,2},{4,3},{5,4},{6,5},{7,6},{0,7},{9,8},{10,9},{11,1... | collective-permute-start | bytes 98312 | tf_op jit(solution)/shard_map/ppermute | solution.py:524
  49.7 12.7 %collective-permute-start.4 = (bf16[2,192,256]{2,1,0:T(8,128)(2,1)}, bf16[2,192,256]{2,1,0:T(8,128)(2,1)S(1)}, u32[]{:S(2)}, u32[]{:S(2)}) collective-permute-start(bf16[2,192,256]{2,1,0:T(8,128)(2,1)} %get-tuple-element.63), channel_id=1, source_target_pairs={{0,3},{1,4},{2,5},{3,6},{4,7},{5,0},{6,1},{7,2},{8,11},{9,12},{10,... | collective-permute-start | bytes 589832 | tf_op jit(solution)/shard_map/ppermute | solution.py:803
  59.2 6.5 %collective-permute-start.5 = (bf16[2,192,256]{2,1,0:T(8,128)(2,1)}, bf16[2,192,256]{2,1,0:T(8,128)(2,1)S(1)}, u32[]{:S(2)}, u32[]{:S(2)}) collective-permute-start(bf16[2,192,256]{2,1,0:T(8,128)(2,1)} %get-tuple-element.64), channel_id=1, source_target_pairs={{0,4},{1,5},{2,6},{3,7},{4,0},{5,1},{6,2},{7,3},{8,12},{9,13},{10,... | collective-permute-start | bytes 589832 | tf_op jit(solution)/shard_map/ppermute | solution.py:803
  59.7 6.8 %collective-permute-start.6 = (bf16[2,192,256]{2,1,0:T(8,128)(2,1)}, bf16[2,192,256]{2,1,0:T(8,128)(2,1)S(1)}, u32[]{:S(2)}, u32[]{:S(2)}) collective-permute-start(bf16[2,192,256]{2,1,0:T(8,128)(2,1)} %get-tuple-element.65), channel_id=1, source_target_pairs={{0,5},{1,6},{2,7},{3,0},{4,1},{5,2},{6,3},{7,4},{8,13},{9,14},{10,... | collective-permute-start | bytes 589832 | tf_op jit(solution)/shard_map/ppermute | solution.py:803
  59.7 8.0 %collective-permute-start.7 = (bf16[2,192,256]{2,1,0:T(8,128)(2,1)}, bf16[2,192,256]{2,1,0:T(8,128)(2,1)S(1)}, u32[]{:S(2)}, u32[]{:S(2)}) collective-permute-start(bf16[2,192,256]{2,1,0:T(8,128)(2,1)} %get-tuple-element.66), channel_id=1, source_target_pairs={{0,6},{1,7},{2,0},{3,1},{4,2},{5,3},{6,4},{7,5},{8,14},{9,15},{10,... | collective-permute-start | bytes 589832 | tf_op jit(solution)/shard_map/ppermute | solution.py:803
  60.3 9.2 %collective-permute-start.8 = (bf16[2,192,256]{2,1,0:T(8,128)(2,1)}, bf16[2,192,256]{2,1,0:T(8,128)(2,1)S(1)}, u32[]{:S(2)}, u32[]{:S(2)}) collective-permute-start(bf16[2,192,256]{2,1,0:T(8,128)(2,1)} %get-tuple-element.67), channel_id=1, source_target_pairs={{0,7},{1,0},{2,1},{3,2},{4,3},{5,4},{6,5},{7,6},{8,15},{9,8},{10,9... | collective-permute-start | bytes 589832 | tf_op jit(solution)/shard_map/ppermute | solution.py:803
  76.7 42.9 %all-to-all-start.3 = ((bf16[4,2,2,192,256]{4,3,2,1,0:T(8,128)(2,1)}), bf16[4,2,2,192,256]{4,3,2,1,0:T(8,128)(2,1)}, u32[]{:S(2)}, u32[]{:S(2)}) async-start(bf16[4,2,2,192,256]{4,3,2,1,0:T(8,128)(2,1)} %bitcast.22), calls=%async_computation.3 | async-start | bytes 3145728 | tf_op jit(solution)/shard_map/all_to_all | solution.py:858
  85.1 11.5 %collective-permute-start.11 = (bf16[2,192,256]{2,1,0:T(8,128)(2,1)}, bf16[2,192,256]{2,1,0:T(8,128)(2,1)S(1)}, u32[]{:S(2)}, u32[]{:S(2)}) collective-permute-start(bf16[2,192,256]{2,1,0:T(8,128)(2,1)} %get-tuple-element.69), channel_id=1, source_target_pairs={{0,1},{1,2},{2,3},{3,4},{4,5},{5,6},{6,7},{7,0},{8,9},{9,10},{10,1... | collective-permute-start | bytes 589832 | tf_op jit(solution)/shard_map/ppermute | solution.py:803
  86.9 11.0 %collective-permute-start.12 = (bf16[2,192,256]{2,1,0:T(8,128)(2,1)}, bf16[2,192,256]{2,1,0:T(8,128)(2,1)S(1)}, u32[]{:S(2)}, u32[]{:S(2)}) collective-permute-start(bf16[2,192,256]{2,1,0:T(8,128)(2,1)} %get-tuple-element.70), channel_id=1, source_target_pairs={{0,2},{1,3},{2,4},{3,5},{4,6},{5,7},{6,0},{7,1},{8,10},{9,11},{10,... | collective-permute-start | bytes 589832 | tf_op jit(solution)/shard_map/ppermute | solution.py:803
  91.1 14.4 %collective-permute-start.13 = (bf16[2,192,256]{2,1,0:T(8,128)(2,1)}, bf16[2,192,256]{2,1,0:T(8,128)(2,1)S(1)}, u32[]{:S(2)}, u32[]{:S(2)}) collective-permute-start(bf16[2,192,256]{2,1,0:T(8,128)(2,1)} %get-tuple-element.71), channel_id=1, source_target_pairs={{0,3},{1,4},{2,5},{3,6},{4,7},{5,0},{6,1},{7,2},{8,11},{9,12},{10,... | collective-permute-start | bytes 589832 | tf_op jit(solution)/shard_map/ppermute | solution.py:803
  91.8 13.9 %collective-permute-start.14 = (bf16[2,192,256]{2,1,0:T(8,128)(2,1)}, bf16[2,192,256]{2,1,0:T(8,128)(2,1)S(1)}, u32[]{:S(2)}, u32[]{:S(2)}) collective-permute-start(bf16[2,192,256]{2,1,0:T(8,128)(2,1)} %get-tuple-element.72), channel_id=1, source_target_pairs={{0,4},{1,5},{2,6},{3,7},{4,0},{5,1},{6,2},{7,3},{8,12},{9,13},{10,... | collective-permute-start | bytes 589832 | tf_op jit(solution)/shard_map/ppermute | solution.py:803
  93.2 14.8 %collective-permute-start.15 = (bf16[2,192,256]{2,1,0:T(8,128)(2,1)}, bf16[2,192,256]{2,1,0:T(8,128)(2,1)S(1)}, u32[]{:S(2)}, u32[]{:S(2)}) collective-permute-start(bf16[2,192,256]{2,1,0:T(8,128)(2,1)} %get-tuple-element.73), channel_id=1, source_target_pairs={{0,5},{1,6},{2,7},{3,0},{4,1},{5,2},{6,3},{7,4},{8,13},{9,14},{10,... | collective-permute-start | bytes 589832 | tf_op jit(solution)/shard_map/ppermute | solution.py:803
  96.6 11.5 %collective-permute-start.16 = (bf16[2,192,256]{2,1,0:T(8,128)(2,1)}, bf16[2,192,256]{2,1,0:T(8,128)(2,1)S(1)}, u32[]{:S(2)}, u32[]{:S(2)}) collective-permute-start(bf16[2,192,256]{2,1,0:T(8,128)(2,1)} %get-tuple-element.74), channel_id=1, source_target_pairs={{0,6},{1,7},{2,0},{3,1},{4,2},{5,3},{6,4},{7,5},{8,14},{9,15},{10,... | collective-permute-start | bytes 589832 | tf_op jit(solution)/shard_map/ppermute | solution.py:803
  97.9 10.2 %collective-permute-start.17 = (bf16[2,192,256]{2,1,0:T(8,128)(2,1)}, bf16[2,192,256]{2,1,0:T(8,128)(2,1)S(1)}, u32[]{:S(2)}, u32[]{:S(2)}) collective-permute-start(bf16[2,192,256]{2,1,0:T(8,128)(2,1)} %get-tuple-element.75), channel_id=1, source_target_pairs={{0,7},{1,0},{2,1},{3,2},{4,3},{5,4},{6,5},{7,6},{8,15},{9,8},{10,9... | collective-permute-start | bytes 589832 | tf_op jit(solution)/shard_map/ppermute | solution.py:803
  119.6 42.4 %all-to-all-start.2 = ((bf16[4,2,2,192,256]{4,3,2,1,0:T(8,128)(2,1)}), bf16[4,2,2,192,256]{4,3,2,1,0:T(8,128)(2,1)}, u32[]{:S(2)}, u32[]{:S(2)}) async-start(bf16[4,2,2,192,256]{4,3,2,1,0:T(8,128)(2,1)} %bitcast.25), calls=%async_computation.2 | async-start | bytes 3145728 | tf_op jit(solution)/shard_map/all_to_all | solution.py:858
  162.0 41.6 %all-to-all-start.4 = ((bf16[4,2,2,192,256]{4,3,2,1,0:T(8,128)(2,1)}), bf16[4,2,2,192,256]{4,3,2,1,0:T(8,128)(2,1)}, u32[]{:S(2)}, u32[]{:S(2)}) async-start(bf16[4,2,2,192,256]{4,3,2,1,0:T(8,128)(2,1)} %copy-done.12), calls=%async_computation.4 | async-start | bytes 3145728 | tf_op jit(solution)/shard_map/all_to_all | solution.py:865
  203.6 40.9 %all-to-all-start.6 = ((bf16[4,2,2,192,256]{4,3,2,1,0:T(8,128)(2,1)}), bf16[4,2,2,192,256]{4,3,2,1,0:T(8,128)(2,1)}, u32[]{:S(2)}, u32[]{:S(2)}) async-start(bf16[4,2,2,192,256]{4,3,2,1,0:T(8,128)(2,1)} %copy-done.14), calls=%async_computation.6 | async-start | bytes 3145728 | tf_op jit(solution)/shard_map/all_to_all | solution.py:865
  207.9 29.5 %copy-start.3 = (f32[2,2,192,1024]{3,2,1,0:T(8,128)S(1)}, f32[2,2,192,1024]{3,2,1,0:T(8,128)}, u32[]{:S(2)}) copy-start(f32[2,2,192,1024]{3,2,1,0:T(8,128)} %copy-done.2) | copy-start | bytes 9437188
  207.9 29.5 %copy-start.5 = (f32[2,2,192,1024]{3,2,1,0:T(8,128)S(1)}, f32[2,2,192,1024]{3,2,1,0:T(8,128)}, u32[]{:S(2)}) copy-start(f32[2,2,192,1024]{3,2,1,0:T(8,128)} %copy-done.4) | copy-start | bytes 9437188
  215.3 7.6 %collective-permute-start.18 = (bf16[2,192,256]{2,1,0:T(8,128)(2,1)}, bf16[2,192,256]{2,1,0:T(8,128)(2,1)S(1)}, u32[]{:S(2)}, u32[]{:S(2)}) collective-permute-start(bf16[2,192,256]{2,1,0:T(8,128)(2,1)} %get-tuple-element.77), channel_id=1, source_target_pairs={{0,1},{1,2},{2,3},{3,4},{4,5},{5,6},{6,7},{7,0},{8,9},{9,10},{10,1... | collective-permute-start | bytes 589832 | tf_op jit(solution)/shard_map/ppermute | solution.py:803
  215.4 11.8 %collective-permute-start.19 = (bf16[2,192,256]{2,1,0:T(8,128)(2,1)}, bf16[2,192,256]{2,1,0:T(8,128)(2,1)S(1)}, u32[]{:S(2)}, u32[]{:S(2)}) collective-permute-start(bf16[2,192,256]{2,1,0:T(8,128)(2,1)} %get-tuple-element.78), channel_id=1, source_target_pairs={{0,2},{1,3},{2,4},{3,5},{4,6},{5,7},{6,0},{7,1},{8,10},{9,11},{10,... | collective-permute-start | bytes 589832 | tf_op jit(solution)/shard_map/ppermute | solution.py:803
  219.8 13.2 %collective-permute-start.20 = (bf16[2,192,256]{2,1,0:T(8,128)(2,1)}, bf16[2,192,256]{2,1,0:T(8,128)(2,1)S(1)}, u32[]{:S(2)}, u32[]{:S(2)}) collective-permute-start(bf16[2,192,256]{2,1,0:T(8,128)(2,1)} %get-tuple-element.79), channel_id=1, source_target_pairs={{0,3},{1,4},{2,5},{3,6},{4,7},{5,0},{6,1},{7,2},{8,11},{9,12},{10,... | collective-permute-start | bytes 589832 | tf_op jit(solution)/shard_map/ppermute | solution.py:803
  221.8 11.4 %collective-permute-start.21 = (bf16[2,192,256]{2,1,0:T(8,128)(2,1)}, bf16[2,192,256]{2,1,0:T(8,128)(2,1)S(1)}, u32[]{:S(2)}, u32[]{:S(2)}) collective-permute-start(bf16[2,192,256]{2,1,0:T(8,128)(2,1)} %get-tuple-element.80), channel_id=1, source_target_pairs={{0,4},{1,5},{2,6},{3,7},{4,0},{5,1},{6,2},{7,3},{8,12},{9,13},{10,... | collective-permute-start | bytes 589832 | tf_op jit(solution)/shard_map/ppermute | solution.py:803
  222.7 13.1 %collective-permute-start.22 = (bf16[2,192,256]{2,1,0:T(8,128)(2,1)}, bf16[2,192,256]{2,1,0:T(8,128)(2,1)S(1)}, u32[]{:S(2)}, u32[]{:S(2)}) collective-permute-start(bf16[2,192,256]{2,1,0:T(8,128)(2,1)} %get-tuple-element.81), channel_id=1, source_target_pairs={{0,5},{1,6},{2,7},{3,0},{4,1},{5,2},{6,3},{7,4},{8,13},{9,14},{10,... | collective-permute-start | bytes 589832 | tf_op jit(solution)/shard_map/ppermute | solution.py:803
  222.9 20.9 %copy-start.22 = (bf16[2,192,256]{2,1,0:T(8,128)(2,1)}, bf16[2,192,256]{2,1,0:T(8,128)(2,1)S(1)}, u32[]{:S(2)}) copy-start(bf16[2,192,256]{2,1,0:T(8,128)(2,1)S(1)} %collective-permute-done.18.refs_5_.refs_1_) | copy-start | bytes 589828
  222.9 12.9 %collective-permute-start.23 = (bf16[2,192,256]{2,1,0:T(8,128)(2,1)}, bf16[2,192,256]{2,1,0:T(8,128)(2,1)S(1)}, u32[]{:S(2)}, u32[]{:S(2)}) collective-permute-start(bf16[2,192,256]{2,1,0:T(8,128)(2,1)} %get-tuple-element.82), channel_id=1, source_target_pairs={{0,6},{1,7},{2,0},{3,1},{4,2},{5,3},{6,4},{7,5},{8,14},{9,15},{10,... | collective-permute-start | bytes 589832 | tf_op jit(solution)/shard_map/ppermute | solution.py:803
  227.2 10.3 %collective-permute-start.24 = (bf16[2,192,256]{2,1,0:T(8,128)(2,1)}, bf16[2,192,256]{2,1,0:T(8,128)(2,1)S(1)}, u32[]{:S(2)}, u32[]{:S(2)}) collective-permute-start(bf16[2,192,256]{2,1,0:T(8,128)(2,1)} %get-tuple-element.83), channel_id=1, source_target_pairs={{0,7},{1,0},{2,1},{3,2},{4,3},{5,4},{6,5},{7,6},{8,15},{9,8},{10,9... | collective-permute-start | bytes 589832 | tf_op jit(solution)/shard_map/ppermute | solution.py:803
  244.5 41.5 %all-to-all-start.5 = ((bf16[4,2,2,192,256]{4,3,2,1,0:T(8,128)(2,1)}), bf16[4,2,2,192,256]{4,3,2,1,0:T(8,128)(2,1)S(1)}, u32[]{:S(2)}, u32[]{:S(2)}) async-start(bf16[4,2,2,192,256]{4,3,2,1,0:T(8,128)(2,1)} %curl_inverse.5), calls=%async_computation.5 | async-start | bytes 3145728 | tf_op jit(solution)/shard_map/all_to_all | solution.py:865
  261.5 9.0 %collective-permute-start.25 = (bf16[2,192,256]{2,1,0:T(8,128)(2,1)}, bf16[2,192,256]{2,1,0:T(8,128)(2,1)S(1)}, u32[]{:S(2)}, u32[]{:S(2)}) collective-permute-start(bf16[2,192,256]{2,1,0:T(8,128)(2,1)} %get-tuple-element.86), channel_id=1, source_target_pairs={{0,1},{1,2},{2,3},{3,4},{4,5},{5,6},{6,7},{7,0},{8,9},{9,10},{10,1... | collective-permute-start | bytes 589832 | tf_op jit(solution)/shard_map/ppermute | solution.py:803
  261.5 10.8 %collective-permute-start.26 = (bf16[2,192,256]{2,1,0:T(8,128)(2,1)}, bf16[2,192,256]{2,1,0:T(8,128)(2,1)S(1)}, u32[]{:S(2)}, u32[]{:S(2)}) collective-permute-start(bf16[2,192,256]{2,1,0:T(8,128)(2,1)} %get-tuple-element.87), channel_id=1, source_target_pairs={{0,2},{1,3},{2,4},{3,5},{4,6},{5,7},{6,0},{7,1},{8,10},{9,11},{10,... | collective-permute-start | bytes 589832 | tf_op jit(solution)/shard_map/ppermute | solution.py:803
  265.1 14.2 %collective-permute-start.27 = (bf16[2,192,256]{2,1,0:T(8,128)(2,1)}, bf16[2,192,256]{2,1,0:T(8,128)(2,1)S(1)}, u32[]{:S(2)}, u32[]{:S(2)}) collective-permute-start(bf16[2,192,256]{2,1,0:T(8,128)(2,1)} %get-tuple-element.88), channel_id=1, source_target_pairs={{0,3},{1,4},{2,5},{3,6},{4,7},{5,0},{6,1},{7,2},{8,11},{9,12},{10,... | collective-permute-start | bytes 589832 | tf_op jit(solution)/shard_map/ppermute | solution.py:803
  267.1 12.4 %collective-permute-start.28 = (bf16[2,192,256]{2,1,0:T(8,128)(2,1)}, bf16[2,192,256]{2,1,0:T(8,128)(2,1)S(1)}, u32[]{:S(2)}, u32[]{:S(2)}) collective-permute-start(bf16[2,192,256]{2,1,0:T(8,128)(2,1)} %get-tuple-element.89), channel_id=1, source_target_pairs={{0,4},{1,5},{2,6},{3,7},{4,0},{5,1},{6,2},{7,3},{8,12},{9,13},{10,... | collective-permute-start | bytes 589832 | tf_op jit(solution)/shard_map/ppermute | solution.py:803
  267.9 14.2 %collective-permute-start.29 = (bf16[2,192,256]{2,1,0:T(8,128)(2,1)}, bf16[2,192,256]{2,1,0:T(8,128)(2,1)S(1)}, u32[]{:S(2)}, u32[]{:S(2)}) collective-permute-start(bf16[2,192,256]{2,1,0:T(8,128)(2,1)} %get-tuple-element.90), channel_id=1, source_target_pairs={{0,5},{1,6},{2,7},{3,0},{4,1},{5,2},{6,3},{7,4},{8,13},{9,14},{10,... | collective-permute-start | bytes 589832 | tf_op jit(solution)/shard_map/ppermute | solution.py:803
  270.4 22.7 %copy-start.20 = (bf16[2,192,256]{2,1,0:T(8,128)(2,1)}, bf16[2,192,256]{2,1,0:T(8,128)(2,1)S(1)}, u32[]{:S(2)}) copy-start(bf16[2,192,256]{2,1,0:T(8,128)(2,1)S(1)} %collective-permute-done.25.refs_1_) | copy-start | bytes 589828
  270.4 11.7 %collective-permute-start.30 = (bf16[2,192,256]{2,1,0:T(8,128)(2,1)}, bf16[2,192,256]{2,1,0:T(8,128)(2,1)S(1)}, u32[]{:S(2)}, u32[]{:S(2)}) collective-permute-start(bf16[2,192,256]{2,1,0:T(8,128)(2,1)} %get-tuple-element.91), channel_id=1, source_target_pairs={{0,6},{1,7},{2,0},{3,1},{4,2},{5,3},{6,4},{7,5},{8,14},{9,15},{10,... | collective-permute-start | bytes 589832 | tf_op jit(solution)/shard_map/ppermute | solution.py:803
  272.4 10.3 %collective-permute-start.31 = (bf16[2,192,256]{2,1,0:T(8,128)(2,1)}, bf16[2,192,256]{2,1,0:T(8,128)(2,1)S(1)}, u32[]{:S(2)}, u32[]{:S(2)}) collective-permute-start(bf16[2,192,256]{2,1,0:T(8,128)(2,1)} %get-tuple-element.92), channel_id=1, source_target_pairs={{0,7},{1,0},{2,1},{3,2},{4,3},{5,4},{6,5},{7,6},{8,15},{9,8},{10,9... | collective-permute-start | bytes 589832 | tf_op jit(solution)/shard_map/ppermute | solution.py:803
  293.2 26.9 %all-to-all-start.7 = ((bf16[8,2,192,256]{3,2,1,0:T(8,128)(2,1)}), bf16[8,2,192,256]{3,2,1,0:T(8,128)(2,1)S(1)}, u32[]{:S(2)}, u32[]{:S(2)}) async-start(bf16[8,2,192,256]{3,2,1,0:T(8,128)(2,1)} %y_inverse.1.refs_13_), calls=%async_computation.7 | async-start | bytes 3145728 | tf_op jit(solution)/shard_map/all_to_all | solution.py:877
  326.4 15.4 %collective-permute-start.34 = (bf16[3,16,256]{2,1,0:T(8,128)(2,1)}, bf16[3,16,256]{2,1,0:T(8,128)(2,1)S(1)}, u32[]{:S(2)}, u32[]{:S(2)}) collective-permute-start(bf16[3,16,256]{2,1,0:T(8,128)(2,1)} %get-tuple-element.108), channel_id=1, source_target_pairs={{0,1},{1,2},{2,3},{3,4},{4,5},{5,6},{6,7},{7,0},{8,9},{9,10},{10,1... | collective-permute-start | bytes 73736 | tf_op jit(solution)/shard_map/ppermute | solution.py:524
  326.4 15.3 %collective-permute-start.35 = (bf16[3,16,256]{2,1,0:T(8,128)(2,1)}, bf16[3,16,256]{2,1,0:T(8,128)(2,1)S(1)}, u32[]{:S(2)}, u32[]{:S(2)}) collective-permute-start(bf16[3,16,256]{2,1,0:T(8,128)(2,1)} %get-tuple-element.109), channel_id=1, source_target_pairs={{1,0},{2,1},{3,2},{4,3},{5,4},{6,5},{7,6},{0,7},{9,8},{10,9},{11,1... | collective-permute-start | bytes 73736 | tf_op jit(solution)/shard_map/ppermute | solution.py:524
  329.1 12.7 %collective-permute-start.32 = (bf16[3,16,192]{2,1,0:T(8,128)(2,1)}, bf16[3,16,192]{2,1,0:T(8,128)(2,1)S(1)}, u32[]{:S(2)}, u32[]{:S(2)}) collective-permute-start(bf16[3,16,192]{2,1,0:T(8,128)(2,1)} %get-tuple-element.106), channel_id=1, source_target_pairs={{0,8},{8,16},{16,24},{24,0},{1,9},{9,17},{17,25},{25,1},{2,10},{10... | collective-permute-start | bytes 55304 | tf_op jit(solution)/shard_map/ppermute | solution.py:524
  329.1 12.7 %collective-permute-start.33 = (bf16[3,16,192]{2,1,0:T(8,128)(2,1)}, bf16[3,16,192]{2,1,0:T(8,128)(2,1)S(1)}, u32[]{:S(2)}, u32[]{:S(2)}) collective-permute-start(bf16[3,16,192]{2,1,0:T(8,128)(2,1)} %get-tuple-element.107), channel_id=1, source_target_pairs={{8,0},{16,8},{24,16},{0,24},{9,1},{17,9},{25,17},{1,25},{10,2},{18... | collective-permute-start | bytes 55304 | tf_op jit(solution)/shard_map/ppermute | solution.py:524
  (53 other events, 304.7 us)

commit v12 on v11

--- a/solution.py
+++ b/solution.py
@@ -119,7 +119,7 @@
     return layers
 
 
-ROWS = 96
+ROWS = 48
 
 
 def tiles(height, width):
@@ -612,12 +612,15 @@
     return jnp.sum(jnp.where(index == n, rows.astype(f32), 0.0), axis=0, keepdims=True)
 
 
-def end_rows(low, high, height):
-    row = lax.broadcasted_iota(jnp.int32, (height, low.shape[1]), 0)
-    return jnp.where(row == 0, low * -0.5, 0.0) + jnp.where(row == height - 1, high * 0.5, 0.0)
-
-
-LAYERS = 4
+def with_end_rows(slope, low, high):
+    height, width = slope.shape
+    row = lax.broadcasted_iota(jnp.int32, (8, width), 0)
+    top = slope[:8] - jnp.where(row == 0, low, 0.0)
+    bottom = slope[height - 8 :] + jnp.where(row == 7, high, 0.0)
+    return jnp.concatenate([top, slope[8 : height - 8], bottom], axis=0)
+
+
+LAYERS = 8
 
 
 def grad_vort_kernel(
@@ -636,8 +639,11 @@
 ):
     before, after = refs
     height, width = velocity.shape[2], velocity.shape[3]
+    factor = 0.5 * step_size
     first = pl.program_id(0) * LAYERS
-    ends = spread_columns(low_x[0], high_x[0], first, LAYERS, width)
+    ends = spread_columns(
+        low_x[0].astype(f32) * step_size, high_x[0].astype(f32) * step_size, first, LAYERS, width
+    )
     layers = velocity[0]
     stacked = layers.reshape(LAYERS * height, width)
     deep = [velocity_below[0, 0]] + [layers[k] for k in range(LAYERS)] + [velocity_above[0, 0]]
@@ -645,13 +651,14 @@
     for k in range(LAYERS):
         n = first + k
         value = adjoint[k]
-        half = value * step_size
         along_x = inner[k * height : (k + 1) * height] + ends[k]
         along_y = jnp.dot(slope_y[...], layers[k], preferred_element_type=f32)
-        along_y = along_y + end_rows(pick_row(low_y[0], n), pick_row(high_y[0], n), height)
-        along_z = (deep[k + 2].astype(f32) - deep[k].astype(f32)) * 0.5
+        along_y = with_end_rows(
+            along_y, pick_row(low_y[0], n) * factor, pick_row(high_y[0], n) * factor
+        )
+        along_z = (deep[k + 2].astype(f32) - deep[k].astype(f32)) * factor
         for j, slope in enumerate((along_x, along_y, along_z)):
-            term = half * slope
+            term = value * slope
             if j == component:
                 term = term + value
             if before is not None:
@@ -820,8 +827,8 @@
 
     y_table, y_back_table = y_tables(size_x * halves)
     x_table, x_back_table = x_tables()
-    slope_x = slope_matrix(width)
-    slope_y = np.ascontiguousarray(slope_matrix(height).T)
+    slopes = [slope_matrix(width), np.ascontiguousarray(slope_matrix(height).T)]
+    slopes = [(slope * np.float32(step_size)).astype(slope.dtype) for slope in slopes]
 
     layers = depth_transform(cot_vel, FORWARD_ORDER[0])
 
@@ -890,7 +897,7 @@
     def vort_of(component, adjoint, before, after):
         kind = f32 if component == three else bf16
         return add_grad_vort(
-            component, (slope_x, slope_y), velocity, adjoint, saved_halos, before, after, kind
+            component, slopes, velocity, adjoint, saved_halos, before, after, kind
         )
 
     adjoint_one, short_one, *edges = make_adjoint(me, layers_one, cot_vort, one, [], ())
@@ -908,9 +915,8 @@
     halos = exchange(edges[0], edges[1], "gx") + exchange(edges[2], edges[3], "gy")
     grad_vort = vort_of(three, adjoint_three, grad_vort, ())
     shorts = {one: short_one, two: short_two, three: short_three}
-    scaled = [(slope * np.float32(-step_size)).astype(slope.dtype) for slope in (slope_x, slope_y)]
     grad_vel = write_grad_vel(
-        scaled, vorticity, [shorts[i] for i in range(3)], saved_halos, halos, (grad_vort,)
+        [-slope for slope in slopes], vorticity, [shorts[i] for i in range(3)], saved_halos, halos, (grad_vort,)
     )
     return grad_vort, grad_vel
 

time: 355 us -> 358 us (level)
  Pallas kernels: 121 us -> 125 us
  transfers between devices with their start and end apart: 44 -> 44, of which waited for: 29 -> 28; matrix products, arithmetic and copies ran while one was open for 1% -> 1% of each run, Pallas kernels for 27% -> 27%
where the time goes in v12:
time: 358 us; the launch traced here: 356 us
  Pallas kernels  125 us (35%)
  waiting for transfers between devices  112 us (31%)
  starting transfers between devices  94.1 us (26%)
  local copies, waits for them, and re-layouts  22 us (6%)
    ppermute x28, starting transfers between devices, shifted(): lax.ppermute(parts[s], axis, [(i, (i + s) % count) for i in range(count)])  42.5 us
    ppermute x28, waiting for transfers between devices, shifted(): lax.ppermute(parts[s], axis, [(i, (i + s) % count) for i in range(count)])  34.6 us
    all_to_all x3, waiting for transfers between devices, spectrum(): lines = lax.all_to_all(sent[place], 'gx', 0, 0, tiled=True)  29.3 us
    all_to_all x3, waiting for transfers between devices, back(): parts = lax.all_to_all(filtered, 'gx', 0, 0, tiled=True)  27.6 us
    pallas_call x3, Pallas kernels, add_grad_vort(): pl.pallas_call(kernel, grid=(Z // LAYERS,), in_specs=in_specs + tied(afte...  20.7 us
    unnamed x118, local copies, waits for them, and re-layouts  20 us
    pallas_call x3, Pallas kernels, make_adjoint(): pl.pallas_call(kernel, grid=(height // ROWS,), in_specs=[pl.BlockSpec(mem...  18.6 us
    ppermute x8, waiting for transfers between devices, exchange(): return (lax.ppermute(last, axis, up), lax.ppermute(first, axis, down))  15.1 us
  transfers between devices with their start and end apart: 44, of which 28 were waited for; matrix products, arithmetic and copies ran while one was open for 1% of the time, Pallas kernels for 27%

profile of v12, /device:TPU:0, one launch (start us, length us, event | category | flops | bytes accessed | tf_op | source)
XLA Modules:
  0.0 355.8 jit_solution(18155065813607935065)
XLA Ops:
  0.6 4.2 %depth_transform.3.refs_0_ = bf16[16,192,256]{2,1,0:T(8,128)(2,1)} custom-call(f32[3,16,192,256]{3,2,1,0:T(8,128)} %refs_1_.11), custom_call_target="tpu_custom_call" | custom-call | flops 1 | bytes 9000000 | tf_op jit(solution)/shard_map/depth_transform/pallas_call | solution.py:161
  4.9 5.2 %all-to-all-start = ((bf16[8,2,192,256]{3,2,1,0:T(8,128)(2,1)}), bf16[8,2,192,256]{3,2,1,0:T(8,128)(2,1)S(1)}, u32[]{:S(2)}, u32[]{:S(2)}) async-start(bf16[8,2,192,256]{3,2,1,0:T(8,128)(2,1)} %bitcast.28), calls=%async_computation | async-start | bytes 3145728 | tf_op jit(solution)/shard_map/all_to_all | solution.py:851
  12.6 4.6 %edge_columns.2 = (bf16[3,16,192]{2,1,0:T(8,128)(2,1)}, bf16[3,16,192]{2,1,0:T(8,128)(2,1)}) custom-call(bf16[3,16,192,256]{3,2,1,0:T(8,128)(2,1)} %refs_4_.6, bf16[16,192,256]{2,1,0:T(8,128)(2,1)} %depth_transform.3.refs_0_), custom_call_target="tpu_custom_call" | custom-call | flops 1 | bytes 12000000 | tf_op jit(solution)/shard_map/edge_columns/pallas_call | solution.py:508
  18.0 3.7 %collective-permute-start.1 = (bf16[4,16,192]{2,1,0:T(8,128)(2,1)S(1)}, bf16[4,16,192]{2,1,0:T(8,128)(2,1)S(1)}, u32[]{:S(2)}, u32[]{:S(2)}) collective-permute-start(bf16[4,16,192]{2,1,0:T(8,128)(2,1)S(1)} %pad_maximum_fusion.1), channel_id=1, source_target_pairs={{8,0},{16,8},{24,16},{0,24},{9,1},{17,9},{25,17},{1,25},{10,2},{18... | collective-permute-start | bytes 73736 | tf_op jit(solution)/shard_map/ppermute | solution.py:524
  23.2 4.9 %collective-permute-done.refs_0_.refs_6_.refs_14_ = bf16[4,16,192]{2,1,0:T(8,128)(2,1)S(1)} collective-permute-done((bf16[4,16,192]{2,1,0:T(8,128)(2,1)S(1)}, bf16[4,16,192]{2,1,0:T(8,128)(2,1)S(1)}, u32[]{:S(2)}, u32[]{:S(2)}) %collective-permute-start) | collective-permute-done | bytes 24608 | tf_op jit(solution)/shard_map/ppermute | solution.py:524
  28.1 2.9 all-to-all-done.columns_ref
  33.4 3.9 %y_transform.1 = bf16[4,1,2,2,192,256]{5,4,3,2,1,0:T(8,128)(2,1)} custom-call(bf16[1536,1536]{1,0:T(8,128)(2,1)S(1)} %copy-done.1, bf16[8,2,192,256]{3,2,1,0:T(8,128)(2,1)S(1)} %all-to-all-done.columns_ref, bf16[4,16,192]{2,1,0:T(8,128)(2,1)S(1)} %collective-permute-done.refs_0_.refs_6_.refs_14_, ...), custom_call_target="tpu_custom_call" | custom-call | flops 1 | bytes 12000000 | tf_op jit(solution)/shard_map/y_transform/pallas_call | solution.py:198
  37.3 4.9 %all-to-all-start.1 = ((bf16[4,2,2,192,256]{4,3,2,1,0:T(8,128)(2,1)}), bf16[4,2,2,192,256]{4,3,2,1,0:T(8,128)(2,1)S(1)}, u32[]{:S(2)}, u32[]{:S(2)}) async-start(bf16[4,2,2,192,256]{4,3,2,1,0:T(8,128)(2,1)} %bitcast.3.refs_2_), calls=%async_computation.1 | async-start | bytes 3145728 | tf_op jit(solution)/shard_map/all_to_all | solution.py:865
  44.2 4.3 %depth_transform.4 = (bf16[2,192,256]{2,1,0:T(8,128)(2,1)}, bf16[2,192,256]{2,1,0:T(8,128)(2,1)}, bf16[2,192,256]{2,1,0:T(8,128)(2,1)}, bf16[2,192,256]{2,1,0:T(...) custom-call(s32[1]{0:T(128)} %bitcast.refs_0_.me_ref, ...), custom_call_target="tpu_custom_call" | custom-call | flops 1 | bytes 9000000 | tf_op jit(solution)/shard_map/depth_transform/pallas_call | solution.py:161
  51.8 9.4 %collective-permute-done.9.refs_8_.refs_16_ = bf16[4,16,256]{2,1,0:T(8,128)(2,1)S(1)} collective-permute-done((bf16[4,16,256]{2,1,0:T(8,128)(2,1)S(1)}, bf16[4,16,256]{2,1,0:T(8,128)(2,1)S(1)}, u32[]{:S(2)}, u32[]{:S(2)}) %collective-permute-start.9) | collective-permute-done | bytes 32800 | tf_op jit(solution)/shard_map/ppermute | solution.py:524
  64.5 3.2 collective-permute-done.5.refs_4_
  72.2 6.6 %y_transform_parts.2 = bf16[4,1,2,2,192,256]{5,4,3,2,1,0:T(8,128)(2,1)} custom-call(s32[1]{0:T(128)} %bitcast.refs_0_.me_ref, bf16[1536,1536]{1,0:T(8,128)(2,1)} %constant.37.clone.table_ref, bf16[2,192,256]{2,1,0:T(8,128)(2,1)} %get-tuple-element.60.refs_0_, bf16[2,192,256]{2,1,0:T(8,128)(2,1)} %copy-done.37, bf16[2,192,256]{2,1,0:T(8,128)(2,1)} %copy-done.38, ...), custom_call_target="tpu_custom_call" | custom-call | flops 1 | bytes 15000000 | tf_op jit(solution)/shard_map/y_transform_parts/pallas_call | solution.py:252
  78.8 5.1 %all-to-all-start.3 = ((bf16[4,2,2,192,256]{4,3,2,1,0:T(8,128)(2,1)}), bf16[4,2,2,192,256]{4,3,2,1,0:T(8,128)(2,1)}, u32[]{:S(2)}, u32[]{:S(2)}) async-start(bf16[4,2,2,192,256]{4,3,2,1,0:T(8,128)(2,1)} %bitcast.22), calls=%async_computation.3 | async-start | bytes 3145728 | tf_op jit(solution)/shard_map/all_to_all | solution.py:865
  83.9 4.3 %depth_transform.5 = (bf16[2,192,256]{2,1,0:T(8,128)(2,1)}, bf16[2,192,256]{2,1,0:T(8,128)(2,1)}, bf16[2,192,256]{2,1,0:T(8,128)(2,1)}, bf16[2,192,256]{2,1,0:T(...) custom-call(s32[1]{0:T(128)} %bitcast.refs_0_.me_ref, ...), custom_call_target="tpu_custom_call" | custom-call | flops 1 | bytes 9000000 | tf_op jit(solution)/shard_map/depth_transform/pallas_call | solution.py:161
  89.9 4.2 %collective-permute-start.12 = (bf16[2,192,256]{2,1,0:T(8,128)(2,1)}, bf16[2,192,256]{2,1,0:T(8,128)(2,1)S(1)}, u32[]{:S(2)}, u32[]{:S(2)}) collective-permute-start(bf16[2,192,256]{2,1,0:T(8,128)(2,1)} %get-tuple-element.70), channel_id=1, source_target_pairs={{0,2},{1,3},{2,4},{3,5},{4,6},{5,7},{6,0},{7,1},{8,10},{9,11},{10,... | collective-permute-start | bytes 589832 | tf_op jit(solution)/shard_map/ppermute | solution.py:810
  103.0 5.3 %collective-permute-done.13.refs_3_ = bf16[2,192,256]{2,1,0:T(8,128)(2,1)S(1)} collective-permute-done((bf16[2,192,256]{2,1,0:T(8,128)(2,1)}, bf16[2,192,256]{2,1,0:T(8,128)(2,1)S(1)}, u32[]{:S(2)}, u32[]{:S(2)}) %collective-permute-start.13) | collective-permute-done | bytes 196640 | tf_op jit(solution)/shard_map/ppermute | solution.py:810
  111.9 6.6 %y_transform_parts.3 = bf16[4,1,2,2,192,256]{5,4,3,2,1,0:T(8,128)(2,1)} custom-call(s32[1]{0:T(128)} %bitcast.refs_0_.me_ref, bf16[1536,1536]{1,0:T(8,128)(2,1)} %constant.37.clone.table_ref, bf16[2,192,256]{2,1,0:T(8,128)(2,1)} %get-tuple-element.68.refs_0_, bf16[2,192,256]{2,1,0:T(8,128)(2,1)} %copy-done.40, bf16[2,192,256]{2,1,0:T(8,128)(2,1)} %copy-done.41, ...), custom_call_target="tpu_custom_call" | custom-call | flops 1 | bytes 15000000 | tf_op jit(solution)/shard_map/y_transform_parts/pallas_call | solution.py:252
  118.5 3.1 all-to-all-done.3.modes_ref
  121.7 4.4 %all-to-all-start.2 = ((bf16[4,2,2,192,256]{4,3,2,1,0:T(8,128)(2,1)}), bf16[4,2,2,192,256]{4,3,2,1,0:T(8,128)(2,1)}, u32[]{:S(2)}, u32[]{:S(2)}) async-start(bf16[4,2,2,192,256]{4,3,2,1,0:T(8,128)(2,1)} %bitcast.25), calls=%async_computation.2 | async-start | bytes 3145728 | tf_op jit(solution)/shard_map/all_to_all | solution.py:865
  129.8 3.9 %x_transform.4.refs_2_.refs_3_ = f32[2,2,192,1024]{3,2,1,0:T(8,128)S(1)} custom-call(bf16[1024,1024]{1,0:T(8,128)(2,1)S(1)} %copy-done.10, bf16[4,2,2,192,256]{4,3,2,1,0:T(8,128)(2,1)} %all-to-all-done.3.modes_ref, bf16[4,2,2,192,256]{4,3,2,1,0:T(8,128)(2,1)S(1)} %bitcast.26), custom_call_target="tpu_custom_call" | custom-call | flops 1 | bytes 9000000 | tf_op jit(solution)/shard_map/x_transform/pallas_call | solution.py:370
  133.7 3.0 curl_inverse.3.refs_0_
  137.8 26.2 %all-to-all-done.2.modes_ref = bf16[4,2,2,192,256]{4,3,2,1,0:T(8,128)(2,1)} async-done(((bf16[4,2,2,192,256]{4,3,2,1,0:T(8,128)(2,1)}), bf16[4,2,2,192,256]{4,3,2,1,0:T(8,128)(2,1)}, u32[]{:S(2)}, u32[]{:S(2)}) %all-to-all-start.2) | async-done | bytes 1572896 | tf_op jit(solution)/shard_map/all_to_all | solution.py:865
  164.0 4.5 %all-to-all-start.4 = ((bf16[4,2,2,192,256]{4,3,2,1,0:T(8,128)(2,1)}), bf16[4,2,2,192,256]{4,3,2,1,0:T(8,128)(2,1)}, u32[]{:S(2)}, u32[]{:S(2)}) async-start(bf16[4,2,2,192,256]{4,3,2,1,0:T(8,128)(2,1)} %copy-done.12), calls=%async_computation.4 | async-start | bytes 3145728 | tf_op jit(solution)/shard_map/all_to_all | solution.py:872
  171.6 3.3 x_transform.5.refs_2_.refs_3_
  174.9 3.0 curl_inverse.4.refs_0_
  180.7 24.9 %all-to-all-done.4 = bf16[4,2,2,192,256]{4,3,2,1,0:T(8,128)(2,1)} async-done(((bf16[4,2,2,192,256]{4,3,2,1,0:T(8,128)(2,1)}), bf16[4,2,2,192,256]{4,3,2,1,0:T(8,128)(2,1)}, u32[]{:S(2)}, u32[]{:S(2)}) %all-to-all-start.4) | async-done | bytes 1572896 | tf_op jit(solution)/shard_map/all_to_all | solution.py:872
  205.6 4.4 %all-to-all-start.6 = ((bf16[4,2,2,192,256]{4,3,2,1,0:T(8,128)(2,1)}), bf16[4,2,2,192,256]{4,3,2,1,0:T(8,128)(2,1)}, u32[]{:S(2)}, u32[]{:S(2)}) async-start(bf16[4,2,2,192,256]{4,3,2,1,0:T(8,128)(2,1)} %copy-done.14), calls=%async_computation.6 | async-start | bytes 3145728 | tf_op jit(solution)/shard_map/all_to_all | solution.py:872
  210.0 7.4 %y_inverse_parts.2 = (bf16[2,192,256]{2,1,0:T(8,128)(2,1)}, bf16[2,192,256]{2,1,0:T(8,128)(2,1)}, bf16[2,192,256]{2,1,0:T(8,128)(2,1)}, bf16[2,192,256]{2,1,0:T(...) custom-call(s32[1]{0:T(128)} %bitcast.refs_0_.me_ref, ...), custom_call_target="tpu_custom_call" | custom-call | flops 1 | bytes 12000000 | tf_op jit(solution)/shard_map/y_inverse_parts/pallas_call | solution.py:340
  217.4 4.4 %collective-permute-start.19 = (bf16[2,192,256]{2,1,0:T(8,128)(2,1)}, bf16[2,192,256]{2,1,0:T(8,128)(2,1)S(1)}, u32[]{:S(2)}, u32[]{:S(2)}) collective-permute-start(bf16[2,192,256]{2,1,0:T(8,128)(2,1)} %get-tuple-element.78), channel_id=1, source_target_pairs={{0,2},{1,3},{2,4},{3,5},{4,6},{5,7},{6,0},{7,1},{8,10},{9,11},{10,... | collective-permute-start | bytes 589832 | tf_op jit(solution)/shard_map/ppermute | solution.py:810
  224.7 4.2 %collective-permute-start.23 = (bf16[2,192,256]{2,1,0:T(8,128)(2,1)}, bf16[2,192,256]{2,1,0:T(8,128)(2,1)S(1)}, u32[]{:S(2)}, u32[]{:S(2)}) collective-permute-start(bf16[2,192,256]{2,1,0:T(8,128)(2,1)} %get-tuple-element.82), channel_id=1, source_target_pairs={{0,6},{1,7},{2,0},{3,1},{4,2},{5,3},{6,4},{7,5},{8,14},{9,15},{10,... | collective-permute-start | bytes 589832 | tf_op jit(solution)/shard_map/ppermute | solution.py:810
  229.0 4.0 %collective-permute-start.24 = (bf16[2,192,256]{2,1,0:T(8,128)(2,1)}, bf16[2,192,256]{2,1,0:T(8,128)(2,1)S(1)}, u32[]{:S(2)}, u32[]{:S(2)}) collective-permute-start(bf16[2,192,256]{2,1,0:T(8,128)(2,1)} %get-tuple-element.83), channel_id=1, source_target_pairs={{0,7},{1,0},{2,1},{3,2},{4,3},{5,4},{6,5},{7,6},{8,15},{9,8},{10,9... | collective-permute-start | bytes 589832 | tf_op jit(solution)/shard_map/ppermute | solution.py:810
  235.0 2.9 collective-permute-done.22.refs_9_.refs_5_
  242.1 3.8 %curl_inverse.5 = bf16[4,2,2,192,256]{4,3,2,1,0:T(8,128)(2,1)} custom-call(s32[2]{0:T(128)S(1)} %pad_add_fusion.refs_0_, bf16[1024,1024]{1,0:T(8,128)(2,1)S(1)} %copy-done.9, f32[2,2,192,1024]{3,2,1,0:T(8,128)S(1)} %copy-done.3, f32[2,2,192,1024]{3,2,1,0:T(8,128)S(1)} %copy-done.5, bf16[2,192,256]{2,1,0:T(8,128)(2,1)S(1)} %copy-done.19, ...), custom_call_target="tpu_custom_call" | custom-call | flops 1 | bytes 12000000 | tf_op jit(solution)/shard_map/curl_inverse/pallas_call | solution.py:446
  246.5 4.4 %all-to-all-start.5 = ((bf16[4,2,2,192,256]{4,3,2,1,0:T(8,128)(2,1)}), bf16[4,2,2,192,256]{4,3,2,1,0:T(8,128)(2,1)S(1)}, u32[]{:S(2)}, u32[]{:S(2)}) async-start(bf16[4,2,2,192,256]{4,3,2,1,0:T(8,128)(2,1)} %curl_inverse.5), calls=%async_computation.5 | async-start | bytes 3145728 | tf_op jit(solution)/shard_map/all_to_all | solution.py:872
  251.0 6.3 %make_adjoint.3 = (f32[16,192,256]{2,1,0:T(8,128)}, bf16[16,192,256]{2,1,0:T(8,128)(2,1)}, bf16[3,16,192]{2,1,0:T(8,128)(2,1)}, bf16[3,16,192]{2,1,0:T(8,128)(2,...) custom-call(s32[1]{0:T(128)} %bitcast.refs_0_.me_ref, ...), custom_call_target="tpu_custom_call" | custom-call | flops 1 | bytes 15000000 | tf_op jit(solution)/shard_map/make_adjoint/pallas_call | solution.py:575
  257.3 7.2 %y_inverse_parts.3 = (bf16[2,192,256]{2,1,0:T(8,128)(2,1)}, bf16[2,192,256]{2,1,0:T(8,128)(2,1)}, bf16[2,192,256]{2,1,0:T(8,128)(2,1)}, bf16[2,192,256]{2,1,0:T(...) custom-call(s32[1]{0:T(128)} %bitcast.refs_0_.me_ref, ...), custom_call_target="tpu_custom_call" | custom-call | flops 1 | bytes 12000000 | tf_op jit(solution)/shard_map/y_inverse_parts/pallas_call | solution.py:340
  264.6 3.6 %collective-permute-start.26 = (bf16[2,192,256]{2,1,0:T(8,128)(2,1)}, bf16[2,192,256]{2,1,0:T(8,128)(2,1)S(1)}, u32[]{:S(2)}, u32[]{:S(2)}) collective-permute-start(bf16[2,192,256]{2,1,0:T(8,128)(2,1)} %get-tuple-element.87), channel_id=1, source_target_pairs={{0,2},{1,3},{2,4},{3,5},{4,6},{5,7},{6,0},{7,1},{8,10},{9,11},{10,... | collective-permute-start | bytes 589832 | tf_op jit(solution)/shard_map/ppermute | solution.py:810
  275.1 3.9 %collective-permute-start.31 = (bf16[2,192,256]{2,1,0:T(8,128)(2,1)}, bf16[2,192,256]{2,1,0:T(8,128)(2,1)S(1)}, u32[]{:S(2)}, u32[]{:S(2)}) collective-permute-start(bf16[2,192,256]{2,1,0:T(8,128)(2,1)} %get-tuple-element.92), channel_id=1, source_target_pairs={{0,7},{1,0},{2,1},{3,2},{4,3},{5,4},{6,5},{7,6},{8,15},{9,8},{10,9... | collective-permute-start | bytes 589832 | tf_op jit(solution)/shard_map/ppermute | solution.py:810
  279.0 3.1 collective-permute-done.27.refs_3_
  291.0 3.9 %y_inverse.1.refs_13_ = bf16[8,2,192,256]{3,2,1,0:T(8,128)(2,1)} custom-call(bf16[1536,1536]{1,0:T(8,128)(2,1)S(1)} %copy-done, bf16[4,1,2,2,192,256]{5,4,3,2,1,0:T(8,128)(2,1)S(1)} %bitcast.27, bf16[2,192,256]{2,1,0:T(8,128)(2,1)S(1)} %copy-done.16, bf16[2,192,256]{2,1,0:T(8,128)(2,1)S(1)} %collective-permute-done.25.refs_1_, ...), custom_call_target="tpu_custom_call" | custom-call | flops 1 | bytes 12000000 | tf_op jit(solution)/shard_map/y_inverse/pallas_call | solution.py:285
  295.0 5.8 %all-to-all-start.7 = ((bf16[8,2,192,256]{3,2,1,0:T(8,128)(2,1)}), bf16[8,2,192,256]{3,2,1,0:T(8,128)(2,1)S(1)}, u32[]{:S(2)}, u32[]{:S(2)}) async-start(bf16[8,2,192,256]{3,2,1,0:T(8,128)(2,1)} %y_inverse.1.refs_13_), calls=%async_computation.7 | async-start | bytes 3145728 | tf_op jit(solution)/shard_map/all_to_all | solution.py:884
  300.8 5.2 %add_grad_vort.3.refs_10_ = bf16[3,16,192,256]{3,2,1,0:T(8,128)(2,1)} custom-call(bf16[256,256]{1,0:T(8,128)(2,1)} %constant.41.clone.refs_0_, bf16[192,192]{1,0:T(8,128)(2,1)} %constant.42.clone.refs_1_, bf16[3,16,192,256]{3,2,1,0:T(8,128)(2,1)} %refs_4_.6, bf16[3,16,192,256]{3,2,1,0:T(8,128)(2,1)} %refs_4_.6, bf16[3,16,192,256]{3,2,1,0:T(8,128)(2,1)} %refs_4_.6, ...), custom_call_target="tpu_custom_call" | custom-call | flops 1 | bytes 27000000 | tf_op jit(solution)/shard_map/add_grad_vort/pallas_call | solution.py:698
  306.0 6.3 %make_adjoint.4 = (f32[16,192,256]{2,1,0:T(8,128)}, bf16[16,192,256]{2,1,0:T(8,128)(2,1)}, bf16[3,16,192]{2,1,0:T(8,128)(2,1)}, bf16[3,16,192]{2,1,0:T(8,128)(2,...) custom-call(s32[1]{0:T(128)} %bitcast.refs_0_.me_ref, ...), custom_call_target="tpu_custom_call", output_to_operand_aliasing={{2}: (10, {}), {3}: (11, {}), {4}: (12, {}), {5}: (13, {})} | custom-call | flops 1 | bytes 15000000 | tf_op jit(solution)/shard_map/make_adjoint/pallas_call | solution.py:575
  312.3 7.1 %add_grad_vort.4.refs_6_.refs_10_ = bf16[3,16,192,256]{3,2,1,0:T(8,128)(2,1)} custom-call(bf16[256,256]{1,0:T(8,128)(2,1)} %constant.41.clone.refs_0_, bf16[192,192]{1,0:T(8,128)(2,1)} %constant.42.clone.refs_1_, bf16[3,16,192,256]{3,2,1,0:T(8,128)(2,1)} %refs_4_.6, bf16[3,16,192,256]{3,2,1,0:T(8,128)(2,1)} %refs_4_.6, bf16[3,16,192,256]{3,2,1,0:T(8,128)(2,1)} %refs_4_.6, ...), custom_call_target="tpu_custom_call" | custom-call | flops 1 | bytes 27000000 | tf_op jit(solution)/shard_map/add_grad_vort/pallas_call | solution.py:698
  323.0 6.0 %make_adjoint.5 = (f32[16,192,256]{2,1,0:T(8,128)}, bf16[16,192,256]{2,1,0:T(8,128)(2,1)}, bf16[3,16,192]{2,1,0:T(8,128)(2,1)}, bf16[3,16,192]{2,1,0:T(8,128)(2,...) custom-call(s32[1]{0:T(128)} %bitcast.refs_0_.me_ref, ...), custom_call_target="tpu_custom_call", output_to_operand_aliasing={{2}: (3, {}), {3}: (4, {}), {4}: (5, {}), {5}: (6, {})} | custom-call | flops 1 | bytes 15000000 | tf_op jit(solution)/shard_map/make_adjoint/pallas_call | solution.py:575
  331.7 3.8 %collective-permute-start.33 = (bf16[3,16,192]{2,1,0:T(8,128)(2,1)}, bf16[3,16,192]{2,1,0:T(8,128)(2,1)S(1)}, u32[]{:S(2)}, u32[]{:S(2)}) collective-permute-start(bf16[3,16,192]{2,1,0:T(8,128)(2,1)} %get-tuple-element.107), channel_id=1, source_target_pairs={{8,0},{16,8},{24,16},{0,24},{9,1},{17,9},{25,17},{1,25},{10,2},{18... | collective-permute-start | bytes 55304 | tf_op jit(solution)/shard_map/ppermute | solution.py:524
  335.5 8.4 %add_grad_vort.5.refs_22_ = f32[3,16,192,256]{3,2,1,0:T(8,128)} custom-call(bf16[256,256]{1,0:T(8,128)(2,1)} %constant.41.clone.refs_0_, bf16[192,192]{1,0:T(8,128)(2,1)} %constant.42.clone.refs_1_, bf16[3,16,192,256]{3,2,1,0:T(8,128)(2,1)} %refs_4_.6, bf16[3,16,192,256]{3,2,1,0:T(8,128)(2,1)} %refs_4_.6, bf16[3,16,192,256]{3,2,1,0:T(8,128)(2,1)} %refs_4_.6, ...), custom_call_target="tpu_custom_call" | custom-call | flops 1 | bytes 27000000 | tf_op jit(solution)/shard_map/add_grad_vort/pallas_call | solution.py:698
  344.6 11.0 %write_grad_vel.1 = f32[3,16,192,256]{3,2,1,0:T(8,128)} custom-call(bf16[256,256]{1,0:T(8,128)(2,1)} %constant.43.clone.refs_0_, bf16[192,192]{1,0:T(8,128)(2,1)} %constant.44.clone.refs_1_, bf16[3,16,192,256]{3,2,1,0:T(8,128)(2,1)} %refs_4_.7, bf16[3,16,192,256]{3,2,1,0:T(8,128)(2,1)} %refs_4_.7, bf16[3,16,192,256]{3,2,1,0:T(8,128)(2,1)} %refs_4_.7, ...), custom_call_target="tpu_custom_call" | custom-call | flops 1 | bytes 36000000 | tf_op jit(solution)/shard_map/write_grad_vel/pallas_call | solution.py:787
  (189 shorter events, 77.9 us)
Async XLA Ops:
  4.9 26.2 %all-to-all-start = ((bf16[8,2,192,256]{3,2,1,0:T(8,128)(2,1)}), bf16[8,2,192,256]{3,2,1,0:T(8,128)(2,1)S(1)}, u32[]{:S(2)}, u32[]{:S(2)}) async-start(bf16[8,2,192,256]{3,2,1,0:T(8,128)(2,1)} %bitcast.28), calls=%async_computation | async-start | bytes 3145728 | tf_op jit(solution)/shard_map/all_to_all | solution.py:851
  18.0 5.3 %collective-permute-start.1 = (bf16[4,16,192]{2,1,0:T(8,128)(2,1)S(1)}, bf16[4,16,192]{2,1,0:T(8,128)(2,1)S(1)}, u32[]{:S(2)}, u32[]{:S(2)}) collective-permute-start(bf16[4,16,192]{2,1,0:T(8,128)(2,1)S(1)} %pad_maximum_fusion.1), channel_id=1, source_target_pairs={{8,0},{16,8},{24,16},{0,24},{9,1},{17,9},{25,17},{1,25},{10,2},{18... | collective-permute-start | bytes 73736 | tf_op jit(solution)/shard_map/ppermute | solution.py:524
  22.4 5.8 %collective-permute-start = (bf16[4,16,192]{2,1,0:T(8,128)(2,1)S(1)}, bf16[4,16,192]{2,1,0:T(8,128)(2,1)S(1)}, u32[]{:S(2)}, u32[]{:S(2)}) collective-permute-start(bf16[4,16,192]{2,1,0:T(8,128)(2,1)S(1)} %pad_maximum_fusion), channel_id=1, source_target_pairs={{0,8},{8,16},{16,24},{24,0},{1,9},{9,17},{17,25},{25,1},{2,10},{10... | collective-permute-start | bytes 73736 | tf_op jit(solution)/shard_map/ppermute | solution.py:524
  37.3 41.5 %all-to-all-start.1 = ((bf16[4,2,2,192,256]{4,3,2,1,0:T(8,128)(2,1)}), bf16[4,2,2,192,256]{4,3,2,1,0:T(8,128)(2,1)S(1)}, u32[]{:S(2)}, u32[]{:S(2)}) async-start(bf16[4,2,2,192,256]{4,3,2,1,0:T(8,128)(2,1)} %bitcast.3.refs_2_), calls=%async_computation.1 | async-start | bytes 3145728 | tf_op jit(solution)/shard_map/all_to_all | solution.py:865
  48.5 13.3 %collective-permute-start.2 = (bf16[2,192,256]{2,1,0:T(8,128)(2,1)}, bf16[2,192,256]{2,1,0:T(8,128)(2,1)S(1)}, u32[]{:S(2)}, u32[]{:S(2)}) collective-permute-start(bf16[2,192,256]{2,1,0:T(8,128)(2,1)} %get-tuple-element.61), channel_id=1, source_target_pairs={{0,1},{1,2},{2,3},{3,4},{4,5},{5,6},{6,7},{7,0},{8,9},{9,10},{10,1... | collective-permute-start | bytes 589832 | tf_op jit(solution)/shard_map/ppermute | solution.py:810
  48.5 13.8 %collective-permute-start.3 = (bf16[2,192,256]{2,1,0:T(8,128)(2,1)}, bf16[2,192,256]{2,1,0:T(8,128)(2,1)S(1)}, u32[]{:S(2)}, u32[]{:S(2)}) collective-permute-start(bf16[2,192,256]{2,1,0:T(8,128)(2,1)} %get-tuple-element.62), channel_id=1, source_target_pairs={{0,2},{1,3},{2,4},{3,5},{4,6},{5,7},{6,0},{7,1},{8,10},{9,11},{10,... | collective-permute-start | bytes 589832 | tf_op jit(solution)/shard_map/ppermute | solution.py:810
  49.1 12.1 %collective-permute-start.9 = (bf16[4,16,256]{2,1,0:T(8,128)(2,1)S(1)}, bf16[4,16,256]{2,1,0:T(8,128)(2,1)S(1)}, u32[]{:S(2)}, u32[]{:S(2)}) collective-permute-start(bf16[4,16,256]{2,1,0:T(8,128)(2,1)S(1)} %pad_maximum_fusion.2), channel_id=1, source_target_pairs={{0,1},{1,2},{2,3},{3,4},{4,5},{5,6},{6,7},{7,0},{8,9},{9,10},{10,1... | collective-permute-start | bytes 98312 | tf_op jit(solution)/shard_map/ppermute | solution.py:524
  50.4 11.4 %collective-permute-start.10 = (bf16[4,16,256]{2,1,0:T(8,128)(2,1)S(1)}, bf16[4,16,256]{2,1,0:T(8,128)(2,1)S(1)}, u32[]{:S(2)}, u32[]{:S(2)}) collective-permute-start(bf16[4,16,256]{2,1,0:T(8,128)(2,1)S(1)} %pad_maximum_fusion.3), channel_id=1, source_target_pairs={{1,0},{2,1},{3,2},{4,3},{5,4},{6,5},{7,6},{0,7},{9,8},{10,9},{11,1... | collective-permute-start | bytes 98312 | tf_op jit(solution)/shard_map/ppermute | solution.py:524
  51.8 12.7 %collective-permute-start.4 = (bf16[2,192,256]{2,1,0:T(8,128)(2,1)}, bf16[2,192,256]{2,1,0:T(8,128)(2,1)S(1)}, u32[]{:S(2)}, u32[]{:S(2)}) collective-permute-start(bf16[2,192,256]{2,1,0:T(8,128)(2,1)} %get-tuple-element.63), channel_id=1, source_target_pairs={{0,3},{1,4},{2,5},{3,6},{4,7},{5,0},{6,1},{7,2},{8,11},{9,12},{10,... | collective-permute-start | bytes 589832 | tf_op jit(solution)/shard_map/ppermute | solution.py:810
  61.2 6.5 %collective-permute-start.5 = (bf16[2,192,256]{2,1,0:T(8,128)(2,1)}, bf16[2,192,256]{2,1,0:T(8,128)(2,1)S(1)}, u32[]{:S(2)}, u32[]{:S(2)}) collective-permute-start(bf16[2,192,256]{2,1,0:T(8,128)(2,1)} %get-tuple-element.64), channel_id=1, source_target_pairs={{0,4},{1,5},{2,6},{3,7},{4,0},{5,1},{6,2},{7,3},{8,12},{9,13},{10,... | collective-permute-start | bytes 589832 | tf_op jit(solution)/shard_map/ppermute | solution.py:810
  61.8 6.8 %collective-permute-start.6 = (bf16[2,192,256]{2,1,0:T(8,128)(2,1)}, bf16[2,192,256]{2,1,0:T(8,128)(2,1)S(1)}, u32[]{:S(2)}, u32[]{:S(2)}) collective-permute-start(bf16[2,192,256]{2,1,0:T(8,128)(2,1)} %get-tuple-element.65), channel_id=1, source_target_pairs={{0,5},{1,6},{2,7},{3,0},{4,1},{5,2},{6,3},{7,4},{8,13},{9,14},{10,... | collective-permute-start | bytes 589832 | tf_op jit(solution)/shard_map/ppermute | solution.py:810
  61.8 8.0 %collective-permute-start.7 = (bf16[2,192,256]{2,1,0:T(8,128)(2,1)}, bf16[2,192,256]{2,1,0:T(8,128)(2,1)S(1)}, u32[]{:S(2)}, u32[]{:S(2)}) collective-permute-start(bf16[2,192,256]{2,1,0:T(8,128)(2,1)} %get-tuple-element.66), channel_id=1, source_target_pairs={{0,6},{1,7},{2,0},{3,1},{4,2},{5,3},{6,4},{7,5},{8,14},{9,15},{10,... | collective-permute-start | bytes 589832 | tf_op jit(solution)/shard_map/ppermute | solution.py:810
  62.3 9.2 %collective-permute-start.8 = (bf16[2,192,256]{2,1,0:T(8,128)(2,1)}, bf16[2,192,256]{2,1,0:T(8,128)(2,1)S(1)}, u32[]{:S(2)}, u32[]{:S(2)}) collective-permute-start(bf16[2,192,256]{2,1,0:T(8,128)(2,1)} %get-tuple-element.67), channel_id=1, source_target_pairs={{0,7},{1,0},{2,1},{3,2},{4,3},{5,4},{6,5},{7,6},{8,15},{9,8},{10,9... | collective-permute-start | bytes 589832 | tf_op jit(solution)/shard_map/ppermute | solution.py:810
  78.8 42.9 %all-to-all-start.3 = ((bf16[4,2,2,192,256]{4,3,2,1,0:T(8,128)(2,1)}), bf16[4,2,2,192,256]{4,3,2,1,0:T(8,128)(2,1)}, u32[]{:S(2)}, u32[]{:S(2)}) async-start(bf16[4,2,2,192,256]{4,3,2,1,0:T(8,128)(2,1)} %bitcast.22), calls=%async_computation.3 | async-start | bytes 3145728 | tf_op jit(solution)/shard_map/all_to_all | solution.py:865
  88.2 11.3 %collective-permute-start.11 = (bf16[2,192,256]{2,1,0:T(8,128)(2,1)}, bf16[2,192,256]{2,1,0:T(8,128)(2,1)S(1)}, u32[]{:S(2)}, u32[]{:S(2)}) collective-permute-start(bf16[2,192,256]{2,1,0:T(8,128)(2,1)} %get-tuple-element.69), channel_id=1, source_target_pairs={{0,1},{1,2},{2,3},{3,4},{4,5},{5,6},{6,7},{7,0},{8,9},{9,10},{10,1... | collective-permute-start | bytes 589832 | tf_op jit(solution)/shard_map/ppermute | solution.py:810
  89.9 10.8 %collective-permute-start.12 = (bf16[2,192,256]{2,1,0:T(8,128)(2,1)}, bf16[2,192,256]{2,1,0:T(8,128)(2,1)S(1)}, u32[]{:S(2)}, u32[]{:S(2)}) collective-permute-start(bf16[2,192,256]{2,1,0:T(8,128)(2,1)} %get-tuple-element.70), channel_id=1, source_target_pairs={{0,2},{1,3},{2,4},{3,5},{4,6},{5,7},{6,0},{7,1},{8,10},{9,11},{10,... | collective-permute-start | bytes 589832 | tf_op jit(solution)/shard_map/ppermute | solution.py:810
  94.1 14.2 %collective-permute-start.13 = (bf16[2,192,256]{2,1,0:T(8,128)(2,1)}, bf16[2,192,256]{2,1,0:T(8,128)(2,1)S(1)}, u32[]{:S(2)}, u32[]{:S(2)}) collective-permute-start(bf16[2,192,256]{2,1,0:T(8,128)(2,1)} %get-tuple-element.71), channel_id=1, source_target_pairs={{0,3},{1,4},{2,5},{3,6},{4,7},{5,0},{6,1},{7,2},{8,11},{9,12},{10,... | collective-permute-start | bytes 589832 | tf_op jit(solution)/shard_map/ppermute | solution.py:810
  94.8 13.7 %collective-permute-start.14 = (bf16[2,192,256]{2,1,0:T(8,128)(2,1)}, bf16[2,192,256]{2,1,0:T(8,128)(2,1)S(1)}, u32[]{:S(2)}, u32[]{:S(2)}) collective-permute-start(bf16[2,192,256]{2,1,0:T(8,128)(2,1)} %get-tuple-element.72), channel_id=1, source_target_pairs={{0,4},{1,5},{2,6},{3,7},{4,0},{5,1},{6,2},{7,3},{8,12},{9,13},{10,... | collective-permute-start | bytes 589832 | tf_op jit(solution)/shard_map/ppermute | solution.py:810
  96.3 14.8 %collective-permute-start.15 = (bf16[2,192,256]{2,1,0:T(8,128)(2,1)}, bf16[2,192,256]{2,1,0:T(8,128)(2,1)S(1)}, u32[]{:S(2)}, u32[]{:S(2)}) collective-permute-start(bf16[2,192,256]{2,1,0:T(8,128)(2,1)} %get-tuple-element.73), channel_id=1, source_target_pairs={{0,5},{1,6},{2,7},{3,0},{4,1},{5,2},{6,3},{7,4},{8,13},{9,14},{10,... | collective-permute-start | bytes 589832 | tf_op jit(solution)/shard_map/ppermute | solution.py:810
  99.5 11.7 %collective-permute-start.16 = (bf16[2,192,256]{2,1,0:T(8,128)(2,1)}, bf16[2,192,256]{2,1,0:T(8,128)(2,1)S(1)}, u32[]{:S(2)}, u32[]{:S(2)}) collective-permute-start(bf16[2,192,256]{2,1,0:T(8,128)(2,1)} %get-tuple-element.74), channel_id=1, source_target_pairs={{0,6},{1,7},{2,0},{3,1},{4,2},{5,3},{6,4},{7,5},{8,14},{9,15},{10,... | collective-permute-start | bytes 589832 | tf_op jit(solution)/shard_map/ppermute | solution.py:810
  100.7 10.4 %collective-permute-start.17 = (bf16[2,192,256]{2,1,0:T(8,128)(2,1)}, bf16[2,192,256]{2,1,0:T(8,128)(2,1)S(1)}, u32[]{:S(2)}, u32[]{:S(2)}) collective-permute-start(bf16[2,192,256]{2,1,0:T(8,128)(2,1)} %get-tuple-element.75), channel_id=1, source_target_pairs={{0,7},{1,0},{2,1},{3,2},{4,3},{5,4},{6,5},{7,6},{8,15},{9,8},{10,9... | collective-permute-start | bytes 589832 | tf_op jit(solution)/shard_map/ppermute | solution.py:810
  121.7 42.4 %all-to-all-start.2 = ((bf16[4,2,2,192,256]{4,3,2,1,0:T(8,128)(2,1)}), bf16[4,2,2,192,256]{4,3,2,1,0:T(8,128)(2,1)}, u32[]{:S(2)}, u32[]{:S(2)}) async-start(bf16[4,2,2,192,256]{4,3,2,1,0:T(8,128)(2,1)} %bitcast.25), calls=%async_computation.2 | async-start | bytes 3145728 | tf_op jit(solution)/shard_map/all_to_all | solution.py:865
  164.0 41.6 %all-to-all-start.4 = ((bf16[4,2,2,192,256]{4,3,2,1,0:T(8,128)(2,1)}), bf16[4,2,2,192,256]{4,3,2,1,0:T(8,128)(2,1)}, u32[]{:S(2)}, u32[]{:S(2)}) async-start(bf16[4,2,2,192,256]{4,3,2,1,0:T(8,128)(2,1)} %copy-done.12), calls=%async_computation.4 | async-start | bytes 3145728 | tf_op jit(solution)/shard_map/all_to_all | solution.py:872
  205.6 40.9 %all-to-all-start.6 = ((bf16[4,2,2,192,256]{4,3,2,1,0:T(8,128)(2,1)}), bf16[4,2,2,192,256]{4,3,2,1,0:T(8,128)(2,1)}, u32[]{:S(2)}, u32[]{:S(2)}) async-start(bf16[4,2,2,192,256]{4,3,2,1,0:T(8,128)(2,1)} %copy-done.14), calls=%async_computation.6 | async-start | bytes 3145728 | tf_op jit(solution)/shard_map/all_to_all | solution.py:872
  210.0 29.5 %copy-start.3 = (f32[2,2,192,1024]{3,2,1,0:T(8,128)S(1)}, f32[2,2,192,1024]{3,2,1,0:T(8,128)}, u32[]{:S(2)}) copy-start(f32[2,2,192,1024]{3,2,1,0:T(8,128)} %copy-done.2) | copy-start | bytes 9437188
  210.0 29.5 %copy-start.5 = (f32[2,2,192,1024]{3,2,1,0:T(8,128)S(1)}, f32[2,2,192,1024]{3,2,1,0:T(8,128)}, u32[]{:S(2)}) copy-start(f32[2,2,192,1024]{3,2,1,0:T(8,128)} %copy-done.4) | copy-start | bytes 9437188
  217.4 7.3 %collective-permute-start.18 = (bf16[2,192,256]{2,1,0:T(8,128)(2,1)}, bf16[2,192,256]{2,1,0:T(8,128)(2,1)S(1)}, u32[]{:S(2)}, u32[]{:S(2)}) collective-permute-start(bf16[2,192,256]{2,1,0:T(8,128)(2,1)} %get-tuple-element.77), channel_id=1, source_target_pairs={{0,1},{1,2},{2,3},{3,4},{4,5},{5,6},{6,7},{7,0},{8,9},{9,10},{10,1... | collective-permute-start | bytes 589832 | tf_op jit(solution)/shard_map/ppermute | solution.py:810
  217.4 11.5 %collective-permute-start.19 = (bf16[2,192,256]{2,1,0:T(8,128)(2,1)}, bf16[2,192,256]{2,1,0:T(8,128)(2,1)S(1)}, u32[]{:S(2)}, u32[]{:S(2)}) collective-permute-start(bf16[2,192,256]{2,1,0:T(8,128)(2,1)} %get-tuple-element.78), channel_id=1, source_target_pairs={{0,2},{1,3},{2,4},{3,5},{4,6},{5,7},{6,0},{7,1},{8,10},{9,11},{10,... | collective-permute-start | bytes 589832 | tf_op jit(solution)/shard_map/ppermute | solution.py:810
  221.8 12.9 %collective-permute-start.20 = (bf16[2,192,256]{2,1,0:T(8,128)(2,1)}, bf16[2,192,256]{2,1,0:T(8,128)(2,1)S(1)}, u32[]{:S(2)}, u32[]{:S(2)}) collective-permute-start(bf16[2,192,256]{2,1,0:T(8,128)(2,1)} %get-tuple-element.79), channel_id=1, source_target_pairs={{0,3},{1,4},{2,5},{3,6},{4,7},{5,0},{6,1},{7,2},{8,11},{9,12},{10,... | collective-permute-start | bytes 589832 | tf_op jit(solution)/shard_map/ppermute | solution.py:810
  223.6 11.4 %collective-permute-start.21 = (bf16[2,192,256]{2,1,0:T(8,128)(2,1)}, bf16[2,192,256]{2,1,0:T(8,128)(2,1)S(1)}, u32[]{:S(2)}, u32[]{:S(2)}) collective-permute-start(bf16[2,192,256]{2,1,0:T(8,128)(2,1)} %get-tuple-element.80), channel_id=1, source_target_pairs={{0,4},{1,5},{2,6},{3,7},{4,0},{5,1},{6,2},{7,3},{8,12},{9,13},{10,... | collective-permute-start | bytes 589832 | tf_op jit(solution)/shard_map/ppermute | solution.py:810
  224.7 13.1 %collective-permute-start.22 = (bf16[2,192,256]{2,1,0:T(8,128)(2,1)}, bf16[2,192,256]{2,1,0:T(8,128)(2,1)S(1)}, u32[]{:S(2)}, u32[]{:S(2)}) collective-permute-start(bf16[2,192,256]{2,1,0:T(8,128)(2,1)} %get-tuple-element.81), channel_id=1, source_target_pairs={{0,5},{1,6},{2,7},{3,0},{4,1},{5,2},{6,3},{7,4},{8,13},{9,14},{10,... | collective-permute-start | bytes 589832 | tf_op jit(solution)/shard_map/ppermute | solution.py:810
  224.7 21.2 %copy-start.22 = (bf16[2,192,256]{2,1,0:T(8,128)(2,1)}, bf16[2,192,256]{2,1,0:T(8,128)(2,1)S(1)}, u32[]{:S(2)}) copy-start(bf16[2,192,256]{2,1,0:T(8,128)(2,1)S(1)} %collective-permute-done.18.refs_5_.refs_1_) | copy-start | bytes 589828
  224.7 13.1 %collective-permute-start.23 = (bf16[2,192,256]{2,1,0:T(8,128)(2,1)}, bf16[2,192,256]{2,1,0:T(8,128)(2,1)S(1)}, u32[]{:S(2)}, u32[]{:S(2)}) collective-permute-start(bf16[2,192,256]{2,1,0:T(8,128)(2,1)} %get-tuple-element.82), channel_id=1, source_target_pairs={{0,6},{1,7},{2,0},{3,1},{4,2},{5,3},{6,4},{7,5},{8,14},{9,15},{10,... | collective-permute-start | bytes 589832 | tf_op jit(solution)/shard_map/ppermute | solution.py:810
  229.0 10.5 %collective-permute-start.24 = (bf16[2,192,256]{2,1,0:T(8,128)(2,1)}, bf16[2,192,256]{2,1,0:T(8,128)(2,1)S(1)}, u32[]{:S(2)}, u32[]{:S(2)}) collective-permute-start(bf16[2,192,256]{2,1,0:T(8,128)(2,1)} %get-tuple-element.83), channel_id=1, source_target_pairs={{0,7},{1,0},{2,1},{3,2},{4,3},{5,4},{6,5},{7,6},{8,15},{9,8},{10,9... | collective-permute-start | bytes 589832 | tf_op jit(solution)/shard_map/ppermute | solution.py:810
  246.5 41.2 %all-to-all-start.5 = ((bf16[4,2,2,192,256]{4,3,2,1,0:T(8,128)(2,1)}), bf16[4,2,2,192,256]{4,3,2,1,0:T(8,128)(2,1)S(1)}, u32[]{:S(2)}, u32[]{:S(2)}) async-start(bf16[4,2,2,192,256]{4,3,2,1,0:T(8,128)(2,1)} %curl_inverse.5), calls=%async_computation.5 | async-start | bytes 3145728 | tf_op jit(solution)/shard_map/all_to_all | solution.py:872
  264.5 8.7 %collective-permute-start.25 = (bf16[2,192,256]{2,1,0:T(8,128)(2,1)}, bf16[2,192,256]{2,1,0:T(8,128)(2,1)S(1)}, u32[]{:S(2)}, u32[]{:S(2)}) collective-permute-start(bf16[2,192,256]{2,1,0:T(8,128)(2,1)} %get-tuple-element.86), channel_id=1, source_target_pairs={{0,1},{1,2},{2,3},{3,4},{4,5},{5,6},{6,7},{7,0},{8,9},{9,10},{10,1... | collective-permute-start | bytes 589832 | tf_op jit(solution)/shard_map/ppermute | solution.py:810
  264.6 10.6 %collective-permute-start.26 = (bf16[2,192,256]{2,1,0:T(8,128)(2,1)}, bf16[2,192,256]{2,1,0:T(8,128)(2,1)S(1)}, u32[]{:S(2)}, u32[]{:S(2)}) collective-permute-start(bf16[2,192,256]{2,1,0:T(8,128)(2,1)} %get-tuple-element.87), channel_id=1, source_target_pairs={{0,2},{1,3},{2,4},{3,5},{4,6},{5,7},{6,0},{7,1},{8,10},{9,11},{10,... | collective-permute-start | bytes 589832 | tf_op jit(solution)/shard_map/ppermute | solution.py:810
  268.1 14.0 %collective-permute-start.27 = (bf16[2,192,256]{2,1,0:T(8,128)(2,1)}, bf16[2,192,256]{2,1,0:T(8,128)(2,1)S(1)}, u32[]{:S(2)}, u32[]{:S(2)}) collective-permute-start(bf16[2,192,256]{2,1,0:T(8,128)(2,1)} %get-tuple-element.88), channel_id=1, source_target_pairs={{0,3},{1,4},{2,5},{3,6},{4,7},{5,0},{6,1},{7,2},{8,11},{9,12},{10,... | collective-permute-start | bytes 589832 | tf_op jit(solution)/shard_map/ppermute | solution.py:810
  269.8 12.5 %collective-permute-start.28 = (bf16[2,192,256]{2,1,0:T(8,128)(2,1)}, bf16[2,192,256]{2,1,0:T(8,128)(2,1)S(1)}, u32[]{:S(2)}, u32[]{:S(2)}) collective-permute-start(bf16[2,192,256]{2,1,0:T(8,128)(2,1)} %get-tuple-element.89), channel_id=1, source_target_pairs={{0,4},{1,5},{2,6},{3,7},{4,0},{5,1},{6,2},{7,3},{8,12},{9,13},{10,... | collective-permute-start | bytes 589832 | tf_op jit(solution)/shard_map/ppermute | solution.py:810
  270.9 14.2 %collective-permute-start.29 = (bf16[2,192,256]{2,1,0:T(8,128)(2,1)}, bf16[2,192,256]{2,1,0:T(8,128)(2,1)S(1)}, u32[]{:S(2)}, u32[]{:S(2)}) collective-permute-start(bf16[2,192,256]{2,1,0:T(8,128)(2,1)} %get-tuple-element.90), channel_id=1, source_target_pairs={{0,5},{1,6},{2,7},{3,0},{4,1},{5,2},{6,3},{7,4},{8,13},{9,14},{10,... | collective-permute-start | bytes 589832 | tf_op jit(solution)/shard_map/ppermute | solution.py:810
  273.2 21.7 %copy-start.20 = (bf16[2,192,256]{2,1,0:T(8,128)(2,1)}, bf16[2,192,256]{2,1,0:T(8,128)(2,1)S(1)}, u32[]{:S(2)}) copy-start(bf16[2,192,256]{2,1,0:T(8,128)(2,1)S(1)} %collective-permute-done.25.refs_1_) | copy-start | bytes 589828
  273.2 11.9 %collective-permute-start.30 = (bf16[2,192,256]{2,1,0:T(8,128)(2,1)}, bf16[2,192,256]{2,1,0:T(8,128)(2,1)S(1)}, u32[]{:S(2)}, u32[]{:S(2)}) collective-permute-start(bf16[2,192,256]{2,1,0:T(8,128)(2,1)} %get-tuple-element.91), channel_id=1, source_target_pairs={{0,6},{1,7},{2,0},{3,1},{4,2},{5,3},{6,4},{7,5},{8,14},{9,15},{10,... | collective-permute-start | bytes 589832 | tf_op jit(solution)/shard_map/ppermute | solution.py:810
  275.1 10.6 %collective-permute-start.31 = (bf16[2,192,256]{2,1,0:T(8,128)(2,1)}, bf16[2,192,256]{2,1,0:T(8,128)(2,1)S(1)}, u32[]{:S(2)}, u32[]{:S(2)}) collective-permute-start(bf16[2,192,256]{2,1,0:T(8,128)(2,1)} %get-tuple-element.92), channel_id=1, source_target_pairs={{0,7},{1,0},{2,1},{3,2},{4,3},{5,4},{6,5},{7,6},{8,15},{9,8},{10,9... | collective-permute-start | bytes 589832 | tf_op jit(solution)/shard_map/ppermute | solution.py:810
  295.0 26.9 %all-to-all-start.7 = ((bf16[8,2,192,256]{3,2,1,0:T(8,128)(2,1)}), bf16[8,2,192,256]{3,2,1,0:T(8,128)(2,1)S(1)}, u32[]{:S(2)}, u32[]{:S(2)}) async-start(bf16[8,2,192,256]{3,2,1,0:T(8,128)(2,1)} %y_inverse.1.refs_13_), calls=%async_computation.7 | async-start | bytes 3145728 | tf_op jit(solution)/shard_map/all_to_all | solution.py:884
  329.0 15.0 %collective-permute-start.34 = (bf16[3,16,256]{2,1,0:T(8,128)(2,1)}, bf16[3,16,256]{2,1,0:T(8,128)(2,1)S(1)}, u32[]{:S(2)}, u32[]{:S(2)}) collective-permute-start(bf16[3,16,256]{2,1,0:T(8,128)(2,1)} %get-tuple-element.108), channel_id=1, source_target_pairs={{0,1},{1,2},{2,3},{3,4},{4,5},{5,6},{6,7},{7,0},{8,9},{9,10},{10,1... | collective-permute-start | bytes 73736 | tf_op jit(solution)/shard_map/ppermute | solution.py:524
  329.1 14.9 %collective-permute-start.35 = (bf16[3,16,256]{2,1,0:T(8,128)(2,1)}, bf16[3,16,256]{2,1,0:T(8,128)(2,1)S(1)}, u32[]{:S(2)}, u32[]{:S(2)}) collective-permute-start(bf16[3,16,256]{2,1,0:T(8,128)(2,1)} %get-tuple-element.109), channel_id=1, source_target_pairs={{1,0},{2,1},{3,2},{4,3},{5,4},{6,5},{7,6},{0,7},{9,8},{10,9},{11,1... | collective-permute-start | bytes 73736 | tf_op jit(solution)/shard_map/ppermute | solution.py:524
  331.7 12.2 %collective-permute-start.32 = (bf16[3,16,192]{2,1,0:T(8,128)(2,1)}, bf16[3,16,192]{2,1,0:T(8,128)(2,1)S(1)}, u32[]{:S(2)}, u32[]{:S(2)}) collective-permute-start(bf16[3,16,192]{2,1,0:T(8,128)(2,1)} %get-tuple-element.106), channel_id=1, source_target_pairs={{0,8},{8,16},{16,24},{24,0},{1,9},{9,17},{17,25},{25,1},{2,10},{10... | collective-permute-start | bytes 55304 | tf_op jit(solution)/shard_map/ppermute | solution.py:524
  331.7 12.2 %collective-permute-start.33 = (bf16[3,16,192]{2,1,0:T(8,128)(2,1)}, bf16[3,16,192]{2,1,0:T(8,128)(2,1)S(1)}, u32[]{:S(2)}, u32[]{:S(2)}) collective-permute-start(bf16[3,16,192]{2,1,0:T(8,128)(2,1)} %get-tuple-element.107), channel_id=1, source_target_pairs={{8,0},{16,8},{24,16},{0,24},{9,1},{17,9},{25,17},{1,25},{10,2},{18... | collective-permute-start | bytes 55304 | tf_op jit(solution)/shard_map/ppermute | solution.py:524
  (53 other events, 298.6 us)

commit v13 on v12

--- a/solution.py
+++ b/solution.py
@@ -119,7 +119,7 @@
     return layers
 
 
-ROWS = 48
+ROWS = 96
 
 
 def tiles(height, width):

time: 358 us -> 354 us (0.989)
  Pallas kernels: 125 us -> 119 us
  transfers between devices with their start and end apart: 44 -> 44, of which waited for: 28 -> 29; matrix products, arithmetic and copies ran while one was open for 1% -> 1% of each run, Pallas kernels for 27% -> 26%
where the time goes in v13:
time: 354 us; the launch traced here: 353 us
  Pallas kernels  119 us (34%)
  waiting for transfers between devices  115 us (32%)
  starting transfers between devices  94.3 us (27%)
  local copies, waits for them, and re-layouts  22 us (6%)
    ppermute x28, starting transfers between devices, shifted(): lax.ppermute(parts[s], axis, [(i, (i + s) % count) for i in range(count)])  42.8 us
    ppermute x28, waiting for transfers between devices, shifted(): lax.ppermute(parts[s], axis, [(i, (i + s) % count) for i in range(count)])  34.3 us
    all_to_all x3, waiting for transfers between devices, spectrum(): lines = lax.all_to_all(sent[place], 'gx', 0, 0, tiled=True)  30.3 us
    all_to_all x3, waiting for transfers between devices, back(): parts = lax.all_to_all(filtered, 'gx', 0, 0, tiled=True)  28.8 us
    pallas_call x3, Pallas kernels, add_grad_vort(): pl.pallas_call(kernel, grid=(Z // LAYERS,), in_specs=in_specs + tied(afte...  20.7 us
    unnamed x118, local copies, waits for them, and re-layouts  20 us
    pallas_call x3, Pallas kernels, make_adjoint(): pl.pallas_call(kernel, grid=(height // ROWS,), in_specs=[pl.BlockSpec(mem...  15.8 us
    ppermute x8, waiting for transfers between devices, exchange(): return (lax.ppermute(last, axis, up), lax.ppermute(first, axis, down))  15.1 us
  transfers between devices with their start and end apart: 44, of which 29 were waited for; matrix products, arithmetic and copies ran while one was open for 1% of the time, Pallas kernels for 26%

profile of v13, /device:TPU:0, one launch (start us, length us, event | category | flops | bytes accessed | tf_op | source)
XLA Modules:
  0.0 353.1 jit_solution(3635372650073340469)
XLA Ops:
  0.6 3.2 depth_transform.3.refs_0_
  3.8 5.2 %all-to-all-start = ((bf16[8,2,192,256]{3,2,1,0:T(8,128)(2,1)}), bf16[8,2,192,256]{3,2,1,0:T(8,128)(2,1)S(1)}, u32[]{:S(2)}, u32[]{:S(2)}) async-start(bf16[8,2,192,256]{3,2,1,0:T(8,128)(2,1)} %bitcast.28), calls=%async_computation | async-start | bytes 3145728 | tf_op jit(solution)/shard_map/all_to_all | solution.py:851
  11.6 4.6 %edge_columns.2 = (bf16[3,16,192]{2,1,0:T(8,128)(2,1)}, bf16[3,16,192]{2,1,0:T(8,128)(2,1)}) custom-call(bf16[3,16,192,256]{3,2,1,0:T(8,128)(2,1)} %refs_4_.6, bf16[16,192,256]{2,1,0:T(8,128)(2,1)} %depth_transform.3.refs_0_), custom_call_target="tpu_custom_call" | custom-call | flops 1 | bytes 12000000 | tf_op jit(solution)/shard_map/edge_columns/pallas_call | solution.py:508
  16.9 3.7 %collective-permute-start.1 = (bf16[4,16,192]{2,1,0:T(8,128)(2,1)S(1)}, bf16[4,16,192]{2,1,0:T(8,128)(2,1)S(1)}, u32[]{:S(2)}, u32[]{:S(2)}) collective-permute-start(bf16[4,16,192]{2,1,0:T(8,128)(2,1)S(1)} %pad_maximum_fusion.1), channel_id=1, source_target_pairs={{8,0},{16,8},{24,16},{0,24},{9,1},{17,9},{25,17},{1,25},{10,2},{18... | collective-permute-start | bytes 73736 | tf_op jit(solution)/shard_map/ppermute | solution.py:524
  22.2 4.9 %collective-permute-done.refs_0_.refs_6_.refs_14_ = bf16[4,16,192]{2,1,0:T(8,128)(2,1)S(1)} collective-permute-done((bf16[4,16,192]{2,1,0:T(8,128)(2,1)S(1)}, bf16[4,16,192]{2,1,0:T(8,128)(2,1)S(1)}, u32[]{:S(2)}, u32[]{:S(2)}) %collective-permute-start) | collective-permute-done | bytes 24608 | tf_op jit(solution)/shard_map/ppermute | solution.py:524
  32.3 3.9 %y_transform.1 = bf16[4,1,2,2,192,256]{5,4,3,2,1,0:T(8,128)(2,1)} custom-call(bf16[1536,1536]{1,0:T(8,128)(2,1)S(1)} %copy-done.1, bf16[8,2,192,256]{3,2,1,0:T(8,128)(2,1)S(1)} %all-to-all-done.columns_ref, bf16[4,16,192]{2,1,0:T(8,128)(2,1)S(1)} %collective-permute-done.refs_0_.refs_6_.refs_14_, ...), custom_call_target="tpu_custom_call" | custom-call | flops 1 | bytes 12000000 | tf_op jit(solution)/shard_map/y_transform/pallas_call | solution.py:198
  36.2 4.9 %all-to-all-start.1 = ((bf16[4,2,2,192,256]{4,3,2,1,0:T(8,128)(2,1)}), bf16[4,2,2,192,256]{4,3,2,1,0:T(8,128)(2,1)S(1)}, u32[]{:S(2)}, u32[]{:S(2)}) async-start(bf16[4,2,2,192,256]{4,3,2,1,0:T(8,128)(2,1)} %bitcast.3.refs_2_), calls=%async_computation.1 | async-start | bytes 3145728 | tf_op jit(solution)/shard_map/all_to_all | solution.py:865
  43.1 3.3 depth_transform.4
  49.7 9.4 %collective-permute-done.9.refs_8_.refs_16_ = bf16[4,16,256]{2,1,0:T(8,128)(2,1)S(1)} collective-permute-done((bf16[4,16,256]{2,1,0:T(8,128)(2,1)S(1)}, bf16[4,16,256]{2,1,0:T(8,128)(2,1)S(1)}, u32[]{:S(2)}, u32[]{:S(2)}) %collective-permute-start.9) | collective-permute-done | bytes 32800 | tf_op jit(solution)/shard_map/ppermute | solution.py:524
  62.5 3.2 collective-permute-done.5.refs_4_
  70.1 6.6 %y_transform_parts.2 = bf16[4,1,2,2,192,256]{5,4,3,2,1,0:T(8,128)(2,1)} custom-call(s32[1]{0:T(128)} %bitcast.refs_0_.me_ref, bf16[1536,1536]{1,0:T(8,128)(2,1)} %constant.37.clone.table_ref, bf16[2,192,256]{2,1,0:T(8,128)(2,1)} %get-tuple-element.60.refs_0_, bf16[2,192,256]{2,1,0:T(8,128)(2,1)} %copy-done.37, bf16[2,192,256]{2,1,0:T(8,128)(2,1)} %copy-done.38, ...), custom_call_target="tpu_custom_call" | custom-call | flops 1 | bytes 15000000 | tf_op jit(solution)/shard_map/y_transform_parts/pallas_call | solution.py:252
  76.7 5.1 %all-to-all-start.3 = ((bf16[4,2,2,192,256]{4,3,2,1,0:T(8,128)(2,1)}), bf16[4,2,2,192,256]{4,3,2,1,0:T(8,128)(2,1)}, u32[]{:S(2)}, u32[]{:S(2)}) async-start(bf16[4,2,2,192,256]{4,3,2,1,0:T(8,128)(2,1)} %bitcast.22), calls=%async_computation.3 | async-start | bytes 3145728 | tf_op jit(solution)/shard_map/all_to_all | solution.py:865
  81.8 3.3 depth_transform.5
  86.9 4.2 %collective-permute-start.12 = (bf16[2,192,256]{2,1,0:T(8,128)(2,1)}, bf16[2,192,256]{2,1,0:T(8,128)(2,1)S(1)}, u32[]{:S(2)}, u32[]{:S(2)}) collective-permute-start(bf16[2,192,256]{2,1,0:T(8,128)(2,1)} %get-tuple-element.70), channel_id=1, source_target_pairs={{0,2},{1,3},{2,4},{3,5},{4,6},{5,7},{6,0},{7,1},{8,10},{9,11},{10,... | collective-permute-start | bytes 589832 | tf_op jit(solution)/shard_map/ppermute | solution.py:810
  100.1 5.3 %collective-permute-done.13.refs_3_ = bf16[2,192,256]{2,1,0:T(8,128)(2,1)S(1)} collective-permute-done((bf16[2,192,256]{2,1,0:T(8,128)(2,1)}, bf16[2,192,256]{2,1,0:T(8,128)(2,1)S(1)}, u32[]{:S(2)}, u32[]{:S(2)}) %collective-permute-start.13) | collective-permute-done | bytes 196640 | tf_op jit(solution)/shard_map/ppermute | solution.py:810
  108.9 6.6 %y_transform_parts.3 = bf16[4,1,2,2,192,256]{5,4,3,2,1,0:T(8,128)(2,1)} custom-call(s32[1]{0:T(128)} %bitcast.refs_0_.me_ref, bf16[1536,1536]{1,0:T(8,128)(2,1)} %constant.37.clone.table_ref, bf16[2,192,256]{2,1,0:T(8,128)(2,1)} %get-tuple-element.68.refs_0_, bf16[2,192,256]{2,1,0:T(8,128)(2,1)} %copy-done.40, bf16[2,192,256]{2,1,0:T(8,128)(2,1)} %copy-done.41, ...), custom_call_target="tpu_custom_call" | custom-call | flops 1 | bytes 15000000 | tf_op jit(solution)/shard_map/y_transform_parts/pallas_call | solution.py:252
  115.5 4.1 %all-to-all-done.3.modes_ref = bf16[4,2,2,192,256]{4,3,2,1,0:T(8,128)(2,1)} async-done(((bf16[4,2,2,192,256]{4,3,2,1,0:T(8,128)(2,1)}), bf16[4,2,2,192,256]{4,3,2,1,0:T(8,128)(2,1)}, u32[]{:S(2)}, u32[]{:S(2)}) %all-to-all-start.3) | async-done | bytes 1572896 | tf_op jit(solution)/shard_map/all_to_all | solution.py:865
  119.6 4.4 %all-to-all-start.2 = ((bf16[4,2,2,192,256]{4,3,2,1,0:T(8,128)(2,1)}), bf16[4,2,2,192,256]{4,3,2,1,0:T(8,128)(2,1)}, u32[]{:S(2)}, u32[]{:S(2)}) async-start(bf16[4,2,2,192,256]{4,3,2,1,0:T(8,128)(2,1)} %bitcast.25), calls=%async_computation.2 | async-start | bytes 3145728 | tf_op jit(solution)/shard_map/all_to_all | solution.py:865
  127.8 3.9 %x_transform.4.refs_2_.refs_3_ = f32[2,2,192,1024]{3,2,1,0:T(8,128)S(1)} custom-call(bf16[1024,1024]{1,0:T(8,128)(2,1)S(1)} %copy-done.10, bf16[4,2,2,192,256]{4,3,2,1,0:T(8,128)(2,1)} %all-to-all-done.3.modes_ref, bf16[4,2,2,192,256]{4,3,2,1,0:T(8,128)(2,1)S(1)} %bitcast.26), custom_call_target="tpu_custom_call" | custom-call | flops 1 | bytes 9000000 | tf_op jit(solution)/shard_map/x_transform/pallas_call | solution.py:370
  131.7 3.0 curl_inverse.3.refs_0_
  135.8 26.2 %all-to-all-done.2.modes_ref = bf16[4,2,2,192,256]{4,3,2,1,0:T(8,128)(2,1)} async-done(((bf16[4,2,2,192,256]{4,3,2,1,0:T(8,128)(2,1)}), bf16[4,2,2,192,256]{4,3,2,1,0:T(8,128)(2,1)}, u32[]{:S(2)}, u32[]{:S(2)}) %all-to-all-start.2) | async-done | bytes 1572896 | tf_op jit(solution)/shard_map/all_to_all | solution.py:865
  162.0 4.5 %all-to-all-start.4 = ((bf16[4,2,2,192,256]{4,3,2,1,0:T(8,128)(2,1)}), bf16[4,2,2,192,256]{4,3,2,1,0:T(8,128)(2,1)}, u32[]{:S(2)}, u32[]{:S(2)}) async-start(bf16[4,2,2,192,256]{4,3,2,1,0:T(8,128)(2,1)} %copy-done.12), calls=%async_computation.4 | async-start | bytes 3145728 | tf_op jit(solution)/shard_map/all_to_all | solution.py:872
  169.5 3.3 x_transform.5.refs_2_.refs_3_
  172.8 3.0 curl_inverse.4.refs_0_
  178.7 24.9 %all-to-all-done.4 = bf16[4,2,2,192,256]{4,3,2,1,0:T(8,128)(2,1)} async-done(((bf16[4,2,2,192,256]{4,3,2,1,0:T(8,128)(2,1)}), bf16[4,2,2,192,256]{4,3,2,1,0:T(8,128)(2,1)}, u32[]{:S(2)}, u32[]{:S(2)}) %all-to-all-start.4) | async-done | bytes 1572896 | tf_op jit(solution)/shard_map/all_to_all | solution.py:872
  203.6 4.4 %all-to-all-start.6 = ((bf16[4,2,2,192,256]{4,3,2,1,0:T(8,128)(2,1)}), bf16[4,2,2,192,256]{4,3,2,1,0:T(8,128)(2,1)}, u32[]{:S(2)}, u32[]{:S(2)}) async-start(bf16[4,2,2,192,256]{4,3,2,1,0:T(8,128)(2,1)} %copy-done.14), calls=%async_computation.6 | async-start | bytes 3145728 | tf_op jit(solution)/shard_map/all_to_all | solution.py:872
  208.0 7.4 %y_inverse_parts.2 = (bf16[2,192,256]{2,1,0:T(8,128)(2,1)}, bf16[2,192,256]{2,1,0:T(8,128)(2,1)}, bf16[2,192,256]{2,1,0:T(8,128)(2,1)}, bf16[2,192,256]{2,1,0:T(...) custom-call(s32[1]{0:T(128)} %bitcast.refs_0_.me_ref, ...), custom_call_target="tpu_custom_call" | custom-call | flops 1 | bytes 12000000 | tf_op jit(solution)/shard_map/y_inverse_parts/pallas_call | solution.py:340
  215.4 4.4 %collective-permute-start.19 = (bf16[2,192,256]{2,1,0:T(8,128)(2,1)}, bf16[2,192,256]{2,1,0:T(8,128)(2,1)S(1)}, u32[]{:S(2)}, u32[]{:S(2)}) collective-permute-start(bf16[2,192,256]{2,1,0:T(8,128)(2,1)} %get-tuple-element.78), channel_id=1, source_target_pairs={{0,2},{1,3},{2,4},{3,5},{4,6},{5,7},{6,0},{7,1},{8,10},{9,11},{10,... | collective-permute-start | bytes 589832 | tf_op jit(solution)/shard_map/ppermute | solution.py:810
  222.9 4.3 %collective-permute-start.23 = (bf16[2,192,256]{2,1,0:T(8,128)(2,1)}, bf16[2,192,256]{2,1,0:T(8,128)(2,1)S(1)}, u32[]{:S(2)}, u32[]{:S(2)}) collective-permute-start(bf16[2,192,256]{2,1,0:T(8,128)(2,1)} %get-tuple-element.82), channel_id=1, source_target_pairs={{0,6},{1,7},{2,0},{3,1},{4,2},{5,3},{6,4},{7,5},{8,14},{9,15},{10,... | collective-permute-start | bytes 589832 | tf_op jit(solution)/shard_map/ppermute | solution.py:810
  227.2 4.0 %collective-permute-start.24 = (bf16[2,192,256]{2,1,0:T(8,128)(2,1)}, bf16[2,192,256]{2,1,0:T(8,128)(2,1)S(1)}, u32[]{:S(2)}, u32[]{:S(2)}) collective-permute-start(bf16[2,192,256]{2,1,0:T(8,128)(2,1)} %get-tuple-element.83), channel_id=1, source_target_pairs={{0,7},{1,0},{2,1},{3,2},{4,3},{5,4},{6,5},{7,6},{8,15},{9,8},{10,9... | collective-permute-start | bytes 589832 | tf_op jit(solution)/shard_map/ppermute | solution.py:810
  240.0 3.8 %curl_inverse.5 = bf16[4,2,2,192,256]{4,3,2,1,0:T(8,128)(2,1)} custom-call(s32[2]{0:T(128)S(1)} %pad_add_fusion.refs_0_, bf16[1024,1024]{1,0:T(8,128)(2,1)S(1)} %copy-done.9, f32[2,2,192,1024]{3,2,1,0:T(8,128)S(1)} %copy-done.3, f32[2,2,192,1024]{3,2,1,0:T(8,128)S(1)} %copy-done.5, bf16[2,192,256]{2,1,0:T(8,128)(2,1)S(1)} %copy-done.19, ...), custom_call_target="tpu_custom_call" | custom-call | flops 1 | bytes 12000000 | tf_op jit(solution)/shard_map/curl_inverse/pallas_call | solution.py:446
  244.5 4.4 %all-to-all-start.5 = ((bf16[4,2,2,192,256]{4,3,2,1,0:T(8,128)(2,1)}), bf16[4,2,2,192,256]{4,3,2,1,0:T(8,128)(2,1)S(1)}, u32[]{:S(2)}, u32[]{:S(2)}) async-start(bf16[4,2,2,192,256]{4,3,2,1,0:T(8,128)(2,1)} %curl_inverse.5), calls=%async_computation.5 | async-start | bytes 3145728 | tf_op jit(solution)/shard_map/all_to_all | solution.py:872
  248.9 5.3 %make_adjoint.3 = (f32[16,192,256]{2,1,0:T(8,128)}, bf16[16,192,256]{2,1,0:T(8,128)(2,1)}, bf16[3,16,192]{2,1,0:T(8,128)(2,1)}, bf16[3,16,192]{2,1,0:T(8,128)(2,...) custom-call(s32[1]{0:T(128)} %bitcast.refs_0_.me_ref, ...), custom_call_target="tpu_custom_call" | custom-call | flops 1 | bytes 15000000 | tf_op jit(solution)/shard_map/make_adjoint/pallas_call | solution.py:575
  254.2 7.2 %y_inverse_parts.3 = (bf16[2,192,256]{2,1,0:T(8,128)(2,1)}, bf16[2,192,256]{2,1,0:T(8,128)(2,1)}, bf16[2,192,256]{2,1,0:T(8,128)(2,1)}, bf16[2,192,256]{2,1,0:T(...) custom-call(s32[1]{0:T(128)} %bitcast.refs_0_.me_ref, ...), custom_call_target="tpu_custom_call" | custom-call | flops 1 | bytes 12000000 | tf_op jit(solution)/shard_map/y_inverse_parts/pallas_call | solution.py:340
  261.5 3.6 %collective-permute-start.26 = (bf16[2,192,256]{2,1,0:T(8,128)(2,1)}, bf16[2,192,256]{2,1,0:T(8,128)(2,1)S(1)}, u32[]{:S(2)}, u32[]{:S(2)}) collective-permute-start(bf16[2,192,256]{2,1,0:T(8,128)(2,1)} %get-tuple-element.87), channel_id=1, source_target_pairs={{0,2},{1,3},{2,4},{3,5},{4,6},{5,7},{6,0},{7,1},{8,10},{9,11},{10,... | collective-permute-start | bytes 589832 | tf_op jit(solution)/shard_map/ppermute | solution.py:810
  272.4 3.9 %collective-permute-start.31 = (bf16[2,192,256]{2,1,0:T(8,128)(2,1)}, bf16[2,192,256]{2,1,0:T(8,128)(2,1)S(1)}, u32[]{:S(2)}, u32[]{:S(2)}) collective-permute-start(bf16[2,192,256]{2,1,0:T(8,128)(2,1)} %get-tuple-element.92), channel_id=1, source_target_pairs={{0,7},{1,0},{2,1},{3,2},{4,3},{5,4},{6,5},{7,6},{8,15},{9,8},{10,9... | collective-permute-start | bytes 589832 | tf_op jit(solution)/shard_map/ppermute | solution.py:810
  276.3 3.0 collective-permute-done.27.refs_3_
  282.7 3.3 all-to-all-done.5
  289.2 3.9 %y_inverse.1.refs_13_ = bf16[8,2,192,256]{3,2,1,0:T(8,128)(2,1)} custom-call(bf16[1536,1536]{1,0:T(8,128)(2,1)S(1)} %copy-done, bf16[4,1,2,2,192,256]{5,4,3,2,1,0:T(8,128)(2,1)S(1)} %bitcast.27, bf16[2,192,256]{2,1,0:T(8,128)(2,1)S(1)} %copy-done.16, bf16[2,192,256]{2,1,0:T(8,128)(2,1)S(1)} %collective-permute-done.25.refs_1_, ...), custom_call_target="tpu_custom_call" | custom-call | flops 1 | bytes 12000000 | tf_op jit(solution)/shard_map/y_inverse/pallas_call | solution.py:285
  293.2 5.8 %all-to-all-start.7 = ((bf16[8,2,192,256]{3,2,1,0:T(8,128)(2,1)}), bf16[8,2,192,256]{3,2,1,0:T(8,128)(2,1)S(1)}, u32[]{:S(2)}, u32[]{:S(2)}) async-start(bf16[8,2,192,256]{3,2,1,0:T(8,128)(2,1)} %y_inverse.1.refs_13_), calls=%async_computation.7 | async-start | bytes 3145728 | tf_op jit(solution)/shard_map/all_to_all | solution.py:884
  299.0 5.2 %add_grad_vort.3.refs_10_ = bf16[3,16,192,256]{3,2,1,0:T(8,128)(2,1)} custom-call(bf16[256,256]{1,0:T(8,128)(2,1)} %constant.41.clone.refs_0_, bf16[192,192]{1,0:T(8,128)(2,1)} %constant.42.clone.refs_1_, bf16[3,16,192,256]{3,2,1,0:T(8,128)(2,1)} %refs_4_.6, bf16[3,16,192,256]{3,2,1,0:T(8,128)(2,1)} %refs_4_.6, bf16[3,16,192,256]{3,2,1,0:T(8,128)(2,1)} %refs_4_.6, ...), custom_call_target="tpu_custom_call" | custom-call | flops 1 | bytes 27000000 | tf_op jit(solution)/shard_map/add_grad_vort/pallas_call | solution.py:698
  304.2 5.3 %make_adjoint.4 = (f32[16,192,256]{2,1,0:T(8,128)}, bf16[16,192,256]{2,1,0:T(8,128)(2,1)}, bf16[3,16,192]{2,1,0:T(8,128)(2,1)}, bf16[3,16,192]{2,1,0:T(8,128)(2,...) custom-call(s32[1]{0:T(128)} %bitcast.refs_0_.me_ref, ...), custom_call_target="tpu_custom_call", output_to_operand_aliasing={{2}: (10, {}), {3}: (11, {}), {4}: (12, {}), {5}: (13, {})} | custom-call | flops 1 | bytes 15000000 | tf_op jit(solution)/shard_map/make_adjoint/pallas_call | solution.py:575
  309.4 7.1 %add_grad_vort.4.refs_6_.refs_10_ = bf16[3,16,192,256]{3,2,1,0:T(8,128)(2,1)} custom-call(bf16[256,256]{1,0:T(8,128)(2,1)} %constant.41.clone.refs_0_, bf16[192,192]{1,0:T(8,128)(2,1)} %constant.42.clone.refs_1_, bf16[3,16,192,256]{3,2,1,0:T(8,128)(2,1)} %refs_4_.6, bf16[3,16,192,256]{3,2,1,0:T(8,128)(2,1)} %refs_4_.6, bf16[3,16,192,256]{3,2,1,0:T(8,128)(2,1)} %refs_4_.6, ...), custom_call_target="tpu_custom_call" | custom-call | flops 1 | bytes 27000000 | tf_op jit(solution)/shard_map/add_grad_vort/pallas_call | solution.py:698
  316.6 3.5 all-to-all-done.7
  321.2 5.2 %make_adjoint.5 = (f32[16,192,256]{2,1,0:T(8,128)}, bf16[16,192,256]{2,1,0:T(8,128)(2,1)}, bf16[3,16,192]{2,1,0:T(8,128)(2,1)}, bf16[3,16,192]{2,1,0:T(8,128)(2,...) custom-call(s32[1]{0:T(128)} %bitcast.refs_0_.me_ref, ...), custom_call_target="tpu_custom_call", output_to_operand_aliasing={{2}: (3, {}), {3}: (4, {}), {4}: (5, {}), {5}: (6, {})} | custom-call | flops 1 | bytes 15000000 | tf_op jit(solution)/shard_map/make_adjoint/pallas_call | solution.py:575
  329.1 3.8 %collective-permute-start.33 = (bf16[3,16,192]{2,1,0:T(8,128)(2,1)}, bf16[3,16,192]{2,1,0:T(8,128)(2,1)S(1)}, u32[]{:S(2)}, u32[]{:S(2)}) collective-permute-start(bf16[3,16,192]{2,1,0:T(8,128)(2,1)} %get-tuple-element.107), channel_id=1, source_target_pairs={{8,0},{16,8},{24,16},{0,24},{9,1},{17,9},{25,17},{1,25},{10,2},{18... | collective-permute-start | bytes 55304 | tf_op jit(solution)/shard_map/ppermute | solution.py:524
  332.9 8.4 %add_grad_vort.5.refs_22_ = f32[3,16,192,256]{3,2,1,0:T(8,128)} custom-call(bf16[256,256]{1,0:T(8,128)(2,1)} %constant.41.clone.refs_0_, bf16[192,192]{1,0:T(8,128)(2,1)} %constant.42.clone.refs_1_, bf16[3,16,192,256]{3,2,1,0:T(8,128)(2,1)} %refs_4_.6, bf16[3,16,192,256]{3,2,1,0:T(8,128)(2,1)} %refs_4_.6, bf16[3,16,192,256]{3,2,1,0:T(8,128)(2,1)} %refs_4_.6, ...), custom_call_target="tpu_custom_call" | custom-call | flops 1 | bytes 27000000 | tf_op jit(solution)/shard_map/add_grad_vort/pallas_call | solution.py:698
  341.9 11.0 %write_grad_vel.1 = f32[3,16,192,256]{3,2,1,0:T(8,128)} custom-call(bf16[256,256]{1,0:T(8,128)(2,1)} %constant.43.clone.refs_0_, bf16[192,192]{1,0:T(8,128)(2,1)} %constant.44.clone.refs_1_, bf16[3,16,192,256]{3,2,1,0:T(8,128)(2,1)} %refs_4_.7, bf16[3,16,192,256]{3,2,1,0:T(8,128)(2,1)} %refs_4_.7, bf16[3,16,192,256]{3,2,1,0:T(8,128)(2,1)} %refs_4_.7, ...), custom_call_target="tpu_custom_call" | custom-call | flops 1 | bytes 36000000 | tf_op jit(solution)/shard_map/write_grad_vel/pallas_call | solution.py:787
  (189 shorter events, 79.2 us)
Async XLA Ops:
  3.8 26.2 %all-to-all-start = ((bf16[8,2,192,256]{3,2,1,0:T(8,128)(2,1)}), bf16[8,2,192,256]{3,2,1,0:T(8,128)(2,1)S(1)}, u32[]{:S(2)}, u32[]{:S(2)}) async-start(bf16[8,2,192,256]{3,2,1,0:T(8,128)(2,1)} %bitcast.28), calls=%async_computation | async-start | bytes 3145728 | tf_op jit(solution)/shard_map/all_to_all | solution.py:851
  16.9 5.3 %collective-permute-start.1 = (bf16[4,16,192]{2,1,0:T(8,128)(2,1)S(1)}, bf16[4,16,192]{2,1,0:T(8,128)(2,1)S(1)}, u32[]{:S(2)}, u32[]{:S(2)}) collective-permute-start(bf16[4,16,192]{2,1,0:T(8,128)(2,1)S(1)} %pad_maximum_fusion.1), channel_id=1, source_target_pairs={{8,0},{16,8},{24,16},{0,24},{9,1},{17,9},{25,17},{1,25},{10,2},{18... | collective-permute-start | bytes 73736 | tf_op jit(solution)/shard_map/ppermute | solution.py:524
  21.3 5.8 %collective-permute-start = (bf16[4,16,192]{2,1,0:T(8,128)(2,1)S(1)}, bf16[4,16,192]{2,1,0:T(8,128)(2,1)S(1)}, u32[]{:S(2)}, u32[]{:S(2)}) collective-permute-start(bf16[4,16,192]{2,1,0:T(8,128)(2,1)S(1)} %pad_maximum_fusion), channel_id=1, source_target_pairs={{0,8},{8,16},{16,24},{24,0},{1,9},{9,17},{17,25},{25,1},{2,10},{10... | collective-permute-start | bytes 73736 | tf_op jit(solution)/shard_map/ppermute | solution.py:524
  36.2 40.5 %all-to-all-start.1 = ((bf16[4,2,2,192,256]{4,3,2,1,0:T(8,128)(2,1)}), bf16[4,2,2,192,256]{4,3,2,1,0:T(8,128)(2,1)S(1)}, u32[]{:S(2)}, u32[]{:S(2)}) async-start(bf16[4,2,2,192,256]{4,3,2,1,0:T(8,128)(2,1)} %bitcast.3.refs_2_), calls=%async_computation.1 | async-start | bytes 3145728 | tf_op jit(solution)/shard_map/all_to_all | solution.py:865
  46.4 13.3 %collective-permute-start.2 = (bf16[2,192,256]{2,1,0:T(8,128)(2,1)}, bf16[2,192,256]{2,1,0:T(8,128)(2,1)S(1)}, u32[]{:S(2)}, u32[]{:S(2)}) collective-permute-start(bf16[2,192,256]{2,1,0:T(8,128)(2,1)} %get-tuple-element.61), channel_id=1, source_target_pairs={{0,1},{1,2},{2,3},{3,4},{4,5},{5,6},{6,7},{7,0},{8,9},{9,10},{10,1... | collective-permute-start | bytes 589832 | tf_op jit(solution)/shard_map/ppermute | solution.py:810
  46.4 13.8 %collective-permute-start.3 = (bf16[2,192,256]{2,1,0:T(8,128)(2,1)}, bf16[2,192,256]{2,1,0:T(8,128)(2,1)S(1)}, u32[]{:S(2)}, u32[]{:S(2)}) collective-permute-start(bf16[2,192,256]{2,1,0:T(8,128)(2,1)} %get-tuple-element.62), channel_id=1, source_target_pairs={{0,2},{1,3},{2,4},{3,5},{4,6},{5,7},{6,0},{7,1},{8,10},{9,11},{10,... | collective-permute-start | bytes 589832 | tf_op jit(solution)/shard_map/ppermute | solution.py:810
  47.0 12.1 %collective-permute-start.9 = (bf16[4,16,256]{2,1,0:T(8,128)(2,1)S(1)}, bf16[4,16,256]{2,1,0:T(8,128)(2,1)S(1)}, u32[]{:S(2)}, u32[]{:S(2)}) collective-permute-start(bf16[4,16,256]{2,1,0:T(8,128)(2,1)S(1)} %pad_maximum_fusion.2), channel_id=1, source_target_pairs={{0,1},{1,2},{2,3},{3,4},{4,5},{5,6},{6,7},{7,0},{8,9},{9,10},{10,1... | collective-permute-start | bytes 98312 | tf_op jit(solution)/shard_map/ppermute | solution.py:524
  48.3 11.4 %collective-permute-start.10 = (bf16[4,16,256]{2,1,0:T(8,128)(2,1)S(1)}, bf16[4,16,256]{2,1,0:T(8,128)(2,1)S(1)}, u32[]{:S(2)}, u32[]{:S(2)}) collective-permute-start(bf16[4,16,256]{2,1,0:T(8,128)(2,1)S(1)} %pad_maximum_fusion.3), channel_id=1, source_target_pairs={{1,0},{2,1},{3,2},{4,3},{5,4},{6,5},{7,6},{0,7},{9,8},{10,9},{11,1... | collective-permute-start | bytes 98312 | tf_op jit(solution)/shard_map/ppermute | solution.py:524
  49.7 12.7 %collective-permute-start.4 = (bf16[2,192,256]{2,1,0:T(8,128)(2,1)}, bf16[2,192,256]{2,1,0:T(8,128)(2,1)S(1)}, u32[]{:S(2)}, u32[]{:S(2)}) collective-permute-start(bf16[2,192,256]{2,1,0:T(8,128)(2,1)} %get-tuple-element.63), channel_id=1, source_target_pairs={{0,3},{1,4},{2,5},{3,6},{4,7},{5,0},{6,1},{7,2},{8,11},{9,12},{10,... | collective-permute-start | bytes 589832 | tf_op jit(solution)/shard_map/ppermute | solution.py:810
  59.2 6.5 %collective-permute-start.5 = (bf16[2,192,256]{2,1,0:T(8,128)(2,1)}, bf16[2,192,256]{2,1,0:T(8,128)(2,1)S(1)}, u32[]{:S(2)}, u32[]{:S(2)}) collective-permute-start(bf16[2,192,256]{2,1,0:T(8,128)(2,1)} %get-tuple-element.64), channel_id=1, source_target_pairs={{0,4},{1,5},{2,6},{3,7},{4,0},{5,1},{6,2},{7,3},{8,12},{9,13},{10,... | collective-permute-start | bytes 589832 | tf_op jit(solution)/shard_map/ppermute | solution.py:810
  59.7 6.8 %collective-permute-start.6 = (bf16[2,192,256]{2,1,0:T(8,128)(2,1)}, bf16[2,192,256]{2,1,0:T(8,128)(2,1)S(1)}, u32[]{:S(2)}, u32[]{:S(2)}) collective-permute-start(bf16[2,192,256]{2,1,0:T(8,128)(2,1)} %get-tuple-element.65), channel_id=1, source_target_pairs={{0,5},{1,6},{2,7},{3,0},{4,1},{5,2},{6,3},{7,4},{8,13},{9,14},{10,... | collective-permute-start | bytes 589832 | tf_op jit(solution)/shard_map/ppermute | solution.py:810
  59.7 8.0 %collective-permute-start.7 = (bf16[2,192,256]{2,1,0:T(8,128)(2,1)}, bf16[2,192,256]{2,1,0:T(8,128)(2,1)S(1)}, u32[]{:S(2)}, u32[]{:S(2)}) collective-permute-start(bf16[2,192,256]{2,1,0:T(8,128)(2,1)} %get-tuple-element.66), channel_id=1, source_target_pairs={{0,6},{1,7},{2,0},{3,1},{4,2},{5,3},{6,4},{7,5},{8,14},{9,15},{10,... | collective-permute-start | bytes 589832 | tf_op jit(solution)/shard_map/ppermute | solution.py:810
  60.3 9.2 %collective-permute-start.8 = (bf16[2,192,256]{2,1,0:T(8,128)(2,1)}, bf16[2,192,256]{2,1,0:T(8,128)(2,1)S(1)}, u32[]{:S(2)}, u32[]{:S(2)}) collective-permute-start(bf16[2,192,256]{2,1,0:T(8,128)(2,1)} %get-tuple-element.67), channel_id=1, source_target_pairs={{0,7},{1,0},{2,1},{3,2},{4,3},{5,4},{6,5},{7,6},{8,15},{9,8},{10,9... | collective-permute-start | bytes 589832 | tf_op jit(solution)/shard_map/ppermute | solution.py:810
  76.7 42.9 %all-to-all-start.3 = ((bf16[4,2,2,192,256]{4,3,2,1,0:T(8,128)(2,1)}), bf16[4,2,2,192,256]{4,3,2,1,0:T(8,128)(2,1)}, u32[]{:S(2)}, u32[]{:S(2)}) async-start(bf16[4,2,2,192,256]{4,3,2,1,0:T(8,128)(2,1)} %bitcast.22), calls=%async_computation.3 | async-start | bytes 3145728 | tf_op jit(solution)/shard_map/all_to_all | solution.py:865
  85.1 11.5 %collective-permute-start.11 = (bf16[2,192,256]{2,1,0:T(8,128)(2,1)}, bf16[2,192,256]{2,1,0:T(8,128)(2,1)S(1)}, u32[]{:S(2)}, u32[]{:S(2)}) collective-permute-start(bf16[2,192,256]{2,1,0:T(8,128)(2,1)} %get-tuple-element.69), channel_id=1, source_target_pairs={{0,1},{1,2},{2,3},{3,4},{4,5},{5,6},{6,7},{7,0},{8,9},{9,10},{10,1... | collective-permute-start | bytes 589832 | tf_op jit(solution)/shard_map/ppermute | solution.py:810
  86.9 11.0 %collective-permute-start.12 = (bf16[2,192,256]{2,1,0:T(8,128)(2,1)}, bf16[2,192,256]{2,1,0:T(8,128)(2,1)S(1)}, u32[]{:S(2)}, u32[]{:S(2)}) collective-permute-start(bf16[2,192,256]{2,1,0:T(8,128)(2,1)} %get-tuple-element.70), channel_id=1, source_target_pairs={{0,2},{1,3},{2,4},{3,5},{4,6},{5,7},{6,0},{7,1},{8,10},{9,11},{10,... | collective-permute-start | bytes 589832 | tf_op jit(solution)/shard_map/ppermute | solution.py:810
  91.1 14.4 %collective-permute-start.13 = (bf16[2,192,256]{2,1,0:T(8,128)(2,1)}, bf16[2,192,256]{2,1,0:T(8,128)(2,1)S(1)}, u32[]{:S(2)}, u32[]{:S(2)}) collective-permute-start(bf16[2,192,256]{2,1,0:T(8,128)(2,1)} %get-tuple-element.71), channel_id=1, source_target_pairs={{0,3},{1,4},{2,5},{3,6},{4,7},{5,0},{6,1},{7,2},{8,11},{9,12},{10,... | collective-permute-start | bytes 589832 | tf_op jit(solution)/shard_map/ppermute | solution.py:810
  91.8 13.9 %collective-permute-start.14 = (bf16[2,192,256]{2,1,0:T(8,128)(2,1)}, bf16[2,192,256]{2,1,0:T(8,128)(2,1)S(1)}, u32[]{:S(2)}, u32[]{:S(2)}) collective-permute-start(bf16[2,192,256]{2,1,0:T(8,128)(2,1)} %get-tuple-element.72), channel_id=1, source_target_pairs={{0,4},{1,5},{2,6},{3,7},{4,0},{5,1},{6,2},{7,3},{8,12},{9,13},{10,... | collective-permute-start | bytes 589832 | tf_op jit(solution)/shard_map/ppermute | solution.py:810
  93.2 14.8 %collective-permute-start.15 = (bf16[2,192,256]{2,1,0:T(8,128)(2,1)}, bf16[2,192,256]{2,1,0:T(8,128)(2,1)S(1)}, u32[]{:S(2)}, u32[]{:S(2)}) collective-permute-start(bf16[2,192,256]{2,1,0:T(8,128)(2,1)} %get-tuple-element.73), channel_id=1, source_target_pairs={{0,5},{1,6},{2,7},{3,0},{4,1},{5,2},{6,3},{7,4},{8,13},{9,14},{10,... | collective-permute-start | bytes 589832 | tf_op jit(solution)/shard_map/ppermute | solution.py:810
  96.6 11.5 %collective-permute-start.16 = (bf16[2,192,256]{2,1,0:T(8,128)(2,1)}, bf16[2,192,256]{2,1,0:T(8,128)(2,1)S(1)}, u32[]{:S(2)}, u32[]{:S(2)}) collective-permute-start(bf16[2,192,256]{2,1,0:T(8,128)(2,1)} %get-tuple-element.74), channel_id=1, source_target_pairs={{0,6},{1,7},{2,0},{3,1},{4,2},{5,3},{6,4},{7,5},{8,14},{9,15},{10,... | collective-permute-start | bytes 589832 | tf_op jit(solution)/shard_map/ppermute | solution.py:810
  97.9 10.2 %collective-permute-start.17 = (bf16[2,192,256]{2,1,0:T(8,128)(2,1)}, bf16[2,192,256]{2,1,0:T(8,128)(2,1)S(1)}, u32[]{:S(2)}, u32[]{:S(2)}) collective-permute-start(bf16[2,192,256]{2,1,0:T(8,128)(2,1)} %get-tuple-element.75), channel_id=1, source_target_pairs={{0,7},{1,0},{2,1},{3,2},{4,3},{5,4},{6,5},{7,6},{8,15},{9,8},{10,9... | collective-permute-start | bytes 589832 | tf_op jit(solution)/shard_map/ppermute | solution.py:810
  119.6 42.4 %all-to-all-start.2 = ((bf16[4,2,2,192,256]{4,3,2,1,0:T(8,128)(2,1)}), bf16[4,2,2,192,256]{4,3,2,1,0:T(8,128)(2,1)}, u32[]{:S(2)}, u32[]{:S(2)}) async-start(bf16[4,2,2,192,256]{4,3,2,1,0:T(8,128)(2,1)} %bitcast.25), calls=%async_computation.2 | async-start | bytes 3145728 | tf_op jit(solution)/shard_map/all_to_all | solution.py:865
  162.0 41.6 %all-to-all-start.4 = ((bf16[4,2,2,192,256]{4,3,2,1,0:T(8,128)(2,1)}), bf16[4,2,2,192,256]{4,3,2,1,0:T(8,128)(2,1)}, u32[]{:S(2)}, u32[]{:S(2)}) async-start(bf16[4,2,2,192,256]{4,3,2,1,0:T(8,128)(2,1)} %copy-done.12), calls=%async_computation.4 | async-start | bytes 3145728 | tf_op jit(solution)/shard_map/all_to_all | solution.py:872
  203.6 40.9 %all-to-all-start.6 = ((bf16[4,2,2,192,256]{4,3,2,1,0:T(8,128)(2,1)}), bf16[4,2,2,192,256]{4,3,2,1,0:T(8,128)(2,1)}, u32[]{:S(2)}, u32[]{:S(2)}) async-start(bf16[4,2,2,192,256]{4,3,2,1,0:T(8,128)(2,1)} %copy-done.14), calls=%async_computation.6 | async-start | bytes 3145728 | tf_op jit(solution)/shard_map/all_to_all | solution.py:872
  207.9 29.5 %copy-start.3 = (f32[2,2,192,1024]{3,2,1,0:T(8,128)S(1)}, f32[2,2,192,1024]{3,2,1,0:T(8,128)}, u32[]{:S(2)}) copy-start(f32[2,2,192,1024]{3,2,1,0:T(8,128)} %copy-done.2) | copy-start | bytes 9437188
  207.9 29.5 %copy-start.5 = (f32[2,2,192,1024]{3,2,1,0:T(8,128)S(1)}, f32[2,2,192,1024]{3,2,1,0:T(8,128)}, u32[]{:S(2)}) copy-start(f32[2,2,192,1024]{3,2,1,0:T(8,128)} %copy-done.4) | copy-start | bytes 9437188
  215.3 7.6 %collective-permute-start.18 = (bf16[2,192,256]{2,1,0:T(8,128)(2,1)}, bf16[2,192,256]{2,1,0:T(8,128)(2,1)S(1)}, u32[]{:S(2)}, u32[]{:S(2)}) collective-permute-start(bf16[2,192,256]{2,1,0:T(8,128)(2,1)} %get-tuple-element.77), channel_id=1, source_target_pairs={{0,1},{1,2},{2,3},{3,4},{4,5},{5,6},{6,7},{7,0},{8,9},{9,10},{10,1... | collective-permute-start | bytes 589832 | tf_op jit(solution)/shard_map/ppermute | solution.py:810
  215.4 11.8 %collective-permute-start.19 = (bf16[2,192,256]{2,1,0:T(8,128)(2,1)}, bf16[2,192,256]{2,1,0:T(8,128)(2,1)S(1)}, u32[]{:S(2)}, u32[]{:S(2)}) collective-permute-start(bf16[2,192,256]{2,1,0:T(8,128)(2,1)} %get-tuple-element.78), channel_id=1, source_target_pairs={{0,2},{1,3},{2,4},{3,5},{4,6},{5,7},{6,0},{7,1},{8,10},{9,11},{10,... | collective-permute-start | bytes 589832 | tf_op jit(solution)/shard_map/ppermute | solution.py:810
  219.8 13.2 %collective-permute-start.20 = (bf16[2,192,256]{2,1,0:T(8,128)(2,1)}, bf16[2,192,256]{2,1,0:T(8,128)(2,1)S(1)}, u32[]{:S(2)}, u32[]{:S(2)}) collective-permute-start(bf16[2,192,256]{2,1,0:T(8,128)(2,1)} %get-tuple-element.79), channel_id=1, source_target_pairs={{0,3},{1,4},{2,5},{3,6},{4,7},{5,0},{6,1},{7,2},{8,11},{9,12},{10,... | collective-permute-start | bytes 589832 | tf_op jit(solution)/shard_map/ppermute | solution.py:810
  221.8 11.4 %collective-permute-start.21 = (bf16[2,192,256]{2,1,0:T(8,128)(2,1)}, bf16[2,192,256]{2,1,0:T(8,128)(2,1)S(1)}, u32[]{:S(2)}, u32[]{:S(2)}) collective-permute-start(bf16[2,192,256]{2,1,0:T(8,128)(2,1)} %get-tuple-element.80), channel_id=1, source_target_pairs={{0,4},{1,5},{2,6},{3,7},{4,0},{5,1},{6,2},{7,3},{8,12},{9,13},{10,... | collective-permute-start | bytes 589832 | tf_op jit(solution)/shard_map/ppermute | solution.py:810
  222.7 13.1 %collective-permute-start.22 = (bf16[2,192,256]{2,1,0:T(8,128)(2,1)}, bf16[2,192,256]{2,1,0:T(8,128)(2,1)S(1)}, u32[]{:S(2)}, u32[]{:S(2)}) collective-permute-start(bf16[2,192,256]{2,1,0:T(8,128)(2,1)} %get-tuple-element.81), channel_id=1, source_target_pairs={{0,5},{1,6},{2,7},{3,0},{4,1},{5,2},{6,3},{7,4},{8,13},{9,14},{10,... | collective-permute-start | bytes 589832 | tf_op jit(solution)/shard_map/ppermute | solution.py:810
  222.9 20.9 %copy-start.22 = (bf16[2,192,256]{2,1,0:T(8,128)(2,1)}, bf16[2,192,256]{2,1,0:T(8,128)(2,1)S(1)}, u32[]{:S(2)}) copy-start(bf16[2,192,256]{2,1,0:T(8,128)(2,1)S(1)} %collective-permute-done.18.refs_5_.refs_1_) | copy-start | bytes 589828
  222.9 12.9 %collective-permute-start.23 = (bf16[2,192,256]{2,1,0:T(8,128)(2,1)}, bf16[2,192,256]{2,1,0:T(8,128)(2,1)S(1)}, u32[]{:S(2)}, u32[]{:S(2)}) collective-permute-start(bf16[2,192,256]{2,1,0:T(8,128)(2,1)} %get-tuple-element.82), channel_id=1, source_target_pairs={{0,6},{1,7},{2,0},{3,1},{4,2},{5,3},{6,4},{7,5},{8,14},{9,15},{10,... | collective-permute-start | bytes 589832 | tf_op jit(solution)/shard_map/ppermute | solution.py:810
  227.2 10.3 %collective-permute-start.24 = (bf16[2,192,256]{2,1,0:T(8,128)(2,1)}, bf16[2,192,256]{2,1,0:T(8,128)(2,1)S(1)}, u32[]{:S(2)}, u32[]{:S(2)}) collective-permute-start(bf16[2,192,256]{2,1,0:T(8,128)(2,1)} %get-tuple-element.83), channel_id=1, source_target_pairs={{0,7},{1,0},{2,1},{3,2},{4,3},{5,4},{6,5},{7,6},{8,15},{9,8},{10,9... | collective-permute-start | bytes 589832 | tf_op jit(solution)/shard_map/ppermute | solution.py:810
  244.5 41.5 %all-to-all-start.5 = ((bf16[4,2,2,192,256]{4,3,2,1,0:T(8,128)(2,1)}), bf16[4,2,2,192,256]{4,3,2,1,0:T(8,128)(2,1)S(1)}, u32[]{:S(2)}, u32[]{:S(2)}) async-start(bf16[4,2,2,192,256]{4,3,2,1,0:T(8,128)(2,1)} %curl_inverse.5), calls=%async_computation.5 | async-start | bytes 3145728 | tf_op jit(solution)/shard_map/all_to_all | solution.py:872
  261.5 9.0 %collective-permute-start.25 = (bf16[2,192,256]{2,1,0:T(8,128)(2,1)}, bf16[2,192,256]{2,1,0:T(8,128)(2,1)S(1)}, u32[]{:S(2)}, u32[]{:S(2)}) collective-permute-start(bf16[2,192,256]{2,1,0:T(8,128)(2,1)} %get-tuple-element.86), channel_id=1, source_target_pairs={{0,1},{1,2},{2,3},{3,4},{4,5},{5,6},{6,7},{7,0},{8,9},{9,10},{10,1... | collective-permute-start | bytes 589832 | tf_op jit(solution)/shard_map/ppermute | solution.py:810
  261.5 10.8 %collective-permute-start.26 = (bf16[2,192,256]{2,1,0:T(8,128)(2,1)}, bf16[2,192,256]{2,1,0:T(8,128)(2,1)S(1)}, u32[]{:S(2)}, u32[]{:S(2)}) collective-permute-start(bf16[2,192,256]{2,1,0:T(8,128)(2,1)} %get-tuple-element.87), channel_id=1, source_target_pairs={{0,2},{1,3},{2,4},{3,5},{4,6},{5,7},{6,0},{7,1},{8,10},{9,11},{10,... | collective-permute-start | bytes 589832 | tf_op jit(solution)/shard_map/ppermute | solution.py:810
  265.1 14.2 %collective-permute-start.27 = (bf16[2,192,256]{2,1,0:T(8,128)(2,1)}, bf16[2,192,256]{2,1,0:T(8,128)(2,1)S(1)}, u32[]{:S(2)}, u32[]{:S(2)}) collective-permute-start(bf16[2,192,256]{2,1,0:T(8,128)(2,1)} %get-tuple-element.88), channel_id=1, source_target_pairs={{0,3},{1,4},{2,5},{3,6},{4,7},{5,0},{6,1},{7,2},{8,11},{9,12},{10,... | collective-permute-start | bytes 589832 | tf_op jit(solution)/shard_map/ppermute | solution.py:810
  267.1 12.4 %collective-permute-start.28 = (bf16[2,192,256]{2,1,0:T(8,128)(2,1)}, bf16[2,192,256]{2,1,0:T(8,128)(2,1)S(1)}, u32[]{:S(2)}, u32[]{:S(2)}) collective-permute-start(bf16[2,192,256]{2,1,0:T(8,128)(2,1)} %get-tuple-element.89), channel_id=1, source_target_pairs={{0,4},{1,5},{2,6},{3,7},{4,0},{5,1},{6,2},{7,3},{8,12},{9,13},{10,... | collective-permute-start | bytes 589832 | tf_op jit(solution)/shard_map/ppermute | solution.py:810
  267.9 14.2 %collective-permute-start.29 = (bf16[2,192,256]{2,1,0:T(8,128)(2,1)}, bf16[2,192,256]{2,1,0:T(8,128)(2,1)S(1)}, u32[]{:S(2)}, u32[]{:S(2)}) collective-permute-start(bf16[2,192,256]{2,1,0:T(8,128)(2,1)} %get-tuple-element.90), channel_id=1, source_target_pairs={{0,5},{1,6},{2,7},{3,0},{4,1},{5,2},{6,3},{7,4},{8,13},{9,14},{10,... | collective-permute-start | bytes 589832 | tf_op jit(solution)/shard_map/ppermute | solution.py:810
  270.4 22.7 %copy-start.20 = (bf16[2,192,256]{2,1,0:T(8,128)(2,1)}, bf16[2,192,256]{2,1,0:T(8,128)(2,1)S(1)}, u32[]{:S(2)}) copy-start(bf16[2,192,256]{2,1,0:T(8,128)(2,1)S(1)} %collective-permute-done.25.refs_1_) | copy-start | bytes 589828
  270.4 11.7 %collective-permute-start.30 = (bf16[2,192,256]{2,1,0:T(8,128)(2,1)}, bf16[2,192,256]{2,1,0:T(8,128)(2,1)S(1)}, u32[]{:S(2)}, u32[]{:S(2)}) collective-permute-start(bf16[2,192,256]{2,1,0:T(8,128)(2,1)} %get-tuple-element.91), channel_id=1, source_target_pairs={{0,6},{1,7},{2,0},{3,1},{4,2},{5,3},{6,4},{7,5},{8,14},{9,15},{10,... | collective-permute-start | bytes 589832 | tf_op jit(solution)/shard_map/ppermute | solution.py:810
  272.4 10.3 %collective-permute-start.31 = (bf16[2,192,256]{2,1,0:T(8,128)(2,1)}, bf16[2,192,256]{2,1,0:T(8,128)(2,1)S(1)}, u32[]{:S(2)}, u32[]{:S(2)}) collective-permute-start(bf16[2,192,256]{2,1,0:T(8,128)(2,1)} %get-tuple-element.92), channel_id=1, source_target_pairs={{0,7},{1,0},{2,1},{3,2},{4,3},{5,4},{6,5},{7,6},{8,15},{9,8},{10,9... | collective-permute-start | bytes 589832 | tf_op jit(solution)/shard_map/ppermute | solution.py:810
  293.2 26.9 %all-to-all-start.7 = ((bf16[8,2,192,256]{3,2,1,0:T(8,128)(2,1)}), bf16[8,2,192,256]{3,2,1,0:T(8,128)(2,1)S(1)}, u32[]{:S(2)}, u32[]{:S(2)}) async-start(bf16[8,2,192,256]{3,2,1,0:T(8,128)(2,1)} %y_inverse.1.refs_13_), calls=%async_computation.7 | async-start | bytes 3145728 | tf_op jit(solution)/shard_map/all_to_all | solution.py:884
  326.4 14.9 %collective-permute-start.34 = (bf16[3,16,256]{2,1,0:T(8,128)(2,1)}, bf16[3,16,256]{2,1,0:T(8,128)(2,1)S(1)}, u32[]{:S(2)}, u32[]{:S(2)}) collective-permute-start(bf16[3,16,256]{2,1,0:T(8,128)(2,1)} %get-tuple-element.108), channel_id=1, source_target_pairs={{0,1},{1,2},{2,3},{3,4},{4,5},{5,6},{6,7},{7,0},{8,9},{9,10},{10,1... | collective-permute-start | bytes 73736 | tf_op jit(solution)/shard_map/ppermute | solution.py:524
  326.4 14.9 %collective-permute-start.35 = (bf16[3,16,256]{2,1,0:T(8,128)(2,1)}, bf16[3,16,256]{2,1,0:T(8,128)(2,1)S(1)}, u32[]{:S(2)}, u32[]{:S(2)}) collective-permute-start(bf16[3,16,256]{2,1,0:T(8,128)(2,1)} %get-tuple-element.109), channel_id=1, source_target_pairs={{1,0},{2,1},{3,2},{4,3},{5,4},{6,5},{7,6},{0,7},{9,8},{10,9},{11,1... | collective-permute-start | bytes 73736 | tf_op jit(solution)/shard_map/ppermute | solution.py:524
  329.1 12.2 %collective-permute-start.32 = (bf16[3,16,192]{2,1,0:T(8,128)(2,1)}, bf16[3,16,192]{2,1,0:T(8,128)(2,1)S(1)}, u32[]{:S(2)}, u32[]{:S(2)}) collective-permute-start(bf16[3,16,192]{2,1,0:T(8,128)(2,1)} %get-tuple-element.106), channel_id=1, source_target_pairs={{0,8},{8,16},{16,24},{24,0},{1,9},{9,17},{17,25},{25,1},{2,10},{10... | collective-permute-start | bytes 55304 | tf_op jit(solution)/shard_map/ppermute | solution.py:524
  329.1 12.2 %collective-permute-start.33 = (bf16[3,16,192]{2,1,0:T(8,128)(2,1)}, bf16[3,16,192]{2,1,0:T(8,128)(2,1)S(1)}, u32[]{:S(2)}, u32[]{:S(2)}) collective-permute-start(bf16[3,16,192]{2,1,0:T(8,128)(2,1)} %get-tuple-element.107), channel_id=1, source_target_pairs={{8,0},{16,8},{24,16},{0,24},{9,1},{17,9},{25,17},{1,25},{10,2},{18... | collective-permute-start | bytes 55304 | tf_op jit(solution)/shard_map/ppermute | solution.py:524
  (53 other events, 304.7 us)

commit v14 on v13

--- a/solution.py
+++ b/solution.py
@@ -865,6 +865,16 @@
         lines = lax.all_to_all(sent[place], "gx", 0, 0, tiled=True)
         return x_transform(x_table, lines, after)
 
+    third = shifted(
+        [
+            lax.dynamic_index_in_dim(sent[2], lax.rem(place_x + s, size_x), 0, keepdims=False)
+            for s in range(size_x)
+        ],
+        "gx",
+    )
+    sources = lax.rem(place_x + size_x - jnp.arange(size_x), size_x)
+    third_lines = jnp.take(jnp.stack(third), sources, axis=0)
+
     def curl(component, after):
         return curl_inverse(where, x_back_table, spectra, component, size_x, after)
 
@@ -886,9 +896,9 @@
 
     one, two, three = BACK_ORDER
     spectra = {FORWARD_ORDER[0]: spectrum(0, (sent[1],))}
-    spectra[FORWARD_ORDER[1]] = spectrum(1, (sent[2],))
+    spectra[FORWARD_ORDER[1]] = spectrum(1, (third[size_x // 2],))
     curl_one = curl(one, ())
-    spectra[FORWARD_ORDER[2]] = spectrum(2, (curl_one,))
+    spectra[FORWARD_ORDER[2]] = x_transform(x_table, third_lines, (curl_one,))
     curl_two = curl(two, ())
     rows_one = rows_of(one, back(curl_one), (curl_two,))
     layers_one = layers_of(rows_one)

time: 354 us -> 373 us (1.054)
  local copies, waits for them, and re-layouts: 22 us -> 31.6 us
  waiting for transfers between devices: 115 us -> 121 us
  other arithmetic: 1.58 us -> 5.95 us
    ppermute x28 -> x31, waiting for transfers between devices: 34.3 us -> 92.3 us  [shifted(): lax.ppermute(parts[s], axis, [(i, (i + s) % count) for i in range(count)])]
    all_to_all x3 -> x2, waiting for transfers between devices: 30.3 us -> 0.01 us  [spectrum(): lines = lax.all_to_all(sent[place], 'gx', 0, 0, tiled=True)]
    all_to_all x3, waiting for transfers between devices: 28.8 us -> 7.69 us  [back(): parts = lax.all_to_all(filtered, 'gx', 0, 0, tiled=True)]
    all_to_all x3, starting transfers between devices: 13.3 us -> 18.7 us  [back(): parts = lax.all_to_all(filtered, 'gx', 0, 0, tiled=True)]
    all_to_all x3 -> x2, starting transfers between devices: 14.3 us -> 9.97 us  [spectrum(): lines = lax.all_to_all(sent[place], 'gx', 0, 0, tiled=True)]
    unnamed x118 -> x120, local copies, waits for them, and re-layouts: 20 us -> 23.7 us
    ppermute x28 -> x31, starting transfers between devices: 42.8 us -> 43 us  [shifted(): lax.ppermute(parts[s], axis, [(i, (i + s) % count) for i in range(count)])]
  transfers between devices with their start and end apart: 44 -> 46, of which waited for: 29 -> 27; matrix products, arithmetic and copies ran while one was open for 1% -> 4% of each run, Pallas kernels for 26% -> 23%
where the time goes in v14:
time: 373 us; the launch traced here: 372 us
  waiting for transfers between devices  121 us (32%)
  Pallas kernels  117 us (31%)
  starting transfers between devices  94.1 us (25%)
  local copies, waits for them, and re-layouts  31.6 us (8%)
  other arithmetic  5.95 us (2%)
    ppermute x31, waiting for transfers between devices, shifted(): lax.ppermute(parts[s], axis, [(i, (i + s) % count) for i in range(count)])  92.3 us
    ppermute x31, starting transfers between devices, shifted(): lax.ppermute(parts[s], axis, [(i, (i + s) % count) for i in range(count)])  43 us
    unnamed x120, local copies, waits for them, and re-layouts  23.7 us
    pallas_call x3, Pallas kernels, add_grad_vort(): pl.pallas_call(kernel, grid=(Z // LAYERS,), in_specs=in_specs + tied(afte...  20.7 us
    all_to_all x3, starting transfers between devices, back(): parts = lax.all_to_all(filtered, 'gx', 0, 0, tiled=True)  18.7 us
    pallas_call x3, Pallas kernels, make_adjoint(): pl.pallas_call(kernel, grid=(height // ROWS,), in_specs=[pl.BlockSpec(mem...  15.8 us
    ppermute x8, waiting for transfers between devices, exchange(): return (lax.ppermute(last, axis, up), lax.ppermute(first, axis, down))  15.1 us
    pallas_call x2, Pallas kernels, y_inverse_parts(): pl.pallas_call(kernel, in_specs=[pl.BlockSpec(memory_space=pltpu.SMEM), a...  14.6 us
  transfers between devices with their start and end apart: 46, of which 27 were waited for; matrix products, arithmetic and copies ran while one was open for 4% of the time, Pallas kernels for 23%

profile of v14, /device:TPU:0, one launch (start us, length us, event | category | flops | bytes accessed | tf_op | source)
XLA Modules:
  0.0 371.6 jit_solution(8065565651692540007)
XLA Ops:
  0.6 3.2 depth_transform.3.refs_0_
  3.8 5.2 %all-to-all-start = ((bf16[8,2,192,256]{3,2,1,0:T(8,128)(2,1)}), bf16[8,2,192,256]{3,2,1,0:T(8,128)(2,1)S(1)}, u32[]{:S(2)}, u32[]{:S(2)}) async-start(bf16[8,2,192,256]{3,2,1,0:T(8,128)(2,1)} %bitcast.39), calls=%async_computation | async-start | bytes 3145728 | tf_op jit(solution)/shard_map/all_to_all | solution.py:851
  11.6 4.6 %edge_columns.2 = (bf16[3,16,192]{2,1,0:T(8,128)(2,1)}, bf16[3,16,192]{2,1,0:T(8,128)(2,1)}) custom-call(bf16[3,16,192,256]{3,2,1,0:T(8,128)(2,1)} %refs_4_.6, bf16[16,192,256]{2,1,0:T(8,128)(2,1)} %depth_transform.3.refs_0_), custom_call_target="tpu_custom_call" | custom-call | flops 1 | bytes 12000000 | tf_op jit(solution)/shard_map/edge_columns/pallas_call | solution.py:508
  16.9 3.7 collective-permute-start.1
  22.2 4.9 %collective-permute-done.refs_0_.refs_6_.refs_14_ = bf16[4,16,192]{2,1,0:T(8,128)(2,1)S(1)} collective-permute-done((bf16[4,16,192]{2,1,0:T(8,128)(2,1)S(1)}, bf16[4,16,192]{2,1,0:T(8,128)(2,1)S(1)}, u32[]{:S(2)}, u32[]{:S(2)}) %collective-permute-start) | collective-permute-done | bytes 24608 | tf_op jit(solution)/shard_map/ppermute | solution.py:524
  27.1 2.9 all-to-all-done.columns_ref
  32.3 3.9 %y_transform.1 = bf16[4,1,2,2,192,256]{5,4,3,2,1,0:T(8,128)(2,1)} custom-call(bf16[1536,1536]{1,0:T(8,128)(2,1)S(1)} %copy-done.1, bf16[8,2,192,256]{3,2,1,0:T(8,128)(2,1)S(1)} %all-to-all-done.columns_ref, bf16[4,16,192]{2,1,0:T(8,128)(2,1)S(1)} %collective-permute-done.refs_0_.refs_6_.refs_14_, ...), custom_call_target="tpu_custom_call" | custom-call | flops 1 | bytes 12000000 | tf_op jit(solution)/shard_map/y_transform/pallas_call | solution.py:198
  36.2 4.9 %all-to-all-start.1 = ((bf16[4,2,2,192,256]{4,3,2,1,0:T(8,128)(2,1)}), bf16[4,2,2,192,256]{4,3,2,1,0:T(8,128)(2,1)S(1)}, u32[]{:S(2)}, u32[]{:S(2)}) async-start(bf16[4,2,2,192,256]{4,3,2,1,0:T(8,128)(2,1)} %bitcast.3.refs_2_), calls=%async_computation.1 | async-start | bytes 3145728 | tf_op jit(solution)/shard_map/all_to_all | solution.py:865
  43.1 3.3 depth_transform.4
  49.7 9.4 %collective-permute-done.9.refs_8_.refs_16_ = bf16[4,16,256]{2,1,0:T(8,128)(2,1)S(1)} collective-permute-done((bf16[4,16,256]{2,1,0:T(8,128)(2,1)S(1)}, bf16[4,16,256]{2,1,0:T(8,128)(2,1)S(1)}, u32[]{:S(2)}, u32[]{:S(2)}) %collective-permute-start.9) | collective-permute-done | bytes 32800 | tf_op jit(solution)/shard_map/ppermute | solution.py:524
  62.5 3.2 collective-permute-done.5.refs_4_
  70.1 6.6 %y_transform_parts.2 = bf16[4,1,2,2,192,256]{5,4,3,2,1,0:T(8,128)(2,1)} custom-call(s32[1]{0:T(128)} %bitcast.refs_0_.me_ref, bf16[1536,1536]{1,0:T(8,128)(2,1)} %constant.83.clone.table_ref, bf16[2,192,256]{2,1,0:T(8,128)(2,1)} %get-tuple-element.60.refs_0_, bf16[2,192,256]{2,1,0:T(8,128)(2,1)} %copy-done.45, bf16[2,192,256]{2,1,0:T(8,128)(2,1)} %copy-done.46, ...), custom_call_target="tpu_custom_call" | custom-call | flops 1 | bytes 15000000 | tf_op jit(solution)/shard_map/y_transform_parts/pallas_call | solution.py:252
  76.7 5.1 %all-to-all-start.2 = ((bf16[4,2,2,192,256]{4,3,2,1,0:T(8,128)(2,1)}), bf16[4,2,2,192,256]{4,3,2,1,0:T(8,128)(2,1)}, u32[]{:S(2)}, u32[]{:S(2)}) async-start(bf16[4,2,2,192,256]{4,3,2,1,0:T(8,128)(2,1)} %bitcast.34), calls=%async_computation.2 | async-start | bytes 3145728 | tf_op jit(solution)/shard_map/all_to_all | solution.py:865
  81.8 3.3 depth_transform.5
  86.8 4.2 %collective-permute-start.12 = (bf16[2,192,256]{2,1,0:T(8,128)(2,1)}, bf16[2,192,256]{2,1,0:T(8,128)(2,1)S(1)}, u32[]{:S(2)}, u32[]{:S(2)}) collective-permute-start(bf16[2,192,256]{2,1,0:T(8,128)(2,1)} %get-tuple-element.70), channel_id=1, source_target_pairs={{0,2},{1,3},{2,4},{3,5},{4,6},{5,7},{6,0},{7,1},{8,10},{9,11},{10,... | collective-permute-start | bytes 589832 | tf_op jit(solution)/shard_map/ppermute | solution.py:810
  100.1 5.3 %collective-permute-done.13.refs_3_ = bf16[2,192,256]{2,1,0:T(8,128)(2,1)S(1)} collective-permute-done((bf16[2,192,256]{2,1,0:T(8,128)(2,1)}, bf16[2,192,256]{2,1,0:T(8,128)(2,1)S(1)}, u32[]{:S(2)}, u32[]{:S(2)}) %collective-permute-start.13) | collective-permute-done | bytes 196640 | tf_op jit(solution)/shard_map/ppermute | solution.py:810
  108.9 6.6 %y_transform_parts.3 = bf16[4,1,2,2,192,256]{5,4,3,2,1,0:T(8,128)(2,1)} custom-call(s32[1]{0:T(128)} %bitcast.refs_0_.me_ref, bf16[1536,1536]{1,0:T(8,128)(2,1)} %constant.83.clone.table_ref, bf16[2,192,256]{2,1,0:T(8,128)(2,1)} %get-tuple-element.68.refs_0_, bf16[2,192,256]{2,1,0:T(8,128)(2,1)} %copy-done.38, bf16[2,192,256]{2,1,0:T(8,128)(2,1)} %copy-done.39, ...), custom_call_target="tpu_custom_call" | custom-call | flops 1 | bytes 15000000 | tf_op jit(solution)/shard_map/y_transform_parts/pallas_call | solution.py:252
  126.4 12.4 %collective-permute-done.19.refs_0_ = bf16[2,2,192,256]{3,2,1,0:T(8,128)(2,1)S(1)} collective-permute-done((bf16[2,2,192,256]{3,2,1,0:T(8,128)(2,1)}, bf16[2,2,192,256]{3,2,1,0:T(8,128)(2,1)S(1)}, u32[]{:S(2)}, u32[]{:S(2)}) %collective-permute-start.19) | collective-permute-done | bytes 393248 | tf_op jit(solution)/shard_map/ppermute | solution.py:810
  140.3 3.3 x_transform.4.refs_2_.refs_3_
  145.2 2.9 curl_inverse.3.refs_0_
  149.3 5.8 %all-to-all-start.3 = ((bf16[4,2,2,192,256]{4,3,2,1,0:T(8,128)(2,1)}), bf16[4,2,2,192,256]{4,3,2,1,0:T(8,128)(2,1)}, u32[]{:S(2)}, u32[]{:S(2)}) async-start(bf16[4,2,2,192,256]{4,3,2,1,0:T(8,128)(2,1)} %copy-done.14), calls=%async_computation.3 | async-start | bytes 3145728 | tf_op jit(solution)/shard_map/all_to_all | solution.py:882
  155.1 3.8 %collective-permute-start.20 = (bf16[2,2,192,256]{3,2,1,0:T(8,128)(2,1)}, bf16[2,2,192,256]{3,2,1,0:T(8,128)(2,1)}, u32[]{:S(2)}, u32[]{:S(2)}) collective-permute-start(bf16[2,2,192,256]{3,2,1,0:T(8,128)(2,1)} %get-tuple-element.115), channel_id=1, source_target_pairs={{0,24},{8,0},{16,8},{24,16},{1,25},{9,1},{17,9},{25,17},{2,26},{10... | collective-permute-start | bytes 1179656 | tf_op jit(solution)/shard_map/ppermute | solution.py:810
  159.0 31.3 %collective-permute-done.20 = bf16[2,2,192,256]{3,2,1,0:T(8,128)(2,1)} collective-permute-done((bf16[2,2,192,256]{3,2,1,0:T(8,128)(2,1)}, bf16[2,2,192,256]{3,2,1,0:T(8,128)(2,1)}, u32[]{:S(2)}, u32[]{:S(2)}) %collective-permute-start.20) | collective-permute-done | bytes 393248 | tf_op jit(solution)/shard_map/ppermute | solution.py:810
  190.3 11.7 %collective-permute-done.18 = bf16[2,2,192,256]{3,2,1,0:T(8,128)(2,1)} collective-permute-done((bf16[2,2,192,256]{3,2,1,0:T(8,128)(2,1)}, bf16[2,2,192,256]{3,2,1,0:T(8,128)(2,1)}, u32[]{:S(2)}, u32[]{:S(2)}) %collective-permute-start.18) | collective-permute-done | bytes 393248 | tf_op jit(solution)/shard_map/ppermute | solution.py:810
  204.5 3.2 gather_fusion
  213.4 3.0 curl_inverse.4.refs_0_
  219.2 9.2 %all-to-all-start.5 = ((bf16[4,2,2,192,256]{4,3,2,1,0:T(8,128)(2,1)}), bf16[4,2,2,192,256]{4,3,2,1,0:T(8,128)(2,1)}, u32[]{:S(2)}, u32[]{:S(2)}) async-start(bf16[4,2,2,192,256]{4,3,2,1,0:T(8,128)(2,1)} %copy-done.16), calls=%async_computation.5 | async-start | bytes 3145728 | tf_op jit(solution)/shard_map/all_to_all | solution.py:882
  228.4 7.4 %y_inverse_parts.2 = (bf16[2,192,256]{2,1,0:T(8,128)(2,1)}, bf16[2,192,256]{2,1,0:T(8,128)(2,1)}, bf16[2,192,256]{2,1,0:T(8,128)(2,1)}, bf16[2,192,256]{2,1,0:T(...) custom-call(s32[1]{0:T(128)} %bitcast.refs_0_.me_ref, ...), custom_call_target="tpu_custom_call" | custom-call | flops 1 | bytes 12000000 | tf_op jit(solution)/shard_map/y_inverse_parts/pallas_call | solution.py:340
  245.5 4.0 %collective-permute-start.27 = (bf16[2,192,256]{2,1,0:T(8,128)(2,1)}, bf16[2,192,256]{2,1,0:T(8,128)(2,1)S(1)}, u32[]{:S(2)}, u32[]{:S(2)}) collective-permute-start(bf16[2,192,256]{2,1,0:T(8,128)(2,1)} %get-tuple-element.83), channel_id=1, source_target_pairs={{0,7},{1,0},{2,1},{3,2},{4,3},{5,4},{6,5},{7,6},{8,15},{9,8},{10,9... | collective-permute-start | bytes 589832 | tf_op jit(solution)/shard_map/ppermute | solution.py:810
  249.5 3.0 collective-permute-done.23.refs_7_.refs_3_
  258.3 3.8 %curl_inverse.5 = bf16[4,2,2,192,256]{4,3,2,1,0:T(8,128)(2,1)} custom-call(s32[2]{0:T(128)S(1)} %pad_add_fusion.refs_0_, bf16[1024,1024]{1,0:T(8,128)(2,1)S(1)} %copy-done.10, f32[2,2,192,1024]{3,2,1,0:T(8,128)S(1)} %copy-done.4, f32[2,2,192,1024]{3,2,1,0:T(8,128)S(1)} %copy-done.6, bf16[2,192,256]{2,1,0:T(8,128)(2,1)S(1)} %copy-done.20, ...), custom_call_target="tpu_custom_call" | custom-call | flops 1 | bytes 12000000 | tf_op jit(solution)/shard_map/curl_inverse/pallas_call | solution.py:446
  262.1 3.2 all-to-all-done.5
  265.3 3.7 all-to-all-start.4
  269.0 5.3 %make_adjoint.3 = (f32[16,192,256]{2,1,0:T(8,128)}, bf16[16,192,256]{2,1,0:T(8,128)(2,1)}, bf16[3,16,192]{2,1,0:T(8,128)(2,1)}, bf16[3,16,192]{2,1,0:T(8,128)(2,...) custom-call(s32[1]{0:T(128)} %bitcast.refs_0_.me_ref, ...), custom_call_target="tpu_custom_call" | custom-call | flops 1 | bytes 15000000 | tf_op jit(solution)/shard_map/make_adjoint/pallas_call | solution.py:575
  274.4 7.2 %y_inverse_parts.3 = (bf16[2,192,256]{2,1,0:T(8,128)(2,1)}, bf16[2,192,256]{2,1,0:T(8,128)(2,1)}, bf16[2,192,256]{2,1,0:T(8,128)(2,1)}, bf16[2,192,256]{2,1,0:T(...) custom-call(s32[1]{0:T(128)} %bitcast.refs_0_.me_ref, ...), custom_call_target="tpu_custom_call" | custom-call | flops 1 | bytes 12000000 | tf_op jit(solution)/shard_map/y_inverse_parts/pallas_call | solution.py:340
  291.3 3.9 %collective-permute-start.34 = (bf16[2,192,256]{2,1,0:T(8,128)(2,1)}, bf16[2,192,256]{2,1,0:T(8,128)(2,1)S(1)}, u32[]{:S(2)}, u32[]{:S(2)}) collective-permute-start(bf16[2,192,256]{2,1,0:T(8,128)(2,1)} %get-tuple-element.92), channel_id=1, source_target_pairs={{0,7},{1,0},{2,1},{3,2},{4,3},{5,4},{6,5},{7,6},{8,15},{9,8},{10,9... | collective-permute-start | bytes 589832 | tf_op jit(solution)/shard_map/ppermute | solution.py:810
  295.2 3.1 collective-permute-done.30.refs_3_
  301.4 4.5 %all-to-all-done.4 = bf16[4,2,2,192,256]{4,3,2,1,0:T(8,128)(2,1)S(1)} async-done(((bf16[4,2,2,192,256]{4,3,2,1,0:T(8,128)(2,1)}), bf16[4,2,2,192,256]{4,3,2,1,0:T(8,128)(2,1)S(1)}, u32[]{:S(2)}, u32[]{:S(2)}) %all-to-all-start.4) | async-done | bytes 1572896 | tf_op jit(solution)/shard_map/all_to_all | solution.py:882
  309.2 3.9 %y_inverse.1.refs_13_ = bf16[8,2,192,256]{3,2,1,0:T(8,128)(2,1)} custom-call(bf16[1536,1536]{1,0:T(8,128)(2,1)S(1)} %copy-done, bf16[4,1,2,2,192,256]{5,4,3,2,1,0:T(8,128)(2,1)S(1)} %bitcast.37, bf16[2,192,256]{2,1,0:T(8,128)(2,1)S(1)} %copy-done.17, bf16[2,192,256]{2,1,0:T(8,128)(2,1)S(1)} %collective-permute-done.28.refs_1_, ...), custom_call_target="tpu_custom_call" | custom-call | flops 1 | bytes 12000000 | tf_op jit(solution)/shard_map/y_inverse/pallas_call | solution.py:285
  313.1 4.3 %all-to-all-start.6 = ((bf16[8,2,192,256]{3,2,1,0:T(8,128)(2,1)}), bf16[8,2,192,256]{3,2,1,0:T(8,128)(2,1)S(1)}, u32[]{:S(2)}, u32[]{:S(2)}) async-start(bf16[8,2,192,256]{3,2,1,0:T(8,128)(2,1)} %y_inverse.1.refs_13_), calls=%async_computation.6 | async-start | bytes 3145728 | tf_op jit(solution)/shard_map/all_to_all | solution.py:894
  317.4 5.2 %add_grad_vort.3.refs_10_ = bf16[3,16,192,256]{3,2,1,0:T(8,128)(2,1)} custom-call(bf16[256,256]{1,0:T(8,128)(2,1)} %constant.87.clone.refs_0_, bf16[192,192]{1,0:T(8,128)(2,1)} %constant.88.clone.refs_1_, bf16[3,16,192,256]{3,2,1,0:T(8,128)(2,1)} %refs_4_.6, bf16[3,16,192,256]{3,2,1,0:T(8,128)(2,1)} %refs_4_.6, bf16[3,16,192,256]{3,2,1,0:T(8,128)(2,1)} %refs_4_.6, ...), custom_call_target="tpu_custom_call" | custom-call | flops 1 | bytes 27000000 | tf_op jit(solution)/shard_map/add_grad_vort/pallas_call | solution.py:698
  322.6 5.3 %make_adjoint.4 = (f32[16,192,256]{2,1,0:T(8,128)}, bf16[16,192,256]{2,1,0:T(8,128)(2,1)}, bf16[3,16,192]{2,1,0:T(8,128)(2,1)}, bf16[3,16,192]{2,1,0:T(8,128)(2,...) custom-call(s32[1]{0:T(128)} %bitcast.refs_0_.me_ref, ...), custom_call_target="tpu_custom_call", output_to_operand_aliasing={{2}: (10, {}), {3}: (11, {}), {4}: (12, {}), {5}: (13, {})} | custom-call | flops 1 | bytes 15000000 | tf_op jit(solution)/shard_map/make_adjoint/pallas_call | solution.py:575
  327.9 7.1 %add_grad_vort.4.refs_6_.refs_10_ = bf16[3,16,192,256]{3,2,1,0:T(8,128)(2,1)} custom-call(bf16[256,256]{1,0:T(8,128)(2,1)} %constant.87.clone.refs_0_, bf16[192,192]{1,0:T(8,128)(2,1)} %constant.88.clone.refs_1_, bf16[3,16,192,256]{3,2,1,0:T(8,128)(2,1)} %refs_4_.6, bf16[3,16,192,256]{3,2,1,0:T(8,128)(2,1)} %refs_4_.6, bf16[3,16,192,256]{3,2,1,0:T(8,128)(2,1)} %refs_4_.6, ...), custom_call_target="tpu_custom_call" | custom-call | flops 1 | bytes 27000000 | tf_op jit(solution)/shard_map/add_grad_vort/pallas_call | solution.py:698
  335.1 3.4 all-to-all-done.6
  339.6 5.2 %make_adjoint.5 = (f32[16,192,256]{2,1,0:T(8,128)}, bf16[16,192,256]{2,1,0:T(8,128)(2,1)}, bf16[3,16,192]{2,1,0:T(8,128)(2,1)}, bf16[3,16,192]{2,1,0:T(8,128)(2,...) custom-call(s32[1]{0:T(128)} %bitcast.refs_0_.me_ref, ...), custom_call_target="tpu_custom_call", output_to_operand_aliasing={{2}: (3, {}), {3}: (4, {}), {4}: (5, {}), {5}: (6, {})} | custom-call | flops 1 | bytes 15000000 | tf_op jit(solution)/shard_map/make_adjoint/pallas_call | solution.py:575
  347.5 3.8 %collective-permute-start.36 = (bf16[3,16,192]{2,1,0:T(8,128)(2,1)}, bf16[3,16,192]{2,1,0:T(8,128)(2,1)S(1)}, u32[]{:S(2)}, u32[]{:S(2)}) collective-permute-start(bf16[3,16,192]{2,1,0:T(8,128)(2,1)} %get-tuple-element.107), channel_id=1, source_target_pairs={{8,0},{16,8},{24,16},{0,24},{9,1},{17,9},{25,17},{1,25},{10,2},{18... | collective-permute-start | bytes 55304 | tf_op jit(solution)/shard_map/ppermute | solution.py:524
  351.3 8.4 %add_grad_vort.5.refs_22_ = f32[3,16,192,256]{3,2,1,0:T(8,128)} custom-call(bf16[256,256]{1,0:T(8,128)(2,1)} %constant.87.clone.refs_0_, bf16[192,192]{1,0:T(8,128)(2,1)} %constant.88.clone.refs_1_, bf16[3,16,192,256]{3,2,1,0:T(8,128)(2,1)} %refs_4_.6, bf16[3,16,192,256]{3,2,1,0:T(8,128)(2,1)} %refs_4_.6, bf16[3,16,192,256]{3,2,1,0:T(8,128)(2,1)} %refs_4_.6, ...), custom_call_target="tpu_custom_call" | custom-call | flops 1 | bytes 27000000 | tf_op jit(solution)/shard_map/add_grad_vort/pallas_call | solution.py:698
  360.4 11.0 %write_grad_vel.1 = f32[3,16,192,256]{3,2,1,0:T(8,128)} custom-call(bf16[256,256]{1,0:T(8,128)(2,1)} %constant.89.clone.refs_0_, bf16[192,192]{1,0:T(8,128)(2,1)} %constant.90.clone.refs_1_, bf16[3,16,192,256]{3,2,1,0:T(8,128)(2,1)} %refs_4_.7, bf16[3,16,192,256]{3,2,1,0:T(8,128)(2,1)} %refs_4_.7, bf16[3,16,192,256]{3,2,1,0:T(8,128)(2,1)} %refs_4_.7, ...), custom_call_target="tpu_custom_call" | custom-call | flops 1 | bytes 36000000 | tf_op jit(solution)/shard_map/write_grad_vel/pallas_call | solution.py:787
  (202 shorter events, 96.7 us)
Async XLA Ops:
  3.8 26.2 %all-to-all-start = ((bf16[8,2,192,256]{3,2,1,0:T(8,128)(2,1)}), bf16[8,2,192,256]{3,2,1,0:T(8,128)(2,1)S(1)}, u32[]{:S(2)}, u32[]{:S(2)}) async-start(bf16[8,2,192,256]{3,2,1,0:T(8,128)(2,1)} %bitcast.39), calls=%async_computation | async-start | bytes 3145728 | tf_op jit(solution)/shard_map/all_to_all | solution.py:851
  16.9 5.3 %collective-permute-start.1 = (bf16[4,16,192]{2,1,0:T(8,128)(2,1)S(1)}, bf16[4,16,192]{2,1,0:T(8,128)(2,1)S(1)}, u32[]{:S(2)}, u32[]{:S(2)}) collective-permute-start(bf16[4,16,192]{2,1,0:T(8,128)(2,1)S(1)} %pad_maximum_fusion.2), channel_id=1, source_target_pairs={{8,0},{16,8},{24,16},{0,24},{9,1},{17,9},{25,17},{1,25},{10,2},{18... | collective-permute-start | bytes 73736 | tf_op jit(solution)/shard_map/ppermute | solution.py:524
  21.3 5.8 %collective-permute-start = (bf16[4,16,192]{2,1,0:T(8,128)(2,1)S(1)}, bf16[4,16,192]{2,1,0:T(8,128)(2,1)S(1)}, u32[]{:S(2)}, u32[]{:S(2)}) collective-permute-start(bf16[4,16,192]{2,1,0:T(8,128)(2,1)S(1)} %pad_maximum_fusion.1), channel_id=1, source_target_pairs={{0,8},{8,16},{16,24},{24,0},{1,9},{9,17},{17,25},{25,1},{2,10},{10... | collective-permute-start | bytes 73736 | tf_op jit(solution)/shard_map/ppermute | solution.py:524
  36.2 40.5 %all-to-all-start.1 = ((bf16[4,2,2,192,256]{4,3,2,1,0:T(8,128)(2,1)}), bf16[4,2,2,192,256]{4,3,2,1,0:T(8,128)(2,1)S(1)}, u32[]{:S(2)}, u32[]{:S(2)}) async-start(bf16[4,2,2,192,256]{4,3,2,1,0:T(8,128)(2,1)} %bitcast.3.refs_2_), calls=%async_computation.1 | async-start | bytes 3145728 | tf_op jit(solution)/shard_map/all_to_all | solution.py:865
  46.4 13.3 %collective-permute-start.2 = (bf16[2,192,256]{2,1,0:T(8,128)(2,1)}, bf16[2,192,256]{2,1,0:T(8,128)(2,1)S(1)}, u32[]{:S(2)}, u32[]{:S(2)}) collective-permute-start(bf16[2,192,256]{2,1,0:T(8,128)(2,1)} %get-tuple-element.61), channel_id=1, source_target_pairs={{0,1},{1,2},{2,3},{3,4},{4,5},{5,6},{6,7},{7,0},{8,9},{9,10},{10,1... | collective-permute-start | bytes 589832 | tf_op jit(solution)/shard_map/ppermute | solution.py:810
  46.4 13.8 %collective-permute-start.3 = (bf16[2,192,256]{2,1,0:T(8,128)(2,1)}, bf16[2,192,256]{2,1,0:T(8,128)(2,1)S(1)}, u32[]{:S(2)}, u32[]{:S(2)}) collective-permute-start(bf16[2,192,256]{2,1,0:T(8,128)(2,1)} %get-tuple-element.62), channel_id=1, source_target_pairs={{0,2},{1,3},{2,4},{3,5},{4,6},{5,7},{6,0},{7,1},{8,10},{9,11},{10,... | collective-permute-start | bytes 589832 | tf_op jit(solution)/shard_map/ppermute | solution.py:810
  47.0 12.1 %collective-permute-start.9 = (bf16[4,16,256]{2,1,0:T(8,128)(2,1)S(1)}, bf16[4,16,256]{2,1,0:T(8,128)(2,1)S(1)}, u32[]{:S(2)}, u32[]{:S(2)}) collective-permute-start(bf16[4,16,256]{2,1,0:T(8,128)(2,1)S(1)} %pad_maximum_fusion.3), channel_id=1, source_target_pairs={{0,1},{1,2},{2,3},{3,4},{4,5},{5,6},{6,7},{7,0},{8,9},{9,10},{10,1... | collective-permute-start | bytes 98312 | tf_op jit(solution)/shard_map/ppermute | solution.py:524
  48.3 11.4 %collective-permute-start.10 = (bf16[4,16,256]{2,1,0:T(8,128)(2,1)S(1)}, bf16[4,16,256]{2,1,0:T(8,128)(2,1)S(1)}, u32[]{:S(2)}, u32[]{:S(2)}) collective-permute-start(bf16[4,16,256]{2,1,0:T(8,128)(2,1)S(1)} %pad_maximum_fusion.4), channel_id=1, source_target_pairs={{1,0},{2,1},{3,2},{4,3},{5,4},{6,5},{7,6},{0,7},{9,8},{10,9},{11,1... | collective-permute-start | bytes 98312 | tf_op jit(solution)/shard_map/ppermute | solution.py:524
  49.7 12.7 %collective-permute-start.4 = (bf16[2,192,256]{2,1,0:T(8,128)(2,1)}, bf16[2,192,256]{2,1,0:T(8,128)(2,1)S(1)}, u32[]{:S(2)}, u32[]{:S(2)}) collective-permute-start(bf16[2,192,256]{2,1,0:T(8,128)(2,1)} %get-tuple-element.63), channel_id=1, source_target_pairs={{0,3},{1,4},{2,5},{3,6},{4,7},{5,0},{6,1},{7,2},{8,11},{9,12},{10,... | collective-permute-start | bytes 589832 | tf_op jit(solution)/shard_map/ppermute | solution.py:810
  59.2 6.5 %collective-permute-start.5 = (bf16[2,192,256]{2,1,0:T(8,128)(2,1)}, bf16[2,192,256]{2,1,0:T(8,128)(2,1)S(1)}, u32[]{:S(2)}, u32[]{:S(2)}) collective-permute-start(bf16[2,192,256]{2,1,0:T(8,128)(2,1)} %get-tuple-element.64), channel_id=1, source_target_pairs={{0,4},{1,5},{2,6},{3,7},{4,0},{5,1},{6,2},{7,3},{8,12},{9,13},{10,... | collective-permute-start | bytes 589832 | tf_op jit(solution)/shard_map/ppermute | solution.py:810
  59.7 6.8 %collective-permute-start.6 = (bf16[2,192,256]{2,1,0:T(8,128)(2,1)}, bf16[2,192,256]{2,1,0:T(8,128)(2,1)S(1)}, u32[]{:S(2)}, u32[]{:S(2)}) collective-permute-start(bf16[2,192,256]{2,1,0:T(8,128)(2,1)} %get-tuple-element.65), channel_id=1, source_target_pairs={{0,5},{1,6},{2,7},{3,0},{4,1},{5,2},{6,3},{7,4},{8,13},{9,14},{10,... | collective-permute-start | bytes 589832 | tf_op jit(solution)/shard_map/ppermute | solution.py:810
  59.7 8.0 %collective-permute-start.7 = (bf16[2,192,256]{2,1,0:T(8,128)(2,1)}, bf16[2,192,256]{2,1,0:T(8,128)(2,1)S(1)}, u32[]{:S(2)}, u32[]{:S(2)}) collective-permute-start(bf16[2,192,256]{2,1,0:T(8,128)(2,1)} %get-tuple-element.66), channel_id=1, source_target_pairs={{0,6},{1,7},{2,0},{3,1},{4,2},{5,3},{6,4},{7,5},{8,14},{9,15},{10,... | collective-permute-start | bytes 589832 | tf_op jit(solution)/shard_map/ppermute | solution.py:810
  60.3 9.2 %collective-permute-start.8 = (bf16[2,192,256]{2,1,0:T(8,128)(2,1)}, bf16[2,192,256]{2,1,0:T(8,128)(2,1)S(1)}, u32[]{:S(2)}, u32[]{:S(2)}) collective-permute-start(bf16[2,192,256]{2,1,0:T(8,128)(2,1)} %get-tuple-element.67), channel_id=1, source_target_pairs={{0,7},{1,0},{2,1},{3,2},{4,3},{5,4},{6,5},{7,6},{8,15},{9,8},{10,9... | collective-permute-start | bytes 589832 | tf_op jit(solution)/shard_map/ppermute | solution.py:810
  76.7 62.0 %all-to-all-start.2 = ((bf16[4,2,2,192,256]{4,3,2,1,0:T(8,128)(2,1)}), bf16[4,2,2,192,256]{4,3,2,1,0:T(8,128)(2,1)}, u32[]{:S(2)}, u32[]{:S(2)}) async-start(bf16[4,2,2,192,256]{4,3,2,1,0:T(8,128)(2,1)} %bitcast.34), calls=%async_computation.2 | async-start | bytes 3145728 | tf_op jit(solution)/shard_map/all_to_all | solution.py:865
  85.1 11.5 %collective-permute-start.11 = (bf16[2,192,256]{2,1,0:T(8,128)(2,1)}, bf16[2,192,256]{2,1,0:T(8,128)(2,1)S(1)}, u32[]{:S(2)}, u32[]{:S(2)}) collective-permute-start(bf16[2,192,256]{2,1,0:T(8,128)(2,1)} %get-tuple-element.69), channel_id=1, source_target_pairs={{0,1},{1,2},{2,3},{3,4},{4,5},{5,6},{6,7},{7,0},{8,9},{9,10},{10,1... | collective-permute-start | bytes 589832 | tf_op jit(solution)/shard_map/ppermute | solution.py:810
  86.8 11.0 %collective-permute-start.12 = (bf16[2,192,256]{2,1,0:T(8,128)(2,1)}, bf16[2,192,256]{2,1,0:T(8,128)(2,1)S(1)}, u32[]{:S(2)}, u32[]{:S(2)}) collective-permute-start(bf16[2,192,256]{2,1,0:T(8,128)(2,1)} %get-tuple-element.70), channel_id=1, source_target_pairs={{0,2},{1,3},{2,4},{3,5},{4,6},{5,7},{6,0},{7,1},{8,10},{9,11},{10,... | collective-permute-start | bytes 589832 | tf_op jit(solution)/shard_map/ppermute | solution.py:810
  91.0 14.4 %collective-permute-start.13 = (bf16[2,192,256]{2,1,0:T(8,128)(2,1)}, bf16[2,192,256]{2,1,0:T(8,128)(2,1)S(1)}, u32[]{:S(2)}, u32[]{:S(2)}) collective-permute-start(bf16[2,192,256]{2,1,0:T(8,128)(2,1)} %get-tuple-element.71), channel_id=1, source_target_pairs={{0,3},{1,4},{2,5},{3,6},{4,7},{5,0},{6,1},{7,2},{8,11},{9,12},{10,... | collective-permute-start | bytes 589832 | tf_op jit(solution)/shard_map/ppermute | solution.py:810
  91.8 13.9 %collective-permute-start.14 = (bf16[2,192,256]{2,1,0:T(8,128)(2,1)}, bf16[2,192,256]{2,1,0:T(8,128)(2,1)S(1)}, u32[]{:S(2)}, u32[]{:S(2)}) collective-permute-start(bf16[2,192,256]{2,1,0:T(8,128)(2,1)} %get-tuple-element.72), channel_id=1, source_target_pairs={{0,4},{1,5},{2,6},{3,7},{4,0},{5,1},{6,2},{7,3},{8,12},{9,13},{10,... | collective-permute-start | bytes 589832 | tf_op jit(solution)/shard_map/ppermute | solution.py:810
  93.2 14.8 %collective-permute-start.15 = (bf16[2,192,256]{2,1,0:T(8,128)(2,1)}, bf16[2,192,256]{2,1,0:T(8,128)(2,1)S(1)}, u32[]{:S(2)}, u32[]{:S(2)}) collective-permute-start(bf16[2,192,256]{2,1,0:T(8,128)(2,1)} %get-tuple-element.73), channel_id=1, source_target_pairs={{0,5},{1,6},{2,7},{3,0},{4,1},{5,2},{6,3},{7,4},{8,13},{9,14},{10,... | collective-permute-start | bytes 589832 | tf_op jit(solution)/shard_map/ppermute | solution.py:810
  96.6 11.5 %collective-permute-start.16 = (bf16[2,192,256]{2,1,0:T(8,128)(2,1)}, bf16[2,192,256]{2,1,0:T(8,128)(2,1)S(1)}, u32[]{:S(2)}, u32[]{:S(2)}) collective-permute-start(bf16[2,192,256]{2,1,0:T(8,128)(2,1)} %get-tuple-element.74), channel_id=1, source_target_pairs={{0,6},{1,7},{2,0},{3,1},{4,2},{5,3},{6,4},{7,5},{8,14},{9,15},{10,... | collective-permute-start | bytes 589832 | tf_op jit(solution)/shard_map/ppermute | solution.py:810
  97.9 10.2 %collective-permute-start.17 = (bf16[2,192,256]{2,1,0:T(8,128)(2,1)}, bf16[2,192,256]{2,1,0:T(8,128)(2,1)S(1)}, u32[]{:S(2)}, u32[]{:S(2)}) collective-permute-start(bf16[2,192,256]{2,1,0:T(8,128)(2,1)} %get-tuple-element.75), channel_id=1, source_target_pairs={{0,7},{1,0},{2,1},{3,2},{4,3},{5,4},{6,5},{7,6},{8,15},{9,8},{10,9... | collective-permute-start | bytes 589832 | tf_op jit(solution)/shard_map/ppermute | solution.py:810
  118.2 20.5 %collective-permute-start.19 = (bf16[2,2,192,256]{3,2,1,0:T(8,128)(2,1)}, bf16[2,2,192,256]{3,2,1,0:T(8,128)(2,1)S(1)}, u32[]{:S(2)}, u32[]{:S(2)}) collective-permute-start(bf16[2,2,192,256]{3,2,1,0:T(8,128)(2,1)} %get-tuple-element.116), channel_id=1, source_target_pairs={{0,16},{8,24},{16,0},{24,8},{1,17},{9,25},{17,1},{25,9},{2,18},{10... | collective-permute-start | bytes 1179656 | tf_op jit(solution)/shard_map/ppermute | solution.py:810
  149.3 69.9 %all-to-all-start.3 = ((bf16[4,2,2,192,256]{4,3,2,1,0:T(8,128)(2,1)}), bf16[4,2,2,192,256]{4,3,2,1,0:T(8,128)(2,1)}, u32[]{:S(2)}, u32[]{:S(2)}) async-start(bf16[4,2,2,192,256]{4,3,2,1,0:T(8,128)(2,1)} %copy-done.14), calls=%async_computation.3 | async-start | bytes 3145728 | tf_op jit(solution)/shard_map/all_to_all | solution.py:882
  155.1 35.2 %collective-permute-start.20 = (bf16[2,2,192,256]{3,2,1,0:T(8,128)(2,1)}, bf16[2,2,192,256]{3,2,1,0:T(8,128)(2,1)}, u32[]{:S(2)}, u32[]{:S(2)}) collective-permute-start(bf16[2,2,192,256]{3,2,1,0:T(8,128)(2,1)} %get-tuple-element.115), channel_id=1, source_target_pairs={{0,24},{8,0},{16,8},{24,16},{1,25},{9,1},{17,9},{25,17},{2,26},{10... | collective-permute-start | bytes 1179656 | tf_op jit(solution)/shard_map/ppermute | solution.py:810
  158.9 43.0 %collective-permute-start.18 = (bf16[2,2,192,256]{3,2,1,0:T(8,128)(2,1)}, bf16[2,2,192,256]{3,2,1,0:T(8,128)(2,1)}, u32[]{:S(2)}, u32[]{:S(2)}) collective-permute-start(bf16[2,2,192,256]{3,2,1,0:T(8,128)(2,1)} %get-tuple-element.117), channel_id=1, source_target_pairs={{0,8},{8,16},{16,24},{24,0},{1,9},{9,17},{17,25},{25,1},{2,10},{10... | collective-permute-start | bytes 1179656 | tf_op jit(solution)/shard_map/ppermute | solution.py:810
  219.2 46.1 %all-to-all-start.5 = ((bf16[4,2,2,192,256]{4,3,2,1,0:T(8,128)(2,1)}), bf16[4,2,2,192,256]{4,3,2,1,0:T(8,128)(2,1)}, u32[]{:S(2)}, u32[]{:S(2)}) async-start(bf16[4,2,2,192,256]{4,3,2,1,0:T(8,128)(2,1)} %copy-done.16), calls=%async_computation.5 | async-start | bytes 3145728 | tf_op jit(solution)/shard_map/all_to_all | solution.py:882
  228.4 27.2 %copy-start.4 = (f32[2,2,192,1024]{3,2,1,0:T(8,128)S(1)}, f32[2,2,192,1024]{3,2,1,0:T(8,128)}, u32[]{:S(2)}) copy-start(f32[2,2,192,1024]{3,2,1,0:T(8,128)} %copy-done.2) | copy-start | bytes 9437188
  228.4 27.2 %copy-start.6 = (f32[2,2,192,1024]{3,2,1,0:T(8,128)S(1)}, f32[2,2,192,1024]{3,2,1,0:T(8,128)}, u32[]{:S(2)}) copy-start(f32[2,2,192,1024]{3,2,1,0:T(8,128)} %copy-done.5) | copy-start | bytes 9437188
  235.8 7.9 %collective-permute-start.21 = (bf16[2,192,256]{2,1,0:T(8,128)(2,1)}, bf16[2,192,256]{2,1,0:T(8,128)(2,1)S(1)}, u32[]{:S(2)}, u32[]{:S(2)}) collective-permute-start(bf16[2,192,256]{2,1,0:T(8,128)(2,1)} %get-tuple-element.77), channel_id=1, source_target_pairs={{0,1},{1,2},{2,3},{3,4},{4,5},{5,6},{6,7},{7,0},{8,9},{9,10},{10,1... | collective-permute-start | bytes 589832 | tf_op jit(solution)/shard_map/ppermute | solution.py:810
  235.9 9.6 %collective-permute-start.22 = (bf16[2,192,256]{2,1,0:T(8,128)(2,1)}, bf16[2,192,256]{2,1,0:T(8,128)(2,1)S(1)}, u32[]{:S(2)}, u32[]{:S(2)}) collective-permute-start(bf16[2,192,256]{2,1,0:T(8,128)(2,1)} %get-tuple-element.78), channel_id=1, source_target_pairs={{0,2},{1,3},{2,4},{3,5},{4,6},{5,7},{6,0},{7,1},{8,10},{9,11},{10,... | collective-permute-start | bytes 589832 | tf_op jit(solution)/shard_map/ppermute | solution.py:810
  237.9 14.6 %collective-permute-start.23 = (bf16[2,192,256]{2,1,0:T(8,128)(2,1)}, bf16[2,192,256]{2,1,0:T(8,128)(2,1)S(1)}, u32[]{:S(2)}, u32[]{:S(2)}) collective-permute-start(bf16[2,192,256]{2,1,0:T(8,128)(2,1)} %get-tuple-element.79), channel_id=1, source_target_pairs={{0,3},{1,4},{2,5},{3,6},{4,7},{5,0},{6,1},{7,2},{8,11},{9,12},{10,... | collective-permute-start | bytes 589832 | tf_op jit(solution)/shard_map/ppermute | solution.py:810
  240.1 12.6 %collective-permute-start.24 = (bf16[2,192,256]{2,1,0:T(8,128)(2,1)}, bf16[2,192,256]{2,1,0:T(8,128)(2,1)S(1)}, u32[]{:S(2)}, u32[]{:S(2)}) collective-permute-start(bf16[2,192,256]{2,1,0:T(8,128)(2,1)} %get-tuple-element.80), channel_id=1, source_target_pairs={{0,4},{1,5},{2,6},{3,7},{4,0},{5,1},{6,2},{7,3},{8,12},{9,13},{10,... | collective-permute-start | bytes 589832 | tf_op jit(solution)/shard_map/ppermute | solution.py:810
  240.8 14.8 %collective-permute-start.25 = (bf16[2,192,256]{2,1,0:T(8,128)(2,1)}, bf16[2,192,256]{2,1,0:T(8,128)(2,1)S(1)}, u32[]{:S(2)}, u32[]{:S(2)}) collective-permute-start(bf16[2,192,256]{2,1,0:T(8,128)(2,1)} %get-tuple-element.81), channel_id=1, source_target_pairs={{0,5},{1,6},{2,7},{3,0},{4,1},{5,2},{6,3},{7,4},{8,13},{9,14},{10,... | collective-permute-start | bytes 589832 | tf_op jit(solution)/shard_map/ppermute | solution.py:810
  243.7 11.9 %collective-permute-start.26 = (bf16[2,192,256]{2,1,0:T(8,128)(2,1)}, bf16[2,192,256]{2,1,0:T(8,128)(2,1)S(1)}, u32[]{:S(2)}, u32[]{:S(2)}) collective-permute-start(bf16[2,192,256]{2,1,0:T(8,128)(2,1)} %get-tuple-element.82), channel_id=1, source_target_pairs={{0,6},{1,7},{2,0},{3,1},{4,2},{5,3},{6,4},{7,5},{8,14},{9,15},{10,... | collective-permute-start | bytes 589832 | tf_op jit(solution)/shard_map/ppermute | solution.py:810
  245.5 10.1 %collective-permute-start.27 = (bf16[2,192,256]{2,1,0:T(8,128)(2,1)}, bf16[2,192,256]{2,1,0:T(8,128)(2,1)S(1)}, u32[]{:S(2)}, u32[]{:S(2)}) collective-permute-start(bf16[2,192,256]{2,1,0:T(8,128)(2,1)} %get-tuple-element.83), channel_id=1, source_target_pairs={{0,7},{1,0},{2,1},{3,2},{4,3},{5,4},{6,5},{7,6},{8,15},{9,8},{10,9... | collective-permute-start | bytes 589832 | tf_op jit(solution)/shard_map/ppermute | solution.py:810
  265.3 40.6 %all-to-all-start.4 = ((bf16[4,2,2,192,256]{4,3,2,1,0:T(8,128)(2,1)}), bf16[4,2,2,192,256]{4,3,2,1,0:T(8,128)(2,1)S(1)}, u32[]{:S(2)}, u32[]{:S(2)}) async-start(bf16[4,2,2,192,256]{4,3,2,1,0:T(8,128)(2,1)} %curl_inverse.5), calls=%async_computation.4 | async-start | bytes 3145728 | tf_op jit(solution)/shard_map/all_to_all | solution.py:882
  281.6 7.9 %collective-permute-start.28 = (bf16[2,192,256]{2,1,0:T(8,128)(2,1)}, bf16[2,192,256]{2,1,0:T(8,128)(2,1)S(1)}, u32[]{:S(2)}, u32[]{:S(2)}) collective-permute-start(bf16[2,192,256]{2,1,0:T(8,128)(2,1)} %get-tuple-element.86), channel_id=1, source_target_pairs={{0,1},{1,2},{2,3},{3,4},{4,5},{5,6},{6,7},{7,0},{8,9},{9,10},{10,1... | collective-permute-start | bytes 589832 | tf_op jit(solution)/shard_map/ppermute | solution.py:810
  281.7 9.6 %collective-permute-start.29 = (bf16[2,192,256]{2,1,0:T(8,128)(2,1)}, bf16[2,192,256]{2,1,0:T(8,128)(2,1)S(1)}, u32[]{:S(2)}, u32[]{:S(2)}) collective-permute-start(bf16[2,192,256]{2,1,0:T(8,128)(2,1)} %get-tuple-element.87), channel_id=1, source_target_pairs={{0,2},{1,3},{2,4},{3,5},{4,6},{5,7},{6,0},{7,1},{8,10},{9,11},{10,... | collective-permute-start | bytes 589832 | tf_op jit(solution)/shard_map/ppermute | solution.py:810
  283.7 14.6 %collective-permute-start.30 = (bf16[2,192,256]{2,1,0:T(8,128)(2,1)}, bf16[2,192,256]{2,1,0:T(8,128)(2,1)S(1)}, u32[]{:S(2)}, u32[]{:S(2)}) collective-permute-start(bf16[2,192,256]{2,1,0:T(8,128)(2,1)} %get-tuple-element.88), channel_id=1, source_target_pairs={{0,3},{1,4},{2,5},{3,6},{4,7},{5,0},{6,1},{7,2},{8,11},{9,12},{10,... | collective-permute-start | bytes 589832 | tf_op jit(solution)/shard_map/ppermute | solution.py:810
  285.9 12.6 %collective-permute-start.31 = (bf16[2,192,256]{2,1,0:T(8,128)(2,1)}, bf16[2,192,256]{2,1,0:T(8,128)(2,1)S(1)}, u32[]{:S(2)}, u32[]{:S(2)}) collective-permute-start(bf16[2,192,256]{2,1,0:T(8,128)(2,1)} %get-tuple-element.89), channel_id=1, source_target_pairs={{0,4},{1,5},{2,6},{3,7},{4,0},{5,1},{6,2},{7,3},{8,12},{9,13},{10,... | collective-permute-start | bytes 589832 | tf_op jit(solution)/shard_map/ppermute | solution.py:810
  286.6 14.8 %collective-permute-start.32 = (bf16[2,192,256]{2,1,0:T(8,128)(2,1)}, bf16[2,192,256]{2,1,0:T(8,128)(2,1)S(1)}, u32[]{:S(2)}, u32[]{:S(2)}) collective-permute-start(bf16[2,192,256]{2,1,0:T(8,128)(2,1)} %get-tuple-element.90), channel_id=1, source_target_pairs={{0,5},{1,6},{2,7},{3,0},{4,1},{5,2},{6,3},{7,4},{8,13},{9,14},{10,... | collective-permute-start | bytes 589832 | tf_op jit(solution)/shard_map/ppermute | solution.py:810
  289.5 11.9 %collective-permute-start.33 = (bf16[2,192,256]{2,1,0:T(8,128)(2,1)}, bf16[2,192,256]{2,1,0:T(8,128)(2,1)S(1)}, u32[]{:S(2)}, u32[]{:S(2)}) collective-permute-start(bf16[2,192,256]{2,1,0:T(8,128)(2,1)} %get-tuple-element.91), channel_id=1, source_target_pairs={{0,6},{1,7},{2,0},{3,1},{4,2},{5,3},{6,4},{7,5},{8,14},{9,15},{10,... | collective-permute-start | bytes 589832 | tf_op jit(solution)/shard_map/ppermute | solution.py:810
  291.3 10.1 %collective-permute-start.34 = (bf16[2,192,256]{2,1,0:T(8,128)(2,1)}, bf16[2,192,256]{2,1,0:T(8,128)(2,1)S(1)}, u32[]{:S(2)}, u32[]{:S(2)}) collective-permute-start(bf16[2,192,256]{2,1,0:T(8,128)(2,1)} %get-tuple-element.92), channel_id=1, source_target_pairs={{0,7},{1,0},{2,1},{3,2},{4,3},{5,4},{6,5},{7,6},{8,15},{9,8},{10,9... | collective-permute-start | bytes 589832 | tf_op jit(solution)/shard_map/ppermute | solution.py:810
  313.1 25.3 %all-to-all-start.6 = ((bf16[8,2,192,256]{3,2,1,0:T(8,128)(2,1)}), bf16[8,2,192,256]{3,2,1,0:T(8,128)(2,1)S(1)}, u32[]{:S(2)}, u32[]{:S(2)}) async-start(bf16[8,2,192,256]{3,2,1,0:T(8,128)(2,1)} %y_inverse.1.refs_13_), calls=%async_computation.6 | async-start | bytes 3145728 | tf_op jit(solution)/shard_map/all_to_all | solution.py:894
  344.8 14.9 %collective-permute-start.37 = (bf16[3,16,256]{2,1,0:T(8,128)(2,1)}, bf16[3,16,256]{2,1,0:T(8,128)(2,1)S(1)}, u32[]{:S(2)}, u32[]{:S(2)}) collective-permute-start(bf16[3,16,256]{2,1,0:T(8,128)(2,1)} %get-tuple-element.108), channel_id=1, source_target_pairs={{0,1},{1,2},{2,3},{3,4},{4,5},{5,6},{6,7},{7,0},{8,9},{9,10},{10,1... | collective-permute-start | bytes 73736 | tf_op jit(solution)/shard_map/ppermute | solution.py:524
  344.8 14.9 %collective-permute-start.38 = (bf16[3,16,256]{2,1,0:T(8,128)(2,1)}, bf16[3,16,256]{2,1,0:T(8,128)(2,1)S(1)}, u32[]{:S(2)}, u32[]{:S(2)}) collective-permute-start(bf16[3,16,256]{2,1,0:T(8,128)(2,1)} %get-tuple-element.109), channel_id=1, source_target_pairs={{1,0},{2,1},{3,2},{4,3},{5,4},{6,5},{7,6},{0,7},{9,8},{10,9},{11,1... | collective-permute-start | bytes 73736 | tf_op jit(solution)/shard_map/ppermute | solution.py:524
  347.5 12.2 %collective-permute-start.35 = (bf16[3,16,192]{2,1,0:T(8,128)(2,1)}, bf16[3,16,192]{2,1,0:T(8,128)(2,1)S(1)}, u32[]{:S(2)}, u32[]{:S(2)}) collective-permute-start(bf16[3,16,192]{2,1,0:T(8,128)(2,1)} %get-tuple-element.106), channel_id=1, source_target_pairs={{0,8},{8,16},{16,24},{24,0},{1,9},{9,17},{17,25},{25,1},{2,10},{10... | collective-permute-start | bytes 55304 | tf_op jit(solution)/shard_map/ppermute | solution.py:524
  347.5 12.2 %collective-permute-start.36 = (bf16[3,16,192]{2,1,0:T(8,128)(2,1)}, bf16[3,16,192]{2,1,0:T(8,128)(2,1)S(1)}, u32[]{:S(2)}, u32[]{:S(2)}) collective-permute-start(bf16[3,16,192]{2,1,0:T(8,128)(2,1)} %get-tuple-element.107), channel_id=1, source_target_pairs={{8,0},{16,8},{24,16},{0,24},{9,1},{17,9},{25,17},{1,25},{10,2},{18... | collective-permute-start | bytes 55304 | tf_op jit(solution)/shard_map/ppermute | solution.py:524
  (56 other events, 341.5 us)
